TPU v7x, 32 devices: a whole 2x2x4 slice. The times are simulated.
32 devices in a mesh: groups: 2 (over x), store: 8 (over z, y), tensor: 2 (over core).
Axes of the slice: x: 2, y: 2, z: 4, core: 2. Of those that a mesh axis runs over, the one named last changes fastest.
Arguments:
- queries: bfloat16 [16, 64, 8192], P(('groups', 'store'), None, 'tensor'), parts along dimension 0, may hold values from -9 to 9
- suffix_key_value: bfloat16 [16, 2, 64, 1024], P(('groups', 'store'), None, None, 'tensor'), parts along dimension 0, may hold values from -6 to 6
- kv_pages: bfloat16 [512, 2, 64, 1024], P(('groups', 'store'), None, None, 'tensor'), parts along dimension 0, may hold values from -6 to 6
- page_table: int32 [16, 64], P(('groups', 'store')), parts along dimension 0, may hold values from 0 to 255, as said below
- prefix_pages: int32 [16], P(('groups', 'store')), parts along dimension 0, may hold values from 1 to 64, as said below
- new_slots: int32 [16], P(('groups', 'store')), parts along dimension 0, may hold values from 0 to 31
Outputs:
- attended: bfloat16 [16, 64, 8192], P(('groups', 'store'), None, 'tensor'), parts along dimension 0
- new_store: bfloat16 [512, 2, 64, 1024], P(('groups', 'store'), None, None, 'tensor'), parts along dimension 0
There are 2 independent parts, one for each index of `groups`. A program takes and returns all parts, laid end to end along the dimension named above; each array names one. Nothing has to cross between parts.
Inputs may be any that keep to these rules, and one draw needn't show every extreme that they name: `page_table`: A page id p lives on store device p // 32. In every row each store device owns exactly 8 of the 64 entries; entries past the prefix length are valid ids that are not read; ids may repeat across requests. `prefix_pages`: some request has exactly 64 prefix pages.
All inputs are finite; a program needn't handle non-finite values.
Results may differ from a plain program's by a relative error of at most 0.0075.
Values may be sent and summed in bfloat16 or wider, within the bound.
No kernel may reach another device: no remote copies, remote signals or barrier semaphores. Data moves between devices by JAX's collectives and lax.ppermute only.
A program may use at most 64 MiB of HBM per device.

v0:
```python
import jax
import jax.numpy as jnp
from jax import lax
from jax.sharding import PartitionSpec as P

HEAD_SIZE = 128


def shifted(block, axis, distance):
    devices = range(lax.axis_size(axis))
    route = [((i - distance) % len(devices), i) for i in devices]
    return lax.ppermute(block, axis, route)


def block_update(state, head_count, key_rows, value_rows, live, scale):
    top_old, total_old, acc_old = state
    scores = (
        jnp.einsum("qhgd,khd->hgqk", head_count, key_rows, preferred_element_type=jnp.float32)
        * scale
    )
    scores = jnp.where(live, scores, -1e30)
    top_new = jnp.maximum(top_old, jnp.max(scores, axis=-1))
    weights = jnp.where(live, jnp.exp(scores - top_new[..., None]), 0.0)
    factor = jnp.exp(top_old - top_new)
    total_new = total_old * factor + jnp.sum(weights, axis=-1)
    product = jnp.einsum(
        "hgqk,khd->hgqd",
        weights.astype(jnp.bfloat16),
        value_rows,
        preferred_element_type=jnp.float32,
    )
    return (top_new, total_new, acc_old * factor[..., None] + product)


def on_device(queries, suffix_key_value, kv_pages, page_table, prefix_pages, new_slots):
    stores = lax.axis_size("store")
    pages_dev = kv_pages.shape[0]
    maxp = page_table.shape[1]
    cap = maxp // stores
    page_len = kv_pages.shape[2]
    width = kv_pages.shape[3]
    kv_heads = width // HEAD_SIZE
    suffix = queries.shape[1]
    groups_per_head = queries.shape[2] // width
    scale = HEAD_SIZE ** (-0.5)
    length = prefix_pages[0]
    table = page_table[0]
    owners = table // pages_dev
    local_ids = table % pages_dev
    entries = jnp.arange(maxp, dtype=jnp.int32)
    same_owner = (owners[:, None] == owners[None, :]) & (entries[:, None] < entries[None, :])
    ranks = jnp.sum(same_owner.astype(jnp.int32), axis=0)
    slots = owners * cap + ranks
    placed = slots[:, None] == entries[None, :]
    slot_entry = jnp.sum(jnp.where(placed, entries[:, None], 0), axis=0)
    wanted = jnp.sum(jnp.where(placed, local_ids[:, None], 0), axis=0)
    flags = (slot_entry < length).astype(jnp.int32)
    asked, asked_live = (
        lax.all_to_all(
            wanted.reshape(stores, cap), "store", split_axis=0, concat_axis=0, tiled=True
        ),
        lax.all_to_all(
            flags.reshape(stores, cap), "store", split_axis=0, concat_axis=0, tiled=True
        ),
    )
    served = kv_pages[asked.reshape(-1)].reshape(stores, cap, 2, page_len, width)
    received = lax.all_to_all(served, "store", split_axis=0, concat_axis=0, tiled=True).reshape(
        maxp, 2, page_len, width
    )
    head_count = queries[0].reshape(suffix, kv_heads, groups_per_head, HEAD_SIZE)
    own_keys = suffix_key_value[0, 0].reshape(suffix, kv_heads, HEAD_SIZE)
    own_values = suffix_key_value[0, 1].reshape(suffix, kv_heads, HEAD_SIZE)
    rows = jnp.arange(suffix, dtype=jnp.int32)
    causal = rows[None, :] <= rows[:, None]
    start_state = (
        jnp.full((kv_heads, groups_per_head, suffix), -1e30, jnp.float32),
        jnp.zeros((kv_heads, groups_per_head, suffix), jnp.float32),
        jnp.zeros((kv_heads, groups_per_head, suffix, HEAD_SIZE), jnp.float32),
    )
    state = block_update(start_state, head_count, own_keys, own_values, causal, scale)
    block_pages = min(8, maxp)
    live_pages = slot_entry < length
    trips = maxp // block_pages

    def step_block(index, carry):
        first = index * block_pages
        block = lax.dynamic_slice_in_dim(received, first, block_pages, 0)
        alive = lax.dynamic_slice_in_dim(live_pages, first, block_pages, 0)
        alive = jnp.broadcast_to(alive[:, None], (block_pages, page_len)).reshape(
            1, block_pages * page_len
        )
        block_keys = block[:, 0].reshape(block_pages * page_len, kv_heads, HEAD_SIZE)
        block_values = block[:, 1].reshape(block_pages * page_len, kv_heads, HEAD_SIZE)
        return block_update(carry, head_count, block_keys, block_values, alive, scale)

    top_final, total_final, acc_final = lax.fori_loop(0, trips, step_block, state)
    output = acc_final / total_final[..., None]
    attended = (
        output.transpose(2, 0, 1, 3)
        .reshape(1, suffix, groups_per_head * width)
        .astype(jnp.bfloat16)
    )
    arrived, arrived_slot = shifted((suffix_key_value, new_slots), "store", stores // 2)
    new_store = lax.dynamic_update_slice_in_dim(kv_pages, arrived, arrived_slot[0], 0)
    return (attended, new_store)


def solution(mesh):
    return jax.shard_map(
        on_device,
        mesh=mesh,
        in_specs=(
            P(("groups", "store"), None, "tensor"),
            P(("groups", "store"), None, None, "tensor"),
            P(("groups", "store"), None, None, "tensor"),
            P(("groups", "store"), None),
            P(("groups", "store")),
            P(("groups", "store")),
        ),
        out_specs=(
            P(("groups", "store"), None, "tensor"),
            P(("groups", "store"), None, None, "tensor"),
        ),
        check_vma=False,
    )
```

profile of v0, /device:TPU:0, one launch (start us, length us, event | category | flops | bytes accessed | tf_op | source)
XLA Modules:
  0.0 310.7 jit_solution(18011526177791281889)
XLA Ops:
  0.6 4.7 %copy.104 = bf16[32,2,64,512]{3,2,1,0:T(8,128)(2,1)} copy(bf16[32,2,64,512]{3,2,1,0:T(8,128)(2,1)} %param.10) | data formatting | bytes 8388608
  5.7 13.5 %all_to_all.14 = s32[8,1,8]{2,1,0:T(1,128)S(1)} all-to-all(s32[8,1,8]{2,1,0:T(1,128)S(1)} %bitcast.95), channel_id=1, replica_groups=mesh['groups'=2,'store'=8,'tensor'=2] {'store'}, dimensions={0} | all-to-all | bytes 512 | tf_op jit(solution)/shard_map/all_to_all | solution.py:59
  19.2 0.5 broadcast.167
  19.7 0.7 reduce.3
  20.5 7.7 %gather_fusion = bf16[64,2,64,512]{3,2,1,0:T(8,128)(2,1)} fusion(bf16[32,2,64,512]{3,2,1,0:T(8,128)(2,1)} %copy.104, s32[1024]{0:T(1024)S(1)} %pad_clamp_fusion), kind=kCustom, calls=%fused_computation | custom fusion | bytes 16777472 | tf_op jit(solution)/shard_map/gather | solution.py:66
  28.2 7.7 %copy.47 = bf16[8,8,2,64,512]{4,3,1,2,0:T(8,128)(2,1)} copy(bf16[8,8,2,64,512]{4,3,2,1,0:T(8,128)(2,1)} %bitcast.87) | data formatting | bytes 16777216 | tf_op jit(solution)/shard_map/reshape | solution.py:66
  35.9 5.1 %all-to-all-start.1 = ((bf16[8,8,2,64,512]{4,3,1,2,0:T(8,128)(2,1)}), bf16[8,8,2,64,512]{4,3,1,2,0:T(8,128)(2,1)}, u32[]{:S(2)}, u32[]{:S(2)}) async-start(bf16[8,8,2,64,512]{4,3,1,2,0:T(8,128)(2,1)} %copy.47), calls=%async_computation.1 | async-start | bytes 16777216 | tf_op jit(solution)/shard_map/all_to_all | solution.py:67
  41.0 2.8 collective-permute-start.1
  43.8 0.2 collective-permute-start
  44.8 0.2 copy.43
  45.0 0.6 fusion.35
  45.7 0.2 fusion.20
  46.0 0.5 convolution_add_fusion
  46.5 180.7 %collective-permute-done.1 = s32[1]{0:T(128)} collective-permute-done((s32[1]{0:T(128)}, s32[1]{0:T(128)}, u32[]{:S(2)}, u32[]{:S(2)}) %collective-permute-start.1) | collective-permute-done | bytes 36 | tf_op jit(solution)/shard_map/ppermute | solution.py:12
  228.9 0.7 constant_dynamic-update-slice_fusion
  229.6 7.7 %copy.48 = bf16[8,8,2,64,512]{4,3,2,1,0:T(8,128)(2,1)} copy(bf16[8,8,2,64,512]{4,3,1,2,0:T(8,128)(2,1)} %all-to-all-done.1) | data formatting | bytes 16777216 | tf_op jit(solution)/shard_map/all_to_all | solution.py:67
  237.3 71.7 %while.17 = (s32[]{:T(128)}, f32[4,8,64]{2,1,0:T(8,128)S(1)}, f32[4,8,64]{2,1,0:T(8,128)S(1)}, f32[4,8,64,128]{3,2,1,0:T(8,128)S(1)}, pred[64]{0:T(512)(128)(4,1...) while((s32[]{:T(128)}, f32[4,8,64]{2,1,0:T(8,128)S(1)}, ...), condition=%wide.region_8.9_spmd, body=%wide.region_5.8_spmd.sunk | while | flops 551030784 | bytes 37358832 | solution.py:96
  237.5 1.3 dynamic-slice_bitcast_fusion.3
  238.8 0.1 squeeze.28
  239.0 0.8 bitcast_reduce_fusion.2
  239.8 1.9 copy-done
  241.7 1.2 fusion.45
  243.1 3.1 fusion.46
  246.5 1.3 dynamic-slice_bitcast_fusion.3
  247.8 0.1 squeeze.28
  247.9 0.8 bitcast_reduce_fusion.2
  248.8 1.9 copy-done
  250.7 1.2 fusion.45
  252.1 3.1 fusion.46
  255.4 1.3 dynamic-slice_bitcast_fusion.3
  256.7 0.1 squeeze.28
  256.9 0.8 bitcast_reduce_fusion.2
  257.7 1.9 copy-done
  259.6 1.2 fusion.45
  261.0 3.1 fusion.46
  264.4 1.3 dynamic-slice_bitcast_fusion.3
  265.7 0.1 squeeze.28
  265.8 0.8 bitcast_reduce_fusion.2
  266.7 1.9 copy-done
  268.6 1.2 fusion.45
  270.0 3.1 fusion.46
  273.4 1.3 dynamic-slice_bitcast_fusion.3
  274.8 0.8 bitcast_reduce_fusion.2
  275.6 1.9 copy-done
  277.5 1.2 fusion.45
  278.9 3.1 fusion.46
  282.3 1.3 dynamic-slice_bitcast_fusion.3
  283.8 0.8 bitcast_reduce_fusion.2
  284.6 1.9 copy-done
  286.5 1.2 fusion.45
  287.9 3.1 fusion.46
  291.3 1.3 dynamic-slice_bitcast_fusion.3
  292.7 0.8 bitcast_reduce_fusion.2
  293.6 1.9 copy-done
  295.5 1.2 fusion.45
  296.9 3.1 fusion.46
  300.2 1.3 dynamic-slice_bitcast_fusion.3
  301.7 0.8 bitcast_reduce_fusion.2
  302.5 1.9 copy-done
  304.4 1.2 fusion.45
  305.8 3.1 fusion.46
  309.0 0.3 fusion.24
  309.3 0.3 copy.51
  309.7 1.0 convert_element_type.34
  (93 shorter events, 4.2 us)
Async XLA Ops:
  0.6 4.7 %copy-start.3 = (s32[1,64]{1,0:T(1,128)S(1)}, s32[1,64]{1,0:T(1,128)}, u32[]{:S(2)}) copy-start(s32[1,64]{1,0:T(1,128)} %param.11) | copy-start | bytes 772
  35.9 7.9 %copy-start.2 = (bf16[1,2,64,512]{3,2,1,0:T(8,128)(2,1)S(1)}, bf16[1,2,64,512]{3,2,1,0:T(8,128)(2,1)}, u32[]{:S(2)}) copy-start(bf16[1,2,64,512]{3,2,1,0:T(8,128)(2,1)} %param.9) | copy-start | bytes 393220
  35.9 8.1 %copy-start.1 = (bf16[1,64,4096]{2,1,0:T(8,128)(2,1)S(1)}, bf16[1,64,4096]{2,1,0:T(8,128)(2,1)}, u32[]{:S(2)}) copy-start(bf16[1,64,4096]{2,1,0:T(8,128)(2,1)} %param.8) | copy-start | bytes 1572868
  35.9 193.7 %all-to-all-start.1 = ((bf16[8,8,2,64,512]{4,3,1,2,0:T(8,128)(2,1)}), bf16[8,8,2,64,512]{4,3,1,2,0:T(8,128)(2,1)}, u32[]{:S(2)}, u32[]{:S(2)}) async-start(bf16[8,8,2,64,512]{4,3,1,2,0:T(8,128)(2,1)} %copy.47), calls=%async_computation.1 | async-start | bytes 16777216 | tf_op jit(solution)/shard_map/all_to_all | solution.py:67
  41.0 186.2 %collective-permute-start.1 = (s32[1]{0:T(128)}, s32[1]{0:T(128)}, u32[]{:S(2)}, u32[]{:S(2)}) collective-permute-start(s32[1]{0:T(128)} %param.13), channel_id=1, source_target_pairs={{8,0},{10,2},{12,4},{14,6},{0,8},{2,10},{4,12},{6,14},{9,1},{11,3}... | collective-permute-start | bytes 20 | tf_op jit(solution)/shard_map/ppermute | solution.py:12
  43.8 185.1 %collective-permute-start = (bf16[1,2,64,512]{3,2,1,0:T(8,128)(2,1)S(1)}, bf16[1,2,64,512]{3,2,1,0:T(8,128)(2,1)S(1)}, u32[]{:S(2)}, u32[]{:S(2)}) collective-permute-start(bf16[1,2,64,512]{3,2,1,0:T(8,128)(2,1)S(1)} %copy-done.2), channel_id=1, source_target_pairs={{8,0},{10,2},{12,4},{14,6},{0,8},{2,10},{4,12},{6,14},{9,1},{11,3}... | collective-permute-start | bytes 393224 | tf_op jit(solution)/shard_map/ppermute | solution.py:12
  239.8 1.9 copy-start
  248.7 1.9 copy-start
  257.7 1.9 copy-start
  266.7 1.9 copy-start
  275.6 1.9 copy-start
  284.6 1.9 copy-start
  293.5 1.9 copy-start
  302.5 1.9 copy-start
where the time goes:
time: 311 us
  waiting for transfers between devices  181 us (58%)
  local copies, waits for them, and re-layouts  60.4 us (19%)
  matrix products  32.5 us (10%)
  blocking collectives  13.5 us (4%)
  other arithmetic  11.6 us (4%)
  starting transfers between devices  8.08 us (3%)
  between operations  3.13 us (1%)
    ppermute x2, waiting for transfers between devices, shifted(): return lax.ppermute(block, axis, route)  181 us
    while x32, local copies, waits for them, and re-layouts  25.6 us
    dot_general x9, matrix products, block_update(): jnp.einsum('hgqk,khd->hgqd', weights.astype(jnp.bfloat16), value_rows, pr...  25.3 us
    all_to_all x1, blocking collectives, on_device(): lax.all_to_all(wanted.reshape(stores, cap), 'store', split_axis=0, concat...  13.5 us
    reduce_sum x9, other arithmetic, block_update(): total_new = total_old * factor + jnp.sum(weights, axis=-1)  10.2 us
    gather x1, local copies, waits for them, and re-layouts, on_device(): kv_pages[asked.reshape(-1)].reshape(stores, cap, 2, page_len, width)  7.71 us
    all_to_all x1, local copies, waits for them, and re-layouts, on_device(): lax.all_to_all(served, 'store', split_axis=0, concat_axis=0, tiled=True)  7.71 us
    reshape x1, local copies, waits for them, and re-layouts, on_device(): kv_pages[asked.reshape(-1)].reshape(stores, cap, 2, page_len, width)  7.71 us
  transfers between devices with their start and end apart: 3, of which 1 were waited for; matrix products, arithmetic and copies ran while one was open for 1% of the time, Pallas kernels for 0%

commit v1 on v0

--- a/solution.py
+++ b/solution.py
@@ -1,9 +1,20 @@
+import functools
+
 import jax
 import jax.numpy as jnp
 from jax import lax
+from jax.experimental import pallas as pl
+from jax.experimental.pallas import tpu as pltpu
 from jax.sharding import PartitionSpec as P
 
 HEAD_SIZE = 128
+LOG2E = 1.4426950408889634
+DEAD = -1e30
+FLOOR = -1e29
+STAT_ROWS = 16
+VMEM = pl.BlockSpec(memory_space=pltpu.VMEM)
+SMEM = pl.BlockSpec(memory_space=pltpu.SMEM)
+HBM = pl.BlockSpec(memory_space=pl.ANY)
 
 
 def shifted(block, axis, distance):
@@ -32,7 +43,7 @@
     return (top_new, total_new, acc_old * factor[..., None] + product)
 
 
-def on_device(queries, suffix_key_value, kv_pages, page_table, prefix_pages, new_slots):
+def pages_travel(queries, suffix_key_value, kv_pages, page_table, prefix_pages, new_slots):
     stores = lax.axis_size("store")
     pages_dev = kv_pages.shape[0]
     maxp = page_table.shape[1]
@@ -54,14 +65,8 @@
     placed = slots[:, None] == entries[None, :]
     slot_entry = jnp.sum(jnp.where(placed, entries[:, None], 0), axis=0)
     wanted = jnp.sum(jnp.where(placed, local_ids[:, None], 0), axis=0)
-    flags = (slot_entry < length).astype(jnp.int32)
-    asked, asked_live = (
-        lax.all_to_all(
-            wanted.reshape(stores, cap), "store", split_axis=0, concat_axis=0, tiled=True
-        ),
-        lax.all_to_all(
-            flags.reshape(stores, cap), "store", split_axis=0, concat_axis=0, tiled=True
-        ),
+    asked = lax.all_to_all(
+        wanted.reshape(stores, cap), "store", split_axis=0, concat_axis=0, tiled=True
     )
     served = kv_pages[asked.reshape(-1)].reshape(stores, cap, 2, page_len, width)
     received = lax.all_to_all(served, "store", split_axis=0, concat_axis=0, tiled=True).reshape(
@@ -103,6 +108,322 @@
     arrived, arrived_slot = shifted((suffix_key_value, new_slots), "store", stores // 2)
     new_store = lax.dynamic_update_slice_in_dim(kv_pages, arrived, arrived_slot[0], 0)
     return (attended, new_store)
+
+
+def dot_nt(a, b):
+    return lax.dot_general(a, b, (((1,), (1,)), ((), ())), preferred_element_type=jnp.float32)
+
+
+def iota(shape, dim):
+    return lax.broadcasted_iota(jnp.int32, shape, dim)
+
+
+def pack_stats(top, total):
+    lane = iota((HEAD_SIZE, HEAD_SIZE), 1)
+    row = iota((STAT_ROWS, HEAD_SIZE), 0)
+    col = iota((STAT_ROWS, HEAD_SIZE), 1)
+    tile = jnp.zeros((STAT_ROWS, HEAD_SIZE), jnp.float32)
+    for j, (m, l) in enumerate(zip(top, total)):
+        high = l.astype(jnp.bfloat16).astype(jnp.float32)
+        low = l - high
+        mixed = jnp.where(lane == 0, m, jnp.where(lane == 1, high, low)).astype(jnp.bfloat16)
+        pick = ((row == col * 4 + j) & (col < 3)).astype(jnp.float32).astype(jnp.bfloat16)
+        tile = tile + dot_nt(pick, mixed)
+    return tile.astype(jnp.bfloat16)
+
+
+def unpack_stats(tile):
+    row = iota((STAT_ROWS, 8 * HEAD_SIZE), 0)
+    block = iota((STAT_ROWS, 8 * HEAD_SIZE), 1) // HEAD_SIZE
+    j = block // 2
+    stat = block % 2
+    spread = (
+        ((row == j) & (stat == 0)) | ((row == j + 4) & (stat == 1)) | ((row == j + 8) & (stat == 1))
+    )
+    spread = spread.astype(jnp.float32).astype(jnp.bfloat16)
+    turned = tile.astype(jnp.float32).T.astype(jnp.bfloat16)
+    wide = jnp.dot(turned, spread, preferred_element_type=jnp.float32)
+    part = lambda b: wide[:, b * HEAD_SIZE:(b + 1) * HEAD_SIZE]
+    return [part(2 * j) for j in range(4)], [part(2 * j + 1) for j in range(4)]
+
+
+def partial_rows(q, k, v, live, own, factor):
+    s = dot_nt(q, k)
+    s = jnp.where(live, s, DEAD)
+    top = jnp.max(s, axis=-1, keepdims=True)
+    if own is not None:
+        k_own, v_own, causal = own
+        s_own = jnp.where(causal, dot_nt(q, k_own), DEAD)
+        top = jnp.maximum(top, jnp.max(s_own, axis=-1, keepdims=True))
+    top = jnp.maximum(top * factor, FLOOR).astype(jnp.bfloat16).astype(jnp.float32)
+    p = jnp.exp2(s * factor - top).astype(jnp.bfloat16)
+    ones = jnp.ones((k.shape[0], HEAD_SIZE), jnp.bfloat16)
+    out = jnp.dot(p, jnp.concatenate([v, ones], 1), preferred_element_type=jnp.float32)
+    if own is not None:
+        p = jnp.exp2(s_own * factor - top).astype(jnp.bfloat16)
+        ones = jnp.ones((k_own.shape[0], HEAD_SIZE), jnp.bfloat16)
+        out = out + jnp.dot(p, jnp.concatenate([v_own, ones], 1), preferred_element_type=jnp.float32)
+    top = jnp.broadcast_to(top, (q.shape[0], HEAD_SIZE))
+    return out[:, :HEAD_SIZE], top, out[:, HEAD_SIZE:]
+
+
+def attend_kernel(sizes, parts, own, wire, *refs):
+    kv_heads, groups, suffix, cap, page_len = sizes
+    refs = list(refs)
+    meta = refs.pop(0)
+    queries = [[refs.pop(0) for _ in range(n)] for n in parts]
+    own_kv = refs.pop(0) if own else None
+    pages = refs.pop(0)
+    outs = [(refs.pop(0), refs.pop(0)) for _ in parts]
+    held, sems = refs
+    copies = [
+        [
+            pltpu.make_async_copy(pages.at[meta[n, c]], held.at[n, c], sems.at[n, c])
+            for c in range(cap)
+        ]
+        for n in range(len(parts))
+    ]
+    for request in copies:
+        for copy in request:
+            copy.start()
+    factor = HEAD_SIZE ** (-0.5) * LOG2E
+    keys = cap * page_len
+    for n, halves in enumerate(queries):
+        for copy in copies[n]:
+            copy.wait()
+        live = iota((1, keys), 1) < meta[n, cap] * page_len
+        heads_each = kv_heads // len(halves)
+        acc_ref, stat_ref = outs[n]
+        for h in range(kv_heads):
+            q_ref = halves[h // heads_each]
+            first = (h % heads_each) * groups
+            lanes = slice(h * HEAD_SIZE, (h + 1) * HEAD_SIZE)
+            k = held[n, :, 0, :, lanes].reshape(keys, HEAD_SIZE)
+            v = held[n, :, 1, :, lanes].reshape(keys, HEAD_SIZE)
+            tops, totals = [], []
+            rows = groups * suffix
+            per_block = HEAD_SIZE // suffix
+            for j in range(rows // HEAD_SIZE):
+                q = jnp.concatenate(
+                    [
+                        q_ref[:, (first + g) * HEAD_SIZE:(first + g + 1) * HEAD_SIZE]
+                        for g in range(j * per_block, (j + 1) * per_block)
+                    ],
+                    0,
+                )
+                extra = None
+                if own:
+                    at = iota((HEAD_SIZE, suffix), 0) % suffix
+                    extra = (own_kv[0, :, lanes], own_kv[1, :, lanes], iota((HEAD_SIZE, suffix), 1) <= at)
+                acc, top, total = partial_rows(q, k, v, live, extra, factor)
+                acc_ref[h, j * HEAD_SIZE:(j + 1) * HEAD_SIZE, :] = acc.astype(acc_ref.dtype)
+                tops.append(top)
+                totals.append(total)
+            tile = pack_stats(tops, totals)
+            if wire:
+                stat_ref[h] = tile
+            else:
+                stat_ref[h] = tile
+
+
+def attend(sizes, meta, queries, own_kv, kv_pages, wire=False):
+    kv_heads, groups, suffix, cap, page_len = sizes
+    parts = [len(q) for q in queries]
+    flat = [x for q in queries for x in q]
+    own = own_kv is not None
+    shapes = []
+    rows = groups * suffix
+    for _ in parts:
+        shapes.append(jax.ShapeDtypeStruct((kv_heads, rows, HEAD_SIZE), jnp.float32))
+        shapes.append(jax.ShapeDtypeStruct((kv_heads, STAT_ROWS, HEAD_SIZE), jnp.bfloat16))
+    keys = cap * page_len
+    count = len(parts)
+    out = pl.pallas_call(
+        functools.partial(attend_kernel, sizes, parts, own, wire),
+        out_shape=shapes,
+        in_specs=[SMEM] + [VMEM] * (len(flat) + own) + [HBM],
+        out_specs=[VMEM] * len(shapes),
+        scratch_shapes=[
+            pltpu.VMEM((count, cap) + kv_pages.shape[1:], jnp.bfloat16),
+            pltpu.SemaphoreType.DMA((count, cap)),
+        ],
+        compiler_params=pltpu.CompilerParams(vmem_limit_bytes=48 * 1024 * 1024),
+        cost_estimate=pl.CostEstimate(
+            flops=count * kv_heads * rows * keys * HEAD_SIZE * 8,
+            bytes_accessed=count * kv_heads * (rows * 6 + keys * 4) * HEAD_SIZE,
+            transcendentals=count * kv_heads * rows * keys,
+        ),
+    )(meta, *flat, *([own_kv] if own else []), kv_pages)
+    return [(out[2 * n], out[2 * n + 1]) for n in range(count)]
+
+
+def blend(parts):
+    top = functools.reduce(jnp.maximum, [m for _, m, _ in parts])
+    scales = [jnp.exp2(m - top) for _, m, _ in parts]
+    acc = sum(a * f for (a, _, _), f in zip(parts, scales))
+    total = sum(l * f for (_, _, l), f in zip(parts, scales))
+    return acc, top, total
+
+
+def block_of(j):
+    return slice(j * HEAD_SIZE, (j + 1) * HEAD_SIZE)
+
+
+def pack_kernel(first, heads, acc_ref, stat_ref, out_ref):
+    rows = acc_ref.shape[1]
+    for h in range(heads):
+        out_ref[h, :rows, :] = acc_ref[first + h].astype(jnp.bfloat16)
+        out_ref[h, rows:, :] = stat_ref[first + h]
+
+
+def merge_kernel(first, heads, in_ref, acc_ref, stat_ref, out_ref):
+    rows = acc_ref.shape[1]
+    for h in range(heads):
+        in_top, in_total = unpack_stats(in_ref[h, rows:, :])
+        my_top, my_total = unpack_stats(stat_ref[first + h])
+        tops, totals = [], []
+        for j in range(rows // HEAD_SIZE):
+            acc, top, total = blend(
+                [
+                    (in_ref[h, block_of(j), :].astype(jnp.float32), in_top[j], in_total[j]),
+                    (acc_ref[first + h, block_of(j), :], my_top[j], my_total[j]),
+                ]
+            )
+            out_ref[h, block_of(j), :] = acc.astype(jnp.bfloat16)
+            tops.append(top)
+            totals.append(total)
+        out_ref[h, rows:, :] = pack_stats(tops, totals)
+
+
+def final_kernel(heads_each, suffix, *refs):
+    arrivals, (acc_ref, stat_ref, out_ref) = refs[:-3], refs[-3:]
+    kv_heads, rows = acc_ref.shape[:2]
+    groups = rows // suffix
+    for h in range(kv_heads):
+        here = arrivals[h // heads_each::kv_heads // heads_each]
+        stats = [unpack_stats(ref[h % heads_each, rows:, :]) for ref in here]
+        stats.append(unpack_stats(stat_ref[h]))
+        for j in range(rows // HEAD_SIZE):
+            blocks = [ref[h % heads_each, block_of(j), :].astype(jnp.float32) for ref in here]
+            blocks.append(acc_ref[h, block_of(j), :])
+            acc, _, total = blend([(a, t[j], l[j]) for a, (t, l) in zip(blocks, stats)])
+            out = (acc / total).astype(jnp.bfloat16)
+            for i in range(HEAD_SIZE // suffix):
+                g = h * groups + j * (HEAD_SIZE // suffix) + i
+                out_ref[0, :, block_of(g)] = out[i * suffix:(i + 1) * suffix]
+
+
+def call(kernel, shape, *args):
+    size = sum(a.size * a.dtype.itemsize for a in args)
+    return pl.pallas_call(
+        kernel,
+        out_shape=shape,
+        in_specs=[VMEM] * len(args),
+        out_specs=VMEM,
+        compiler_params=pltpu.CompilerParams(vmem_limit_bytes=48 * 1024 * 1024),
+        cost_estimate=pl.CostEstimate(flops=size, bytes_accessed=2 * size, transcendentals=size // 8),
+    )(*args)
+
+
+def queries_travel(queries, suffix_key_value, kv_pages, page_table, prefix_pages, new_slots):
+    stores = lax.axis_size("store")
+    pages_dev, _, page_len, width = kv_pages.shape
+    maxp = page_table.shape[1]
+    cap = maxp // stores
+    kv_heads = width // HEAD_SIZE
+    suffix = queries.shape[1]
+    groups = queries.shape[2] // width
+    sizes = (kv_heads, groups, suffix, cap, page_len)
+    half = stores // 2
+    me = lax.axis_index("store")
+
+    order = list(range(0, stores, 2)) + list(range(1, stores, 2))[::-1]
+    up = [(order[i], order[(i + 1) % stores]) for i in range(stores)]
+    down = [(order[i], order[i - 1]) for i in range(stores)]
+    place = [order.index(i) for i in range(stores)]
+    my_place = jnp.asarray(place, jnp.int32)[me]
+    order_now = jnp.asarray(order, jnp.int32)
+
+    mine_row = jnp.concatenate([page_table, prefix_pages[:, None]], 1)
+    rows = lax.all_gather(mine_row, "store", axis=0, tiled=True)
+
+    def listing(rows):
+        table, length = rows[:, :maxp], rows[:, maxp:]
+        entries = jnp.arange(maxp, dtype=jnp.int32)
+        held = table // pages_dev == me
+        before = entries[:, None] < entries[None, :]
+        rank = jnp.sum((held[:, :, None] & before[None]).astype(jnp.int32), 1)
+        placed = held[:, :, None] & (rank[:, :, None] == jnp.arange(cap, dtype=jnp.int32))
+        ids = jnp.sum(jnp.where(placed, (table % pages_dev)[:, :, None], 0), 1)
+        live = jnp.sum((held & (entries[None] < length)).astype(jnp.int32), 1, keepdims=True)
+        return jnp.concatenate([ids, live], 1)
+
+    lists = listing(rows)
+
+    def listed(*distances):
+        which = [order_now[(my_place - d) % stores] for d in distances]
+        return jnp.stack([lists[w] for w in which])
+
+    heads_each = kv_heads // 2
+    cut = heads_each * groups * HEAD_SIZE
+    mine = [queries[0, :, :cut], queries[0, :, cut:]]
+    ups, downs = list(mine), list(mine)
+    partials = {}
+    partials[0], = attend(sizes, listing(mine_row), [[queries[0]]], suffix_key_value[0], kv_pages)
+    for step in range(1, half):
+        ups = [lax.ppermute(x, "store", up) for x in ups]
+        downs = [lax.ppermute(x, "store", down) for x in downs]
+        got = attend(sizes, listed(step, -step), [ups, downs], None, kv_pages)
+        partials[step], partials[-step] = got
+    ups[0] = lax.ppermute(ups[0], "store", up)
+    downs[1] = lax.ppermute(downs[1], "store", down)
+    (far,) = attend(sizes, listed(half), [[ups[0], downs[1]]], None, kv_pages)
+
+    rows_head = groups * suffix
+    wire = jax.ShapeDtypeStruct((heads_each, rows_head + STAT_ROWS, HEAD_SIZE), jnp.bfloat16)
+
+    def packed(part, side):
+        return call(functools.partial(pack_kernel, side * heads_each, heads_each), wire, *part)
+
+    def merged(block, part, side):
+        return call(
+            functools.partial(merge_kernel, side * heads_each, heads_each), wire, block, *part
+        )
+
+    flows = {}
+    for side in range(2):
+        for sign, route in ((1, down), (-1, up)):
+            if (side == 0) == (sign == 1):
+                block = packed(far, side)
+                distance = half
+            else:
+                block = packed(partials[sign * (half - 1)], side)
+                distance = half - 1
+            while True:
+                block = lax.ppermute(block, "store", route)
+                distance -= 1
+                if distance == 0:
+                    break
+                block = merged(block, partials[sign * distance], side)
+            flows[sign, side] = block
+    attended = call(
+        functools.partial(final_kernel, heads_each, suffix),
+        jax.ShapeDtypeStruct(queries.shape, queries.dtype),
+        flows[1, 0], flows[1, 1], flows[-1, 0], flows[-1, 1], *partials[0],
+    )
+    arrived, arrived_slot = shifted((suffix_key_value, new_slots), "store", stores // 2)
+    new_store = lax.dynamic_update_slice_in_dim(kv_pages, arrived, arrived_slot[0], 0)
+    return (attended, new_store)
+
+
+def on_device(queries, suffix_key_value, kv_pages, page_table, prefix_pages, new_slots):
+    stores = lax.axis_size("store")
+    pulled = page_table.shape[1] // stores * kv_pages[0].size
+    pushed = 2 * queries[0].size
+    arrays = (queries, suffix_key_value, kv_pages, page_table, prefix_pages, new_slots)
+    if pulled >= pushed and stores % 2 == 0:
+        return queries_travel(*arrays)
+    return pages_travel(*arrays)
 
 
 def solution(mesh):

time: 311 us -> 143 us (0.46)
  waiting for transfers between devices: 181 us -> 10.3 us
  local copies, waits for them, and re-layouts: 60.4 us -> 10.1 us
  Pallas kernels: 0 us -> 44.6 us
  matrix products: 32.5 us -> 0 us
  starting transfers between devices: 8.08 us -> 33.5 us
  between operations: 3.13 us -> 21.1 us
  other arithmetic: 11.6 us -> 2.34 us
  blocking collectives: 13.5 us -> 20.5 us
    ppermute x2, waiting for transfers between devices: 181 us -> 0.01 us  [shifted(): return lax.ppermute(block, axis, route)]
    pallas_call x0 -> x20, Pallas kernels: none -> 44.6 us  [the longest x5 33 us: attend(): pl.pallas_call(functools.partial(attend_kernel, sizes, parts, own, wire),...]
    dot_general x18 -> x0, matrix products: 32.5 us -> none  [the longest x9 25.3 us: block_update(): jnp.einsum('hgqk,khd->hgqd', weights.astype(jnp.bfloat16), value_rows, pr...]
    ppermute x0 -> x28, starting transfers between devices: none -> 30.4 us  [the longest x14 15 us: queries_travel(): block = lax.ppermute(block, 'store', route)]
    while x32 -> x0, local copies, waits for them, and re-layouts: 25.6 us -> none
    all_gather x0 -> x1, blocking collectives: none -> 20.5 us  [queries_travel(): rows = lax.all_gather(mine_row, 'store', axis=0, tiled=True)]
    all_to_all x1 -> x0, blocking collectives: 13.5 us -> none  [on_device(): lax.all_to_all(wanted.reshape(stores, cap), 'store', split_axis=0, concat...]
    ppermute x0 -> x28, waiting for transfers between devices: none -> 10.3 us  [the longest x6 10.1 us: queries_travel(): ups = [lax.ppermute(x, 'store', up) for x in ups]]
  transfers between devices with their start and end apart: 3 -> 30, of which waited for: 1 -> 4; matrix products, arithmetic and copies ran while one was open for 1% -> 4% of each run, Pallas kernels for 0% -> 29%
where the time goes in v1:
time: 143 us; the launch traced here: 142 us
  Pallas kernels  44.6 us (31%)
  starting transfers between devices  33.5 us (23%)
  between operations  21.1 us (15%)
  blocking collectives  20.5 us (14%)
  waiting for transfers between devices  10.3 us (7%)
  local copies, waits for them, and re-layouts  10.1 us (7%)
  other arithmetic  2.34 us (2%)
    pallas_call x5, Pallas kernels, attend(): pl.pallas_call(functools.partial(attend_kernel, sizes, parts, own, wire),...  33 us
    all_gather x1, blocking collectives, queries_travel(): rows = lax.all_gather(mine_row, 'store', axis=0, tiled=True)  20.5 us
    ppermute x14, starting transfers between devices, queries_travel(): block = lax.ppermute(block, 'store', route)  15 us
    pallas_call x15, Pallas kernels, call(): pl.pallas_call(kernel, out_shape=shape, in_specs=[VMEM] * len(args), out_...  11.6 us
    ppermute x6, starting transfers between devices, queries_travel(): downs = [lax.ppermute(x, 'store', down) for x in downs]  11.1 us
    ppermute x6, waiting for transfers between devices, queries_travel(): ups = [lax.ppermute(x, 'store', up) for x in ups]  10.1 us
    unnamed x13, local copies, waits for them, and re-layouts  6.97 us
    ppermute x2, starting transfers between devices, shifted(): return lax.ppermute(block, axis, route)  3.05 us
  transfers between devices with their start and end apart: 30, of which 4 were waited for; matrix products, arithmetic and copies ran while one was open for 4% of the time, Pallas kernels for 29%

profile of v1, /device:TPU:0, one launch (start us, length us, event | category | flops | bytes accessed | tf_op | source)
XLA Modules:
  0.0 142.4 jit_solution(9562895579564625503)
XLA Ops:
  0.7 4.8 %copy.17.refs_3_.refs_5_ = bf16[32,2,64,512]{3,2,1,0:T(8,128)(2,1)} copy(bf16[32,2,64,512]{3,2,1,0:T(8,128)(2,1)} %param.10) | data formatting | bytes 8388608
  5.5 3.0 %collective-permute-start.4 = (bf16[64,2048]{1,0:T(8,128)(2,1)S(1)}, bf16[64,2048]{1,0:T(8,128)(2,1)S(1)}, u32[]{:S(2)}, u32[]{:S(2)}) collective-permute-start(bf16[64,2048]{1,0:T(8,128)(2,1)S(1)} %get-tuple-element.40), channel_id=1, source_target_pairs={{0,2},{4,0},{8,4},{12,8},{14,12},{10,14},{6,10},{2,6},{1,3},{5,1},... | collective-permute-start | bytes 786440 | tf_op jit(solution)/shard_map/ppermute | solution.py:375
  8.5 0.1 collective-permute-start.9
  8.6 2.0 %collective-permute-start = (bf16[64,2048]{1,0:T(8,128)(2,1)S(1)}, bf16[64,2048]{1,0:T(8,128)(2,1)S(1)}, u32[]{:S(2)}, u32[]{:S(2)}) collective-permute-start(bf16[64,2048]{1,0:T(8,128)(2,1)S(1)} %get-tuple-element.41), channel_id=1, source_target_pairs={{0,4},{4,8},{8,12},{12,14},{14,10},{10,6},{6,2},{2,0},{1,5},{5,9},... | collective-permute-start | bytes 786440 | tf_op jit(solution)/shard_map/ppermute | solution.py:374
  10.6 0.1 collective-permute-start.12
  10.7 3.0 %collective-permute-start.29 = (s32[1]{0:T(128)}, s32[1]{0:T(128)}, u32[]{:S(2)}, u32[]{:S(2)}) collective-permute-start(s32[1]{0:T(128)} %param.13), channel_id=1, source_target_pairs={{8,0},{10,2},{12,4},{14,6},{0,8},{2,10},{4,12},{6,14},{9,1},{11,3}... | collective-permute-start | bytes 20 | tf_op jit(solution)/shard_map/ppermute | solution.py:23
  14.3 0.1 add_bitcast_fusion
  14.4 20.5 %all-gather = s32[8,1,65]{2,1,0:T(1,128)S(1)} all-gather(s32[1,1,65]{2,1,0:T(1,128)S(1)} %add_bitcast_fusion), channel_id=1, replica_groups=mesh['groups'=2,'store'=8,'tensor'=2] {'store'}, dimensions={0}, use_global_device_ids=true | all-gather | bytes 2340 | tf_op jit(solution)/shard_map/all_gather | solution.py:348
  34.9 0.2 slice_reduce_fusion
  35.1 0.2 convert_reduce_fusion.2
  35.3 2.0 %collective-permute-start.5 = (bf16[64,2048]{1,0:T(8,128)(2,1)S(1)}, bf16[64,2048]{1,0:T(8,128)(2,1)S(1)}, u32[]{:S(2)}, u32[]{:S(2)}) collective-permute-start(bf16[64,2048]{1,0:T(8,128)(2,1)S(1)} %collective-permute-done.4.refs_4_), channel_id=1, source_target_pairs={{0,2},{4,0},{8,4},{12,8},{14,12},{10,14},{6,10},{2,6},{1,3},{5,1},... | collective-permute-start | bytes 786440 | tf_op jit(solution)/shard_map/ppermute | solution.py:375
  37.4 0.1 convert_reduce_fusion
  37.5 6.8 %collective-permute-done.1.refs_1_ = bf16[64,2048]{1,0:T(8,128)(2,1)S(1)} collective-permute-done((bf16[64,2048]{1,0:T(8,128)(2,1)S(1)}, bf16[64,2048]{1,0:T(8,128)(2,1)S(1)}, u32[]{:S(2)}, u32[]{:S(2)}) %collective-permute-start.1) | collective-permute-done | bytes 262176 | tf_op jit(solution)/shard_map/ppermute | solution.py:374
  44.3 0.1 collective-permute-done.5.refs_4_
  44.4 2.1 %collective-permute-start.6 = (bf16[64,2048]{1,0:T(8,128)(2,1)S(1)}, bf16[64,2048]{1,0:T(8,128)(2,1)}, u32[]{:S(2)}, u32[]{:S(2)}) collective-permute-start(bf16[64,2048]{1,0:T(8,128)(2,1)S(1)} %collective-permute-done.5.refs_4_), channel_id=1, source_target_pairs={{0,2},{4,0},{8,4},{12,8},{14,12},{10,14},{6,10},{2,6},{1,3},{5,1},... | collective-permute-start | bytes 786440 | tf_op jit(solution)/shard_map/ppermute | solution.py:375
  46.5 0.2 select_reduce_fusion
  46.7 0.1 convert_reduce_fusion.1
  46.9 2.0 %collective-permute-start.13 = (bf16[64,2048]{1,0:T(8,128)(2,1)S(1)}, bf16[64,2048]{1,0:T(8,128)(2,1)S(1)}, u32[]{:S(2)}, u32[]{:S(2)}) collective-permute-start(bf16[64,2048]{1,0:T(8,128)(2,1)S(1)} %collective-permute-done.12.refs_3_), channel_id=1, source_target_pairs={{0,2},{4,0},{8,4},{12,8},{14,12},{10,14},{6,10},{2,6},{1,3},{5,1},... | collective-permute-start | bytes 786440 | tf_op jit(solution)/shard_map/ppermute | solution.py:375
  48.9 0.7 fusion.8
  49.6 0.1 copy.13
  49.7 3.2 %collective-permute-done.2.refs_1_ = bf16[64,2048]{1,0:T(8,128)(2,1)S(1)} collective-permute-done((bf16[64,2048]{1,0:T(8,128)(2,1)S(1)}, bf16[64,2048]{1,0:T(8,128)(2,1)S(1)}, u32[]{:S(2)}, u32[]{:S(2)}) %collective-permute-start.2) | collective-permute-done | bytes 262176 | tf_op jit(solution)/shard_map/ppermute | solution.py:374
  52.9 0.1 collective-permute-start.3
  53.0 0.1 collective-permute-done.6.refs_4_
  53.1 1.8 %collective-permute-start.7 = (bf16[64,2048]{1,0:T(8,128)(2,1)}, bf16[64,2048]{1,0:T(8,128)(2,1)S(1)}, u32[]{:S(2)}, u32[]{:S(2)}) collective-permute-start(bf16[64,2048]{1,0:T(8,128)(2,1)} %collective-permute-done.6.refs_4_), channel_id=1, source_target_pairs={{0,2},{4,0},{8,4},{12,8},{14,12},{10,14},{6,10},{2,6},{1,3},{5,1},... | collective-permute-start | bytes 786440 | tf_op jit(solution)/shard_map/ppermute | solution.py:379
  54.9 0.1 pad_add_fusion
  55.0 0.6 dynamic_slice.45
  60.3 0.7 fusion.10
  73.9 0.1 select_reduce_fusion.1
  74.0 0.2 collective-permute-start.11
  74.3 1.8 %collective-permute-start.14 = (bf16[64,2048]{1,0:T(8,128)(2,1)S(1)}, bf16[64,2048]{1,0:T(8,128)(2,1)S(1)}, u32[]{:S(2)}, u32[]{:S(2)}) collective-permute-start(bf16[64,2048]{1,0:T(8,128)(2,1)S(1)} %collective-permute-done.13.refs_3_), channel_id=1, source_target_pairs={{0,2},{4,0},{8,4},{12,8},{14,12},{10,14},{6,10},{2,6},{1,3},{5,1},... | collective-permute-start | bytes 786440 | tf_op jit(solution)/shard_map/ppermute | solution.py:375
  76.2 2.2 %copy-done = bf16[32,2,64,512]{3,2,1,0:T(8,128)(2,1)S(1)} copy-done((bf16[32,2,64,512]{3,2,1,0:T(8,128)(2,1)S(1)}, bf16[32,2,64,512]{3,2,1,0:T(8,128)(2,1)}, u32[]{:S(2)}) %copy-start) | copy-done | bytes 4194328
  78.4 4.6 %shard_map.95 = (f32[4,512,128]{2,1,0:T(8,128)S(1)}, bf16[4,16,128]{2,1,0:T(8,128)(2,1)S(1)}) custom-call(s32[1,9]{1,0:T(1,128)S(1)} %get-tuple-element.48.refs_0_, bf16[64,2048]{1,0:T(8,128)(2,1)S(1)} %collective-permute-done.3.refs_1_, bf16[64,2048]{1,0:T(8,128)(2,1)S(1)} %collective-permute-done.7.refs_2_, bf16[32,2,64,512]{3,2,1,0:T(8,128)(2,1)S(1)} %copy-done), custom_call_target="tpu_custom_call" | custom-call | flops 1073741824 | bytes 2621440 | tf_op jit(solution)/shard_map/pallas_call | solution.py:241
  83.0 0.2 collective-permute-start.24
  83.3 1.9 %collective-permute-start.8 = (bf16[2,528,128]{2,1,0:T(8,128)(2,1)S(1)}, bf16[2,528,128]{2,1,0:T(8,128)(2,1)S(1)}, u32[]{:S(2)}, u32[]{:S(2)}) collective-permute-start(bf16[2,528,128]{2,1,0:T(8,128)(2,1)S(1)} %shard_map.96), channel_id=1, source_target_pairs={{0,2},{4,0},{8,4},{12,8},{14,12},{10,14},{6,10},{2,6},{1,3},{5,1},... | collective-permute-start | bytes 811016 | tf_op jit(solution)/shard_map/ppermute | solution.py:403
  85.2 7.8 %shard_map.97 = (f32[4,512,128]{2,1,0:T(8,128)S(1)}, bf16[4,16,128]{2,1,0:T(8,128)(2,1)S(1)}, f32[4,512,128]{2,1,0:T(8,128)S(1)}, bf16[4,16,128]{2,1,0:T(8,128)(2,1)S(1)}) custom-call(s32[2,9]{1,0:T(2,128)S(1)} %pad_add_fusion.1.refs_0_, bf16[64,2048]{1,0:T(8,128)(2,1)S(1)} %collective-permute-done.2.refs_1_, ...), custom_call_target="tpu_custom_call" | custom-call | flops 2147483648 | bytes 5242880 | tf_op jit(solution)/shard_map/pallas_call | solution.py:241
  93.1 0.2 collective-permute-start.21
  93.3 1.9 %collective-permute-start.18 = (bf16[2,528,128]{2,1,0:T(8,128)(2,1)S(1)}, bf16[2,528,128]{2,1,0:T(8,128)(2,1)S(1)}, u32[]{:S(2)}, u32[]{:S(2)}) collective-permute-start(bf16[2,528,128]{2,1,0:T(8,128)(2,1)S(1)} %shard_map.103), channel_id=1, source_target_pairs={{0,2},{4,0},{8,4},{12,8},{14,12},{10,14},{6,10},{2,6},{1,3},{5,1},... | collective-permute-start | bytes 811016 | tf_op jit(solution)/shard_map/ppermute | solution.py:403
  95.2 0.8 shard_map.110
  96.0 0.2 collective-permute-start.25
  96.2 0.8 shard_map.98
  97.0 2.0 %collective-permute-start.15 = (bf16[2,528,128]{2,1,0:T(8,128)(2,1)S(1)}, bf16[2,528,128]{2,1,0:T(8,128)(2,1)S(1)}, u32[]{:S(2)}, u32[]{:S(2)}) collective-permute-start(bf16[2,528,128]{2,1,0:T(8,128)(2,1)S(1)} %shard_map.98), channel_id=1, source_target_pairs={{0,2},{4,0},{8,4},{12,8},{14,12},{10,14},{6,10},{2,6},{1,3},{5,1},... | collective-permute-start | bytes 811016 | tf_op jit(solution)/shard_map/ppermute | solution.py:403
  99.1 7.4 %shard_map.99 = (f32[4,512,128]{2,1,0:T(8,128)S(1)}, bf16[4,16,128]{2,1,0:T(8,128)(2,1)S(1)}, f32[4,512,128]{2,1,0:T(8,128)S(1)}, bf16[4,16,128]{2,1,0:T(8,128)(2,1)S(1)}) custom-call(s32[2,9]{1,0:T(2,128)S(1)} %pad_add_fusion.2.refs_0_, bf16[64,2048]{1,0:T(8,128)(2,1)S(1)} %collective-permute-done.1.refs_1_, ...), custom_call_target="tpu_custom_call" | custom-call | flops 2147483648 | bytes 5242880 | tf_op jit(solution)/shard_map/pallas_call | solution.py:241
  106.4 0.8 shard_map.107
  107.2 0.2 collective-permute-start.22
  107.4 0.8 shard_map.104
  108.2 1.9 %collective-permute-start.19 = (bf16[2,528,128]{2,1,0:T(8,128)(2,1)S(1)}, bf16[2,528,128]{2,1,0:T(8,128)(2,1)S(1)}, u32[]{:S(2)}, u32[]{:S(2)}) collective-permute-start(bf16[2,528,128]{2,1,0:T(8,128)(2,1)S(1)} %shard_map.104), channel_id=1, source_target_pairs={{0,2},{4,0},{8,4},{12,8},{14,12},{10,14},{6,10},{2,6},{1,3},{5,1},... | collective-permute-start | bytes 811016 | tf_op jit(solution)/shard_map/ppermute | solution.py:403
  110.2 0.8 shard_map.111
  111.0 0.2 collective-permute-start.26
  111.1 0.8 shard_map.100
  111.9 2.1 %collective-permute-start.16 = (bf16[2,528,128]{2,1,0:T(8,128)(2,1)S(1)}, bf16[2,528,128]{2,1,0:T(8,128)(2,1)S(1)}, u32[]{:S(2)}, u32[]{:S(2)}) collective-permute-start(bf16[2,528,128]{2,1,0:T(8,128)(2,1)S(1)} %shard_map.100), channel_id=1, source_target_pairs={{0,2},{4,0},{8,4},{12,8},{14,12},{10,14},{6,10},{2,6},{1,3},{5,1},... | collective-permute-start | bytes 811016 | tf_op jit(solution)/shard_map/ppermute | solution.py:403
  114.0 7.3 %shard_map.101 = (f32[4,512,128]{2,1,0:T(8,128)S(1)}, bf16[4,16,128]{2,1,0:T(8,128)(2,1)S(1)}, f32[4,512,128]{2,1,0:T(8,128)S(1)}, bf16[4,16,128]{2,1,0:T(8,128)(2,1)S(1)}) custom-call(s32[2,9]{1,0:T(2,128)S(1)} %pad_add_fusion.3.refs_0_, bf16[64,2048]{1,0:T(8,128)(2,1)S(1)} %collective-permute-done.refs_1_, ...), custom_call_target="tpu_custom_call" | custom-call | flops 2147483648 | bytes 5242880 | tf_op jit(solution)/shard_map/pallas_call | solution.py:241
  121.4 0.1 collective-permute-start.28
  121.5 0.8 shard_map.108
  122.3 0.8 collective-permute-start.23
  123.1 0.8 shard_map.105
  123.9 1.3 collective-permute-start.20
  125.2 0.8 shard_map.112
  126.0 1.5 %collective-permute-start.27 = (bf16[2,528,128]{2,1,0:T(8,128)(2,1)S(1)}, bf16[2,528,128]{2,1,0:T(8,128)(2,1)S(1)}, u32[]{:S(2)}, u32[]{:S(2)}) collective-permute-start(bf16[2,528,128]{2,1,0:T(8,128)(2,1)S(1)} %shard_map.112), channel_id=1, source_target_pairs={{0,4},{4,8},{8,12},{12,14},{14,10},{10,6},{6,2},{2,0},{1,5},{5,9},... | collective-permute-start | bytes 811016 | tf_op jit(solution)/shard_map/ppermute | solution.py:403
  127.5 0.8 shard_map.102
  128.3 0.6 collective-permute-start.17
  128.9 0.7 pad_add_fusion.4.refs_0_
  129.6 5.9 %shard_map.113 = (f32[4,512,128]{2,1,0:T(8,128)S(1)}, bf16[4,16,128]{2,1,0:T(8,128)(2,1)S(1)}) custom-call(s32[1,9]{1,0:T(1,128)S(1)} %pad_add_fusion.4.refs_0_, bf16[64,4096]{1,0:T(8,128)(2,1)S(1)} %bitcast.35, bf16[2,64,512]{2,1,0:T(8,128)(2,1)} %bitcast.26.refs_2_, bf16[32,2,64,512]{3,2,1,0:T(8,128)(2,1)S(1)} %copy-done.1), custom_call_target="tpu_custom_call" | custom-call | flops 1073741824 | bytes 2621440 | tf_op jit(solution)/shard_map/pallas_call | solution.py:241
  137.4 1.6 %constant_dynamic-update-slice_fusion = bf16[32,2,64,512]{3,2,1,0:T(8,128)(2,1)} fusion(bf16[32,2,64,512]{3,2,1,0:T(8,128)(2,1)} %copy.17.refs_3_.refs_5_, bf16[1,2,64,512]{3,2,1,0:T(8,128)(2,1)} %collective-permute-done.28, s32[]{:T(128)S(6)} %select_n.148), kind=kLoop, calls=%fused_computation.28 | loop fusion | bytes 262148 | tf_op jit(solution)/shard_map/dynamic_update_slice | solution.py:415
  139.0 3.4 %shard_map.114 = bf16[1,64,4096]{2,1,0:T(8,128)(2,1)} custom-call(bf16[2,528,128]{2,1,0:T(8,128)(2,1)} %collective-permute-done.17.refs_0_, bf16[2,528,128]{2,1,0:T(8,128)(2,1)S(1)} %collective-permute-done.20.refs_1_, bf16[2,528,128]{2,1,0:T(8,128)(2,1)S(1)} %collective-permute-done.23.refs_2_, bf16[2,528,128]{2,1,0:T(8,128)(2,1)S(1)} %collective-permute-done.27.refs_3_, ...), custom_call_target="tpu_custom_call" | custom-call | flops 2146304 | bytes 4292608 | tf_op jit(solution)/shard_map/pallas_call | solution.py:318
  (53 shorter events, 0.5 us)
Async XLA Ops:
  0.6 54.4 %copy-start.5 = (s32[8]{0:T(128)S(1)}, s32[8]{0:T(128)}, u32[]{:S(2)}) copy-start(s32[8]{0:T(128)} %constant.120.clone) | copy-start | bytes 100
  0.6 59.6 %copy-start.3 = (s32[8]{0:T(128)S(1)}, s32[8]{0:T(128)}, u32[]{:S(2)}) copy-start(s32[8]{0:T(128)} %constant.121.clone) | copy-start | bytes 100
  0.7 4.8 %copy-start.2 = (bf16[1,64,4096]{2,1,0:T(8,128)(2,1)S(1)}, bf16[1,64,4096]{2,1,0:T(8,128)(2,1)}, u32[]{:S(2)}) copy-start(bf16[1,64,4096]{2,1,0:T(8,128)(2,1)} %param.8) | copy-start | bytes 1572868
  0.7 13.6 %copy-start.4 = (s32[1,64]{1,0:T(1,128)S(1)}, s32[1,64]{1,0:T(1,128)}, u32[]{:S(2)}) copy-start(s32[1,64]{1,0:T(1,128)} %param.11) | copy-start | bytes 772
  5.5 29.8 %collective-permute-start.4 = (bf16[64,2048]{1,0:T(8,128)(2,1)S(1)}, bf16[64,2048]{1,0:T(8,128)(2,1)S(1)}, u32[]{:S(2)}, u32[]{:S(2)}) collective-permute-start(bf16[64,2048]{1,0:T(8,128)(2,1)S(1)} %get-tuple-element.40), channel_id=1, source_target_pairs={{0,2},{4,0},{8,4},{12,8},{14,12},{10,14},{6,10},{2,6},{1,3},{5,1},... | collective-permute-start | bytes 786440 | tf_op jit(solution)/shard_map/ppermute | solution.py:375
  8.5 38.3 %collective-permute-start.9 = (bf16[64,2048]{1,0:T(8,128)(2,1)S(1)}, bf16[64,2048]{1,0:T(8,128)(2,1)S(1)}, u32[]{:S(2)}, u32[]{:S(2)}) collective-permute-start(bf16[64,2048]{1,0:T(8,128)(2,1)S(1)} %get-tuple-element.40), channel_id=1, source_target_pairs={{0,4},{4,8},{8,12},{12,14},{14,10},{10,6},{6,2},{2,0},{1,5},{5,9},... | collective-permute-start | bytes 786440 | tf_op jit(solution)/shard_map/ppermute | solution.py:374
  8.6 26.6 %collective-permute-start = (bf16[64,2048]{1,0:T(8,128)(2,1)S(1)}, bf16[64,2048]{1,0:T(8,128)(2,1)S(1)}, u32[]{:S(2)}, u32[]{:S(2)}) collective-permute-start(bf16[64,2048]{1,0:T(8,128)(2,1)S(1)} %get-tuple-element.41), channel_id=1, source_target_pairs={{0,4},{4,8},{8,12},{12,14},{14,10},{10,6},{6,2},{2,0},{1,5},{5,9},... | collective-permute-start | bytes 786440 | tf_op jit(solution)/shard_map/ppermute | solution.py:374
  10.6 36.3 %collective-permute-start.12 = (bf16[64,2048]{1,0:T(8,128)(2,1)S(1)}, bf16[64,2048]{1,0:T(8,128)(2,1)S(1)}, u32[]{:S(2)}, u32[]{:S(2)}) collective-permute-start(bf16[64,2048]{1,0:T(8,128)(2,1)S(1)} %get-tuple-element.41), channel_id=1, source_target_pairs={{0,2},{4,0},{8,4},{12,8},{14,12},{10,14},{6,10},{2,6},{1,3},{5,1},... | collective-permute-start | bytes 786440 | tf_op jit(solution)/shard_map/ppermute | solution.py:375
  10.7 117.6 %collective-permute-start.29 = (s32[1]{0:T(128)}, s32[1]{0:T(128)}, u32[]{:S(2)}, u32[]{:S(2)}) collective-permute-start(s32[1]{0:T(128)} %param.13), channel_id=1, source_target_pairs={{8,0},{10,2},{12,4},{14,6},{0,8},{2,10},{4,12},{6,14},{9,1},{11,3}... | collective-permute-start | bytes 20 | tf_op jit(solution)/shard_map/ppermute | solution.py:23
  35.2 9.1 %collective-permute-start.1 = (bf16[64,2048]{1,0:T(8,128)(2,1)S(1)}, bf16[64,2048]{1,0:T(8,128)(2,1)S(1)}, u32[]{:S(2)}, u32[]{:S(2)}) collective-permute-start(bf16[64,2048]{1,0:T(8,128)(2,1)S(1)} %collective-permute-done.refs_1_), channel_id=1, source_target_pairs={{0,4},{4,8},{8,12},{12,14},{14,10},{10,6},{6,2},{2,0},{1,5},{5,9},... | collective-permute-start | bytes 786440 | tf_op jit(solution)/shard_map/ppermute | solution.py:374
  35.3 9.1 %collective-permute-start.5 = (bf16[64,2048]{1,0:T(8,128)(2,1)S(1)}, bf16[64,2048]{1,0:T(8,128)(2,1)S(1)}, u32[]{:S(2)}, u32[]{:S(2)}) collective-permute-start(bf16[64,2048]{1,0:T(8,128)(2,1)S(1)} %collective-permute-done.4.refs_4_), channel_id=1, source_target_pairs={{0,2},{4,0},{8,4},{12,8},{14,12},{10,14},{6,10},{2,6},{1,3},{5,1},... | collective-permute-start | bytes 786440 | tf_op jit(solution)/shard_map/ppermute | solution.py:375
  44.3 8.6 %collective-permute-start.2 = (bf16[64,2048]{1,0:T(8,128)(2,1)S(1)}, bf16[64,2048]{1,0:T(8,128)(2,1)S(1)}, u32[]{:S(2)}, u32[]{:S(2)}) collective-permute-start(bf16[64,2048]{1,0:T(8,128)(2,1)S(1)} %collective-permute-done.1.refs_1_), channel_id=1, source_target_pairs={{0,4},{4,8},{8,12},{12,14},{14,10},{10,6},{6,2},{2,0},{1,5},{5,9},... | collective-permute-start | bytes 786440 | tf_op jit(solution)/shard_map/ppermute | solution.py:374
  44.4 8.7 %collective-permute-start.6 = (bf16[64,2048]{1,0:T(8,128)(2,1)S(1)}, bf16[64,2048]{1,0:T(8,128)(2,1)}, u32[]{:S(2)}, u32[]{:S(2)}) collective-permute-start(bf16[64,2048]{1,0:T(8,128)(2,1)S(1)} %collective-permute-done.5.refs_4_), channel_id=1, source_target_pairs={{0,2},{4,0},{8,4},{12,8},{14,12},{10,14},{6,10},{2,6},{1,3},{5,1},... | collective-permute-start | bytes 786440 | tf_op jit(solution)/shard_map/ppermute | solution.py:375
  46.8 27.2 %collective-permute-start.10 = (bf16[64,2048]{1,0:T(8,128)(2,1)S(1)}, bf16[64,2048]{1,0:T(8,128)(2,1)S(1)}, u32[]{:S(2)}, u32[]{:S(2)}) collective-permute-start(bf16[64,2048]{1,0:T(8,128)(2,1)S(1)} %collective-permute-done.9.refs_2_), channel_id=1, source_target_pairs={{0,4},{4,8},{8,12},{12,14},{14,10},{10,6},{6,2},{2,0},{1,5},{5,9},... | collective-permute-start | bytes 786440 | tf_op jit(solution)/shard_map/ppermute | solution.py:374
  46.9 27.4 %collective-permute-start.13 = (bf16[64,2048]{1,0:T(8,128)(2,1)S(1)}, bf16[64,2048]{1,0:T(8,128)(2,1)S(1)}, u32[]{:S(2)}, u32[]{:S(2)}) collective-permute-start(bf16[64,2048]{1,0:T(8,128)(2,1)S(1)} %collective-permute-done.12.refs_3_), channel_id=1, source_target_pairs={{0,2},{4,0},{8,4},{12,8},{14,12},{10,14},{6,10},{2,6},{1,3},{5,1},... | collective-permute-start | bytes 786440 | tf_op jit(solution)/shard_map/ppermute | solution.py:375
  52.9 23.2 %collective-permute-start.3 = (bf16[64,2048]{1,0:T(8,128)(2,1)S(1)}, bf16[64,2048]{1,0:T(8,128)(2,1)S(1)}, u32[]{:S(2)}, u32[]{:S(2)}) collective-permute-start(bf16[64,2048]{1,0:T(8,128)(2,1)S(1)} %collective-permute-done.2.refs_1_), channel_id=1, source_target_pairs={{0,4},{4,8},{8,12},{12,14},{14,10},{10,6},{6,2},{2,0},{1,5},{5,9},... | collective-permute-start | bytes 786440 | tf_op jit(solution)/shard_map/ppermute | solution.py:378
  53.1 23.1 %collective-permute-start.7 = (bf16[64,2048]{1,0:T(8,128)(2,1)}, bf16[64,2048]{1,0:T(8,128)(2,1)S(1)}, u32[]{:S(2)}, u32[]{:S(2)}) collective-permute-start(bf16[64,2048]{1,0:T(8,128)(2,1)} %collective-permute-done.6.refs_4_), channel_id=1, source_target_pairs={{0,2},{4,0},{8,4},{12,8},{14,12},{10,14},{6,10},{2,6},{1,3},{5,1},... | collective-permute-start | bytes 786440 | tf_op jit(solution)/shard_map/ppermute | solution.py:379
  74.0 11.2 %collective-permute-start.11 = (bf16[64,2048]{1,0:T(8,128)(2,1)S(1)}, bf16[64,2048]{1,0:T(8,128)(2,1)S(1)}, u32[]{:S(2)}, u32[]{:S(2)}) collective-permute-start(bf16[64,2048]{1,0:T(8,128)(2,1)S(1)} %collective-permute-done.10.refs_2_), channel_id=1, source_target_pairs={{0,4},{4,8},{8,12},{12,14},{14,10},{10,6},{6,2},{2,0},{1,5},{5,9},... | collective-permute-start | bytes 786440 | tf_op jit(solution)/shard_map/ppermute | solution.py:374
  74.3 10.9 %collective-permute-start.14 = (bf16[64,2048]{1,0:T(8,128)(2,1)S(1)}, bf16[64,2048]{1,0:T(8,128)(2,1)S(1)}, u32[]{:S(2)}, u32[]{:S(2)}) collective-permute-start(bf16[64,2048]{1,0:T(8,128)(2,1)S(1)} %collective-permute-done.13.refs_3_), channel_id=1, source_target_pairs={{0,2},{4,0},{8,4},{12,8},{14,12},{10,14},{6,10},{2,6},{1,3},{5,1},... | collective-permute-start | bytes 786440 | tf_op jit(solution)/shard_map/ppermute | solution.py:375
  76.2 2.2 %copy-start = (bf16[32,2,64,512]{3,2,1,0:T(8,128)(2,1)S(1)}, bf16[32,2,64,512]{3,2,1,0:T(8,128)(2,1)}, u32[]{:S(2)}) copy-start(bf16[32,2,64,512]{3,2,1,0:T(8,128)(2,1)} %copy.17.refs_3_.refs_5_) | copy-start | bytes 12582916
  83.0 12.2 %collective-permute-start.24 = (bf16[2,528,128]{2,1,0:T(8,128)(2,1)S(1)}, bf16[2,528,128]{2,1,0:T(8,128)(2,1)S(1)}, u32[]{:S(2)}, u32[]{:S(2)}) collective-permute-start(bf16[2,528,128]{2,1,0:T(8,128)(2,1)S(1)} %shard_map.109), channel_id=1, source_target_pairs={{0,4},{4,8},{8,12},{12,14},{14,10},{10,6},{6,2},{2,0},{1,5},{5,9},... | collective-permute-start | bytes 811016 | tf_op jit(solution)/shard_map/ppermute | solution.py:403
  83.3 12.9 %collective-permute-start.8 = (bf16[2,528,128]{2,1,0:T(8,128)(2,1)S(1)}, bf16[2,528,128]{2,1,0:T(8,128)(2,1)S(1)}, u32[]{:S(2)}, u32[]{:S(2)}) collective-permute-start(bf16[2,528,128]{2,1,0:T(8,128)(2,1)S(1)} %shard_map.96), channel_id=1, source_target_pairs={{0,2},{4,0},{8,4},{12,8},{14,12},{10,14},{6,10},{2,6},{1,3},{5,1},... | collective-permute-start | bytes 811016 | tf_op jit(solution)/shard_map/ppermute | solution.py:403
  93.1 13.4 %collective-permute-start.21 = (bf16[2,528,128]{2,1,0:T(8,128)(2,1)S(1)}, bf16[2,528,128]{2,1,0:T(8,128)(2,1)S(1)}, u32[]{:S(2)}, u32[]{:S(2)}) collective-permute-start(bf16[2,528,128]{2,1,0:T(8,128)(2,1)S(1)} %shard_map.106), channel_id=1, source_target_pairs={{0,4},{4,8},{8,12},{12,14},{14,10},{10,6},{6,2},{2,0},{1,5},{5,9},... | collective-permute-start | bytes 811016 | tf_op jit(solution)/shard_map/ppermute | solution.py:403
  93.3 14.1 %collective-permute-start.18 = (bf16[2,528,128]{2,1,0:T(8,128)(2,1)S(1)}, bf16[2,528,128]{2,1,0:T(8,128)(2,1)S(1)}, u32[]{:S(2)}, u32[]{:S(2)}) collective-permute-start(bf16[2,528,128]{2,1,0:T(8,128)(2,1)S(1)} %shard_map.103), channel_id=1, source_target_pairs={{0,2},{4,0},{8,4},{12,8},{14,12},{10,14},{6,10},{2,6},{1,3},{5,1},... | collective-permute-start | bytes 811016 | tf_op jit(solution)/shard_map/ppermute | solution.py:403
  96.0 14.1 %collective-permute-start.25 = (bf16[2,528,128]{2,1,0:T(8,128)(2,1)S(1)}, bf16[2,528,128]{2,1,0:T(8,128)(2,1)S(1)}, u32[]{:S(2)}, u32[]{:S(2)}) collective-permute-start(bf16[2,528,128]{2,1,0:T(8,128)(2,1)S(1)} %shard_map.110), channel_id=1, source_target_pairs={{0,4},{4,8},{8,12},{12,14},{14,10},{10,6},{6,2},{2,0},{1,5},{5,9},... | collective-permute-start | bytes 811016 | tf_op jit(solution)/shard_map/ppermute | solution.py:403
  97.0 14.1 %collective-permute-start.15 = (bf16[2,528,128]{2,1,0:T(8,128)(2,1)S(1)}, bf16[2,528,128]{2,1,0:T(8,128)(2,1)S(1)}, u32[]{:S(2)}, u32[]{:S(2)}) collective-permute-start(bf16[2,528,128]{2,1,0:T(8,128)(2,1)S(1)} %shard_map.98), channel_id=1, source_target_pairs={{0,2},{4,0},{8,4},{12,8},{14,12},{10,14},{6,10},{2,6},{1,3},{5,1},... | collective-permute-start | bytes 811016 | tf_op jit(solution)/shard_map/ppermute | solution.py:403
  107.2 14.1 %collective-permute-start.22 = (bf16[2,528,128]{2,1,0:T(8,128)(2,1)S(1)}, bf16[2,528,128]{2,1,0:T(8,128)(2,1)S(1)}, u32[]{:S(2)}, u32[]{:S(2)}) collective-permute-start(bf16[2,528,128]{2,1,0:T(8,128)(2,1)S(1)} %shard_map.107), channel_id=1, source_target_pairs={{0,4},{4,8},{8,12},{12,14},{14,10},{10,6},{6,2},{2,0},{1,5},{5,9},... | collective-permute-start | bytes 811016 | tf_op jit(solution)/shard_map/ppermute | solution.py:403
  108.2 14.1 %collective-permute-start.19 = (bf16[2,528,128]{2,1,0:T(8,128)(2,1)S(1)}, bf16[2,528,128]{2,1,0:T(8,128)(2,1)S(1)}, u32[]{:S(2)}, u32[]{:S(2)}) collective-permute-start(bf16[2,528,128]{2,1,0:T(8,128)(2,1)S(1)} %shard_map.104), channel_id=1, source_target_pairs={{0,2},{4,0},{8,4},{12,8},{14,12},{10,14},{6,10},{2,6},{1,3},{5,1},... | collective-permute-start | bytes 811016 | tf_op jit(solution)/shard_map/ppermute | solution.py:403
  111.0 13.0 %collective-permute-start.26 = (bf16[2,528,128]{2,1,0:T(8,128)(2,1)S(1)}, bf16[2,528,128]{2,1,0:T(8,128)(2,1)S(1)}, u32[]{:S(2)}, u32[]{:S(2)}) collective-permute-start(bf16[2,528,128]{2,1,0:T(8,128)(2,1)S(1)} %shard_map.111), channel_id=1, source_target_pairs={{0,4},{4,8},{8,12},{12,14},{14,10},{10,6},{6,2},{2,0},{1,5},{5,9},... | collective-permute-start | bytes 811016 | tf_op jit(solution)/shard_map/ppermute | solution.py:403
  111.9 14.1 %collective-permute-start.16 = (bf16[2,528,128]{2,1,0:T(8,128)(2,1)S(1)}, bf16[2,528,128]{2,1,0:T(8,128)(2,1)S(1)}, u32[]{:S(2)}, u32[]{:S(2)}) collective-permute-start(bf16[2,528,128]{2,1,0:T(8,128)(2,1)S(1)} %shard_map.100), channel_id=1, source_target_pairs={{0,2},{4,0},{8,4},{12,8},{14,12},{10,14},{6,10},{2,6},{1,3},{5,1},... | collective-permute-start | bytes 811016 | tf_op jit(solution)/shard_map/ppermute | solution.py:403
  121.4 8.2 %copy-start.1 = (bf16[32,2,64,512]{3,2,1,0:T(8,128)(2,1)S(1)}, bf16[32,2,64,512]{3,2,1,0:T(8,128)(2,1)}, u32[]{:S(2)}) copy-start(bf16[32,2,64,512]{3,2,1,0:T(8,128)(2,1)} %copy.17.refs_3_.refs_5_) | copy-start | bytes 12582916
  121.4 16.1 %collective-permute-start.28 = (bf16[1,2,64,512]{3,2,1,0:T(8,128)(2,1)}, bf16[1,2,64,512]{3,2,1,0:T(8,128)(2,1)}, u32[]{:S(2)}, u32[]{:S(2)}) collective-permute-start(bf16[1,2,64,512]{3,2,1,0:T(8,128)(2,1)} %param.9), channel_id=1, source_target_pairs={{8,0},{10,2},{12,4},{14,6},{0,8},{2,10},{4,12},{6,14},{9,1},{11,3}... | collective-permute-start | bytes 393224 | tf_op jit(solution)/shard_map/ppermute | solution.py:23
  122.3 16.7 %collective-permute-start.23 = (bf16[2,528,128]{2,1,0:T(8,128)(2,1)S(1)}, bf16[2,528,128]{2,1,0:T(8,128)(2,1)S(1)}, u32[]{:S(2)}, u32[]{:S(2)}) collective-permute-start(bf16[2,528,128]{2,1,0:T(8,128)(2,1)S(1)} %shard_map.108), channel_id=1, source_target_pairs={{0,4},{4,8},{8,12},{12,14},{14,10},{10,6},{6,2},{2,0},{1,5},{5,9},... | collective-permute-start | bytes 811016 | tf_op jit(solution)/shard_map/ppermute | solution.py:403
  123.9 15.1 %collective-permute-start.20 = (bf16[2,528,128]{2,1,0:T(8,128)(2,1)S(1)}, bf16[2,528,128]{2,1,0:T(8,128)(2,1)S(1)}, u32[]{:S(2)}, u32[]{:S(2)}) collective-permute-start(bf16[2,528,128]{2,1,0:T(8,128)(2,1)S(1)} %shard_map.105), channel_id=1, source_target_pairs={{0,2},{4,0},{8,4},{12,8},{14,12},{10,14},{6,10},{2,6},{1,3},{5,1},... | collective-permute-start | bytes 811016 | tf_op jit(solution)/shard_map/ppermute | solution.py:403
  126.0 13.0 %collective-permute-start.27 = (bf16[2,528,128]{2,1,0:T(8,128)(2,1)S(1)}, bf16[2,528,128]{2,1,0:T(8,128)(2,1)S(1)}, u32[]{:S(2)}, u32[]{:S(2)}) collective-permute-start(bf16[2,528,128]{2,1,0:T(8,128)(2,1)S(1)} %shard_map.112), channel_id=1, source_target_pairs={{0,4},{4,8},{8,12},{12,14},{14,10},{10,6},{6,2},{2,0},{1,5},{5,9},... | collective-permute-start | bytes 811016 | tf_op jit(solution)/shard_map/ppermute | solution.py:403
  128.3 10.7 %collective-permute-start.17 = (bf16[2,528,128]{2,1,0:T(8,128)(2,1)S(1)}, bf16[2,528,128]{2,1,0:T(8,128)(2,1)}, u32[]{:S(2)}, u32[]{:S(2)}) collective-permute-start(bf16[2,528,128]{2,1,0:T(8,128)(2,1)S(1)} %shard_map.102), channel_id=1, source_target_pairs={{0,2},{4,0},{8,4},{12,8},{14,12},{10,14},{6,10},{2,6},{1,3},{5,1},... | collective-permute-start | bytes 811016 | tf_op jit(solution)/shard_map/ppermute | solution.py:403

commit v2 on v1

--- a/solution.py
+++ b/solution.py
@@ -14,7 +14,7 @@
 STAT_ROWS = 16
 VMEM = pl.BlockSpec(memory_space=pltpu.VMEM)
 SMEM = pl.BlockSpec(memory_space=pltpu.SMEM)
-HBM = pl.BlockSpec(memory_space=pl.ANY)
+HBM = pl.BlockSpec(memory_space=pltpu.HBM)
 
 
 def shifted(block, axis, distance):
@@ -114,6 +114,10 @@
     return lax.dot_general(a, b, (((1,), (1,)), ((), ())), preferred_element_type=jnp.float32)
 
 
+def block_of(j):
+    return slice(j * HEAD_SIZE, (j + 1) * HEAD_SIZE)
+
+
 def iota(shape, dim):
     return lax.broadcasted_iota(jnp.int32, shape, dim)
 
@@ -167,7 +171,7 @@
     return out[:, :HEAD_SIZE], top, out[:, HEAD_SIZE:]
 
 
-def attend_kernel(sizes, parts, own, wire, *refs):
+def attend_kernel(sizes, parts, own, *refs):
     kv_heads, groups, suffix, cap, page_len = sizes
     refs = list(refs)
     meta = refs.pop(0)
@@ -175,7 +179,8 @@
     own_kv = refs.pop(0) if own else None
     pages = refs.pop(0)
     outs = [(refs.pop(0), refs.pop(0)) for _ in parts]
-    held, sems = refs
+    stored = refs.pop(0) if own else None
+    held, sems = refs[:2]
     copies = [
         [
             pltpu.make_async_copy(pages.at[meta[n, c]], held.at[n, c], sems.at[n, c])
@@ -186,6 +191,9 @@
     for request in copies:
         for copy in request:
             copy.start()
+    if own:
+        keep = pltpu.make_async_copy(pages, stored, refs[2])
+        keep.start()
     factor = HEAD_SIZE ** (-0.5) * LOG2E
     keys = cap * page_len
     for n, halves in enumerate(queries):
@@ -200,33 +208,22 @@
             lanes = slice(h * HEAD_SIZE, (h + 1) * HEAD_SIZE)
             k = held[n, :, 0, :, lanes].reshape(keys, HEAD_SIZE)
             v = held[n, :, 1, :, lanes].reshape(keys, HEAD_SIZE)
-            tops, totals = [], []
             rows = groups * suffix
-            per_block = HEAD_SIZE // suffix
-            for j in range(rows // HEAD_SIZE):
-                q = jnp.concatenate(
-                    [
-                        q_ref[:, (first + g) * HEAD_SIZE:(first + g + 1) * HEAD_SIZE]
-                        for g in range(j * per_block, (j + 1) * per_block)
-                    ],
-                    0,
-                )
-                extra = None
-                if own:
-                    at = iota((HEAD_SIZE, suffix), 0) % suffix
-                    extra = (own_kv[0, :, lanes], own_kv[1, :, lanes], iota((HEAD_SIZE, suffix), 1) <= at)
-                acc, top, total = partial_rows(q, k, v, live, extra, factor)
-                acc_ref[h, j * HEAD_SIZE:(j + 1) * HEAD_SIZE, :] = acc.astype(acc_ref.dtype)
-                tops.append(top)
-                totals.append(total)
-            tile = pack_stats(tops, totals)
-            if wire:
-                stat_ref[h] = tile
-            else:
-                stat_ref[h] = tile
-
-
-def attend(sizes, meta, queries, own_kv, kv_pages, wire=False):
+            q = jnp.concatenate([q_ref[:, block_of(first + g)] for g in range(groups)], 0)
+            extra = None
+            if own:
+                at = iota((rows, suffix), 0) % suffix
+                causal = iota((rows, suffix), 1) <= at
+                extra = (own_kv[0, :, lanes], own_kv[1, :, lanes], causal)
+            acc, top, total = partial_rows(q, k, v, live, extra, factor)
+            acc_ref[h] = acc
+            blocks = [block_of(j) for j in range(rows // HEAD_SIZE)]
+            stat_ref[h] = pack_stats([top[j] for j in blocks], [total[j] for j in blocks])
+    if own:
+        keep.wait()
+
+
+def attend(sizes, meta, queries, own_kv, kv_pages):
     kv_heads, groups, suffix, cap, page_len = sizes
     parts = [len(q) for q in queries]
     flat = [x for q in queries for x in q]
@@ -238,15 +235,21 @@
         shapes.append(jax.ShapeDtypeStruct((kv_heads, STAT_ROWS, HEAD_SIZE), jnp.bfloat16))
     keys = cap * page_len
     count = len(parts)
+    scratch = [
+        pltpu.VMEM((count, cap) + kv_pages.shape[1:], jnp.bfloat16),
+        pltpu.SemaphoreType.DMA((count, cap)),
+    ]
+    specs = [VMEM] * len(shapes)
+    if own:
+        shapes.append(jax.ShapeDtypeStruct(kv_pages.shape, kv_pages.dtype))
+        specs.append(HBM)
+        scratch.append(pltpu.SemaphoreType.DMA)
     out = pl.pallas_call(
-        functools.partial(attend_kernel, sizes, parts, own, wire),
+        functools.partial(attend_kernel, sizes, parts, own),
         out_shape=shapes,
         in_specs=[SMEM] + [VMEM] * (len(flat) + own) + [HBM],
-        out_specs=[VMEM] * len(shapes),
-        scratch_shapes=[
-            pltpu.VMEM((count, cap) + kv_pages.shape[1:], jnp.bfloat16),
-            pltpu.SemaphoreType.DMA((count, cap)),
-        ],
+        out_specs=specs,
+        scratch_shapes=scratch,
         compiler_params=pltpu.CompilerParams(vmem_limit_bytes=48 * 1024 * 1024),
         cost_estimate=pl.CostEstimate(
             flops=count * kv_heads * rows * keys * HEAD_SIZE * 8,
@@ -254,7 +257,28 @@
             transcendentals=count * kv_heads * rows * keys,
         ),
     )(meta, *flat, *([own_kv] if own else []), kv_pages)
-    return [(out[2 * n], out[2 * n + 1]) for n in range(count)]
+    return [(out[2 * n], out[2 * n + 1]) for n in range(count)] + list(out[2 * count:])
+
+
+def place_kernel(half, column, me_ref, lists_ref, page_ref, old_ref, out_ref, sem):
+    me = me_ref[0]
+    from_below = (me >= half) == (me % 2 == 0)
+    slot = jnp.where(from_below, lists_ref[0, column], lists_ref[1, column])
+    copy = pltpu.make_async_copy(page_ref.at[0], out_ref.at[slot], sem)
+    copy.start()
+    copy.wait()
+
+
+def place_page(half, column, me, lists, page, store):
+    return pl.pallas_call(
+        functools.partial(place_kernel, half, column),
+        out_shape=jax.ShapeDtypeStruct(store.shape, store.dtype),
+        in_specs=[SMEM, SMEM, VMEM, HBM],
+        out_specs=HBM,
+        scratch_shapes=[pltpu.SemaphoreType.DMA],
+        input_output_aliases={3: 0},
+        cost_estimate=pl.CostEstimate(flops=0, bytes_accessed=2 * page.size, transcendentals=0),
+    )(me, lists, page, store)
 
 
 def blend(parts):
@@ -265,10 +289,6 @@
     return acc, top, total
 
 
-def block_of(j):
-    return slice(j * HEAD_SIZE, (j + 1) * HEAD_SIZE)
-
-
 def pack_kernel(first, heads, acc_ref, stat_ref, out_ref):
     rows = acc_ref.shape[1]
     for h in range(heads):
@@ -276,7 +296,7 @@
         out_ref[h, rows:, :] = stat_ref[first + h]
 
 
-def merge_kernel(first, heads, in_ref, acc_ref, stat_ref, out_ref):
+def merge_kernel(first, heads, in_ref, acc_ref, stat_ref, out_ref, out_stat_ref=None):
     rows = acc_ref.shape[1]
     for h in range(heads):
         in_top, in_total = unpack_stats(in_ref[h, rows:, :])
@@ -289,28 +309,34 @@
                     (acc_ref[first + h, block_of(j), :], my_top[j], my_total[j]),
                 ]
             )
-            out_ref[h, block_of(j), :] = acc.astype(jnp.bfloat16)
+            out_ref[h, block_of(j), :] = acc.astype(out_ref.dtype)
             tops.append(top)
             totals.append(total)
-        out_ref[h, rows:, :] = pack_stats(tops, totals)
-
-
-def final_kernel(heads_each, suffix, *refs):
-    arrivals, (acc_ref, stat_ref, out_ref) = refs[:-3], refs[-3:]
-    kv_heads, rows = acc_ref.shape[:2]
-    groups = rows // suffix
-    for h in range(kv_heads):
-        here = arrivals[h // heads_each::kv_heads // heads_each]
-        stats = [unpack_stats(ref[h % heads_each, rows:, :]) for ref in here]
-        stats.append(unpack_stats(stat_ref[h]))
-        for j in range(rows // HEAD_SIZE):
-            blocks = [ref[h % heads_each, block_of(j), :].astype(jnp.float32) for ref in here]
-            blocks.append(acc_ref[h, block_of(j), :])
-            acc, _, total = blend([(a, t[j], l[j]) for a, (t, l) in zip(blocks, stats)])
-            out = (acc / total).astype(jnp.bfloat16)
-            for i in range(HEAD_SIZE // suffix):
-                g = h * groups + j * (HEAD_SIZE // suffix) + i
-                out_ref[0, :, block_of(g)] = out[i * suffix:(i + 1) * suffix]
+        if out_stat_ref is None:
+            out_ref[h, rows:, :] = pack_stats(tops, totals)
+        else:
+            out_stat_ref[h] = pack_stats(tops, totals)
+
+
+def final_kernel(suffix, *refs):
+    sides, out_ref = (refs[0:3], refs[3:6]), refs[6]
+    for side, (in_ref, acc_ref, stat_ref) in enumerate(sides):
+        heads, rows = acc_ref.shape[:2]
+        groups = rows // suffix
+        for h in range(heads):
+            in_top, in_total = unpack_stats(in_ref[h, rows:, :])
+            my_top, my_total = unpack_stats(stat_ref[h])
+            for j in range(rows // HEAD_SIZE):
+                acc, _, total = blend(
+                    [
+                        (in_ref[h, block_of(j), :].astype(jnp.float32), in_top[j], in_total[j]),
+                        (acc_ref[h, block_of(j), :], my_top[j], my_total[j]),
+                    ]
+                )
+                out = (acc / total).astype(jnp.bfloat16)
+                for i in range(HEAD_SIZE // suffix):
+                    g = (side * heads + h) * groups + j * (HEAD_SIZE // suffix) + i
+                    out_ref[0, :, block_of(g)] = out[i * suffix:(i + 1) * suffix]
 
 
 def call(kernel, shape, *args):
@@ -319,7 +345,7 @@
         kernel,
         out_shape=shape,
         in_specs=[VMEM] * len(args),
-        out_specs=VMEM,
+        out_specs=[VMEM] * len(shape) if isinstance(shape, list) else VMEM,
         compiler_params=pltpu.CompilerParams(vmem_limit_bytes=48 * 1024 * 1024),
         cost_estimate=pl.CostEstimate(flops=size, bytes_accessed=2 * size, transcendentals=size // 8),
     )(*args)
@@ -340,44 +366,62 @@
     order = list(range(0, stores, 2)) + list(range(1, stores, 2))[::-1]
     up = [(order[i], order[(i + 1) % stores]) for i in range(stores)]
     down = [(order[i], order[i - 1]) for i in range(stores)]
-    place = [order.index(i) for i in range(stores)]
-    my_place = jnp.asarray(place, jnp.int32)[me]
-    order_now = jnp.asarray(order, jnp.int32)
-
-    mine_row = jnp.concatenate([page_table, prefix_pages[:, None]], 1)
-    rows = lax.all_gather(mine_row, "store", axis=0, tiled=True)
-
-    def listing(rows):
-        table, length = rows[:, :maxp], rows[:, maxp:]
-        entries = jnp.arange(maxp, dtype=jnp.int32)
-        held = table // pages_dev == me
-        before = entries[:, None] < entries[None, :]
-        rank = jnp.sum((held[:, :, None] & before[None]).astype(jnp.int32), 1)
-        placed = held[:, :, None] & (rank[:, :, None] == jnp.arange(cap, dtype=jnp.int32))
-        ids = jnp.sum(jnp.where(placed, (table % pages_dev)[:, :, None], 0), 1)
-        live = jnp.sum((held & (entries[None] < length)).astype(jnp.int32), 1, keepdims=True)
-        return jnp.concatenate([ids, live], 1)
-
-    lists = listing(rows)
-
-    def listed(*distances):
-        which = [order_now[(my_place - d) % stores] for d in distances]
-        return jnp.stack([lists[w] for w in which])
+
+    table, length = page_table[0], prefix_pages[0]
+    entries = jnp.arange(maxp, dtype=jnp.int32)
+    owners = table // pages_dev
+    before = (owners[:, None] == owners[None, :]) & (entries[:, None] < entries[None, :])
+    rank = jnp.sum(before.astype(jnp.int32), 0)
+    place = jnp.arange(HEAD_SIZE, dtype=jnp.int32)
+    field = jnp.where(place[:, None] < cap, rank[None, :] == place[:, None], place[:, None] == cap)
+    value = jnp.where(
+        place[:, None] < cap, (table % pages_dev)[None], (entries < length).astype(jnp.int32)[None]
+    )
+    owned = owners[None, :] == jnp.arange(suffix, dtype=jnp.int32)[:, None]
+    lists = jnp.sum(jnp.where(owned[:, None, :] & field[None], value[None], 0), -1)
+    lists = jnp.where(place[None, :] == cap + 1, new_slots[0], lists)
 
     heads_each = kv_heads // 2
     cut = heads_each * groups * HEAD_SIZE
-    mine = [queries[0, :, :cut], queries[0, :, cut:]]
+    mine = [
+        jnp.concatenate([queries[0, :, :cut], lists.astype(queries.dtype)], 1),
+        queries[0, :, cut:],
+    ]
+
+    def listed(*arrays):
+        rows = [lax.dynamic_slice(x, (me, cut), (1, HEAD_SIZE)) for x in arrays]
+        return jnp.concatenate(rows).astype(jnp.int32)
+
+    def after(values, token):
+        return lax.optimization_barrier((values, token))
+
     ups, downs = list(mine), list(mine)
-    partials = {}
-    partials[0], = attend(sizes, listing(mine_row), [[queries[0]]], suffix_key_value[0], kv_pages)
+    partials, lists_of = {}, {}
     for step in range(1, half):
         ups = [lax.ppermute(x, "store", up) for x in ups]
         downs = [lax.ppermute(x, "store", down) for x in downs]
-        got = attend(sizes, listed(step, -step), [ups, downs], None, kv_pages)
+        if step == 1:
+            partials[0], store = attend(
+                sizes,
+                lax.dynamic_slice(lists, (me, 0), (1, HEAD_SIZE)),
+                [[queries[0]]],
+                suffix_key_value[0],
+                kv_pages,
+            )
+            (ups, downs), partials[0] = after((ups, downs), partials[0])
+        else:
+            (ups, downs), (partials[step - 1], partials[1 - step]) = after(
+                (ups, downs), (partials[step - 1], partials[1 - step])
+            )
+        lists_of[step] = listed(ups[0], downs[0])
+        got = attend(sizes, lists_of[step], [ups, downs], None, kv_pages)
         partials[step], partials[-step] = got
     ups[0] = lax.ppermute(ups[0], "store", up)
     downs[1] = lax.ppermute(downs[1], "store", down)
-    (far,) = attend(sizes, listed(half), [[ups[0], downs[1]]], None, kv_pages)
+    (ups, downs), (partials[half - 1], partials[1 - half]) = after(
+        (ups, downs), (partials[half - 1], partials[1 - half])
+    )
+    (far,) = attend(sizes, listed(ups[0]), [[ups[0], downs[1]]], None, kv_pages)
 
     rows_head = groups * suffix
     wire = jax.ShapeDtypeStruct((heads_each, rows_head + STAT_ROWS, HEAD_SIZE), jnp.bfloat16)
@@ -390,29 +434,41 @@
             functools.partial(merge_kernel, side * heads_each, heads_each), wire, block, *part
         )
 
-    flows = {}
-    for side in range(2):
-        for sign, route in ((1, down), (-1, up)):
-            if (side == 0) == (sign == 1):
-                block = packed(far, side)
-                distance = half
-            else:
-                block = packed(partials[sign * (half - 1)], side)
-                distance = half - 1
-            while True:
-                block = lax.ppermute(block, "store", route)
-                distance -= 1
-                if distance == 0:
-                    break
-                block = merged(block, partials[sign * distance], side)
-            flows[sign, side] = block
+    late, early = {}, {}
+    blocks = {}
+    for side, sign in ((0, 1), (1, -1)):
+        blocks[side, sign] = packed(far, side), half
+        blocks[1 - side, sign] = packed(partials[sign * (half - 1)], 1 - side), half - 1
+    for (side, sign), (block, distance) in blocks.items():
+        route = down if sign == 1 else up
+        first = distance
+        while True:
+            block = lax.ppermute(block, "store", route)
+            distance -= 1
+            if distance == 0:
+                break
+            block = merged(block, partials[sign * distance], side)
+        (late if first == half else early)[side] = block
+    kept = [
+        jax.ShapeDtypeStruct((heads_each, rows_head, HEAD_SIZE), jnp.float32),
+        jax.ShapeDtypeStruct((heads_each, STAT_ROWS, HEAD_SIZE), jnp.bfloat16),
+    ]
+    rest = [
+        call(
+            functools.partial(merge_kernel, side * heads_each, heads_each),
+            kept, early[side], *partials[0],
+        )
+        for side in range(2)
+    ]
     attended = call(
-        functools.partial(final_kernel, heads_each, suffix),
+        functools.partial(final_kernel, suffix),
         jax.ShapeDtypeStruct(queries.shape, queries.dtype),
-        flows[1, 0], flows[1, 1], flows[-1, 0], flows[-1, 1], *partials[0],
-    )
-    arrived, arrived_slot = shifted((suffix_key_value, new_slots), "store", stores // 2)
-    new_store = lax.dynamic_update_slice_in_dim(kv_pages, arrived, arrived_slot[0], 0)
+        late[0], *rest[0], late[1], *rest[1],
+    )
+
+    page, _ = after(suffix_key_value, partials[half - 1])
+    arrived = shifted(page, "store", half)
+    new_store = place_page(half, cap + 1, me[None], lists_of[stores // 4], arrived, store)
     return (attended, new_store)
 
 
@@ -421,7 +477,7 @@
     pulled = page_table.shape[1] // stores * kv_pages[0].size
     pushed = 2 * queries[0].size
     arrays = (queries, suffix_key_value, kv_pages, page_table, prefix_pages, new_slots)
-    if pulled >= pushed and stores % 2 == 0:
+    if pulled >= pushed and stores % 4 == 0:
         return queries_travel(*arrays)
     return pages_travel(*arrays)
 

time: 143 us -> 117 us (0.82); the launches traced: 142 us -> 115 us
  blocking collectives: 20.5 us -> 0 us
  between operations: 21.1 us -> 2.19 us
  waiting for transfers between devices: 10.3 us -> 26 us
  local copies, waits for them, and re-layouts: 10.1 us -> 5.92 us
  Pallas kernels: 44.6 us -> 47.3 us
  starting transfers between devices: 33.5 us -> 31 us
    all_gather x1 -> x0, blocking collectives: 20.5 us -> none  [queries_travel(): rows = lax.all_gather(mine_row, 'store', axis=0, tiled=True)]
    ppermute x14, waiting for transfers between devices: 0.04 us -> 14.2 us  [queries_travel(): block = lax.ppermute(block, 'store', route)]
    ppermute x6, starting transfers between devices: 11.1 us -> 3.2 us  [queries_travel(): downs = [lax.ppermute(x, 'store', down) for x in downs]]
    ppermute x6, starting transfers between devices: 2.43 us -> 10.1 us  [queries_travel(): ups = [lax.ppermute(x, 'store', up) for x in ups]]
    ppermute x2 -> x1, waiting for transfers between devices: 0.01 us -> 6.78 us  [shifted(): return lax.ppermute(block, axis, route)]
    ppermute x6, waiting for transfers between devices: 10.1 us -> 3.45 us  [queries_travel(): ups = [lax.ppermute(x, 'store', up) for x in ups]]
    pallas_call x5 -> x6, Pallas kernels: 33 us -> 35.7 us  [the longest x5 34.1 us: attend(): pl.pallas_call(functools.partial(attend_kernel, sizes, parts, own), out_s...]
    ppermute x2 -> x1, starting transfers between devices: 3.05 us -> 0.7 us  [shifted(): return lax.ppermute(block, axis, route)]
  transfers between devices with their start and end apart: 30 -> 29, of which waited for: 4 -> 9; matrix products, arithmetic and copies ran while one was open for 4% -> 0% of each run, Pallas kernels for 29% -> 35%
where the time goes in v2:
time: 117 us; the launch traced here: 115 us
  Pallas kernels  47.3 us (40%)
  starting transfers between devices  31 us (26%)
  waiting for transfers between devices  26 us (22%)
  local copies, waits for them, and re-layouts  5.92 us (5%)
  other arithmetic  2.46 us (2%)
  between operations  2.19 us (2%)
    pallas_call x5, Pallas kernels, attend(): pl.pallas_call(functools.partial(attend_kernel, sizes, parts, own), out_s...  34.1 us
    ppermute x14, starting transfers between devices, queries_travel(): block = lax.ppermute(block, 'store', route)  14.9 us
    ppermute x14, waiting for transfers between devices, queries_travel(): block = lax.ppermute(block, 'store', route)  14.2 us
    pallas_call x17, Pallas kernels, call(): pl.pallas_call(kernel, out_shape=shape, in_specs=[VMEM] * len(args), out_...  11.6 us
    ppermute x6, starting transfers between devices, queries_travel(): ups = [lax.ppermute(x, 'store', up) for x in ups]  10.1 us
    ppermute x1, waiting for transfers between devices, shifted(): return lax.ppermute(block, axis, route)  6.78 us
    unnamed x14, local copies, waits for them, and re-layouts  4.8 us
    ppermute x6, waiting for transfers between devices, queries_travel(): ups = [lax.ppermute(x, 'store', up) for x in ups]  3.45 us
  transfers between devices with their start and end apart: 29, of which 9 were waited for; matrix products, arithmetic and copies ran while one was open for 0% of the time, Pallas kernels for 35%

profile of v2, /device:TPU:0, one launch (start us, length us, event | category | flops | bytes accessed | tf_op | source)
XLA Modules:
  0.0 114.8 jit_solution(13735384180055117554)
XLA Ops:
  0.6 0.7 fusion.4
  1.3 0.7 and_select_fusion.1
  2.7 0.1 convert_reduce_fusion
  3.4 1.1 slice_bitcast_fusion
  4.7 0.8 select_reduce_fusion
  5.5 3.1 %collective-permute-start = (bf16[64,2176]{1,0:T(8,128)(2,1)S(1)}, bf16[64,2176]{1,0:T(8,128)(2,1)S(1)}, u32[]{:S(2)}, u32[]{:S(2)}) collective-permute-start(bf16[64,2176]{1,0:T(8,128)(2,1)S(1)} %pad_maximum_fusion), channel_id=1, source_target_pairs={{0,4},{4,8},{8,12},{12,14},{14,10},{10,6},{6,2},{2,0},{1,5},{5,9},... | collective-permute-start | bytes 835592 | tf_op jit(solution)/shard_map/ppermute | solution.py:401
  8.6 2.0 %collective-permute-start.1 = (bf16[64,2048]{1,0:T(8,128)(2,1)S(1)}, bf16[64,2048]{1,0:T(8,128)(2,1)S(1)}, u32[]{:S(2)}, u32[]{:S(2)}) collective-permute-start(bf16[64,2048]{1,0:T(8,128)(2,1)S(1)} %get-tuple-element.104), channel_id=1, source_target_pairs={{0,4},{4,8},{8,12},{12,14},{14,10},{10,6},{6,2},{2,0},{1,5},{5,9},... | collective-permute-start | bytes 786440 | tf_op jit(solution)/shard_map/ppermute | solution.py:401
  10.6 2.2 %copy-done = bf16[32,2,64,512]{3,2,1,0:T(8,128)(2,1)S(1)} copy-done((bf16[32,2,64,512]{3,2,1,0:T(8,128)(2,1)S(1)}, bf16[32,2,64,512]{3,2,1,0:T(8,128)(2,1)}, u32[]{:S(2)}) %copy-start) | copy-done | bytes 4194328
  12.8 1.0 copy-done.2
  13.8 0.9 copy-done.3
  14.7 6.0 %shard_map.77 = (f32[4,512,128]{2,1,0:T(8,128)S(1)}, bf16[4,16,128]{2,1,0:T(8,128)(2,1)S(1)}, bf16[32,2,64,512]{3,2,1,0:T(8,128)(2,1)}) custom-call(s32[1,128]{1,0:T(1,128)S(1)} %constant_dynamic-slice_fusion.7.refs_0_, bf16[64,4096]{1,0:T(8,128)(2,1)S(1)} %bitcast.23, bf16[2,64,512]{2,1,0:T(8,128)(2,1)S(1)} %bitcast.24, bf16[32,2,64,512]{3,2,1,0:T(8,128)(2,1)S(1)} %copy-done), custom_call_target="tpu_custom_call" | custom-call | flops 1073741824 | bytes 2621440 | tf_op jit(solution)/shard_map/pallas_call | solution.py:247
  20.8 1.5 %collective-permute-done.3.refs_4_ = bf16[64,2048]{1,0:T(8,128)(2,1)S(1)} collective-permute-done((bf16[64,2048]{1,0:T(8,128)(2,1)S(1)}, bf16[64,2048]{1,0:T(8,128)(2,1)S(1)}, u32[]{:S(2)}, u32[]{:S(2)}) %collective-permute-start.3) | collective-permute-done | bytes 262176 | tf_op jit(solution)/shard_map/ppermute | solution.py:402
  22.3 0.5 collective-permute-start.6
  22.8 1.5 %collective-permute-start.4 = (bf16[64,2176]{1,0:T(8,128)(2,1)S(1)}, bf16[64,2176]{1,0:T(8,128)(2,1)S(1)}, u32[]{:S(2)}, u32[]{:S(2)}) collective-permute-start(bf16[64,2176]{1,0:T(8,128)(2,1)S(1)} %collective-permute-done.refs_1_), channel_id=1, source_target_pairs={{0,4},{4,8},{8,12},{12,14},{14,10},{10,6},{6,2},{2,0},{1,5},{5,9},... | collective-permute-start | bytes 835592 | tf_op jit(solution)/shard_map/ppermute | solution.py:401
  24.3 1.6 %collective-permute-start.5 = (bf16[64,2048]{1,0:T(8,128)(2,1)S(1)}, bf16[64,2048]{1,0:T(8,128)(2,1)S(1)}, u32[]{:S(2)}, u32[]{:S(2)}) collective-permute-start(bf16[64,2048]{1,0:T(8,128)(2,1)S(1)} %collective-permute-done.1.refs_2_), channel_id=1, source_target_pairs={{0,4},{4,8},{8,12},{12,14},{14,10},{10,6},{6,2},{2,0},{1,5},{5,9},... | collective-permute-start | bytes 786440 | tf_op jit(solution)/shard_map/ppermute | solution.py:401
  25.9 0.4 collective-permute-start.7
  26.4 7.7 %shard_map.78 = (f32[4,512,128]{2,1,0:T(8,128)S(1)}, bf16[4,16,128]{2,1,0:T(8,128)(2,1)S(1)}, f32[4,512,128]{2,1,0:T(8,128)S(1)}, bf16[4,16,128]{2,1,0:T(8,128)(2,1)S(1)}) custom-call(s32[2,128]{1,0:T(2,128)S(1)} %maximum_convert_fusion.refs_0_, bf16[64,2176]{1,0:T(8,128)(2,1)S(1)} %collective-permute-done.refs_1_, ...), custom_call_target="tpu_custom_call" | custom-call | flops 2147483648 | bytes 5242880 | tf_op jit(solution)/shard_map/pallas_call | solution.py:247
  34.1 1.4 %collective-permute-done.5.refs_2_ = bf16[64,2048]{1,0:T(8,128)(2,1)S(1)} collective-permute-done((bf16[64,2048]{1,0:T(8,128)(2,1)S(1)}, bf16[64,2048]{1,0:T(8,128)(2,1)S(1)}, u32[]{:S(2)}, u32[]{:S(2)}) %collective-permute-start.5) | collective-permute-done | bytes 262176 | tf_op jit(solution)/shard_map/ppermute | solution.py:401
  35.5 1.6 %collective-permute-start.10 = (bf16[64,2176]{1,0:T(8,128)(2,1)S(1)}, bf16[64,2176]{1,0:T(8,128)(2,1)S(1)}, u32[]{:S(2)}, u32[]{:S(2)}) collective-permute-start(bf16[64,2176]{1,0:T(8,128)(2,1)S(1)} %collective-permute-done.6.refs_3_), channel_id=1, source_target_pairs={{0,2},{4,0},{8,4},{12,8},{14,12},{10,14},{6,10},{2,6},{1,3},{5,1},... | collective-permute-start | bytes 835592 | tf_op jit(solution)/shard_map/ppermute | solution.py:402
  37.1 0.5 collective-permute-start.8
  37.6 1.4 %collective-permute-start.9 = (bf16[64,2048]{1,0:T(8,128)(2,1)S(1)}, bf16[64,2048]{1,0:T(8,128)(2,1)S(1)}, u32[]{:S(2)}, u32[]{:S(2)}) collective-permute-start(bf16[64,2048]{1,0:T(8,128)(2,1)S(1)} %collective-permute-done.5.refs_2_), channel_id=1, source_target_pairs={{0,4},{4,8},{8,12},{12,14},{14,10},{10,6},{6,2},{2,0},{1,5},{5,9},... | collective-permute-start | bytes 786440 | tf_op jit(solution)/shard_map/ppermute | solution.py:401
  39.0 0.6 collective-permute-start.11
  39.6 7.7 %shard_map.79 = (f32[4,512,128]{2,1,0:T(8,128)S(1)}, bf16[4,16,128]{2,1,0:T(8,128)(2,1)S(1)}, f32[4,512,128]{2,1,0:T(8,128)S(1)}, bf16[4,16,128]{2,1,0:T(8,128)(2,1)S(1)}) custom-call(s32[2,128]{1,0:T(2,128)S(1)} %maximum_convert_fusion.1.refs_0_.lists_ref, bf16[64,2176]{1,0:T(8,128)(2,1)S(1)} %collective-permute-done.4.refs_1_, ...), custom_call_target="tpu_custom_call" | custom-call | flops 2147483648 | bytes 5242880 | tf_op jit(solution)/shard_map/pallas_call | solution.py:247
  47.4 2.1 %collective-permute-done.9.refs_2_ = bf16[64,2048]{1,0:T(8,128)(2,1)S(1)} collective-permute-done((bf16[64,2048]{1,0:T(8,128)(2,1)S(1)}, bf16[64,2048]{1,0:T(8,128)(2,1)S(1)}, u32[]{:S(2)}, u32[]{:S(2)}) %collective-permute-start.9) | collective-permute-done | bytes 262176 | tf_op jit(solution)/shard_map/ppermute | solution.py:401
  49.5 0.5 collective-permute-start.12
  50.0 1.6 %collective-permute-start.13 = (bf16[64,2048]{1,0:T(8,128)(2,1)S(1)}, bf16[64,2048]{1,0:T(8,128)(2,1)S(1)}, u32[]{:S(2)}, u32[]{:S(2)}) collective-permute-start(bf16[64,2048]{1,0:T(8,128)(2,1)S(1)} %collective-permute-done.11.refs_4_), channel_id=1, source_target_pairs={{0,2},{4,0},{8,4},{12,8},{14,12},{10,14},{6,10},{2,6},{1,3},{5,1},... | collective-permute-start | bytes 786440 | tf_op jit(solution)/shard_map/ppermute | solution.py:420
  51.6 7.8 %shard_map.80 = (f32[4,512,128]{2,1,0:T(8,128)S(1)}, bf16[4,16,128]{2,1,0:T(8,128)(2,1)S(1)}, f32[4,512,128]{2,1,0:T(8,128)S(1)}, bf16[4,16,128]{2,1,0:T(8,128)(2,1)S(1)}) custom-call(s32[2,128]{1,0:T(2,128)S(1)} %maximum_convert_fusion.2.refs_0_, bf16[64,2176]{1,0:T(8,128)(2,1)S(1)} %collective-permute-done.8.refs_1_, ...), custom_call_target="tpu_custom_call" | custom-call | flops 2147483648 | bytes 5242880 | tf_op jit(solution)/shard_map/pallas_call | solution.py:247
  59.4 4.9 %shard_map.81 = (f32[4,512,128]{2,1,0:T(8,128)S(1)}, bf16[4,16,128]{2,1,0:T(8,128)(2,1)S(1)}) custom-call(s32[1,128]{1,0:T(1,128)S(1)} %fusion.3.refs_0_, bf16[64,2176]{1,0:T(8,128)(2,1)S(1)} %collective-permute-done.12.refs_1_, bf16[64,2048]{1,0:T(8,128)(2,1)S(1)} %collective-permute-done.13.refs_2_, bf16[32,2,64,512]{3,2,1,0:T(8,128)(2,1)S(1)} %copy-done.1), custom_call_target="tpu_custom_call" | custom-call | flops 1073741824 | bytes 2621440 | tf_op jit(solution)/shard_map/pallas_call | solution.py:247
  64.3 1.6 %collective-permute-start.14 = (bf16[2,528,128]{2,1,0:T(8,128)(2,1)S(1)}, bf16[2,528,128]{2,1,0:T(8,128)(2,1)S(1)}, u32[]{:S(2)}, u32[]{:S(2)}) collective-permute-start(bf16[2,528,128]{2,1,0:T(8,128)(2,1)S(1)} %shard_map.82), channel_id=1, source_target_pairs={{0,2},{4,0},{8,4},{12,8},{14,12},{10,14},{6,10},{2,6},{1,3},{5,1},... | collective-permute-start | bytes 811016 | tf_op jit(solution)/shard_map/ppermute | solution.py:446
  66.0 0.5 collective-permute-start.21
  66.5 0.7 collective-permute-start.18
  67.3 1.6 %collective-permute-start.25 = (bf16[2,528,128]{2,1,0:T(8,128)(2,1)S(1)}, bf16[2,528,128]{2,1,0:T(8,128)(2,1)S(1)}, u32[]{:S(2)}, u32[]{:S(2)}) collective-permute-start(bf16[2,528,128]{2,1,0:T(8,128)(2,1)S(1)} %shard_map.94), channel_id=1, source_target_pairs={{0,2},{4,0},{8,4},{12,8},{14,12},{10,14},{6,10},{2,6},{1,3},{5,1},... | collective-permute-start | bytes 811016 | tf_op jit(solution)/shard_map/ppermute | solution.py:446
  68.9 4.8 %collective-permute-done.14.in_ref = bf16[2,528,128]{2,1,0:T(8,128)(2,1)S(1)} collective-permute-done((bf16[2,528,128]{2,1,0:T(8,128)(2,1)S(1)}, bf16[2,528,128]{2,1,0:T(8,128)(2,1)S(1)}, u32[]{:S(2)}, u32[]{:S(2)}) %collective-permute-start.14) | collective-permute-done | bytes 270368 | tf_op jit(solution)/shard_map/ppermute | solution.py:446
  73.7 0.8 shard_map.83
  74.5 1.6 %collective-permute-start.15 = (bf16[2,528,128]{2,1,0:T(8,128)(2,1)S(1)}, bf16[2,528,128]{2,1,0:T(8,128)(2,1)S(1)}, u32[]{:S(2)}, u32[]{:S(2)}) collective-permute-start(bf16[2,528,128]{2,1,0:T(8,128)(2,1)S(1)} %shard_map.83), channel_id=1, source_target_pairs={{0,2},{4,0},{8,4},{12,8},{14,12},{10,14},{6,10},{2,6},{1,3},{5,1},... | collective-permute-start | bytes 811016 | tf_op jit(solution)/shard_map/ppermute | solution.py:446
  76.2 0.8 shard_map.91
  77.0 0.5 collective-permute-start.22
  77.4 3.4 %collective-permute-done.18.in_ref = bf16[2,528,128]{2,1,0:T(8,128)(2,1)S(1)} collective-permute-done((bf16[2,528,128]{2,1,0:T(8,128)(2,1)S(1)}, bf16[2,528,128]{2,1,0:T(8,128)(2,1)S(1)}, u32[]{:S(2)}, u32[]{:S(2)}) %collective-permute-start.18) | collective-permute-done | bytes 270368 | tf_op jit(solution)/shard_map/ppermute | solution.py:446
  80.9 0.8 shard_map.87
  81.7 0.4 collective-permute-start.19
  82.1 0.8 shard_map.95
  82.9 1.7 %collective-permute-start.26 = (bf16[2,528,128]{2,1,0:T(8,128)(2,1)S(1)}, bf16[2,528,128]{2,1,0:T(8,128)(2,1)S(1)}, u32[]{:S(2)}, u32[]{:S(2)}) collective-permute-start(bf16[2,528,128]{2,1,0:T(8,128)(2,1)S(1)} %shard_map.95), channel_id=1, source_target_pairs={{0,2},{4,0},{8,4},{12,8},{14,12},{10,14},{6,10},{2,6},{1,3},{5,1},... | collective-permute-start | bytes 811016 | tf_op jit(solution)/shard_map/ppermute | solution.py:446
  84.6 0.8 collective-permute-done.15.in_ref
  85.3 0.8 shard_map.84
  86.1 1.6 %collective-permute-start.16 = (bf16[2,528,128]{2,1,0:T(8,128)(2,1)S(1)}, bf16[2,528,128]{2,1,0:T(8,128)(2,1)S(1)}, u32[]{:S(2)}, u32[]{:S(2)}) collective-permute-start(bf16[2,528,128]{2,1,0:T(8,128)(2,1)S(1)} %shard_map.84), channel_id=1, source_target_pairs={{0,2},{4,0},{8,4},{12,8},{14,12},{10,14},{6,10},{2,6},{1,3},{5,1},... | collective-permute-start | bytes 811016 | tf_op jit(solution)/shard_map/ppermute | solution.py:446
  87.7 0.8 shard_map.92
  88.5 0.5 collective-permute-start.23
  89.0 3.4 %collective-permute-done.19.in_ref = bf16[2,528,128]{2,1,0:T(8,128)(2,1)S(1)} collective-permute-done((bf16[2,528,128]{2,1,0:T(8,128)(2,1)S(1)}, bf16[2,528,128]{2,1,0:T(8,128)(2,1)S(1)}, u32[]{:S(2)}, u32[]{:S(2)}) %collective-permute-start.19) | collective-permute-done | bytes 270368 | tf_op jit(solution)/shard_map/ppermute | solution.py:446
  92.4 0.8 shard_map.88
  93.3 0.4 collective-permute-start.20
  93.7 0.8 shard_map.96
  94.5 1.7 %collective-permute-start.27 = (bf16[2,528,128]{2,1,0:T(8,128)(2,1)S(1)}, bf16[2,528,128]{2,1,0:T(8,128)(2,1)S(1)}, u32[]{:S(2)}, u32[]{:S(2)}) collective-permute-start(bf16[2,528,128]{2,1,0:T(8,128)(2,1)S(1)} %shard_map.96), channel_id=1, source_target_pairs={{0,2},{4,0},{8,4},{12,8},{14,12},{10,14},{6,10},{2,6},{1,3},{5,1},... | collective-permute-start | bytes 811016 | tf_op jit(solution)/shard_map/ppermute | solution.py:446
  96.2 1.8 %collective-permute-done.16.in_ref = bf16[2,528,128]{2,1,0:T(8,128)(2,1)S(1)} collective-permute-done((bf16[2,528,128]{2,1,0:T(8,128)(2,1)S(1)}, bf16[2,528,128]{2,1,0:T(8,128)(2,1)S(1)}, u32[]{:S(2)}, u32[]{:S(2)}) %collective-permute-start.16) | collective-permute-done | bytes 270368 | tf_op jit(solution)/shard_map/ppermute | solution.py:446
  97.9 0.8 shard_map.85
  98.8 1.4 %collective-permute-start.17 = (bf16[2,528,128]{2,1,0:T(8,128)(2,1)S(1)}, bf16[2,528,128]{2,1,0:T(8,128)(2,1)S(1)}, u32[]{:S(2)}, u32[]{:S(2)}) collective-permute-start(bf16[2,528,128]{2,1,0:T(8,128)(2,1)S(1)} %shard_map.85), channel_id=1, source_target_pairs={{0,2},{4,0},{8,4},{12,8},{14,12},{10,14},{6,10},{2,6},{1,3},{5,1},... | collective-permute-start | bytes 811016 | tf_op jit(solution)/shard_map/ppermute | solution.py:446
  100.1 0.8 shard_map.93
  100.9 0.7 collective-permute-start.24
  101.7 0.7 collective-permute-start.28
  102.4 6.8 %collective-permute-done.28.page_ref = bf16[1,2,64,512]{3,2,1,0:T(8,128)(2,1)S(1)} collective-permute-done((bf16[1,2,64,512]{3,2,1,0:T(8,128)(2,1)S(1)}, bf16[1,2,64,512]{3,2,1,0:T(8,128)(2,1)S(1)}, u32[]{:S(2)}, u32[]{:S(2)}) %collective-permute-start.28) | collective-permute-done | bytes 131104 | tf_op jit(solution)/shard_map/ppermute | solution.py:23
  109.1 0.7 copy-done.6
  109.8 1.6 %shard_map.99 = bf16[32,2,64,512]{3,2,1,0:T(8,128)(2,1)} custom-call(s32[1]{0:T(128)} %bitcast.9.me_ref, s32[2,128]{1,0:T(2,128)} %copy-done.5, bf16[1,2,64,512]{3,2,1,0:T(8,128)(2,1)} %copy-done.6, bf16[32,2,64,512]{3,2,1,0:T(8,128)(2,1)} %get-tuple-element.101.old_ref), custom_call_target="tpu_custom_call", output_to_operand_aliasing={{}: (3, {})} | custom-call | bytes 131072 | tf_op jit(solution)/shard_map/pallas_call | solution.py:273
  111.4 0.8 shard_map.89
  112.2 0.8 shard_map.97
  113.1 1.8 %shard_map.98 = bf16[1,64,4096]{2,1,0:T(8,128)(2,1)} custom-call(bf16[2,528,128]{2,1,0:T(8,128)(2,1)S(1)} %collective-permute-done.17.refs_0_, f32[2,512,128]{2,1,0:T(8,128)S(1)} %get-tuple-element.96.refs_1_, bf16[2,16,128]{2,1,0:T(8,128)(2,1)S(1)} %get-tuple-element.97.refs_2_, bf16[2,528,128]{2,1,0:T(8,128)(2,1)S(1)} %collective-permute-done.24.refs_3_, ...), custom_call_target="tpu_custom_call" | custom-call | flops 1605632 | bytes 3211264 | tf_op jit(solution)/shard_map/pallas_call | solution.py:344
  (55 shorter events, 0.5 us)
Async XLA Ops:
  5.5 16.8 %collective-permute-start = (bf16[64,2176]{1,0:T(8,128)(2,1)S(1)}, bf16[64,2176]{1,0:T(8,128)(2,1)S(1)}, u32[]{:S(2)}, u32[]{:S(2)}) collective-permute-start(bf16[64,2176]{1,0:T(8,128)(2,1)S(1)} %pad_maximum_fusion), channel_id=1, source_target_pairs={{0,4},{4,8},{8,12},{12,14},{14,10},{10,6},{6,2},{2,0},{1,5},{5,9},... | collective-permute-start | bytes 835592 | tf_op jit(solution)/shard_map/ppermute | solution.py:401
  8.6 13.7 %collective-permute-start.2 = (bf16[64,2176]{1,0:T(8,128)(2,1)S(1)}, bf16[64,2176]{1,0:T(8,128)(2,1)S(1)}, u32[]{:S(2)}, u32[]{:S(2)}) collective-permute-start(bf16[64,2176]{1,0:T(8,128)(2,1)S(1)} %pad_maximum_fusion), channel_id=1, source_target_pairs={{0,2},{4,0},{8,4},{12,8},{14,12},{10,14},{6,10},{2,6},{1,3},{5,1},... | collective-permute-start | bytes 835592 | tf_op jit(solution)/shard_map/ppermute | solution.py:402
  8.6 12.2 %collective-permute-start.1 = (bf16[64,2048]{1,0:T(8,128)(2,1)S(1)}, bf16[64,2048]{1,0:T(8,128)(2,1)S(1)}, u32[]{:S(2)}, u32[]{:S(2)}) collective-permute-start(bf16[64,2048]{1,0:T(8,128)(2,1)S(1)} %get-tuple-element.104), channel_id=1, source_target_pairs={{0,4},{4,8},{8,12},{12,14},{14,10},{10,6},{6,2},{2,0},{1,5},{5,9},... | collective-permute-start | bytes 786440 | tf_op jit(solution)/shard_map/ppermute | solution.py:401
  10.6 11.7 %collective-permute-start.3 = (bf16[64,2048]{1,0:T(8,128)(2,1)S(1)}, bf16[64,2048]{1,0:T(8,128)(2,1)S(1)}, u32[]{:S(2)}, u32[]{:S(2)}) collective-permute-start(bf16[64,2048]{1,0:T(8,128)(2,1)S(1)} %get-tuple-element.104), channel_id=1, source_target_pairs={{0,2},{4,0},{8,4},{12,8},{14,12},{10,14},{6,10},{2,6},{1,3},{5,1},... | collective-permute-start | bytes 786440 | tf_op jit(solution)/shard_map/ppermute | solution.py:402
  10.6 2.2 %copy-start = (bf16[32,2,64,512]{3,2,1,0:T(8,128)(2,1)S(1)}, bf16[32,2,64,512]{3,2,1,0:T(8,128)(2,1)}, u32[]{:S(2)}) copy-start(bf16[32,2,64,512]{3,2,1,0:T(8,128)(2,1)} %refs_3_.3) | copy-start | bytes 12582916
  12.8 1.0 copy-start.2
  13.8 0.9 copy-start.3
  22.3 13.2 %collective-permute-start.6 = (bf16[64,2176]{1,0:T(8,128)(2,1)S(1)}, bf16[64,2176]{1,0:T(8,128)(2,1)S(1)}, u32[]{:S(2)}, u32[]{:S(2)}) collective-permute-start(bf16[64,2176]{1,0:T(8,128)(2,1)S(1)} %collective-permute-done.2.refs_3_), channel_id=1, source_target_pairs={{0,2},{4,0},{8,4},{12,8},{14,12},{10,14},{6,10},{2,6},{1,3},{5,1},... | collective-permute-start | bytes 835592 | tf_op jit(solution)/shard_map/ppermute | solution.py:402
  22.8 12.7 %collective-permute-start.4 = (bf16[64,2176]{1,0:T(8,128)(2,1)S(1)}, bf16[64,2176]{1,0:T(8,128)(2,1)S(1)}, u32[]{:S(2)}, u32[]{:S(2)}) collective-permute-start(bf16[64,2176]{1,0:T(8,128)(2,1)S(1)} %collective-permute-done.refs_1_), channel_id=1, source_target_pairs={{0,4},{4,8},{8,12},{12,14},{14,10},{10,6},{6,2},{2,0},{1,5},{5,9},... | collective-permute-start | bytes 835592 | tf_op jit(solution)/shard_map/ppermute | solution.py:401
  24.3 11.1 %collective-permute-start.5 = (bf16[64,2048]{1,0:T(8,128)(2,1)S(1)}, bf16[64,2048]{1,0:T(8,128)(2,1)S(1)}, u32[]{:S(2)}, u32[]{:S(2)}) collective-permute-start(bf16[64,2048]{1,0:T(8,128)(2,1)S(1)} %collective-permute-done.1.refs_2_), channel_id=1, source_target_pairs={{0,4},{4,8},{8,12},{12,14},{14,10},{10,6},{6,2},{2,0},{1,5},{5,9},... | collective-permute-start | bytes 786440 | tf_op jit(solution)/shard_map/ppermute | solution.py:401
  25.9 9.6 %collective-permute-start.7 = (bf16[64,2048]{1,0:T(8,128)(2,1)S(1)}, bf16[64,2048]{1,0:T(8,128)(2,1)S(1)}, u32[]{:S(2)}, u32[]{:S(2)}) collective-permute-start(bf16[64,2048]{1,0:T(8,128)(2,1)S(1)} %collective-permute-done.3.refs_4_), channel_id=1, source_target_pairs={{0,2},{4,0},{8,4},{12,8},{14,12},{10,14},{6,10},{2,6},{1,3},{5,1},... | collective-permute-start | bytes 786440 | tf_op jit(solution)/shard_map/ppermute | solution.py:402
  35.5 14.0 %collective-permute-start.10 = (bf16[64,2176]{1,0:T(8,128)(2,1)S(1)}, bf16[64,2176]{1,0:T(8,128)(2,1)S(1)}, u32[]{:S(2)}, u32[]{:S(2)}) collective-permute-start(bf16[64,2176]{1,0:T(8,128)(2,1)S(1)} %collective-permute-done.6.refs_3_), channel_id=1, source_target_pairs={{0,2},{4,0},{8,4},{12,8},{14,12},{10,14},{6,10},{2,6},{1,3},{5,1},... | collective-permute-start | bytes 835592 | tf_op jit(solution)/shard_map/ppermute | solution.py:402
  37.1 12.4 %collective-permute-start.8 = (bf16[64,2176]{1,0:T(8,128)(2,1)S(1)}, bf16[64,2176]{1,0:T(8,128)(2,1)S(1)}, u32[]{:S(2)}, u32[]{:S(2)}) collective-permute-start(bf16[64,2176]{1,0:T(8,128)(2,1)S(1)} %collective-permute-done.4.refs_1_), channel_id=1, source_target_pairs={{0,4},{4,8},{8,12},{12,14},{14,10},{10,6},{6,2},{2,0},{1,5},{5,9},... | collective-permute-start | bytes 835592 | tf_op jit(solution)/shard_map/ppermute | solution.py:401
  37.6 11.9 %collective-permute-start.9 = (bf16[64,2048]{1,0:T(8,128)(2,1)S(1)}, bf16[64,2048]{1,0:T(8,128)(2,1)S(1)}, u32[]{:S(2)}, u32[]{:S(2)}) collective-permute-start(bf16[64,2048]{1,0:T(8,128)(2,1)S(1)} %collective-permute-done.5.refs_2_), channel_id=1, source_target_pairs={{0,4},{4,8},{8,12},{12,14},{14,10},{10,6},{6,2},{2,0},{1,5},{5,9},... | collective-permute-start | bytes 786440 | tf_op jit(solution)/shard_map/ppermute | solution.py:401
  39.0 10.5 %collective-permute-start.11 = (bf16[64,2048]{1,0:T(8,128)(2,1)S(1)}, bf16[64,2048]{1,0:T(8,128)(2,1)S(1)}, u32[]{:S(2)}, u32[]{:S(2)}) collective-permute-start(bf16[64,2048]{1,0:T(8,128)(2,1)S(1)} %collective-permute-done.7.refs_4_), channel_id=1, source_target_pairs={{0,2},{4,0},{8,4},{12,8},{14,12},{10,14},{6,10},{2,6},{1,3},{5,1},... | collective-permute-start | bytes 786440 | tf_op jit(solution)/shard_map/ppermute | solution.py:402
  39.6 19.7 %copy-start.5 = (s32[2,128]{1,0:T(2,128)}, s32[2,128]{1,0:T(2,128)S(1)}, u32[]{:S(2)}) copy-start(s32[2,128]{1,0:T(2,128)S(1)} %maximum_convert_fusion.1.refs_0_.lists_ref) | copy-start | bytes 3076
  47.4 12.0 %copy-start.1 = (bf16[32,2,64,512]{3,2,1,0:T(8,128)(2,1)S(1)}, bf16[32,2,64,512]{3,2,1,0:T(8,128)(2,1)}, u32[]{:S(2)}) copy-start(bf16[32,2,64,512]{3,2,1,0:T(8,128)(2,1)} %refs_3_.3) | copy-start | bytes 12582916
  49.5 9.9 %collective-permute-start.12 = (bf16[64,2176]{1,0:T(8,128)(2,1)S(1)}, bf16[64,2176]{1,0:T(8,128)(2,1)S(1)}, u32[]{:S(2)}, u32[]{:S(2)}) collective-permute-start(bf16[64,2176]{1,0:T(8,128)(2,1)S(1)} %collective-permute-done.8.refs_1_), channel_id=1, source_target_pairs={{0,4},{4,8},{8,12},{12,14},{14,10},{10,6},{6,2},{2,0},{1,5},{5,9},... | collective-permute-start | bytes 835592 | tf_op jit(solution)/shard_map/ppermute | solution.py:419
  50.0 9.3 %collective-permute-start.13 = (bf16[64,2048]{1,0:T(8,128)(2,1)S(1)}, bf16[64,2048]{1,0:T(8,128)(2,1)S(1)}, u32[]{:S(2)}, u32[]{:S(2)}) collective-permute-start(bf16[64,2048]{1,0:T(8,128)(2,1)S(1)} %collective-permute-done.11.refs_4_), channel_id=1, source_target_pairs={{0,2},{4,0},{8,4},{12,8},{14,12},{10,14},{6,10},{2,6},{1,3},{5,1},... | collective-permute-start | bytes 786440 | tf_op jit(solution)/shard_map/ppermute | solution.py:420
  64.3 9.4 %collective-permute-start.14 = (bf16[2,528,128]{2,1,0:T(8,128)(2,1)S(1)}, bf16[2,528,128]{2,1,0:T(8,128)(2,1)S(1)}, u32[]{:S(2)}, u32[]{:S(2)}) collective-permute-start(bf16[2,528,128]{2,1,0:T(8,128)(2,1)S(1)} %shard_map.82), channel_id=1, source_target_pairs={{0,2},{4,0},{8,4},{12,8},{14,12},{10,14},{6,10},{2,6},{1,3},{5,1},... | collective-permute-start | bytes 811016 | tf_op jit(solution)/shard_map/ppermute | solution.py:446
  66.0 10.2 %collective-permute-start.21 = (bf16[2,528,128]{2,1,0:T(8,128)(2,1)S(1)}, bf16[2,528,128]{2,1,0:T(8,128)(2,1)S(1)}, u32[]{:S(2)}, u32[]{:S(2)}) collective-permute-start(bf16[2,528,128]{2,1,0:T(8,128)(2,1)S(1)} %shard_map.90), channel_id=1, source_target_pairs={{0,4},{4,8},{8,12},{12,14},{14,10},{10,6},{6,2},{2,0},{1,5},{5,9},... | collective-permute-start | bytes 811016 | tf_op jit(solution)/shard_map/ppermute | solution.py:446
  66.5 14.3 %collective-permute-start.18 = (bf16[2,528,128]{2,1,0:T(8,128)(2,1)S(1)}, bf16[2,528,128]{2,1,0:T(8,128)(2,1)S(1)}, u32[]{:S(2)}, u32[]{:S(2)}) collective-permute-start(bf16[2,528,128]{2,1,0:T(8,128)(2,1)S(1)} %shard_map.86), channel_id=1, source_target_pairs={{0,4},{4,8},{8,12},{12,14},{14,10},{10,6},{6,2},{2,0},{1,5},{5,9},... | collective-permute-start | bytes 811016 | tf_op jit(solution)/shard_map/ppermute | solution.py:446
  67.3 14.8 %collective-permute-start.25 = (bf16[2,528,128]{2,1,0:T(8,128)(2,1)S(1)}, bf16[2,528,128]{2,1,0:T(8,128)(2,1)S(1)}, u32[]{:S(2)}, u32[]{:S(2)}) collective-permute-start(bf16[2,528,128]{2,1,0:T(8,128)(2,1)S(1)} %shard_map.94), channel_id=1, source_target_pairs={{0,2},{4,0},{8,4},{12,8},{14,12},{10,14},{6,10},{2,6},{1,3},{5,1},... | collective-permute-start | bytes 811016 | tf_op jit(solution)/shard_map/ppermute | solution.py:446
  74.5 10.8 %collective-permute-start.15 = (bf16[2,528,128]{2,1,0:T(8,128)(2,1)S(1)}, bf16[2,528,128]{2,1,0:T(8,128)(2,1)S(1)}, u32[]{:S(2)}, u32[]{:S(2)}) collective-permute-start(bf16[2,528,128]{2,1,0:T(8,128)(2,1)S(1)} %shard_map.83), channel_id=1, source_target_pairs={{0,2},{4,0},{8,4},{12,8},{14,12},{10,14},{6,10},{2,6},{1,3},{5,1},... | collective-permute-start | bytes 811016 | tf_op jit(solution)/shard_map/ppermute | solution.py:446
  77.0 10.7 %collective-permute-start.22 = (bf16[2,528,128]{2,1,0:T(8,128)(2,1)S(1)}, bf16[2,528,128]{2,1,0:T(8,128)(2,1)S(1)}, u32[]{:S(2)}, u32[]{:S(2)}) collective-permute-start(bf16[2,528,128]{2,1,0:T(8,128)(2,1)S(1)} %shard_map.91), channel_id=1, source_target_pairs={{0,4},{4,8},{8,12},{12,14},{14,10},{10,6},{6,2},{2,0},{1,5},{5,9},... | collective-permute-start | bytes 811016 | tf_op jit(solution)/shard_map/ppermute | solution.py:446
  81.7 10.8 %collective-permute-start.19 = (bf16[2,528,128]{2,1,0:T(8,128)(2,1)S(1)}, bf16[2,528,128]{2,1,0:T(8,128)(2,1)S(1)}, u32[]{:S(2)}, u32[]{:S(2)}) collective-permute-start(bf16[2,528,128]{2,1,0:T(8,128)(2,1)S(1)} %shard_map.87), channel_id=1, source_target_pairs={{0,4},{4,8},{8,12},{12,14},{14,10},{10,6},{6,2},{2,0},{1,5},{5,9},... | collective-permute-start | bytes 811016 | tf_op jit(solution)/shard_map/ppermute | solution.py:446
  82.9 10.8 %collective-permute-start.26 = (bf16[2,528,128]{2,1,0:T(8,128)(2,1)S(1)}, bf16[2,528,128]{2,1,0:T(8,128)(2,1)S(1)}, u32[]{:S(2)}, u32[]{:S(2)}) collective-permute-start(bf16[2,528,128]{2,1,0:T(8,128)(2,1)S(1)} %shard_map.95), channel_id=1, source_target_pairs={{0,2},{4,0},{8,4},{12,8},{14,12},{10,14},{6,10},{2,6},{1,3},{5,1},... | collective-permute-start | bytes 811016 | tf_op jit(solution)/shard_map/ppermute | solution.py:446
  86.1 15.5 %copy-start.4 = (bf16[1,2,64,512]{3,2,1,0:T(8,128)(2,1)S(1)}, bf16[1,2,64,512]{3,2,1,0:T(8,128)(2,1)}, u32[]{:S(2)}) copy-start(bf16[1,2,64,512]{3,2,1,0:T(8,128)(2,1)} %param.7) | copy-start | bytes 393220
  86.1 11.8 %collective-permute-start.16 = (bf16[2,528,128]{2,1,0:T(8,128)(2,1)S(1)}, bf16[2,528,128]{2,1,0:T(8,128)(2,1)S(1)}, u32[]{:S(2)}, u32[]{:S(2)}) collective-permute-start(bf16[2,528,128]{2,1,0:T(8,128)(2,1)S(1)} %shard_map.84), channel_id=1, source_target_pairs={{0,2},{4,0},{8,4},{12,8},{14,12},{10,14},{6,10},{2,6},{1,3},{5,1},... | collective-permute-start | bytes 811016 | tf_op jit(solution)/shard_map/ppermute | solution.py:446
  88.5 11.6 %collective-permute-start.23 = (bf16[2,528,128]{2,1,0:T(8,128)(2,1)S(1)}, bf16[2,528,128]{2,1,0:T(8,128)(2,1)S(1)}, u32[]{:S(2)}, u32[]{:S(2)}) collective-permute-start(bf16[2,528,128]{2,1,0:T(8,128)(2,1)S(1)} %shard_map.92), channel_id=1, source_target_pairs={{0,4},{4,8},{8,12},{12,14},{14,10},{10,6},{6,2},{2,0},{1,5},{5,9},... | collective-permute-start | bytes 811016 | tf_op jit(solution)/shard_map/ppermute | solution.py:446
  93.3 18.1 %collective-permute-start.20 = (bf16[2,528,128]{2,1,0:T(8,128)(2,1)S(1)}, bf16[2,528,128]{2,1,0:T(8,128)(2,1)S(1)}, u32[]{:S(2)}, u32[]{:S(2)}) collective-permute-start(bf16[2,528,128]{2,1,0:T(8,128)(2,1)S(1)} %shard_map.88), channel_id=1, source_target_pairs={{0,4},{4,8},{8,12},{12,14},{14,10},{10,6},{6,2},{2,0},{1,5},{5,9},... | collective-permute-start | bytes 811016 | tf_op jit(solution)/shard_map/ppermute | solution.py:446
  94.5 17.7 %collective-permute-start.27 = (bf16[2,528,128]{2,1,0:T(8,128)(2,1)S(1)}, bf16[2,528,128]{2,1,0:T(8,128)(2,1)S(1)}, u32[]{:S(2)}, u32[]{:S(2)}) collective-permute-start(bf16[2,528,128]{2,1,0:T(8,128)(2,1)S(1)} %shard_map.96), channel_id=1, source_target_pairs={{0,2},{4,0},{8,4},{12,8},{14,12},{10,14},{6,10},{2,6},{1,3},{5,1},... | collective-permute-start | bytes 811016 | tf_op jit(solution)/shard_map/ppermute | solution.py:446
  98.8 14.3 %collective-permute-start.17 = (bf16[2,528,128]{2,1,0:T(8,128)(2,1)S(1)}, bf16[2,528,128]{2,1,0:T(8,128)(2,1)S(1)}, u32[]{:S(2)}, u32[]{:S(2)}) collective-permute-start(bf16[2,528,128]{2,1,0:T(8,128)(2,1)S(1)} %shard_map.85), channel_id=1, source_target_pairs={{0,2},{4,0},{8,4},{12,8},{14,12},{10,14},{6,10},{2,6},{1,3},{5,1},... | collective-permute-start | bytes 811016 | tf_op jit(solution)/shard_map/ppermute | solution.py:446
  100.9 12.1 %collective-permute-start.24 = (bf16[2,528,128]{2,1,0:T(8,128)(2,1)S(1)}, bf16[2,528,128]{2,1,0:T(8,128)(2,1)S(1)}, u32[]{:S(2)}, u32[]{:S(2)}) collective-permute-start(bf16[2,528,128]{2,1,0:T(8,128)(2,1)S(1)} %shard_map.93), channel_id=1, source_target_pairs={{0,4},{4,8},{8,12},{12,14},{14,10},{10,6},{6,2},{2,0},{1,5},{5,9},... | collective-permute-start | bytes 811016 | tf_op jit(solution)/shard_map/ppermute | solution.py:446
  101.7 7.5 %collective-permute-start.28 = (bf16[1,2,64,512]{3,2,1,0:T(8,128)(2,1)S(1)}, bf16[1,2,64,512]{3,2,1,0:T(8,128)(2,1)S(1)}, u32[]{:S(2)}, u32[]{:S(2)}) collective-permute-start(bf16[1,2,64,512]{3,2,1,0:T(8,128)(2,1)S(1)} %copy-done.4), channel_id=1, source_target_pairs={{8,0},{10,2},{12,4},{14,6},{0,8},{2,10},{4,12},{6,14},{9,1},{11,3}... | collective-permute-start | bytes 393224 | tf_op jit(solution)/shard_map/ppermute | solution.py:23
  109.1 0.7 copy-start.6

commit v3 on v2

--- a/solution.py
+++ b/solution.py
@@ -123,16 +123,18 @@
 
 
 def pack_stats(top, total):
-    lane = iota((HEAD_SIZE, HEAD_SIZE), 1)
+    diagonal = iota((HEAD_SIZE, HEAD_SIZE), 0) == iota((HEAD_SIZE, HEAD_SIZE), 1)
     row = iota((STAT_ROWS, HEAD_SIZE), 0)
-    col = iota((STAT_ROWS, HEAD_SIZE), 1)
     tile = jnp.zeros((STAT_ROWS, HEAD_SIZE), jnp.float32)
+
+    def along(x):
+        return jnp.sum(jnp.where(diagonal, x, 0.0), 0, keepdims=True)
+
     for j, (m, l) in enumerate(zip(top, total)):
+        l = along(l)
         high = l.astype(jnp.bfloat16).astype(jnp.float32)
-        low = l - high
-        mixed = jnp.where(lane == 0, m, jnp.where(lane == 1, high, low)).astype(jnp.bfloat16)
-        pick = ((row == col * 4 + j) & (col < 3)).astype(jnp.float32).astype(jnp.bfloat16)
-        tile = tile + dot_nt(pick, mixed)
+        for t, x in enumerate((along(m), high, l - high)):
+            tile = jnp.where(row == 4 * t + j, x, tile)
     return tile.astype(jnp.bfloat16)
 
 
@@ -149,26 +151,6 @@
     wide = jnp.dot(turned, spread, preferred_element_type=jnp.float32)
     part = lambda b: wide[:, b * HEAD_SIZE:(b + 1) * HEAD_SIZE]
     return [part(2 * j) for j in range(4)], [part(2 * j + 1) for j in range(4)]
-
-
-def partial_rows(q, k, v, live, own, factor):
-    s = dot_nt(q, k)
-    s = jnp.where(live, s, DEAD)
-    top = jnp.max(s, axis=-1, keepdims=True)
-    if own is not None:
-        k_own, v_own, causal = own
-        s_own = jnp.where(causal, dot_nt(q, k_own), DEAD)
-        top = jnp.maximum(top, jnp.max(s_own, axis=-1, keepdims=True))
-    top = jnp.maximum(top * factor, FLOOR).astype(jnp.bfloat16).astype(jnp.float32)
-    p = jnp.exp2(s * factor - top).astype(jnp.bfloat16)
-    ones = jnp.ones((k.shape[0], HEAD_SIZE), jnp.bfloat16)
-    out = jnp.dot(p, jnp.concatenate([v, ones], 1), preferred_element_type=jnp.float32)
-    if own is not None:
-        p = jnp.exp2(s_own * factor - top).astype(jnp.bfloat16)
-        ones = jnp.ones((k_own.shape[0], HEAD_SIZE), jnp.bfloat16)
-        out = out + jnp.dot(p, jnp.concatenate([v_own, ones], 1), preferred_element_type=jnp.float32)
-    top = jnp.broadcast_to(top, (q.shape[0], HEAD_SIZE))
-    return out[:, :HEAD_SIZE], top, out[:, HEAD_SIZE:]
 
 
 def attend_kernel(sizes, parts, own, *refs):
@@ -180,7 +162,9 @@
     pages = refs.pop(0)
     outs = [(refs.pop(0), refs.pop(0)) for _ in parts]
     stored = refs.pop(0) if own else None
-    held, sems = refs[:2]
+    held, sems, scores = refs[:3]
+    if own:
+        late_scores, store_sem = refs[3:]
     copies = [
         [
             pltpu.make_async_copy(pages.at[meta[n, c]], held.at[n, c], sems.at[n, c])
@@ -192,33 +176,60 @@
         for copy in request:
             copy.start()
     if own:
-        keep = pltpu.make_async_copy(pages, stored, refs[2])
+        keep = pltpu.make_async_copy(pages, stored, store_sem)
         keep.start()
     factor = HEAD_SIZE ** (-0.5) * LOG2E
     keys = cap * page_len
-    for n, halves in enumerate(queries):
-        for copy in copies[n]:
-            copy.wait()
+    rows = groups * suffix
+    jobs = [(n, h) for n in range(len(parts)) for h in range(kv_heads)]
+
+    def lanes(h):
+        return slice(h * HEAD_SIZE, (h + 1) * HEAD_SIZE)
+
+    def score(i):
+        n, h = jobs[i]
+        if h == 0:
+            for copy in copies[n]:
+                copy.wait()
+        heads_each = kv_heads // len(queries[n])
+        q_ref, first = queries[n][h // heads_each], (h % heads_each) * groups
+        q = jnp.concatenate([q_ref[:, block_of(first + g)] for g in range(groups)], 0)
+        k = held[n, :, 0, :, lanes(h)].reshape(keys, HEAD_SIZE)
+        scores[i % 2, :, :keys] = dot_nt(q, k)
+        if own:
+            at = iota((rows, suffix), 0) % suffix
+            causal = iota((rows, suffix), 1) <= at
+            late_scores[i % 2] = jnp.where(causal, dot_nt(q, own_kv[0, :, lanes(h)]), DEAD)
+
+    def weigh(i):
+        n, h = jobs[i]
         live = iota((1, keys), 1) < meta[n, cap] * page_len
-        heads_each = kv_heads // len(halves)
+        s = jnp.where(live, scores[i % 2], DEAD)
+        top = jnp.max(s, axis=-1, keepdims=True)
+        if own:
+            top = jnp.maximum(top, jnp.max(late_scores[i % 2], axis=-1, keepdims=True))
+        top = jnp.maximum(top * factor, FLOOR).astype(jnp.bfloat16).astype(jnp.float32)
+        p = jnp.exp2(s * factor - top).astype(jnp.bfloat16)
+        v = held[n, :, 1, :, lanes(h)].reshape(keys, HEAD_SIZE)
+        v = jnp.concatenate([v, jnp.ones_like(v)], 1)
+        out = jnp.dot(p, v, preferred_element_type=jnp.float32)
+        if own:
+            p = jnp.exp2(late_scores[i % 2] * factor - top).astype(jnp.bfloat16)
+            v = own_kv[1, :, lanes(h)]
+            v = jnp.concatenate([v, jnp.ones_like(v)], 1)
+            out = out + jnp.dot(p, v, preferred_element_type=jnp.float32)
         acc_ref, stat_ref = outs[n]
-        for h in range(kv_heads):
-            q_ref = halves[h // heads_each]
-            first = (h % heads_each) * groups
-            lanes = slice(h * HEAD_SIZE, (h + 1) * HEAD_SIZE)
-            k = held[n, :, 0, :, lanes].reshape(keys, HEAD_SIZE)
-            v = held[n, :, 1, :, lanes].reshape(keys, HEAD_SIZE)
-            rows = groups * suffix
-            q = jnp.concatenate([q_ref[:, block_of(first + g)] for g in range(groups)], 0)
-            extra = None
-            if own:
-                at = iota((rows, suffix), 0) % suffix
-                causal = iota((rows, suffix), 1) <= at
-                extra = (own_kv[0, :, lanes], own_kv[1, :, lanes], causal)
-            acc, top, total = partial_rows(q, k, v, live, extra, factor)
-            acc_ref[h] = acc
-            blocks = [block_of(j) for j in range(rows // HEAD_SIZE)]
-            stat_ref[h] = pack_stats([top[j] for j in blocks], [total[j] for j in blocks])
+        acc_ref[h] = out[:, :HEAD_SIZE]
+        total = out[:, HEAD_SIZE:]
+        top = jnp.broadcast_to(top, total.shape)
+        blocks = [block_of(j) for j in range(rows // HEAD_SIZE)]
+        stat_ref[h] = pack_stats([top[j] for j in blocks], [total[j] for j in blocks])
+
+    for i in range(len(jobs) + 1):
+        if i < len(jobs):
+            score(i)
+        if i > 0:
+            weigh(i - 1)
     if own:
         keep.wait()
 
@@ -238,11 +249,13 @@
     scratch = [
         pltpu.VMEM((count, cap) + kv_pages.shape[1:], jnp.bfloat16),
         pltpu.SemaphoreType.DMA((count, cap)),
+        pltpu.VMEM((2, rows, keys), jnp.float32),
     ]
     specs = [VMEM] * len(shapes)
     if own:
         shapes.append(jax.ShapeDtypeStruct(kv_pages.shape, kv_pages.dtype))
         specs.append(HBM)
+        scratch.append(pltpu.VMEM((2, rows, suffix), jnp.float32))
         scratch.append(pltpu.SemaphoreType.DMA)
     out = pl.pallas_call(
         functools.partial(attend_kernel, sizes, parts, own),
@@ -351,6 +364,48 @@
     )(*args)
 
 
+def prepare_kernel(cut, cap, pages_dev, length_ref, slot_ref, table_ref, q_ref, first_ref, second_ref):
+    maxp = table_ref.shape[1]
+    suffix = q_ref.shape[1]
+    second_ref[...] = q_ref[0, :, cut:]
+    first_ref[:, :cut] = q_ref[0, :, :cut]
+    table = table_ref[...]
+    owner = lax.div(table, pages_dev)
+    local = (table - owner * pages_dev).astype(jnp.float32)
+    owner = owner.astype(jnp.float32)
+    down, along = iota((maxp, maxp), 0), iota((maxp, maxp), 1)
+
+    def turned(x):
+        return jnp.sum(jnp.where(down == along, x, 0.0), 1, keepdims=True)
+
+    before = (turned(owner) == owner) & (along < down)
+    rank = jnp.sum(jnp.where(before, 1.0, 0.0), 1, keepdims=True)
+    place = iota((maxp, HEAD_SIZE), 1)
+    live = jnp.where(iota((maxp, HEAD_SIZE), 0) < length_ref[0], 1.0, 0.0)
+    ids = jnp.where(rank == place.astype(jnp.float32), turned(local), 0.0)
+    fields = jnp.where(place < cap, ids, jnp.where(place == cap, live, 0.0))
+    owned = jnp.where(owner == iota((suffix, maxp), 0).astype(jnp.float32), 1.0, 0.0)
+    lists = jnp.dot(
+        owned.astype(jnp.bfloat16), fields.astype(jnp.bfloat16), preferred_element_type=jnp.float32
+    )
+    slot = slot_ref[0].astype(jnp.float32)
+    lists = jnp.where(iota(lists.shape, 1) == cap + 1, slot, lists)
+    first_ref[:, cut:] = lists.astype(jnp.bfloat16)
+
+
+def prepare(cut, cap, pages_dev, queries, page_table, prefix_pages, new_slots):
+    suffix, columns = queries.shape[1:]
+    return pl.pallas_call(
+        functools.partial(prepare_kernel, cut, cap, pages_dev),
+        out_shape=[
+            jax.ShapeDtypeStruct((suffix, cut + HEAD_SIZE), queries.dtype),
+            jax.ShapeDtypeStruct((suffix, columns - cut), queries.dtype),
+        ],
+        in_specs=[SMEM, SMEM, VMEM, VMEM],
+        out_specs=[VMEM, VMEM],
+    )(prefix_pages, new_slots, page_table, queries)
+
+
 def queries_travel(queries, suffix_key_value, kv_pages, page_table, prefix_pages, new_slots):
     stores = lax.axis_size("store")
     pages_dev, _, page_len, width = kv_pages.shape
@@ -367,26 +422,9 @@
     up = [(order[i], order[(i + 1) % stores]) for i in range(stores)]
     down = [(order[i], order[i - 1]) for i in range(stores)]
 
-    table, length = page_table[0], prefix_pages[0]
-    entries = jnp.arange(maxp, dtype=jnp.int32)
-    owners = table // pages_dev
-    before = (owners[:, None] == owners[None, :]) & (entries[:, None] < entries[None, :])
-    rank = jnp.sum(before.astype(jnp.int32), 0)
-    place = jnp.arange(HEAD_SIZE, dtype=jnp.int32)
-    field = jnp.where(place[:, None] < cap, rank[None, :] == place[:, None], place[:, None] == cap)
-    value = jnp.where(
-        place[:, None] < cap, (table % pages_dev)[None], (entries < length).astype(jnp.int32)[None]
-    )
-    owned = owners[None, :] == jnp.arange(suffix, dtype=jnp.int32)[:, None]
-    lists = jnp.sum(jnp.where(owned[:, None, :] & field[None], value[None], 0), -1)
-    lists = jnp.where(place[None, :] == cap + 1, new_slots[0], lists)
-
     heads_each = kv_heads // 2
     cut = heads_each * groups * HEAD_SIZE
-    mine = [
-        jnp.concatenate([queries[0, :, :cut], lists.astype(queries.dtype)], 1),
-        queries[0, :, cut:],
-    ]
+    mine = prepare(cut, cap, pages_dev, queries, page_table, prefix_pages, new_slots)
 
     def listed(*arrays):
         rows = [lax.dynamic_slice(x, (me, cut), (1, HEAD_SIZE)) for x in arrays]
@@ -403,8 +441,8 @@
         if step == 1:
             partials[0], store = attend(
                 sizes,
-                lax.dynamic_slice(lists, (me, 0), (1, HEAD_SIZE)),
-                [[queries[0]]],
+                listed(mine[0]),
+                [mine],
                 suffix_key_value[0],
                 kv_pages,
             )
@@ -418,10 +456,6 @@
         partials[step], partials[-step] = got
     ups[0] = lax.ppermute(ups[0], "store", up)
     downs[1] = lax.ppermute(downs[1], "store", down)
-    (ups, downs), (partials[half - 1], partials[1 - half]) = after(
-        (ups, downs), (partials[half - 1], partials[1 - half])
-    )
-    (far,) = attend(sizes, listed(ups[0]), [[ups[0], downs[1]]], None, kv_pages)
 
     rows_head = groups * suffix
     wire = jax.ShapeDtypeStruct((heads_each, rows_head + STAT_ROWS, HEAD_SIZE), jnp.bfloat16)
@@ -434,21 +468,44 @@
             functools.partial(merge_kernel, side * heads_each, heads_each), wire, block, *part
         )
 
-    late, early = {}, {}
-    blocks = {}
-    for side, sign in ((0, 1), (1, -1)):
-        blocks[side, sign] = packed(far, side), half
-        blocks[1 - side, sign] = packed(partials[sign * (half - 1)], 1 - side), half - 1
-    for (side, sign), (block, distance) in blocks.items():
-        route = down if sign == 1 else up
-        first = distance
-        while True:
-            block = lax.ppermute(block, "store", route)
-            distance -= 1
-            if distance == 0:
-                break
-            block = merged(block, partials[sign * distance], side)
-        (late if first == half else early)[side] = block
+    routes = {1: down, -1: up}
+    nearer = {sign: packed(partials[sign * (half - 1)], side) for side, sign in ((1, 1), (0, -1))}
+    hop = {sign: lax.ppermute(block, "store", routes[sign]) for sign, block in nearer.items()}
+    page, _ = after(suffix_key_value, partials[half - 2])
+    arrived = shifted(page, "store", half)
+    (ups, downs), (_, arrived) = after((ups, downs), (nearer, arrived))
+    (far,) = attend(sizes, listed(ups[0]), [[ups[0], downs[1]]], None, kv_pages)
+    store = place_page(half, cap + 1, me[None], lists_of[stores // 4], arrived, store)
+
+    side_of = {1: {"late": 0, "early": 1}, -1: {"late": 1, "early": 0}}
+    turns = [("early", half - 1)]
+    for distance in range(half, 0, -1):
+        turns += [("late", distance)] + [("early", distance - 2)] * (distance > 2)
+    flows = {("early", sign): hop[sign] for sign in routes}
+    sent = None
+    for flow, distance in turns[1:]:
+        blocks = {}
+        if flow == "late" and distance == half:
+            far, hop = after(far, hop)
+            for sign in routes:
+                flows["early", sign] = hop[sign]
+                blocks[sign] = packed(far, side_of[sign][flow])
+        else:
+            came = {sign: flows[flow, sign] for sign in routes}
+            if distance == 1:
+                ended = {sign: flows["early", sign] for sign in routes}
+                came, ended = after(came, ended)
+                flows.update({("early", sign): ended[sign] for sign in routes})
+            came, _ = after(came, sent)
+            for sign in routes:
+                blocks[sign] = merged(
+                    came[sign], partials[sign * distance], side_of[sign][flow]
+                )
+        for sign in routes:
+            flows[flow, sign] = lax.ppermute(blocks[sign], "store", routes[sign])
+        sent = blocks
+    late = {side_of[sign]["late"]: flows["late", sign] for sign in routes}
+    early, _ = after({side_of[sign]["early"]: flows["early", sign] for sign in routes}, sent)
     kept = [
         jax.ShapeDtypeStruct((heads_each, rows_head, HEAD_SIZE), jnp.float32),
         jax.ShapeDtypeStruct((heads_each, STAT_ROWS, HEAD_SIZE), jnp.bfloat16),
@@ -466,10 +523,7 @@
         late[0], *rest[0], late[1], *rest[1],
     )
 
-    page, _ = after(suffix_key_value, partials[half - 1])
-    arrived = shifted(page, "store", half)
-    new_store = place_page(half, cap + 1, me[None], lists_of[stores // 4], arrived, store)
-    return (attended, new_store)
+    return (attended, store)
 
 
 def on_device(queries, suffix_key_value, kv_pages, page_table, prefix_pages, new_slots):

time: 117 us -> 110 us (0.940); the launches traced: 115 us -> 109 us
  Pallas kernels: 47.3 us -> 37.1 us
  waiting for transfers between devices: 26 us -> 30.3 us
  starting transfers between devices: 31 us -> 34 us
  other arithmetic: 2.46 us -> 0.73 us
    pallas_call x5, Pallas kernels: 34.1 us -> 24.1 us  [attend(): pl.pallas_call(functools.partial(attend_kernel, sizes, parts, own), out_s...]
    ppermute x1, waiting for transfers between devices: 6.78 us -> 0.01 us  [shifted(): return lax.ppermute(block, axis, route)]
    ppermute x14, waiting for transfers between devices: 14.2 us -> 20 us  [the longest x12 17.6 us: queries_travel(): flows[flow, sign] = lax.ppermute(blocks[sign], 'store', routes[sign])]
    ppermute x6, waiting for transfers between devices: 3.45 us -> 8.84 us  [queries_travel(): ups = [lax.ppermute(x, 'store', up) for x in ups]]
    ppermute x14, starting transfers between devices: 14.9 us -> 17.4 us  [the longest x12 14.6 us: queries_travel(): flows[flow, sign] = lax.ppermute(blocks[sign], 'store', routes[sign])]
    pallas_call x17, Pallas kernels: 11.6 us -> 9.35 us  [call(): pl.pallas_call(kernel, out_shape=shape, in_specs=[VMEM] * len(args), out_...]
    pallas_call x0 -> x1, Pallas kernels: none -> 2.06 us  [prepare(): pl.pallas_call(functools.partial(prepare_kernel, cut, cap, pages_dev), ou...]
  transfers between devices with their start and end apart: 29 -> 29, of which waited for: 9 -> 16; matrix products, arithmetic and copies ran while one was open for 0% -> 1% of each run, Pallas kernels for 35% -> 30%
where the time goes in v3:
time: 110 us; the launch traced here: 109 us
  Pallas kernels  37.1 us (34%)
  starting transfers between devices  34 us (31%)
  waiting for transfers between devices  30.3 us (28%)
  local copies, waits for them, and re-layouts  5.05 us (5%)
  between operations  2.19 us (2%)
    pallas_call x5, Pallas kernels, attend(): pl.pallas_call(functools.partial(attend_kernel, sizes, parts, own), out_s...  24.1 us
    ppermute x12, waiting for transfers between devices, queries_travel(): flows[flow, sign] = lax.ppermute(blocks[sign], 'store', routes[sign])  17.6 us
    ppermute x12, starting transfers between devices, queries_travel(): flows[flow, sign] = lax.ppermute(blocks[sign], 'store', routes[sign])  14.6 us
    ppermute x6, starting transfers between devices, queries_travel(): ups = [lax.ppermute(x, 'store', up) for x in ups]  10.2 us
    pallas_call x17, Pallas kernels, call(): pl.pallas_call(kernel, out_shape=shape, in_specs=[VMEM] * len(args), out_...  9.35 us
    ppermute x6, waiting for transfers between devices, queries_travel(): ups = [lax.ppermute(x, 'store', up) for x in ups]  8.84 us
    unnamed x14, local copies, waits for them, and re-layouts  5.01 us
    ppermute x6, starting transfers between devices, queries_travel(): downs = [lax.ppermute(x, 'store', down) for x in downs]  3 us
  transfers between devices with their start and end apart: 29, of which 16 were waited for; matrix products, arithmetic and copies ran while one was open for 1% of the time, Pallas kernels for 30%

profile of v3, /device:TPU:0, one launch (start us, length us, event | category | flops | bytes accessed | tf_op | source)
XLA Modules:
  0.0 109.4 jit_solution(6617526857963209330)
XLA Ops:
  1.9 2.1 %shard_map.77 = (bf16[64,2176]{1,0:T(8,128)(2,1)}, bf16[64,2048]{1,0:T(8,128)(2,1)}) custom-call(s32[1]{0:T(128)S(6)} %copy.10.length_ref, s32[1]{0:T(128)S(6)} %copy.11.slot_ref, s32[1,64]{1,0:T(1,128)} %table_ref.1, bf16[1,64,4096]{2,1,0:T(8,128)(2,1)} %q_ref.1), custom_call_target="tpu_custom_call" | custom-call | tf_op jit(solution)/shard_map/pallas_call | solution.py:398
  4.0 3.0 %collective-permute-start = (bf16[64,2176]{1,0:T(8,128)(2,1)}, bf16[64,2176]{1,0:T(8,128)(2,1)S(1)}, u32[]{:S(2)}, u32[]{:S(2)}) collective-permute-start(bf16[64,2176]{1,0:T(8,128)(2,1)} %get-tuple-element.73.refs_1_), channel_id=1, source_target_pairs={{0,4},{4,8},{8,12},{12,14},{14,10},{10,6},{6,2},{2,0},{1,5},{5,9},... | collective-permute-start | bytes 835592 | tf_op jit(solution)/shard_map/ppermute | solution.py:439
  7.0 2.0 %collective-permute-start.1 = (bf16[64,2048]{1,0:T(8,128)(2,1)}, bf16[64,2048]{1,0:T(8,128)(2,1)S(1)}, u32[]{:S(2)}, u32[]{:S(2)}) collective-permute-start(bf16[64,2048]{1,0:T(8,128)(2,1)} %get-tuple-element.74.refs_2_), channel_id=1, source_target_pairs={{0,4},{4,8},{8,12},{12,14},{14,10},{10,6},{6,2},{2,0},{1,5},{5,9},... | collective-permute-start | bytes 786440 | tf_op jit(solution)/shard_map/ppermute | solution.py:439
  9.0 0.7 fusion.refs_0_
  9.7 2.2 %copy-done = bf16[32,2,64,512]{3,2,1,0:T(8,128)(2,1)S(1)} copy-done((bf16[32,2,64,512]{3,2,1,0:T(8,128)(2,1)S(1)}, bf16[32,2,64,512]{3,2,1,0:T(8,128)(2,1)}, u32[]{:S(2)}) %copy-start) | copy-done | bytes 4194328
  11.9 1.0 copy-done.2
  12.9 0.9 copy-done.3
  13.8 0.9 copy-done.4
  14.7 4.2 %shard_map.78 = (f32[4,512,128]{2,1,0:T(8,128)S(1)}, bf16[4,16,128]{2,1,0:T(8,128)(2,1)S(1)}, bf16[32,2,64,512]{3,2,1,0:T(8,128)(2,1)}) custom-call(s32[1,128]{1,0:T(1,128)S(1)} %fusion.refs_0_, bf16[64,2176]{1,0:T(8,128)(2,1)S(1)} %copy-done.2, bf16[64,2048]{1,0:T(8,128)(2,1)S(1)} %copy-done.3, bf16[2,64,512]{2,1,0:T(8,128)(2,1)S(1)} %bitcast.2, ...), custom_call_target="tpu_custom_call" | custom-call | flops 1073741824 | bytes 2621440 | tf_op jit(solution)/shard_map/pallas_call | solution.py:260
  18.9 0.5 collective-permute-done.1.refs_2_
  19.4 1.5 %collective-permute-done.3.refs_4_ = bf16[64,2048]{1,0:T(8,128)(2,1)S(1)} collective-permute-done((bf16[64,2048]{1,0:T(8,128)(2,1)}, bf16[64,2048]{1,0:T(8,128)(2,1)S(1)}, u32[]{:S(2)}, u32[]{:S(2)}) %collective-permute-start.3) | collective-permute-done | bytes 262176 | tf_op jit(solution)/shard_map/ppermute | solution.py:440
  21.3 1.7 %collective-permute-start.4 = (bf16[64,2176]{1,0:T(8,128)(2,1)S(1)}, bf16[64,2176]{1,0:T(8,128)(2,1)S(1)}, u32[]{:S(2)}, u32[]{:S(2)}) collective-permute-start(bf16[64,2176]{1,0:T(8,128)(2,1)S(1)} %collective-permute-done.refs_1_), channel_id=1, source_target_pairs={{0,4},{4,8},{8,12},{12,14},{14,10},{10,6},{6,2},{2,0},{1,5},{5,9},... | collective-permute-start | bytes 835592 | tf_op jit(solution)/shard_map/ppermute | solution.py:439
  23.0 1.6 %collective-permute-start.5 = (bf16[64,2048]{1,0:T(8,128)(2,1)S(1)}, bf16[64,2048]{1,0:T(8,128)(2,1)S(1)}, u32[]{:S(2)}, u32[]{:S(2)}) collective-permute-start(bf16[64,2048]{1,0:T(8,128)(2,1)S(1)} %collective-permute-done.1.refs_2_), channel_id=1, source_target_pairs={{0,4},{4,8},{8,12},{12,14},{14,10},{10,6},{6,2},{2,0},{1,5},{5,9},... | collective-permute-start | bytes 786440 | tf_op jit(solution)/shard_map/ppermute | solution.py:439
  25.0 5.3 %shard_map.79 = (f32[4,512,128]{2,1,0:T(8,128)S(1)}, bf16[4,16,128]{2,1,0:T(8,128)(2,1)S(1)}, f32[4,512,128]{2,1,0:T(8,128)S(1)}, bf16[4,16,128]{2,1,0:T(8,128)(2,1)S(1)}) custom-call(s32[2,128]{1,0:T(2,128)S(1)} %maximum_convert_fusion.refs_0_, bf16[64,2176]{1,0:T(8,128)(2,1)S(1)} %collective-permute-done.refs_1_, ...), custom_call_target="tpu_custom_call" | custom-call | flops 2147483648 | bytes 5242880 | tf_op jit(solution)/shard_map/pallas_call | solution.py:260
  30.3 3.8 %collective-permute-done.5.refs_2_ = bf16[64,2048]{1,0:T(8,128)(2,1)S(1)} collective-permute-done((bf16[64,2048]{1,0:T(8,128)(2,1)S(1)}, bf16[64,2048]{1,0:T(8,128)(2,1)S(1)}, u32[]{:S(2)}, u32[]{:S(2)}) %collective-permute-start.5) | collective-permute-done | bytes 262176 | tf_op jit(solution)/shard_map/ppermute | solution.py:439
  34.2 1.6 %collective-permute-start.10 = (bf16[64,2176]{1,0:T(8,128)(2,1)S(1)}, bf16[64,2176]{1,0:T(8,128)(2,1)S(1)}, u32[]{:S(2)}, u32[]{:S(2)}) collective-permute-start(bf16[64,2176]{1,0:T(8,128)(2,1)S(1)} %collective-permute-done.6.refs_3_), channel_id=1, source_target_pairs={{0,2},{4,0},{8,4},{12,8},{14,12},{10,14},{6,10},{2,6},{1,3},{5,1},... | collective-permute-start | bytes 835592 | tf_op jit(solution)/shard_map/ppermute | solution.py:440
  35.8 0.5 collective-permute-start.8
  36.3 1.4 %collective-permute-start.9 = (bf16[64,2048]{1,0:T(8,128)(2,1)S(1)}, bf16[64,2048]{1,0:T(8,128)(2,1)S(1)}, u32[]{:S(2)}, u32[]{:S(2)}) collective-permute-start(bf16[64,2048]{1,0:T(8,128)(2,1)S(1)} %collective-permute-done.5.refs_2_), channel_id=1, source_target_pairs={{0,4},{4,8},{8,12},{12,14},{14,10},{10,6},{6,2},{2,0},{1,5},{5,9},... | collective-permute-start | bytes 786440 | tf_op jit(solution)/shard_map/ppermute | solution.py:439
  37.6 0.6 collective-permute-start.11
  38.3 5.3 %shard_map.80 = (f32[4,512,128]{2,1,0:T(8,128)S(1)}, bf16[4,16,128]{2,1,0:T(8,128)(2,1)S(1)}, f32[4,512,128]{2,1,0:T(8,128)S(1)}, bf16[4,16,128]{2,1,0:T(8,128)(2,1)S(1)}) custom-call(s32[2,128]{1,0:T(2,128)S(1)} %maximum_convert_fusion.1.refs_0_.lists_ref, bf16[64,2176]{1,0:T(8,128)(2,1)S(1)} %collective-permute-done.4.refs_1_, ...), custom_call_target="tpu_custom_call" | custom-call | flops 2147483648 | bytes 5242880 | tf_op jit(solution)/shard_map/pallas_call | solution.py:260
  43.7 4.5 %collective-permute-done.9.refs_2_ = bf16[64,2048]{1,0:T(8,128)(2,1)S(1)} collective-permute-done((bf16[64,2048]{1,0:T(8,128)(2,1)S(1)}, bf16[64,2048]{1,0:T(8,128)(2,1)S(1)}, u32[]{:S(2)}, u32[]{:S(2)}) %collective-permute-start.9) | collective-permute-done | bytes 262176 | tf_op jit(solution)/shard_map/ppermute | solution.py:439
  48.1 0.5 collective-permute-start.12
  48.7 1.5 %collective-permute-start.13 = (bf16[64,2048]{1,0:T(8,128)(2,1)S(1)}, bf16[64,2048]{1,0:T(8,128)(2,1)S(1)}, u32[]{:S(2)}, u32[]{:S(2)}) collective-permute-start(bf16[64,2048]{1,0:T(8,128)(2,1)S(1)} %collective-permute-done.11.refs_4_), channel_id=1, source_target_pairs={{0,2},{4,0},{8,4},{12,8},{14,12},{10,14},{6,10},{2,6},{1,3},{5,1},... | collective-permute-start | bytes 786440 | tf_op jit(solution)/shard_map/ppermute | solution.py:458
  50.2 1.3 %collective-permute-start.14 = (bf16[1,2,64,512]{3,2,1,0:T(8,128)(2,1)S(1)}, bf16[1,2,64,512]{3,2,1,0:T(8,128)(2,1)S(1)}, u32[]{:S(2)}, u32[]{:S(2)}) collective-permute-start(bf16[1,2,64,512]{3,2,1,0:T(8,128)(2,1)S(1)} %copy-done.4), channel_id=1, source_target_pairs={{8,0},{10,2},{12,4},{14,6},{0,8},{2,10},{4,12},{6,14},{9,1},{11,3}... | collective-permute-start | bytes 393224 | tf_op jit(solution)/shard_map/ppermute | solution.py:23
  51.6 5.6 %shard_map.81 = (f32[4,512,128]{2,1,0:T(8,128)S(1)}, bf16[4,16,128]{2,1,0:T(8,128)(2,1)S(1)}, f32[4,512,128]{2,1,0:T(8,128)S(1)}, bf16[4,16,128]{2,1,0:T(8,128)(2,1)S(1)}) custom-call(s32[2,128]{1,0:T(2,128)S(1)} %maximum_convert_fusion.2.refs_0_, bf16[64,2176]{1,0:T(8,128)(2,1)S(1)} %collective-permute-done.8.refs_1_, ...), custom_call_target="tpu_custom_call" | custom-call | flops 2147483648 | bytes 5242880 | tf_op jit(solution)/shard_map/pallas_call | solution.py:260
  57.2 1.7 %collective-permute-start.15 = (bf16[2,528,128]{2,1,0:T(8,128)(2,1)S(1)}, bf16[2,528,128]{2,1,0:T(8,128)(2,1)S(1)}, u32[]{:S(2)}, u32[]{:S(2)}) collective-permute-start(bf16[2,528,128]{2,1,0:T(8,128)(2,1)S(1)} %shard_map.82), channel_id=1, source_target_pairs={{0,4},{4,8},{8,12},{12,14},{14,10},{10,6},{6,2},{2,0},{1,5},{5,9},... | collective-permute-start | bytes 811016 | tf_op jit(solution)/shard_map/ppermute | solution.py:473
  58.9 1.2 %collective-permute-start.16 = (bf16[2,528,128]{2,1,0:T(8,128)(2,1)S(1)}, bf16[2,528,128]{2,1,0:T(8,128)(2,1)S(1)}, u32[]{:S(2)}, u32[]{:S(2)}) collective-permute-start(bf16[2,528,128]{2,1,0:T(8,128)(2,1)S(1)} %shard_map.83), channel_id=1, source_target_pairs={{0,2},{4,0},{8,4},{12,8},{14,12},{10,14},{6,10},{2,6},{1,3},{5,1},... | collective-permute-start | bytes 811016 | tf_op jit(solution)/shard_map/ppermute | solution.py:473
  60.1 3.7 %shard_map.84 = (f32[4,512,128]{2,1,0:T(8,128)S(1)}, bf16[4,16,128]{2,1,0:T(8,128)(2,1)S(1)}) custom-call(s32[1,128]{1,0:T(1,128)S(1)} %fusion.1.refs_0_, bf16[64,2176]{1,0:T(8,128)(2,1)S(1)} %collective-permute-done.12.refs_1_, bf16[64,2048]{1,0:T(8,128)(2,1)S(1)} %collective-permute-done.13.refs_2_, bf16[32,2,64,512]{3,2,1,0:T(8,128)(2,1)S(1)} %copy-done.1), custom_call_target="tpu_custom_call" | custom-call | flops 1073741824 | bytes 2621440 | tf_op jit(solution)/shard_map/pallas_call | solution.py:260
  63.8 2.4 %collective-permute-done.15.in_ref = bf16[2,528,128]{2,1,0:T(8,128)(2,1)S(1)} collective-permute-done((bf16[2,528,128]{2,1,0:T(8,128)(2,1)S(1)}, bf16[2,528,128]{2,1,0:T(8,128)(2,1)S(1)}, u32[]{:S(2)}, u32[]{:S(2)}) %collective-permute-start.15) | collective-permute-done | bytes 270368 | tf_op jit(solution)/shard_map/ppermute | solution.py:473
  66.4 2.3 %collective-permute-start.18 = (bf16[2,528,128]{2,1,0:T(8,128)(2,1)S(1)}, bf16[2,528,128]{2,1,0:T(8,128)(2,1)S(1)}, u32[]{:S(2)}, u32[]{:S(2)}) collective-permute-start(bf16[2,528,128]{2,1,0:T(8,128)(2,1)S(1)} %shard_map.86), channel_id=1, source_target_pairs={{0,2},{4,0},{8,4},{12,8},{14,12},{10,14},{6,10},{2,6},{1,3},{5,1},... | collective-permute-start | bytes 811016 | tf_op jit(solution)/shard_map/ppermute | solution.py:505
  68.6 0.6 shard_map.88
  69.3 0.6 shard_map.87
  70.0 2.0 %collective-permute-start.22 = (bf16[2,528,128]{2,1,0:T(8,128)(2,1)S(1)}, bf16[2,528,128]{2,1,0:T(8,128)(2,1)S(1)}, u32[]{:S(2)}, u32[]{:S(2)}) collective-permute-start(bf16[2,528,128]{2,1,0:T(8,128)(2,1)S(1)} %shard_map.88), channel_id=1, source_target_pairs={{0,2},{4,0},{8,4},{12,8},{14,12},{10,14},{6,10},{2,6},{1,3},{5,1},... | collective-permute-start | bytes 811016 | tf_op jit(solution)/shard_map/ppermute | solution.py:505
  72.0 2.7 %collective-permute-done.17.in_ref = bf16[2,528,128]{2,1,0:T(8,128)(2,1)S(1)} collective-permute-done((bf16[2,528,128]{2,1,0:T(8,128)(2,1)S(1)}, bf16[2,528,128]{2,1,0:T(8,128)(2,1)S(1)}, u32[]{:S(2)}, u32[]{:S(2)}) %collective-permute-start.17) | collective-permute-done | bytes 270368 | tf_op jit(solution)/shard_map/ppermute | solution.py:505
  74.7 0.6 collective-permute-done.18.in_ref
  75.4 0.6 shard_map.89
  76.0 1.0 collective-permute-start.19
  77.0 0.6 shard_map.90
  77.6 1.7 %collective-permute-start.20 = (bf16[2,528,128]{2,1,0:T(8,128)(2,1)S(1)}, bf16[2,528,128]{2,1,0:T(8,128)(2,1)S(1)}, u32[]{:S(2)}, u32[]{:S(2)}) collective-permute-start(bf16[2,528,128]{2,1,0:T(8,128)(2,1)S(1)} %shard_map.90), channel_id=1, source_target_pairs={{0,2},{4,0},{8,4},{12,8},{14,12},{10,14},{6,10},{2,6},{1,3},{5,1},... | collective-permute-start | bytes 811016 | tf_op jit(solution)/shard_map/ppermute | solution.py:505
  79.4 1.2 %collective-permute-done.21.in_ref = bf16[2,528,128]{2,1,0:T(8,128)(2,1)S(1)} collective-permute-done((bf16[2,528,128]{2,1,0:T(8,128)(2,1)S(1)}, bf16[2,528,128]{2,1,0:T(8,128)(2,1)S(1)}, u32[]{:S(2)}, u32[]{:S(2)}) %collective-permute-start.21) | collective-permute-done | bytes 270368 | tf_op jit(solution)/shard_map/ppermute | solution.py:505
  80.5 0.6 collective-permute-done.22.in_ref
  81.2 0.6 shard_map.91
  81.8 1.0 collective-permute-start.25
  82.8 0.6 shard_map.92
  83.4 1.8 %collective-permute-start.26 = (bf16[2,528,128]{2,1,0:T(8,128)(2,1)S(1)}, bf16[2,528,128]{2,1,0:T(8,128)(2,1)S(1)}, u32[]{:S(2)}, u32[]{:S(2)}) collective-permute-start(bf16[2,528,128]{2,1,0:T(8,128)(2,1)S(1)} %shard_map.92), channel_id=1, source_target_pairs={{0,2},{4,0},{8,4},{12,8},{14,12},{10,14},{6,10},{2,6},{1,3},{5,1},... | collective-permute-start | bytes 811016 | tf_op jit(solution)/shard_map/ppermute | solution.py:505
  85.2 1.2 %collective-permute-done.19.in_ref = bf16[2,528,128]{2,1,0:T(8,128)(2,1)S(1)} collective-permute-done((bf16[2,528,128]{2,1,0:T(8,128)(2,1)S(1)}, bf16[2,528,128]{2,1,0:T(8,128)(2,1)S(1)}, u32[]{:S(2)}, u32[]{:S(2)}) %collective-permute-start.19) | collective-permute-done | bytes 270368 | tf_op jit(solution)/shard_map/ppermute | solution.py:505
  86.3 0.8 collective-permute-done.20.in_ref
  87.1 0.6 shard_map.93
  87.7 1.0 collective-permute-start.23
  88.8 0.6 shard_map.94
  89.4 1.6 %collective-permute-start.24 = (bf16[2,528,128]{2,1,0:T(8,128)(2,1)S(1)}, bf16[2,528,128]{2,1,0:T(8,128)(2,1)S(1)}, u32[]{:S(2)}, u32[]{:S(2)}) collective-permute-start(bf16[2,528,128]{2,1,0:T(8,128)(2,1)S(1)} %shard_map.94), channel_id=1, source_target_pairs={{0,2},{4,0},{8,4},{12,8},{14,12},{10,14},{6,10},{2,6},{1,3},{5,1},... | collective-permute-start | bytes 811016 | tf_op jit(solution)/shard_map/ppermute | solution.py:505
  91.0 0.5 collective-permute-done.26.in_ref
  91.5 3.2 %collective-permute-done.23.in_ref = bf16[2,528,128]{2,1,0:T(8,128)(2,1)S(1)} collective-permute-done((bf16[2,528,128]{2,1,0:T(8,128)(2,1)S(1)}, bf16[2,528,128]{2,1,0:T(8,128)(2,1)S(1)}, u32[]{:S(2)}, u32[]{:S(2)}) %collective-permute-start.23) | collective-permute-done | bytes 270368 | tf_op jit(solution)/shard_map/ppermute | solution.py:505
  94.7 3.7 %collective-permute-done.24.in_ref = bf16[2,528,128]{2,1,0:T(8,128)(2,1)S(1)} collective-permute-done((bf16[2,528,128]{2,1,0:T(8,128)(2,1)S(1)}, bf16[2,528,128]{2,1,0:T(8,128)(2,1)S(1)}, u32[]{:S(2)}, u32[]{:S(2)}) %collective-permute-start.24) | collective-permute-done | bytes 270368 | tf_op jit(solution)/shard_map/ppermute | solution.py:505
  98.4 0.6 shard_map.95
  99.0 1.6 %collective-permute-start.27 = (bf16[2,528,128]{2,1,0:T(8,128)(2,1)S(1)}, bf16[2,528,128]{2,1,0:T(8,128)(2,1)S(1)}, u32[]{:S(2)}, u32[]{:S(2)}) collective-permute-start(bf16[2,528,128]{2,1,0:T(8,128)(2,1)S(1)} %shard_map.95), channel_id=1, source_target_pairs={{0,2},{4,0},{8,4},{12,8},{14,12},{10,14},{6,10},{2,6},{1,3},{5,1},... | collective-permute-start | bytes 811016 | tf_op jit(solution)/shard_map/ppermute | solution.py:505
  100.6 0.6 shard_map.96
  101.2 0.6 collective-permute-start.28
  101.8 1.6 %shard_map.100 = bf16[32,2,64,512]{3,2,1,0:T(8,128)(2,1)} custom-call(s32[1]{0:T(128)} %bitcast.1.me_ref, s32[2,128]{1,0:T(2,128)} %copy-done.5, bf16[1,2,64,512]{3,2,1,0:T(8,128)(2,1)} %copy-done.6, bf16[32,2,64,512]{3,2,1,0:T(8,128)(2,1)} %get-tuple-element.143.old_ref), custom_call_target="tpu_custom_call", output_to_operand_aliasing={{}: (3, {})} | custom-call | bytes 131072 | tf_op jit(solution)/shard_map/pallas_call | solution.py:286
  103.4 0.6 shard_map.97
  104.0 0.6 shard_map.98
  104.6 0.9 collective-permute-done.27.refs_0_
  105.5 2.2 %collective-permute-done.28.refs_3_ = bf16[2,528,128]{2,1,0:T(8,128)(2,1)S(1)} collective-permute-done((bf16[2,528,128]{2,1,0:T(8,128)(2,1)S(1)}, bf16[2,528,128]{2,1,0:T(8,128)(2,1)S(1)}, u32[]{:S(2)}, u32[]{:S(2)}) %collective-permute-start.28) | collective-permute-done | bytes 270368 | tf_op jit(solution)/shard_map/ppermute | solution.py:505
  107.7 1.7 %shard_map.99 = bf16[1,64,4096]{2,1,0:T(8,128)(2,1)} custom-call(bf16[2,528,128]{2,1,0:T(8,128)(2,1)S(1)} %collective-permute-done.27.refs_0_, f32[2,512,128]{2,1,0:T(8,128)S(1)} %get-tuple-element.137.refs_1_, bf16[2,16,128]{2,1,0:T(8,128)(2,1)S(1)} %get-tuple-element.138.refs_2_, bf16[2,528,128]{2,1,0:T(8,128)(2,1)S(1)} %collective-permute-done.28.refs_3_, ...), custom_call_target="tpu_custom_call" | custom-call | flops 1605632 | bytes 3211264 | tf_op jit(solution)/shard_map/pallas_call | solution.py:357
  (42 shorter events, 1.1 us)
Async XLA Ops:
  4.0 17.0 %collective-permute-start = (bf16[64,2176]{1,0:T(8,128)(2,1)}, bf16[64,2176]{1,0:T(8,128)(2,1)S(1)}, u32[]{:S(2)}, u32[]{:S(2)}) collective-permute-start(bf16[64,2176]{1,0:T(8,128)(2,1)} %get-tuple-element.73.refs_1_), channel_id=1, source_target_pairs={{0,4},{4,8},{8,12},{12,14},{14,10},{10,6},{6,2},{2,0},{1,5},{5,9},... | collective-permute-start | bytes 835592 | tf_op jit(solution)/shard_map/ppermute | solution.py:439
  7.0 14.0 %collective-permute-start.2 = (bf16[64,2176]{1,0:T(8,128)(2,1)}, bf16[64,2176]{1,0:T(8,128)(2,1)S(1)}, u32[]{:S(2)}, u32[]{:S(2)}) collective-permute-start(bf16[64,2176]{1,0:T(8,128)(2,1)} %get-tuple-element.73.refs_1_), channel_id=1, source_target_pairs={{0,2},{4,0},{8,4},{12,8},{14,12},{10,14},{6,10},{2,6},{1,3},{5,1},... | collective-permute-start | bytes 835592 | tf_op jit(solution)/shard_map/ppermute | solution.py:440
  7.0 12.4 %collective-permute-start.1 = (bf16[64,2048]{1,0:T(8,128)(2,1)}, bf16[64,2048]{1,0:T(8,128)(2,1)S(1)}, u32[]{:S(2)}, u32[]{:S(2)}) collective-permute-start(bf16[64,2048]{1,0:T(8,128)(2,1)} %get-tuple-element.74.refs_2_), channel_id=1, source_target_pairs={{0,4},{4,8},{8,12},{12,14},{14,10},{10,6},{6,2},{2,0},{1,5},{5,9},... | collective-permute-start | bytes 786440 | tf_op jit(solution)/shard_map/ppermute | solution.py:439
  9.0 11.9 %collective-permute-start.3 = (bf16[64,2048]{1,0:T(8,128)(2,1)}, bf16[64,2048]{1,0:T(8,128)(2,1)S(1)}, u32[]{:S(2)}, u32[]{:S(2)}) collective-permute-start(bf16[64,2048]{1,0:T(8,128)(2,1)} %get-tuple-element.74.refs_2_), channel_id=1, source_target_pairs={{0,2},{4,0},{8,4},{12,8},{14,12},{10,14},{6,10},{2,6},{1,3},{5,1},... | collective-permute-start | bytes 786440 | tf_op jit(solution)/shard_map/ppermute | solution.py:440
  9.7 2.2 %copy-start = (bf16[32,2,64,512]{3,2,1,0:T(8,128)(2,1)S(1)}, bf16[32,2,64,512]{3,2,1,0:T(8,128)(2,1)}, u32[]{:S(2)}) copy-start(bf16[32,2,64,512]{3,2,1,0:T(8,128)(2,1)} %refs_3_.1) | copy-start | bytes 12582916
  11.9 1.0 copy-start.2
  12.9 0.9 copy-start.3
  13.8 0.9 copy-start.4
  21.0 13.2 %collective-permute-start.6 = (bf16[64,2176]{1,0:T(8,128)(2,1)S(1)}, bf16[64,2176]{1,0:T(8,128)(2,1)S(1)}, u32[]{:S(2)}, u32[]{:S(2)}) collective-permute-start(bf16[64,2176]{1,0:T(8,128)(2,1)S(1)} %collective-permute-done.2.refs_3_), channel_id=1, source_target_pairs={{0,2},{4,0},{8,4},{12,8},{14,12},{10,14},{6,10},{2,6},{1,3},{5,1},... | collective-permute-start | bytes 835592 | tf_op jit(solution)/shard_map/ppermute | solution.py:440
  21.3 12.9 %collective-permute-start.4 = (bf16[64,2176]{1,0:T(8,128)(2,1)S(1)}, bf16[64,2176]{1,0:T(8,128)(2,1)S(1)}, u32[]{:S(2)}, u32[]{:S(2)}) collective-permute-start(bf16[64,2176]{1,0:T(8,128)(2,1)S(1)} %collective-permute-done.refs_1_), channel_id=1, source_target_pairs={{0,4},{4,8},{8,12},{12,14},{14,10},{10,6},{6,2},{2,0},{1,5},{5,9},... | collective-permute-start | bytes 835592 | tf_op jit(solution)/shard_map/ppermute | solution.py:439
  23.0 11.1 %collective-permute-start.5 = (bf16[64,2048]{1,0:T(8,128)(2,1)S(1)}, bf16[64,2048]{1,0:T(8,128)(2,1)S(1)}, u32[]{:S(2)}, u32[]{:S(2)}) collective-permute-start(bf16[64,2048]{1,0:T(8,128)(2,1)S(1)} %collective-permute-done.1.refs_2_), channel_id=1, source_target_pairs={{0,4},{4,8},{8,12},{12,14},{14,10},{10,6},{6,2},{2,0},{1,5},{5,9},... | collective-permute-start | bytes 786440 | tf_op jit(solution)/shard_map/ppermute | solution.py:439
  24.6 9.6 %collective-permute-start.7 = (bf16[64,2048]{1,0:T(8,128)(2,1)S(1)}, bf16[64,2048]{1,0:T(8,128)(2,1)S(1)}, u32[]{:S(2)}, u32[]{:S(2)}) collective-permute-start(bf16[64,2048]{1,0:T(8,128)(2,1)S(1)} %collective-permute-done.3.refs_4_), channel_id=1, source_target_pairs={{0,2},{4,0},{8,4},{12,8},{14,12},{10,14},{6,10},{2,6},{1,3},{5,1},... | collective-permute-start | bytes 786440 | tf_op jit(solution)/shard_map/ppermute | solution.py:440
  34.2 14.0 %collective-permute-start.10 = (bf16[64,2176]{1,0:T(8,128)(2,1)S(1)}, bf16[64,2176]{1,0:T(8,128)(2,1)S(1)}, u32[]{:S(2)}, u32[]{:S(2)}) collective-permute-start(bf16[64,2176]{1,0:T(8,128)(2,1)S(1)} %collective-permute-done.6.refs_3_), channel_id=1, source_target_pairs={{0,2},{4,0},{8,4},{12,8},{14,12},{10,14},{6,10},{2,6},{1,3},{5,1},... | collective-permute-start | bytes 835592 | tf_op jit(solution)/shard_map/ppermute | solution.py:440
  35.8 12.4 %collective-permute-start.8 = (bf16[64,2176]{1,0:T(8,128)(2,1)S(1)}, bf16[64,2176]{1,0:T(8,128)(2,1)S(1)}, u32[]{:S(2)}, u32[]{:S(2)}) collective-permute-start(bf16[64,2176]{1,0:T(8,128)(2,1)S(1)} %collective-permute-done.4.refs_1_), channel_id=1, source_target_pairs={{0,4},{4,8},{8,12},{12,14},{14,10},{10,6},{6,2},{2,0},{1,5},{5,9},... | collective-permute-start | bytes 835592 | tf_op jit(solution)/shard_map/ppermute | solution.py:439
  36.3 11.9 %collective-permute-start.9 = (bf16[64,2048]{1,0:T(8,128)(2,1)S(1)}, bf16[64,2048]{1,0:T(8,128)(2,1)S(1)}, u32[]{:S(2)}, u32[]{:S(2)}) collective-permute-start(bf16[64,2048]{1,0:T(8,128)(2,1)S(1)} %collective-permute-done.5.refs_2_), channel_id=1, source_target_pairs={{0,4},{4,8},{8,12},{12,14},{14,10},{10,6},{6,2},{2,0},{1,5},{5,9},... | collective-permute-start | bytes 786440 | tf_op jit(solution)/shard_map/ppermute | solution.py:439
  37.6 10.5 %collective-permute-start.11 = (bf16[64,2048]{1,0:T(8,128)(2,1)S(1)}, bf16[64,2048]{1,0:T(8,128)(2,1)S(1)}, u32[]{:S(2)}, u32[]{:S(2)}) collective-permute-start(bf16[64,2048]{1,0:T(8,128)(2,1)S(1)} %collective-permute-done.7.refs_4_), channel_id=1, source_target_pairs={{0,2},{4,0},{8,4},{12,8},{14,12},{10,14},{6,10},{2,6},{1,3},{5,1},... | collective-permute-start | bytes 786440 | tf_op jit(solution)/shard_map/ppermute | solution.py:440
  38.3 18.9 %copy-start.5 = (s32[2,128]{1,0:T(2,128)}, s32[2,128]{1,0:T(2,128)S(1)}, u32[]{:S(2)}) copy-start(s32[2,128]{1,0:T(2,128)S(1)} %maximum_convert_fusion.1.refs_0_.lists_ref) | copy-start | bytes 3076
  48.1 12.0 %collective-permute-start.12 = (bf16[64,2176]{1,0:T(8,128)(2,1)S(1)}, bf16[64,2176]{1,0:T(8,128)(2,1)S(1)}, u32[]{:S(2)}, u32[]{:S(2)}) collective-permute-start(bf16[64,2176]{1,0:T(8,128)(2,1)S(1)} %collective-permute-done.8.refs_1_), channel_id=1, source_target_pairs={{0,4},{4,8},{8,12},{12,14},{14,10},{10,6},{6,2},{2,0},{1,5},{5,9},... | collective-permute-start | bytes 835592 | tf_op jit(solution)/shard_map/ppermute | solution.py:457
  48.7 11.4 %collective-permute-start.13 = (bf16[64,2048]{1,0:T(8,128)(2,1)S(1)}, bf16[64,2048]{1,0:T(8,128)(2,1)S(1)}, u32[]{:S(2)}, u32[]{:S(2)}) collective-permute-start(bf16[64,2048]{1,0:T(8,128)(2,1)S(1)} %collective-permute-done.11.refs_4_), channel_id=1, source_target_pairs={{0,2},{4,0},{8,4},{12,8},{14,12},{10,14},{6,10},{2,6},{1,3},{5,1},... | collective-permute-start | bytes 786440 | tf_op jit(solution)/shard_map/ppermute | solution.py:458
  50.2 9.9 %collective-permute-start.14 = (bf16[1,2,64,512]{3,2,1,0:T(8,128)(2,1)S(1)}, bf16[1,2,64,512]{3,2,1,0:T(8,128)(2,1)S(1)}, u32[]{:S(2)}, u32[]{:S(2)}) collective-permute-start(bf16[1,2,64,512]{3,2,1,0:T(8,128)(2,1)S(1)} %copy-done.4), channel_id=1, source_target_pairs={{8,0},{10,2},{12,4},{14,6},{0,8},{2,10},{4,12},{6,14},{9,1},{11,3}... | collective-permute-start | bytes 393224 | tf_op jit(solution)/shard_map/ppermute | solution.py:23
  51.6 8.5 %copy-start.1 = (bf16[32,2,64,512]{3,2,1,0:T(8,128)(2,1)S(1)}, bf16[32,2,64,512]{3,2,1,0:T(8,128)(2,1)}, u32[]{:S(2)}) copy-start(bf16[32,2,64,512]{3,2,1,0:T(8,128)(2,1)} %refs_3_.1) | copy-start | bytes 12582916
  57.2 9.0 %collective-permute-start.15 = (bf16[2,528,128]{2,1,0:T(8,128)(2,1)S(1)}, bf16[2,528,128]{2,1,0:T(8,128)(2,1)S(1)}, u32[]{:S(2)}, u32[]{:S(2)}) collective-permute-start(bf16[2,528,128]{2,1,0:T(8,128)(2,1)S(1)} %shard_map.82), channel_id=1, source_target_pairs={{0,4},{4,8},{8,12},{12,14},{14,10},{10,6},{6,2},{2,0},{1,5},{5,9},... | collective-permute-start | bytes 811016 | tf_op jit(solution)/shard_map/ppermute | solution.py:473
  58.9 7.3 %collective-permute-start.16 = (bf16[2,528,128]{2,1,0:T(8,128)(2,1)S(1)}, bf16[2,528,128]{2,1,0:T(8,128)(2,1)S(1)}, u32[]{:S(2)}, u32[]{:S(2)}) collective-permute-start(bf16[2,528,128]{2,1,0:T(8,128)(2,1)S(1)} %shard_map.83), channel_id=1, source_target_pairs={{0,2},{4,0},{8,4},{12,8},{14,12},{10,14},{6,10},{2,6},{1,3},{5,1},... | collective-permute-start | bytes 811016 | tf_op jit(solution)/shard_map/ppermute | solution.py:473
  60.1 9.2 %copy-start.6 = (bf16[1,2,64,512]{3,2,1,0:T(8,128)(2,1)}, bf16[1,2,64,512]{3,2,1,0:T(8,128)(2,1)S(1)}, u32[]{:S(2)}) copy-start(bf16[1,2,64,512]{3,2,1,0:T(8,128)(2,1)S(1)} %collective-permute-done.14.page_ref) | copy-start | bytes 393220
  66.3 8.4 %collective-permute-start.17 = (bf16[2,528,128]{2,1,0:T(8,128)(2,1)S(1)}, bf16[2,528,128]{2,1,0:T(8,128)(2,1)S(1)}, u32[]{:S(2)}, u32[]{:S(2)}) collective-permute-start(bf16[2,528,128]{2,1,0:T(8,128)(2,1)S(1)} %shard_map.85), channel_id=1, source_target_pairs={{0,4},{4,8},{8,12},{12,14},{14,10},{10,6},{6,2},{2,0},{1,5},{5,9},... | collective-permute-start | bytes 811016 | tf_op jit(solution)/shard_map/ppermute | solution.py:505
  66.4 9.0 %collective-permute-start.18 = (bf16[2,528,128]{2,1,0:T(8,128)(2,1)S(1)}, bf16[2,528,128]{2,1,0:T(8,128)(2,1)S(1)}, u32[]{:S(2)}, u32[]{:S(2)}) collective-permute-start(bf16[2,528,128]{2,1,0:T(8,128)(2,1)S(1)} %shard_map.86), channel_id=1, source_target_pairs={{0,2},{4,0},{8,4},{12,8},{14,12},{10,14},{6,10},{2,6},{1,3},{5,1},... | collective-permute-start | bytes 811016 | tf_op jit(solution)/shard_map/ppermute | solution.py:505
  69.9 10.6 %collective-permute-start.21 = (bf16[2,528,128]{2,1,0:T(8,128)(2,1)S(1)}, bf16[2,528,128]{2,1,0:T(8,128)(2,1)S(1)}, u32[]{:S(2)}, u32[]{:S(2)}) collective-permute-start(bf16[2,528,128]{2,1,0:T(8,128)(2,1)S(1)} %shard_map.87), channel_id=1, source_target_pairs={{0,4},{4,8},{8,12},{12,14},{14,10},{10,6},{6,2},{2,0},{1,5},{5,9},... | collective-permute-start | bytes 811016 | tf_op jit(solution)/shard_map/ppermute | solution.py:505
  70.0 11.2 %collective-permute-start.22 = (bf16[2,528,128]{2,1,0:T(8,128)(2,1)S(1)}, bf16[2,528,128]{2,1,0:T(8,128)(2,1)S(1)}, u32[]{:S(2)}, u32[]{:S(2)}) collective-permute-start(bf16[2,528,128]{2,1,0:T(8,128)(2,1)S(1)} %shard_map.88), channel_id=1, source_target_pairs={{0,2},{4,0},{8,4},{12,8},{14,12},{10,14},{6,10},{2,6},{1,3},{5,1},... | collective-permute-start | bytes 811016 | tf_op jit(solution)/shard_map/ppermute | solution.py:505
  76.0 10.3 %collective-permute-start.19 = (bf16[2,528,128]{2,1,0:T(8,128)(2,1)S(1)}, bf16[2,528,128]{2,1,0:T(8,128)(2,1)S(1)}, u32[]{:S(2)}, u32[]{:S(2)}) collective-permute-start(bf16[2,528,128]{2,1,0:T(8,128)(2,1)S(1)} %shard_map.89), channel_id=1, source_target_pairs={{0,4},{4,8},{8,12},{12,14},{14,10},{10,6},{6,2},{2,0},{1,5},{5,9},... | collective-permute-start | bytes 811016 | tf_op jit(solution)/shard_map/ppermute | solution.py:505
  77.6 9.5 %collective-permute-start.20 = (bf16[2,528,128]{2,1,0:T(8,128)(2,1)S(1)}, bf16[2,528,128]{2,1,0:T(8,128)(2,1)S(1)}, u32[]{:S(2)}, u32[]{:S(2)}) collective-permute-start(bf16[2,528,128]{2,1,0:T(8,128)(2,1)S(1)} %shard_map.90), channel_id=1, source_target_pairs={{0,2},{4,0},{8,4},{12,8},{14,12},{10,14},{6,10},{2,6},{1,3},{5,1},... | collective-permute-start | bytes 811016 | tf_op jit(solution)/shard_map/ppermute | solution.py:505
  81.8 9.2 %collective-permute-start.25 = (bf16[2,528,128]{2,1,0:T(8,128)(2,1)S(1)}, bf16[2,528,128]{2,1,0:T(8,128)(2,1)S(1)}, u32[]{:S(2)}, u32[]{:S(2)}) collective-permute-start(bf16[2,528,128]{2,1,0:T(8,128)(2,1)S(1)} %shard_map.91), channel_id=1, source_target_pairs={{0,4},{4,8},{8,12},{12,14},{14,10},{10,6},{6,2},{2,0},{1,5},{5,9},... | collective-permute-start | bytes 811016 | tf_op jit(solution)/shard_map/ppermute | solution.py:505
  83.4 8.1 %collective-permute-start.26 = (bf16[2,528,128]{2,1,0:T(8,128)(2,1)S(1)}, bf16[2,528,128]{2,1,0:T(8,128)(2,1)S(1)}, u32[]{:S(2)}, u32[]{:S(2)}) collective-permute-start(bf16[2,528,128]{2,1,0:T(8,128)(2,1)S(1)} %shard_map.92), channel_id=1, source_target_pairs={{0,2},{4,0},{8,4},{12,8},{14,12},{10,14},{6,10},{2,6},{1,3},{5,1},... | collective-permute-start | bytes 811016 | tf_op jit(solution)/shard_map/ppermute | solution.py:505
  87.7 7.0 %collective-permute-start.23 = (bf16[2,528,128]{2,1,0:T(8,128)(2,1)S(1)}, bf16[2,528,128]{2,1,0:T(8,128)(2,1)S(1)}, u32[]{:S(2)}, u32[]{:S(2)}) collective-permute-start(bf16[2,528,128]{2,1,0:T(8,128)(2,1)S(1)} %shard_map.93), channel_id=1, source_target_pairs={{0,4},{4,8},{8,12},{12,14},{14,10},{10,6},{6,2},{2,0},{1,5},{5,9},... | collective-permute-start | bytes 811016 | tf_op jit(solution)/shard_map/ppermute | solution.py:505
  89.4 9.0 %collective-permute-start.24 = (bf16[2,528,128]{2,1,0:T(8,128)(2,1)S(1)}, bf16[2,528,128]{2,1,0:T(8,128)(2,1)S(1)}, u32[]{:S(2)}, u32[]{:S(2)}) collective-permute-start(bf16[2,528,128]{2,1,0:T(8,128)(2,1)S(1)} %shard_map.94), channel_id=1, source_target_pairs={{0,2},{4,0},{8,4},{12,8},{14,12},{10,14},{6,10},{2,6},{1,3},{5,1},... | collective-permute-start | bytes 811016 | tf_op jit(solution)/shard_map/ppermute | solution.py:505
  99.0 6.5 %collective-permute-start.27 = (bf16[2,528,128]{2,1,0:T(8,128)(2,1)S(1)}, bf16[2,528,128]{2,1,0:T(8,128)(2,1)S(1)}, u32[]{:S(2)}, u32[]{:S(2)}) collective-permute-start(bf16[2,528,128]{2,1,0:T(8,128)(2,1)S(1)} %shard_map.95), channel_id=1, source_target_pairs={{0,2},{4,0},{8,4},{12,8},{14,12},{10,14},{6,10},{2,6},{1,3},{5,1},... | collective-permute-start | bytes 811016 | tf_op jit(solution)/shard_map/ppermute | solution.py:505
  101.2 6.5 %collective-permute-start.28 = (bf16[2,528,128]{2,1,0:T(8,128)(2,1)S(1)}, bf16[2,528,128]{2,1,0:T(8,128)(2,1)S(1)}, u32[]{:S(2)}, u32[]{:S(2)}) collective-permute-start(bf16[2,528,128]{2,1,0:T(8,128)(2,1)S(1)} %shard_map.96), channel_id=1, source_target_pairs={{0,4},{4,8},{8,12},{12,14},{14,10},{10,6},{6,2},{2,0},{1,5},{5,9},... | collective-permute-start | bytes 811016 | tf_op jit(solution)/shard_map/ppermute | solution.py:505

commit v4 on v3

--- a/solution.py
+++ b/solution.py
@@ -12,6 +12,7 @@
 DEAD = -1e30
 FLOOR = -1e29
 STAT_ROWS = 16
+LIGHT = pl.CostEstimate(flops=1, bytes_accessed=1, transcendentals=0)
 VMEM = pl.BlockSpec(memory_space=pltpu.VMEM)
 SMEM = pl.BlockSpec(memory_space=pltpu.SMEM)
 HBM = pl.BlockSpec(memory_space=pltpu.HBM)
@@ -153,56 +154,50 @@
     return [part(2 * j) for j in range(4)], [part(2 * j + 1) for j in range(4)]
 
 
-def attend_kernel(sizes, parts, own, *refs):
-    kv_heads, groups, suffix, cap, page_len = sizes
+def attend_kernel(sizes, jobs, *refs):
+    groups, suffix, cap, page_len, count, own = sizes
     refs = list(refs)
     meta = refs.pop(0)
-    queries = [[refs.pop(0) for _ in range(n)] for n in parts]
-    own_kv = refs.pop(0) if own else None
-    pages = refs.pop(0)
-    outs = [(refs.pop(0), refs.pop(0)) for _ in parts]
-    stored = refs.pop(0) if own else None
-    held, sems, scores = refs[:3]
+    queries = [refs.pop(0) for _ in range(count)]
     if own:
-        late_scores, store_sem = refs[3:]
-    copies = [
-        [
-            pltpu.make_async_copy(pages.at[meta[n, c]], held.at[n, c], sems.at[n, c])
-            for c in range(cap)
-        ]
-        for n in range(len(parts))
-    ]
-    for request in copies:
-        for copy in request:
-            copy.start()
+        own_kv, pages = refs.pop(0), refs.pop(0)
+    else:
+        held = refs.pop(0)
+    results = len({job[-1] for job in jobs})
+    outs = [(refs.pop(0), refs.pop(0)) for _ in range(results)]
     if own:
-        keep = pltpu.make_async_copy(pages, stored, store_sem)
+        held, stored, scores, late_scores, sems = refs
+        fetch = pltpu.make_async_copy(pages, held, sems.at[0])
+        fetch.start()
+        fetch.wait()
+        keep = pltpu.make_async_copy(held, stored, sems.at[1])
         keep.start()
+    else:
+        (scores,) = refs
     factor = HEAD_SIZE ** (-0.5) * LOG2E
     keys = cap * page_len
     rows = groups * suffix
-    jobs = [(n, h) for n in range(len(parts)) for h in range(kv_heads)]
-
-    def lanes(h):
-        return slice(h * HEAD_SIZE, (h + 1) * HEAD_SIZE)
+    filled = [0] * results
+    spots = []
+    for job in jobs:
+        spots.append(filled[job[-1]])
+        filled[job[-1]] += 1
+
+    def stacked(n, part, h):
+        return jnp.concatenate([held[meta[n, c], part, :, block_of(h)] for c in range(cap)], 0)
 
     def score(i):
-        n, h = jobs[i]
-        if h == 0:
-            for copy in copies[n]:
-                copy.wait()
-        heads_each = kv_heads // len(queries[n])
-        q_ref, first = queries[n][h // heads_each], (h % heads_each) * groups
-        q = jnp.concatenate([q_ref[:, block_of(first + g)] for g in range(groups)], 0)
-        k = held[n, :, 0, :, lanes(h)].reshape(keys, HEAD_SIZE)
-        scores[i % 2, :, :keys] = dot_nt(q, k)
+        n, array, first, h, _ = jobs[i]
+        q_ref = queries[array]
+        q = jnp.concatenate([q_ref[:, block_of(first * groups + g)] for g in range(groups)], 0)
+        scores[i % 2] = dot_nt(q, stacked(n, 0, h))
         if own:
             at = iota((rows, suffix), 0) % suffix
             causal = iota((rows, suffix), 1) <= at
-            late_scores[i % 2] = jnp.where(causal, dot_nt(q, own_kv[0, :, lanes(h)]), DEAD)
+            late_scores[i % 2] = jnp.where(causal, dot_nt(q, own_kv[0, :, block_of(h)]), DEAD)
 
     def weigh(i):
-        n, h = jobs[i]
+        n, _, _, h, result = jobs[i]
         live = iota((1, keys), 1) < meta[n, cap] * page_len
         s = jnp.where(live, scores[i % 2], DEAD)
         top = jnp.max(s, axis=-1, keepdims=True)
@@ -210,20 +205,21 @@
             top = jnp.maximum(top, jnp.max(late_scores[i % 2], axis=-1, keepdims=True))
         top = jnp.maximum(top * factor, FLOOR).astype(jnp.bfloat16).astype(jnp.float32)
         p = jnp.exp2(s * factor - top).astype(jnp.bfloat16)
-        v = held[n, :, 1, :, lanes(h)].reshape(keys, HEAD_SIZE)
+        v = stacked(n, 1, h)
         v = jnp.concatenate([v, jnp.ones_like(v)], 1)
         out = jnp.dot(p, v, preferred_element_type=jnp.float32)
         if own:
             p = jnp.exp2(late_scores[i % 2] * factor - top).astype(jnp.bfloat16)
-            v = own_kv[1, :, lanes(h)]
+            v = own_kv[1, :, block_of(h)]
             v = jnp.concatenate([v, jnp.ones_like(v)], 1)
             out = out + jnp.dot(p, v, preferred_element_type=jnp.float32)
-        acc_ref, stat_ref = outs[n]
-        acc_ref[h] = out[:, :HEAD_SIZE]
+        acc_ref, stat_ref = outs[result]
+        spot = spots[i]
+        acc_ref[spot] = out[:, :HEAD_SIZE]
         total = out[:, HEAD_SIZE:]
         top = jnp.broadcast_to(top, total.shape)
         blocks = [block_of(j) for j in range(rows // HEAD_SIZE)]
-        stat_ref[h] = pack_stats([top[j] for j in blocks], [total[j] for j in blocks])
+        stat_ref[spot] = pack_stats([top[j] for j in blocks], [total[j] for j in blocks])
 
     for i in range(len(jobs) + 1):
         if i < len(jobs):
@@ -234,43 +230,34 @@
         keep.wait()
 
 
-def attend(sizes, meta, queries, own_kv, kv_pages):
-    kv_heads, groups, suffix, cap, page_len = sizes
-    parts = [len(q) for q in queries]
-    flat = [x for q in queries for x in q]
-    own = own_kv is not None
-    shapes = []
-    rows = groups * suffix
-    for _ in parts:
-        shapes.append(jax.ShapeDtypeStruct((kv_heads, rows, HEAD_SIZE), jnp.float32))
-        shapes.append(jax.ShapeDtypeStruct((kv_heads, STAT_ROWS, HEAD_SIZE), jnp.bfloat16))
-    keys = cap * page_len
-    count = len(parts)
-    scratch = [
-        pltpu.VMEM((count, cap) + kv_pages.shape[1:], jnp.bfloat16),
-        pltpu.SemaphoreType.DMA((count, cap)),
-        pltpu.VMEM((2, rows, keys), jnp.float32),
-    ]
-    specs = [VMEM] * len(shapes)
-    if own:
-        shapes.append(jax.ShapeDtypeStruct(kv_pages.shape, kv_pages.dtype))
-        specs.append(HBM)
+def attend(shape, jobs, meta, queries, held, own=None):
+    groups, suffix, cap, page_len = shape
+    rows, keys = groups * suffix, cap * page_len
+    results = len({job[-1] for job in jobs})
+    heads = len(jobs) // results
+    shapes, specs = [], []
+    for _ in range(results):
+        shapes.append(jax.ShapeDtypeStruct((heads, rows, HEAD_SIZE), jnp.float32))
+        shapes.append(jax.ShapeDtypeStruct((heads, STAT_ROWS, HEAD_SIZE), jnp.bfloat16))
+        specs += [VMEM, VMEM]
+    scratch = [pltpu.VMEM((2, rows, keys), jnp.float32)]
+    more = [held]
+    if own is not None:
+        more = [own, held]
+        shapes += [jax.ShapeDtypeStruct(held.shape, held.dtype)] * 2
+        specs += [VMEM, HBM]
         scratch.append(pltpu.VMEM((2, rows, suffix), jnp.float32))
-        scratch.append(pltpu.SemaphoreType.DMA)
+        scratch.append(pltpu.SemaphoreType.DMA((2,)))
     out = pl.pallas_call(
-        functools.partial(attend_kernel, sizes, parts, own),
+        functools.partial(attend_kernel, shape + (len(queries), own is not None), jobs),
         out_shape=shapes,
-        in_specs=[SMEM] + [VMEM] * (len(flat) + own) + [HBM],
+        in_specs=[SMEM] + [VMEM] * len(queries) + ([VMEM] if own is None else [VMEM, HBM]),
         out_specs=specs,
         scratch_shapes=scratch,
-        compiler_params=pltpu.CompilerParams(vmem_limit_bytes=48 * 1024 * 1024),
-        cost_estimate=pl.CostEstimate(
-            flops=count * kv_heads * rows * keys * HEAD_SIZE * 8,
-            bytes_accessed=count * kv_heads * (rows * 6 + keys * 4) * HEAD_SIZE,
-            transcendentals=count * kv_heads * rows * keys,
-        ),
-    )(meta, *flat, *([own_kv] if own else []), kv_pages)
-    return [(out[2 * n], out[2 * n + 1]) for n in range(count)] + list(out[2 * count:])
+        compiler_params=pltpu.CompilerParams(vmem_limit_bytes=40 * 1024 * 1024),
+        cost_estimate=LIGHT,
+    )(meta, *queries, *more)
+    return [(out[2 * n], out[2 * n + 1]) for n in range(results)] + list(out[2 * results:])
 
 
 def place_kernel(half, column, me_ref, lists_ref, page_ref, old_ref, out_ref, sem):
@@ -290,7 +277,7 @@
         out_specs=HBM,
         scratch_shapes=[pltpu.SemaphoreType.DMA],
         input_output_aliases={3: 0},
-        cost_estimate=pl.CostEstimate(flops=0, bytes_accessed=2 * page.size, transcendentals=0),
+        cost_estimate=LIGHT,
     )(me, lists, page, store)
 
 
@@ -302,24 +289,24 @@
     return acc, top, total
 
 
-def pack_kernel(first, heads, acc_ref, stat_ref, out_ref):
-    rows = acc_ref.shape[1]
+def pack_kernel(acc_ref, stat_ref, out_ref):
+    heads, rows = acc_ref.shape[:2]
     for h in range(heads):
-        out_ref[h, :rows, :] = acc_ref[first + h].astype(jnp.bfloat16)
-        out_ref[h, rows:, :] = stat_ref[first + h]
-
-
-def merge_kernel(first, heads, in_ref, acc_ref, stat_ref, out_ref, out_stat_ref=None):
-    rows = acc_ref.shape[1]
+        out_ref[h, :rows, :] = acc_ref[h].astype(jnp.bfloat16)
+        out_ref[h, rows:, :] = stat_ref[h]
+
+
+def merge_kernel(in_ref, acc_ref, stat_ref, out_ref, out_stat_ref=None):
+    heads, rows = acc_ref.shape[:2]
     for h in range(heads):
         in_top, in_total = unpack_stats(in_ref[h, rows:, :])
-        my_top, my_total = unpack_stats(stat_ref[first + h])
+        my_top, my_total = unpack_stats(stat_ref[h])
         tops, totals = [], []
         for j in range(rows // HEAD_SIZE):
             acc, top, total = blend(
                 [
                     (in_ref[h, block_of(j), :].astype(jnp.float32), in_top[j], in_total[j]),
-                    (acc_ref[first + h, block_of(j), :], my_top[j], my_total[j]),
+                    (acc_ref[h, block_of(j), :], my_top[j], my_total[j]),
                 ]
             )
             out_ref[h, block_of(j), :] = acc.astype(out_ref.dtype)
@@ -360,7 +347,7 @@
         in_specs=[VMEM] * len(args),
         out_specs=[VMEM] * len(shape) if isinstance(shape, list) else VMEM,
         compiler_params=pltpu.CompilerParams(vmem_limit_bytes=48 * 1024 * 1024),
-        cost_estimate=pl.CostEstimate(flops=size, bytes_accessed=2 * size, transcendentals=size // 8),
+        cost_estimate=pl.CostEstimate(flops=size, bytes_accessed=2 * size, transcendentals=0),
     )(*args)
 
 
@@ -403,6 +390,7 @@
         ],
         in_specs=[SMEM, SMEM, VMEM, VMEM],
         out_specs=[VMEM, VMEM],
+        cost_estimate=LIGHT,
     )(prefix_pages, new_slots, page_table, queries)
 
 
@@ -414,116 +402,118 @@
     kv_heads = width // HEAD_SIZE
     suffix = queries.shape[1]
     groups = queries.shape[2] // width
-    sizes = (kv_heads, groups, suffix, cap, page_len)
+    shape = (groups, suffix, cap, page_len)
     half = stores // 2
     me = lax.axis_index("store")
+    heads_each = kv_heads // 2
+    cut = heads_each * groups * HEAD_SIZE
 
     order = list(range(0, stores, 2)) + list(range(1, stores, 2))[::-1]
     up = [(order[i], order[(i + 1) % stores]) for i in range(stores)]
     down = [(order[i], order[i - 1]) for i in range(stores)]
-
-    heads_each = kv_heads // 2
-    cut = heads_each * groups * HEAD_SIZE
-    mine = prepare(cut, cap, pages_dev, queries, page_table, prefix_pages, new_slots)
+    routes = {1: up, -1: down}
 
     def listed(*arrays):
         rows = [lax.dynamic_slice(x, (me, cut), (1, HEAD_SIZE)) for x in arrays]
         return jnp.concatenate(rows).astype(jnp.int32)
 
     def after(values, token):
-        return lax.optimization_barrier((values, token))
-
-    ups, downs = list(mine), list(mine)
-    partials, lists_of = {}, {}
+        return lax.optimization_barrier((values, token))[0]
+
+    arrived = shifted(suffix_key_value, "store", half)
+    mine = prepare(cut, cap, pages_dev, queries, page_table, prefix_pages, new_slots)
+
+    moving = {
+        (side, sign): lax.ppermute(mine[side], "store", routes[sign])
+        for side in range(2)
+        for sign in routes
+    }
+    jobs = [(0, side, h, side * heads_each + h, side) for side in range(2) for h in range(heads_each)]
+    first, second = after(mine, arrived)
+    *own, held, store = attend(
+        shape, jobs, listed(first), [first, second], kv_pages, suffix_key_value[0]
+    )
+    parts = {(0, side): own[side] for side in range(2)}
+    token = own
+    lists_of = {}
+    sent = {}
     for step in range(1, half):
-        ups = [lax.ppermute(x, "store", up) for x in ups]
-        downs = [lax.ppermute(x, "store", down) for x in downs]
-        if step == 1:
-            partials[0], store = attend(
-                sizes,
-                listed(mine[0]),
-                [mine],
-                suffix_key_value[0],
-                kv_pages,
-            )
-            (ups, downs), partials[0] = after((ups, downs), partials[0])
+        for side in range(2):
+            came = {sign: after(moving[side, sign], token) for sign in routes}
+            for sign in routes:
+                if step < half - 1 or (side == 0) == (sign == 1):
+                    moving[side, sign] = lax.ppermute(came[sign], "store", routes[sign])
+            if side == 0:
+                lists_of[step] = listed(came[1], came[-1])
+            jobs = [(n, n, h, side * heads_each + h, n) for n in range(2) for h in range(heads_each)]
+            got = attend(shape, jobs, lists_of[step], [came[1], came[-1]], held)
+            parts[step, side], parts[-step, side] = got
+            token = got
+            if step == half - 1:
+                sign = 1 if side == 1 else -1
+                sent["early", sign] = packed(parts[sign * step, side])
+                token = sent["early", sign]
+    came = after([moving[0, 1], moving[1, -1]], token)
+    jobs = [(0, side, h, side * heads_each + h, side) for side in range(2) for h in range(heads_each)]
+    far = attend(shape, jobs, listed(came[0]), came, held)
+    token = far
+
+    back = {1: down, -1: up}
+    side_of = {("late", 1): 0, ("late", -1): 1, ("early", 1): 1, ("early", -1): 0}
+    flows = {key: lax.ppermute(block, "store", back[key[1]]) for key, block in sent.items()}
+    store = place_page(
+        half, cap + 1, me[None], lists_of[stores // 4], arrived, after(store, token)
+    )
+    turns = [("late", half)]
+    for distance in range(half - 1, 0, -1):
+        turns += [("early", distance - 1)] * (distance > 1) + [("late", distance)]
+    for flow, distance in turns:
+        if distance == half:
+            far, ended = lax.optimization_barrier((far, {sign: flows["early", sign] for sign in back}))
+            flows.update({("early", sign): ended[sign] for sign in back})
+            blocks = {sign: packed(far[side_of[flow, sign]]) for sign in back}
         else:
-            (ups, downs), (partials[step - 1], partials[1 - step]) = after(
-                (ups, downs), (partials[step - 1], partials[1 - step])
-            )
-        lists_of[step] = listed(ups[0], downs[0])
-        got = attend(sizes, lists_of[step], [ups, downs], None, kv_pages)
-        partials[step], partials[-step] = got
-    ups[0] = lax.ppermute(ups[0], "store", up)
-    downs[1] = lax.ppermute(downs[1], "store", down)
-
-    rows_head = groups * suffix
-    wire = jax.ShapeDtypeStruct((heads_each, rows_head + STAT_ROWS, HEAD_SIZE), jnp.bfloat16)
-
-    def packed(part, side):
-        return call(functools.partial(pack_kernel, side * heads_each, heads_each), wire, *part)
-
-    def merged(block, part, side):
-        return call(
-            functools.partial(merge_kernel, side * heads_each, heads_each), wire, block, *part
-        )
-
-    routes = {1: down, -1: up}
-    nearer = {sign: packed(partials[sign * (half - 1)], side) for side, sign in ((1, 1), (0, -1))}
-    hop = {sign: lax.ppermute(block, "store", routes[sign]) for sign, block in nearer.items()}
-    page, _ = after(suffix_key_value, partials[half - 2])
-    arrived = shifted(page, "store", half)
-    (ups, downs), (_, arrived) = after((ups, downs), (nearer, arrived))
-    (far,) = attend(sizes, listed(ups[0]), [[ups[0], downs[1]]], None, kv_pages)
-    store = place_page(half, cap + 1, me[None], lists_of[stores // 4], arrived, store)
-
-    side_of = {1: {"late": 0, "early": 1}, -1: {"late": 1, "early": 0}}
-    turns = [("early", half - 1)]
-    for distance in range(half, 0, -1):
-        turns += [("late", distance)] + [("early", distance - 2)] * (distance > 2)
-    flows = {("early", sign): hop[sign] for sign in routes}
-    sent = None
-    for flow, distance in turns[1:]:
-        blocks = {}
-        if flow == "late" and distance == half:
-            far, hop = after(far, hop)
-            for sign in routes:
-                flows["early", sign] = hop[sign]
-                blocks[sign] = packed(far, side_of[sign][flow])
-        else:
-            came = {sign: flows[flow, sign] for sign in routes}
-            if distance == 1:
-                ended = {sign: flows["early", sign] for sign in routes}
-                came, ended = after(came, ended)
-                flows.update({("early", sign): ended[sign] for sign in routes})
-            came, _ = after(came, sent)
-            for sign in routes:
-                blocks[sign] = merged(
-                    came[sign], partials[sign * distance], side_of[sign][flow]
-                )
-        for sign in routes:
-            flows[flow, sign] = lax.ppermute(blocks[sign], "store", routes[sign])
-        sent = blocks
-    late = {side_of[sign]["late"]: flows["late", sign] for sign in routes}
-    early, _ = after({side_of[sign]["early"]: flows["early", sign] for sign in routes}, sent)
-    kept = [
-        jax.ShapeDtypeStruct((heads_each, rows_head, HEAD_SIZE), jnp.float32),
-        jax.ShapeDtypeStruct((heads_each, STAT_ROWS, HEAD_SIZE), jnp.bfloat16),
-    ]
-    rest = [
-        call(
-            functools.partial(merge_kernel, side * heads_each, heads_each),
-            kept, early[side], *partials[0],
-        )
-        for side in range(2)
-    ]
+            came = {sign: flows[flow, sign] for sign in back}
+            if distance == 1 and flow == "late":
+                ended = {sign: flows["early", sign] for sign in back}
+                came, ended = lax.optimization_barrier((came, ended))
+                flows.update({("early", sign): ended[sign] for sign in back})
+            came = after(came, token)
+            blocks = {
+                sign: merged(came[sign], parts[sign * distance, side_of[flow, sign]])
+                for sign in back
+            }
+        for sign in back:
+            flows[flow, sign] = lax.ppermute(blocks[sign], "store", back[sign])
+        token = blocks
+    rest, late = [None, None], [None, None]
+    for sign in (1, -1):
+        side = side_of["early", sign]
+        rest[side] = kept(after(flows["early", sign], token), parts[0, side])
+        late[1 - side] = flows["late", sign]
     attended = call(
         functools.partial(final_kernel, suffix),
         jax.ShapeDtypeStruct(queries.shape, queries.dtype),
         late[0], *rest[0], late[1], *rest[1],
     )
-
     return (attended, store)
+
+
+def wire_of(part):
+    heads, rows, columns = part[0].shape
+    return jax.ShapeDtypeStruct((heads, rows + STAT_ROWS, columns), jnp.bfloat16)
+
+
+def packed(part):
+    return call(pack_kernel, wire_of(part), *part)
+
+
+def merged(block, part):
+    return call(merge_kernel, wire_of(part), block, *part)
+
+
+def kept(block, part):
+    return call(merge_kernel, [jax.ShapeDtypeStruct(x.shape, x.dtype) for x in part], block, *part)
 
 
 def on_device(queries, suffix_key_value, kv_pages, page_table, prefix_pages, new_slots):

time: 110 us -> 112 us (1.018)
  Pallas kernels: 37.1 us -> 32.1 us
  starting transfers between devices: 34 us -> 39 us
  waiting for transfers between devices: 30.3 us -> 32.5 us
    ppermute x1, waiting for transfers between devices: 0.01 us -> 5.18 us  [shifted(): return lax.ppermute(block, axis, route)]
    pallas_call x5 -> x8, Pallas kernels: 24.1 us -> 19.2 us  [attend(): pl.pallas_call(functools.partial(attend_kernel, shape + (len(queries), ow...]
    ppermute x28, starting transfers between devices: 32.7 us -> 36.4 us  [the longest x10 15.8 us: queries_travel(): moving[side, sign] = lax.ppermute(came[sign], 'store', routes[sign])]
    ppermute x28, waiting for transfers between devices: 30.3 us -> 27.3 us  [the longest x12 21.2 us: queries_travel(): flows[flow, sign] = lax.ppermute(blocks[sign], 'store', back[sign])]
    ppermute x1, starting transfers between devices: 1.34 us -> 2.59 us  [shifted(): return lax.ppermute(block, axis, route)]
    unnamed x14 -> x12, local copies, waits for them, and re-layouts: 5.01 us -> 5 us
  transfers between devices with their start and end apart: 29 -> 29, of which waited for: 16 -> 19; matrix products, arithmetic and copies ran while one was open for 1% -> 1% of each run, Pallas kernels for 30% -> 24%
where the time goes in v4:
time: 112 us
  starting transfers between devices  39 us (35%)
  waiting for transfers between devices  32.5 us (29%)
  Pallas kernels  32.1 us (29%)
  local copies, waits for them, and re-layouts  5.05 us (5%)
  between operations  2.18 us (2%)
    ppermute x12, waiting for transfers between devices, queries_travel(): flows[flow, sign] = lax.ppermute(blocks[sign], 'store', back[sign])  21.2 us
    pallas_call x8, Pallas kernels, attend(): pl.pallas_call(functools.partial(attend_kernel, shape + (len(queries), ow...  19.2 us
    ppermute x10, starting transfers between devices, queries_travel(): moving[side, sign] = lax.ppermute(came[sign], 'store', routes[sign])  15.8 us
    ppermute x12, starting transfers between devices, queries_travel(): flows[flow, sign] = lax.ppermute(blocks[sign], 'store', back[sign])  12.7 us
    pallas_call x17, Pallas kernels, call(): pl.pallas_call(kernel, out_shape=shape, in_specs=[VMEM] * len(args), out_...  9.25 us
    ppermute x4, starting transfers between devices, queries_travel(): lax.ppermute(mine[side], 'store', routes[sign])  5.44 us
    ppermute x1, waiting for transfers between devices, shifted(): return lax.ppermute(block, axis, route)  5.18 us
    unnamed x12, local copies, waits for them, and re-layouts  5 us
  transfers between devices with their start and end apart: 29, of which 19 were waited for; matrix products, arithmetic and copies ran while one was open for 1% of the time, Pallas kernels for 24%

profile of v4, /device:TPU:0, one launch (start us, length us, event | category | flops | bytes accessed | tf_op | source)
XLA Modules:
  0.0 111.6 jit_solution(14814180455697371987)
XLA Ops:
  1.9 2.1 %shard_map.77 = (bf16[64,2176]{1,0:T(8,128)(2,1)}, bf16[64,2048]{1,0:T(8,128)(2,1)}) custom-call(s32[1]{0:T(128)S(6)} %copy.10.length_ref, s32[1]{0:T(128)S(6)} %copy.11.slot_ref, s32[1,64]{1,0:T(1,128)} %table_ref.1, bf16[1,64,4096]{2,1,0:T(8,128)(2,1)} %q_ref.1), custom_call_target="tpu_custom_call" | custom-call | flops 1 | bytes 1 | tf_op jit(solution)/shard_map/pallas_call | solution.py:385
  4.0 3.0 %collective-permute-start = (bf16[64,2176]{1,0:T(8,128)(2,1)}, bf16[64,2176]{1,0:T(8,128)(2,1)S(1)}, u32[]{:S(2)}, u32[]{:S(2)}) collective-permute-start(bf16[64,2176]{1,0:T(8,128)(2,1)} %get-tuple-element.83.refs_1_), channel_id=1, source_target_pairs={{0,4},{4,8},{8,12},{12,14},{14,10},{10,6},{6,2},{2,0},{1,5},{5,9},... | collective-permute-start | bytes 835592 | tf_op jit(solution)/shard_map/ppermute | solution.py:427
  7.0 2.6 %collective-permute-start.1 = (bf16[1,2,64,512]{3,2,1,0:T(8,128)(2,1)}, bf16[1,2,64,512]{3,2,1,0:T(8,128)(2,1)S(1)}, u32[]{:S(2)}, u32[]{:S(2)}) collective-permute-start(bf16[1,2,64,512]{3,2,1,0:T(8,128)(2,1)} %param.7), channel_id=1, source_target_pairs={{8,0},{10,2},{12,4},{14,6},{0,8},{2,10},{4,12},{6,14},{9,1},{11,3}... | collective-permute-start | bytes 393224 | tf_op jit(solution)/shard_map/ppermute | solution.py:24
  10.0 1.6 %collective-permute-start.5 = (bf16[64,2048]{1,0:T(8,128)(2,1)}, bf16[64,2048]{1,0:T(8,128)(2,1)S(1)}, u32[]{:S(2)}, u32[]{:S(2)}) collective-permute-start(bf16[64,2048]{1,0:T(8,128)(2,1)} %get-tuple-element.84.refs_2_), channel_id=1, source_target_pairs={{0,2},{4,0},{8,4},{12,8},{14,12},{10,14},{6,10},{2,6},{1,3},{5,1},... | collective-permute-start | bytes 786440 | tf_op jit(solution)/shard_map/ppermute | solution.py:427
  11.6 0.4 collective-permute-start.4
  12.0 5.2 %collective-permute-done.1.page_ref = bf16[1,2,64,512]{3,2,1,0:T(8,128)(2,1)S(1)} collective-permute-done((bf16[1,2,64,512]{3,2,1,0:T(8,128)(2,1)}, bf16[1,2,64,512]{3,2,1,0:T(8,128)(2,1)S(1)}, u32[]{:S(2)}, u32[]{:S(2)}) %collective-permute-start.1) | collective-permute-done | bytes 131104 | tf_op jit(solution)/shard_map/ppermute | solution.py:24
  17.2 0.7 fusion.refs_0_
  17.9 2.2 %copy-done = bf16[32,2,64,512]{3,2,1,0:T(8,128)(2,1)S(1)} copy-done((bf16[32,2,64,512]{3,2,1,0:T(8,128)(2,1)S(1)}, bf16[32,2,64,512]{3,2,1,0:T(8,128)(2,1)}, u32[]{:S(2)}) %copy-start) | copy-done | bytes 4194328
  20.1 1.0 copy-done.1
  21.0 0.9 copy-done.2
  22.0 0.9 copy-done.3
  22.9 3.5 %shard_map.78 = (f32[2,512,128]{2,1,0:T(8,128)S(1)}, bf16[2,16,128]{2,1,0:T(8,128)(2,1)S(1)}, f32[2,512,128]{2,1,0:T(8,128)S(1)}, bf16[2,16,128]{2,1,0:T(8,128)(...) custom-call(s32[1,128]{1,0:T(1,128)S(1)} %fusion.refs_0_, ...), custom_call_target="tpu_custom_call" | custom-call | flops 1 | bytes 1 | tf_op jit(solution)/shard_map/pallas_call | solution.py:251
  26.4 4.4 %collective-permute-start.2 = (bf16[64,2176]{1,0:T(8,128)(2,1)S(1)}, bf16[64,2176]{1,0:T(8,128)(2,1)S(1)}, u32[]{:S(2)}, u32[]{:S(2)}) collective-permute-start(bf16[64,2176]{1,0:T(8,128)(2,1)S(1)} %collective-permute-done.refs_1_), channel_id=1, source_target_pairs={{0,4},{4,8},{8,12},{12,14},{14,10},{10,6},{6,2},{2,0},{1,5},{5,9},... | collective-permute-start | bytes 835592 | tf_op jit(solution)/shard_map/ppermute | solution.py:445
  30.9 1.8 %collective-permute-start.7 = (bf16[64,2176]{1,0:T(8,128)(2,1)S(1)}, bf16[64,2176]{1,0:T(8,128)(2,1)S(1)}, u32[]{:S(2)}, u32[]{:S(2)}) collective-permute-start(bf16[64,2176]{1,0:T(8,128)(2,1)S(1)} %collective-permute-done.3.refs_2_), channel_id=1, source_target_pairs={{0,2},{4,0},{8,4},{12,8},{14,12},{10,14},{6,10},{2,6},{1,3},{5,1},... | collective-permute-start | bytes 835592 | tf_op jit(solution)/shard_map/ppermute | solution.py:445
  32.7 2.2 %shard_map.79 = (f32[2,512,128]{2,1,0:T(8,128)S(1)}, bf16[2,16,128]{2,1,0:T(8,128)(2,1)S(1)}, f32[2,512,128]{2,1,0:T(8,128)S(1)}, bf16[2,16,128]{2,1,0:T(8,128)(2,1)S(1)}) custom-call(s32[2,128]{1,0:T(2,128)S(1)} %maximum_convert_fusion.refs_0_, bf16[64,2176]{1,0:T(8,128)(2,1)S(1)} %collective-permute-done.refs_1_, ...), custom_call_target="tpu_custom_call" | custom-call | flops 1 | bytes 1 | tf_op jit(solution)/shard_map/pallas_call | solution.py:251
  35.3 1.8 %collective-permute-start.9 = (bf16[64,2048]{1,0:T(8,128)(2,1)S(1)}, bf16[64,2048]{1,0:T(8,128)(2,1)S(1)}, u32[]{:S(2)}, u32[]{:S(2)}) collective-permute-start(bf16[64,2048]{1,0:T(8,128)(2,1)S(1)} %collective-permute-done.5.refs_2_), channel_id=1, source_target_pairs={{0,2},{4,0},{8,4},{12,8},{14,12},{10,14},{6,10},{2,6},{1,3},{5,1},... | collective-permute-start | bytes 786440 | tf_op jit(solution)/shard_map/ppermute | solution.py:445
  37.1 2.2 %shard_map.80 = (f32[2,512,128]{2,1,0:T(8,128)S(1)}, bf16[2,16,128]{2,1,0:T(8,128)(2,1)S(1)}, f32[2,512,128]{2,1,0:T(8,128)S(1)}, bf16[2,16,128]{2,1,0:T(8,128)(2,1)S(1)}) custom-call(s32[2,128]{1,0:T(2,128)S(1)} %maximum_convert_fusion.refs_0_, bf16[64,2048]{1,0:T(8,128)(2,1)S(1)} %collective-permute-done.4.refs_1_, ...), custom_call_target="tpu_custom_call" | custom-call | flops 1 | bytes 1 | tf_op jit(solution)/shard_map/pallas_call | solution.py:251
  39.9 2.2 %collective-permute-start.12 = (bf16[64,2176]{1,0:T(8,128)(2,1)S(1)}, bf16[64,2176]{1,0:T(8,128)(2,1)S(1)}, u32[]{:S(2)}, u32[]{:S(2)}) collective-permute-start(bf16[64,2176]{1,0:T(8,128)(2,1)S(1)} %collective-permute-done.7.refs_2_), channel_id=1, source_target_pairs={{0,2},{4,0},{8,4},{12,8},{14,12},{10,14},{6,10},{2,6},{1,3},{5,1},... | collective-permute-start | bytes 835592 | tf_op jit(solution)/shard_map/ppermute | solution.py:445
  42.1 2.2 %shard_map.81 = (f32[2,512,128]{2,1,0:T(8,128)S(1)}, bf16[2,16,128]{2,1,0:T(8,128)(2,1)S(1)}, f32[2,512,128]{2,1,0:T(8,128)S(1)}, bf16[2,16,128]{2,1,0:T(8,128)(2,1)S(1)}) custom-call(s32[2,128]{1,0:T(2,128)S(1)} %maximum_convert_fusion.1.refs_0_.lists_ref, bf16[64,2176]{1,0:T(8,128)(2,1)S(1)} %collective-permute-done.2.refs_1_, ...), custom_call_target="tpu_custom_call" | custom-call | flops 1 | bytes 1 | tf_op jit(solution)/shard_map/pallas_call | solution.py:251
  44.4 1.0 collective-permute-done.9.refs_2_
  45.4 1.9 %collective-permute-start.14 = (bf16[64,2048]{1,0:T(8,128)(2,1)S(1)}, bf16[64,2048]{1,0:T(8,128)(2,1)S(1)}, u32[]{:S(2)}, u32[]{:S(2)}) collective-permute-start(bf16[64,2048]{1,0:T(8,128)(2,1)S(1)} %collective-permute-done.8.refs_1_), channel_id=1, source_target_pairs={{0,4},{4,8},{8,12},{12,14},{14,10},{10,6},{6,2},{2,0},{1,5},{5,9},... | collective-permute-start | bytes 786440 | tf_op jit(solution)/shard_map/ppermute | solution.py:445
  47.7 2.2 %shard_map.82 = (f32[2,512,128]{2,1,0:T(8,128)S(1)}, bf16[2,16,128]{2,1,0:T(8,128)(2,1)S(1)}, f32[2,512,128]{2,1,0:T(8,128)S(1)}, bf16[2,16,128]{2,1,0:T(8,128)(2,1)S(1)}) custom-call(s32[2,128]{1,0:T(2,128)S(1)} %maximum_convert_fusion.1.refs_0_.lists_ref, bf16[64,2048]{1,0:T(8,128)(2,1)S(1)} %collective-permute-done.8.refs_1_, ...), custom_call_target="tpu_custom_call" | custom-call | flops 1 | bytes 1 | tf_op jit(solution)/shard_map/pallas_call | solution.py:251
  50.0 1.3 %collective-permute-done.6.refs_1_ = bf16[64,2176]{1,0:T(8,128)(2,1)S(1)} collective-permute-done((bf16[64,2176]{1,0:T(8,128)(2,1)S(1)}, bf16[64,2176]{1,0:T(8,128)(2,1)S(1)}, u32[]{:S(2)}, u32[]{:S(2)}) %collective-permute-start.6) | collective-permute-done | bytes 278560 | tf_op jit(solution)/shard_map/ppermute | solution.py:445
  51.3 0.9 collective-permute-start.10
  52.2 2.2 %shard_map.83 = (f32[2,512,128]{2,1,0:T(8,128)S(1)}, bf16[2,16,128]{2,1,0:T(8,128)(2,1)S(1)}, f32[2,512,128]{2,1,0:T(8,128)S(1)}, bf16[2,16,128]{2,1,0:T(8,128)(2,1)S(1)}) custom-call(s32[2,128]{1,0:T(2,128)S(1)} %maximum_convert_fusion.2.refs_0_, bf16[64,2176]{1,0:T(8,128)(2,1)S(1)} %collective-permute-done.6.refs_1_, ...), custom_call_target="tpu_custom_call" | custom-call | flops 1 | bytes 1 | tf_op jit(solution)/shard_map/pallas_call | solution.py:251
  54.7 1.8 %collective-permute-start.13 = (bf16[64,2048]{1,0:T(8,128)(2,1)S(1)}, bf16[64,2048]{1,0:T(8,128)(2,1)S(1)}, u32[]{:S(2)}, u32[]{:S(2)}) collective-permute-start(bf16[64,2048]{1,0:T(8,128)(2,1)S(1)} %collective-permute-done.11.refs_2_), channel_id=1, source_target_pairs={{0,2},{4,0},{8,4},{12,8},{14,12},{10,14},{6,10},{2,6},{1,3},{5,1},... | collective-permute-start | bytes 786440 | tf_op jit(solution)/shard_map/ppermute | solution.py:445
  56.9 2.3 %shard_map.85 = (f32[2,512,128]{2,1,0:T(8,128)S(1)}, bf16[2,16,128]{2,1,0:T(8,128)(2,1)S(1)}, f32[2,512,128]{2,1,0:T(8,128)S(1)}, bf16[2,16,128]{2,1,0:T(8,128)(2,1)S(1)}) custom-call(s32[2,128]{1,0:T(2,128)S(1)} %maximum_convert_fusion.2.refs_0_, bf16[64,2048]{1,0:T(8,128)(2,1)S(1)} %collective-permute-done.14.refs_1_, ...), custom_call_target="tpu_custom_call" | custom-call | flops 1 | bytes 1 | tf_op jit(solution)/shard_map/pallas_call | solution.py:251
  59.2 2.3 %collective-permute-start.16 = (bf16[2,528,128]{2,1,0:T(8,128)(2,1)S(1)}, bf16[2,528,128]{2,1,0:T(8,128)(2,1)S(1)}, u32[]{:S(2)}, u32[]{:S(2)}) collective-permute-start(bf16[2,528,128]{2,1,0:T(8,128)(2,1)S(1)} %shard_map.86), channel_id=1, source_target_pairs={{0,2},{4,0},{8,4},{12,8},{14,12},{10,14},{6,10},{2,6},{1,3},{5,1},... | collective-permute-start | bytes 811016 | tf_op jit(solution)/shard_map/ppermute | solution.py:463
  61.5 1.7 %collective-permute-done.13.refs_2_ = bf16[64,2048]{1,0:T(8,128)(2,1)S(1)} collective-permute-done((bf16[64,2048]{1,0:T(8,128)(2,1)S(1)}, bf16[64,2048]{1,0:T(8,128)(2,1)S(1)}, u32[]{:S(2)}, u32[]{:S(2)}) %collective-permute-start.13) | collective-permute-done | bytes 262176 | tf_op jit(solution)/shard_map/ppermute | solution.py:445
  63.2 2.2 %shard_map.87 = (f32[2,512,128]{2,1,0:T(8,128)S(1)}, bf16[2,16,128]{2,1,0:T(8,128)(2,1)S(1)}, f32[2,512,128]{2,1,0:T(8,128)S(1)}, bf16[2,16,128]{2,1,0:T(8,128)(2,1)S(1)}) custom-call(s32[1,128]{1,0:T(1,128)S(1)} %fusion.1.refs_0_, bf16[64,2176]{1,0:T(8,128)(2,1)S(1)} %collective-permute-done.10.refs_1_, ...), custom_call_target="tpu_custom_call" | custom-call | flops 1 | bytes 1 | tf_op jit(solution)/shard_map/pallas_call | solution.py:251
  65.5 0.6 collective-permute-done.15.in_ref
  66.1 0.7 collective-permute-done.16.in_ref
  66.9 1.9 %collective-permute-start.18 = (bf16[2,528,128]{2,1,0:T(8,128)(2,1)S(1)}, bf16[2,528,128]{2,1,0:T(8,128)(2,1)S(1)}, u32[]{:S(2)}, u32[]{:S(2)}) collective-permute-start(bf16[2,528,128]{2,1,0:T(8,128)(2,1)S(1)} %shard_map.89), channel_id=1, source_target_pairs={{0,2},{4,0},{8,4},{12,8},{14,12},{10,14},{6,10},{2,6},{1,3},{5,1},... | collective-permute-start | bytes 811016 | tf_op jit(solution)/shard_map/ppermute | solution.py:487
  69.0 0.6 shard_map.90
  69.7 1.9 %collective-permute-start.21 = (bf16[2,528,128]{2,1,0:T(8,128)(2,1)S(1)}, bf16[2,528,128]{2,1,0:T(8,128)(2,1)S(1)}, u32[]{:S(2)}, u32[]{:S(2)}) collective-permute-start(bf16[2,528,128]{2,1,0:T(8,128)(2,1)S(1)} %shard_map.90), channel_id=1, source_target_pairs={{0,4},{4,8},{8,12},{12,14},{14,10},{10,6},{6,2},{2,0},{1,5},{5,9},... | collective-permute-start | bytes 811016 | tf_op jit(solution)/shard_map/ppermute | solution.py:487
  71.6 0.6 shard_map.91
  72.4 3.2 %collective-permute-done.18.in_ref = bf16[2,528,128]{2,1,0:T(8,128)(2,1)S(1)} collective-permute-done((bf16[2,528,128]{2,1,0:T(8,128)(2,1)S(1)}, bf16[2,528,128]{2,1,0:T(8,128)(2,1)S(1)}, u32[]{:S(2)}, u32[]{:S(2)}) %collective-permute-start.18) | collective-permute-done | bytes 270368 | tf_op jit(solution)/shard_map/ppermute | solution.py:487
  75.6 2.5 %collective-permute-done.17.in_ref = bf16[2,528,128]{2,1,0:T(8,128)(2,1)S(1)} collective-permute-done((bf16[2,528,128]{2,1,0:T(8,128)(2,1)S(1)}, bf16[2,528,128]{2,1,0:T(8,128)(2,1)S(1)}, u32[]{:S(2)}, u32[]{:S(2)}) %collective-permute-start.17) | collective-permute-done | bytes 270368 | tf_op jit(solution)/shard_map/ppermute | solution.py:487
  78.1 0.6 shard_map.93
  78.7 1.8 %collective-permute-start.20 = (bf16[2,528,128]{2,1,0:T(8,128)(2,1)S(1)}, bf16[2,528,128]{2,1,0:T(8,128)(2,1)S(1)}, u32[]{:S(2)}, u32[]{:S(2)}) collective-permute-start(bf16[2,528,128]{2,1,0:T(8,128)(2,1)S(1)} %shard_map.93), channel_id=1, source_target_pairs={{0,2},{4,0},{8,4},{12,8},{14,12},{10,14},{6,10},{2,6},{1,3},{5,1},... | collective-permute-start | bytes 811016 | tf_op jit(solution)/shard_map/ppermute | solution.py:487
  80.5 0.6 shard_map.92
  81.5 2.4 %collective-permute-done.21.in_ref = bf16[2,528,128]{2,1,0:T(8,128)(2,1)S(1)} collective-permute-done((bf16[2,528,128]{2,1,0:T(8,128)(2,1)S(1)}, bf16[2,528,128]{2,1,0:T(8,128)(2,1)S(1)}, u32[]{:S(2)}, u32[]{:S(2)}) %collective-permute-start.21) | collective-permute-done | bytes 270368 | tf_op jit(solution)/shard_map/ppermute | solution.py:487
  83.9 0.6 shard_map.94
  84.9 0.6 shard_map.95
  85.5 1.7 %collective-permute-start.26 = (bf16[2,528,128]{2,1,0:T(8,128)(2,1)S(1)}, bf16[2,528,128]{2,1,0:T(8,128)(2,1)S(1)}, u32[]{:S(2)}, u32[]{:S(2)}) collective-permute-start(bf16[2,528,128]{2,1,0:T(8,128)(2,1)S(1)} %shard_map.95), channel_id=1, source_target_pairs={{0,2},{4,0},{8,4},{12,8},{14,12},{10,14},{6,10},{2,6},{1,3},{5,1},... | collective-permute-start | bytes 811016 | tf_op jit(solution)/shard_map/ppermute | solution.py:487
  87.3 0.9 collective-permute-done.20.in_ref
  88.1 2.2 %collective-permute-done.19.in_ref = bf16[2,528,128]{2,1,0:T(8,128)(2,1)S(1)} collective-permute-done((bf16[2,528,128]{2,1,0:T(8,128)(2,1)S(1)}, bf16[2,528,128]{2,1,0:T(8,128)(2,1)S(1)}, u32[]{:S(2)}, u32[]{:S(2)}) %collective-permute-start.19) | collective-permute-done | bytes 270368 | tf_op jit(solution)/shard_map/ppermute | solution.py:487
  90.4 0.6 shard_map.96
  91.0 0.6 shard_map.97
  91.6 1.1 %collective-permute-start.24 = (bf16[2,528,128]{2,1,0:T(8,128)(2,1)S(1)}, bf16[2,528,128]{2,1,0:T(8,128)(2,1)S(1)}, u32[]{:S(2)}, u32[]{:S(2)}) collective-permute-start(bf16[2,528,128]{2,1,0:T(8,128)(2,1)S(1)} %shard_map.97), channel_id=1, source_target_pairs={{0,2},{4,0},{8,4},{12,8},{14,12},{10,14},{6,10},{2,6},{1,3},{5,1},... | collective-permute-start | bytes 811016 | tf_op jit(solution)/shard_map/ppermute | solution.py:487
  92.7 1.0 collective-permute-start.23
  93.7 0.9 collective-permute-done.25.in_ref
  94.6 3.5 %collective-permute-done.24.in_ref = bf16[2,528,128]{2,1,0:T(8,128)(2,1)S(1)} collective-permute-done((bf16[2,528,128]{2,1,0:T(8,128)(2,1)S(1)}, bf16[2,528,128]{2,1,0:T(8,128)(2,1)S(1)}, u32[]{:S(2)}, u32[]{:S(2)}) %collective-permute-start.24) | collective-permute-done | bytes 270368 | tf_op jit(solution)/shard_map/ppermute | solution.py:487
  98.1 3.2 %collective-permute-done.23.in_ref = bf16[2,528,128]{2,1,0:T(8,128)(2,1)S(1)} collective-permute-done((bf16[2,528,128]{2,1,0:T(8,128)(2,1)S(1)}, bf16[2,528,128]{2,1,0:T(8,128)(2,1)S(1)}, u32[]{:S(2)}, u32[]{:S(2)}) %collective-permute-start.23) | collective-permute-done | bytes 270368 | tf_op jit(solution)/shard_map/ppermute | solution.py:487
  101.3 0.6 shard_map.98
  101.9 0.6 shard_map.99
  102.6 0.8 collective-permute-start.28
  103.4 1.2 %collective-permute-start.27 = (bf16[2,528,128]{2,1,0:T(8,128)(2,1)S(1)}, bf16[2,528,128]{2,1,0:T(8,128)(2,1)S(1)}, u32[]{:S(2)}, u32[]{:S(2)}) collective-permute-start(bf16[2,528,128]{2,1,0:T(8,128)(2,1)S(1)} %shard_map.98), channel_id=1, source_target_pairs={{0,2},{4,0},{8,4},{12,8},{14,12},{10,14},{6,10},{2,6},{1,3},{5,1},... | collective-permute-start | bytes 811016 | tf_op jit(solution)/shard_map/ppermute | solution.py:487
  104.6 1.6 %shard_map.103 = bf16[32,2,64,512]{3,2,1,0:T(8,128)(2,1)} custom-call(s32[1]{0:T(128)} %bitcast.1.me_ref, s32[2,128]{1,0:T(2,128)} %copy-done.4, bf16[1,2,64,512]{3,2,1,0:T(8,128)(2,1)} %copy-done.5, bf16[32,2,64,512]{3,2,1,0:T(8,128)(2,1)} %get-tuple-element.159.old_ref), custom_call_target="tpu_custom_call", output_to_operand_aliasing={{}: (3, {})} | custom-call | flops 1 | bytes 1 | tf_op jit(solution)/shard_map/pallas_call | solution.py:273
  106.2 0.6 shard_map.101
  106.9 0.6 shard_map.100
  107.5 1.6 %collective-permute-done.28.refs_3_ = bf16[2,528,128]{2,1,0:T(8,128)(2,1)S(1)} collective-permute-done((bf16[2,528,128]{2,1,0:T(8,128)(2,1)S(1)}, bf16[2,528,128]{2,1,0:T(8,128)(2,1)S(1)}, u32[]{:S(2)}, u32[]{:S(2)}) %collective-permute-start.28) | collective-permute-done | bytes 270368 | tf_op jit(solution)/shard_map/ppermute | solution.py:487
  109.1 0.8 collective-permute-done.27.refs_0_
  109.9 1.7 %shard_map.102 = bf16[1,64,4096]{2,1,0:T(8,128)(2,1)} custom-call(bf16[2,528,128]{2,1,0:T(8,128)(2,1)S(1)} %collective-permute-done.27.refs_0_, f32[2,512,128]{2,1,0:T(8,128)S(1)} %get-tuple-element.152.refs_1_, bf16[2,16,128]{2,1,0:T(8,128)(2,1)S(1)} %get-tuple-element.153.refs_2_, bf16[2,528,128]{2,1,0:T(8,128)(2,1)S(1)} %collective-permute-done.28.refs_3_, ...), custom_call_target="tpu_custom_call" | custom-call | flops 1605632 | bytes 3211264 | tf_op jit(solution)/shard_map/pallas_call | solution.py:344
  (44 shorter events, 3.6 us)
Async XLA Ops:
  4.0 22.4 %collective-permute-start = (bf16[64,2176]{1,0:T(8,128)(2,1)}, bf16[64,2176]{1,0:T(8,128)(2,1)S(1)}, u32[]{:S(2)}, u32[]{:S(2)}) collective-permute-start(bf16[64,2176]{1,0:T(8,128)(2,1)} %get-tuple-element.83.refs_1_), channel_id=1, source_target_pairs={{0,4},{4,8},{8,12},{12,14},{14,10},{10,6},{6,2},{2,0},{1,5},{5,9},... | collective-permute-start | bytes 835592 | tf_op jit(solution)/shard_map/ppermute | solution.py:427
  7.0 10.2 %collective-permute-start.1 = (bf16[1,2,64,512]{3,2,1,0:T(8,128)(2,1)}, bf16[1,2,64,512]{3,2,1,0:T(8,128)(2,1)S(1)}, u32[]{:S(2)}, u32[]{:S(2)}) collective-permute-start(bf16[1,2,64,512]{3,2,1,0:T(8,128)(2,1)} %param.7), channel_id=1, source_target_pairs={{8,0},{10,2},{12,4},{14,6},{0,8},{2,10},{4,12},{6,14},{9,1},{11,3}... | collective-permute-start | bytes 393224 | tf_op jit(solution)/shard_map/ppermute | solution.py:24
  9.6 21.3 %collective-permute-start.3 = (bf16[64,2176]{1,0:T(8,128)(2,1)}, bf16[64,2176]{1,0:T(8,128)(2,1)S(1)}, u32[]{:S(2)}, u32[]{:S(2)}) collective-permute-start(bf16[64,2176]{1,0:T(8,128)(2,1)} %get-tuple-element.83.refs_1_), channel_id=1, source_target_pairs={{0,2},{4,0},{8,4},{12,8},{14,12},{10,14},{6,10},{2,6},{1,3},{5,1},... | collective-permute-start | bytes 835592 | tf_op jit(solution)/shard_map/ppermute | solution.py:427
  10.0 25.0 %collective-permute-start.5 = (bf16[64,2048]{1,0:T(8,128)(2,1)}, bf16[64,2048]{1,0:T(8,128)(2,1)S(1)}, u32[]{:S(2)}, u32[]{:S(2)}) collective-permute-start(bf16[64,2048]{1,0:T(8,128)(2,1)} %get-tuple-element.84.refs_2_), channel_id=1, source_target_pairs={{0,2},{4,0},{8,4},{12,8},{14,12},{10,14},{6,10},{2,6},{1,3},{5,1},... | collective-permute-start | bytes 786440 | tf_op jit(solution)/shard_map/ppermute | solution.py:427
  11.6 23.4 %collective-permute-start.4 = (bf16[64,2048]{1,0:T(8,128)(2,1)}, bf16[64,2048]{1,0:T(8,128)(2,1)S(1)}, u32[]{:S(2)}, u32[]{:S(2)}) collective-permute-start(bf16[64,2048]{1,0:T(8,128)(2,1)} %get-tuple-element.84.refs_2_), channel_id=1, source_target_pairs={{0,4},{4,8},{8,12},{12,14},{14,10},{10,6},{6,2},{2,0},{1,5},{5,9},... | collective-permute-start | bytes 786440 | tf_op jit(solution)/shard_map/ppermute | solution.py:427
  17.2 17.8 %copy-start.5 = (bf16[1,2,64,512]{3,2,1,0:T(8,128)(2,1)}, bf16[1,2,64,512]{3,2,1,0:T(8,128)(2,1)S(1)}, u32[]{:S(2)}) copy-start(bf16[1,2,64,512]{3,2,1,0:T(8,128)(2,1)S(1)} %collective-permute-done.1.page_ref) | copy-start | bytes 393220
  17.9 2.2 %copy-start = (bf16[32,2,64,512]{3,2,1,0:T(8,128)(2,1)S(1)}, bf16[32,2,64,512]{3,2,1,0:T(8,128)(2,1)}, u32[]{:S(2)}) copy-start(bf16[32,2,64,512]{3,2,1,0:T(8,128)(2,1)} %refs_4_.1) | copy-start | bytes 12582916
  20.1 1.0 copy-start.1
  21.0 0.9 copy-start.2
  22.0 0.9 copy-start.3
  26.4 13.3 %collective-permute-start.2 = (bf16[64,2176]{1,0:T(8,128)(2,1)S(1)}, bf16[64,2176]{1,0:T(8,128)(2,1)S(1)}, u32[]{:S(2)}, u32[]{:S(2)}) collective-permute-start(bf16[64,2176]{1,0:T(8,128)(2,1)S(1)} %collective-permute-done.refs_1_), channel_id=1, source_target_pairs={{0,4},{4,8},{8,12},{12,14},{14,10},{10,6},{6,2},{2,0},{1,5},{5,9},... | collective-permute-start | bytes 835592 | tf_op jit(solution)/shard_map/ppermute | solution.py:445
  30.9 9.0 %collective-permute-start.7 = (bf16[64,2176]{1,0:T(8,128)(2,1)S(1)}, bf16[64,2176]{1,0:T(8,128)(2,1)S(1)}, u32[]{:S(2)}, u32[]{:S(2)}) collective-permute-start(bf16[64,2176]{1,0:T(8,128)(2,1)S(1)} %collective-permute-done.3.refs_2_), channel_id=1, source_target_pairs={{0,2},{4,0},{8,4},{12,8},{14,12},{10,14},{6,10},{2,6},{1,3},{5,1},... | collective-permute-start | bytes 835592 | tf_op jit(solution)/shard_map/ppermute | solution.py:445
  35.0 10.4 %collective-permute-start.8 = (bf16[64,2048]{1,0:T(8,128)(2,1)S(1)}, bf16[64,2048]{1,0:T(8,128)(2,1)S(1)}, u32[]{:S(2)}, u32[]{:S(2)}) collective-permute-start(bf16[64,2048]{1,0:T(8,128)(2,1)S(1)} %collective-permute-done.4.refs_1_), channel_id=1, source_target_pairs={{0,4},{4,8},{8,12},{12,14},{14,10},{10,6},{6,2},{2,0},{1,5},{5,9},... | collective-permute-start | bytes 786440 | tf_op jit(solution)/shard_map/ppermute | solution.py:445
  35.3 10.1 %collective-permute-start.9 = (bf16[64,2048]{1,0:T(8,128)(2,1)S(1)}, bf16[64,2048]{1,0:T(8,128)(2,1)S(1)}, u32[]{:S(2)}, u32[]{:S(2)}) collective-permute-start(bf16[64,2048]{1,0:T(8,128)(2,1)S(1)} %collective-permute-done.5.refs_2_), channel_id=1, source_target_pairs={{0,2},{4,0},{8,4},{12,8},{14,12},{10,14},{6,10},{2,6},{1,3},{5,1},... | collective-permute-start | bytes 786440 | tf_op jit(solution)/shard_map/ppermute | solution.py:445
  39.7 11.6 %collective-permute-start.6 = (bf16[64,2176]{1,0:T(8,128)(2,1)S(1)}, bf16[64,2176]{1,0:T(8,128)(2,1)S(1)}, u32[]{:S(2)}, u32[]{:S(2)}) collective-permute-start(bf16[64,2176]{1,0:T(8,128)(2,1)S(1)} %collective-permute-done.2.refs_1_), channel_id=1, source_target_pairs={{0,4},{4,8},{8,12},{12,14},{14,10},{10,6},{6,2},{2,0},{1,5},{5,9},... | collective-permute-start | bytes 835592 | tf_op jit(solution)/shard_map/ppermute | solution.py:445
  39.9 12.3 %collective-permute-start.12 = (bf16[64,2176]{1,0:T(8,128)(2,1)S(1)}, bf16[64,2176]{1,0:T(8,128)(2,1)S(1)}, u32[]{:S(2)}, u32[]{:S(2)}) collective-permute-start(bf16[64,2176]{1,0:T(8,128)(2,1)S(1)} %collective-permute-done.7.refs_2_), channel_id=1, source_target_pairs={{0,2},{4,0},{8,4},{12,8},{14,12},{10,14},{6,10},{2,6},{1,3},{5,1},... | collective-permute-start | bytes 835592 | tf_op jit(solution)/shard_map/ppermute | solution.py:445
  42.1 7.9 %copy-start.4 = (s32[2,128]{1,0:T(2,128)}, s32[2,128]{1,0:T(2,128)S(1)}, u32[]{:S(2)}) copy-start(s32[2,128]{1,0:T(2,128)S(1)} %maximum_convert_fusion.1.refs_0_.lists_ref) | copy-start | bytes 3076
  45.4 11.5 %collective-permute-start.14 = (bf16[64,2048]{1,0:T(8,128)(2,1)S(1)}, bf16[64,2048]{1,0:T(8,128)(2,1)S(1)}, u32[]{:S(2)}, u32[]{:S(2)}) collective-permute-start(bf16[64,2048]{1,0:T(8,128)(2,1)S(1)} %collective-permute-done.8.refs_1_), channel_id=1, source_target_pairs={{0,4},{4,8},{8,12},{12,14},{14,10},{10,6},{6,2},{2,0},{1,5},{5,9},... | collective-permute-start | bytes 786440 | tf_op jit(solution)/shard_map/ppermute | solution.py:445
  47.3 7.4 %collective-permute-start.11 = (bf16[64,2048]{1,0:T(8,128)(2,1)S(1)}, bf16[64,2048]{1,0:T(8,128)(2,1)S(1)}, u32[]{:S(2)}, u32[]{:S(2)}) collective-permute-start(bf16[64,2048]{1,0:T(8,128)(2,1)S(1)} %collective-permute-done.9.refs_2_), channel_id=1, source_target_pairs={{0,2},{4,0},{8,4},{12,8},{14,12},{10,14},{6,10},{2,6},{1,3},{5,1},... | collective-permute-start | bytes 786440 | tf_op jit(solution)/shard_map/ppermute | solution.py:445
  51.3 11.9 %collective-permute-start.10 = (bf16[64,2176]{1,0:T(8,128)(2,1)S(1)}, bf16[64,2176]{1,0:T(8,128)(2,1)S(1)}, u32[]{:S(2)}, u32[]{:S(2)}) collective-permute-start(bf16[64,2176]{1,0:T(8,128)(2,1)S(1)} %collective-permute-done.6.refs_1_), channel_id=1, source_target_pairs={{0,4},{4,8},{8,12},{12,14},{14,10},{10,6},{6,2},{2,0},{1,5},{5,9},... | collective-permute-start | bytes 835592 | tf_op jit(solution)/shard_map/ppermute | solution.py:445
  54.7 8.5 %collective-permute-start.13 = (bf16[64,2048]{1,0:T(8,128)(2,1)S(1)}, bf16[64,2048]{1,0:T(8,128)(2,1)S(1)}, u32[]{:S(2)}, u32[]{:S(2)}) collective-permute-start(bf16[64,2048]{1,0:T(8,128)(2,1)S(1)} %collective-permute-done.11.refs_2_), channel_id=1, source_target_pairs={{0,2},{4,0},{8,4},{12,8},{14,12},{10,14},{6,10},{2,6},{1,3},{5,1},... | collective-permute-start | bytes 786440 | tf_op jit(solution)/shard_map/ppermute | solution.py:445
  56.5 9.6 %collective-permute-start.15 = (bf16[2,528,128]{2,1,0:T(8,128)(2,1)S(1)}, bf16[2,528,128]{2,1,0:T(8,128)(2,1)S(1)}, u32[]{:S(2)}, u32[]{:S(2)}) collective-permute-start(bf16[2,528,128]{2,1,0:T(8,128)(2,1)S(1)} %shard_map.84), channel_id=1, source_target_pairs={{0,4},{4,8},{8,12},{12,14},{14,10},{10,6},{6,2},{2,0},{1,5},{5,9},... | collective-permute-start | bytes 811016 | tf_op jit(solution)/shard_map/ppermute | solution.py:463
  59.2 7.7 %collective-permute-start.16 = (bf16[2,528,128]{2,1,0:T(8,128)(2,1)S(1)}, bf16[2,528,128]{2,1,0:T(8,128)(2,1)S(1)}, u32[]{:S(2)}, u32[]{:S(2)}) collective-permute-start(bf16[2,528,128]{2,1,0:T(8,128)(2,1)S(1)} %shard_map.86), channel_id=1, source_target_pairs={{0,2},{4,0},{8,4},{12,8},{14,12},{10,14},{6,10},{2,6},{1,3},{5,1},... | collective-permute-start | bytes 811016 | tf_op jit(solution)/shard_map/ppermute | solution.py:463
  66.9 8.8 %collective-permute-start.18 = (bf16[2,528,128]{2,1,0:T(8,128)(2,1)S(1)}, bf16[2,528,128]{2,1,0:T(8,128)(2,1)S(1)}, u32[]{:S(2)}, u32[]{:S(2)}) collective-permute-start(bf16[2,528,128]{2,1,0:T(8,128)(2,1)S(1)} %shard_map.89), channel_id=1, source_target_pairs={{0,2},{4,0},{8,4},{12,8},{14,12},{10,14},{6,10},{2,6},{1,3},{5,1},... | collective-permute-start | bytes 811016 | tf_op jit(solution)/shard_map/ppermute | solution.py:487
  68.8 9.3 %collective-permute-start.17 = (bf16[2,528,128]{2,1,0:T(8,128)(2,1)S(1)}, bf16[2,528,128]{2,1,0:T(8,128)(2,1)S(1)}, u32[]{:S(2)}, u32[]{:S(2)}) collective-permute-start(bf16[2,528,128]{2,1,0:T(8,128)(2,1)S(1)} %shard_map.88), channel_id=1, source_target_pairs={{0,4},{4,8},{8,12},{12,14},{14,10},{10,6},{6,2},{2,0},{1,5},{5,9},... | collective-permute-start | bytes 811016 | tf_op jit(solution)/shard_map/ppermute | solution.py:487
  69.7 14.2 %collective-permute-start.21 = (bf16[2,528,128]{2,1,0:T(8,128)(2,1)S(1)}, bf16[2,528,128]{2,1,0:T(8,128)(2,1)S(1)}, u32[]{:S(2)}, u32[]{:S(2)}) collective-permute-start(bf16[2,528,128]{2,1,0:T(8,128)(2,1)S(1)} %shard_map.90), channel_id=1, source_target_pairs={{0,4},{4,8},{8,12},{12,14},{14,10},{10,6},{6,2},{2,0},{1,5},{5,9},... | collective-permute-start | bytes 811016 | tf_op jit(solution)/shard_map/ppermute | solution.py:487
  72.2 11.7 %collective-permute-start.22 = (bf16[2,528,128]{2,1,0:T(8,128)(2,1)S(1)}, bf16[2,528,128]{2,1,0:T(8,128)(2,1)S(1)}, u32[]{:S(2)}, u32[]{:S(2)}) collective-permute-start(bf16[2,528,128]{2,1,0:T(8,128)(2,1)S(1)} %shard_map.91), channel_id=1, source_target_pairs={{0,2},{4,0},{8,4},{12,8},{14,12},{10,14},{6,10},{2,6},{1,3},{5,1},... | collective-permute-start | bytes 811016 | tf_op jit(solution)/shard_map/ppermute | solution.py:487
  78.7 9.4 %collective-permute-start.20 = (bf16[2,528,128]{2,1,0:T(8,128)(2,1)S(1)}, bf16[2,528,128]{2,1,0:T(8,128)(2,1)S(1)}, u32[]{:S(2)}, u32[]{:S(2)}) collective-permute-start(bf16[2,528,128]{2,1,0:T(8,128)(2,1)S(1)} %shard_map.93), channel_id=1, source_target_pairs={{0,2},{4,0},{8,4},{12,8},{14,12},{10,14},{6,10},{2,6},{1,3},{5,1},... | collective-permute-start | bytes 811016 | tf_op jit(solution)/shard_map/ppermute | solution.py:487
  81.2 9.2 %collective-permute-start.19 = (bf16[2,528,128]{2,1,0:T(8,128)(2,1)S(1)}, bf16[2,528,128]{2,1,0:T(8,128)(2,1)S(1)}, u32[]{:S(2)}, u32[]{:S(2)}) collective-permute-start(bf16[2,528,128]{2,1,0:T(8,128)(2,1)S(1)} %shard_map.92), channel_id=1, source_target_pairs={{0,4},{4,8},{8,12},{12,14},{14,10},{10,6},{6,2},{2,0},{1,5},{5,9},... | collective-permute-start | bytes 811016 | tf_op jit(solution)/shard_map/ppermute | solution.py:487
  84.5 10.1 %collective-permute-start.25 = (bf16[2,528,128]{2,1,0:T(8,128)(2,1)S(1)}, bf16[2,528,128]{2,1,0:T(8,128)(2,1)S(1)}, u32[]{:S(2)}, u32[]{:S(2)}) collective-permute-start(bf16[2,528,128]{2,1,0:T(8,128)(2,1)S(1)} %shard_map.94), channel_id=1, source_target_pairs={{0,4},{4,8},{8,12},{12,14},{14,10},{10,6},{6,2},{2,0},{1,5},{5,9},... | collective-permute-start | bytes 811016 | tf_op jit(solution)/shard_map/ppermute | solution.py:487
  85.5 9.1 %collective-permute-start.26 = (bf16[2,528,128]{2,1,0:T(8,128)(2,1)S(1)}, bf16[2,528,128]{2,1,0:T(8,128)(2,1)S(1)}, u32[]{:S(2)}, u32[]{:S(2)}) collective-permute-start(bf16[2,528,128]{2,1,0:T(8,128)(2,1)S(1)} %shard_map.95), channel_id=1, source_target_pairs={{0,2},{4,0},{8,4},{12,8},{14,12},{10,14},{6,10},{2,6},{1,3},{5,1},... | collective-permute-start | bytes 811016 | tf_op jit(solution)/shard_map/ppermute | solution.py:487
  91.6 6.5 %collective-permute-start.24 = (bf16[2,528,128]{2,1,0:T(8,128)(2,1)S(1)}, bf16[2,528,128]{2,1,0:T(8,128)(2,1)S(1)}, u32[]{:S(2)}, u32[]{:S(2)}) collective-permute-start(bf16[2,528,128]{2,1,0:T(8,128)(2,1)S(1)} %shard_map.97), channel_id=1, source_target_pairs={{0,2},{4,0},{8,4},{12,8},{14,12},{10,14},{6,10},{2,6},{1,3},{5,1},... | collective-permute-start | bytes 811016 | tf_op jit(solution)/shard_map/ppermute | solution.py:487
  92.7 8.6 %collective-permute-start.23 = (bf16[2,528,128]{2,1,0:T(8,128)(2,1)S(1)}, bf16[2,528,128]{2,1,0:T(8,128)(2,1)S(1)}, u32[]{:S(2)}, u32[]{:S(2)}) collective-permute-start(bf16[2,528,128]{2,1,0:T(8,128)(2,1)S(1)} %shard_map.96), channel_id=1, source_target_pairs={{0,4},{4,8},{8,12},{12,14},{14,10},{10,6},{6,2},{2,0},{1,5},{5,9},... | collective-permute-start | bytes 811016 | tf_op jit(solution)/shard_map/ppermute | solution.py:487
  102.6 6.5 %collective-permute-start.28 = (bf16[2,528,128]{2,1,0:T(8,128)(2,1)S(1)}, bf16[2,528,128]{2,1,0:T(8,128)(2,1)S(1)}, u32[]{:S(2)}, u32[]{:S(2)}) collective-permute-start(bf16[2,528,128]{2,1,0:T(8,128)(2,1)S(1)} %shard_map.99), channel_id=1, source_target_pairs={{0,4},{4,8},{8,12},{12,14},{14,10},{10,6},{6,2},{2,0},{1,5},{5,9},... | collective-permute-start | bytes 811016 | tf_op jit(solution)/shard_map/ppermute | solution.py:487
  103.4 6.5 %collective-permute-start.27 = (bf16[2,528,128]{2,1,0:T(8,128)(2,1)S(1)}, bf16[2,528,128]{2,1,0:T(8,128)(2,1)S(1)}, u32[]{:S(2)}, u32[]{:S(2)}) collective-permute-start(bf16[2,528,128]{2,1,0:T(8,128)(2,1)S(1)} %shard_map.98), channel_id=1, source_target_pairs={{0,2},{4,0},{8,4},{12,8},{14,12},{10,14},{6,10},{2,6},{1,3},{5,1},... | collective-permute-start | bytes 811016 | tf_op jit(solution)/shard_map/ppermute | solution.py:487

commit v5 on v4

--- a/solution.py
+++ b/solution.py
@@ -12,6 +12,7 @@
 DEAD = -1e30
 FLOOR = -1e29
 STAT_ROWS = 16
+GRANT = 20 * 1024 * 1024
 LIGHT = pl.CostEstimate(flops=1, bytes_accessed=1, transcendentals=0)
 VMEM = pl.BlockSpec(memory_space=pltpu.VMEM)
 SMEM = pl.BlockSpec(memory_space=pltpu.SMEM)
@@ -160,17 +161,13 @@
     meta = refs.pop(0)
     queries = [refs.pop(0) for _ in range(count)]
     if own:
-        own_kv, pages = refs.pop(0), refs.pop(0)
-    else:
-        held = refs.pop(0)
+        own_kv = refs.pop(0)
+    held = refs.pop(0)
     results = len({job[-1] for job in jobs})
     outs = [(refs.pop(0), refs.pop(0)) for _ in range(results)]
     if own:
-        held, stored, scores, late_scores, sems = refs
-        fetch = pltpu.make_async_copy(pages, held, sems.at[0])
-        fetch.start()
-        fetch.wait()
-        keep = pltpu.make_async_copy(held, stored, sems.at[1])
+        stored, scores, late_scores, sem = refs
+        keep = pltpu.make_async_copy(held, stored, sem)
         keep.start()
     else:
         (scores,) = refs
@@ -244,18 +241,22 @@
     more = [held]
     if own is not None:
         more = [own, held]
-        shapes += [jax.ShapeDtypeStruct(held.shape, held.dtype)] * 2
-        specs += [VMEM, HBM]
+        shapes.append(jax.ShapeDtypeStruct(held.shape, held.dtype))
+        specs.append(HBM)
         scratch.append(pltpu.VMEM((2, rows, suffix), jnp.float32))
-        scratch.append(pltpu.SemaphoreType.DMA((2,)))
+        scratch.append(pltpu.SemaphoreType.DMA)
     out = pl.pallas_call(
         functools.partial(attend_kernel, shape + (len(queries), own is not None), jobs),
         out_shape=shapes,
-        in_specs=[SMEM] + [VMEM] * len(queries) + ([VMEM] if own is None else [VMEM, HBM]),
+        in_specs=[SMEM] + [VMEM] * (len(queries) + len(more)),
         out_specs=specs,
         scratch_shapes=scratch,
-        compiler_params=pltpu.CompilerParams(vmem_limit_bytes=40 * 1024 * 1024),
-        cost_estimate=LIGHT,
+        compiler_params=pltpu.CompilerParams(vmem_limit_bytes=GRANT),
+        cost_estimate=pl.CostEstimate(
+            flops=len(jobs) * rows * keys * HEAD_SIZE * 8,
+            bytes_accessed=len(jobs) * (rows * 6 + keys * 4) * HEAD_SIZE,
+            transcendentals=len(jobs) * rows * keys,
+        ),
     )(meta, *queries, *more)
     return [(out[2 * n], out[2 * n + 1]) for n in range(results)] + list(out[2 * results:])
 
@@ -277,6 +278,7 @@
         out_specs=HBM,
         scratch_shapes=[pltpu.SemaphoreType.DMA],
         input_output_aliases={3: 0},
+        compiler_params=pltpu.CompilerParams(vmem_limit_bytes=GRANT),
         cost_estimate=LIGHT,
     )(me, lists, page, store)
 
@@ -346,7 +348,7 @@
         out_shape=shape,
         in_specs=[VMEM] * len(args),
         out_specs=[VMEM] * len(shape) if isinstance(shape, list) else VMEM,
-        compiler_params=pltpu.CompilerParams(vmem_limit_bytes=48 * 1024 * 1024),
+        compiler_params=pltpu.CompilerParams(vmem_limit_bytes=GRANT),
         cost_estimate=pl.CostEstimate(flops=size, bytes_accessed=2 * size, transcendentals=0),
     )(*args)
 
@@ -390,7 +392,8 @@
         ],
         in_specs=[SMEM, SMEM, VMEM, VMEM],
         out_specs=[VMEM, VMEM],
-        cost_estimate=LIGHT,
+        compiler_params=pltpu.CompilerParams(vmem_limit_bytes=GRANT),
+        cost_estimate=pl.CostEstimate(flops=1, bytes_accessed=1 << 24, transcendentals=0),
     )(prefix_pages, new_slots, page_table, queries)
 
 
@@ -429,12 +432,10 @@
         for sign in routes
     }
     jobs = [(0, side, h, side * heads_each + h, side) for side in range(2) for h in range(heads_each)]
-    first, second = after(mine, arrived)
-    *own, held, store = attend(
-        shape, jobs, listed(first), [first, second], kv_pages, suffix_key_value[0]
-    )
+    held = kv_pages
+    *own, store = attend(shape, jobs, listed(mine[0]), mine, held, suffix_key_value[0])
     parts = {(0, side): own[side] for side in range(2)}
-    token = own
+    token = [own, arrived]
     lists_of = {}
     sent = {}
     for step in range(1, half):

time: 112 us -> 107 us (0.955)
  starting transfers between devices: 39 us -> 33.2 us
  waiting for transfers between devices: 32.5 us -> 36.2 us
  Pallas kernels: 32.1 us -> 30.1 us
    ppermute x10, starting transfers between devices: 15.8 us -> 10.2 us  [queries_travel(): moving[side, sign] = lax.ppermute(came[sign], 'store', routes[sign])]
    ppermute x1, waiting for transfers between devices: 5.18 us -> 8.96 us  [shifted(): return lax.ppermute(block, axis, route)]
    pallas_call x1, Pallas kernels: 2.06 us -> 0.29 us  [prepare(): pl.pallas_call(functools.partial(prepare_kernel, cut, cap, pages_dev), ou...]
    ppermute x12, waiting for transfers between devices: 21.2 us -> 19.4 us  [queries_travel(): flows[flow, sign] = lax.ppermute(blocks[sign], 'store', back[sign])]
    ppermute x10, waiting for transfers between devices: 4.77 us -> 6.18 us  [queries_travel(): moving[side, sign] = lax.ppermute(came[sign], 'store', routes[sign])]
    unnamed x12 -> x10, local copies, waits for them, and re-layouts: 5 us -> 4.78 us
  transfers between devices with their start and end apart: 29 -> 29, of which waited for: 19 -> 21; matrix products, arithmetic and copies ran while one was open for 1% -> 0% of each run, Pallas kernels for 24% -> 26%
where the time goes in v5:
time: 107 us
  waiting for transfers between devices  36.2 us (34%)
  starting transfers between devices  33.2 us (31%)
  Pallas kernels  30.1 us (28%)
  local copies, waits for them, and re-layouts  4.85 us (5%)
  between operations  2.2 us (2%)
    ppermute x12, waiting for transfers between devices, queries_travel(): flows[flow, sign] = lax.ppermute(blocks[sign], 'store', back[sign])  19.4 us
    pallas_call x8, Pallas kernels, attend(): pl.pallas_call(functools.partial(attend_kernel, shape + (len(queries), ow...  19.2 us
    ppermute x12, starting transfers between devices, queries_travel(): flows[flow, sign] = lax.ppermute(blocks[sign], 'store', back[sign])  12.8 us
    ppermute x10, starting transfers between devices, queries_travel(): moving[side, sign] = lax.ppermute(came[sign], 'store', routes[sign])  10.2 us
    pallas_call x17, Pallas kernels, call(): pl.pallas_call(kernel, out_shape=shape, in_specs=[VMEM] * len(args), out_...  9.4 us
    ppermute x1, waiting for transfers between devices, shifted(): return lax.ppermute(block, axis, route)  8.96 us
    ppermute x10, waiting for transfers between devices, queries_travel(): moving[side, sign] = lax.ppermute(came[sign], 'store', routes[sign])  6.18 us
    ppermute x4, starting transfers between devices, queries_travel(): lax.ppermute(mine[side], 'store', routes[sign])  5.05 us
  transfers between devices with their start and end apart: 29, of which 21 were waited for; matrix products, arithmetic and copies ran while one was open for 0% of the time, Pallas kernels for 26%

profile of v5, /device:TPU:0, one launch (start us, length us, event | category | flops | bytes accessed | tf_op | source)
XLA Modules:
  0.0 106.6 jit_solution(5795035038568781840)
XLA Ops:
  1.9 1.0 copy-done.2
  3.0 0.7 copy-done.4
  3.9 3.0 %collective-permute-start = (bf16[64,2176]{1,0:T(8,128)(2,1)S(1)}, bf16[64,2176]{1,0:T(8,128)(2,1)S(1)}, u32[]{:S(2)}, u32[]{:S(2)}) collective-permute-start(bf16[64,2176]{1,0:T(8,128)(2,1)S(1)} %get-tuple-element.78.refs_1_), channel_id=1, source_target_pairs={{0,4},{4,8},{8,12},{12,14},{14,10},{10,6},{6,2},{2,0},{1,5},{5,9},... | collective-permute-start | bytes 835592 | tf_op jit(solution)/shard_map/ppermute | solution.py:430
  6.9 2.0 %collective-permute-start.4 = (bf16[64,2048]{1,0:T(8,128)(2,1)S(1)}, bf16[64,2048]{1,0:T(8,128)(2,1)S(1)}, u32[]{:S(2)}, u32[]{:S(2)}) collective-permute-start(bf16[64,2048]{1,0:T(8,128)(2,1)S(1)} %get-tuple-element.79.refs_2_), channel_id=1, source_target_pairs={{0,4},{4,8},{8,12},{12,14},{14,10},{10,6},{6,2},{2,0},{1,5},{5,9},... | collective-permute-start | bytes 786440 | tf_op jit(solution)/shard_map/ppermute | solution.py:430
  9.0 3.0 %collective-permute-start.1 = (bf16[1,2,64,512]{3,2,1,0:T(8,128)(2,1)}, bf16[1,2,64,512]{3,2,1,0:T(8,128)(2,1)S(1)}, u32[]{:S(2)}, u32[]{:S(2)}) collective-permute-start(bf16[1,2,64,512]{3,2,1,0:T(8,128)(2,1)} %param.7), channel_id=1, source_target_pairs={{8,0},{10,2},{12,4},{14,6},{0,8},{2,10},{4,12},{6,14},{9,1},{11,3}... | collective-permute-start | bytes 393224 | tf_op jit(solution)/shard_map/ppermute | solution.py:25
  12.0 2.2 %copy-done = bf16[32,2,64,512]{3,2,1,0:T(8,128)(2,1)S(1)} copy-done((bf16[32,2,64,512]{3,2,1,0:T(8,128)(2,1)S(1)}, bf16[32,2,64,512]{3,2,1,0:T(8,128)(2,1)}, u32[]{:S(2)}) %copy-start) | copy-done | bytes 4194328
  14.2 0.9 copy-done.3
  15.1 3.2 %shard_map.78 = (f32[2,512,128]{2,1,0:T(8,128)S(1)}, bf16[2,16,128]{2,1,0:T(8,128)(2,1)S(1)}, f32[2,512,128]{2,1,0:T(8,128)S(1)}, bf16[2,16,128]{2,1,0:T(8,128)(2,1)S(1)}, bf16[32,2,64,512]{3,2,1,0:T(8,128)(2,1)}) custom-call(s32[1,128]{1,0:T(1,128)S(1)} %fusion.refs_0_, bf16[64,2176]{1,0:T(8,128)(2,1)S(1)} %get-tuple-element.78.refs_1_, ...), custom_call_target="tpu_custom_call" | custom-call | flops 1073741824 | bytes 2621440 | tf_op jit(solution)/shard_map/pallas_call | solution.py:248
  18.3 9.0 %collective-permute-done.1.page_ref = bf16[1,2,64,512]{3,2,1,0:T(8,128)(2,1)S(1)} collective-permute-done((bf16[1,2,64,512]{3,2,1,0:T(8,128)(2,1)}, bf16[1,2,64,512]{3,2,1,0:T(8,128)(2,1)S(1)}, u32[]{:S(2)}, u32[]{:S(2)}) %collective-permute-start.1) | collective-permute-done | bytes 131104 | tf_op jit(solution)/shard_map/ppermute | solution.py:25
  27.4 2.1 %collective-permute-start.7 = (bf16[64,2176]{1,0:T(8,128)(2,1)S(1)}, bf16[64,2176]{1,0:T(8,128)(2,1)S(1)}, u32[]{:S(2)}, u32[]{:S(2)}) collective-permute-start(bf16[64,2176]{1,0:T(8,128)(2,1)S(1)} %collective-permute-done.3.refs_2_), channel_id=1, source_target_pairs={{0,2},{4,0},{8,4},{12,8},{14,12},{10,14},{6,10},{2,6},{1,3},{5,1},... | collective-permute-start | bytes 835592 | tf_op jit(solution)/shard_map/ppermute | solution.py:446
  29.4 2.3 %shard_map.79 = (f32[2,512,128]{2,1,0:T(8,128)S(1)}, bf16[2,16,128]{2,1,0:T(8,128)(2,1)S(1)}, f32[2,512,128]{2,1,0:T(8,128)S(1)}, bf16[2,16,128]{2,1,0:T(8,128)(2,1)S(1)}) custom-call(s32[2,128]{1,0:T(2,128)S(1)} %maximum_convert_fusion.refs_0_, bf16[64,2176]{1,0:T(8,128)(2,1)S(1)} %collective-permute-done.refs_1_, ...), custom_call_target="tpu_custom_call" | custom-call | flops 1073741824 | bytes 2621440 | tf_op jit(solution)/shard_map/pallas_call | solution.py:248
  31.8 2.0 %collective-permute-start.9 = (bf16[64,2048]{1,0:T(8,128)(2,1)S(1)}, bf16[64,2048]{1,0:T(8,128)(2,1)S(1)}, u32[]{:S(2)}, u32[]{:S(2)}) collective-permute-start(bf16[64,2048]{1,0:T(8,128)(2,1)S(1)} %collective-permute-done.5.refs_2_), channel_id=1, source_target_pairs={{0,2},{4,0},{8,4},{12,8},{14,12},{10,14},{6,10},{2,6},{1,3},{5,1},... | collective-permute-start | bytes 786440 | tf_op jit(solution)/shard_map/ppermute | solution.py:446
  33.8 2.3 %shard_map.80 = (f32[2,512,128]{2,1,0:T(8,128)S(1)}, bf16[2,16,128]{2,1,0:T(8,128)(2,1)S(1)}, f32[2,512,128]{2,1,0:T(8,128)S(1)}, bf16[2,16,128]{2,1,0:T(8,128)(2,1)S(1)}) custom-call(s32[2,128]{1,0:T(2,128)S(1)} %maximum_convert_fusion.refs_0_, bf16[64,2048]{1,0:T(8,128)(2,1)S(1)} %collective-permute-done.4.refs_1_, ...), custom_call_target="tpu_custom_call" | custom-call | flops 1073741824 | bytes 2621440 | tf_op jit(solution)/shard_map/pallas_call | solution.py:248
  36.5 1.8 %collective-permute-start.12 = (bf16[64,2176]{1,0:T(8,128)(2,1)S(1)}, bf16[64,2176]{1,0:T(8,128)(2,1)S(1)}, u32[]{:S(2)}, u32[]{:S(2)}) collective-permute-start(bf16[64,2176]{1,0:T(8,128)(2,1)S(1)} %collective-permute-done.7.refs_2_), channel_id=1, source_target_pairs={{0,2},{4,0},{8,4},{12,8},{14,12},{10,14},{6,10},{2,6},{1,3},{5,1},... | collective-permute-start | bytes 835592 | tf_op jit(solution)/shard_map/ppermute | solution.py:446
  38.4 2.3 %shard_map.81 = (f32[2,512,128]{2,1,0:T(8,128)S(1)}, bf16[2,16,128]{2,1,0:T(8,128)(2,1)S(1)}, f32[2,512,128]{2,1,0:T(8,128)S(1)}, bf16[2,16,128]{2,1,0:T(8,128)(2,1)S(1)}) custom-call(s32[2,128]{1,0:T(2,128)S(1)} %maximum_convert_fusion.1.refs_0_.lists_ref, bf16[64,2176]{1,0:T(8,128)(2,1)S(1)} %collective-permute-done.2.refs_1_, ...), custom_call_target="tpu_custom_call" | custom-call | flops 1073741824 | bytes 2621440 | tf_op jit(solution)/shard_map/pallas_call | solution.py:248
  40.6 1.2 %collective-permute-done.8.refs_1_ = bf16[64,2048]{1,0:T(8,128)(2,1)S(1)} collective-permute-done((bf16[64,2048]{1,0:T(8,128)(2,1)S(1)}, bf16[64,2048]{1,0:T(8,128)(2,1)S(1)}, u32[]{:S(2)}, u32[]{:S(2)}) %collective-permute-start.8) | collective-permute-done | bytes 262176 | tf_op jit(solution)/shard_map/ppermute | solution.py:446
  42.0 1.8 %collective-permute-start.11 = (bf16[64,2048]{1,0:T(8,128)(2,1)S(1)}, bf16[64,2048]{1,0:T(8,128)(2,1)S(1)}, u32[]{:S(2)}, u32[]{:S(2)}) collective-permute-start(bf16[64,2048]{1,0:T(8,128)(2,1)S(1)} %collective-permute-done.9.refs_2_), channel_id=1, source_target_pairs={{0,2},{4,0},{8,4},{12,8},{14,12},{10,14},{6,10},{2,6},{1,3},{5,1},... | collective-permute-start | bytes 786440 | tf_op jit(solution)/shard_map/ppermute | solution.py:446
  44.0 2.3 %shard_map.82 = (f32[2,512,128]{2,1,0:T(8,128)S(1)}, bf16[2,16,128]{2,1,0:T(8,128)(2,1)S(1)}, f32[2,512,128]{2,1,0:T(8,128)S(1)}, bf16[2,16,128]{2,1,0:T(8,128)(2,1)S(1)}) custom-call(s32[2,128]{1,0:T(2,128)S(1)} %maximum_convert_fusion.1.refs_0_.lists_ref, bf16[64,2048]{1,0:T(8,128)(2,1)S(1)} %collective-permute-done.8.refs_1_, ...), custom_call_target="tpu_custom_call" | custom-call | flops 1073741824 | bytes 2621440 | tf_op jit(solution)/shard_map/pallas_call | solution.py:248
  46.3 1.5 %collective-permute-done.6.refs_1_ = bf16[64,2176]{1,0:T(8,128)(2,1)S(1)} collective-permute-done((bf16[64,2176]{1,0:T(8,128)(2,1)S(1)}, bf16[64,2176]{1,0:T(8,128)(2,1)S(1)}, u32[]{:S(2)}, u32[]{:S(2)}) %collective-permute-start.6) | collective-permute-done | bytes 278560 | tf_op jit(solution)/shard_map/ppermute | solution.py:446
  48.1 2.3 %shard_map.83 = (f32[2,512,128]{2,1,0:T(8,128)S(1)}, bf16[2,16,128]{2,1,0:T(8,128)(2,1)S(1)}, f32[2,512,128]{2,1,0:T(8,128)S(1)}, bf16[2,16,128]{2,1,0:T(8,128)(2,1)S(1)}) custom-call(s32[2,128]{1,0:T(2,128)S(1)} %maximum_convert_fusion.2.refs_0_, bf16[64,2176]{1,0:T(8,128)(2,1)S(1)} %collective-permute-done.6.refs_1_, ...), custom_call_target="tpu_custom_call" | custom-call | flops 1073741824 | bytes 2621440 | tf_op jit(solution)/shard_map/pallas_call | solution.py:248
  50.4 1.1 %collective-permute-done.11.refs_2_ = bf16[64,2048]{1,0:T(8,128)(2,1)S(1)} collective-permute-done((bf16[64,2048]{1,0:T(8,128)(2,1)S(1)}, bf16[64,2048]{1,0:T(8,128)(2,1)S(1)}, u32[]{:S(2)}, u32[]{:S(2)}) %collective-permute-start.11) | collective-permute-done | bytes 262176 | tf_op jit(solution)/shard_map/ppermute | solution.py:446
  51.5 1.7 %collective-permute-start.13 = (bf16[64,2048]{1,0:T(8,128)(2,1)S(1)}, bf16[64,2048]{1,0:T(8,128)(2,1)S(1)}, u32[]{:S(2)}, u32[]{:S(2)}) collective-permute-start(bf16[64,2048]{1,0:T(8,128)(2,1)S(1)} %collective-permute-done.11.refs_2_), channel_id=1, source_target_pairs={{0,2},{4,0},{8,4},{12,8},{14,12},{10,14},{6,10},{2,6},{1,3},{5,1},... | collective-permute-start | bytes 786440 | tf_op jit(solution)/shard_map/ppermute | solution.py:446
  53.6 2.3 %shard_map.85 = (f32[2,512,128]{2,1,0:T(8,128)S(1)}, bf16[2,16,128]{2,1,0:T(8,128)(2,1)S(1)}, f32[2,512,128]{2,1,0:T(8,128)S(1)}, bf16[2,16,128]{2,1,0:T(8,128)(2,1)S(1)}) custom-call(s32[2,128]{1,0:T(2,128)S(1)} %maximum_convert_fusion.2.refs_0_, bf16[64,2048]{1,0:T(8,128)(2,1)S(1)} %collective-permute-done.14.refs_1_, ...), custom_call_target="tpu_custom_call" | custom-call | flops 1073741824 | bytes 2621440 | tf_op jit(solution)/shard_map/pallas_call | solution.py:248
  55.9 1.8 %collective-permute-start.16 = (bf16[2,528,128]{2,1,0:T(8,128)(2,1)S(1)}, bf16[2,528,128]{2,1,0:T(8,128)(2,1)S(1)}, u32[]{:S(2)}, u32[]{:S(2)}) collective-permute-start(bf16[2,528,128]{2,1,0:T(8,128)(2,1)S(1)} %shard_map.86), channel_id=1, source_target_pairs={{0,2},{4,0},{8,4},{12,8},{14,12},{10,14},{6,10},{2,6},{1,3},{5,1},... | collective-permute-start | bytes 811016 | tf_op jit(solution)/shard_map/ppermute | solution.py:464
  57.7 2.1 %collective-permute-done.13.refs_2_ = bf16[64,2048]{1,0:T(8,128)(2,1)S(1)} collective-permute-done((bf16[64,2048]{1,0:T(8,128)(2,1)S(1)}, bf16[64,2048]{1,0:T(8,128)(2,1)S(1)}, u32[]{:S(2)}, u32[]{:S(2)}) %collective-permute-start.13) | collective-permute-done | bytes 262176 | tf_op jit(solution)/shard_map/ppermute | solution.py:446
  59.8 2.3 %shard_map.87 = (f32[2,512,128]{2,1,0:T(8,128)S(1)}, bf16[2,16,128]{2,1,0:T(8,128)(2,1)S(1)}, f32[2,512,128]{2,1,0:T(8,128)S(1)}, bf16[2,16,128]{2,1,0:T(8,128)(2,1)S(1)}) custom-call(s32[1,128]{1,0:T(1,128)S(1)} %fusion.1.refs_0_, bf16[64,2176]{1,0:T(8,128)(2,1)S(1)} %collective-permute-done.10.refs_1_, ...), custom_call_target="tpu_custom_call" | custom-call | flops 1073741824 | bytes 2621440 | tf_op jit(solution)/shard_map/pallas_call | solution.py:248
  62.1 1.1 %collective-permute-done.15.in_ref = bf16[2,528,128]{2,1,0:T(8,128)(2,1)S(1)} collective-permute-done((bf16[2,528,128]{2,1,0:T(8,128)(2,1)S(1)}, bf16[2,528,128]{2,1,0:T(8,128)(2,1)S(1)}, u32[]{:S(2)}, u32[]{:S(2)}) %collective-permute-start.15) | collective-permute-done | bytes 270368 | tf_op jit(solution)/shard_map/ppermute | solution.py:464
  63.2 0.5 collective-permute-done.16.in_ref
  63.7 0.9 collective-permute-start.17
  64.7 1.2 %collective-permute-start.18 = (bf16[2,528,128]{2,1,0:T(8,128)(2,1)S(1)}, bf16[2,528,128]{2,1,0:T(8,128)(2,1)S(1)}, u32[]{:S(2)}, u32[]{:S(2)}) collective-permute-start(bf16[2,528,128]{2,1,0:T(8,128)(2,1)S(1)} %shard_map.89), channel_id=1, source_target_pairs={{0,2},{4,0},{8,4},{12,8},{14,12},{10,14},{6,10},{2,6},{1,3},{5,1},... | collective-permute-start | bytes 811016 | tf_op jit(solution)/shard_map/ppermute | solution.py:488
  65.9 0.6 shard_map.90
  66.5 0.9 collective-permute-start.21
  67.5 0.6 shard_map.91
  68.1 1.2 %collective-permute-start.22 = (bf16[2,528,128]{2,1,0:T(8,128)(2,1)S(1)}, bf16[2,528,128]{2,1,0:T(8,128)(2,1)S(1)}, u32[]{:S(2)}, u32[]{:S(2)}) collective-permute-start(bf16[2,528,128]{2,1,0:T(8,128)(2,1)S(1)} %shard_map.91), channel_id=1, source_target_pairs={{0,2},{4,0},{8,4},{12,8},{14,12},{10,14},{6,10},{2,6},{1,3},{5,1},... | collective-permute-start | bytes 811016 | tf_op jit(solution)/shard_map/ppermute | solution.py:488
  69.3 3.9 %collective-permute-done.17.in_ref = bf16[2,528,128]{2,1,0:T(8,128)(2,1)S(1)} collective-permute-done((bf16[2,528,128]{2,1,0:T(8,128)(2,1)S(1)}, bf16[2,528,128]{2,1,0:T(8,128)(2,1)S(1)}, u32[]{:S(2)}, u32[]{:S(2)}) %collective-permute-start.17) | collective-permute-done | bytes 270368 | tf_op jit(solution)/shard_map/ppermute | solution.py:488
  73.2 1.0 collective-permute-done.18.in_ref
  74.2 0.6 shard_map.92
  74.8 1.8 %collective-permute-start.19 = (bf16[2,528,128]{2,1,0:T(8,128)(2,1)S(1)}, bf16[2,528,128]{2,1,0:T(8,128)(2,1)S(1)}, u32[]{:S(2)}, u32[]{:S(2)}) collective-permute-start(bf16[2,528,128]{2,1,0:T(8,128)(2,1)S(1)} %shard_map.92), channel_id=1, source_target_pairs={{0,4},{4,8},{8,12},{12,14},{14,10},{10,6},{6,2},{2,0},{1,5},{5,9},... | collective-permute-start | bytes 811016 | tf_op jit(solution)/shard_map/ppermute | solution.py:488
  76.6 0.6 shard_map.93
  77.6 1.4 %collective-permute-done.21.in_ref = bf16[2,528,128]{2,1,0:T(8,128)(2,1)S(1)} collective-permute-done((bf16[2,528,128]{2,1,0:T(8,128)(2,1)S(1)}, bf16[2,528,128]{2,1,0:T(8,128)(2,1)S(1)}, u32[]{:S(2)}, u32[]{:S(2)}) %collective-permute-start.21) | collective-permute-done | bytes 270368 | tf_op jit(solution)/shard_map/ppermute | solution.py:488
  79.0 1.0 collective-permute-done.22.in_ref
  80.0 0.6 shard_map.94
  80.6 1.8 %collective-permute-start.25 = (bf16[2,528,128]{2,1,0:T(8,128)(2,1)S(1)}, bf16[2,528,128]{2,1,0:T(8,128)(2,1)S(1)}, u32[]{:S(2)}, u32[]{:S(2)}) collective-permute-start(bf16[2,528,128]{2,1,0:T(8,128)(2,1)S(1)} %shard_map.94), channel_id=1, source_target_pairs={{0,4},{4,8},{8,12},{12,14},{14,10},{10,6},{6,2},{2,0},{1,5},{5,9},... | collective-permute-start | bytes 811016 | tf_op jit(solution)/shard_map/ppermute | solution.py:488
  82.4 0.6 shard_map.95
  83.0 0.3 collective-permute-start.26
  83.4 1.4 %collective-permute-done.19.in_ref = bf16[2,528,128]{2,1,0:T(8,128)(2,1)S(1)} collective-permute-done((bf16[2,528,128]{2,1,0:T(8,128)(2,1)S(1)}, bf16[2,528,128]{2,1,0:T(8,128)(2,1)S(1)}, u32[]{:S(2)}, u32[]{:S(2)}) %collective-permute-start.19) | collective-permute-done | bytes 270368 | tf_op jit(solution)/shard_map/ppermute | solution.py:488
  84.8 1.3 %collective-permute-done.20.in_ref = bf16[2,528,128]{2,1,0:T(8,128)(2,1)S(1)} collective-permute-done((bf16[2,528,128]{2,1,0:T(8,128)(2,1)S(1)}, bf16[2,528,128]{2,1,0:T(8,128)(2,1)S(1)}, u32[]{:S(2)}, u32[]{:S(2)}) %collective-permute-start.20) | collective-permute-done | bytes 270368 | tf_op jit(solution)/shard_map/ppermute | solution.py:488
  86.1 0.6 shard_map.96
  86.7 1.8 %collective-permute-start.23 = (bf16[2,528,128]{2,1,0:T(8,128)(2,1)S(1)}, bf16[2,528,128]{2,1,0:T(8,128)(2,1)S(1)}, u32[]{:S(2)}, u32[]{:S(2)}) collective-permute-start(bf16[2,528,128]{2,1,0:T(8,128)(2,1)S(1)} %shard_map.96), channel_id=1, source_target_pairs={{0,4},{4,8},{8,12},{12,14},{14,10},{10,6},{6,2},{2,0},{1,5},{5,9},... | collective-permute-start | bytes 811016 | tf_op jit(solution)/shard_map/ppermute | solution.py:488
  88.5 0.6 shard_map.97
  89.1 0.3 collective-permute-start.24
  89.5 1.1 %collective-permute-done.25.in_ref = bf16[2,528,128]{2,1,0:T(8,128)(2,1)S(1)} collective-permute-done((bf16[2,528,128]{2,1,0:T(8,128)(2,1)S(1)}, bf16[2,528,128]{2,1,0:T(8,128)(2,1)S(1)}, u32[]{:S(2)}, u32[]{:S(2)}) %collective-permute-start.25) | collective-permute-done | bytes 270368 | tf_op jit(solution)/shard_map/ppermute | solution.py:488
  90.6 0.8 collective-permute-done.26.in_ref
  91.3 2.2 %collective-permute-done.23.in_ref = bf16[2,528,128]{2,1,0:T(8,128)(2,1)S(1)} collective-permute-done((bf16[2,528,128]{2,1,0:T(8,128)(2,1)S(1)}, bf16[2,528,128]{2,1,0:T(8,128)(2,1)S(1)}, u32[]{:S(2)}, u32[]{:S(2)}) %collective-permute-start.23) | collective-permute-done | bytes 270368 | tf_op jit(solution)/shard_map/ppermute | solution.py:488
  93.6 3.4 %collective-permute-done.24.in_ref = bf16[2,528,128]{2,1,0:T(8,128)(2,1)S(1)} collective-permute-done((bf16[2,528,128]{2,1,0:T(8,128)(2,1)S(1)}, bf16[2,528,128]{2,1,0:T(8,128)(2,1)S(1)}, u32[]{:S(2)}, u32[]{:S(2)}) %collective-permute-start.24) | collective-permute-done | bytes 270368 | tf_op jit(solution)/shard_map/ppermute | solution.py:488
  97.0 0.6 shard_map.98
  97.7 0.6 shard_map.99
  98.3 2.1 %collective-permute-start.28 = (bf16[2,528,128]{2,1,0:T(8,128)(2,1)S(1)}, bf16[2,528,128]{2,1,0:T(8,128)(2,1)S(1)}, u32[]{:S(2)}, u32[]{:S(2)}) collective-permute-start(bf16[2,528,128]{2,1,0:T(8,128)(2,1)S(1)} %shard_map.99), channel_id=1, source_target_pairs={{0,4},{4,8},{8,12},{12,14},{14,10},{10,6},{6,2},{2,0},{1,5},{5,9},... | collective-permute-start | bytes 811016 | tf_op jit(solution)/shard_map/ppermute | solution.py:488
  100.4 1.2 %shard_map.103 = bf16[32,2,64,512]{3,2,1,0:T(8,128)(2,1)} custom-call(s32[1]{0:T(128)} %bitcast.1.me_ref, s32[2,128]{1,0:T(2,128)S(1)} %maximum_convert_fusion.1.refs_0_.lists_ref, bf16[1,2,64,512]{3,2,1,0:T(8,128)(2,1)S(1)} %collective-permute-done.1.page_ref, bf16[32,2,64,512]{3,2,1,0:T(8,128)(2,1)} %get-tuple-element.153.old_ref), custom_call_target="tpu_custom_call", output_to_operand_aliasing={{}: (3, {})} | custom-call | flops 1 | bytes 1 | tf_op jit(solution)/shard_map/pallas_call | solution.py:274
  101.6 0.6 shard_map.100
  102.3 0.6 shard_map.101
  102.9 1.2 %collective-permute-done.27.refs_0_ = bf16[2,528,128]{2,1,0:T(8,128)(2,1)S(1)} collective-permute-done((bf16[2,528,128]{2,1,0:T(8,128)(2,1)S(1)}, bf16[2,528,128]{2,1,0:T(8,128)(2,1)S(1)}, u32[]{:S(2)}, u32[]{:S(2)}) %collective-permute-start.27) | collective-permute-done | bytes 270368 | tf_op jit(solution)/shard_map/ppermute | solution.py:488
  104.2 0.7 collective-permute-done.28.refs_3_
  104.9 1.7 %shard_map.102 = bf16[1,64,4096]{2,1,0:T(8,128)(2,1)} custom-call(bf16[2,528,128]{2,1,0:T(8,128)(2,1)S(1)} %collective-permute-done.27.refs_0_, f32[2,512,128]{2,1,0:T(8,128)S(1)} %get-tuple-element.146.refs_1_, bf16[2,16,128]{2,1,0:T(8,128)(2,1)S(1)} %get-tuple-element.147.refs_2_, bf16[2,528,128]{2,1,0:T(8,128)(2,1)S(1)} %collective-permute-done.28.refs_3_, ...), custom_call_target="tpu_custom_call" | custom-call | flops 1605632 | bytes 3211264 | tf_op jit(solution)/shard_map/pallas_call | solution.py:346
  (42 shorter events, 2.3 us)
Async XLA Ops:
  1.9 1.0 copy-start.2
  3.0 0.7 copy-start.4
  3.9 23.4 %collective-permute-start = (bf16[64,2176]{1,0:T(8,128)(2,1)S(1)}, bf16[64,2176]{1,0:T(8,128)(2,1)S(1)}, u32[]{:S(2)}, u32[]{:S(2)}) collective-permute-start(bf16[64,2176]{1,0:T(8,128)(2,1)S(1)} %get-tuple-element.78.refs_1_), channel_id=1, source_target_pairs={{0,4},{4,8},{8,12},{12,14},{14,10},{10,6},{6,2},{2,0},{1,5},{5,9},... | collective-permute-start | bytes 835592 | tf_op jit(solution)/shard_map/ppermute | solution.py:430
  6.9 20.4 %collective-permute-start.3 = (bf16[64,2176]{1,0:T(8,128)(2,1)S(1)}, bf16[64,2176]{1,0:T(8,128)(2,1)S(1)}, u32[]{:S(2)}, u32[]{:S(2)}) collective-permute-start(bf16[64,2176]{1,0:T(8,128)(2,1)S(1)} %get-tuple-element.78.refs_1_), channel_id=1, source_target_pairs={{0,2},{4,0},{8,4},{12,8},{14,12},{10,14},{6,10},{2,6},{1,3},{5,1},... | collective-permute-start | bytes 835592 | tf_op jit(solution)/shard_map/ppermute | solution.py:430
  6.9 24.8 %collective-permute-start.4 = (bf16[64,2048]{1,0:T(8,128)(2,1)S(1)}, bf16[64,2048]{1,0:T(8,128)(2,1)S(1)}, u32[]{:S(2)}, u32[]{:S(2)}) collective-permute-start(bf16[64,2048]{1,0:T(8,128)(2,1)S(1)} %get-tuple-element.79.refs_2_), channel_id=1, source_target_pairs={{0,4},{4,8},{8,12},{12,14},{14,10},{10,6},{6,2},{2,0},{1,5},{5,9},... | collective-permute-start | bytes 786440 | tf_op jit(solution)/shard_map/ppermute | solution.py:430
  9.0 22.8 %collective-permute-start.5 = (bf16[64,2048]{1,0:T(8,128)(2,1)S(1)}, bf16[64,2048]{1,0:T(8,128)(2,1)S(1)}, u32[]{:S(2)}, u32[]{:S(2)}) collective-permute-start(bf16[64,2048]{1,0:T(8,128)(2,1)S(1)} %get-tuple-element.79.refs_2_), channel_id=1, source_target_pairs={{0,2},{4,0},{8,4},{12,8},{14,12},{10,14},{6,10},{2,6},{1,3},{5,1},... | collective-permute-start | bytes 786440 | tf_op jit(solution)/shard_map/ppermute | solution.py:430
  9.0 18.3 %collective-permute-start.1 = (bf16[1,2,64,512]{3,2,1,0:T(8,128)(2,1)}, bf16[1,2,64,512]{3,2,1,0:T(8,128)(2,1)S(1)}, u32[]{:S(2)}, u32[]{:S(2)}) collective-permute-start(bf16[1,2,64,512]{3,2,1,0:T(8,128)(2,1)} %param.7), channel_id=1, source_target_pairs={{8,0},{10,2},{12,4},{14,6},{0,8},{2,10},{4,12},{6,14},{9,1},{11,3}... | collective-permute-start | bytes 393224 | tf_op jit(solution)/shard_map/ppermute | solution.py:25
  12.0 2.2 %copy-start = (bf16[32,2,64,512]{3,2,1,0:T(8,128)(2,1)S(1)}, bf16[32,2,64,512]{3,2,1,0:T(8,128)(2,1)}, u32[]{:S(2)}) copy-start(bf16[32,2,64,512]{3,2,1,0:T(8,128)(2,1)} %refs_3_.13) | copy-start | bytes 12582916
  14.2 0.9 copy-start.3
  15.1 14.3 %copy-start.1 = (bf16[32,2,64,512]{3,2,1,0:T(8,128)(2,1)S(1)}, bf16[32,2,64,512]{3,2,1,0:T(8,128)(2,1)}, u32[]{:S(2)}) copy-start(bf16[32,2,64,512]{3,2,1,0:T(8,128)(2,1)} %refs_3_.13) | copy-start | bytes 12582916
  27.3 8.9 %collective-permute-start.2 = (bf16[64,2176]{1,0:T(8,128)(2,1)S(1)}, bf16[64,2176]{1,0:T(8,128)(2,1)S(1)}, u32[]{:S(2)}, u32[]{:S(2)}) collective-permute-start(bf16[64,2176]{1,0:T(8,128)(2,1)S(1)} %collective-permute-done.refs_1_), channel_id=1, source_target_pairs={{0,4},{4,8},{8,12},{12,14},{14,10},{10,6},{6,2},{2,0},{1,5},{5,9},... | collective-permute-start | bytes 835592 | tf_op jit(solution)/shard_map/ppermute | solution.py:446
  27.4 9.1 %collective-permute-start.7 = (bf16[64,2176]{1,0:T(8,128)(2,1)S(1)}, bf16[64,2176]{1,0:T(8,128)(2,1)S(1)}, u32[]{:S(2)}, u32[]{:S(2)}) collective-permute-start(bf16[64,2176]{1,0:T(8,128)(2,1)S(1)} %collective-permute-done.3.refs_2_), channel_id=1, source_target_pairs={{0,2},{4,0},{8,4},{12,8},{14,12},{10,14},{6,10},{2,6},{1,3},{5,1},... | collective-permute-start | bytes 835592 | tf_op jit(solution)/shard_map/ppermute | solution.py:446
  31.7 10.1 %collective-permute-start.8 = (bf16[64,2048]{1,0:T(8,128)(2,1)S(1)}, bf16[64,2048]{1,0:T(8,128)(2,1)S(1)}, u32[]{:S(2)}, u32[]{:S(2)}) collective-permute-start(bf16[64,2048]{1,0:T(8,128)(2,1)S(1)} %collective-permute-done.4.refs_1_), channel_id=1, source_target_pairs={{0,4},{4,8},{8,12},{12,14},{14,10},{10,6},{6,2},{2,0},{1,5},{5,9},... | collective-permute-start | bytes 786440 | tf_op jit(solution)/shard_map/ppermute | solution.py:446
  31.8 10.2 %collective-permute-start.9 = (bf16[64,2048]{1,0:T(8,128)(2,1)S(1)}, bf16[64,2048]{1,0:T(8,128)(2,1)S(1)}, u32[]{:S(2)}, u32[]{:S(2)}) collective-permute-start(bf16[64,2048]{1,0:T(8,128)(2,1)S(1)} %collective-permute-done.5.refs_2_), channel_id=1, source_target_pairs={{0,2},{4,0},{8,4},{12,8},{14,12},{10,14},{6,10},{2,6},{1,3},{5,1},... | collective-permute-start | bytes 786440 | tf_op jit(solution)/shard_map/ppermute | solution.py:446
  36.2 11.6 %collective-permute-start.6 = (bf16[64,2176]{1,0:T(8,128)(2,1)S(1)}, bf16[64,2176]{1,0:T(8,128)(2,1)S(1)}, u32[]{:S(2)}, u32[]{:S(2)}) collective-permute-start(bf16[64,2176]{1,0:T(8,128)(2,1)S(1)} %collective-permute-done.2.refs_1_), channel_id=1, source_target_pairs={{0,4},{4,8},{8,12},{12,14},{14,10},{10,6},{6,2},{2,0},{1,5},{5,9},... | collective-permute-start | bytes 835592 | tf_op jit(solution)/shard_map/ppermute | solution.py:446
  36.5 11.6 %collective-permute-start.12 = (bf16[64,2176]{1,0:T(8,128)(2,1)S(1)}, bf16[64,2176]{1,0:T(8,128)(2,1)S(1)}, u32[]{:S(2)}, u32[]{:S(2)}) collective-permute-start(bf16[64,2176]{1,0:T(8,128)(2,1)S(1)} %collective-permute-done.7.refs_2_), channel_id=1, source_target_pairs={{0,2},{4,0},{8,4},{12,8},{14,12},{10,14},{6,10},{2,6},{1,3},{5,1},... | collective-permute-start | bytes 835592 | tf_op jit(solution)/shard_map/ppermute | solution.py:446
  42.0 9.5 %collective-permute-start.11 = (bf16[64,2048]{1,0:T(8,128)(2,1)S(1)}, bf16[64,2048]{1,0:T(8,128)(2,1)S(1)}, u32[]{:S(2)}, u32[]{:S(2)}) collective-permute-start(bf16[64,2048]{1,0:T(8,128)(2,1)S(1)} %collective-permute-done.9.refs_2_), channel_id=1, source_target_pairs={{0,2},{4,0},{8,4},{12,8},{14,12},{10,14},{6,10},{2,6},{1,3},{5,1},... | collective-permute-start | bytes 786440 | tf_op jit(solution)/shard_map/ppermute | solution.py:446
  43.8 9.7 %collective-permute-start.14 = (bf16[64,2048]{1,0:T(8,128)(2,1)S(1)}, bf16[64,2048]{1,0:T(8,128)(2,1)S(1)}, u32[]{:S(2)}, u32[]{:S(2)}) collective-permute-start(bf16[64,2048]{1,0:T(8,128)(2,1)S(1)} %collective-permute-done.8.refs_1_), channel_id=1, source_target_pairs={{0,4},{4,8},{8,12},{12,14},{14,10},{10,6},{6,2},{2,0},{1,5},{5,9},... | collective-permute-start | bytes 786440 | tf_op jit(solution)/shard_map/ppermute | solution.py:446
  47.8 12.0 %collective-permute-start.10 = (bf16[64,2176]{1,0:T(8,128)(2,1)S(1)}, bf16[64,2176]{1,0:T(8,128)(2,1)S(1)}, u32[]{:S(2)}, u32[]{:S(2)}) collective-permute-start(bf16[64,2176]{1,0:T(8,128)(2,1)S(1)} %collective-permute-done.6.refs_1_), channel_id=1, source_target_pairs={{0,4},{4,8},{8,12},{12,14},{14,10},{10,6},{6,2},{2,0},{1,5},{5,9},... | collective-permute-start | bytes 835592 | tf_op jit(solution)/shard_map/ppermute | solution.py:446
  51.5 8.2 %collective-permute-start.13 = (bf16[64,2048]{1,0:T(8,128)(2,1)S(1)}, bf16[64,2048]{1,0:T(8,128)(2,1)S(1)}, u32[]{:S(2)}, u32[]{:S(2)}) collective-permute-start(bf16[64,2048]{1,0:T(8,128)(2,1)S(1)} %collective-permute-done.11.refs_2_), channel_id=1, source_target_pairs={{0,2},{4,0},{8,4},{12,8},{14,12},{10,14},{6,10},{2,6},{1,3},{5,1},... | collective-permute-start | bytes 786440 | tf_op jit(solution)/shard_map/ppermute | solution.py:446
  53.3 9.9 %collective-permute-start.15 = (bf16[2,528,128]{2,1,0:T(8,128)(2,1)S(1)}, bf16[2,528,128]{2,1,0:T(8,128)(2,1)S(1)}, u32[]{:S(2)}, u32[]{:S(2)}) collective-permute-start(bf16[2,528,128]{2,1,0:T(8,128)(2,1)S(1)} %shard_map.84), channel_id=1, source_target_pairs={{0,4},{4,8},{8,12},{12,14},{14,10},{10,6},{6,2},{2,0},{1,5},{5,9},... | collective-permute-start | bytes 811016 | tf_op jit(solution)/shard_map/ppermute | solution.py:464
  55.9 7.8 %collective-permute-start.16 = (bf16[2,528,128]{2,1,0:T(8,128)(2,1)S(1)}, bf16[2,528,128]{2,1,0:T(8,128)(2,1)S(1)}, u32[]{:S(2)}, u32[]{:S(2)}) collective-permute-start(bf16[2,528,128]{2,1,0:T(8,128)(2,1)S(1)} %shard_map.86), channel_id=1, source_target_pairs={{0,2},{4,0},{8,4},{12,8},{14,12},{10,14},{6,10},{2,6},{1,3},{5,1},... | collective-permute-start | bytes 811016 | tf_op jit(solution)/shard_map/ppermute | solution.py:464
  63.7 9.5 %collective-permute-start.17 = (bf16[2,528,128]{2,1,0:T(8,128)(2,1)S(1)}, bf16[2,528,128]{2,1,0:T(8,128)(2,1)S(1)}, u32[]{:S(2)}, u32[]{:S(2)}) collective-permute-start(bf16[2,528,128]{2,1,0:T(8,128)(2,1)S(1)} %shard_map.88), channel_id=1, source_target_pairs={{0,4},{4,8},{8,12},{12,14},{14,10},{10,6},{6,2},{2,0},{1,5},{5,9},... | collective-permute-start | bytes 811016 | tf_op jit(solution)/shard_map/ppermute | solution.py:488
  64.7 9.5 %collective-permute-start.18 = (bf16[2,528,128]{2,1,0:T(8,128)(2,1)S(1)}, bf16[2,528,128]{2,1,0:T(8,128)(2,1)S(1)}, u32[]{:S(2)}, u32[]{:S(2)}) collective-permute-start(bf16[2,528,128]{2,1,0:T(8,128)(2,1)S(1)} %shard_map.89), channel_id=1, source_target_pairs={{0,2},{4,0},{8,4},{12,8},{14,12},{10,14},{6,10},{2,6},{1,3},{5,1},... | collective-permute-start | bytes 811016 | tf_op jit(solution)/shard_map/ppermute | solution.py:488
  66.5 12.5 %collective-permute-start.21 = (bf16[2,528,128]{2,1,0:T(8,128)(2,1)S(1)}, bf16[2,528,128]{2,1,0:T(8,128)(2,1)S(1)}, u32[]{:S(2)}, u32[]{:S(2)}) collective-permute-start(bf16[2,528,128]{2,1,0:T(8,128)(2,1)S(1)} %shard_map.90), channel_id=1, source_target_pairs={{0,4},{4,8},{8,12},{12,14},{14,10},{10,6},{6,2},{2,0},{1,5},{5,9},... | collective-permute-start | bytes 811016 | tf_op jit(solution)/shard_map/ppermute | solution.py:488
  68.1 11.9 %collective-permute-start.22 = (bf16[2,528,128]{2,1,0:T(8,128)(2,1)S(1)}, bf16[2,528,128]{2,1,0:T(8,128)(2,1)S(1)}, u32[]{:S(2)}, u32[]{:S(2)}) collective-permute-start(bf16[2,528,128]{2,1,0:T(8,128)(2,1)S(1)} %shard_map.91), channel_id=1, source_target_pairs={{0,2},{4,0},{8,4},{12,8},{14,12},{10,14},{6,10},{2,6},{1,3},{5,1},... | collective-permute-start | bytes 811016 | tf_op jit(solution)/shard_map/ppermute | solution.py:488
  74.8 10.0 %collective-permute-start.19 = (bf16[2,528,128]{2,1,0:T(8,128)(2,1)S(1)}, bf16[2,528,128]{2,1,0:T(8,128)(2,1)S(1)}, u32[]{:S(2)}, u32[]{:S(2)}) collective-permute-start(bf16[2,528,128]{2,1,0:T(8,128)(2,1)S(1)} %shard_map.92), channel_id=1, source_target_pairs={{0,4},{4,8},{8,12},{12,14},{14,10},{10,6},{6,2},{2,0},{1,5},{5,9},... | collective-permute-start | bytes 811016 | tf_op jit(solution)/shard_map/ppermute | solution.py:488
  77.2 8.8 %collective-permute-start.20 = (bf16[2,528,128]{2,1,0:T(8,128)(2,1)S(1)}, bf16[2,528,128]{2,1,0:T(8,128)(2,1)S(1)}, u32[]{:S(2)}, u32[]{:S(2)}) collective-permute-start(bf16[2,528,128]{2,1,0:T(8,128)(2,1)S(1)} %shard_map.93), channel_id=1, source_target_pairs={{0,2},{4,0},{8,4},{12,8},{14,12},{10,14},{6,10},{2,6},{1,3},{5,1},... | collective-permute-start | bytes 811016 | tf_op jit(solution)/shard_map/ppermute | solution.py:488
  80.6 10.0 %collective-permute-start.25 = (bf16[2,528,128]{2,1,0:T(8,128)(2,1)S(1)}, bf16[2,528,128]{2,1,0:T(8,128)(2,1)S(1)}, u32[]{:S(2)}, u32[]{:S(2)}) collective-permute-start(bf16[2,528,128]{2,1,0:T(8,128)(2,1)S(1)} %shard_map.94), channel_id=1, source_target_pairs={{0,4},{4,8},{8,12},{12,14},{14,10},{10,6},{6,2},{2,0},{1,5},{5,9},... | collective-permute-start | bytes 811016 | tf_op jit(solution)/shard_map/ppermute | solution.py:488
  83.0 8.3 %collective-permute-start.26 = (bf16[2,528,128]{2,1,0:T(8,128)(2,1)S(1)}, bf16[2,528,128]{2,1,0:T(8,128)(2,1)S(1)}, u32[]{:S(2)}, u32[]{:S(2)}) collective-permute-start(bf16[2,528,128]{2,1,0:T(8,128)(2,1)S(1)} %shard_map.95), channel_id=1, source_target_pairs={{0,2},{4,0},{8,4},{12,8},{14,12},{10,14},{6,10},{2,6},{1,3},{5,1},... | collective-permute-start | bytes 811016 | tf_op jit(solution)/shard_map/ppermute | solution.py:488
  86.7 6.9 %collective-permute-start.23 = (bf16[2,528,128]{2,1,0:T(8,128)(2,1)S(1)}, bf16[2,528,128]{2,1,0:T(8,128)(2,1)S(1)}, u32[]{:S(2)}, u32[]{:S(2)}) collective-permute-start(bf16[2,528,128]{2,1,0:T(8,128)(2,1)S(1)} %shard_map.96), channel_id=1, source_target_pairs={{0,4},{4,8},{8,12},{12,14},{14,10},{10,6},{6,2},{2,0},{1,5},{5,9},... | collective-permute-start | bytes 811016 | tf_op jit(solution)/shard_map/ppermute | solution.py:488
  89.1 7.9 %collective-permute-start.24 = (bf16[2,528,128]{2,1,0:T(8,128)(2,1)S(1)}, bf16[2,528,128]{2,1,0:T(8,128)(2,1)S(1)}, u32[]{:S(2)}, u32[]{:S(2)}) collective-permute-start(bf16[2,528,128]{2,1,0:T(8,128)(2,1)S(1)} %shard_map.97), channel_id=1, source_target_pairs={{0,2},{4,0},{8,4},{12,8},{14,12},{10,14},{6,10},{2,6},{1,3},{5,1},... | collective-permute-start | bytes 811016 | tf_op jit(solution)/shard_map/ppermute | solution.py:488
  97.6 6.5 %collective-permute-start.27 = (bf16[2,528,128]{2,1,0:T(8,128)(2,1)S(1)}, bf16[2,528,128]{2,1,0:T(8,128)(2,1)S(1)}, u32[]{:S(2)}, u32[]{:S(2)}) collective-permute-start(bf16[2,528,128]{2,1,0:T(8,128)(2,1)S(1)} %shard_map.98), channel_id=1, source_target_pairs={{0,2},{4,0},{8,4},{12,8},{14,12},{10,14},{6,10},{2,6},{1,3},{5,1},... | collective-permute-start | bytes 811016 | tf_op jit(solution)/shard_map/ppermute | solution.py:488
  98.3 6.5 %collective-permute-start.28 = (bf16[2,528,128]{2,1,0:T(8,128)(2,1)S(1)}, bf16[2,528,128]{2,1,0:T(8,128)(2,1)S(1)}, u32[]{:S(2)}, u32[]{:S(2)}) collective-permute-start(bf16[2,528,128]{2,1,0:T(8,128)(2,1)S(1)} %shard_map.99), channel_id=1, source_target_pairs={{0,4},{4,8},{8,12},{12,14},{14,10},{10,6},{6,2},{2,0},{1,5},{5,9},... | collective-permute-start | bytes 811016 | tf_op jit(solution)/shard_map/ppermute | solution.py:488

commit v6 on v5

--- a/solution.py
+++ b/solution.py
@@ -156,7 +156,7 @@
 
 
 def attend_kernel(sizes, jobs, *refs):
-    groups, suffix, cap, page_len, count, own = sizes
+    groups, suffix, cap, page_len, count, own, keeping = sizes
     refs = list(refs)
     meta = refs.pop(0)
     queries = [refs.pop(0) for _ in range(count)]
@@ -165,12 +165,12 @@
     held = refs.pop(0)
     results = len({job[-1] for job in jobs})
     outs = [(refs.pop(0), refs.pop(0)) for _ in range(results)]
-    if own:
-        stored, scores, late_scores, sem = refs
-        keep = pltpu.make_async_copy(held, stored, sem)
+    stored = refs.pop(0) if keeping else None
+    scores = refs.pop(0)
+    late_scores = refs.pop(0) if own else None
+    if keeping:
+        keep = pltpu.make_async_copy(held, stored, refs.pop(0))
         keep.start()
-    else:
-        (scores,) = refs
     factor = HEAD_SIZE ** (-0.5) * LOG2E
     keys = cap * page_len
     rows = groups * suffix
@@ -223,11 +223,11 @@
             score(i)
         if i > 0:
             weigh(i - 1)
-    if own:
+    if keeping:
         keep.wait()
 
 
-def attend(shape, jobs, meta, queries, held, own=None):
+def attend(shape, jobs, meta, queries, held, own=None, keeping=False):
     groups, suffix, cap, page_len = shape
     rows, keys = groups * suffix, cap * page_len
     results = len({job[-1] for job in jobs})
@@ -241,12 +241,13 @@
     more = [held]
     if own is not None:
         more = [own, held]
+        scratch.append(pltpu.VMEM((2, rows, suffix), jnp.float32))
+    if keeping:
         shapes.append(jax.ShapeDtypeStruct(held.shape, held.dtype))
         specs.append(HBM)
-        scratch.append(pltpu.VMEM((2, rows, suffix), jnp.float32))
         scratch.append(pltpu.SemaphoreType.DMA)
     out = pl.pallas_call(
-        functools.partial(attend_kernel, shape + (len(queries), own is not None), jobs),
+        functools.partial(attend_kernel, shape + (len(queries), own is not None, keeping), jobs),
         out_shape=shapes,
         in_specs=[SMEM] + [VMEM] * (len(queries) + len(more)),
         out_specs=specs,
@@ -431,11 +432,9 @@
         for side in range(2)
         for sign in routes
     }
-    jobs = [(0, side, h, side * heads_each + h, side) for side in range(2) for h in range(heads_each)]
     held = kv_pages
-    *own, store = attend(shape, jobs, listed(mine[0]), mine, held, suffix_key_value[0])
-    parts = {(0, side): own[side] for side in range(2)}
-    token = [own, arrived]
+    parts = {}
+    token = []
     lists_of = {}
     sent = {}
     for step in range(1, half):
@@ -447,9 +446,14 @@
             if side == 0:
                 lists_of[step] = listed(came[1], came[-1])
             jobs = [(n, n, h, side * heads_each + h, n) for n in range(2) for h in range(heads_each)]
-            got = attend(shape, jobs, lists_of[step], [came[1], came[-1]], held)
+            keeping = (step, side) == (1, 1)
+            got = attend(shape, jobs, lists_of[step], [came[1], came[-1]], held, None, keeping)
+            if keeping:
+                store = got.pop()
             parts[step, side], parts[-step, side] = got
             token = got
+            if (step, side) == (half // 2, 0):
+                token = [got, arrived]
             if step == half - 1:
                 sign = 1 if side == 1 else -1
                 sent["early", sign] = packed(parts[sign * step, side])
@@ -487,6 +491,13 @@
         for sign in back:
             flows[flow, sign] = lax.ppermute(blocks[sign], "store", back[sign])
         token = blocks
+        if flow == "early" and distance <= 2:
+            side = 2 - distance
+            jobs = [(0, 0, h, side * heads_each + h, 0) for h in range(heads_each)]
+            parts[0, side], = attend(
+                shape, jobs, listed(mine[0]), [after(mine[side], token)], held, suffix_key_value[0]
+            )
+            token = [blocks, parts[0, side]]
     rest, late = [None, None], [None, None]
     for sign in (1, -1):
         side = side_of["early", sign]
@@ -522,7 +533,7 @@
     pulled = page_table.shape[1] // stores * kv_pages[0].size
     pushed = 2 * queries[0].size
     arrays = (queries, suffix_key_value, kv_pages, page_table, prefix_pages, new_slots)
-    if pulled >= pushed and stores % 4 == 0:
+    if pulled >= pushed and stores % 8 == 0:
         return queries_travel(*arrays)
     return pages_travel(*arrays)
 

time: 107 us -> 105 us (0.981)
  waiting for transfers between devices: 36.2 us -> 27.4 us
  starting transfers between devices: 33.2 us -> 39 us
  Pallas kernels: 30.1 us -> 31.9 us
    ppermute x1, waiting for transfers between devices: 8.96 us -> 0.01 us  [shifted(): return lax.ppermute(block, axis, route)]
    ppermute x10, starting transfers between devices: 10.2 us -> 14.7 us  [queries_travel(): moving[side, sign] = lax.ppermute(came[sign], 'store', routes[sign])]
    ppermute x4, waiting for transfers between devices: 0.01 us -> 4.47 us  [queries_travel(): lax.ppermute(mine[side], 'store', routes[sign])]
    ppermute x12, waiting for transfers between devices: 19.4 us -> 15.6 us  [queries_travel(): flows[flow, sign] = lax.ppermute(blocks[sign], 'store', back[sign])]
    pallas_call x8 -> x9, Pallas kernels: 19.2 us -> 21 us  [attend(): pl.pallas_call(functools.partial(attend_kernel, shape + (len(queries), ow...]
    ppermute x2, starting transfers between devices: 2.08 us -> 3.42 us  [queries_travel(): lax.ppermute(block, 'store', back[key[1]])]
  transfers between devices with their start and end apart: 29 -> 29, of which waited for: 21 -> 16; matrix products, arithmetic and copies ran while one was open for 0% -> 0% of each run, Pallas kernels for 26% -> 28%
where the time goes in v6:
time: 105 us
  starting transfers between devices  39 us (37%)
  Pallas kernels  31.9 us (30%)
  waiting for transfers between devices  27.4 us (26%)
  local copies, waits for them, and re-layouts  3.95 us (4%)
  between operations  2.27 us (2%)
    pallas_call x9, Pallas kernels, attend(): pl.pallas_call(functools.partial(attend_kernel, shape + (len(queries), ow...  21 us
    ppermute x12, waiting for transfers between devices, queries_travel(): flows[flow, sign] = lax.ppermute(blocks[sign], 'store', back[sign])  15.6 us
    ppermute x10, starting transfers between devices, queries_travel(): moving[side, sign] = lax.ppermute(came[sign], 'store', routes[sign])  14.7 us
    ppermute x12, starting transfers between devices, queries_travel(): flows[flow, sign] = lax.ppermute(blocks[sign], 'store', back[sign])  12.8 us
    pallas_call x17, Pallas kernels, call(): pl.pallas_call(kernel, out_shape=shape, in_specs=[VMEM] * len(args), out_...  9.39 us
    ppermute x10, waiting for transfers between devices, queries_travel(): moving[side, sign] = lax.ppermute(came[sign], 'store', routes[sign])  5.59 us
    ppermute x4, starting transfers between devices, queries_travel(): lax.ppermute(mine[side], 'store', routes[sign])  5.05 us
    ppermute x4, waiting for transfers between devices, queries_travel(): lax.ppermute(mine[side], 'store', routes[sign])  4.47 us
  transfers between devices with their start and end apart: 29, of which 16 were waited for; matrix products, arithmetic and copies ran while one was open for 0% of the time, Pallas kernels for 28%

profile of v6, /device:TPU:0, one launch (start us, length us, event | category | flops | bytes accessed | tf_op | source)
XLA Modules:
  0.0 104.6 jit_solution(7100354796712488856)
XLA Ops:
  1.9 1.0 copy-done.3
  3.0 0.7 copy-done.4
  3.6 0.3 shard_map.77
  3.9 3.0 %collective-permute-start = (bf16[64,2176]{1,0:T(8,128)(2,1)S(1)}, bf16[64,2176]{1,0:T(8,128)(2,1)S(1)}, u32[]{:S(2)}, u32[]{:S(2)}) collective-permute-start(bf16[64,2176]{1,0:T(8,128)(2,1)S(1)} %get-tuple-element.124.refs_1_), channel_id=1, source_target_pairs={{0,4},{4,8},{8,12},{12,14},{14,10},{10,6},{6,2},{2,0},{1,5},{5,9},... | collective-permute-start | bytes 835592 | tf_op jit(solution)/shard_map/ppermute | solution.py:431
  6.9 2.0 %collective-permute-start.3 = (bf16[64,2048]{1,0:T(8,128)(2,1)S(1)}, bf16[64,2048]{1,0:T(8,128)(2,1)S(1)}, u32[]{:S(2)}, u32[]{:S(2)}) collective-permute-start(bf16[64,2048]{1,0:T(8,128)(2,1)S(1)} %get-tuple-element.135.refs_1_), channel_id=1, source_target_pairs={{0,4},{4,8},{8,12},{12,14},{14,10},{10,6},{6,2},{2,0},{1,5},{5,9},... | collective-permute-start | bytes 786440 | tf_op jit(solution)/shard_map/ppermute | solution.py:431
  9.0 3.0 %collective-permute-start.8 = (bf16[1,2,64,512]{3,2,1,0:T(8,128)(2,1)}, bf16[1,2,64,512]{3,2,1,0:T(8,128)(2,1)S(1)}, u32[]{:S(2)}, u32[]{:S(2)}) collective-permute-start(bf16[1,2,64,512]{3,2,1,0:T(8,128)(2,1)} %param.7), channel_id=1, source_target_pairs={{8,0},{10,2},{12,4},{14,6},{0,8},{2,10},{4,12},{6,14},{9,1},{11,3}... | collective-permute-start | bytes 393224 | tf_op jit(solution)/shard_map/ppermute | solution.py:25
  12.0 2.4 %collective-permute-done.refs_1_ = bf16[64,2176]{1,0:T(8,128)(2,1)S(1)} collective-permute-done((bf16[64,2176]{1,0:T(8,128)(2,1)S(1)}, bf16[64,2176]{1,0:T(8,128)(2,1)S(1)}, u32[]{:S(2)}, u32[]{:S(2)}) %collective-permute-start) | collective-permute-done | bytes 278560 | tf_op jit(solution)/shard_map/ppermute | solution.py:431
  14.4 2.1 %collective-permute-start.1 = (bf16[64,2176]{1,0:T(8,128)(2,1)S(1)}, bf16[64,2176]{1,0:T(8,128)(2,1)S(1)}, u32[]{:S(2)}, u32[]{:S(2)}) collective-permute-start(bf16[64,2176]{1,0:T(8,128)(2,1)S(1)} %collective-permute-done.refs_1_), channel_id=1, source_target_pairs={{0,4},{4,8},{8,12},{12,14},{14,10},{10,6},{6,2},{2,0},{1,5},{5,9},... | collective-permute-start | bytes 835592 | tf_op jit(solution)/shard_map/ppermute | solution.py:445
  16.6 2.2 %copy-done = bf16[32,2,64,512]{3,2,1,0:T(8,128)(2,1)S(1)} copy-done((bf16[32,2,64,512]{3,2,1,0:T(8,128)(2,1)S(1)}, bf16[32,2,64,512]{3,2,1,0:T(8,128)(2,1)}, u32[]{:S(2)}) %copy-start) | copy-done | bytes 4194328
  18.8 2.2 %shard_map.78 = (f32[2,512,128]{2,1,0:T(8,128)S(1)}, bf16[2,16,128]{2,1,0:T(8,128)(2,1)S(1)}, f32[2,512,128]{2,1,0:T(8,128)S(1)}, bf16[2,16,128]{2,1,0:T(8,128)(2,1)S(1)}) custom-call(s32[2,128]{1,0:T(2,128)S(1)} %maximum_convert_fusion.refs_0_, bf16[64,2176]{1,0:T(8,128)(2,1)S(1)} %collective-permute-done.refs_1_, ...), custom_call_target="tpu_custom_call" | custom-call | flops 1073741824 | bytes 2621440 | tf_op jit(solution)/shard_map/pallas_call | solution.py:249
  21.0 2.1 %collective-permute-done.4.refs_2_ = bf16[64,2048]{1,0:T(8,128)(2,1)S(1)} collective-permute-done((bf16[64,2048]{1,0:T(8,128)(2,1)S(1)}, bf16[64,2048]{1,0:T(8,128)(2,1)S(1)}, u32[]{:S(2)}, u32[]{:S(2)}) %collective-permute-start.4) | collective-permute-done | bytes 262176 | tf_op jit(solution)/shard_map/ppermute | solution.py:431
  23.1 2.4 %collective-permute-start.7 = (bf16[64,2048]{1,0:T(8,128)(2,1)S(1)}, bf16[64,2048]{1,0:T(8,128)(2,1)S(1)}, u32[]{:S(2)}, u32[]{:S(2)}) collective-permute-start(bf16[64,2048]{1,0:T(8,128)(2,1)S(1)} %collective-permute-done.3.refs_1_), channel_id=1, source_target_pairs={{0,4},{4,8},{8,12},{12,14},{14,10},{10,6},{6,2},{2,0},{1,5},{5,9},... | collective-permute-start | bytes 786440 | tf_op jit(solution)/shard_map/ppermute | solution.py:445
  25.5 3.9 %shard_map.79 = (f32[2,512,128]{2,1,0:T(8,128)S(1)}, bf16[2,16,128]{2,1,0:T(8,128)(2,1)S(1)}, f32[2,512,128]{2,1,0:T(8,128)S(1)}, bf16[2,16,128]{2,1,0:T(8,128)(2,1)S(1)}, bf16[32,2,64,512]{3,2,1,0:T(8,128)(2,1)}) custom-call(s32[2,128]{1,0:T(2,128)S(1)} %maximum_convert_fusion.refs_0_, bf16[64,2048]{1,0:T(8,128)(2,1)S(1)} %collective-permute-done.3.refs_1_, ...), custom_call_target="tpu_custom_call" | custom-call | flops 1073741824 | bytes 2621440 | tf_op jit(solution)/shard_map/pallas_call | solution.py:249
  29.4 3.4 %collective-permute-start.5 = (bf16[64,2176]{1,0:T(8,128)(2,1)S(1)}, bf16[64,2176]{1,0:T(8,128)(2,1)S(1)}, u32[]{:S(2)}, u32[]{:S(2)}) collective-permute-start(bf16[64,2176]{1,0:T(8,128)(2,1)S(1)} %collective-permute-done.1.refs_1_), channel_id=1, source_target_pairs={{0,4},{4,8},{8,12},{12,14},{14,10},{10,6},{6,2},{2,0},{1,5},{5,9},... | collective-permute-start | bytes 835592 | tf_op jit(solution)/shard_map/ppermute | solution.py:445
  32.9 2.2 %shard_map.80 = (f32[2,512,128]{2,1,0:T(8,128)S(1)}, bf16[2,16,128]{2,1,0:T(8,128)(2,1)S(1)}, f32[2,512,128]{2,1,0:T(8,128)S(1)}, bf16[2,16,128]{2,1,0:T(8,128)(2,1)S(1)}) custom-call(s32[2,128]{1,0:T(2,128)S(1)} %maximum_convert_fusion.1.refs_0_.lists_ref, bf16[64,2176]{1,0:T(8,128)(2,1)S(1)} %collective-permute-done.1.refs_1_, ...), custom_call_target="tpu_custom_call" | custom-call | flops 1073741824 | bytes 2621440 | tf_op jit(solution)/shard_map/pallas_call | solution.py:249
  35.2 1.1 %collective-permute-done.9.refs_2_ = bf16[64,2048]{1,0:T(8,128)(2,1)S(1)} collective-permute-done((bf16[64,2048]{1,0:T(8,128)(2,1)S(1)}, bf16[64,2048]{1,0:T(8,128)(2,1)S(1)}, u32[]{:S(2)}, u32[]{:S(2)}) %collective-permute-start.9) | collective-permute-done | bytes 262176 | tf_op jit(solution)/shard_map/ppermute | solution.py:445
  36.3 1.3 %collective-permute-start.11 = (bf16[64,2048]{1,0:T(8,128)(2,1)S(1)}, bf16[64,2048]{1,0:T(8,128)(2,1)S(1)}, u32[]{:S(2)}, u32[]{:S(2)}) collective-permute-start(bf16[64,2048]{1,0:T(8,128)(2,1)S(1)} %collective-permute-done.9.refs_2_), channel_id=1, source_target_pairs={{0,2},{4,0},{8,4},{12,8},{14,12},{10,14},{6,10},{2,6},{1,3},{5,1},... | collective-permute-start | bytes 786440 | tf_op jit(solution)/shard_map/ppermute | solution.py:445
  37.7 3.3 %collective-permute-start.14 = (bf16[64,2048]{1,0:T(8,128)(2,1)S(1)}, bf16[64,2048]{1,0:T(8,128)(2,1)S(1)}, u32[]{:S(2)}, u32[]{:S(2)}) collective-permute-start(bf16[64,2048]{1,0:T(8,128)(2,1)S(1)} %collective-permute-done.7.refs_1_), channel_id=1, source_target_pairs={{0,4},{4,8},{8,12},{12,14},{14,10},{10,6},{6,2},{2,0},{1,5},{5,9},... | collective-permute-start | bytes 786440 | tf_op jit(solution)/shard_map/ppermute | solution.py:445
  40.9 2.3 %shard_map.81 = (f32[2,512,128]{2,1,0:T(8,128)S(1)}, bf16[2,16,128]{2,1,0:T(8,128)(2,1)S(1)}, f32[2,512,128]{2,1,0:T(8,128)S(1)}, bf16[2,16,128]{2,1,0:T(8,128)(2,1)S(1)}) custom-call(s32[2,128]{1,0:T(2,128)S(1)} %maximum_convert_fusion.1.refs_0_.lists_ref, bf16[64,2048]{1,0:T(8,128)(2,1)S(1)} %collective-permute-done.7.refs_1_, ...), custom_call_target="tpu_custom_call" | custom-call | flops 1073741824 | bytes 2621440 | tf_op jit(solution)/shard_map/pallas_call | solution.py:249
  43.2 2.1 %collective-permute-start.10 = (bf16[64,2176]{1,0:T(8,128)(2,1)S(1)}, bf16[64,2176]{1,0:T(8,128)(2,1)S(1)}, u32[]{:S(2)}, u32[]{:S(2)}) collective-permute-start(bf16[64,2176]{1,0:T(8,128)(2,1)S(1)} %collective-permute-done.5.refs_1_), channel_id=1, source_target_pairs={{0,4},{4,8},{8,12},{12,14},{14,10},{10,6},{6,2},{2,0},{1,5},{5,9},... | collective-permute-start | bytes 835592 | tf_op jit(solution)/shard_map/ppermute | solution.py:445
  45.3 2.2 %shard_map.82 = (f32[2,512,128]{2,1,0:T(8,128)S(1)}, bf16[2,16,128]{2,1,0:T(8,128)(2,1)S(1)}, f32[2,512,128]{2,1,0:T(8,128)S(1)}, bf16[2,16,128]{2,1,0:T(8,128)(2,1)S(1)}) custom-call(s32[2,128]{1,0:T(2,128)S(1)} %maximum_convert_fusion.2.refs_0_, bf16[64,2176]{1,0:T(8,128)(2,1)S(1)} %collective-permute-done.5.refs_1_, ...), custom_call_target="tpu_custom_call" | custom-call | flops 1073741824 | bytes 2621440 | tf_op jit(solution)/shard_map/pallas_call | solution.py:249
  47.7 3.4 %collective-permute-start.15 = (bf16[2,528,128]{2,1,0:T(8,128)(2,1)S(1)}, bf16[2,528,128]{2,1,0:T(8,128)(2,1)S(1)}, u32[]{:S(2)}, u32[]{:S(2)}) collective-permute-start(bf16[2,528,128]{2,1,0:T(8,128)(2,1)S(1)} %shard_map.83), channel_id=1, source_target_pairs={{0,4},{4,8},{8,12},{12,14},{14,10},{10,6},{6,2},{2,0},{1,5},{5,9},... | collective-permute-start | bytes 811016 | tf_op jit(solution)/shard_map/ppermute | solution.py:468
  51.0 2.3 %shard_map.84 = (f32[2,512,128]{2,1,0:T(8,128)S(1)}, bf16[2,16,128]{2,1,0:T(8,128)(2,1)S(1)}, f32[2,512,128]{2,1,0:T(8,128)S(1)}, bf16[2,16,128]{2,1,0:T(8,128)(2,1)S(1)}) custom-call(s32[2,128]{1,0:T(2,128)S(1)} %maximum_convert_fusion.2.refs_0_, bf16[64,2048]{1,0:T(8,128)(2,1)S(1)} %collective-permute-done.14.refs_1_, ...), custom_call_target="tpu_custom_call" | custom-call | flops 1073741824 | bytes 2621440 | tf_op jit(solution)/shard_map/pallas_call | solution.py:249
  53.4 4.4 %collective-permute-done.13.refs_2_ = bf16[64,2048]{1,0:T(8,128)(2,1)S(1)} collective-permute-done((bf16[64,2048]{1,0:T(8,128)(2,1)S(1)}, bf16[64,2048]{1,0:T(8,128)(2,1)S(1)}, u32[]{:S(2)}, u32[]{:S(2)}) %collective-permute-start.13) | collective-permute-done | bytes 262176 | tf_op jit(solution)/shard_map/ppermute | solution.py:445
  57.9 2.3 %shard_map.86 = (f32[2,512,128]{2,1,0:T(8,128)S(1)}, bf16[2,16,128]{2,1,0:T(8,128)(2,1)S(1)}, f32[2,512,128]{2,1,0:T(8,128)S(1)}, bf16[2,16,128]{2,1,0:T(8,128)(2,1)S(1)}) custom-call(s32[1,128]{1,0:T(1,128)S(1)} %fusion.refs_0_, bf16[64,2176]{1,0:T(8,128)(2,1)S(1)} %collective-permute-done.10.refs_1_, bf16[64,2048]{1,0:T(8,128)(2,1)S(1)} %collective-permute-done.13.refs_2_, ...), custom_call_target="tpu_custom_call" | custom-call | flops 1073741824 | bytes 2621440 | tf_op jit(solution)/shard_map/pallas_call | solution.py:249
  60.2 1.8 %collective-permute-done.16.in_ref = bf16[2,528,128]{2,1,0:T(8,128)(2,1)S(1)} collective-permute-done((bf16[2,528,128]{2,1,0:T(8,128)(2,1)S(1)}, bf16[2,528,128]{2,1,0:T(8,128)(2,1)S(1)}, u32[]{:S(2)}, u32[]{:S(2)}) %collective-permute-start.16) | collective-permute-done | bytes 270368 | tf_op jit(solution)/shard_map/ppermute | solution.py:468
  62.0 1.8 %collective-permute-start.17 = (bf16[2,528,128]{2,1,0:T(8,128)(2,1)S(1)}, bf16[2,528,128]{2,1,0:T(8,128)(2,1)S(1)}, u32[]{:S(2)}, u32[]{:S(2)}) collective-permute-start(bf16[2,528,128]{2,1,0:T(8,128)(2,1)S(1)} %shard_map.87), channel_id=1, source_target_pairs={{0,4},{4,8},{8,12},{12,14},{14,10},{10,6},{6,2},{2,0},{1,5},{5,9},... | collective-permute-start | bytes 811016 | tf_op jit(solution)/shard_map/ppermute | solution.py:492
  63.8 0.3 collective-permute-start.18
  64.1 0.6 shard_map.89
  64.8 1.8 %collective-permute-start.21 = (bf16[2,528,128]{2,1,0:T(8,128)(2,1)S(1)}, bf16[2,528,128]{2,1,0:T(8,128)(2,1)S(1)}, u32[]{:S(2)}, u32[]{:S(2)}) collective-permute-start(bf16[2,528,128]{2,1,0:T(8,128)(2,1)S(1)} %shard_map.89), channel_id=1, source_target_pairs={{0,4},{4,8},{8,12},{12,14},{14,10},{10,6},{6,2},{2,0},{1,5},{5,9},... | collective-permute-start | bytes 811016 | tf_op jit(solution)/shard_map/ppermute | solution.py:492
  66.6 0.6 shard_map.90
  67.2 0.3 collective-permute-start.22
  67.6 1.8 %shard_map.91 = (f32[2,512,128]{2,1,0:T(8,128)S(1)}, bf16[2,16,128]{2,1,0:T(8,128)(2,1)S(1)}) custom-call(s32[1,128]{1,0:T(1,128)S(1)} %fusion.1.refs_0_, bf16[64,2176]{1,0:T(8,128)(2,1)S(1)} %get-tuple-element.124.refs_1_, bf16[2,64,512]{2,1,0:T(8,128)(2,1)S(1)} %bitcast.2, bf16[32,2,64,512]{3,2,1,0:T(8,128)(2,1)S(1)} %copy-done.1), custom_call_target="tpu_custom_call" | custom-call | flops 536870912 | bytes 1310720 | tf_op jit(solution)/shard_map/pallas_call | solution.py:249
  69.3 2.1 %collective-permute-done.17.in_ref = bf16[2,528,128]{2,1,0:T(8,128)(2,1)S(1)} collective-permute-done((bf16[2,528,128]{2,1,0:T(8,128)(2,1)S(1)}, bf16[2,528,128]{2,1,0:T(8,128)(2,1)S(1)}, u32[]{:S(2)}, u32[]{:S(2)}) %collective-permute-start.17) | collective-permute-done | bytes 270368 | tf_op jit(solution)/shard_map/ppermute | solution.py:492
  71.4 1.8 %collective-permute-done.18.in_ref = bf16[2,528,128]{2,1,0:T(8,128)(2,1)S(1)} collective-permute-done((bf16[2,528,128]{2,1,0:T(8,128)(2,1)S(1)}, bf16[2,528,128]{2,1,0:T(8,128)(2,1)S(1)}, u32[]{:S(2)}, u32[]{:S(2)}) %collective-permute-start.18) | collective-permute-done | bytes 270368 | tf_op jit(solution)/shard_map/ppermute | solution.py:492
  73.3 0.6 shard_map.92
  73.9 0.1 collective-permute-start.19
  74.0 0.6 shard_map.93
  74.6 2.1 %collective-permute-start.20 = (bf16[2,528,128]{2,1,0:T(8,128)(2,1)S(1)}, bf16[2,528,128]{2,1,0:T(8,128)(2,1)S(1)}, u32[]{:S(2)}, u32[]{:S(2)}) collective-permute-start(bf16[2,528,128]{2,1,0:T(8,128)(2,1)S(1)} %shard_map.93), channel_id=1, source_target_pairs={{0,2},{4,0},{8,4},{12,8},{14,12},{10,14},{6,10},{2,6},{1,3},{5,1},... | collective-permute-start | bytes 811016 | tf_op jit(solution)/shard_map/ppermute | solution.py:492
  76.7 0.6 collective-permute-done.21.in_ref
  77.2 1.8 %collective-permute-done.22.in_ref = bf16[2,528,128]{2,1,0:T(8,128)(2,1)S(1)} collective-permute-done((bf16[2,528,128]{2,1,0:T(8,128)(2,1)S(1)}, bf16[2,528,128]{2,1,0:T(8,128)(2,1)S(1)}, u32[]{:S(2)}, u32[]{:S(2)}) %collective-permute-start.22) | collective-permute-done | bytes 270368 | tf_op jit(solution)/shard_map/ppermute | solution.py:492
  79.1 0.6 shard_map.94
  79.7 0.1 collective-permute-start.25
  79.8 0.6 shard_map.95
  80.4 2.1 %collective-permute-start.26 = (bf16[2,528,128]{2,1,0:T(8,128)(2,1)S(1)}, bf16[2,528,128]{2,1,0:T(8,128)(2,1)S(1)}, u32[]{:S(2)}, u32[]{:S(2)}) collective-permute-start(bf16[2,528,128]{2,1,0:T(8,128)(2,1)S(1)} %shard_map.95), channel_id=1, source_target_pairs={{0,2},{4,0},{8,4},{12,8},{14,12},{10,14},{6,10},{2,6},{1,3},{5,1},... | collective-permute-start | bytes 811016 | tf_op jit(solution)/shard_map/ppermute | solution.py:492
  82.5 1.8 %shard_map.96 = (f32[2,512,128]{2,1,0:T(8,128)S(1)}, bf16[2,16,128]{2,1,0:T(8,128)(2,1)S(1)}) custom-call(s32[1,128]{1,0:T(1,128)S(1)} %fusion.1.refs_0_, bf16[64,2048]{1,0:T(8,128)(2,1)S(1)} %get-tuple-element.135.refs_1_, bf16[2,64,512]{2,1,0:T(8,128)(2,1)S(1)} %bitcast.3, bf16[32,2,64,512]{3,2,1,0:T(8,128)(2,1)S(1)} %copy-done.1), custom_call_target="tpu_custom_call" | custom-call | flops 536870912 | bytes 1310720 | tf_op jit(solution)/shard_map/pallas_call | solution.py:249
  84.3 0.6 collective-permute-done.20.in_ref
  84.9 0.6 shard_map.97
  85.6 0.6 shard_map.98
  86.2 2.1 %collective-permute-start.24 = (bf16[2,528,128]{2,1,0:T(8,128)(2,1)S(1)}, bf16[2,528,128]{2,1,0:T(8,128)(2,1)S(1)}, u32[]{:S(2)}, u32[]{:S(2)}) collective-permute-start(bf16[2,528,128]{2,1,0:T(8,128)(2,1)S(1)} %shard_map.98), channel_id=1, source_target_pairs={{0,2},{4,0},{8,4},{12,8},{14,12},{10,14},{6,10},{2,6},{1,3},{5,1},... | collective-permute-start | bytes 811016 | tf_op jit(solution)/shard_map/ppermute | solution.py:492
  88.3 0.8 collective-permute-done.25.in_ref
  89.1 1.5 %collective-permute-done.26.in_ref = bf16[2,528,128]{2,1,0:T(8,128)(2,1)S(1)} collective-permute-done((bf16[2,528,128]{2,1,0:T(8,128)(2,1)S(1)}, bf16[2,528,128]{2,1,0:T(8,128)(2,1)S(1)}, u32[]{:S(2)}, u32[]{:S(2)}) %collective-permute-start.26) | collective-permute-done | bytes 270368 | tf_op jit(solution)/shard_map/ppermute | solution.py:492
  90.6 1.4 %collective-permute-done.23.in_ref = bf16[2,528,128]{2,1,0:T(8,128)(2,1)S(1)} collective-permute-done((bf16[2,528,128]{2,1,0:T(8,128)(2,1)S(1)}, bf16[2,528,128]{2,1,0:T(8,128)(2,1)S(1)}, u32[]{:S(2)}, u32[]{:S(2)}) %collective-permute-start.23) | collective-permute-done | bytes 270368 | tf_op jit(solution)/shard_map/ppermute | solution.py:492
  92.0 1.5 %collective-permute-done.24.in_ref = bf16[2,528,128]{2,1,0:T(8,128)(2,1)S(1)} collective-permute-done((bf16[2,528,128]{2,1,0:T(8,128)(2,1)S(1)}, bf16[2,528,128]{2,1,0:T(8,128)(2,1)S(1)}, u32[]{:S(2)}, u32[]{:S(2)}) %collective-permute-start.24) | collective-permute-done | bytes 270368 | tf_op jit(solution)/shard_map/ppermute | solution.py:492
  93.5 0.6 shard_map.99
  94.2 1.5 %collective-permute-start.27 = (bf16[2,528,128]{2,1,0:T(8,128)(2,1)S(1)}, bf16[2,528,128]{2,1,0:T(8,128)(2,1)S(1)}, u32[]{:S(2)}, u32[]{:S(2)}) collective-permute-start(bf16[2,528,128]{2,1,0:T(8,128)(2,1)S(1)} %shard_map.99), channel_id=1, source_target_pairs={{0,2},{4,0},{8,4},{12,8},{14,12},{10,14},{6,10},{2,6},{1,3},{5,1},... | collective-permute-start | bytes 811016 | tf_op jit(solution)/shard_map/ppermute | solution.py:492
  95.7 0.6 shard_map.100
  96.4 0.6 collective-permute-start.28
  96.9 1.2 %shard_map.104 = bf16[32,2,64,512]{3,2,1,0:T(8,128)(2,1)} custom-call(s32[1]{0:T(128)} %bitcast.1.me_ref, s32[2,128]{1,0:T(2,128)S(1)} %maximum_convert_fusion.1.refs_0_.lists_ref, bf16[1,2,64,512]{3,2,1,0:T(8,128)(2,1)S(1)} %collective-permute-done.8.page_ref, bf16[32,2,64,512]{3,2,1,0:T(8,128)(2,1)} %get-tuple-element.153.old_ref), custom_call_target="tpu_custom_call", output_to_operand_aliasing={{}: (3, {})} | custom-call | flops 1 | bytes 1 | tf_op jit(solution)/shard_map/pallas_call | solution.py:275
  98.2 0.6 shard_map.101
  98.8 0.6 shard_map.102
  99.4 1.2 %collective-permute-done.27.refs_0_ = bf16[2,528,128]{2,1,0:T(8,128)(2,1)S(1)} collective-permute-done((bf16[2,528,128]{2,1,0:T(8,128)(2,1)S(1)}, bf16[2,528,128]{2,1,0:T(8,128)(2,1)S(1)}, u32[]{:S(2)}, u32[]{:S(2)}) %collective-permute-start.27) | collective-permute-done | bytes 270368 | tf_op jit(solution)/shard_map/ppermute | solution.py:492
  100.7 2.2 %collective-permute-done.28.refs_3_ = bf16[2,528,128]{2,1,0:T(8,128)(2,1)S(1)} collective-permute-done((bf16[2,528,128]{2,1,0:T(8,128)(2,1)S(1)}, bf16[2,528,128]{2,1,0:T(8,128)(2,1)S(1)}, u32[]{:S(2)}, u32[]{:S(2)}) %collective-permute-start.28) | collective-permute-done | bytes 270368 | tf_op jit(solution)/shard_map/ppermute | solution.py:492
  102.9 1.7 %shard_map.103 = bf16[1,64,4096]{2,1,0:T(8,128)(2,1)} custom-call(bf16[2,528,128]{2,1,0:T(8,128)(2,1)S(1)} %collective-permute-done.27.refs_0_, f32[2,512,128]{2,1,0:T(8,128)S(1)} %get-tuple-element.146.refs_1_, bf16[2,16,128]{2,1,0:T(8,128)(2,1)S(1)} %get-tuple-element.147.refs_2_, bf16[2,528,128]{2,1,0:T(8,128)(2,1)S(1)} %collective-permute-done.28.refs_3_, ...), custom_call_target="tpu_custom_call" | custom-call | flops 1605632 | bytes 3211264 | tf_op jit(solution)/shard_map/pallas_call | solution.py:347
  (43 shorter events, 0.6 us)
Async XLA Ops:
  1.9 1.0 copy-start.3
  3.0 0.7 copy-start.4
  3.9 10.4 %collective-permute-start = (bf16[64,2176]{1,0:T(8,128)(2,1)S(1)}, bf16[64,2176]{1,0:T(8,128)(2,1)S(1)}, u32[]{:S(2)}, u32[]{:S(2)}) collective-permute-start(bf16[64,2176]{1,0:T(8,128)(2,1)S(1)} %get-tuple-element.124.refs_1_), channel_id=1, source_target_pairs={{0,4},{4,8},{8,12},{12,14},{14,10},{10,6},{6,2},{2,0},{1,5},{5,9},... | collective-permute-start | bytes 835592 | tf_op jit(solution)/shard_map/ppermute | solution.py:431
  6.9 9.6 %collective-permute-start.2 = (bf16[64,2176]{1,0:T(8,128)(2,1)S(1)}, bf16[64,2176]{1,0:T(8,128)(2,1)S(1)}, u32[]{:S(2)}, u32[]{:S(2)}) collective-permute-start(bf16[64,2176]{1,0:T(8,128)(2,1)S(1)} %get-tuple-element.124.refs_1_), channel_id=1, source_target_pairs={{0,2},{4,0},{8,4},{12,8},{14,12},{10,14},{6,10},{2,6},{1,3},{5,1},... | collective-permute-start | bytes 835592 | tf_op jit(solution)/shard_map/ppermute | solution.py:431
  6.9 14.1 %collective-permute-start.3 = (bf16[64,2048]{1,0:T(8,128)(2,1)S(1)}, bf16[64,2048]{1,0:T(8,128)(2,1)S(1)}, u32[]{:S(2)}, u32[]{:S(2)}) collective-permute-start(bf16[64,2048]{1,0:T(8,128)(2,1)S(1)} %get-tuple-element.135.refs_1_), channel_id=1, source_target_pairs={{0,4},{4,8},{8,12},{12,14},{14,10},{10,6},{6,2},{2,0},{1,5},{5,9},... | collective-permute-start | bytes 786440 | tf_op jit(solution)/shard_map/ppermute | solution.py:431
  9.0 14.1 %collective-permute-start.4 = (bf16[64,2048]{1,0:T(8,128)(2,1)S(1)}, bf16[64,2048]{1,0:T(8,128)(2,1)S(1)}, u32[]{:S(2)}, u32[]{:S(2)}) collective-permute-start(bf16[64,2048]{1,0:T(8,128)(2,1)S(1)} %get-tuple-element.135.refs_1_), channel_id=1, source_target_pairs={{0,2},{4,0},{8,4},{12,8},{14,12},{10,14},{6,10},{2,6},{1,3},{5,1},... | collective-permute-start | bytes 786440 | tf_op jit(solution)/shard_map/ppermute | solution.py:431
  9.0 26.2 %collective-permute-start.8 = (bf16[1,2,64,512]{3,2,1,0:T(8,128)(2,1)}, bf16[1,2,64,512]{3,2,1,0:T(8,128)(2,1)S(1)}, u32[]{:S(2)}, u32[]{:S(2)}) collective-permute-start(bf16[1,2,64,512]{3,2,1,0:T(8,128)(2,1)} %param.7), channel_id=1, source_target_pairs={{8,0},{10,2},{12,4},{14,6},{0,8},{2,10},{4,12},{6,14},{9,1},{11,3}... | collective-permute-start | bytes 393224 | tf_op jit(solution)/shard_map/ppermute | solution.py:25
  14.4 15.0 %collective-permute-start.1 = (bf16[64,2176]{1,0:T(8,128)(2,1)S(1)}, bf16[64,2176]{1,0:T(8,128)(2,1)S(1)}, u32[]{:S(2)}, u32[]{:S(2)}) collective-permute-start(bf16[64,2176]{1,0:T(8,128)(2,1)S(1)} %collective-permute-done.refs_1_), channel_id=1, source_target_pairs={{0,4},{4,8},{8,12},{12,14},{14,10},{10,6},{6,2},{2,0},{1,5},{5,9},... | collective-permute-start | bytes 835592 | tf_op jit(solution)/shard_map/ppermute | solution.py:445
  16.5 16.3 %collective-permute-start.6 = (bf16[64,2176]{1,0:T(8,128)(2,1)S(1)}, bf16[64,2176]{1,0:T(8,128)(2,1)S(1)}, u32[]{:S(2)}, u32[]{:S(2)}) collective-permute-start(bf16[64,2176]{1,0:T(8,128)(2,1)S(1)} %collective-permute-done.2.refs_2_), channel_id=1, source_target_pairs={{0,2},{4,0},{8,4},{12,8},{14,12},{10,14},{6,10},{2,6},{1,3},{5,1},... | collective-permute-start | bytes 835592 | tf_op jit(solution)/shard_map/ppermute | solution.py:445
  16.6 2.2 %copy-start = (bf16[32,2,64,512]{3,2,1,0:T(8,128)(2,1)S(1)}, bf16[32,2,64,512]{3,2,1,0:T(8,128)(2,1)}, u32[]{:S(2)}) copy-start(bf16[32,2,64,512]{3,2,1,0:T(8,128)(2,1)} %refs_3_.17) | copy-start | bytes 12582916
  23.1 12.0 %collective-permute-start.7 = (bf16[64,2048]{1,0:T(8,128)(2,1)S(1)}, bf16[64,2048]{1,0:T(8,128)(2,1)S(1)}, u32[]{:S(2)}, u32[]{:S(2)}) collective-permute-start(bf16[64,2048]{1,0:T(8,128)(2,1)S(1)} %collective-permute-done.3.refs_1_), channel_id=1, source_target_pairs={{0,4},{4,8},{8,12},{12,14},{14,10},{10,6},{6,2},{2,0},{1,5},{5,9},... | collective-permute-start | bytes 786440 | tf_op jit(solution)/shard_map/ppermute | solution.py:445
  25.5 10.8 %collective-permute-start.9 = (bf16[64,2048]{1,0:T(8,128)(2,1)S(1)}, bf16[64,2048]{1,0:T(8,128)(2,1)S(1)}, u32[]{:S(2)}, u32[]{:S(2)}) collective-permute-start(bf16[64,2048]{1,0:T(8,128)(2,1)S(1)} %collective-permute-done.4.refs_2_), channel_id=1, source_target_pairs={{0,2},{4,0},{8,4},{12,8},{14,12},{10,14},{6,10},{2,6},{1,3},{5,1},... | collective-permute-start | bytes 786440 | tf_op jit(solution)/shard_map/ppermute | solution.py:445
  29.4 13.8 %collective-permute-start.5 = (bf16[64,2176]{1,0:T(8,128)(2,1)S(1)}, bf16[64,2176]{1,0:T(8,128)(2,1)S(1)}, u32[]{:S(2)}, u32[]{:S(2)}) collective-permute-start(bf16[64,2176]{1,0:T(8,128)(2,1)S(1)} %collective-permute-done.1.refs_1_), channel_id=1, source_target_pairs={{0,4},{4,8},{8,12},{12,14},{14,10},{10,6},{6,2},{2,0},{1,5},{5,9},... | collective-permute-start | bytes 835592 | tf_op jit(solution)/shard_map/ppermute | solution.py:445
  32.8 12.5 %collective-permute-start.12 = (bf16[64,2176]{1,0:T(8,128)(2,1)S(1)}, bf16[64,2176]{1,0:T(8,128)(2,1)S(1)}, u32[]{:S(2)}, u32[]{:S(2)}) collective-permute-start(bf16[64,2176]{1,0:T(8,128)(2,1)S(1)} %collective-permute-done.6.refs_2_), channel_id=1, source_target_pairs={{0,2},{4,0},{8,4},{12,8},{14,12},{10,14},{6,10},{2,6},{1,3},{5,1},... | collective-permute-start | bytes 835592 | tf_op jit(solution)/shard_map/ppermute | solution.py:445
  35.2 15.9 %copy-start.1 = (bf16[32,2,64,512]{3,2,1,0:T(8,128)(2,1)S(1)}, bf16[32,2,64,512]{3,2,1,0:T(8,128)(2,1)}, u32[]{:S(2)}) copy-start(bf16[32,2,64,512]{3,2,1,0:T(8,128)(2,1)} %refs_3_.17) | copy-start | bytes 12582916
  36.3 11.3 %collective-permute-start.11 = (bf16[64,2048]{1,0:T(8,128)(2,1)S(1)}, bf16[64,2048]{1,0:T(8,128)(2,1)S(1)}, u32[]{:S(2)}, u32[]{:S(2)}) collective-permute-start(bf16[64,2048]{1,0:T(8,128)(2,1)S(1)} %collective-permute-done.9.refs_2_), channel_id=1, source_target_pairs={{0,2},{4,0},{8,4},{12,8},{14,12},{10,14},{6,10},{2,6},{1,3},{5,1},... | collective-permute-start | bytes 786440 | tf_op jit(solution)/shard_map/ppermute | solution.py:445
  37.7 13.4 %collective-permute-start.14 = (bf16[64,2048]{1,0:T(8,128)(2,1)S(1)}, bf16[64,2048]{1,0:T(8,128)(2,1)S(1)}, u32[]{:S(2)}, u32[]{:S(2)}) collective-permute-start(bf16[64,2048]{1,0:T(8,128)(2,1)S(1)} %collective-permute-done.7.refs_1_), channel_id=1, source_target_pairs={{0,4},{4,8},{8,12},{12,14},{14,10},{10,6},{6,2},{2,0},{1,5},{5,9},... | collective-permute-start | bytes 786440 | tf_op jit(solution)/shard_map/ppermute | solution.py:445
  43.2 14.7 %collective-permute-start.10 = (bf16[64,2176]{1,0:T(8,128)(2,1)S(1)}, bf16[64,2176]{1,0:T(8,128)(2,1)S(1)}, u32[]{:S(2)}, u32[]{:S(2)}) collective-permute-start(bf16[64,2176]{1,0:T(8,128)(2,1)S(1)} %collective-permute-done.5.refs_1_), channel_id=1, source_target_pairs={{0,4},{4,8},{8,12},{12,14},{14,10},{10,6},{6,2},{2,0},{1,5},{5,9},... | collective-permute-start | bytes 835592 | tf_op jit(solution)/shard_map/ppermute | solution.py:445
  47.6 10.2 %collective-permute-start.13 = (bf16[64,2048]{1,0:T(8,128)(2,1)S(1)}, bf16[64,2048]{1,0:T(8,128)(2,1)S(1)}, u32[]{:S(2)}, u32[]{:S(2)}) collective-permute-start(bf16[64,2048]{1,0:T(8,128)(2,1)S(1)} %collective-permute-done.11.refs_2_), channel_id=1, source_target_pairs={{0,2},{4,0},{8,4},{12,8},{14,12},{10,14},{6,10},{2,6},{1,3},{5,1},... | collective-permute-start | bytes 786440 | tf_op jit(solution)/shard_map/ppermute | solution.py:445
  47.7 12.5 %collective-permute-start.15 = (bf16[2,528,128]{2,1,0:T(8,128)(2,1)S(1)}, bf16[2,528,128]{2,1,0:T(8,128)(2,1)S(1)}, u32[]{:S(2)}, u32[]{:S(2)}) collective-permute-start(bf16[2,528,128]{2,1,0:T(8,128)(2,1)S(1)} %shard_map.83), channel_id=1, source_target_pairs={{0,4},{4,8},{8,12},{12,14},{14,10},{10,6},{6,2},{2,0},{1,5},{5,9},... | collective-permute-start | bytes 811016 | tf_op jit(solution)/shard_map/ppermute | solution.py:468
  53.4 8.6 %collective-permute-start.16 = (bf16[2,528,128]{2,1,0:T(8,128)(2,1)S(1)}, bf16[2,528,128]{2,1,0:T(8,128)(2,1)S(1)}, u32[]{:S(2)}, u32[]{:S(2)}) collective-permute-start(bf16[2,528,128]{2,1,0:T(8,128)(2,1)S(1)} %shard_map.85), channel_id=1, source_target_pairs={{0,2},{4,0},{8,4},{12,8},{14,12},{10,14},{6,10},{2,6},{1,3},{5,1},... | collective-permute-start | bytes 811016 | tf_op jit(solution)/shard_map/ppermute | solution.py:468
  57.9 9.7 %copy-start.2 = (bf16[1,2,64,512]{3,2,1,0:T(8,128)(2,1)S(1)}, bf16[1,2,64,512]{3,2,1,0:T(8,128)(2,1)}, u32[]{:S(2)}) copy-start(bf16[1,2,64,512]{3,2,1,0:T(8,128)(2,1)} %param.7) | copy-start | bytes 393220
  62.0 9.5 %collective-permute-start.17 = (bf16[2,528,128]{2,1,0:T(8,128)(2,1)S(1)}, bf16[2,528,128]{2,1,0:T(8,128)(2,1)S(1)}, u32[]{:S(2)}, u32[]{:S(2)}) collective-permute-start(bf16[2,528,128]{2,1,0:T(8,128)(2,1)S(1)} %shard_map.87), channel_id=1, source_target_pairs={{0,4},{4,8},{8,12},{12,14},{14,10},{10,6},{6,2},{2,0},{1,5},{5,9},... | collective-permute-start | bytes 811016 | tf_op jit(solution)/shard_map/ppermute | solution.py:492
  63.8 9.5 %collective-permute-start.18 = (bf16[2,528,128]{2,1,0:T(8,128)(2,1)S(1)}, bf16[2,528,128]{2,1,0:T(8,128)(2,1)S(1)}, u32[]{:S(2)}, u32[]{:S(2)}) collective-permute-start(bf16[2,528,128]{2,1,0:T(8,128)(2,1)S(1)} %shard_map.88), channel_id=1, source_target_pairs={{0,2},{4,0},{8,4},{12,8},{14,12},{10,14},{6,10},{2,6},{1,3},{5,1},... | collective-permute-start | bytes 811016 | tf_op jit(solution)/shard_map/ppermute | solution.py:492
  64.8 12.5 %collective-permute-start.21 = (bf16[2,528,128]{2,1,0:T(8,128)(2,1)S(1)}, bf16[2,528,128]{2,1,0:T(8,128)(2,1)S(1)}, u32[]{:S(2)}, u32[]{:S(2)}) collective-permute-start(bf16[2,528,128]{2,1,0:T(8,128)(2,1)S(1)} %shard_map.89), channel_id=1, source_target_pairs={{0,4},{4,8},{8,12},{12,14},{14,10},{10,6},{6,2},{2,0},{1,5},{5,9},... | collective-permute-start | bytes 811016 | tf_op jit(solution)/shard_map/ppermute | solution.py:492
  67.2 11.9 %collective-permute-start.22 = (bf16[2,528,128]{2,1,0:T(8,128)(2,1)S(1)}, bf16[2,528,128]{2,1,0:T(8,128)(2,1)S(1)}, u32[]{:S(2)}, u32[]{:S(2)}) collective-permute-start(bf16[2,528,128]{2,1,0:T(8,128)(2,1)S(1)} %shard_map.90), channel_id=1, source_target_pairs={{0,2},{4,0},{8,4},{12,8},{14,12},{10,14},{6,10},{2,6},{1,3},{5,1},... | collective-permute-start | bytes 811016 | tf_op jit(solution)/shard_map/ppermute | solution.py:492
  73.9 10.4 %collective-permute-start.19 = (bf16[2,528,128]{2,1,0:T(8,128)(2,1)S(1)}, bf16[2,528,128]{2,1,0:T(8,128)(2,1)S(1)}, u32[]{:S(2)}, u32[]{:S(2)}) collective-permute-start(bf16[2,528,128]{2,1,0:T(8,128)(2,1)S(1)} %shard_map.92), channel_id=1, source_target_pairs={{0,4},{4,8},{8,12},{12,14},{14,10},{10,6},{6,2},{2,0},{1,5},{5,9},... | collective-permute-start | bytes 811016 | tf_op jit(solution)/shard_map/ppermute | solution.py:492
  74.6 10.2 %collective-permute-start.20 = (bf16[2,528,128]{2,1,0:T(8,128)(2,1)S(1)}, bf16[2,528,128]{2,1,0:T(8,128)(2,1)S(1)}, u32[]{:S(2)}, u32[]{:S(2)}) collective-permute-start(bf16[2,528,128]{2,1,0:T(8,128)(2,1)S(1)} %shard_map.93), channel_id=1, source_target_pairs={{0,2},{4,0},{8,4},{12,8},{14,12},{10,14},{6,10},{2,6},{1,3},{5,1},... | collective-permute-start | bytes 811016 | tf_op jit(solution)/shard_map/ppermute | solution.py:492
  79.7 9.4 %collective-permute-start.25 = (bf16[2,528,128]{2,1,0:T(8,128)(2,1)S(1)}, bf16[2,528,128]{2,1,0:T(8,128)(2,1)S(1)}, u32[]{:S(2)}, u32[]{:S(2)}) collective-permute-start(bf16[2,528,128]{2,1,0:T(8,128)(2,1)S(1)} %shard_map.94), channel_id=1, source_target_pairs={{0,4},{4,8},{8,12},{12,14},{14,10},{10,6},{6,2},{2,0},{1,5},{5,9},... | collective-permute-start | bytes 811016 | tf_op jit(solution)/shard_map/ppermute | solution.py:492
  80.4 10.2 %collective-permute-start.26 = (bf16[2,528,128]{2,1,0:T(8,128)(2,1)S(1)}, bf16[2,528,128]{2,1,0:T(8,128)(2,1)S(1)}, u32[]{:S(2)}, u32[]{:S(2)}) collective-permute-start(bf16[2,528,128]{2,1,0:T(8,128)(2,1)S(1)} %shard_map.95), channel_id=1, source_target_pairs={{0,2},{4,0},{8,4},{12,8},{14,12},{10,14},{6,10},{2,6},{1,3},{5,1},... | collective-permute-start | bytes 811016 | tf_op jit(solution)/shard_map/ppermute | solution.py:492
  85.5 6.5 %collective-permute-start.23 = (bf16[2,528,128]{2,1,0:T(8,128)(2,1)S(1)}, bf16[2,528,128]{2,1,0:T(8,128)(2,1)S(1)}, u32[]{:S(2)}, u32[]{:S(2)}) collective-permute-start(bf16[2,528,128]{2,1,0:T(8,128)(2,1)S(1)} %shard_map.97), channel_id=1, source_target_pairs={{0,4},{4,8},{8,12},{12,14},{14,10},{10,6},{6,2},{2,0},{1,5},{5,9},... | collective-permute-start | bytes 811016 | tf_op jit(solution)/shard_map/ppermute | solution.py:492
  86.2 7.3 %collective-permute-start.24 = (bf16[2,528,128]{2,1,0:T(8,128)(2,1)S(1)}, bf16[2,528,128]{2,1,0:T(8,128)(2,1)S(1)}, u32[]{:S(2)}, u32[]{:S(2)}) collective-permute-start(bf16[2,528,128]{2,1,0:T(8,128)(2,1)S(1)} %shard_map.98), channel_id=1, source_target_pairs={{0,2},{4,0},{8,4},{12,8},{14,12},{10,14},{6,10},{2,6},{1,3},{5,1},... | collective-permute-start | bytes 811016 | tf_op jit(solution)/shard_map/ppermute | solution.py:492
  94.2 6.5 %collective-permute-start.27 = (bf16[2,528,128]{2,1,0:T(8,128)(2,1)S(1)}, bf16[2,528,128]{2,1,0:T(8,128)(2,1)S(1)}, u32[]{:S(2)}, u32[]{:S(2)}) collective-permute-start(bf16[2,528,128]{2,1,0:T(8,128)(2,1)S(1)} %shard_map.99), channel_id=1, source_target_pairs={{0,2},{4,0},{8,4},{12,8},{14,12},{10,14},{6,10},{2,6},{1,3},{5,1},... | collective-permute-start | bytes 811016 | tf_op jit(solution)/shard_map/ppermute | solution.py:492
  96.4 6.5 %collective-permute-start.28 = (bf16[2,528,128]{2,1,0:T(8,128)(2,1)S(1)}, bf16[2,528,128]{2,1,0:T(8,128)(2,1)S(1)}, u32[]{:S(2)}, u32[]{:S(2)}) collective-permute-start(bf16[2,528,128]{2,1,0:T(8,128)(2,1)S(1)} %shard_map.100), channel_id=1, source_target_pairs={{0,4},{4,8},{8,12},{12,14},{14,10},{10,6},{6,2},{2,0},{1,5},{5,9},... | collective-permute-start | bytes 811016 | tf_op jit(solution)/shard_map/ppermute | solution.py:492

commit v7 on v6

--- a/solution.py
+++ b/solution.py
@@ -159,6 +159,7 @@
     groups, suffix, cap, page_len, count, own, keeping = sizes
     refs = list(refs)
     meta = refs.pop(0)
+    who = None if own else refs.pop(0)
     queries = [refs.pop(0) for _ in range(count)]
     if own:
         own_kv = refs.pop(0)
@@ -181,11 +182,16 @@
         filled[job[-1]] += 1
 
     def stacked(n, part, h):
-        return jnp.concatenate([held[meta[n, c], part, :, block_of(h)] for c in range(cap)], 0)
+        return jnp.concatenate([held[wanted(n, c), part, :, block_of(h)] for c in range(cap)], 0)
+
+    def wanted(n, field):
+        return meta[0 if own else who[n], field]
 
     def score(i):
         n, array, first, h, _ = jobs[i]
         q_ref = queries[array]
+        if not own:
+            q_ref = q_ref.at[who[n]]
         q = jnp.concatenate([q_ref[:, block_of(first * groups + g)] for g in range(groups)], 0)
         scores[i % 2] = dot_nt(q, stacked(n, 0, h))
         if own:
@@ -195,7 +201,7 @@
 
     def weigh(i):
         n, _, _, h, result = jobs[i]
-        live = iota((1, keys), 1) < meta[n, cap] * page_len
+        live = iota((1, keys), 1) < wanted(n, cap) * page_len
         s = jnp.where(live, scores[i % 2], DEAD)
         top = jnp.max(s, axis=-1, keepdims=True)
         if own:
@@ -249,7 +255,7 @@
     out = pl.pallas_call(
         functools.partial(attend_kernel, shape + (len(queries), own is not None, keeping), jobs),
         out_shape=shapes,
-        in_specs=[SMEM] + [VMEM] * (len(queries) + len(more)),
+        in_specs=[SMEM] * len(meta) + [VMEM] * (len(queries) + len(more)),
         out_specs=specs,
         scratch_shapes=scratch,
         compiler_params=pltpu.CompilerParams(vmem_limit_bytes=GRANT),
@@ -258,14 +264,13 @@
             bytes_accessed=len(jobs) * (rows * 6 + keys * 4) * HEAD_SIZE,
             transcendentals=len(jobs) * rows * keys,
         ),
-    )(meta, *queries, *more)
+    )(*meta, *queries, *more)
     return [(out[2 * n], out[2 * n + 1]) for n in range(results)] + list(out[2 * results:])
 
 
 def place_kernel(half, column, me_ref, lists_ref, page_ref, old_ref, out_ref, sem):
     me = me_ref[0]
-    from_below = (me >= half) == (me % 2 == 0)
-    slot = jnp.where(from_below, lists_ref[0, column], lists_ref[1, column])
+    slot = lists_ref[jnp.where(me >= half, me - half, me + half), column]
     copy = pltpu.make_async_copy(page_ref.at[0], out_ref.at[slot], sem)
     copy.start()
     copy.wait()
@@ -417,66 +422,65 @@
     down = [(order[i], order[i - 1]) for i in range(stores)]
     routes = {1: up, -1: down}
 
-    def listed(*arrays):
-        rows = [lax.dynamic_slice(x, (me, cut), (1, HEAD_SIZE)) for x in arrays]
-        return jnp.concatenate(rows).astype(jnp.int32)
-
     def after(values, token):
         return lax.optimization_barrier((values, token))[0]
 
     arrived = shifted(suffix_key_value, "store", half)
     mine = prepare(cut, cap, pages_dev, queries, page_table, prefix_pages, new_slots)
-
-    moving = {
-        (side, sign): lax.ppermute(mine[side], "store", routes[sign])
-        for side in range(2)
-        for sign in routes
+    gathered = [lax.all_gather(x, "store") for x in mine]
+
+    lists = lax.dynamic_slice(gathered[0], (0, me, cut), (stores, 1, HEAD_SIZE))
+    lists = lists.reshape(stores, HEAD_SIZE).astype(jnp.int32)
+    whose = [[order[(order.index(i) - d) % stores] for d in range(stores)] for i in range(stores)]
+    whose = jnp.asarray(whose, jnp.int32)[me]
+    held = kv_pages
+
+    def attended_to(side, distances, token, keeping=False):
+        jobs = [
+            (d % stores, 0, h, side * heads_each + h, n)
+            for n, d in enumerate(distances)
+            for h in range(heads_each)
+        ]
+        got = attend(
+            shape, jobs, [lists, whose], [after(gathered[side], token)], held, None, keeping
+        )
+        parts.update({(d, side): got[n] for n, d in enumerate(distances)})
+        return got
+
+    def attended_own(side, token):
+        jobs = [(0, 0, h, side * heads_each + h, 0) for h in range(heads_each)]
+        mine_list = lax.dynamic_slice(mine[0], (me, cut), (1, HEAD_SIZE)).astype(jnp.int32)
+        got = attend(
+            shape, jobs, [mine_list], [after(mine[side], token)], held, suffix_key_value[0]
+        )
+        parts[0, side] = got[0]
+        return got
+
+    parts = {}
+    far, near = half, half - 1
+    token = attended_to(0, [far, -near, near, 1 - near], [], True)
+    store = token.pop()
+    token = attended_to(0, list(range(near - 1, 0, -1)) + list(range(2 - near, 0)), token)
+    token = attended_to(1, [far, near], token)
+    sent = {("early", 1): packed(parts[near, 1]), ("early", -1): packed(parts[-near, 0])}
+    extra = {
+        ("late", half): lambda t: attended_to(1, [-near, near - 1], t),
+        ("early", near - 1): lambda t: attended_to(1, [1 - near] + list(range(near - 2, 0, -1)), t),
+        ("late", near): lambda t: attended_to(1, list(range(2 - near, 0)), t),
+        ("early", near - 2): lambda t: attended_own(0, t),
+        ("late", near - 1): lambda t: attended_own(1, t),
     }
-    held = kv_pages
-    parts = {}
-    token = []
-    lists_of = {}
-    sent = {}
-    for step in range(1, half):
-        for side in range(2):
-            came = {sign: after(moving[side, sign], token) for sign in routes}
-            for sign in routes:
-                if step < half - 1 or (side == 0) == (sign == 1):
-                    moving[side, sign] = lax.ppermute(came[sign], "store", routes[sign])
-            if side == 0:
-                lists_of[step] = listed(came[1], came[-1])
-            jobs = [(n, n, h, side * heads_each + h, n) for n in range(2) for h in range(heads_each)]
-            keeping = (step, side) == (1, 1)
-            got = attend(shape, jobs, lists_of[step], [came[1], came[-1]], held, None, keeping)
-            if keeping:
-                store = got.pop()
-            parts[step, side], parts[-step, side] = got
-            token = got
-            if (step, side) == (half // 2, 0):
-                token = [got, arrived]
-            if step == half - 1:
-                sign = 1 if side == 1 else -1
-                sent["early", sign] = packed(parts[sign * step, side])
-                token = sent["early", sign]
-    came = after([moving[0, 1], moving[1, -1]], token)
-    jobs = [(0, side, h, side * heads_each + h, side) for side in range(2) for h in range(heads_each)]
-    far = attend(shape, jobs, listed(came[0]), came, held)
-    token = far
 
     back = {1: down, -1: up}
     side_of = {("late", 1): 0, ("late", -1): 1, ("early", 1): 1, ("early", -1): 0}
     flows = {key: lax.ppermute(block, "store", back[key[1]]) for key, block in sent.items()}
-    store = place_page(
-        half, cap + 1, me[None], lists_of[stores // 4], arrived, after(store, token)
-    )
+    store = place_page(half, cap + 1, me[None], lists, arrived, after(store, token))
     turns = [("late", half)]
     for distance in range(half - 1, 0, -1):
         turns += [("early", distance - 1)] * (distance > 1) + [("late", distance)]
     for flow, distance in turns:
         if distance == half:
-            far, ended = lax.optimization_barrier((far, {sign: flows["early", sign] for sign in back}))
-            flows.update({("early", sign): ended[sign] for sign in back})
-            blocks = {sign: packed(far[side_of[flow, sign]]) for sign in back}
+            blocks = {sign: packed(parts[half, side_of[flow, sign]]) for sign in back}
         else:
             came = {sign: flows[flow, sign] for sign in back}
             if distance == 1 and flow == "late":
@@ -491,13 +495,8 @@
         for sign in back:
             flows[flow, sign] = lax.ppermute(blocks[sign], "store", back[sign])
         token = blocks
-        if flow == "early" and distance <= 2:
-            side = 2 - distance
-            jobs = [(0, 0, h, side * heads_each + h, 0) for h in range(heads_each)]
-            parts[0, side], = attend(
-                shape, jobs, listed(mine[0]), [after(mine[side], token)], held, suffix_key_value[0]
-            )
-            token = [blocks, parts[0, side]]
+        if (flow, distance) in extra:
+            token = [blocks, extra[flow, distance](token)]
     rest, late = [None, None], [None, None]
     for sign in (1, -1):
         side = side_of["early", sign]

time: 105 us -> 186 us (1.77)
  waiting for transfers between devices: 27.4 us -> 109 us
  starting transfers between devices: 39 us -> 16.4 us
  between operations: 2.27 us -> 15.6 us
  local copies, waits for them, and re-layouts: 3.95 us -> 10.7 us
    all_gather x0 -> x2, waiting for transfers between devices: none -> 89.2 us  [queries_travel(): gathered = [lax.all_gather(x, 'store') for x in mine]]
    ppermute x14 -> x0, starting transfers between devices: 19.8 us -> none  [the longest x10 14.7 us: queries_travel(): moving[side, sign] = lax.ppermute(came[sign], 'store', routes[sign])]
    ppermute x14 -> x0, waiting for transfers between devices: 10.1 us -> none  [the longest x10 5.59 us: queries_travel(): moving[side, sign] = lax.ppermute(came[sign], 'store', routes[sign])]
    ppermute x12, waiting for transfers between devices: 15.6 us -> 7.06 us  [queries_travel(): flows[flow, sign] = lax.ppermute(blocks[sign], 'store', back[sign])]
    ppermute x1, waiting for transfers between devices: 0.01 us -> 8.14 us  [shifted(): return lax.ppermute(block, axis, route)]
    unnamed x10 -> x18, local copies, waits for them, and re-layouts: 3.89 us -> 9.29 us
    ppermute x2, waiting for transfers between devices: 1.78 us -> 4.42 us  [queries_travel(): lax.ppermute(block, 'store', back[key[1]])]
    pallas_call x9 -> x8, Pallas kernels: 21 us -> 21.1 us  [attend(): pl.pallas_call(functools.partial(attend_kernel, shape + (len(queries), ow...]
  transfers between devices with their start and end apart: 29 -> 17, of which waited for: 16 -> 10; matrix products, arithmetic and copies ran while one was open for 0% -> 1% of each run, Pallas kernels for 28% -> 14%
where the time goes in v7:
time: 186 us
  waiting for transfers between devices  109 us (59%)
  Pallas kernels  32.7 us (18%)
  starting transfers between devices  16.4 us (9%)
  between operations  15.6 us (8%)
  local copies, waits for them, and re-layouts  10.7 us (6%)
    all_gather x2, waiting for transfers between devices, queries_travel(): gathered = [lax.all_gather(x, 'store') for x in mine]  89.2 us
    pallas_call x8, Pallas kernels, attend(): pl.pallas_call(functools.partial(attend_kernel, shape + (len(queries), ow...  21.1 us
    ppermute x12, starting transfers between devices, queries_travel(): flows[flow, sign] = lax.ppermute(blocks[sign], 'store', back[sign])  12.8 us
    pallas_call x17, Pallas kernels, call(): pl.pallas_call(kernel, out_shape=shape, in_specs=[VMEM] * len(args), out_...  9.33 us
    unnamed x18, local copies, waits for them, and re-layouts  9.29 us
    ppermute x1, waiting for transfers between devices, shifted(): return lax.ppermute(block, axis, route)  8.14 us
    ppermute x12, waiting for transfers between devices, queries_travel(): flows[flow, sign] = lax.ppermute(blocks[sign], 'store', back[sign])  7.06 us
    ppermute x2, waiting for transfers between devices, queries_travel(): lax.ppermute(block, 'store', back[key[1]])  4.42 us
  transfers between devices with their start and end apart: 17, of which 10 were waited for; matrix products, arithmetic and copies ran while one was open for 1% of the time, Pallas kernels for 14%

profile of v7, /device:TPU:0, one launch (start us, length us, event | category | flops | bytes accessed | tf_op | source)
XLA Modules:
  0.0 185.6 jit_solution(2683409714420878374)
XLA Ops:
  7.2 0.0 all-gather.5.cloned.1.call-start
  8.5 1.0 copy-done.7
  9.5 0.7 copy-done.8
  10.2 1.0 shard_map.86
  11.2 0.0 all-gather.5.cloned.1.call-update
  11.2 0.0 all-gather.7.cloned.1.call-start
  11.3 0.7 all-gather.7.cloned.1.call-update
  12.0 0.7 dynamic-slice_bitcast_fusion.refs_1_
  12.7 52.1 %all-gather.5.cloned.1.call-done = bf16[512,2176]{1,0:T(8,128)(2,1)} async-done(((bf16[64,2176]{1,0:T(8,128)(2,1)}), bf16[512,2176]{1,0:T(8,128)(2,1)}) %all-gather.5.cloned.1.call-update) | async-done | bytes 2228240 | tf_op jit(solution)/shard_map/all_gather | solution.py:430
  64.8 0.7 constant_dynamic-slice_fusion.1
  65.5 2.2 %copy-done = bf16[32,2,64,512]{3,2,1,0:T(8,128)(2,1)S(1)} copy-done((bf16[32,2,64,512]{3,2,1,0:T(8,128)(2,1)S(1)}, bf16[32,2,64,512]{3,2,1,0:T(8,128)(2,1)}, u32[]{:S(2)}) %copy-start) | copy-done | bytes 4194328
  67.7 1.6 copy-done.4
  69.3 5.3 %shard_map.87 = (f32[2,512,128]{2,1,0:T(8,128)S(1)}, bf16[2,16,128]{2,1,0:T(8,128)(2,1)S(1)}, f32[2,512,128]{2,1,0:T(8,128)S(1)}, bf16[2,16,128]{2,1,0:T(8,128)(...) custom-call(s32[8,128]{1,0:T(8,128)S(1)} %fusion.refs_0_.lists_ref, ...), custom_call_target="tpu_custom_call" | custom-call | flops 2147483648 | bytes 5242880 | tf_op jit(solution)/shard_map/pallas_call | solution.py:255
  74.6 3.0 %shard_map.88 = (f32[2,512,128]{2,1,0:T(8,128)S(1)}, bf16[2,16,128]{2,1,0:T(8,128)(2,1)S(1)}, f32[2,512,128]{2,1,0:T(8,128)S(1)}, bf16[2,16,128]{2,1,0:T(8,128)(...) custom-call(s32[8,128]{1,0:T(8,128)S(1)} %fusion.refs_0_.lists_ref, ...), custom_call_target="tpu_custom_call" | custom-call | flops 1610612736 | bytes 3932160 | tf_op jit(solution)/shard_map/pallas_call | solution.py:255
  77.6 37.1 %all-gather.7.cloned.1.call-done = bf16[512,2048]{1,0:T(8,128)(2,1)} async-done(((bf16[64,2048]{1,0:T(8,128)(2,1)}), bf16[512,2048]{1,0:T(8,128)(2,1)}) %all-gather.7.cloned.1.call-update) | async-done | bytes 2097168 | tf_op jit(solution)/shard_map/all_gather | solution.py:430
  114.7 2.2 %copy-done.1 = bf16[32,2,64,512]{3,2,1,0:T(8,128)(2,1)S(1)} copy-done((bf16[32,2,64,512]{3,2,1,0:T(8,128)(2,1)S(1)}, bf16[32,2,64,512]{3,2,1,0:T(8,128)(2,1)}, u32[]{:S(2)}) %copy-start.1) | copy-done | bytes 4194328
  116.9 1.6 copy-done.3
  118.5 2.3 %shard_map.89 = (f32[2,512,128]{2,1,0:T(8,128)S(1)}, bf16[2,16,128]{2,1,0:T(8,128)(2,1)S(1)}, f32[2,512,128]{2,1,0:T(8,128)S(1)}, bf16[2,16,128]{2,1,0:T(8,128)(2,1)S(1)}) custom-call(s32[8,128]{1,0:T(8,128)S(1)} %fusion.refs_0_.lists_ref, s32[8]{0:T(128)S(1)} %dynamic-slice_bitcast_fusion.refs_1_, bf16[8,64,2048]{2,1,0:T(8,128)(2,1)S(1)} %bitcast.11, ...), custom_call_target="tpu_custom_call" | custom-call | flops 1073741824 | bytes 2621440 | tf_op jit(solution)/shard_map/pallas_call | solution.py:255
  120.8 1.5 collective-permute-start.2
  122.4 0.6 collective-permute-start.3
  123.0 1.5 collective-permute-start
  124.6 0.5 collective-permute-start.1
  125.1 2.3 %shard_map.94 = (f32[2,512,128]{2,1,0:T(8,128)S(1)}, bf16[2,16,128]{2,1,0:T(8,128)(2,1)S(1)}, f32[2,512,128]{2,1,0:T(8,128)S(1)}, bf16[2,16,128]{2,1,0:T(8,128)(2,1)S(1)}) custom-call(s32[8,128]{1,0:T(8,128)S(1)} %fusion.refs_0_.lists_ref, s32[8]{0:T(128)S(1)} %dynamic-slice_bitcast_fusion.refs_1_, bf16[8,64,2048]{2,1,0:T(8,128)(2,1)S(1)} %bitcast.12, ...), custom_call_target="tpu_custom_call" | custom-call | flops 1073741824 | bytes 2621440 | tf_op jit(solution)/shard_map/pallas_call | solution.py:255
  127.4 2.9 %collective-permute-done.2.in_ref = bf16[2,528,128]{2,1,0:T(8,128)(2,1)S(1)} collective-permute-done((bf16[2,528,128]{2,1,0:T(8,128)(2,1)S(1)}, bf16[2,528,128]{2,1,0:T(8,128)(2,1)S(1)}, u32[]{:S(2)}, u32[]{:S(2)}) %collective-permute-start.2) | collective-permute-done | bytes 270368 | tf_op jit(solution)/shard_map/ppermute | solution.py:476
  130.3 1.6 collective-permute-done.3.in_ref
  131.8 0.6 shard_map.95
  132.5 1.0 collective-permute-start.6
  133.4 0.6 shard_map.96
  134.0 1.4 collective-permute-start.7
  135.4 2.3 %shard_map.97 = (f32[2,512,128]{2,1,0:T(8,128)S(1)}, bf16[2,16,128]{2,1,0:T(8,128)(2,1)S(1)}, f32[2,512,128]{2,1,0:T(8,128)S(1)}, bf16[2,16,128]{2,1,0:T(8,128)(2,1)S(1)}) custom-call(s32[8,128]{1,0:T(8,128)S(1)} %fusion.refs_0_.lists_ref, s32[8]{0:T(128)S(1)} %dynamic-slice_bitcast_fusion.refs_1_, bf16[8,64,2048]{2,1,0:T(8,128)(2,1)S(1)} %bitcast.13, ...), custom_call_target="tpu_custom_call" | custom-call | flops 1073741824 | bytes 2621440 | tf_op jit(solution)/shard_map/pallas_call | solution.py:255
  137.7 0.0 collective-permute-done.1.in_ref
  137.7 0.6 shard_map.98
  138.4 1.0 collective-permute-start.4
  139.3 0.6 shard_map.99
  139.9 1.2 collective-permute-start.5
  141.1 0.7 fusion.1.refs_0_
  141.8 1.6 shard_map.100
  143.4 0.3 collective-permute-done.7.in_ref
  143.7 0.6 shard_map.101
  144.3 0.6 shard_map.102
  145.0 2.2 %shard_map.103 = (f32[2,512,128]{2,1,0:T(8,128)S(1)}, bf16[2,16,128]{2,1,0:T(8,128)(2,1)S(1)}) custom-call(s32[1,128]{1,0:T(1,128)S(1)} %fusion.1.refs_0_, bf16[64,2176]{1,0:T(8,128)(2,1)} %get-tuple-element.106.refs_1_, bf16[2,64,512]{2,1,0:T(8,128)(2,1)S(1)} %bitcast.18, bf16[32,2,64,512]{3,2,1,0:T(8,128)(2,1)S(1)} %copy-done.2), custom_call_target="tpu_custom_call" | custom-call | flops 536870912 | bytes 1310720 | tf_op jit(solution)/shard_map/pallas_call | solution.py:255
  147.2 0.0 collective-permute-done.4.in_ref
  147.2 0.0 collective-permute-done.5.in_ref
  147.2 0.6 shard_map.104
  147.8 1.0 collective-permute-start.8
  148.8 0.6 shard_map.105
  149.4 1.1 collective-permute-start.9
  150.6 1.0 collective-permute-start.10
  151.5 1.1 collective-permute-start.11
  152.6 2.2 %shard_map.106 = (f32[2,512,128]{2,1,0:T(8,128)S(1)}, bf16[2,16,128]{2,1,0:T(8,128)(2,1)S(1)}) custom-call(s32[1,128]{1,0:T(1,128)S(1)} %fusion.1.refs_0_, bf16[64,2048]{1,0:T(8,128)(2,1)} %get-tuple-element.113.refs_1_, bf16[2,64,512]{2,1,0:T(8,128)(2,1)S(1)} %bitcast.19, bf16[32,2,64,512]{3,2,1,0:T(8,128)(2,1)S(1)} %copy-done.2), custom_call_target="tpu_custom_call" | custom-call | flops 536870912 | bytes 1310720 | tf_op jit(solution)/shard_map/pallas_call | solution.py:255
  154.8 1.6 collective-permute-done.8.in_ref
  156.4 2.3 %collective-permute-done.9.in_ref = bf16[2,528,128]{2,1,0:T(8,128)(2,1)S(1)} collective-permute-done((bf16[2,528,128]{2,1,0:T(8,128)(2,1)S(1)}, bf16[2,528,128]{2,1,0:T(8,128)(2,1)S(1)}, u32[]{:S(2)}, u32[]{:S(2)}) %collective-permute-start.9) | collective-permute-done | bytes 270368 | tf_op jit(solution)/shard_map/ppermute | solution.py:496
  158.6 0.6 collective-permute-done.10.in_ref
  159.3 2.3 %collective-permute-done.11.in_ref = bf16[2,528,128]{2,1,0:T(8,128)(2,1)S(1)} collective-permute-done((bf16[2,528,128]{2,1,0:T(8,128)(2,1)S(1)}, bf16[2,528,128]{2,1,0:T(8,128)(2,1)S(1)}, u32[]{:S(2)}, u32[]{:S(2)}) %collective-permute-start.11) | collective-permute-done | bytes 270368 | tf_op jit(solution)/shard_map/ppermute | solution.py:496
  161.5 0.6 shard_map.107
  162.2 0.3 collective-permute-start.12
  162.5 0.6 shard_map.108
  163.1 1.8 collective-permute-start.13
  164.9 1.4 collective-permute-start.14
  166.3 8.1 %collective-permute-done.14.page_ref = bf16[1,2,64,512]{3,2,1,0:T(8,128)(2,1)S(1)} collective-permute-done((bf16[1,2,64,512]{3,2,1,0:T(8,128)(2,1)S(1)}, bf16[1,2,64,512]{3,2,1,0:T(8,128)(2,1)S(1)}, u32[]{:S(2)}, u32[]{:S(2)}) %collective-permute-start.14) | collective-permute-done | bytes 131104 | tf_op jit(solution)/shard_map/ppermute | solution.py:25
  174.5 1.3 shard_map.112
  175.7 0.6 shard_map.109
  176.4 0.6 shard_map.110
  177.0 1.7 shard_map.111
  (21 shorter events, 0.2 us)
Async XLA Ops:
  7.2 57.6 %all-gather.5.cloned.1.call-start = ((), (), s32[]{:S(2)}) async-start(), calls=%async_computation | async-start | bytes 2506752 | tf_op jit(solution)/shard_map/all_gather | solution.py:430
  8.5 1.0 copy-start.7
  9.5 0.7 copy-start.8
  11.2 103.5 %all-gather.7.cloned.1.call-start = ((), (), s32[]{:S(2)}) async-start(), calls=%async_computation.1 | async-start | bytes 2359296 | tf_op jit(solution)/shard_map/all_gather | solution.py:430
  65.5 2.2 %copy-start = (bf16[32,2,64,512]{3,2,1,0:T(8,128)(2,1)S(1)}, bf16[32,2,64,512]{3,2,1,0:T(8,128)(2,1)}, u32[]{:S(2)}) copy-start(bf16[32,2,64,512]{3,2,1,0:T(8,128)(2,1)} %refs_3_.15) | copy-start | bytes 12582916
  67.7 1.6 copy-start.4
  69.3 5.3 %copy-start.5 = (bf16[512,2176]{1,0:T(8,128)(2,1)S(1)}, bf16[512,2176]{1,0:T(8,128)(2,1)}, u32[]{:S(2)}) copy-start(bf16[512,2176]{1,0:T(8,128)(2,1)} %all-gather.5.cloned.1.call-done) | copy-start | bytes 6684676
  114.7 2.2 %copy-start.1 = (bf16[32,2,64,512]{3,2,1,0:T(8,128)(2,1)S(1)}, bf16[32,2,64,512]{3,2,1,0:T(8,128)(2,1)}, u32[]{:S(2)}) copy-start(bf16[32,2,64,512]{3,2,1,0:T(8,128)(2,1)} %refs_3_.15) | copy-start | bytes 12582916
  116.9 1.6 copy-start.3
  118.5 6.6 %copy-start.2 = (bf16[32,2,64,512]{3,2,1,0:T(8,128)(2,1)S(1)}, bf16[32,2,64,512]{3,2,1,0:T(8,128)(2,1)}, u32[]{:S(2)}) copy-start(bf16[32,2,64,512]{3,2,1,0:T(8,128)(2,1)} %refs_3_.15) | copy-start | bytes 12582916
  120.8 9.5 %collective-permute-start.2 = (bf16[2,528,128]{2,1,0:T(8,128)(2,1)S(1)}, bf16[2,528,128]{2,1,0:T(8,128)(2,1)S(1)}, u32[]{:S(2)}, u32[]{:S(2)}) collective-permute-start(bf16[2,528,128]{2,1,0:T(8,128)(2,1)S(1)} %shard_map.92), channel_id=1, source_target_pairs={{0,4},{4,8},{8,12},{12,14},{14,10},{10,6},{6,2},{2,0},{1,5},{5,9},... | collective-permute-start | bytes 811016 | tf_op jit(solution)/shard_map/ppermute | solution.py:476
  122.4 9.5 %collective-permute-start.3 = (bf16[2,528,128]{2,1,0:T(8,128)(2,1)S(1)}, bf16[2,528,128]{2,1,0:T(8,128)(2,1)S(1)}, u32[]{:S(2)}, u32[]{:S(2)}) collective-permute-start(bf16[2,528,128]{2,1,0:T(8,128)(2,1)S(1)} %shard_map.93), channel_id=1, source_target_pairs={{0,2},{4,0},{8,4},{12,8},{14,12},{10,14},{6,10},{2,6},{1,3},{5,1},... | collective-permute-start | bytes 811016 | tf_op jit(solution)/shard_map/ppermute | solution.py:476
  123.0 14.7 %collective-permute-start = (bf16[2,528,128]{2,1,0:T(8,128)(2,1)S(1)}, bf16[2,528,128]{2,1,0:T(8,128)(2,1)S(1)}, u32[]{:S(2)}, u32[]{:S(2)}) collective-permute-start(bf16[2,528,128]{2,1,0:T(8,128)(2,1)S(1)} %shard_map.90), channel_id=1, source_target_pairs={{0,4},{4,8},{8,12},{12,14},{14,10},{10,6},{6,2},{2,0},{1,5},{5,9},... | collective-permute-start | bytes 811016 | tf_op jit(solution)/shard_map/ppermute | solution.py:496
  124.6 13.2 %collective-permute-start.1 = (bf16[2,528,128]{2,1,0:T(8,128)(2,1)S(1)}, bf16[2,528,128]{2,1,0:T(8,128)(2,1)S(1)}, u32[]{:S(2)}, u32[]{:S(2)}) collective-permute-start(bf16[2,528,128]{2,1,0:T(8,128)(2,1)S(1)} %shard_map.91), channel_id=1, source_target_pairs={{0,2},{4,0},{8,4},{12,8},{14,12},{10,14},{6,10},{2,6},{1,3},{5,1},... | collective-permute-start | bytes 811016 | tf_op jit(solution)/shard_map/ppermute | solution.py:496
  132.5 10.9 %collective-permute-start.6 = (bf16[2,528,128]{2,1,0:T(8,128)(2,1)S(1)}, bf16[2,528,128]{2,1,0:T(8,128)(2,1)S(1)}, u32[]{:S(2)}, u32[]{:S(2)}) collective-permute-start(bf16[2,528,128]{2,1,0:T(8,128)(2,1)S(1)} %shard_map.95), channel_id=1, source_target_pairs={{0,4},{4,8},{8,12},{12,14},{14,10},{10,6},{6,2},{2,0},{1,5},{5,9},... | collective-permute-start | bytes 811016 | tf_op jit(solution)/shard_map/ppermute | solution.py:496
  134.0 9.7 %collective-permute-start.7 = (bf16[2,528,128]{2,1,0:T(8,128)(2,1)S(1)}, bf16[2,528,128]{2,1,0:T(8,128)(2,1)S(1)}, u32[]{:S(2)}, u32[]{:S(2)}) collective-permute-start(bf16[2,528,128]{2,1,0:T(8,128)(2,1)S(1)} %shard_map.96), channel_id=1, source_target_pairs={{0,2},{4,0},{8,4},{12,8},{14,12},{10,14},{6,10},{2,6},{1,3},{5,1},... | collective-permute-start | bytes 811016 | tf_op jit(solution)/shard_map/ppermute | solution.py:496
  138.4 8.8 %collective-permute-start.4 = (bf16[2,528,128]{2,1,0:T(8,128)(2,1)S(1)}, bf16[2,528,128]{2,1,0:T(8,128)(2,1)S(1)}, u32[]{:S(2)}, u32[]{:S(2)}) collective-permute-start(bf16[2,528,128]{2,1,0:T(8,128)(2,1)S(1)} %shard_map.98), channel_id=1, source_target_pairs={{0,4},{4,8},{8,12},{12,14},{14,10},{10,6},{6,2},{2,0},{1,5},{5,9},... | collective-permute-start | bytes 811016 | tf_op jit(solution)/shard_map/ppermute | solution.py:496
  139.9 7.2 %collective-permute-start.5 = (bf16[2,528,128]{2,1,0:T(8,128)(2,1)S(1)}, bf16[2,528,128]{2,1,0:T(8,128)(2,1)S(1)}, u32[]{:S(2)}, u32[]{:S(2)}) collective-permute-start(bf16[2,528,128]{2,1,0:T(8,128)(2,1)S(1)} %shard_map.99), channel_id=1, source_target_pairs={{0,2},{4,0},{8,4},{12,8},{14,12},{10,14},{6,10},{2,6},{1,3},{5,1},... | collective-permute-start | bytes 811016 | tf_op jit(solution)/shard_map/ppermute | solution.py:496
  141.8 3.1 %copy-start.6 = (bf16[1,2,64,512]{3,2,1,0:T(8,128)(2,1)S(1)}, bf16[1,2,64,512]{3,2,1,0:T(8,128)(2,1)}, u32[]{:S(2)}) copy-start(bf16[1,2,64,512]{3,2,1,0:T(8,128)(2,1)} %param.8) | copy-start | bytes 393220
  147.8 8.6 %collective-permute-start.8 = (bf16[2,528,128]{2,1,0:T(8,128)(2,1)S(1)}, bf16[2,528,128]{2,1,0:T(8,128)(2,1)S(1)}, u32[]{:S(2)}, u32[]{:S(2)}) collective-permute-start(bf16[2,528,128]{2,1,0:T(8,128)(2,1)S(1)} %shard_map.104), channel_id=1, source_target_pairs={{0,4},{4,8},{8,12},{12,14},{14,10},{10,6},{6,2},{2,0},{1,5},{5,9},... | collective-permute-start | bytes 811016 | tf_op jit(solution)/shard_map/ppermute | solution.py:496
  149.4 9.2 %collective-permute-start.9 = (bf16[2,528,128]{2,1,0:T(8,128)(2,1)S(1)}, bf16[2,528,128]{2,1,0:T(8,128)(2,1)S(1)}, u32[]{:S(2)}, u32[]{:S(2)}) collective-permute-start(bf16[2,528,128]{2,1,0:T(8,128)(2,1)S(1)} %shard_map.105), channel_id=1, source_target_pairs={{0,2},{4,0},{8,4},{12,8},{14,12},{10,14},{6,10},{2,6},{1,3},{5,1},... | collective-permute-start | bytes 811016 | tf_op jit(solution)/shard_map/ppermute | solution.py:496
  150.6 8.7 %collective-permute-start.10 = (bf16[2,528,128]{2,1,0:T(8,128)(2,1)S(1)}, bf16[2,528,128]{2,1,0:T(8,128)(2,1)S(1)}, u32[]{:S(2)}, u32[]{:S(2)}) collective-permute-start(bf16[2,528,128]{2,1,0:T(8,128)(2,1)S(1)} %shard_map.101), channel_id=1, source_target_pairs={{0,4},{4,8},{8,12},{12,14},{14,10},{10,6},{6,2},{2,0},{1,5},{5,9},... | collective-permute-start | bytes 811016 | tf_op jit(solution)/shard_map/ppermute | solution.py:496
  151.5 10.0 %collective-permute-start.11 = (bf16[2,528,128]{2,1,0:T(8,128)(2,1)S(1)}, bf16[2,528,128]{2,1,0:T(8,128)(2,1)S(1)}, u32[]{:S(2)}, u32[]{:S(2)}) collective-permute-start(bf16[2,528,128]{2,1,0:T(8,128)(2,1)S(1)} %shard_map.102), channel_id=1, source_target_pairs={{0,2},{4,0},{8,4},{12,8},{14,12},{10,14},{6,10},{2,6},{1,3},{5,1},... | collective-permute-start | bytes 811016 | tf_op jit(solution)/shard_map/ppermute | solution.py:496
  162.2 14.9 %collective-permute-start.12 = (bf16[2,528,128]{2,1,0:T(8,128)(2,1)S(1)}, bf16[2,528,128]{2,1,0:T(8,128)(2,1)S(1)}, u32[]{:S(2)}, u32[]{:S(2)}) collective-permute-start(bf16[2,528,128]{2,1,0:T(8,128)(2,1)S(1)} %shard_map.107), channel_id=1, source_target_pairs={{0,2},{4,0},{8,4},{12,8},{14,12},{10,14},{6,10},{2,6},{1,3},{5,1},... | collective-permute-start | bytes 811016 | tf_op jit(solution)/shard_map/ppermute | solution.py:496
  163.1 13.9 %collective-permute-start.13 = (bf16[2,528,128]{2,1,0:T(8,128)(2,1)S(1)}, bf16[2,528,128]{2,1,0:T(8,128)(2,1)S(1)}, u32[]{:S(2)}, u32[]{:S(2)}) collective-permute-start(bf16[2,528,128]{2,1,0:T(8,128)(2,1)S(1)} %shard_map.108), channel_id=1, source_target_pairs={{0,4},{4,8},{8,12},{12,14},{14,10},{10,6},{6,2},{2,0},{1,5},{5,9},... | collective-permute-start | bytes 811016 | tf_op jit(solution)/shard_map/ppermute | solution.py:496
  164.9 9.5 %collective-permute-start.14 = (bf16[1,2,64,512]{3,2,1,0:T(8,128)(2,1)S(1)}, bf16[1,2,64,512]{3,2,1,0:T(8,128)(2,1)S(1)}, u32[]{:S(2)}, u32[]{:S(2)}) collective-permute-start(bf16[1,2,64,512]{3,2,1,0:T(8,128)(2,1)S(1)} %copy-done.6), channel_id=1, source_target_pairs={{8,0},{10,2},{12,4},{14,6},{0,8},{2,10},{4,12},{6,14},{9,1},{11,3}... | collective-permute-start | bytes 393224 | tf_op jit(solution)/shard_map/ppermute | solution.py:25
Sparse Core Ops, SparseCore 0:
  11.3 53.3 all-gather.4
  66.9 47.7 all-gather.6

commit v8 on v6

--- a/solution.py
+++ b/solution.py
@@ -424,7 +424,6 @@
     def after(values, token):
         return lax.optimization_barrier((values, token))[0]
 
-    arrived = shifted(suffix_key_value, "store", half)
     mine = prepare(cut, cap, pages_dev, queries, page_table, prefix_pages, new_slots)
 
     moving = {
@@ -446,19 +445,16 @@
             if side == 0:
                 lists_of[step] = listed(came[1], came[-1])
             jobs = [(n, n, h, side * heads_each + h, n) for n in range(2) for h in range(heads_each)]
-            keeping = (step, side) == (1, 1)
-            got = attend(shape, jobs, lists_of[step], [came[1], came[-1]], held, None, keeping)
-            if keeping:
-                store = got.pop()
+            got = attend(shape, jobs, lists_of[step], [came[1], came[-1]], held)
             parts[step, side], parts[-step, side] = got
             token = got
-            if (step, side) == (half // 2, 0):
-                token = [got, arrived]
+            if (step, side) == (half - 2, 1):
+                arrived = shifted(after(suffix_key_value, token), "store", half)
             if step == half - 1:
                 sign = 1 if side == 1 else -1
                 sent["early", sign] = packed(parts[sign * step, side])
                 token = sent["early", sign]
-    came = after([moving[0, 1], moving[1, -1]], token)
+    came = after([moving[0, 1], moving[1, -1]], [token, arrived])
     jobs = [(0, side, h, side * heads_each + h, side) for side in range(2) for h in range(heads_each)]
     far = attend(shape, jobs, listed(came[0]), came, held)
     token = far
@@ -466,9 +462,6 @@
     back = {1: down, -1: up}
     side_of = {("late", 1): 0, ("late", -1): 1, ("early", 1): 1, ("early", -1): 0}
     flows = {key: lax.ppermute(block, "store", back[key[1]]) for key, block in sent.items()}
-    store = place_page(
-        half, cap + 1, me[None], lists_of[stores // 4], arrived, after(store, token)
-    )
     turns = [("late", half)]
     for distance in range(half - 1, 0, -1):
         turns += [("early", distance - 1)] * (distance > 1) + [("late", distance)]
@@ -494,10 +487,21 @@
         if flow == "early" and distance <= 2:
             side = 2 - distance
             jobs = [(0, 0, h, side * heads_each + h, 0) for h in range(heads_each)]
-            parts[0, side], = attend(
-                shape, jobs, listed(mine[0]), [after(mine[side], token)], held, suffix_key_value[0]
+            parts[0, side], *kept_pages = attend(
+                shape,
+                jobs,
+                listed(mine[0]),
+                [after(mine[side], token)],
+                held,
+                suffix_key_value[0],
+                side == 0,
             )
             token = [blocks, parts[0, side]]
+            if kept_pages:
+                store, = kept_pages
+    store = place_page(
+        half, cap + 1, me[None], lists_of[stores // 4], arrived, after(store, token)
+    )
     rest, late = [None, None], [None, None]
     for sign in (1, -1):
         side = side_of["early", sign]

time: 105 us -> 104 us (level)
  starting transfers between devices: 39 us -> 32.9 us
  waiting for transfers between devices: 27.4 us -> 32.6 us
    ppermute x1, waiting for transfers between devices: 0.01 us -> 8.42 us  [shifted(): return lax.ppermute(block, axis, route)]
    ppermute x10, starting transfers between devices: 14.7 us -> 10.2 us  [queries_travel(): moving[side, sign] = lax.ppermute(came[sign], 'store', routes[sign])]
    ppermute x12, waiting for transfers between devices: 15.6 us -> 12.9 us  [queries_travel(): flows[flow, sign] = lax.ppermute(blocks[sign], 'store', back[sign])]
    ppermute x4, waiting for transfers between devices: 4.47 us -> 6.53 us  [queries_travel(): lax.ppermute(mine[side], 'store', routes[sign])]
    ppermute x2, waiting for transfers between devices: 1.78 us -> 0.01 us  [queries_travel(): lax.ppermute(block, 'store', back[key[1]])]
    ppermute x2, starting transfers between devices: 3.42 us -> 2.08 us  [queries_travel(): lax.ppermute(block, 'store', back[key[1]])]
where the time goes in v8:
time: 104 us; the launch traced here: 103 us
  starting transfers between devices  32.9 us (32%)
  waiting for transfers between devices  32.6 us (31%)
  Pallas kernels  31.7 us (30%)
  local copies, waits for them, and re-layouts  3.93 us (4%)
  between operations  2.22 us (2%)
    pallas_call x9, Pallas kernels, attend(): pl.pallas_call(functools.partial(attend_kernel, shape + (len(queries), ow...  20.8 us
    ppermute x12, waiting for transfers between devices, queries_travel(): flows[flow, sign] = lax.ppermute(blocks[sign], 'store', back[sign])  12.9 us
    ppermute x12, starting transfers between devices, queries_travel(): flows[flow, sign] = lax.ppermute(blocks[sign], 'store', back[sign])  12.8 us
    ppermute x10, starting transfers between devices, queries_travel(): moving[side, sign] = lax.ppermute(came[sign], 'store', routes[sign])  10.2 us
    pallas_call x17, Pallas kernels, call(): pl.pallas_call(kernel, out_shape=shape, in_specs=[VMEM] * len(args), out_...  9.39 us
    ppermute x1, waiting for transfers between devices, shifted(): return lax.ppermute(block, axis, route)  8.42 us
    ppermute x4, waiting for transfers between devices, queries_travel(): lax.ppermute(mine[side], 'store', routes[sign])  6.53 us
    ppermute x4, starting transfers between devices, queries_travel(): lax.ppermute(mine[side], 'store', routes[sign])  5.05 us
  transfers between devices with their start and end apart: 29, of which 16 were waited for; matrix products, arithmetic and copies ran while one was open for 0% of the time, Pallas kernels for 28%

profile of v8, /device:TPU:0, one launch (start us, length us, event | category | flops | bytes accessed | tf_op | source)
XLA Modules:
  0.0 103.5 jit_solution(11428312400998665571)
XLA Ops:
  1.9 1.0 copy-done.3
  3.0 0.7 copy-done.4
  3.9 3.0 %collective-permute-start = (bf16[64,2176]{1,0:T(8,128)(2,1)S(1)}, bf16[64,2176]{1,0:T(8,128)(2,1)S(1)}, u32[]{:S(2)}, u32[]{:S(2)}) collective-permute-start(bf16[64,2176]{1,0:T(8,128)(2,1)S(1)} %get-tuple-element.126.refs_1_), channel_id=1, source_target_pairs={{0,4},{4,8},{8,12},{12,14},{14,10},{10,6},{6,2},{2,0},{1,5},{5,9},... | collective-permute-start | bytes 835592 | tf_op jit(solution)/shard_map/ppermute | solution.py:430
  6.9 2.0 %collective-permute-start.3 = (bf16[64,2048]{1,0:T(8,128)(2,1)S(1)}, bf16[64,2048]{1,0:T(8,128)(2,1)S(1)}, u32[]{:S(2)}, u32[]{:S(2)}) collective-permute-start(bf16[64,2048]{1,0:T(8,128)(2,1)S(1)} %get-tuple-element.137.refs_1_), channel_id=1, source_target_pairs={{0,4},{4,8},{8,12},{12,14},{14,10},{10,6},{6,2},{2,0},{1,5},{5,9},... | collective-permute-start | bytes 786440 | tf_op jit(solution)/shard_map/ppermute | solution.py:430
  9.0 5.4 %collective-permute-done.refs_1_ = bf16[64,2176]{1,0:T(8,128)(2,1)S(1)} collective-permute-done((bf16[64,2176]{1,0:T(8,128)(2,1)S(1)}, bf16[64,2176]{1,0:T(8,128)(2,1)S(1)}, u32[]{:S(2)}, u32[]{:S(2)}) %collective-permute-start) | collective-permute-done | bytes 278560 | tf_op jit(solution)/shard_map/ppermute | solution.py:430
  14.4 2.1 %collective-permute-start.1 = (bf16[64,2176]{1,0:T(8,128)(2,1)S(1)}, bf16[64,2176]{1,0:T(8,128)(2,1)S(1)}, u32[]{:S(2)}, u32[]{:S(2)}) collective-permute-start(bf16[64,2176]{1,0:T(8,128)(2,1)S(1)} %collective-permute-done.refs_1_), channel_id=1, source_target_pairs={{0,4},{4,8},{8,12},{12,14},{14,10},{10,6},{6,2},{2,0},{1,5},{5,9},... | collective-permute-start | bytes 835592 | tf_op jit(solution)/shard_map/ppermute | solution.py:444
  16.6 2.2 %copy-done = bf16[32,2,64,512]{3,2,1,0:T(8,128)(2,1)S(1)} copy-done((bf16[32,2,64,512]{3,2,1,0:T(8,128)(2,1)S(1)}, bf16[32,2,64,512]{3,2,1,0:T(8,128)(2,1)}, u32[]{:S(2)}) %copy-start) | copy-done | bytes 4194328
  18.8 2.2 %shard_map.78 = (f32[2,512,128]{2,1,0:T(8,128)S(1)}, bf16[2,16,128]{2,1,0:T(8,128)(2,1)S(1)}, f32[2,512,128]{2,1,0:T(8,128)S(1)}, bf16[2,16,128]{2,1,0:T(8,128)(2,1)S(1)}) custom-call(s32[2,128]{1,0:T(2,128)S(1)} %maximum_convert_fusion.refs_0_, bf16[64,2176]{1,0:T(8,128)(2,1)S(1)} %collective-permute-done.refs_1_, ...), custom_call_target="tpu_custom_call" | custom-call | flops 1073741824 | bytes 2621440 | tf_op jit(solution)/shard_map/pallas_call | solution.py:249
  21.0 1.1 %collective-permute-done.4.refs_2_ = bf16[64,2048]{1,0:T(8,128)(2,1)S(1)} collective-permute-done((bf16[64,2048]{1,0:T(8,128)(2,1)S(1)}, bf16[64,2048]{1,0:T(8,128)(2,1)S(1)}, u32[]{:S(2)}, u32[]{:S(2)}) %collective-permute-start.4) | collective-permute-done | bytes 262176 | tf_op jit(solution)/shard_map/ppermute | solution.py:430
  22.1 1.6 %collective-permute-start.7 = (bf16[64,2048]{1,0:T(8,128)(2,1)S(1)}, bf16[64,2048]{1,0:T(8,128)(2,1)S(1)}, u32[]{:S(2)}, u32[]{:S(2)}) collective-permute-start(bf16[64,2048]{1,0:T(8,128)(2,1)S(1)} %collective-permute-done.3.refs_1_), channel_id=1, source_target_pairs={{0,4},{4,8},{8,12},{12,14},{14,10},{10,6},{6,2},{2,0},{1,5},{5,9},... | collective-permute-start | bytes 786440 | tf_op jit(solution)/shard_map/ppermute | solution.py:444
  23.7 0.4 collective-permute-start.8
  24.2 2.2 %shard_map.79 = (f32[2,512,128]{2,1,0:T(8,128)S(1)}, bf16[2,16,128]{2,1,0:T(8,128)(2,1)S(1)}, f32[2,512,128]{2,1,0:T(8,128)S(1)}, bf16[2,16,128]{2,1,0:T(8,128)(2,1)S(1)}) custom-call(s32[2,128]{1,0:T(2,128)S(1)} %maximum_convert_fusion.refs_0_, bf16[64,2048]{1,0:T(8,128)(2,1)S(1)} %collective-permute-done.3.refs_1_, ...), custom_call_target="tpu_custom_call" | custom-call | flops 1073741824 | bytes 2621440 | tf_op jit(solution)/shard_map/pallas_call | solution.py:249
  26.4 1.6 %collective-permute-start.5 = (bf16[64,2176]{1,0:T(8,128)(2,1)S(1)}, bf16[64,2176]{1,0:T(8,128)(2,1)S(1)}, u32[]{:S(2)}, u32[]{:S(2)}) collective-permute-start(bf16[64,2176]{1,0:T(8,128)(2,1)S(1)} %collective-permute-done.1.refs_1_), channel_id=1, source_target_pairs={{0,4},{4,8},{8,12},{12,14},{14,10},{10,6},{6,2},{2,0},{1,5},{5,9},... | collective-permute-start | bytes 835592 | tf_op jit(solution)/shard_map/ppermute | solution.py:444
  28.1 0.5 collective-permute-start.11
  28.6 2.2 %shard_map.80 = (f32[2,512,128]{2,1,0:T(8,128)S(1)}, bf16[2,16,128]{2,1,0:T(8,128)(2,1)S(1)}, f32[2,512,128]{2,1,0:T(8,128)S(1)}, bf16[2,16,128]{2,1,0:T(8,128)(2,1)S(1)}) custom-call(s32[2,128]{1,0:T(2,128)S(1)} %maximum_convert_fusion.1.refs_0_.lists_ref, bf16[64,2176]{1,0:T(8,128)(2,1)S(1)} %collective-permute-done.1.refs_1_, ...), custom_call_target="tpu_custom_call" | custom-call | flops 1073741824 | bytes 2621440 | tf_op jit(solution)/shard_map/pallas_call | solution.py:249
  30.8 0.7 collective-permute-done.7.refs_1_
  31.6 2.2 %collective-permute-done.8.refs_2_ = bf16[64,2048]{1,0:T(8,128)(2,1)S(1)} collective-permute-done((bf16[64,2048]{1,0:T(8,128)(2,1)S(1)}, bf16[64,2048]{1,0:T(8,128)(2,1)S(1)}, u32[]{:S(2)}, u32[]{:S(2)}) %collective-permute-start.8) | collective-permute-done | bytes 262176 | tf_op jit(solution)/shard_map/ppermute | solution.py:444
  33.7 2.0 %collective-permute-start.13 = (bf16[64,2048]{1,0:T(8,128)(2,1)S(1)}, bf16[64,2048]{1,0:T(8,128)(2,1)S(1)}, u32[]{:S(2)}, u32[]{:S(2)}) collective-permute-start(bf16[64,2048]{1,0:T(8,128)(2,1)S(1)} %collective-permute-done.7.refs_1_), channel_id=1, source_target_pairs={{0,4},{4,8},{8,12},{12,14},{14,10},{10,6},{6,2},{2,0},{1,5},{5,9},... | collective-permute-start | bytes 786440 | tf_op jit(solution)/shard_map/ppermute | solution.py:444
  35.7 2.3 %shard_map.81 = (f32[2,512,128]{2,1,0:T(8,128)S(1)}, bf16[2,16,128]{2,1,0:T(8,128)(2,1)S(1)}, f32[2,512,128]{2,1,0:T(8,128)S(1)}, bf16[2,16,128]{2,1,0:T(8,128)(2,1)S(1)}) custom-call(s32[2,128]{1,0:T(2,128)S(1)} %maximum_convert_fusion.1.refs_0_.lists_ref, bf16[64,2048]{1,0:T(8,128)(2,1)S(1)} %collective-permute-done.7.refs_1_, ...), custom_call_target="tpu_custom_call" | custom-call | flops 1073741824 | bytes 2621440 | tf_op jit(solution)/shard_map/pallas_call | solution.py:249
  38.0 1.6 %collective-permute-start.9 = (bf16[64,2176]{1,0:T(8,128)(2,1)S(1)}, bf16[64,2176]{1,0:T(8,128)(2,1)S(1)}, u32[]{:S(2)}, u32[]{:S(2)}) collective-permute-start(bf16[64,2176]{1,0:T(8,128)(2,1)S(1)} %collective-permute-done.5.refs_1_), channel_id=1, source_target_pairs={{0,4},{4,8},{8,12},{12,14},{14,10},{10,6},{6,2},{2,0},{1,5},{5,9},... | collective-permute-start | bytes 835592 | tf_op jit(solution)/shard_map/ppermute | solution.py:444
  39.7 2.2 %shard_map.82 = (f32[2,512,128]{2,1,0:T(8,128)S(1)}, bf16[2,16,128]{2,1,0:T(8,128)(2,1)S(1)}, f32[2,512,128]{2,1,0:T(8,128)S(1)}, bf16[2,16,128]{2,1,0:T(8,128)(2,1)S(1)}) custom-call(s32[2,128]{1,0:T(2,128)S(1)} %maximum_convert_fusion.2.refs_0_, bf16[64,2176]{1,0:T(8,128)(2,1)S(1)} %collective-permute-done.5.refs_1_, ...), custom_call_target="tpu_custom_call" | custom-call | flops 1073741824 | bytes 2621440 | tf_op jit(solution)/shard_map/pallas_call | solution.py:249
  42.0 1.8 %collective-permute-done.10.refs_2_ = bf16[64,2048]{1,0:T(8,128)(2,1)S(1)} collective-permute-done((bf16[64,2048]{1,0:T(8,128)(2,1)S(1)}, bf16[64,2048]{1,0:T(8,128)(2,1)S(1)}, u32[]{:S(2)}, u32[]{:S(2)}) %collective-permute-start.10) | collective-permute-done | bytes 262176 | tf_op jit(solution)/shard_map/ppermute | solution.py:444
  44.1 2.8 %collective-permute-start.14 = (bf16[1,2,64,512]{3,2,1,0:T(8,128)(2,1)S(1)}, bf16[1,2,64,512]{3,2,1,0:T(8,128)(2,1)S(1)}, u32[]{:S(2)}, u32[]{:S(2)}) collective-permute-start(bf16[1,2,64,512]{3,2,1,0:T(8,128)(2,1)S(1)} %copy-done.2), channel_id=1, source_target_pairs={{8,0},{10,2},{12,4},{14,6},{0,8},{2,10},{4,12},{6,14},{9,1},{11,3}... | collective-permute-start | bytes 393224 | tf_op jit(solution)/shard_map/ppermute | solution.py:25
  46.9 1.6 %collective-permute-start.15 = (bf16[2,528,128]{2,1,0:T(8,128)(2,1)S(1)}, bf16[2,528,128]{2,1,0:T(8,128)(2,1)S(1)}, u32[]{:S(2)}, u32[]{:S(2)}) collective-permute-start(bf16[2,528,128]{2,1,0:T(8,128)(2,1)S(1)} %shard_map.83), channel_id=1, source_target_pairs={{0,4},{4,8},{8,12},{12,14},{14,10},{10,6},{6,2},{2,0},{1,5},{5,9},... | collective-permute-start | bytes 811016 | tf_op jit(solution)/shard_map/ppermute | solution.py:464
  48.5 2.3 %shard_map.84 = (f32[2,512,128]{2,1,0:T(8,128)S(1)}, bf16[2,16,128]{2,1,0:T(8,128)(2,1)S(1)}, f32[2,512,128]{2,1,0:T(8,128)S(1)}, bf16[2,16,128]{2,1,0:T(8,128)(2,1)S(1)}) custom-call(s32[2,128]{1,0:T(2,128)S(1)} %maximum_convert_fusion.2.refs_0_, bf16[64,2048]{1,0:T(8,128)(2,1)S(1)} %collective-permute-done.13.refs_1_, ...), custom_call_target="tpu_custom_call" | custom-call | flops 1073741824 | bytes 2621440 | tf_op jit(solution)/shard_map/pallas_call | solution.py:249
  50.8 0.5 collective-permute-start.16
  51.3 8.4 %collective-permute-done.14.page_ref = bf16[1,2,64,512]{3,2,1,0:T(8,128)(2,1)S(1)} collective-permute-done((bf16[1,2,64,512]{3,2,1,0:T(8,128)(2,1)S(1)}, bf16[1,2,64,512]{3,2,1,0:T(8,128)(2,1)S(1)}, u32[]{:S(2)}, u32[]{:S(2)}) %collective-permute-start.14) | collective-permute-done | bytes 131104 | tf_op jit(solution)/shard_map/ppermute | solution.py:25
  59.7 2.3 %shard_map.86 = (f32[2,512,128]{2,1,0:T(8,128)S(1)}, bf16[2,16,128]{2,1,0:T(8,128)(2,1)S(1)}, f32[2,512,128]{2,1,0:T(8,128)S(1)}, bf16[2,16,128]{2,1,0:T(8,128)(2,1)S(1)}) custom-call(s32[1,128]{1,0:T(1,128)S(1)} %fusion.refs_0_, bf16[64,2176]{1,0:T(8,128)(2,1)S(1)} %collective-permute-done.9.refs_1_, bf16[64,2048]{1,0:T(8,128)(2,1)S(1)} %collective-permute-done.12.refs_2_, ...), custom_call_target="tpu_custom_call" | custom-call | flops 1073741824 | bytes 2621440 | tf_op jit(solution)/shard_map/pallas_call | solution.py:249
  62.1 1.7 %collective-permute-start.17 = (bf16[2,528,128]{2,1,0:T(8,128)(2,1)S(1)}, bf16[2,528,128]{2,1,0:T(8,128)(2,1)S(1)}, u32[]{:S(2)}, u32[]{:S(2)}) collective-permute-start(bf16[2,528,128]{2,1,0:T(8,128)(2,1)S(1)} %shard_map.87), channel_id=1, source_target_pairs={{0,4},{4,8},{8,12},{12,14},{14,10},{10,6},{6,2},{2,0},{1,5},{5,9},... | collective-permute-start | bytes 811016 | tf_op jit(solution)/shard_map/ppermute | solution.py:485
  63.8 0.4 collective-permute-start.18
  64.2 0.6 shard_map.89
  64.9 1.7 %collective-permute-start.21 = (bf16[2,528,128]{2,1,0:T(8,128)(2,1)S(1)}, bf16[2,528,128]{2,1,0:T(8,128)(2,1)S(1)}, u32[]{:S(2)}, u32[]{:S(2)}) collective-permute-start(bf16[2,528,128]{2,1,0:T(8,128)(2,1)S(1)} %shard_map.89), channel_id=1, source_target_pairs={{0,4},{4,8},{8,12},{12,14},{14,10},{10,6},{6,2},{2,0},{1,5},{5,9},... | collective-permute-start | bytes 811016 | tf_op jit(solution)/shard_map/ppermute | solution.py:485
  66.6 0.6 shard_map.90
  67.2 0.4 collective-permute-start.22
  67.6 3.3 %shard_map.91 = (f32[2,512,128]{2,1,0:T(8,128)S(1)}, bf16[2,16,128]{2,1,0:T(8,128)(2,1)S(1)}, bf16[32,2,64,512]{3,2,1,0:T(8,128)(2,1)}) custom-call(s32[1,128]{1,0:T(1,128)S(1)} %fusion.1.refs_0_, bf16[64,2176]{1,0:T(8,128)(2,1)S(1)} %get-tuple-element.126.refs_1_, bf16[2,64,512]{2,1,0:T(8,128)(2,1)S(1)} %bitcast.2, bf16[32,2,64,512]{3,2,1,0:T(8,128)(2,1)S(1)} %copy-done.1), custom_call_target="tpu_custom_call" | custom-call | flops 536870912 | bytes 1310720 | tf_op jit(solution)/shard_map/pallas_call | solution.py:249
  70.9 1.7 %collective-permute-done.18.in_ref = bf16[2,528,128]{2,1,0:T(8,128)(2,1)S(1)} collective-permute-done((bf16[2,528,128]{2,1,0:T(8,128)(2,1)S(1)}, bf16[2,528,128]{2,1,0:T(8,128)(2,1)S(1)}, u32[]{:S(2)}, u32[]{:S(2)}) %collective-permute-start.18) | collective-permute-done | bytes 270368 | tf_op jit(solution)/shard_map/ppermute | solution.py:485
  72.6 0.6 shard_map.92
  73.2 0.7 collective-permute-start.19
  73.9 0.6 shard_map.93
  74.5 1.4 %collective-permute-start.20 = (bf16[2,528,128]{2,1,0:T(8,128)(2,1)S(1)}, bf16[2,528,128]{2,1,0:T(8,128)(2,1)S(1)}, u32[]{:S(2)}, u32[]{:S(2)}) collective-permute-start(bf16[2,528,128]{2,1,0:T(8,128)(2,1)S(1)} %shard_map.93), channel_id=1, source_target_pairs={{0,2},{4,0},{8,4},{12,8},{14,12},{10,14},{6,10},{2,6},{1,3},{5,1},... | collective-permute-start | bytes 811016 | tf_op jit(solution)/shard_map/ppermute | solution.py:485
  76.3 1.7 %collective-permute-done.22.in_ref = bf16[2,528,128]{2,1,0:T(8,128)(2,1)S(1)} collective-permute-done((bf16[2,528,128]{2,1,0:T(8,128)(2,1)S(1)}, bf16[2,528,128]{2,1,0:T(8,128)(2,1)S(1)}, u32[]{:S(2)}, u32[]{:S(2)}) %collective-permute-start.22) | collective-permute-done | bytes 270368 | tf_op jit(solution)/shard_map/ppermute | solution.py:485
  78.0 0.6 shard_map.94
  78.6 0.9 collective-permute-start.25
  79.5 0.6 shard_map.95
  80.1 1.3 %collective-permute-start.26 = (bf16[2,528,128]{2,1,0:T(8,128)(2,1)S(1)}, bf16[2,528,128]{2,1,0:T(8,128)(2,1)S(1)}, u32[]{:S(2)}, u32[]{:S(2)}) collective-permute-start(bf16[2,528,128]{2,1,0:T(8,128)(2,1)S(1)} %shard_map.95), channel_id=1, source_target_pairs={{0,2},{4,0},{8,4},{12,8},{14,12},{10,14},{6,10},{2,6},{1,3},{5,1},... | collective-permute-start | bytes 811016 | tf_op jit(solution)/shard_map/ppermute | solution.py:485
  81.4 1.8 %shard_map.96 = (f32[2,512,128]{2,1,0:T(8,128)S(1)}, bf16[2,16,128]{2,1,0:T(8,128)(2,1)S(1)}) custom-call(s32[1,128]{1,0:T(1,128)S(1)} %fusion.1.refs_0_, bf16[64,2048]{1,0:T(8,128)(2,1)S(1)} %get-tuple-element.137.refs_1_, bf16[2,64,512]{2,1,0:T(8,128)(2,1)S(1)} %bitcast.3, bf16[32,2,64,512]{3,2,1,0:T(8,128)(2,1)S(1)} %copy-done.1), custom_call_target="tpu_custom_call" | custom-call | flops 536870912 | bytes 1310720 | tf_op jit(solution)/shard_map/pallas_call | solution.py:249
  83.2 0.8 collective-permute-done.20.in_ref
  84.0 0.6 shard_map.97
  84.7 0.6 collective-permute-start.23
  85.3 0.6 shard_map.98
  85.9 1.5 %collective-permute-start.24 = (bf16[2,528,128]{2,1,0:T(8,128)(2,1)S(1)}, bf16[2,528,128]{2,1,0:T(8,128)(2,1)S(1)}, u32[]{:S(2)}, u32[]{:S(2)}) collective-permute-start(bf16[2,528,128]{2,1,0:T(8,128)(2,1)S(1)} %shard_map.98), channel_id=1, source_target_pairs={{0,2},{4,0},{8,4},{12,8},{14,12},{10,14},{6,10},{2,6},{1,3},{5,1},... | collective-permute-start | bytes 811016 | tf_op jit(solution)/shard_map/ppermute | solution.py:485
  87.8 2.0 %collective-permute-done.26.in_ref = bf16[2,528,128]{2,1,0:T(8,128)(2,1)S(1)} collective-permute-done((bf16[2,528,128]{2,1,0:T(8,128)(2,1)S(1)}, bf16[2,528,128]{2,1,0:T(8,128)(2,1)S(1)}, u32[]{:S(2)}, u32[]{:S(2)}) %collective-permute-start.26) | collective-permute-done | bytes 270368 | tf_op jit(solution)/shard_map/ppermute | solution.py:485
  89.8 1.4 %collective-permute-done.23.in_ref = bf16[2,528,128]{2,1,0:T(8,128)(2,1)S(1)} collective-permute-done((bf16[2,528,128]{2,1,0:T(8,128)(2,1)S(1)}, bf16[2,528,128]{2,1,0:T(8,128)(2,1)S(1)}, u32[]{:S(2)}, u32[]{:S(2)}) %collective-permute-start.23) | collective-permute-done | bytes 270368 | tf_op jit(solution)/shard_map/ppermute | solution.py:485
  91.2 1.7 %collective-permute-done.24.in_ref = bf16[2,528,128]{2,1,0:T(8,128)(2,1)S(1)} collective-permute-done((bf16[2,528,128]{2,1,0:T(8,128)(2,1)S(1)}, bf16[2,528,128]{2,1,0:T(8,128)(2,1)S(1)}, u32[]{:S(2)}, u32[]{:S(2)}) %collective-permute-start.24) | collective-permute-done | bytes 270368 | tf_op jit(solution)/shard_map/ppermute | solution.py:485
  92.9 0.6 shard_map.99
  93.5 1.1 %collective-permute-start.27 = (bf16[2,528,128]{2,1,0:T(8,128)(2,1)S(1)}, bf16[2,528,128]{2,1,0:T(8,128)(2,1)S(1)}, u32[]{:S(2)}, u32[]{:S(2)}) collective-permute-start(bf16[2,528,128]{2,1,0:T(8,128)(2,1)S(1)} %shard_map.99), channel_id=1, source_target_pairs={{0,2},{4,0},{8,4},{12,8},{14,12},{10,14},{6,10},{2,6},{1,3},{5,1},... | collective-permute-start | bytes 811016 | tf_op jit(solution)/shard_map/ppermute | solution.py:485
  94.6 0.6 shard_map.100
  95.2 1.0 collective-permute-start.28
  96.2 1.2 %shard_map.104 = bf16[32,2,64,512]{3,2,1,0:T(8,128)(2,1)} custom-call(s32[1]{0:T(128)} %bitcast.1.me_ref, s32[2,128]{1,0:T(2,128)S(1)} %maximum_convert_fusion.1.refs_0_.lists_ref, bf16[1,2,64,512]{3,2,1,0:T(8,128)(2,1)S(1)} %collective-permute-done.14.page_ref, bf16[32,2,64,512]{3,2,1,0:T(8,128)(2,1)} %get-tuple-element.155.old_ref), custom_call_target="tpu_custom_call", output_to_operand_aliasing={{}: (3, {})} | custom-call | flops 1 | bytes 1 | tf_op jit(solution)/shard_map/pallas_call | solution.py:275
  97.5 0.6 shard_map.101
  98.1 0.6 shard_map.102
  98.8 1.3 %collective-permute-done.27.refs_0_ = bf16[2,528,128]{2,1,0:T(8,128)(2,1)S(1)} collective-permute-done((bf16[2,528,128]{2,1,0:T(8,128)(2,1)S(1)}, bf16[2,528,128]{2,1,0:T(8,128)(2,1)S(1)}, u32[]{:S(2)}, u32[]{:S(2)}) %collective-permute-start.27) | collective-permute-done | bytes 270368 | tf_op jit(solution)/shard_map/ppermute | solution.py:485
  100.0 1.7 %collective-permute-done.28.refs_3_ = bf16[2,528,128]{2,1,0:T(8,128)(2,1)S(1)} collective-permute-done((bf16[2,528,128]{2,1,0:T(8,128)(2,1)S(1)}, bf16[2,528,128]{2,1,0:T(8,128)(2,1)S(1)}, u32[]{:S(2)}, u32[]{:S(2)}) %collective-permute-start.28) | collective-permute-done | bytes 270368 | tf_op jit(solution)/shard_map/ppermute | solution.py:485
  101.7 1.7 %shard_map.103 = bf16[1,64,4096]{2,1,0:T(8,128)(2,1)} custom-call(bf16[2,528,128]{2,1,0:T(8,128)(2,1)S(1)} %collective-permute-done.27.refs_0_, f32[2,512,128]{2,1,0:T(8,128)S(1)} %get-tuple-element.148.refs_1_, bf16[2,16,128]{2,1,0:T(8,128)(2,1)S(1)} %get-tuple-element.149.refs_2_, bf16[2,528,128]{2,1,0:T(8,128)(2,1)S(1)} %collective-permute-done.28.refs_3_, ...), custom_call_target="tpu_custom_call" | custom-call | flops 1605632 | bytes 3211264 | tf_op jit(solution)/shard_map/pallas_call | solution.py:347
  (43 shorter events, 1.7 us)
Async XLA Ops:
  1.9 1.0 %copy-start.3 = (bf16[1,64,4096]{2,1,0:T(8,128)(2,1)S(1)}, bf16[1,64,4096]{2,1,0:T(8,128)(2,1)}, u32[]{:S(2)}) copy-start(bf16[1,64,4096]{2,1,0:T(8,128)(2,1)} %q_ref.1) | copy-start | bytes 1572868
  3.0 0.7 copy-start.4
  3.9 10.4 %collective-permute-start = (bf16[64,2176]{1,0:T(8,128)(2,1)S(1)}, bf16[64,2176]{1,0:T(8,128)(2,1)S(1)}, u32[]{:S(2)}, u32[]{:S(2)}) collective-permute-start(bf16[64,2176]{1,0:T(8,128)(2,1)S(1)} %get-tuple-element.126.refs_1_), channel_id=1, source_target_pairs={{0,4},{4,8},{8,12},{12,14},{14,10},{10,6},{6,2},{2,0},{1,5},{5,9},... | collective-permute-start | bytes 835592 | tf_op jit(solution)/shard_map/ppermute | solution.py:430
  6.9 9.6 %collective-permute-start.2 = (bf16[64,2176]{1,0:T(8,128)(2,1)S(1)}, bf16[64,2176]{1,0:T(8,128)(2,1)S(1)}, u32[]{:S(2)}, u32[]{:S(2)}) collective-permute-start(bf16[64,2176]{1,0:T(8,128)(2,1)S(1)} %get-tuple-element.126.refs_1_), channel_id=1, source_target_pairs={{0,2},{4,0},{8,4},{12,8},{14,12},{10,14},{6,10},{2,6},{1,3},{5,1},... | collective-permute-start | bytes 835592 | tf_op jit(solution)/shard_map/ppermute | solution.py:430
  6.9 14.1 %collective-permute-start.3 = (bf16[64,2048]{1,0:T(8,128)(2,1)S(1)}, bf16[64,2048]{1,0:T(8,128)(2,1)S(1)}, u32[]{:S(2)}, u32[]{:S(2)}) collective-permute-start(bf16[64,2048]{1,0:T(8,128)(2,1)S(1)} %get-tuple-element.137.refs_1_), channel_id=1, source_target_pairs={{0,4},{4,8},{8,12},{12,14},{14,10},{10,6},{6,2},{2,0},{1,5},{5,9},... | collective-permute-start | bytes 786440 | tf_op jit(solution)/shard_map/ppermute | solution.py:430
  9.0 13.2 %collective-permute-start.4 = (bf16[64,2048]{1,0:T(8,128)(2,1)S(1)}, bf16[64,2048]{1,0:T(8,128)(2,1)S(1)}, u32[]{:S(2)}, u32[]{:S(2)}) collective-permute-start(bf16[64,2048]{1,0:T(8,128)(2,1)S(1)} %get-tuple-element.137.refs_1_), channel_id=1, source_target_pairs={{0,2},{4,0},{8,4},{12,8},{14,12},{10,14},{6,10},{2,6},{1,3},{5,1},... | collective-permute-start | bytes 786440 | tf_op jit(solution)/shard_map/ppermute | solution.py:430
  14.4 12.0 %collective-permute-start.1 = (bf16[64,2176]{1,0:T(8,128)(2,1)S(1)}, bf16[64,2176]{1,0:T(8,128)(2,1)S(1)}, u32[]{:S(2)}, u32[]{:S(2)}) collective-permute-start(bf16[64,2176]{1,0:T(8,128)(2,1)S(1)} %collective-permute-done.refs_1_), channel_id=1, source_target_pairs={{0,4},{4,8},{8,12},{12,14},{14,10},{10,6},{6,2},{2,0},{1,5},{5,9},... | collective-permute-start | bytes 835592 | tf_op jit(solution)/shard_map/ppermute | solution.py:444
  16.5 11.6 %collective-permute-start.6 = (bf16[64,2176]{1,0:T(8,128)(2,1)S(1)}, bf16[64,2176]{1,0:T(8,128)(2,1)S(1)}, u32[]{:S(2)}, u32[]{:S(2)}) collective-permute-start(bf16[64,2176]{1,0:T(8,128)(2,1)S(1)} %collective-permute-done.2.refs_2_), channel_id=1, source_target_pairs={{0,2},{4,0},{8,4},{12,8},{14,12},{10,14},{6,10},{2,6},{1,3},{5,1},... | collective-permute-start | bytes 835592 | tf_op jit(solution)/shard_map/ppermute | solution.py:444
  16.6 2.2 %copy-start = (bf16[32,2,64,512]{3,2,1,0:T(8,128)(2,1)S(1)}, bf16[32,2,64,512]{3,2,1,0:T(8,128)(2,1)}, u32[]{:S(2)}) copy-start(bf16[32,2,64,512]{3,2,1,0:T(8,128)(2,1)} %refs_3_.17) | copy-start | bytes 12582916
  22.1 9.4 %collective-permute-start.7 = (bf16[64,2048]{1,0:T(8,128)(2,1)S(1)}, bf16[64,2048]{1,0:T(8,128)(2,1)S(1)}, u32[]{:S(2)}, u32[]{:S(2)}) collective-permute-start(bf16[64,2048]{1,0:T(8,128)(2,1)S(1)} %collective-permute-done.3.refs_1_), channel_id=1, source_target_pairs={{0,4},{4,8},{8,12},{12,14},{14,10},{10,6},{6,2},{2,0},{1,5},{5,9},... | collective-permute-start | bytes 786440 | tf_op jit(solution)/shard_map/ppermute | solution.py:444
  23.7 10.0 %collective-permute-start.8 = (bf16[64,2048]{1,0:T(8,128)(2,1)S(1)}, bf16[64,2048]{1,0:T(8,128)(2,1)S(1)}, u32[]{:S(2)}, u32[]{:S(2)}) collective-permute-start(bf16[64,2048]{1,0:T(8,128)(2,1)S(1)} %collective-permute-done.4.refs_2_), channel_id=1, source_target_pairs={{0,2},{4,0},{8,4},{12,8},{14,12},{10,14},{6,10},{2,6},{1,3},{5,1},... | collective-permute-start | bytes 786440 | tf_op jit(solution)/shard_map/ppermute | solution.py:444
  26.4 11.6 %collective-permute-start.5 = (bf16[64,2176]{1,0:T(8,128)(2,1)S(1)}, bf16[64,2176]{1,0:T(8,128)(2,1)S(1)}, u32[]{:S(2)}, u32[]{:S(2)}) collective-permute-start(bf16[64,2176]{1,0:T(8,128)(2,1)S(1)} %collective-permute-done.1.refs_1_), channel_id=1, source_target_pairs={{0,4},{4,8},{8,12},{12,14},{14,10},{10,6},{6,2},{2,0},{1,5},{5,9},... | collective-permute-start | bytes 835592 | tf_op jit(solution)/shard_map/ppermute | solution.py:444
  28.1 11.6 %collective-permute-start.11 = (bf16[64,2176]{1,0:T(8,128)(2,1)S(1)}, bf16[64,2176]{1,0:T(8,128)(2,1)S(1)}, u32[]{:S(2)}, u32[]{:S(2)}) collective-permute-start(bf16[64,2176]{1,0:T(8,128)(2,1)S(1)} %collective-permute-done.6.refs_2_), channel_id=1, source_target_pairs={{0,2},{4,0},{8,4},{12,8},{14,12},{10,14},{6,10},{2,6},{1,3},{5,1},... | collective-permute-start | bytes 835592 | tf_op jit(solution)/shard_map/ppermute | solution.py:444
  31.6 12.6 %copy-start.2 = (bf16[1,2,64,512]{3,2,1,0:T(8,128)(2,1)S(1)}, bf16[1,2,64,512]{3,2,1,0:T(8,128)(2,1)}, u32[]{:S(2)}) copy-start(bf16[1,2,64,512]{3,2,1,0:T(8,128)(2,1)} %param.7) | copy-start | bytes 393220
  31.6 16.9 %copy-start.1 = (bf16[32,2,64,512]{3,2,1,0:T(8,128)(2,1)S(1)}, bf16[32,2,64,512]{3,2,1,0:T(8,128)(2,1)}, u32[]{:S(2)}) copy-start(bf16[32,2,64,512]{3,2,1,0:T(8,128)(2,1)} %refs_3_.17) | copy-start | bytes 12582916
  33.7 10.1 %collective-permute-start.10 = (bf16[64,2048]{1,0:T(8,128)(2,1)S(1)}, bf16[64,2048]{1,0:T(8,128)(2,1)S(1)}, u32[]{:S(2)}, u32[]{:S(2)}) collective-permute-start(bf16[64,2048]{1,0:T(8,128)(2,1)S(1)} %collective-permute-done.8.refs_2_), channel_id=1, source_target_pairs={{0,2},{4,0},{8,4},{12,8},{14,12},{10,14},{6,10},{2,6},{1,3},{5,1},... | collective-permute-start | bytes 786440 | tf_op jit(solution)/shard_map/ppermute | solution.py:444
  33.7 14.7 %collective-permute-start.13 = (bf16[64,2048]{1,0:T(8,128)(2,1)S(1)}, bf16[64,2048]{1,0:T(8,128)(2,1)S(1)}, u32[]{:S(2)}, u32[]{:S(2)}) collective-permute-start(bf16[64,2048]{1,0:T(8,128)(2,1)S(1)} %collective-permute-done.7.refs_1_), channel_id=1, source_target_pairs={{0,4},{4,8},{8,12},{12,14},{14,10},{10,6},{6,2},{2,0},{1,5},{5,9},... | collective-permute-start | bytes 786440 | tf_op jit(solution)/shard_map/ppermute | solution.py:444
  38.0 21.7 %collective-permute-start.9 = (bf16[64,2176]{1,0:T(8,128)(2,1)S(1)}, bf16[64,2176]{1,0:T(8,128)(2,1)S(1)}, u32[]{:S(2)}, u32[]{:S(2)}) collective-permute-start(bf16[64,2176]{1,0:T(8,128)(2,1)S(1)} %collective-permute-done.5.refs_1_), channel_id=1, source_target_pairs={{0,4},{4,8},{8,12},{12,14},{14,10},{10,6},{6,2},{2,0},{1,5},{5,9},... | collective-permute-start | bytes 835592 | tf_op jit(solution)/shard_map/ppermute | solution.py:444
  43.8 15.9 %collective-permute-start.12 = (bf16[64,2048]{1,0:T(8,128)(2,1)S(1)}, bf16[64,2048]{1,0:T(8,128)(2,1)S(1)}, u32[]{:S(2)}, u32[]{:S(2)}) collective-permute-start(bf16[64,2048]{1,0:T(8,128)(2,1)S(1)} %collective-permute-done.10.refs_2_), channel_id=1, source_target_pairs={{0,2},{4,0},{8,4},{12,8},{14,12},{10,14},{6,10},{2,6},{1,3},{5,1},... | collective-permute-start | bytes 786440 | tf_op jit(solution)/shard_map/ppermute | solution.py:444
  44.1 15.6 %collective-permute-start.14 = (bf16[1,2,64,512]{3,2,1,0:T(8,128)(2,1)S(1)}, bf16[1,2,64,512]{3,2,1,0:T(8,128)(2,1)S(1)}, u32[]{:S(2)}, u32[]{:S(2)}) collective-permute-start(bf16[1,2,64,512]{3,2,1,0:T(8,128)(2,1)S(1)} %copy-done.2), channel_id=1, source_target_pairs={{8,0},{10,2},{12,4},{14,6},{0,8},{2,10},{4,12},{6,14},{9,1},{11,3}... | collective-permute-start | bytes 393224 | tf_op jit(solution)/shard_map/ppermute | solution.py:25
  46.9 15.1 %collective-permute-start.15 = (bf16[2,528,128]{2,1,0:T(8,128)(2,1)S(1)}, bf16[2,528,128]{2,1,0:T(8,128)(2,1)S(1)}, u32[]{:S(2)}, u32[]{:S(2)}) collective-permute-start(bf16[2,528,128]{2,1,0:T(8,128)(2,1)S(1)} %shard_map.83), channel_id=1, source_target_pairs={{0,4},{4,8},{8,12},{12,14},{14,10},{10,6},{6,2},{2,0},{1,5},{5,9},... | collective-permute-start | bytes 811016 | tf_op jit(solution)/shard_map/ppermute | solution.py:464
  50.8 11.2 %collective-permute-start.16 = (bf16[2,528,128]{2,1,0:T(8,128)(2,1)S(1)}, bf16[2,528,128]{2,1,0:T(8,128)(2,1)S(1)}, u32[]{:S(2)}, u32[]{:S(2)}) collective-permute-start(bf16[2,528,128]{2,1,0:T(8,128)(2,1)S(1)} %shard_map.85), channel_id=1, source_target_pairs={{0,2},{4,0},{8,4},{12,8},{14,12},{10,14},{6,10},{2,6},{1,3},{5,1},... | collective-permute-start | bytes 811016 | tf_op jit(solution)/shard_map/ppermute | solution.py:464
  62.1 8.8 %collective-permute-start.17 = (bf16[2,528,128]{2,1,0:T(8,128)(2,1)S(1)}, bf16[2,528,128]{2,1,0:T(8,128)(2,1)S(1)}, u32[]{:S(2)}, u32[]{:S(2)}) collective-permute-start(bf16[2,528,128]{2,1,0:T(8,128)(2,1)S(1)} %shard_map.87), channel_id=1, source_target_pairs={{0,4},{4,8},{8,12},{12,14},{14,10},{10,6},{6,2},{2,0},{1,5},{5,9},... | collective-permute-start | bytes 811016 | tf_op jit(solution)/shard_map/ppermute | solution.py:485
  63.8 8.8 %collective-permute-start.18 = (bf16[2,528,128]{2,1,0:T(8,128)(2,1)S(1)}, bf16[2,528,128]{2,1,0:T(8,128)(2,1)S(1)}, u32[]{:S(2)}, u32[]{:S(2)}) collective-permute-start(bf16[2,528,128]{2,1,0:T(8,128)(2,1)S(1)} %shard_map.88), channel_id=1, source_target_pairs={{0,2},{4,0},{8,4},{12,8},{14,12},{10,14},{6,10},{2,6},{1,3},{5,1},... | collective-permute-start | bytes 811016 | tf_op jit(solution)/shard_map/ppermute | solution.py:485
  64.9 11.4 %collective-permute-start.21 = (bf16[2,528,128]{2,1,0:T(8,128)(2,1)S(1)}, bf16[2,528,128]{2,1,0:T(8,128)(2,1)S(1)}, u32[]{:S(2)}, u32[]{:S(2)}) collective-permute-start(bf16[2,528,128]{2,1,0:T(8,128)(2,1)S(1)} %shard_map.89), channel_id=1, source_target_pairs={{0,4},{4,8},{8,12},{12,14},{14,10},{10,6},{6,2},{2,0},{1,5},{5,9},... | collective-permute-start | bytes 811016 | tf_op jit(solution)/shard_map/ppermute | solution.py:485
  67.2 10.8 %collective-permute-start.22 = (bf16[2,528,128]{2,1,0:T(8,128)(2,1)S(1)}, bf16[2,528,128]{2,1,0:T(8,128)(2,1)S(1)}, u32[]{:S(2)}, u32[]{:S(2)}) collective-permute-start(bf16[2,528,128]{2,1,0:T(8,128)(2,1)S(1)} %shard_map.90), channel_id=1, source_target_pairs={{0,2},{4,0},{8,4},{12,8},{14,12},{10,14},{6,10},{2,6},{1,3},{5,1},... | collective-permute-start | bytes 811016 | tf_op jit(solution)/shard_map/ppermute | solution.py:485
  73.2 10.0 %collective-permute-start.19 = (bf16[2,528,128]{2,1,0:T(8,128)(2,1)S(1)}, bf16[2,528,128]{2,1,0:T(8,128)(2,1)S(1)}, u32[]{:S(2)}, u32[]{:S(2)}) collective-permute-start(bf16[2,528,128]{2,1,0:T(8,128)(2,1)S(1)} %shard_map.92), channel_id=1, source_target_pairs={{0,4},{4,8},{8,12},{12,14},{14,10},{10,6},{6,2},{2,0},{1,5},{5,9},... | collective-permute-start | bytes 811016 | tf_op jit(solution)/shard_map/ppermute | solution.py:485
  74.5 9.5 %collective-permute-start.20 = (bf16[2,528,128]{2,1,0:T(8,128)(2,1)S(1)}, bf16[2,528,128]{2,1,0:T(8,128)(2,1)S(1)}, u32[]{:S(2)}, u32[]{:S(2)}) collective-permute-start(bf16[2,528,128]{2,1,0:T(8,128)(2,1)S(1)} %shard_map.93), channel_id=1, source_target_pairs={{0,2},{4,0},{8,4},{12,8},{14,12},{10,14},{6,10},{2,6},{1,3},{5,1},... | collective-permute-start | bytes 811016 | tf_op jit(solution)/shard_map/ppermute | solution.py:485
  78.6 9.2 %collective-permute-start.25 = (bf16[2,528,128]{2,1,0:T(8,128)(2,1)S(1)}, bf16[2,528,128]{2,1,0:T(8,128)(2,1)S(1)}, u32[]{:S(2)}, u32[]{:S(2)}) collective-permute-start(bf16[2,528,128]{2,1,0:T(8,128)(2,1)S(1)} %shard_map.94), channel_id=1, source_target_pairs={{0,4},{4,8},{8,12},{12,14},{14,10},{10,6},{6,2},{2,0},{1,5},{5,9},... | collective-permute-start | bytes 811016 | tf_op jit(solution)/shard_map/ppermute | solution.py:485
  80.1 9.7 %collective-permute-start.26 = (bf16[2,528,128]{2,1,0:T(8,128)(2,1)S(1)}, bf16[2,528,128]{2,1,0:T(8,128)(2,1)S(1)}, u32[]{:S(2)}, u32[]{:S(2)}) collective-permute-start(bf16[2,528,128]{2,1,0:T(8,128)(2,1)S(1)} %shard_map.95), channel_id=1, source_target_pairs={{0,2},{4,0},{8,4},{12,8},{14,12},{10,14},{6,10},{2,6},{1,3},{5,1},... | collective-permute-start | bytes 811016 | tf_op jit(solution)/shard_map/ppermute | solution.py:485
  84.7 6.5 %collective-permute-start.23 = (bf16[2,528,128]{2,1,0:T(8,128)(2,1)S(1)}, bf16[2,528,128]{2,1,0:T(8,128)(2,1)S(1)}, u32[]{:S(2)}, u32[]{:S(2)}) collective-permute-start(bf16[2,528,128]{2,1,0:T(8,128)(2,1)S(1)} %shard_map.97), channel_id=1, source_target_pairs={{0,4},{4,8},{8,12},{12,14},{14,10},{10,6},{6,2},{2,0},{1,5},{5,9},... | collective-permute-start | bytes 811016 | tf_op jit(solution)/shard_map/ppermute | solution.py:485
  85.9 6.9 %collective-permute-start.24 = (bf16[2,528,128]{2,1,0:T(8,128)(2,1)S(1)}, bf16[2,528,128]{2,1,0:T(8,128)(2,1)S(1)}, u32[]{:S(2)}, u32[]{:S(2)}) collective-permute-start(bf16[2,528,128]{2,1,0:T(8,128)(2,1)S(1)} %shard_map.98), channel_id=1, source_target_pairs={{0,2},{4,0},{8,4},{12,8},{14,12},{10,14},{6,10},{2,6},{1,3},{5,1},... | collective-permute-start | bytes 811016 | tf_op jit(solution)/shard_map/ppermute | solution.py:485
  93.5 6.5 %collective-permute-start.27 = (bf16[2,528,128]{2,1,0:T(8,128)(2,1)S(1)}, bf16[2,528,128]{2,1,0:T(8,128)(2,1)S(1)}, u32[]{:S(2)}, u32[]{:S(2)}) collective-permute-start(bf16[2,528,128]{2,1,0:T(8,128)(2,1)S(1)} %shard_map.99), channel_id=1, source_target_pairs={{0,2},{4,0},{8,4},{12,8},{14,12},{10,14},{6,10},{2,6},{1,3},{5,1},... | collective-permute-start | bytes 811016 | tf_op jit(solution)/shard_map/ppermute | solution.py:485
  95.2 6.5 %collective-permute-start.28 = (bf16[2,528,128]{2,1,0:T(8,128)(2,1)S(1)}, bf16[2,528,128]{2,1,0:T(8,128)(2,1)S(1)}, u32[]{:S(2)}, u32[]{:S(2)}) collective-permute-start(bf16[2,528,128]{2,1,0:T(8,128)(2,1)S(1)} %shard_map.100), channel_id=1, source_target_pairs={{0,4},{4,8},{8,12},{12,14},{14,10},{10,6},{6,2},{2,0},{1,5},{5,9},... | collective-permute-start | bytes 811016 | tf_op jit(solution)/shard_map/ppermute | solution.py:485

commit v9 on v8

--- a/solution.py
+++ b/solution.py
@@ -246,6 +246,7 @@
         shapes.append(jax.ShapeDtypeStruct(held.shape, held.dtype))
         specs.append(HBM)
         scratch.append(pltpu.SemaphoreType.DMA)
+    weight = 16 if own is not None and not keeping else 1
     out = pl.pallas_call(
         functools.partial(attend_kernel, shape + (len(queries), own is not None, keeping), jobs),
         out_shape=shapes,
@@ -254,9 +255,9 @@
         scratch_shapes=scratch,
         compiler_params=pltpu.CompilerParams(vmem_limit_bytes=GRANT),
         cost_estimate=pl.CostEstimate(
-            flops=len(jobs) * rows * keys * HEAD_SIZE * 8,
-            bytes_accessed=len(jobs) * (rows * 6 + keys * 4) * HEAD_SIZE,
-            transcendentals=len(jobs) * rows * keys,
+            flops=weight * len(jobs) * rows * keys * HEAD_SIZE * 8,
+            bytes_accessed=weight * len(jobs) * (rows * 6 + keys * 4) * HEAD_SIZE,
+            transcendentals=weight * len(jobs) * rows * keys,
         ),
     )(meta, *queries, *more)
     return [(out[2 * n], out[2 * n + 1]) for n in range(results)] + list(out[2 * results:])
@@ -394,7 +395,6 @@
         in_specs=[SMEM, SMEM, VMEM, VMEM],
         out_specs=[VMEM, VMEM],
         compiler_params=pltpu.CompilerParams(vmem_limit_bytes=GRANT),
-        cost_estimate=pl.CostEstimate(flops=1, bytes_accessed=1 << 24, transcendentals=0),
     )(prefix_pages, new_slots, page_table, queries)
 
 
@@ -424,6 +424,7 @@
     def after(values, token):
         return lax.optimization_barrier((values, token))[0]
 
+    arrived = shifted(suffix_key_value, "store", half)
     mine = prepare(cut, cap, pages_dev, queries, page_table, prefix_pages, new_slots)
 
     moving = {
@@ -433,7 +434,18 @@
     }
     held = kv_pages
     parts = {}
-    token = []
+
+    def attend_own(side, token, keeping):
+        jobs = [(0, 0, h, side * heads_each + h, 0) for h in range(heads_each)]
+        lists = listed(mine[0])
+        own = suffix_key_value[0]
+        parts[0, side], *pages = attend(
+            shape, jobs, lists, [after(mine[side], token)], held, own, keeping
+        )
+        return pages
+
+    attend_own(0, arrived, False)
+    token = parts[0, 0]
     lists_of = {}
     sent = {}
     for step in range(1, half):
@@ -448,13 +460,11 @@
             got = attend(shape, jobs, lists_of[step], [came[1], came[-1]], held)
             parts[step, side], parts[-step, side] = got
             token = got
-            if (step, side) == (half - 2, 1):
-                arrived = shifted(after(suffix_key_value, token), "store", half)
             if step == half - 1:
                 sign = 1 if side == 1 else -1
                 sent["early", sign] = packed(parts[sign * step, side])
                 token = sent["early", sign]
-    came = after([moving[0, 1], moving[1, -1]], [token, arrived])
+    came = after([moving[0, 1], moving[1, -1]], token)
     jobs = [(0, side, h, side * heads_each + h, side) for side in range(2) for h in range(heads_each)]
     far = attend(shape, jobs, listed(came[0]), came, held)
     token = far
@@ -467,8 +477,6 @@
         turns += [("early", distance - 1)] * (distance > 1) + [("late", distance)]
     for flow, distance in turns:
         if distance == half:
-            far, ended = lax.optimization_barrier((far, {sign: flows["early", sign] for sign in back}))
-            flows.update({("early", sign): ended[sign] for sign in back})
             blocks = {sign: packed(far[side_of[flow, sign]]) for sign in back}
         else:
             came = {sign: flows[flow, sign] for sign in back}
@@ -484,21 +492,9 @@
         for sign in back:
             flows[flow, sign] = lax.ppermute(blocks[sign], "store", back[sign])
         token = blocks
-        if flow == "early" and distance <= 2:
-            side = 2 - distance
-            jobs = [(0, 0, h, side * heads_each + h, 0) for h in range(heads_each)]
-            parts[0, side], *kept_pages = attend(
-                shape,
-                jobs,
-                listed(mine[0]),
-                [after(mine[side], token)],
-                held,
-                suffix_key_value[0],
-                side == 0,
-            )
-            token = [blocks, parts[0, side]]
-            if kept_pages:
-                store, = kept_pages
+        if flow == "early" and distance == 1:
+            (store,) = attend_own(1, token, True)
+            token = [token, store]
     store = place_page(
         half, cap + 1, me[None], lists_of[stores // 4], arrived, after(store, token)
     )

time: 104 us -> 98.9 us (0.951)
  waiting for transfers between devices: 32.6 us -> 25.7 us
    ppermute x1, waiting for transfers between devices: 8.42 us -> 0.01 us  [shifted(): return lax.ppermute(block, axis, route)]
    ppermute x4, waiting for transfers between devices: 6.53 us -> 3.45 us  [queries_travel(): lax.ppermute(mine[side], 'store', routes[sign])]
    ppermute x10, waiting for transfers between devices: 4.79 us -> 7.81 us  [queries_travel(): moving[side, sign] = lax.ppermute(came[sign], 'store', routes[sign])]
    ppermute x12, waiting for transfers between devices: 12.9 us -> 14.4 us  [queries_travel(): flows[flow, sign] = lax.ppermute(blocks[sign], 'store', back[sign])]
    ppermute x1, starting transfers between devices: 2.76 us -> 4.1 us  [shifted(): return lax.ppermute(block, axis, route)]
    unnamed x10 -> x12, local copies, waits for them, and re-layouts: 3.88 us -> 4.79 us
  transfers between devices with their start and end apart: 29 -> 29, of which waited for: 16 -> 16; matrix products, arithmetic and copies ran while one was open for 0% -> 0% of each run, Pallas kernels for 28% -> 30%
where the time goes in v9:
time: 98.9 us; the launch traced here: 98.4 us
  starting transfers between devices  33.6 us (34%)
  Pallas kernels  31.9 us (32%)
  waiting for transfers between devices  25.7 us (26%)
  local copies, waits for them, and re-layouts  4.84 us (5%)
  between operations  2.26 us (2%)
    pallas_call x9, Pallas kernels, attend(): pl.pallas_call(functools.partial(attend_kernel, shape + (len(queries), ow...  21 us
    ppermute x12, waiting for transfers between devices, queries_travel(): flows[flow, sign] = lax.ppermute(blocks[sign], 'store', back[sign])  14.4 us
    ppermute x12, starting transfers between devices, queries_travel(): flows[flow, sign] = lax.ppermute(blocks[sign], 'store', back[sign])  13.1 us
    ppermute x10, starting transfers between devices, queries_travel(): moving[side, sign] = lax.ppermute(came[sign], 'store', routes[sign])  10.3 us
    pallas_call x17, Pallas kernels, call(): pl.pallas_call(kernel, out_shape=shape, in_specs=[VMEM] * len(args), out_...  9.42 us
    ppermute x10, waiting for transfers between devices, queries_travel(): moving[side, sign] = lax.ppermute(came[sign], 'store', routes[sign])  7.81 us
    unnamed x12, local copies, waits for them, and re-layouts  4.79 us
    ppermute x1, starting transfers between devices, shifted(): return lax.ppermute(block, axis, route)  4.1 us
  transfers between devices with their start and end apart: 29, of which 16 were waited for; matrix products, arithmetic and copies ran while one was open for 0% of the time, Pallas kernels for 30%

profile of v9, /device:TPU:0, one launch (start us, length us, event | category | flops | bytes accessed | tf_op | source)
XLA Modules:
  0.0 98.4 jit_solution(5455273809769052314)
XLA Ops:
  0.6 4.1 %collective-permute-start.1 = (bf16[1,2,64,512]{3,2,1,0:T(8,128)(2,1)}, bf16[1,2,64,512]{3,2,1,0:T(8,128)(2,1)S(1)}, u32[]{:S(2)}, u32[]{:S(2)}) collective-permute-start(bf16[1,2,64,512]{3,2,1,0:T(8,128)(2,1)} %param.7), channel_id=1, source_target_pairs={{8,0},{10,2},{12,4},{14,6},{0,8},{2,10},{4,12},{6,14},{9,1},{11,3}... | collective-permute-start | bytes 393224 | tf_op jit(solution)/shard_map/ppermute | solution.py:25
  6.0 1.0 %copy-done.2 = bf16[1,64,4096]{2,1,0:T(8,128)(2,1)S(1)} copy-done((bf16[1,64,4096]{2,1,0:T(8,128)(2,1)S(1)}, bf16[1,64,4096]{2,1,0:T(8,128)(2,1)}, u32[]{:S(2)}) %copy-start.2) | copy-done | bytes 524312
  7.1 0.7 copy-done.5
  8.0 1.6 %collective-permute-start = (bf16[64,2176]{1,0:T(8,128)(2,1)S(1)}, bf16[64,2176]{1,0:T(8,128)(2,1)S(1)}, u32[]{:S(2)}, u32[]{:S(2)}) collective-permute-start(bf16[64,2176]{1,0:T(8,128)(2,1)S(1)} %get-tuple-element.75.refs_1_), channel_id=1, source_target_pairs={{0,4},{4,8},{8,12},{12,14},{14,10},{10,6},{6,2},{2,0},{1,5},{5,9},... | collective-permute-start | bytes 835592 | tf_op jit(solution)/shard_map/ppermute | solution.py:431
  9.6 0.4 collective-permute-start.3
  10.0 1.6 %collective-permute-start.4 = (bf16[64,2048]{1,0:T(8,128)(2,1)S(1)}, bf16[64,2048]{1,0:T(8,128)(2,1)S(1)}, u32[]{:S(2)}, u32[]{:S(2)}) collective-permute-start(bf16[64,2048]{1,0:T(8,128)(2,1)S(1)} %get-tuple-element.127.refs_1_), channel_id=1, source_target_pairs={{0,4},{4,8},{8,12},{12,14},{14,10},{10,6},{6,2},{2,0},{1,5},{5,9},... | collective-permute-start | bytes 786440 | tf_op jit(solution)/shard_map/ppermute | solution.py:431
  11.6 0.4 collective-permute-start.5
  12.1 2.2 %copy-done = bf16[32,2,64,512]{3,2,1,0:T(8,128)(2,1)S(1)} copy-done((bf16[32,2,64,512]{3,2,1,0:T(8,128)(2,1)S(1)}, bf16[32,2,64,512]{3,2,1,0:T(8,128)(2,1)}, u32[]{:S(2)}) %copy-start) | copy-done | bytes 4194328
  14.3 0.9 copy-done.3
  15.2 1.8 %shard_map.78 = (f32[2,512,128]{2,1,0:T(8,128)S(1)}, bf16[2,16,128]{2,1,0:T(8,128)(2,1)S(1)}) custom-call(s32[1,128]{1,0:T(1,128)S(1)} %fusion.refs_0_, bf16[64,2176]{1,0:T(8,128)(2,1)S(1)} %get-tuple-element.75.refs_1_, bf16[2,64,512]{2,1,0:T(8,128)(2,1)S(1)} %bitcast.2, bf16[32,2,64,512]{3,2,1,0:T(8,128)(2,1)S(1)} %copy-done), custom_call_target="tpu_custom_call" | custom-call | flops 8589934592 | bytes 20971520 | tf_op jit(solution)/shard_map/pallas_call | solution.py:250
  17.0 0.6 collective-permute-done.refs_1_
  17.6 1.6 %collective-permute-start.2 = (bf16[64,2176]{1,0:T(8,128)(2,1)S(1)}, bf16[64,2176]{1,0:T(8,128)(2,1)S(1)}, u32[]{:S(2)}, u32[]{:S(2)}) collective-permute-start(bf16[64,2176]{1,0:T(8,128)(2,1)S(1)} %collective-permute-done.refs_1_), channel_id=1, source_target_pairs={{0,4},{4,8},{8,12},{12,14},{14,10},{10,6},{6,2},{2,0},{1,5},{5,9},... | collective-permute-start | bytes 835592 | tf_op jit(solution)/shard_map/ppermute | solution.py:456
  19.2 0.5 collective-permute-start.7
  19.7 2.3 %shard_map.79 = (f32[2,512,128]{2,1,0:T(8,128)S(1)}, bf16[2,16,128]{2,1,0:T(8,128)(2,1)S(1)}, f32[2,512,128]{2,1,0:T(8,128)S(1)}, bf16[2,16,128]{2,1,0:T(8,128)(2,1)S(1)}) custom-call(s32[2,128]{1,0:T(2,128)S(1)} %maximum_convert_fusion.refs_0_, bf16[64,2176]{1,0:T(8,128)(2,1)S(1)} %collective-permute-done.refs_1_, ...), custom_call_target="tpu_custom_call" | custom-call | flops 1073741824 | bytes 2621440 | tf_op jit(solution)/shard_map/pallas_call | solution.py:250
  22.0 1.2 %collective-permute-done.4.refs_1_ = bf16[64,2048]{1,0:T(8,128)(2,1)S(1)} collective-permute-done((bf16[64,2048]{1,0:T(8,128)(2,1)S(1)}, bf16[64,2048]{1,0:T(8,128)(2,1)S(1)}, u32[]{:S(2)}, u32[]{:S(2)}) %collective-permute-start.4) | collective-permute-done | bytes 262176 | tf_op jit(solution)/shard_map/ppermute | solution.py:431
  23.2 1.6 %collective-permute-done.5.refs_2_ = bf16[64,2048]{1,0:T(8,128)(2,1)S(1)} collective-permute-done((bf16[64,2048]{1,0:T(8,128)(2,1)S(1)}, bf16[64,2048]{1,0:T(8,128)(2,1)S(1)}, u32[]{:S(2)}, u32[]{:S(2)}) %collective-permute-start.5) | collective-permute-done | bytes 262176 | tf_op jit(solution)/shard_map/ppermute | solution.py:431
  24.8 2.0 %collective-permute-start.9 = (bf16[64,2048]{1,0:T(8,128)(2,1)S(1)}, bf16[64,2048]{1,0:T(8,128)(2,1)S(1)}, u32[]{:S(2)}, u32[]{:S(2)}) collective-permute-start(bf16[64,2048]{1,0:T(8,128)(2,1)S(1)} %collective-permute-done.5.refs_2_), channel_id=1, source_target_pairs={{0,2},{4,0},{8,4},{12,8},{14,12},{10,14},{6,10},{2,6},{1,3},{5,1},... | collective-permute-start | bytes 786440 | tf_op jit(solution)/shard_map/ppermute | solution.py:456
  26.8 2.3 %shard_map.80 = (f32[2,512,128]{2,1,0:T(8,128)S(1)}, bf16[2,16,128]{2,1,0:T(8,128)(2,1)S(1)}, f32[2,512,128]{2,1,0:T(8,128)S(1)}, bf16[2,16,128]{2,1,0:T(8,128)(2,1)S(1)}) custom-call(s32[2,128]{1,0:T(2,128)S(1)} %maximum_convert_fusion.refs_0_, bf16[64,2048]{1,0:T(8,128)(2,1)S(1)} %collective-permute-done.4.refs_1_, ...), custom_call_target="tpu_custom_call" | custom-call | flops 1073741824 | bytes 2621440 | tf_op jit(solution)/shard_map/pallas_call | solution.py:250
  29.2 1.6 %collective-permute-start.6 = (bf16[64,2176]{1,0:T(8,128)(2,1)S(1)}, bf16[64,2176]{1,0:T(8,128)(2,1)S(1)}, u32[]{:S(2)}, u32[]{:S(2)}) collective-permute-start(bf16[64,2176]{1,0:T(8,128)(2,1)S(1)} %collective-permute-done.2.refs_1_), channel_id=1, source_target_pairs={{0,4},{4,8},{8,12},{12,14},{14,10},{10,6},{6,2},{2,0},{1,5},{5,9},... | collective-permute-start | bytes 835592 | tf_op jit(solution)/shard_map/ppermute | solution.py:456
  30.8 0.5 collective-permute-start.12
  31.3 2.3 %shard_map.81 = (f32[2,512,128]{2,1,0:T(8,128)S(1)}, bf16[2,16,128]{2,1,0:T(8,128)(2,1)S(1)}, f32[2,512,128]{2,1,0:T(8,128)S(1)}, bf16[2,16,128]{2,1,0:T(8,128)(2,1)S(1)}) custom-call(s32[2,128]{1,0:T(2,128)S(1)} %maximum_convert_fusion.1.refs_0_.lists_ref, bf16[64,2176]{1,0:T(8,128)(2,1)S(1)} %collective-permute-done.2.refs_1_, ...), custom_call_target="tpu_custom_call" | custom-call | flops 1073741824 | bytes 2621440 | tf_op jit(solution)/shard_map/pallas_call | solution.py:250
  33.6 1.2 %collective-permute-done.8.refs_1_ = bf16[64,2048]{1,0:T(8,128)(2,1)S(1)} collective-permute-done((bf16[64,2048]{1,0:T(8,128)(2,1)S(1)}, bf16[64,2048]{1,0:T(8,128)(2,1)S(1)}, u32[]{:S(2)}, u32[]{:S(2)}) %collective-permute-start.8) | collective-permute-done | bytes 262176 | tf_op jit(solution)/shard_map/ppermute | solution.py:456
  34.8 1.6 %collective-permute-done.9.refs_2_ = bf16[64,2048]{1,0:T(8,128)(2,1)S(1)} collective-permute-done((bf16[64,2048]{1,0:T(8,128)(2,1)S(1)}, bf16[64,2048]{1,0:T(8,128)(2,1)S(1)}, u32[]{:S(2)}, u32[]{:S(2)}) %collective-permute-start.9) | collective-permute-done | bytes 262176 | tf_op jit(solution)/shard_map/ppermute | solution.py:456
  36.8 1.6 %collective-permute-start.14 = (bf16[64,2048]{1,0:T(8,128)(2,1)S(1)}, bf16[64,2048]{1,0:T(8,128)(2,1)S(1)}, u32[]{:S(2)}, u32[]{:S(2)}) collective-permute-start(bf16[64,2048]{1,0:T(8,128)(2,1)S(1)} %collective-permute-done.8.refs_1_), channel_id=1, source_target_pairs={{0,4},{4,8},{8,12},{12,14},{14,10},{10,6},{6,2},{2,0},{1,5},{5,9},... | collective-permute-start | bytes 786440 | tf_op jit(solution)/shard_map/ppermute | solution.py:456
  38.4 2.3 %shard_map.82 = (f32[2,512,128]{2,1,0:T(8,128)S(1)}, bf16[2,16,128]{2,1,0:T(8,128)(2,1)S(1)}, f32[2,512,128]{2,1,0:T(8,128)S(1)}, bf16[2,16,128]{2,1,0:T(8,128)(2,1)S(1)}) custom-call(s32[2,128]{1,0:T(2,128)S(1)} %maximum_convert_fusion.1.refs_0_.lists_ref, bf16[64,2048]{1,0:T(8,128)(2,1)S(1)} %collective-permute-done.8.refs_1_, ...), custom_call_target="tpu_custom_call" | custom-call | flops 1073741824 | bytes 2621440 | tf_op jit(solution)/shard_map/pallas_call | solution.py:250
  40.7 1.6 %collective-permute-start.10 = (bf16[64,2176]{1,0:T(8,128)(2,1)S(1)}, bf16[64,2176]{1,0:T(8,128)(2,1)S(1)}, u32[]{:S(2)}, u32[]{:S(2)}) collective-permute-start(bf16[64,2176]{1,0:T(8,128)(2,1)S(1)} %collective-permute-done.6.refs_1_), channel_id=1, source_target_pairs={{0,4},{4,8},{8,12},{12,14},{14,10},{10,6},{6,2},{2,0},{1,5},{5,9},... | collective-permute-start | bytes 835592 | tf_op jit(solution)/shard_map/ppermute | solution.py:456
  42.4 2.3 %shard_map.83 = (f32[2,512,128]{2,1,0:T(8,128)S(1)}, bf16[2,16,128]{2,1,0:T(8,128)(2,1)S(1)}, f32[2,512,128]{2,1,0:T(8,128)S(1)}, bf16[2,16,128]{2,1,0:T(8,128)(2,1)S(1)}) custom-call(s32[2,128]{1,0:T(2,128)S(1)} %maximum_convert_fusion.2.refs_0_, bf16[64,2176]{1,0:T(8,128)(2,1)S(1)} %collective-permute-done.6.refs_1_, ...), custom_call_target="tpu_custom_call" | custom-call | flops 1073741824 | bytes 2621440 | tf_op jit(solution)/shard_map/pallas_call | solution.py:250
  44.7 1.5 %collective-permute-done.11.refs_2_ = bf16[64,2048]{1,0:T(8,128)(2,1)S(1)} collective-permute-done((bf16[64,2048]{1,0:T(8,128)(2,1)S(1)}, bf16[64,2048]{1,0:T(8,128)(2,1)S(1)}, u32[]{:S(2)}, u32[]{:S(2)}) %collective-permute-start.11) | collective-permute-done | bytes 262176 | tf_op jit(solution)/shard_map/ppermute | solution.py:456
  46.7 1.6 %collective-permute-start.17 = (bf16[2,528,128]{2,1,0:T(8,128)(2,1)S(1)}, bf16[2,528,128]{2,1,0:T(8,128)(2,1)S(1)}, u32[]{:S(2)}, u32[]{:S(2)}) collective-permute-start(bf16[2,528,128]{2,1,0:T(8,128)(2,1)S(1)} %shard_map.84), channel_id=1, source_target_pairs={{0,4},{4,8},{8,12},{12,14},{14,10},{10,6},{6,2},{2,0},{1,5},{5,9},... | collective-permute-start | bytes 811016 | tf_op jit(solution)/shard_map/ppermute | solution.py:474
  48.3 2.3 %shard_map.85 = (f32[2,512,128]{2,1,0:T(8,128)S(1)}, bf16[2,16,128]{2,1,0:T(8,128)(2,1)S(1)}, f32[2,512,128]{2,1,0:T(8,128)S(1)}, bf16[2,16,128]{2,1,0:T(8,128)(2,1)S(1)}) custom-call(s32[2,128]{1,0:T(2,128)S(1)} %maximum_convert_fusion.2.refs_0_, bf16[64,2048]{1,0:T(8,128)(2,1)S(1)} %collective-permute-done.14.refs_1_, ...), custom_call_target="tpu_custom_call" | custom-call | flops 1073741824 | bytes 2621440 | tf_op jit(solution)/shard_map/pallas_call | solution.py:250
  50.6 0.5 collective-permute-start.18
  51.1 3.4 %collective-permute-done.13.refs_2_ = bf16[64,2048]{1,0:T(8,128)(2,1)S(1)} collective-permute-done((bf16[64,2048]{1,0:T(8,128)(2,1)S(1)}, bf16[64,2048]{1,0:T(8,128)(2,1)S(1)}, u32[]{:S(2)}, u32[]{:S(2)}) %collective-permute-start.13) | collective-permute-done | bytes 262176 | tf_op jit(solution)/shard_map/ppermute | solution.py:456
  54.5 2.3 %shard_map.87 = (f32[2,512,128]{2,1,0:T(8,128)S(1)}, bf16[2,16,128]{2,1,0:T(8,128)(2,1)S(1)}, f32[2,512,128]{2,1,0:T(8,128)S(1)}, bf16[2,16,128]{2,1,0:T(8,128)(2,1)S(1)}) custom-call(s32[1,128]{1,0:T(1,128)S(1)} %fusion.1.refs_0_, bf16[64,2176]{1,0:T(8,128)(2,1)S(1)} %collective-permute-done.10.refs_1_, ...), custom_call_target="tpu_custom_call" | custom-call | flops 1073741824 | bytes 2621440 | tf_op jit(solution)/shard_map/pallas_call | solution.py:250
  56.8 1.0 %collective-permute-start.15 = (bf16[2,528,128]{2,1,0:T(8,128)(2,1)S(1)}, bf16[2,528,128]{2,1,0:T(8,128)(2,1)S(1)}, u32[]{:S(2)}, u32[]{:S(2)}) collective-permute-start(bf16[2,528,128]{2,1,0:T(8,128)(2,1)S(1)} %shard_map.88), channel_id=1, source_target_pairs={{0,4},{4,8},{8,12},{12,14},{14,10},{10,6},{6,2},{2,0},{1,5},{5,9},... | collective-permute-start | bytes 811016 | tf_op jit(solution)/shard_map/ppermute | solution.py:493
  57.9 1.1 %collective-permute-start.16 = (bf16[2,528,128]{2,1,0:T(8,128)(2,1)S(1)}, bf16[2,528,128]{2,1,0:T(8,128)(2,1)S(1)}, u32[]{:S(2)}, u32[]{:S(2)}) collective-permute-start(bf16[2,528,128]{2,1,0:T(8,128)(2,1)S(1)} %shard_map.89), channel_id=1, source_target_pairs={{0,2},{4,0},{8,4},{12,8},{14,12},{10,14},{6,10},{2,6},{1,3},{5,1},... | collective-permute-start | bytes 811016 | tf_op jit(solution)/shard_map/ppermute | solution.py:493
  59.0 0.6 shard_map.90
  59.7 0.6 shard_map.91
  60.3 1.0 %collective-permute-start.21 = (bf16[2,528,128]{2,1,0:T(8,128)(2,1)S(1)}, bf16[2,528,128]{2,1,0:T(8,128)(2,1)S(1)}, u32[]{:S(2)}, u32[]{:S(2)}) collective-permute-start(bf16[2,528,128]{2,1,0:T(8,128)(2,1)S(1)} %shard_map.90), channel_id=1, source_target_pairs={{0,4},{4,8},{8,12},{12,14},{14,10},{10,6},{6,2},{2,0},{1,5},{5,9},... | collective-permute-start | bytes 811016 | tf_op jit(solution)/shard_map/ppermute | solution.py:493
  61.3 1.0 %collective-permute-start.22 = (bf16[2,528,128]{2,1,0:T(8,128)(2,1)S(1)}, bf16[2,528,128]{2,1,0:T(8,128)(2,1)S(1)}, u32[]{:S(2)}, u32[]{:S(2)}) collective-permute-start(bf16[2,528,128]{2,1,0:T(8,128)(2,1)S(1)} %shard_map.91), channel_id=1, source_target_pairs={{0,2},{4,0},{8,4},{12,8},{14,12},{10,14},{6,10},{2,6},{1,3},{5,1},... | collective-permute-start | bytes 811016 | tf_op jit(solution)/shard_map/ppermute | solution.py:493
  62.4 3.0 %collective-permute-done.15.in_ref = bf16[2,528,128]{2,1,0:T(8,128)(2,1)S(1)} collective-permute-done((bf16[2,528,128]{2,1,0:T(8,128)(2,1)S(1)}, bf16[2,528,128]{2,1,0:T(8,128)(2,1)S(1)}, u32[]{:S(2)}, u32[]{:S(2)}) %collective-permute-start.15) | collective-permute-done | bytes 270368 | tf_op jit(solution)/shard_map/ppermute | solution.py:493
  65.4 0.5 collective-permute-done.16.in_ref
  65.9 0.6 shard_map.92
  66.5 2.2 %collective-permute-start.19 = (bf16[2,528,128]{2,1,0:T(8,128)(2,1)S(1)}, bf16[2,528,128]{2,1,0:T(8,128)(2,1)S(1)}, u32[]{:S(2)}, u32[]{:S(2)}) collective-permute-start(bf16[2,528,128]{2,1,0:T(8,128)(2,1)S(1)} %shard_map.92), channel_id=1, source_target_pairs={{0,4},{4,8},{8,12},{12,14},{14,10},{10,6},{6,2},{2,0},{1,5},{5,9},... | collective-permute-start | bytes 811016 | tf_op jit(solution)/shard_map/ppermute | solution.py:493
  68.8 0.6 shard_map.93
  69.5 1.7 %collective-permute-done.21.in_ref = bf16[2,528,128]{2,1,0:T(8,128)(2,1)S(1)} collective-permute-done((bf16[2,528,128]{2,1,0:T(8,128)(2,1)S(1)}, bf16[2,528,128]{2,1,0:T(8,128)(2,1)S(1)}, u32[]{:S(2)}, u32[]{:S(2)}) %collective-permute-start.21) | collective-permute-done | bytes 270368 | tf_op jit(solution)/shard_map/ppermute | solution.py:493
  71.2 0.5 collective-permute-done.22.in_ref
  71.7 0.6 shard_map.94
  72.3 2.2 %collective-permute-start.25 = (bf16[2,528,128]{2,1,0:T(8,128)(2,1)S(1)}, bf16[2,528,128]{2,1,0:T(8,128)(2,1)S(1)}, u32[]{:S(2)}, u32[]{:S(2)}) collective-permute-start(bf16[2,528,128]{2,1,0:T(8,128)(2,1)S(1)} %shard_map.94), channel_id=1, source_target_pairs={{0,4},{4,8},{8,12},{12,14},{14,10},{10,6},{6,2},{2,0},{1,5},{5,9},... | collective-permute-start | bytes 811016 | tf_op jit(solution)/shard_map/ppermute | solution.py:493
  74.5 0.6 shard_map.95
  75.3 3.3 %shard_map.96 = (f32[2,512,128]{2,1,0:T(8,128)S(1)}, bf16[2,16,128]{2,1,0:T(8,128)(2,1)S(1)}, bf16[32,2,64,512]{3,2,1,0:T(8,128)(2,1)}) custom-call(s32[1,128]{1,0:T(1,128)S(1)} %fusion.refs_0_, bf16[64,2048]{1,0:T(8,128)(2,1)S(1)} %get-tuple-element.127.refs_1_, bf16[2,64,512]{2,1,0:T(8,128)(2,1)S(1)} %bitcast.3, bf16[32,2,64,512]{3,2,1,0:T(8,128)(2,1)S(1)} %copy-done.1), custom_call_target="tpu_custom_call" | custom-call | flops 536870912 | bytes 1310720 | tf_op jit(solution)/shard_map/pallas_call | solution.py:250
  78.6 0.6 shard_map.97
  79.2 2.1 %collective-permute-start.23 = (bf16[2,528,128]{2,1,0:T(8,128)(2,1)S(1)}, bf16[2,528,128]{2,1,0:T(8,128)(2,1)S(1)}, u32[]{:S(2)}, u32[]{:S(2)}) collective-permute-start(bf16[2,528,128]{2,1,0:T(8,128)(2,1)S(1)} %shard_map.97), channel_id=1, source_target_pairs={{0,4},{4,8},{8,12},{12,14},{14,10},{10,6},{6,2},{2,0},{1,5},{5,9},... | collective-permute-start | bytes 811016 | tf_op jit(solution)/shard_map/ppermute | solution.py:493
  81.3 0.6 shard_map.98
  82.0 4.5 %collective-permute-done.23.in_ref = bf16[2,528,128]{2,1,0:T(8,128)(2,1)S(1)} collective-permute-done((bf16[2,528,128]{2,1,0:T(8,128)(2,1)S(1)}, bf16[2,528,128]{2,1,0:T(8,128)(2,1)S(1)}, u32[]{:S(2)}, u32[]{:S(2)}) %collective-permute-start.23) | collective-permute-done | bytes 270368 | tf_op jit(solution)/shard_map/ppermute | solution.py:493
  86.5 1.9 %collective-permute-done.24.in_ref = bf16[2,528,128]{2,1,0:T(8,128)(2,1)S(1)} collective-permute-done((bf16[2,528,128]{2,1,0:T(8,128)(2,1)S(1)}, bf16[2,528,128]{2,1,0:T(8,128)(2,1)S(1)}, u32[]{:S(2)}, u32[]{:S(2)}) %collective-permute-start.24) | collective-permute-done | bytes 270368 | tf_op jit(solution)/shard_map/ppermute | solution.py:493
  88.4 0.6 shard_map.99
  89.3 0.6 shard_map.100
  90.0 1.9 %collective-permute-start.28 = (bf16[2,528,128]{2,1,0:T(8,128)(2,1)S(1)}, bf16[2,528,128]{2,1,0:T(8,128)(2,1)S(1)}, u32[]{:S(2)}, u32[]{:S(2)}) collective-permute-start(bf16[2,528,128]{2,1,0:T(8,128)(2,1)S(1)} %shard_map.100), channel_id=1, source_target_pairs={{0,4},{4,8},{8,12},{12,14},{14,10},{10,6},{6,2},{2,0},{1,5},{5,9},... | collective-permute-start | bytes 811016 | tf_op jit(solution)/shard_map/ppermute | solution.py:493
  91.8 1.2 %shard_map.104 = bf16[32,2,64,512]{3,2,1,0:T(8,128)(2,1)} custom-call(s32[1]{0:T(128)} %bitcast.1.me_ref, s32[2,128]{1,0:T(2,128)S(1)} %maximum_convert_fusion.1.refs_0_.lists_ref, bf16[1,2,64,512]{3,2,1,0:T(8,128)(2,1)S(1)} %collective-permute-done.1.page_ref, bf16[32,2,64,512]{3,2,1,0:T(8,128)(2,1)} %get-tuple-element.145.old_ref), custom_call_target="tpu_custom_call", output_to_operand_aliasing={{}: (3, {})} | custom-call | flops 1 | bytes 1 | tf_op jit(solution)/shard_map/pallas_call | solution.py:276
  93.1 0.6 shard_map.101
  93.7 0.6 shard_map.102
  94.4 1.2 %collective-permute-done.27.refs_0_ = bf16[2,528,128]{2,1,0:T(8,128)(2,1)S(1)} collective-permute-done((bf16[2,528,128]{2,1,0:T(8,128)(2,1)S(1)}, bf16[2,528,128]{2,1,0:T(8,128)(2,1)S(1)}, u32[]{:S(2)}, u32[]{:S(2)}) %collective-permute-start.27) | collective-permute-done | bytes 270368 | tf_op jit(solution)/shard_map/ppermute | solution.py:493
  95.6 1.1 %collective-permute-done.28.refs_3_ = bf16[2,528,128]{2,1,0:T(8,128)(2,1)S(1)} collective-permute-done((bf16[2,528,128]{2,1,0:T(8,128)(2,1)S(1)}, bf16[2,528,128]{2,1,0:T(8,128)(2,1)S(1)}, u32[]{:S(2)}, u32[]{:S(2)}) %collective-permute-start.28) | collective-permute-done | bytes 270368 | tf_op jit(solution)/shard_map/ppermute | solution.py:493
  96.6 1.7 %shard_map.103 = bf16[1,64,4096]{2,1,0:T(8,128)(2,1)} custom-call(bf16[2,528,128]{2,1,0:T(8,128)(2,1)S(1)} %collective-permute-done.27.refs_0_, f32[2,512,128]{2,1,0:T(8,128)S(1)} %get-tuple-element.137.refs_1_, bf16[2,16,128]{2,1,0:T(8,128)(2,1)S(1)} %get-tuple-element.138.refs_2_, bf16[2,528,128]{2,1,0:T(8,128)(2,1)S(1)} %collective-permute-done.28.refs_3_, ...), custom_call_target="tpu_custom_call" | custom-call | flops 1605632 | bytes 3211264 | tf_op jit(solution)/shard_map/pallas_call | solution.py:348
  (45 shorter events, 2.0 us)
Async XLA Ops:
  0.6 11.5 %collective-permute-start.1 = (bf16[1,2,64,512]{3,2,1,0:T(8,128)(2,1)}, bf16[1,2,64,512]{3,2,1,0:T(8,128)(2,1)S(1)}, u32[]{:S(2)}, u32[]{:S(2)}) collective-permute-start(bf16[1,2,64,512]{3,2,1,0:T(8,128)(2,1)} %param.7), channel_id=1, source_target_pairs={{8,0},{10,2},{12,4},{14,6},{0,8},{2,10},{4,12},{6,14},{9,1},{11,3}... | collective-permute-start | bytes 393224 | tf_op jit(solution)/shard_map/ppermute | solution.py:25
  6.0 1.0 %copy-start.2 = (bf16[1,64,4096]{2,1,0:T(8,128)(2,1)S(1)}, bf16[1,64,4096]{2,1,0:T(8,128)(2,1)}, u32[]{:S(2)}) copy-start(bf16[1,64,4096]{2,1,0:T(8,128)(2,1)} %q_ref.1) | copy-start | bytes 1572868
  7.1 0.7 copy-start.5
  8.0 9.6 %collective-permute-start = (bf16[64,2176]{1,0:T(8,128)(2,1)S(1)}, bf16[64,2176]{1,0:T(8,128)(2,1)S(1)}, u32[]{:S(2)}, u32[]{:S(2)}) collective-permute-start(bf16[64,2176]{1,0:T(8,128)(2,1)S(1)} %get-tuple-element.75.refs_1_), channel_id=1, source_target_pairs={{0,4},{4,8},{8,12},{12,14},{14,10},{10,6},{6,2},{2,0},{1,5},{5,9},... | collective-permute-start | bytes 835592 | tf_op jit(solution)/shard_map/ppermute | solution.py:431
  9.6 9.6 %collective-permute-start.3 = (bf16[64,2176]{1,0:T(8,128)(2,1)S(1)}, bf16[64,2176]{1,0:T(8,128)(2,1)S(1)}, u32[]{:S(2)}, u32[]{:S(2)}) collective-permute-start(bf16[64,2176]{1,0:T(8,128)(2,1)S(1)} %get-tuple-element.75.refs_1_), channel_id=1, source_target_pairs={{0,2},{4,0},{8,4},{12,8},{14,12},{10,14},{6,10},{2,6},{1,3},{5,1},... | collective-permute-start | bytes 835592 | tf_op jit(solution)/shard_map/ppermute | solution.py:431
  10.0 13.2 %collective-permute-start.4 = (bf16[64,2048]{1,0:T(8,128)(2,1)S(1)}, bf16[64,2048]{1,0:T(8,128)(2,1)S(1)}, u32[]{:S(2)}, u32[]{:S(2)}) collective-permute-start(bf16[64,2048]{1,0:T(8,128)(2,1)S(1)} %get-tuple-element.127.refs_1_), channel_id=1, source_target_pairs={{0,4},{4,8},{8,12},{12,14},{14,10},{10,6},{6,2},{2,0},{1,5},{5,9},... | collective-permute-start | bytes 786440 | tf_op jit(solution)/shard_map/ppermute | solution.py:431
  11.6 13.2 %collective-permute-start.5 = (bf16[64,2048]{1,0:T(8,128)(2,1)S(1)}, bf16[64,2048]{1,0:T(8,128)(2,1)S(1)}, u32[]{:S(2)}, u32[]{:S(2)}) collective-permute-start(bf16[64,2048]{1,0:T(8,128)(2,1)S(1)} %get-tuple-element.127.refs_1_), channel_id=1, source_target_pairs={{0,2},{4,0},{8,4},{12,8},{14,12},{10,14},{6,10},{2,6},{1,3},{5,1},... | collective-permute-start | bytes 786440 | tf_op jit(solution)/shard_map/ppermute | solution.py:431
  12.1 2.2 %copy-start = (bf16[32,2,64,512]{3,2,1,0:T(8,128)(2,1)S(1)}, bf16[32,2,64,512]{3,2,1,0:T(8,128)(2,1)}, u32[]{:S(2)}) copy-start(bf16[32,2,64,512]{3,2,1,0:T(8,128)(2,1)} %refs_3_.17) | copy-start | bytes 12582916
  14.3 0.9 copy-start.3
  15.2 4.5 %copy-start.1 = (bf16[32,2,64,512]{3,2,1,0:T(8,128)(2,1)S(1)}, bf16[32,2,64,512]{3,2,1,0:T(8,128)(2,1)}, u32[]{:S(2)}) copy-start(bf16[32,2,64,512]{3,2,1,0:T(8,128)(2,1)} %refs_3_.17) | copy-start | bytes 12582916
  17.6 11.6 %collective-permute-start.2 = (bf16[64,2176]{1,0:T(8,128)(2,1)S(1)}, bf16[64,2176]{1,0:T(8,128)(2,1)S(1)}, u32[]{:S(2)}, u32[]{:S(2)}) collective-permute-start(bf16[64,2176]{1,0:T(8,128)(2,1)S(1)} %collective-permute-done.refs_1_), channel_id=1, source_target_pairs={{0,4},{4,8},{8,12},{12,14},{14,10},{10,6},{6,2},{2,0},{1,5},{5,9},... | collective-permute-start | bytes 835592 | tf_op jit(solution)/shard_map/ppermute | solution.py:456
  19.2 11.6 %collective-permute-start.7 = (bf16[64,2176]{1,0:T(8,128)(2,1)S(1)}, bf16[64,2176]{1,0:T(8,128)(2,1)S(1)}, u32[]{:S(2)}, u32[]{:S(2)}) collective-permute-start(bf16[64,2176]{1,0:T(8,128)(2,1)S(1)} %collective-permute-done.3.refs_2_), channel_id=1, source_target_pairs={{0,2},{4,0},{8,4},{12,8},{14,12},{10,14},{6,10},{2,6},{1,3},{5,1},... | collective-permute-start | bytes 835592 | tf_op jit(solution)/shard_map/ppermute | solution.py:456
  24.8 10.0 %collective-permute-start.8 = (bf16[64,2048]{1,0:T(8,128)(2,1)S(1)}, bf16[64,2048]{1,0:T(8,128)(2,1)S(1)}, u32[]{:S(2)}, u32[]{:S(2)}) collective-permute-start(bf16[64,2048]{1,0:T(8,128)(2,1)S(1)} %collective-permute-done.4.refs_1_), channel_id=1, source_target_pairs={{0,4},{4,8},{8,12},{12,14},{14,10},{10,6},{6,2},{2,0},{1,5},{5,9},... | collective-permute-start | bytes 786440 | tf_op jit(solution)/shard_map/ppermute | solution.py:456
  24.8 11.6 %collective-permute-start.9 = (bf16[64,2048]{1,0:T(8,128)(2,1)S(1)}, bf16[64,2048]{1,0:T(8,128)(2,1)S(1)}, u32[]{:S(2)}, u32[]{:S(2)}) collective-permute-start(bf16[64,2048]{1,0:T(8,128)(2,1)S(1)} %collective-permute-done.5.refs_2_), channel_id=1, source_target_pairs={{0,2},{4,0},{8,4},{12,8},{14,12},{10,14},{6,10},{2,6},{1,3},{5,1},... | collective-permute-start | bytes 786440 | tf_op jit(solution)/shard_map/ppermute | solution.py:456
  29.2 11.5 %collective-permute-start.6 = (bf16[64,2176]{1,0:T(8,128)(2,1)S(1)}, bf16[64,2176]{1,0:T(8,128)(2,1)S(1)}, u32[]{:S(2)}, u32[]{:S(2)}) collective-permute-start(bf16[64,2176]{1,0:T(8,128)(2,1)S(1)} %collective-permute-done.2.refs_1_), channel_id=1, source_target_pairs={{0,4},{4,8},{8,12},{12,14},{14,10},{10,6},{6,2},{2,0},{1,5},{5,9},... | collective-permute-start | bytes 835592 | tf_op jit(solution)/shard_map/ppermute | solution.py:456
  30.8 11.6 %collective-permute-start.12 = (bf16[64,2176]{1,0:T(8,128)(2,1)S(1)}, bf16[64,2176]{1,0:T(8,128)(2,1)S(1)}, u32[]{:S(2)}, u32[]{:S(2)}) collective-permute-start(bf16[64,2176]{1,0:T(8,128)(2,1)S(1)} %collective-permute-done.7.refs_2_), channel_id=1, source_target_pairs={{0,2},{4,0},{8,4},{12,8},{14,12},{10,14},{6,10},{2,6},{1,3},{5,1},... | collective-permute-start | bytes 835592 | tf_op jit(solution)/shard_map/ppermute | solution.py:456
  36.4 9.8 %collective-permute-start.11 = (bf16[64,2048]{1,0:T(8,128)(2,1)S(1)}, bf16[64,2048]{1,0:T(8,128)(2,1)S(1)}, u32[]{:S(2)}, u32[]{:S(2)}) collective-permute-start(bf16[64,2048]{1,0:T(8,128)(2,1)S(1)} %collective-permute-done.9.refs_2_), channel_id=1, source_target_pairs={{0,2},{4,0},{8,4},{12,8},{14,12},{10,14},{6,10},{2,6},{1,3},{5,1},... | collective-permute-start | bytes 786440 | tf_op jit(solution)/shard_map/ppermute | solution.py:456
  36.8 11.4 %collective-permute-start.14 = (bf16[64,2048]{1,0:T(8,128)(2,1)S(1)}, bf16[64,2048]{1,0:T(8,128)(2,1)S(1)}, u32[]{:S(2)}, u32[]{:S(2)}) collective-permute-start(bf16[64,2048]{1,0:T(8,128)(2,1)S(1)} %collective-permute-done.8.refs_1_), channel_id=1, source_target_pairs={{0,4},{4,8},{8,12},{12,14},{14,10},{10,6},{6,2},{2,0},{1,5},{5,9},... | collective-permute-start | bytes 786440 | tf_op jit(solution)/shard_map/ppermute | solution.py:456
  40.7 13.8 %collective-permute-start.10 = (bf16[64,2176]{1,0:T(8,128)(2,1)S(1)}, bf16[64,2176]{1,0:T(8,128)(2,1)S(1)}, u32[]{:S(2)}, u32[]{:S(2)}) collective-permute-start(bf16[64,2176]{1,0:T(8,128)(2,1)S(1)} %collective-permute-done.6.refs_1_), channel_id=1, source_target_pairs={{0,4},{4,8},{8,12},{12,14},{14,10},{10,6},{6,2},{2,0},{1,5},{5,9},... | collective-permute-start | bytes 835592 | tf_op jit(solution)/shard_map/ppermute | solution.py:456
  46.2 8.3 %collective-permute-start.13 = (bf16[64,2048]{1,0:T(8,128)(2,1)S(1)}, bf16[64,2048]{1,0:T(8,128)(2,1)S(1)}, u32[]{:S(2)}, u32[]{:S(2)}) collective-permute-start(bf16[64,2048]{1,0:T(8,128)(2,1)S(1)} %collective-permute-done.11.refs_2_), channel_id=1, source_target_pairs={{0,2},{4,0},{8,4},{12,8},{14,12},{10,14},{6,10},{2,6},{1,3},{5,1},... | collective-permute-start | bytes 786440 | tf_op jit(solution)/shard_map/ppermute | solution.py:456
  46.7 12.3 %collective-permute-start.17 = (bf16[2,528,128]{2,1,0:T(8,128)(2,1)S(1)}, bf16[2,528,128]{2,1,0:T(8,128)(2,1)S(1)}, u32[]{:S(2)}, u32[]{:S(2)}) collective-permute-start(bf16[2,528,128]{2,1,0:T(8,128)(2,1)S(1)} %shard_map.84), channel_id=1, source_target_pairs={{0,4},{4,8},{8,12},{12,14},{14,10},{10,6},{6,2},{2,0},{1,5},{5,9},... | collective-permute-start | bytes 811016 | tf_op jit(solution)/shard_map/ppermute | solution.py:474
  50.6 8.4 %collective-permute-start.18 = (bf16[2,528,128]{2,1,0:T(8,128)(2,1)S(1)}, bf16[2,528,128]{2,1,0:T(8,128)(2,1)S(1)}, u32[]{:S(2)}, u32[]{:S(2)}) collective-permute-start(bf16[2,528,128]{2,1,0:T(8,128)(2,1)S(1)} %shard_map.86), channel_id=1, source_target_pairs={{0,2},{4,0},{8,4},{12,8},{14,12},{10,14},{6,10},{2,6},{1,3},{5,1},... | collective-permute-start | bytes 811016 | tf_op jit(solution)/shard_map/ppermute | solution.py:474
  56.8 18.5 %copy-start.4 = (bf16[1,2,64,512]{3,2,1,0:T(8,128)(2,1)S(1)}, bf16[1,2,64,512]{3,2,1,0:T(8,128)(2,1)}, u32[]{:S(2)}) copy-start(bf16[1,2,64,512]{3,2,1,0:T(8,128)(2,1)} %param.7) | copy-start | bytes 393220
  56.8 8.5 %collective-permute-start.15 = (bf16[2,528,128]{2,1,0:T(8,128)(2,1)S(1)}, bf16[2,528,128]{2,1,0:T(8,128)(2,1)S(1)}, u32[]{:S(2)}, u32[]{:S(2)}) collective-permute-start(bf16[2,528,128]{2,1,0:T(8,128)(2,1)S(1)} %shard_map.88), channel_id=1, source_target_pairs={{0,4},{4,8},{8,12},{12,14},{14,10},{10,6},{6,2},{2,0},{1,5},{5,9},... | collective-permute-start | bytes 811016 | tf_op jit(solution)/shard_map/ppermute | solution.py:493
  57.9 8.0 %collective-permute-start.16 = (bf16[2,528,128]{2,1,0:T(8,128)(2,1)S(1)}, bf16[2,528,128]{2,1,0:T(8,128)(2,1)S(1)}, u32[]{:S(2)}, u32[]{:S(2)}) collective-permute-start(bf16[2,528,128]{2,1,0:T(8,128)(2,1)S(1)} %shard_map.89), channel_id=1, source_target_pairs={{0,2},{4,0},{8,4},{12,8},{14,12},{10,14},{6,10},{2,6},{1,3},{5,1},... | collective-permute-start | bytes 811016 | tf_op jit(solution)/shard_map/ppermute | solution.py:493
  60.3 10.9 %collective-permute-start.21 = (bf16[2,528,128]{2,1,0:T(8,128)(2,1)S(1)}, bf16[2,528,128]{2,1,0:T(8,128)(2,1)S(1)}, u32[]{:S(2)}, u32[]{:S(2)}) collective-permute-start(bf16[2,528,128]{2,1,0:T(8,128)(2,1)S(1)} %shard_map.90), channel_id=1, source_target_pairs={{0,4},{4,8},{8,12},{12,14},{14,10},{10,6},{6,2},{2,0},{1,5},{5,9},... | collective-permute-start | bytes 811016 | tf_op jit(solution)/shard_map/ppermute | solution.py:493
  61.3 10.3 %collective-permute-start.22 = (bf16[2,528,128]{2,1,0:T(8,128)(2,1)S(1)}, bf16[2,528,128]{2,1,0:T(8,128)(2,1)S(1)}, u32[]{:S(2)}, u32[]{:S(2)}) collective-permute-start(bf16[2,528,128]{2,1,0:T(8,128)(2,1)S(1)} %shard_map.91), channel_id=1, source_target_pairs={{0,2},{4,0},{8,4},{12,8},{14,12},{10,14},{6,10},{2,6},{1,3},{5,1},... | collective-permute-start | bytes 811016 | tf_op jit(solution)/shard_map/ppermute | solution.py:493
  66.5 12.0 %collective-permute-start.19 = (bf16[2,528,128]{2,1,0:T(8,128)(2,1)S(1)}, bf16[2,528,128]{2,1,0:T(8,128)(2,1)S(1)}, u32[]{:S(2)}, u32[]{:S(2)}) collective-permute-start(bf16[2,528,128]{2,1,0:T(8,128)(2,1)S(1)} %shard_map.92), channel_id=1, source_target_pairs={{0,4},{4,8},{8,12},{12,14},{14,10},{10,6},{6,2},{2,0},{1,5},{5,9},... | collective-permute-start | bytes 811016 | tf_op jit(solution)/shard_map/ppermute | solution.py:493
  69.4 9.2 %collective-permute-start.20 = (bf16[2,528,128]{2,1,0:T(8,128)(2,1)S(1)}, bf16[2,528,128]{2,1,0:T(8,128)(2,1)S(1)}, u32[]{:S(2)}, u32[]{:S(2)}) collective-permute-start(bf16[2,528,128]{2,1,0:T(8,128)(2,1)S(1)} %shard_map.93), channel_id=1, source_target_pairs={{0,2},{4,0},{8,4},{12,8},{14,12},{10,14},{6,10},{2,6},{1,3},{5,1},... | collective-permute-start | bytes 811016 | tf_op jit(solution)/shard_map/ppermute | solution.py:493
  72.3 9.7 %collective-permute-start.25 = (bf16[2,528,128]{2,1,0:T(8,128)(2,1)S(1)}, bf16[2,528,128]{2,1,0:T(8,128)(2,1)S(1)}, u32[]{:S(2)}, u32[]{:S(2)}) collective-permute-start(bf16[2,528,128]{2,1,0:T(8,128)(2,1)S(1)} %shard_map.94), channel_id=1, source_target_pairs={{0,4},{4,8},{8,12},{12,14},{14,10},{10,6},{6,2},{2,0},{1,5},{5,9},... | collective-permute-start | bytes 811016 | tf_op jit(solution)/shard_map/ppermute | solution.py:493
  75.2 6.8 %collective-permute-start.26 = (bf16[2,528,128]{2,1,0:T(8,128)(2,1)S(1)}, bf16[2,528,128]{2,1,0:T(8,128)(2,1)S(1)}, u32[]{:S(2)}, u32[]{:S(2)}) collective-permute-start(bf16[2,528,128]{2,1,0:T(8,128)(2,1)S(1)} %shard_map.95), channel_id=1, source_target_pairs={{0,2},{4,0},{8,4},{12,8},{14,12},{10,14},{6,10},{2,6},{1,3},{5,1},... | collective-permute-start | bytes 811016 | tf_op jit(solution)/shard_map/ppermute | solution.py:493
  79.2 7.3 %collective-permute-start.23 = (bf16[2,528,128]{2,1,0:T(8,128)(2,1)S(1)}, bf16[2,528,128]{2,1,0:T(8,128)(2,1)S(1)}, u32[]{:S(2)}, u32[]{:S(2)}) collective-permute-start(bf16[2,528,128]{2,1,0:T(8,128)(2,1)S(1)} %shard_map.97), channel_id=1, source_target_pairs={{0,4},{4,8},{8,12},{12,14},{14,10},{10,6},{6,2},{2,0},{1,5},{5,9},... | collective-permute-start | bytes 811016 | tf_op jit(solution)/shard_map/ppermute | solution.py:493
  81.9 6.5 %collective-permute-start.24 = (bf16[2,528,128]{2,1,0:T(8,128)(2,1)S(1)}, bf16[2,528,128]{2,1,0:T(8,128)(2,1)S(1)}, u32[]{:S(2)}, u32[]{:S(2)}) collective-permute-start(bf16[2,528,128]{2,1,0:T(8,128)(2,1)S(1)} %shard_map.98), channel_id=1, source_target_pairs={{0,2},{4,0},{8,4},{12,8},{14,12},{10,14},{6,10},{2,6},{1,3},{5,1},... | collective-permute-start | bytes 811016 | tf_op jit(solution)/shard_map/ppermute | solution.py:493
  89.1 6.5 %collective-permute-start.27 = (bf16[2,528,128]{2,1,0:T(8,128)(2,1)S(1)}, bf16[2,528,128]{2,1,0:T(8,128)(2,1)S(1)}, u32[]{:S(2)}, u32[]{:S(2)}) collective-permute-start(bf16[2,528,128]{2,1,0:T(8,128)(2,1)S(1)} %shard_map.99), channel_id=1, source_target_pairs={{0,2},{4,0},{8,4},{12,8},{14,12},{10,14},{6,10},{2,6},{1,3},{5,1},... | collective-permute-start | bytes 811016 | tf_op jit(solution)/shard_map/ppermute | solution.py:493
  90.0 6.7 %collective-permute-start.28 = (bf16[2,528,128]{2,1,0:T(8,128)(2,1)S(1)}, bf16[2,528,128]{2,1,0:T(8,128)(2,1)S(1)}, u32[]{:S(2)}, u32[]{:S(2)}) collective-permute-start(bf16[2,528,128]{2,1,0:T(8,128)(2,1)S(1)} %shard_map.100), channel_id=1, source_target_pairs={{0,4},{4,8},{8,12},{12,14},{14,10},{10,6},{6,2},{2,0},{1,5},{5,9},... | collective-permute-start | bytes 811016 | tf_op jit(solution)/shard_map/ppermute | solution.py:493

commit v10 on v9

--- a/solution.py
+++ b/solution.py
@@ -12,6 +12,7 @@
 DEAD = -1e30
 FLOOR = -1e29
 STAT_ROWS = 16
+LIST_ROWS = 16
 GRANT = 20 * 1024 * 1024
 LIGHT = pl.CostEstimate(flops=1, bytes_accessed=1, transcendentals=0)
 VMEM = pl.BlockSpec(memory_space=pltpu.VMEM)
@@ -186,7 +187,7 @@
     def score(i):
         n, array, first, h, _ = jobs[i]
         q_ref = queries[array]
-        q = jnp.concatenate([q_ref[:, block_of(first * groups + g)] for g in range(groups)], 0)
+        q = q_ref[first * rows:(first + 1) * rows, :]
         scores[i % 2] = dot_nt(q, stacked(n, 0, h))
         if own:
             at = iota((rows, suffix), 0) % suffix
@@ -323,7 +324,8 @@
 
 
 def final_kernel(suffix, *refs):
-    sides, out_ref = (refs[0:3], refs[3:6]), refs[6]
+    sides, (out_ref, done, sems) = (refs[0:3], refs[3:6]), refs[6:]
+    copies = []
     for side, (in_ref, acc_ref, stat_ref) in enumerate(sides):
         heads, rows = acc_ref.shape[:2]
         groups = rows // suffix
@@ -340,7 +342,30 @@
                 out = (acc / total).astype(jnp.bfloat16)
                 for i in range(HEAD_SIZE // suffix):
                     g = (side * heads + h) * groups + j * (HEAD_SIZE // suffix) + i
-                    out_ref[0, :, block_of(g)] = out[i * suffix:(i + 1) * suffix]
+                    done[0, :, block_of(g)] = out[i * suffix:(i + 1) * suffix]
+            head = side * heads + h
+            span = pl.ds(head * groups * HEAD_SIZE, groups * HEAD_SIZE)
+            copies.append(
+                pltpu.make_async_copy(done.at[:, :, span], out_ref.at[:, :, span], sems.at[head])
+            )
+            copies[-1].start()
+    for copy in copies:
+        copy.wait()
+
+
+def finish(suffix, like, *args):
+    heads = sum(x.shape[0] for x in args[1::3])
+    return pl.pallas_call(
+        functools.partial(final_kernel, suffix),
+        out_shape=jax.ShapeDtypeStruct(like.shape, like.dtype),
+        in_specs=[VMEM] * len(args),
+        out_specs=HBM,
+        scratch_shapes=[
+            pltpu.VMEM(like.shape, like.dtype),
+            pltpu.SemaphoreType.DMA((heads,)),
+        ],
+        compiler_params=pltpu.CompilerParams(vmem_limit_bytes=GRANT),
+    )(*args)
 
 
 def call(kernel, shape, *args):
@@ -355,11 +380,15 @@
     )(*args)
 
 
-def prepare_kernel(cut, cap, pages_dev, length_ref, slot_ref, table_ref, q_ref, first_ref, second_ref):
+def prepare_kernel(cap, pages_dev, length_ref, slot_ref, table_ref, q_ref, first_ref, second_ref):
     maxp = table_ref.shape[1]
     suffix = q_ref.shape[1]
-    second_ref[...] = q_ref[0, :, cut:]
-    first_ref[:, :cut] = q_ref[0, :, :cut]
+    rows = second_ref.shape[0]
+    blocks = rows // suffix
+    for g in range(blocks):
+        into = slice(g * suffix, (g + 1) * suffix)
+        first_ref[into, :] = q_ref[0, :, block_of(g)]
+        second_ref[into, :] = q_ref[0, :, block_of(blocks + g)]
     table = table_ref[...]
     owner = lax.div(table, pages_dev)
     local = (table - owner * pages_dev).astype(jnp.float32)
@@ -375,22 +404,22 @@
     live = jnp.where(iota((maxp, HEAD_SIZE), 0) < length_ref[0], 1.0, 0.0)
     ids = jnp.where(rank == place.astype(jnp.float32), turned(local), 0.0)
     fields = jnp.where(place < cap, ids, jnp.where(place == cap, live, 0.0))
-    owned = jnp.where(owner == iota((suffix, maxp), 0).astype(jnp.float32), 1.0, 0.0)
+    owned = jnp.where(owner == iota((LIST_ROWS, maxp), 0).astype(jnp.float32), 1.0, 0.0)
     lists = jnp.dot(
         owned.astype(jnp.bfloat16), fields.astype(jnp.bfloat16), preferred_element_type=jnp.float32
     )
     slot = slot_ref[0].astype(jnp.float32)
     lists = jnp.where(iota(lists.shape, 1) == cap + 1, slot, lists)
-    first_ref[:, cut:] = lists.astype(jnp.bfloat16)
-
-
-def prepare(cut, cap, pages_dev, queries, page_table, prefix_pages, new_slots):
-    suffix, columns = queries.shape[1:]
+    first_ref[rows:, :] = lists.astype(jnp.bfloat16)
+
+
+def prepare(cap, pages_dev, queries, page_table, prefix_pages, new_slots):
+    rows = queries.size // HEAD_SIZE // 2
     return pl.pallas_call(
-        functools.partial(prepare_kernel, cut, cap, pages_dev),
+        functools.partial(prepare_kernel, cap, pages_dev),
         out_shape=[
-            jax.ShapeDtypeStruct((suffix, cut + HEAD_SIZE), queries.dtype),
-            jax.ShapeDtypeStruct((suffix, columns - cut), queries.dtype),
+            jax.ShapeDtypeStruct((rows + LIST_ROWS, HEAD_SIZE), queries.dtype),
+            jax.ShapeDtypeStruct((rows, HEAD_SIZE), queries.dtype),
         ],
         in_specs=[SMEM, SMEM, VMEM, VMEM],
         out_specs=[VMEM, VMEM],
@@ -410,7 +439,7 @@
     half = stores // 2
     me = lax.axis_index("store")
     heads_each = kv_heads // 2
-    cut = heads_each * groups * HEAD_SIZE
+    below = heads_each * groups * suffix
 
     order = list(range(0, stores, 2)) + list(range(1, stores, 2))[::-1]
     up = [(order[i], order[(i + 1) % stores]) for i in range(stores)]
@@ -418,14 +447,14 @@
     routes = {1: up, -1: down}
 
     def listed(*arrays):
-        rows = [lax.dynamic_slice(x, (me, cut), (1, HEAD_SIZE)) for x in arrays]
+        rows = [lax.dynamic_slice(x, (below + me, 0), (1, HEAD_SIZE)) for x in arrays]
         return jnp.concatenate(rows).astype(jnp.int32)
 
     def after(values, token):
         return lax.optimization_barrier((values, token))[0]
 
-    arrived = shifted(suffix_key_value, "store", half)
-    mine = prepare(cut, cap, pages_dev, queries, page_table, prefix_pages, new_slots)
+    mine = prepare(cap, pages_dev, queries, page_table, prefix_pages, new_slots)
+    arrived = shifted(after(suffix_key_value, mine), "store", half)
 
     moving = {
         (side, sign): lax.ppermute(mine[side], "store", routes[sign])
@@ -464,10 +493,14 @@
                 sign = 1 if side == 1 else -1
                 sent["early", sign] = packed(parts[sign * step, side])
                 token = sent["early", sign]
-    came = after([moving[0, 1], moving[1, -1]], token)
-    jobs = [(0, side, h, side * heads_each + h, side) for side in range(2) for h in range(heads_each)]
-    far = attend(shape, jobs, listed(came[0]), came, held)
-    token = far
+    lists, far = None, []
+    for side, sign in ((0, 1), (1, -1)):
+        came = after(moving[side, sign], token)
+        lists = listed(came) if side == 0 else lists
+        jobs = [(0, 0, h, side * heads_each + h, 0) for h in range(heads_each)]
+        part, = attend(shape, jobs, lists, [came], held)
+        far.append(packed(part))
+        token = far
 
     back = {1: down, -1: up}
     side_of = {("late", 1): 0, ("late", -1): 1, ("early", 1): 1, ("early", -1): 0}
@@ -477,7 +510,7 @@
         turns += [("early", distance - 1)] * (distance > 1) + [("late", distance)]
     for flow, distance in turns:
         if distance == half:
-            blocks = {sign: packed(far[side_of[flow, sign]]) for sign in back}
+            blocks = {sign: far[side_of[flow, sign]] for sign in back}
         else:
             came = {sign: flows[flow, sign] for sign in back}
             if distance == 1 and flow == "late":
@@ -492,7 +525,7 @@
         for sign in back:
             flows[flow, sign] = lax.ppermute(blocks[sign], "store", back[sign])
         token = blocks
-        if flow == "early" and distance == 1:
+        if flow == "late" and distance == 2:
             (store,) = attend_own(1, token, True)
             token = [token, store]
     store = place_page(
@@ -503,11 +536,7 @@
         side = side_of["early", sign]
         rest[side] = kept(after(flows["early", sign], token), parts[0, side])
         late[1 - side] = flows["late", sign]
-    attended = call(
-        functools.partial(final_kernel, suffix),
-        jax.ShapeDtypeStruct(queries.shape, queries.dtype),
-        late[0], *rest[0], late[1], *rest[1],
-    )
+    attended = finish(suffix, queries, late[0], *rest[0], late[1], *rest[1])
     return (attended, store)
 
 
@@ -533,7 +562,7 @@
     pulled = page_table.shape[1] // stores * kv_pages[0].size
     pushed = 2 * queries[0].size
     arrays = (queries, suffix_key_value, kv_pages, page_table, prefix_pages, new_slots)
-    if pulled >= pushed and stores % 8 == 0:
+    if pulled >= pushed and stores % 8 == 0 and stores <= LIST_ROWS:
         return queries_travel(*arrays)
     return pages_travel(*arrays)
 

time: 98.9 us -> 103 us (1.041)
  starting transfers between devices: 33.6 us -> 41 us
  waiting for transfers between devices: 25.7 us -> 21.5 us
    ppermute x10, waiting for transfers between devices: 7.81 us -> 3.34 us  [queries_travel(): moving[side, sign] = lax.ppermute(came[sign], 'store', routes[sign])]
    ppermute x2, starting transfers between devices: 2.08 us -> 5.67 us  [queries_travel(): lax.ppermute(block, 'store', back[key[1]])]
    ppermute x4, waiting for transfers between devices: 3.45 us -> 0.01 us  [queries_travel(): lax.ppermute(mine[side], 'store', routes[sign])]
    ppermute x1, waiting for transfers between devices: 0.01 us -> 3.29 us  [shifted(): return lax.ppermute(block, axis, route)]
    ppermute x10, starting transfers between devices: 10.3 us -> 13.1 us  [queries_travel(): moving[side, sign] = lax.ppermute(came[sign], 'store', routes[sign])]
    pallas_call x17 -> x16, Pallas kernels: 9.42 us -> 7.75 us  [call(): pl.pallas_call(kernel, out_shape=shape, in_specs=[VMEM] * len(args), out_...]
    pallas_call x1 -> x2, Pallas kernels: 0.29 us -> 1.91 us  [the longest x1 1.62 us: finish(): pl.pallas_call(functools.partial(final_kernel, suffix), out_shape=jax.Sha...]
    ppermute x12, starting transfers between devices: 13.1 us -> 14.1 us  [queries_travel(): flows[flow, sign] = lax.ppermute(blocks[sign], 'store', back[sign])]
  transfers between devices with their start and end apart: 29 -> 29, of which waited for: 16 -> 14; matrix products, arithmetic and copies ran while one was open for 0% -> 0% of each run, Pallas kernels for 30% -> 29%
where the time goes in v10:
time: 103 us; the launch traced here: 102 us
  starting transfers between devices  41 us (40%)
  Pallas kernels  32.6 us (32%)
  waiting for transfers between devices  21.5 us (21%)
  local copies, waits for them, and re-layouts  4.86 us (5%)
  between operations  2.45 us (2%)
    pallas_call x10, Pallas kernels, attend(): pl.pallas_call(functools.partial(attend_kernel, shape + (len(queries), ow...  21.7 us
    ppermute x12, starting transfers between devices, queries_travel(): flows[flow, sign] = lax.ppermute(blocks[sign], 'store', back[sign])  14.1 us
    ppermute x12, waiting for transfers between devices, queries_travel(): flows[flow, sign] = lax.ppermute(blocks[sign], 'store', back[sign])  13.9 us
    ppermute x10, starting transfers between devices, queries_travel(): moving[side, sign] = lax.ppermute(came[sign], 'store', routes[sign])  13.1 us
    pallas_call x16, Pallas kernels, call(): pl.pallas_call(kernel, out_shape=shape, in_specs=[VMEM] * len(args), out_...  7.75 us
    ppermute x2, starting transfers between devices, queries_travel(): lax.ppermute(block, 'store', back[key[1]])  5.67 us
    unnamed x12, local copies, waits for them, and re-layouts  4.79 us
    ppermute x1, starting transfers between devices, shifted(): return lax.ppermute(block, axis, route)  4.06 us
  transfers between devices with their start and end apart: 29, of which 14 were waited for; matrix products, arithmetic and copies ran while one was open for 0% of the time, Pallas kernels for 29%

profile of v10, /device:TPU:0, one launch (start us, length us, event | category | flops | bytes accessed | tf_op | source)
XLA Modules:
  0.0 102.4 jit_solution(13707483935947637588)
XLA Ops:
  1.9 1.0 %copy-done.2 = bf16[1,64,4096]{2,1,0:T(8,128)(2,1)S(1)} copy-done((bf16[1,64,4096]{2,1,0:T(8,128)(2,1)S(1)}, bf16[1,64,4096]{2,1,0:T(8,128)(2,1)}, u32[]{:S(2)}) %copy-start.2) | copy-done | bytes 524312
  3.0 0.7 copy-done.5
  3.6 0.3 shard_map.77
  3.9 4.1 %collective-permute-start.1 = (bf16[1,2,64,512]{3,2,1,0:T(8,128)(2,1)}, bf16[1,2,64,512]{3,2,1,0:T(8,128)(2,1)S(1)}, u32[]{:S(2)}, u32[]{:S(2)}) collective-permute-start(bf16[1,2,64,512]{3,2,1,0:T(8,128)(2,1)} %param.7), channel_id=1, source_target_pairs={{8,0},{10,2},{12,4},{14,6},{0,8},{2,10},{4,12},{6,14},{9,1},{11,3}... | collective-permute-start | bytes 393224 | tf_op jit(solution)/shard_map/ppermute | solution.py:26
  8.0 1.6 %collective-permute-start = (bf16[1040,128]{1,0:T(8,128)(2,1)S(1)}, bf16[1040,128]{1,0:T(8,128)(2,1)S(1)}, u32[]{:S(2)}, u32[]{:S(2)}) collective-permute-start(bf16[1040,128]{1,0:T(8,128)(2,1)S(1)} %get-tuple-element.78.refs_1_), channel_id=1, source_target_pairs={{0,4},{4,8},{8,12},{12,14},{14,10},{10,6},{6,2},{2,0},{1,5},{5,9},... | collective-permute-start | bytes 798728 | tf_op jit(solution)/shard_map/ppermute | solution.py:460
  9.5 0.4 collective-permute-start.3
  10.0 1.6 %collective-permute-start.4 = (bf16[1024,128]{1,0:T(8,128)(2,1)S(1)}, bf16[1024,128]{1,0:T(8,128)(2,1)S(1)}, u32[]{:S(2)}, u32[]{:S(2)}) collective-permute-start(bf16[1024,128]{1,0:T(8,128)(2,1)S(1)} %get-tuple-element.133.refs_1_), channel_id=1, source_target_pairs={{0,4},{4,8},{8,12},{12,14},{14,10},{10,6},{6,2},{2,0},{1,5},{5,9},... | collective-permute-start | bytes 786440 | tf_op jit(solution)/shard_map/ppermute | solution.py:460
  11.6 0.4 collective-permute-start.5
  12.0 3.3 %collective-permute-done.1.page_ref = bf16[1,2,64,512]{3,2,1,0:T(8,128)(2,1)S(1)} collective-permute-done((bf16[1,2,64,512]{3,2,1,0:T(8,128)(2,1)}, bf16[1,2,64,512]{3,2,1,0:T(8,128)(2,1)S(1)}, u32[]{:S(2)}, u32[]{:S(2)}) %collective-permute-start.1) | collective-permute-done | bytes 131104 | tf_op jit(solution)/shard_map/ppermute | solution.py:26
  15.3 2.2 %copy-done = bf16[32,2,64,512]{3,2,1,0:T(8,128)(2,1)S(1)} copy-done((bf16[32,2,64,512]{3,2,1,0:T(8,128)(2,1)S(1)}, bf16[32,2,64,512]{3,2,1,0:T(8,128)(2,1)}, u32[]{:S(2)}) %copy-start) | copy-done | bytes 4194328
  17.5 0.9 copy-done.3
  18.4 1.8 %shard_map.78 = (f32[2,512,128]{2,1,0:T(8,128)S(1)}, bf16[2,16,128]{2,1,0:T(8,128)(2,1)S(1)}) custom-call(s32[1,128]{1,0:T(1,128)S(1)} %fusion.refs_0_, bf16[1040,128]{1,0:T(8,128)(2,1)S(1)} %get-tuple-element.78.refs_1_, bf16[2,64,512]{2,1,0:T(8,128)(2,1)S(1)} %bitcast.2, bf16[32,2,64,512]{3,2,1,0:T(8,128)(2,1)S(1)} %copy-done), custom_call_target="tpu_custom_call" | custom-call | flops 8589934592 | bytes 20971520 | tf_op jit(solution)/shard_map/pallas_call | solution.py:251
  20.2 0.8 collective-permute-start.2
  21.1 1.3 %collective-permute-start.7 = (bf16[1040,128]{1,0:T(8,128)(2,1)S(1)}, bf16[1040,128]{1,0:T(8,128)(2,1)S(1)}, u32[]{:S(2)}, u32[]{:S(2)}) collective-permute-start(bf16[1040,128]{1,0:T(8,128)(2,1)S(1)} %collective-permute-done.3.refs_2_), channel_id=1, source_target_pairs={{0,2},{4,0},{8,4},{12,8},{14,12},{10,14},{6,10},{2,6},{1,3},{5,1},... | collective-permute-start | bytes 798728 | tf_op jit(solution)/shard_map/ppermute | solution.py:485
  22.4 2.3 %shard_map.79 = (f32[2,512,128]{2,1,0:T(8,128)S(1)}, bf16[2,16,128]{2,1,0:T(8,128)(2,1)S(1)}, f32[2,512,128]{2,1,0:T(8,128)S(1)}, bf16[2,16,128]{2,1,0:T(8,128)(2,1)S(1)}) custom-call(s32[2,128]{1,0:T(2,128)S(1)} %maximum_convert_fusion.refs_0_, bf16[1040,128]{1,0:T(8,128)(2,1)S(1)} %collective-permute-done.refs_1_, ...), custom_call_target="tpu_custom_call" | custom-call | flops 1073741824 | bytes 2621440 | tf_op jit(solution)/shard_map/pallas_call | solution.py:251
  24.7 2.1 %collective-permute-start.8 = (bf16[1024,128]{1,0:T(8,128)(2,1)S(1)}, bf16[1024,128]{1,0:T(8,128)(2,1)S(1)}, u32[]{:S(2)}, u32[]{:S(2)}) collective-permute-start(bf16[1024,128]{1,0:T(8,128)(2,1)S(1)} %collective-permute-done.4.refs_1_), channel_id=1, source_target_pairs={{0,4},{4,8},{8,12},{12,14},{14,10},{10,6},{6,2},{2,0},{1,5},{5,9},... | collective-permute-start | bytes 786440 | tf_op jit(solution)/shard_map/ppermute | solution.py:485
  26.8 2.3 %shard_map.80 = (f32[2,512,128]{2,1,0:T(8,128)S(1)}, bf16[2,16,128]{2,1,0:T(8,128)(2,1)S(1)}, f32[2,512,128]{2,1,0:T(8,128)S(1)}, bf16[2,16,128]{2,1,0:T(8,128)(2,1)S(1)}) custom-call(s32[2,128]{1,0:T(2,128)S(1)} %maximum_convert_fusion.refs_0_, bf16[1024,128]{1,0:T(8,128)(2,1)S(1)} %collective-permute-done.4.refs_1_, ...), custom_call_target="tpu_custom_call" | custom-call | flops 1073741824 | bytes 2621440 | tf_op jit(solution)/shard_map/pallas_call | solution.py:251
  29.1 3.2 %collective-permute-start.6 = (bf16[1040,128]{1,0:T(8,128)(2,1)S(1)}, bf16[1040,128]{1,0:T(8,128)(2,1)S(1)}, u32[]{:S(2)}, u32[]{:S(2)}) collective-permute-start(bf16[1040,128]{1,0:T(8,128)(2,1)S(1)} %collective-permute-done.2.refs_1_), channel_id=1, source_target_pairs={{0,4},{4,8},{8,12},{12,14},{14,10},{10,6},{6,2},{2,0},{1,5},{5,9},... | collective-permute-start | bytes 798728 | tf_op jit(solution)/shard_map/ppermute | solution.py:485
  32.5 2.3 %shard_map.81 = (f32[2,512,128]{2,1,0:T(8,128)S(1)}, bf16[2,16,128]{2,1,0:T(8,128)(2,1)S(1)}, f32[2,512,128]{2,1,0:T(8,128)S(1)}, bf16[2,16,128]{2,1,0:T(8,128)(2,1)S(1)}) custom-call(s32[2,128]{1,0:T(2,128)S(1)} %maximum_convert_fusion.1.refs_0_.lists_ref, bf16[1040,128]{1,0:T(8,128)(2,1)S(1)} %collective-permute-done.2.refs_1_, ...), custom_call_target="tpu_custom_call" | custom-call | flops 1073741824 | bytes 2621440 | tf_op jit(solution)/shard_map/pallas_call | solution.py:251
  34.8 1.1 %collective-permute-done.9.refs_2_ = bf16[1024,128]{1,0:T(8,128)(2,1)S(1)} collective-permute-done((bf16[1024,128]{1,0:T(8,128)(2,1)S(1)}, bf16[1024,128]{1,0:T(8,128)(2,1)S(1)}, u32[]{:S(2)}, u32[]{:S(2)}) %collective-permute-start.9) | collective-permute-done | bytes 262176 | tf_op jit(solution)/shard_map/ppermute | solution.py:485
  35.9 2.2 %collective-permute-start.12 = (bf16[1024,128]{1,0:T(8,128)(2,1)S(1)}, bf16[1024,128]{1,0:T(8,128)(2,1)S(1)}, u32[]{:S(2)}, u32[]{:S(2)}) collective-permute-start(bf16[1024,128]{1,0:T(8,128)(2,1)S(1)} %collective-permute-done.8.refs_1_), channel_id=1, source_target_pairs={{0,4},{4,8},{8,12},{12,14},{14,10},{10,6},{6,2},{2,0},{1,5},{5,9},... | collective-permute-start | bytes 786440 | tf_op jit(solution)/shard_map/ppermute | solution.py:485
  38.1 2.3 %shard_map.82 = (f32[2,512,128]{2,1,0:T(8,128)S(1)}, bf16[2,16,128]{2,1,0:T(8,128)(2,1)S(1)}, f32[2,512,128]{2,1,0:T(8,128)S(1)}, bf16[2,16,128]{2,1,0:T(8,128)(2,1)S(1)}) custom-call(s32[2,128]{1,0:T(2,128)S(1)} %maximum_convert_fusion.1.refs_0_.lists_ref, bf16[1024,128]{1,0:T(8,128)(2,1)S(1)} %collective-permute-done.8.refs_1_, ...), custom_call_target="tpu_custom_call" | custom-call | flops 1073741824 | bytes 2621440 | tf_op jit(solution)/shard_map/pallas_call | solution.py:251
  40.4 3.3 %collective-permute-start.10 = (bf16[1040,128]{1,0:T(8,128)(2,1)S(1)}, bf16[1040,128]{1,0:T(8,128)(2,1)S(1)}, u32[]{:S(2)}, u32[]{:S(2)}) collective-permute-start(bf16[1040,128]{1,0:T(8,128)(2,1)S(1)} %collective-permute-done.6.refs_1_), channel_id=1, source_target_pairs={{0,4},{4,8},{8,12},{12,14},{14,10},{10,6},{6,2},{2,0},{1,5},{5,9},... | collective-permute-start | bytes 798728 | tf_op jit(solution)/shard_map/ppermute | solution.py:485
  43.7 2.3 %shard_map.83 = (f32[2,512,128]{2,1,0:T(8,128)S(1)}, bf16[2,16,128]{2,1,0:T(8,128)(2,1)S(1)}, f32[2,512,128]{2,1,0:T(8,128)S(1)}, bf16[2,16,128]{2,1,0:T(8,128)(2,1)S(1)}) custom-call(s32[2,128]{1,0:T(2,128)S(1)} %maximum_convert_fusion.2.refs_0_, bf16[1040,128]{1,0:T(8,128)(2,1)S(1)} %collective-permute-done.6.refs_1_, ...), custom_call_target="tpu_custom_call" | custom-call | flops 1073741824 | bytes 2621440 | tf_op jit(solution)/shard_map/pallas_call | solution.py:251
  46.1 2.5 %collective-permute-start.17 = (bf16[2,528,128]{2,1,0:T(8,128)(2,1)S(1)}, bf16[2,528,128]{2,1,0:T(8,128)(2,1)S(1)}, u32[]{:S(2)}, u32[]{:S(2)}) collective-permute-start(bf16[2,528,128]{2,1,0:T(8,128)(2,1)S(1)} %shard_map.84), channel_id=1, source_target_pairs={{0,4},{4,8},{8,12},{12,14},{14,10},{10,6},{6,2},{2,0},{1,5},{5,9},... | collective-permute-start | bytes 811016 | tf_op jit(solution)/shard_map/ppermute | solution.py:507
  48.6 2.3 %shard_map.85 = (f32[2,512,128]{2,1,0:T(8,128)S(1)}, bf16[2,16,128]{2,1,0:T(8,128)(2,1)S(1)}, f32[2,512,128]{2,1,0:T(8,128)S(1)}, bf16[2,16,128]{2,1,0:T(8,128)(2,1)S(1)}) custom-call(s32[2,128]{1,0:T(2,128)S(1)} %maximum_convert_fusion.2.refs_0_, bf16[1024,128]{1,0:T(8,128)(2,1)S(1)} %collective-permute-done.12.refs_1_, ...), custom_call_target="tpu_custom_call" | custom-call | flops 1073741824 | bytes 2621440 | tf_op jit(solution)/shard_map/pallas_call | solution.py:251
  51.0 3.1 %collective-permute-start.18 = (bf16[2,528,128]{2,1,0:T(8,128)(2,1)S(1)}, bf16[2,528,128]{2,1,0:T(8,128)(2,1)S(1)}, u32[]{:S(2)}, u32[]{:S(2)}) collective-permute-start(bf16[2,528,128]{2,1,0:T(8,128)(2,1)S(1)} %shard_map.86), channel_id=1, source_target_pairs={{0,2},{4,0},{8,4},{12,8},{14,12},{10,14},{6,10},{2,6},{1,3},{5,1},... | collective-permute-start | bytes 811016 | tf_op jit(solution)/shard_map/ppermute | solution.py:507
  54.1 1.5 %shard_map.87 = (f32[2,512,128]{2,1,0:T(8,128)S(1)}, bf16[2,16,128]{2,1,0:T(8,128)(2,1)S(1)}) custom-call(s32[1,128]{1,0:T(1,128)S(1)} %fusion.1.refs_0_, bf16[1040,128]{1,0:T(8,128)(2,1)S(1)} %collective-permute-done.10.refs_1_, bf16[32,2,64,512]{3,2,1,0:T(8,128)(2,1)S(1)} %copy-done.1), custom_call_target="tpu_custom_call" | custom-call | flops 536870912 | bytes 1310720 | tf_op jit(solution)/shard_map/pallas_call | solution.py:251
  55.6 2.2 %collective-permute-done.14.refs_1_ = bf16[1024,128]{1,0:T(8,128)(2,1)S(1)} collective-permute-done((bf16[1024,128]{1,0:T(8,128)(2,1)S(1)}, bf16[1024,128]{1,0:T(8,128)(2,1)S(1)}, u32[]{:S(2)}, u32[]{:S(2)}) %collective-permute-start.14) | collective-permute-done | bytes 262176 | tf_op jit(solution)/shard_map/ppermute | solution.py:485
  57.8 1.5 %shard_map.89 = (f32[2,512,128]{2,1,0:T(8,128)S(1)}, bf16[2,16,128]{2,1,0:T(8,128)(2,1)S(1)}) custom-call(s32[1,128]{1,0:T(1,128)S(1)} %fusion.1.refs_0_, bf16[1024,128]{1,0:T(8,128)(2,1)S(1)} %collective-permute-done.14.refs_1_, bf16[32,2,64,512]{3,2,1,0:T(8,128)(2,1)S(1)} %copy-done.1), custom_call_target="tpu_custom_call" | custom-call | flops 536870912 | bytes 1310720 | tf_op jit(solution)/shard_map/pallas_call | solution.py:251
  59.4 1.1 %collective-permute-start.15 = (bf16[2,528,128]{2,1,0:T(8,128)(2,1)S(1)}, bf16[2,528,128]{2,1,0:T(8,128)(2,1)S(1)}, u32[]{:S(2)}, u32[]{:S(2)}) collective-permute-start(bf16[2,528,128]{2,1,0:T(8,128)(2,1)S(1)} %shard_map.90), channel_id=1, source_target_pairs={{0,4},{4,8},{8,12},{12,14},{14,10},{10,6},{6,2},{2,0},{1,5},{5,9},... | collective-permute-start | bytes 811016 | tf_op jit(solution)/shard_map/ppermute | solution.py:526
  60.5 1.0 collective-permute-start.16
  61.5 0.9 collective-permute-done.18.in_ref
  62.4 0.6 shard_map.91
  63.1 2.4 %collective-permute-start.21 = (bf16[2,528,128]{2,1,0:T(8,128)(2,1)S(1)}, bf16[2,528,128]{2,1,0:T(8,128)(2,1)S(1)}, u32[]{:S(2)}, u32[]{:S(2)}) collective-permute-start(bf16[2,528,128]{2,1,0:T(8,128)(2,1)S(1)} %shard_map.91), channel_id=1, source_target_pairs={{0,4},{4,8},{8,12},{12,14},{14,10},{10,6},{6,2},{2,0},{1,5},{5,9},... | collective-permute-start | bytes 811016 | tf_op jit(solution)/shard_map/ppermute | solution.py:526
  65.4 0.6 shard_map.92
  66.1 2.0 %collective-permute-done.15.in_ref = bf16[2,528,128]{2,1,0:T(8,128)(2,1)S(1)} collective-permute-done((bf16[2,528,128]{2,1,0:T(8,128)(2,1)S(1)}, bf16[2,528,128]{2,1,0:T(8,128)(2,1)S(1)}, u32[]{:S(2)}, u32[]{:S(2)}) %collective-permute-start.15) | collective-permute-done | bytes 270368 | tf_op jit(solution)/shard_map/ppermute | solution.py:526
  68.1 0.3 collective-permute-done.16.in_ref
  68.4 0.6 shard_map.93
  69.0 2.6 %collective-permute-start.19 = (bf16[2,528,128]{2,1,0:T(8,128)(2,1)S(1)}, bf16[2,528,128]{2,1,0:T(8,128)(2,1)S(1)}, u32[]{:S(2)}, u32[]{:S(2)}) collective-permute-start(bf16[2,528,128]{2,1,0:T(8,128)(2,1)S(1)} %shard_map.93), channel_id=1, source_target_pairs={{0,4},{4,8},{8,12},{12,14},{14,10},{10,6},{6,2},{2,0},{1,5},{5,9},... | collective-permute-start | bytes 811016 | tf_op jit(solution)/shard_map/ppermute | solution.py:526
  71.7 0.6 shard_map.94
  72.4 1.5 %collective-permute-done.21.in_ref = bf16[2,528,128]{2,1,0:T(8,128)(2,1)S(1)} collective-permute-done((bf16[2,528,128]{2,1,0:T(8,128)(2,1)S(1)}, bf16[2,528,128]{2,1,0:T(8,128)(2,1)S(1)}, u32[]{:S(2)}, u32[]{:S(2)}) %collective-permute-start.21) | collective-permute-done | bytes 270368 | tf_op jit(solution)/shard_map/ppermute | solution.py:526
  73.9 0.6 collective-permute-done.22.in_ref
  74.5 0.6 shard_map.95
  75.1 2.3 %collective-permute-start.25 = (bf16[2,528,128]{2,1,0:T(8,128)(2,1)S(1)}, bf16[2,528,128]{2,1,0:T(8,128)(2,1)S(1)}, u32[]{:S(2)}, u32[]{:S(2)}) collective-permute-start(bf16[2,528,128]{2,1,0:T(8,128)(2,1)S(1)} %shard_map.95), channel_id=1, source_target_pairs={{0,4},{4,8},{8,12},{12,14},{14,10},{10,6},{6,2},{2,0},{1,5},{5,9},... | collective-permute-start | bytes 811016 | tf_op jit(solution)/shard_map/ppermute | solution.py:526
  77.5 0.6 shard_map.96
  78.2 1.5 %collective-permute-done.19.in_ref = bf16[2,528,128]{2,1,0:T(8,128)(2,1)S(1)} collective-permute-done((bf16[2,528,128]{2,1,0:T(8,128)(2,1)S(1)}, bf16[2,528,128]{2,1,0:T(8,128)(2,1)S(1)}, u32[]{:S(2)}, u32[]{:S(2)}) %collective-permute-start.19) | collective-permute-done | bytes 270368 | tf_op jit(solution)/shard_map/ppermute | solution.py:526
  79.7 0.6 collective-permute-done.20.in_ref
  80.3 0.6 shard_map.97
  81.0 2.3 %collective-permute-start.23 = (bf16[2,528,128]{2,1,0:T(8,128)(2,1)S(1)}, bf16[2,528,128]{2,1,0:T(8,128)(2,1)S(1)}, u32[]{:S(2)}, u32[]{:S(2)}) collective-permute-start(bf16[2,528,128]{2,1,0:T(8,128)(2,1)S(1)} %shard_map.97), channel_id=1, source_target_pairs={{0,4},{4,8},{8,12},{12,14},{14,10},{10,6},{6,2},{2,0},{1,5},{5,9},... | collective-permute-start | bytes 811016 | tf_op jit(solution)/shard_map/ppermute | solution.py:526
  83.3 0.6 shard_map.98
  84.0 3.3 %shard_map.99 = (f32[2,512,128]{2,1,0:T(8,128)S(1)}, bf16[2,16,128]{2,1,0:T(8,128)(2,1)S(1)}, bf16[32,2,64,512]{3,2,1,0:T(8,128)(2,1)}) custom-call(s32[1,128]{1,0:T(1,128)S(1)} %fusion.refs_0_, bf16[1024,128]{1,0:T(8,128)(2,1)S(1)} %get-tuple-element.133.refs_1_, bf16[2,64,512]{2,1,0:T(8,128)(2,1)S(1)} %bitcast.3, bf16[32,2,64,512]{3,2,1,0:T(8,128)(2,1)S(1)} %copy-done.1), custom_call_target="tpu_custom_call" | custom-call | flops 536870912 | bytes 1310720 | tf_op jit(solution)/shard_map/pallas_call | solution.py:251
  87.3 1.8 %collective-permute-done.23.in_ref = bf16[2,528,128]{2,1,0:T(8,128)(2,1)S(1)} collective-permute-done((bf16[2,528,128]{2,1,0:T(8,128)(2,1)S(1)}, bf16[2,528,128]{2,1,0:T(8,128)(2,1)S(1)}, u32[]{:S(2)}, u32[]{:S(2)}) %collective-permute-start.23) | collective-permute-done | bytes 270368 | tf_op jit(solution)/shard_map/ppermute | solution.py:526
  89.1 1.9 %collective-permute-done.24.in_ref = bf16[2,528,128]{2,1,0:T(8,128)(2,1)S(1)} collective-permute-done((bf16[2,528,128]{2,1,0:T(8,128)(2,1)S(1)}, bf16[2,528,128]{2,1,0:T(8,128)(2,1)S(1)}, u32[]{:S(2)}, u32[]{:S(2)}) %collective-permute-start.24) | collective-permute-done | bytes 270368 | tf_op jit(solution)/shard_map/ppermute | solution.py:526
  90.9 0.6 shard_map.100
  91.6 0.4 collective-permute-start.27
  91.9 0.6 shard_map.101
  92.6 1.8 %collective-permute-start.28 = (bf16[2,528,128]{2,1,0:T(8,128)(2,1)S(1)}, bf16[2,528,128]{2,1,0:T(8,128)(2,1)S(1)}, u32[]{:S(2)}, u32[]{:S(2)}) collective-permute-start(bf16[2,528,128]{2,1,0:T(8,128)(2,1)S(1)} %shard_map.101), channel_id=1, source_target_pairs={{0,4},{4,8},{8,12},{12,14},{14,10},{10,6},{6,2},{2,0},{1,5},{5,9},... | collective-permute-start | bytes 811016 | tf_op jit(solution)/shard_map/ppermute | solution.py:526
  94.4 1.2 %shard_map.105 = bf16[32,2,64,512]{3,2,1,0:T(8,128)(2,1)} custom-call(s32[1]{0:T(128)} %bitcast.1.me_ref, s32[2,128]{1,0:T(2,128)S(1)} %maximum_convert_fusion.1.refs_0_.lists_ref, bf16[1,2,64,512]{3,2,1,0:T(8,128)(2,1)S(1)} %collective-permute-done.1.page_ref, bf16[32,2,64,512]{3,2,1,0:T(8,128)(2,1)} %get-tuple-element.147.old_ref), custom_call_target="tpu_custom_call", output_to_operand_aliasing={{}: (3, {})} | custom-call | flops 1 | bytes 1 | tf_op jit(solution)/shard_map/pallas_call | solution.py:277
  95.6 0.6 shard_map.102
  96.2 0.6 shard_map.103
  96.9 1.5 %collective-permute-done.27.refs_0_ = bf16[2,528,128]{2,1,0:T(8,128)(2,1)S(1)} collective-permute-done((bf16[2,528,128]{2,1,0:T(8,128)(2,1)S(1)}, bf16[2,528,128]{2,1,0:T(8,128)(2,1)S(1)}, u32[]{:S(2)}, u32[]{:S(2)}) %collective-permute-start.27) | collective-permute-done | bytes 270368 | tf_op jit(solution)/shard_map/ppermute | solution.py:526
  98.4 2.2 %collective-permute-done.28.refs_3_ = bf16[2,528,128]{2,1,0:T(8,128)(2,1)S(1)} collective-permute-done((bf16[2,528,128]{2,1,0:T(8,128)(2,1)S(1)}, bf16[2,528,128]{2,1,0:T(8,128)(2,1)S(1)}, u32[]{:S(2)}, u32[]{:S(2)}) %collective-permute-start.28) | collective-permute-done | bytes 270368 | tf_op jit(solution)/shard_map/ppermute | solution.py:526
  100.6 1.6 %shard_map.104 = bf16[1,64,4096]{2,1,0:T(8,128)(2,1)} custom-call(bf16[2,528,128]{2,1,0:T(8,128)(2,1)S(1)} %collective-permute-done.27.refs_0_, f32[2,512,128]{2,1,0:T(8,128)S(1)} %get-tuple-element.139.refs_1_, bf16[2,16,128]{2,1,0:T(8,128)(2,1)S(1)} %get-tuple-element.140.refs_2_, bf16[2,528,128]{2,1,0:T(8,128)(2,1)S(1)} %collective-permute-done.28.refs_3_, ...), custom_call_target="tpu_custom_call" | custom-call | tf_op jit(solution)/shard_map/pallas_call | solution.py:358
  (46 shorter events, 0.6 us)
Async XLA Ops:
  1.9 1.0 %copy-start.2 = (bf16[1,64,4096]{2,1,0:T(8,128)(2,1)S(1)}, bf16[1,64,4096]{2,1,0:T(8,128)(2,1)}, u32[]{:S(2)}) copy-start(bf16[1,64,4096]{2,1,0:T(8,128)(2,1)} %q_ref.1) | copy-start | bytes 1572868
  3.0 0.7 copy-start.5
  3.9 11.4 %collective-permute-start.1 = (bf16[1,2,64,512]{3,2,1,0:T(8,128)(2,1)}, bf16[1,2,64,512]{3,2,1,0:T(8,128)(2,1)S(1)}, u32[]{:S(2)}, u32[]{:S(2)}) collective-permute-start(bf16[1,2,64,512]{3,2,1,0:T(8,128)(2,1)} %param.7), channel_id=1, source_target_pairs={{8,0},{10,2},{12,4},{14,6},{0,8},{2,10},{4,12},{6,14},{9,1},{11,3}... | collective-permute-start | bytes 393224 | tf_op jit(solution)/shard_map/ppermute | solution.py:26
  8.0 12.2 %collective-permute-start = (bf16[1040,128]{1,0:T(8,128)(2,1)S(1)}, bf16[1040,128]{1,0:T(8,128)(2,1)S(1)}, u32[]{:S(2)}, u32[]{:S(2)}) collective-permute-start(bf16[1040,128]{1,0:T(8,128)(2,1)S(1)} %get-tuple-element.78.refs_1_), channel_id=1, source_target_pairs={{0,4},{4,8},{8,12},{12,14},{14,10},{10,6},{6,2},{2,0},{1,5},{5,9},... | collective-permute-start | bytes 798728 | tf_op jit(solution)/shard_map/ppermute | solution.py:460
  9.5 11.5 %collective-permute-start.3 = (bf16[1040,128]{1,0:T(8,128)(2,1)S(1)}, bf16[1040,128]{1,0:T(8,128)(2,1)S(1)}, u32[]{:S(2)}, u32[]{:S(2)}) collective-permute-start(bf16[1040,128]{1,0:T(8,128)(2,1)S(1)} %get-tuple-element.78.refs_1_), channel_id=1, source_target_pairs={{0,2},{4,0},{8,4},{12,8},{14,12},{10,14},{6,10},{2,6},{1,3},{5,1},... | collective-permute-start | bytes 798728 | tf_op jit(solution)/shard_map/ppermute | solution.py:460
  10.0 14.7 %collective-permute-start.4 = (bf16[1024,128]{1,0:T(8,128)(2,1)S(1)}, bf16[1024,128]{1,0:T(8,128)(2,1)S(1)}, u32[]{:S(2)}, u32[]{:S(2)}) collective-permute-start(bf16[1024,128]{1,0:T(8,128)(2,1)S(1)} %get-tuple-element.133.refs_1_), channel_id=1, source_target_pairs={{0,4},{4,8},{8,12},{12,14},{14,10},{10,6},{6,2},{2,0},{1,5},{5,9},... | collective-permute-start | bytes 786440 | tf_op jit(solution)/shard_map/ppermute | solution.py:460
  11.6 13.1 %collective-permute-start.5 = (bf16[1024,128]{1,0:T(8,128)(2,1)S(1)}, bf16[1024,128]{1,0:T(8,128)(2,1)S(1)}, u32[]{:S(2)}, u32[]{:S(2)}) collective-permute-start(bf16[1024,128]{1,0:T(8,128)(2,1)S(1)} %get-tuple-element.133.refs_1_), channel_id=1, source_target_pairs={{0,2},{4,0},{8,4},{12,8},{14,12},{10,14},{6,10},{2,6},{1,3},{5,1},... | collective-permute-start | bytes 786440 | tf_op jit(solution)/shard_map/ppermute | solution.py:460
  15.3 2.2 %copy-start = (bf16[32,2,64,512]{3,2,1,0:T(8,128)(2,1)S(1)}, bf16[32,2,64,512]{3,2,1,0:T(8,128)(2,1)}, u32[]{:S(2)}) copy-start(bf16[32,2,64,512]{3,2,1,0:T(8,128)(2,1)} %refs_3_.15) | copy-start | bytes 12582916
  17.5 0.9 copy-start.3
  18.4 4.0 %copy-start.1 = (bf16[32,2,64,512]{3,2,1,0:T(8,128)(2,1)S(1)}, bf16[32,2,64,512]{3,2,1,0:T(8,128)(2,1)}, u32[]{:S(2)}) copy-start(bf16[32,2,64,512]{3,2,1,0:T(8,128)(2,1)} %refs_3_.15) | copy-start | bytes 12582916
  20.2 8.9 %collective-permute-start.2 = (bf16[1040,128]{1,0:T(8,128)(2,1)S(1)}, bf16[1040,128]{1,0:T(8,128)(2,1)S(1)}, u32[]{:S(2)}, u32[]{:S(2)}) collective-permute-start(bf16[1040,128]{1,0:T(8,128)(2,1)S(1)} %collective-permute-done.refs_1_), channel_id=1, source_target_pairs={{0,4},{4,8},{8,12},{12,14},{14,10},{10,6},{6,2},{2,0},{1,5},{5,9},... | collective-permute-start | bytes 798728 | tf_op jit(solution)/shard_map/ppermute | solution.py:485
  21.1 11.3 %collective-permute-start.7 = (bf16[1040,128]{1,0:T(8,128)(2,1)S(1)}, bf16[1040,128]{1,0:T(8,128)(2,1)S(1)}, u32[]{:S(2)}, u32[]{:S(2)}) collective-permute-start(bf16[1040,128]{1,0:T(8,128)(2,1)S(1)} %collective-permute-done.3.refs_2_), channel_id=1, source_target_pairs={{0,2},{4,0},{8,4},{12,8},{14,12},{10,14},{6,10},{2,6},{1,3},{5,1},... | collective-permute-start | bytes 798728 | tf_op jit(solution)/shard_map/ppermute | solution.py:485
  24.7 10.1 %collective-permute-start.8 = (bf16[1024,128]{1,0:T(8,128)(2,1)S(1)}, bf16[1024,128]{1,0:T(8,128)(2,1)S(1)}, u32[]{:S(2)}, u32[]{:S(2)}) collective-permute-start(bf16[1024,128]{1,0:T(8,128)(2,1)S(1)} %collective-permute-done.4.refs_1_), channel_id=1, source_target_pairs={{0,4},{4,8},{8,12},{12,14},{14,10},{10,6},{6,2},{2,0},{1,5},{5,9},... | collective-permute-start | bytes 786440 | tf_op jit(solution)/shard_map/ppermute | solution.py:485
  26.8 9.1 %collective-permute-start.9 = (bf16[1024,128]{1,0:T(8,128)(2,1)S(1)}, bf16[1024,128]{1,0:T(8,128)(2,1)S(1)}, u32[]{:S(2)}, u32[]{:S(2)}) collective-permute-start(bf16[1024,128]{1,0:T(8,128)(2,1)S(1)} %collective-permute-done.5.refs_2_), channel_id=1, source_target_pairs={{0,2},{4,0},{8,4},{12,8},{14,12},{10,14},{6,10},{2,6},{1,3},{5,1},... | collective-permute-start | bytes 786440 | tf_op jit(solution)/shard_map/ppermute | solution.py:485
  29.1 11.3 %collective-permute-start.6 = (bf16[1040,128]{1,0:T(8,128)(2,1)S(1)}, bf16[1040,128]{1,0:T(8,128)(2,1)S(1)}, u32[]{:S(2)}, u32[]{:S(2)}) collective-permute-start(bf16[1040,128]{1,0:T(8,128)(2,1)S(1)} %collective-permute-done.2.refs_1_), channel_id=1, source_target_pairs={{0,4},{4,8},{8,12},{12,14},{14,10},{10,6},{6,2},{2,0},{1,5},{5,9},... | collective-permute-start | bytes 798728 | tf_op jit(solution)/shard_map/ppermute | solution.py:485
  32.4 11.3 %collective-permute-start.11 = (bf16[1040,128]{1,0:T(8,128)(2,1)S(1)}, bf16[1040,128]{1,0:T(8,128)(2,1)S(1)}, u32[]{:S(2)}, u32[]{:S(2)}) collective-permute-start(bf16[1040,128]{1,0:T(8,128)(2,1)S(1)} %collective-permute-done.7.refs_2_), channel_id=1, source_target_pairs={{0,2},{4,0},{8,4},{12,8},{14,12},{10,14},{6,10},{2,6},{1,3},{5,1},... | collective-permute-start | bytes 798728 | tf_op jit(solution)/shard_map/ppermute | solution.py:485
  35.9 12.7 %collective-permute-start.12 = (bf16[1024,128]{1,0:T(8,128)(2,1)S(1)}, bf16[1024,128]{1,0:T(8,128)(2,1)S(1)}, u32[]{:S(2)}, u32[]{:S(2)}) collective-permute-start(bf16[1024,128]{1,0:T(8,128)(2,1)S(1)} %collective-permute-done.8.refs_1_), channel_id=1, source_target_pairs={{0,4},{4,8},{8,12},{12,14},{14,10},{10,6},{6,2},{2,0},{1,5},{5,9},... | collective-permute-start | bytes 786440 | tf_op jit(solution)/shard_map/ppermute | solution.py:485
  38.1 10.5 %collective-permute-start.13 = (bf16[1024,128]{1,0:T(8,128)(2,1)S(1)}, bf16[1024,128]{1,0:T(8,128)(2,1)S(1)}, u32[]{:S(2)}, u32[]{:S(2)}) collective-permute-start(bf16[1024,128]{1,0:T(8,128)(2,1)S(1)} %collective-permute-done.9.refs_2_), channel_id=1, source_target_pairs={{0,2},{4,0},{8,4},{12,8},{14,12},{10,14},{6,10},{2,6},{1,3},{5,1},... | collective-permute-start | bytes 786440 | tf_op jit(solution)/shard_map/ppermute | solution.py:485
  40.4 13.7 %collective-permute-start.10 = (bf16[1040,128]{1,0:T(8,128)(2,1)S(1)}, bf16[1040,128]{1,0:T(8,128)(2,1)S(1)}, u32[]{:S(2)}, u32[]{:S(2)}) collective-permute-start(bf16[1040,128]{1,0:T(8,128)(2,1)S(1)} %collective-permute-done.6.refs_1_), channel_id=1, source_target_pairs={{0,4},{4,8},{8,12},{12,14},{14,10},{10,6},{6,2},{2,0},{1,5},{5,9},... | collective-permute-start | bytes 798728 | tf_op jit(solution)/shard_map/ppermute | solution.py:485
  46.1 15.4 %collective-permute-start.17 = (bf16[2,528,128]{2,1,0:T(8,128)(2,1)S(1)}, bf16[2,528,128]{2,1,0:T(8,128)(2,1)S(1)}, u32[]{:S(2)}, u32[]{:S(2)}) collective-permute-start(bf16[2,528,128]{2,1,0:T(8,128)(2,1)S(1)} %shard_map.84), channel_id=1, source_target_pairs={{0,4},{4,8},{8,12},{12,14},{14,10},{10,6},{6,2},{2,0},{1,5},{5,9},... | collective-permute-start | bytes 811016 | tf_op jit(solution)/shard_map/ppermute | solution.py:507
  48.6 9.2 %collective-permute-start.14 = (bf16[1024,128]{1,0:T(8,128)(2,1)S(1)}, bf16[1024,128]{1,0:T(8,128)(2,1)S(1)}, u32[]{:S(2)}, u32[]{:S(2)}) collective-permute-start(bf16[1024,128]{1,0:T(8,128)(2,1)S(1)} %collective-permute-done.13.refs_2_), channel_id=1, source_target_pairs={{0,2},{4,0},{8,4},{12,8},{14,12},{10,14},{6,10},{2,6},{1,3},{5,1},... | collective-permute-start | bytes 786440 | tf_op jit(solution)/shard_map/ppermute | solution.py:485
  51.0 11.4 %collective-permute-start.18 = (bf16[2,528,128]{2,1,0:T(8,128)(2,1)S(1)}, bf16[2,528,128]{2,1,0:T(8,128)(2,1)S(1)}, u32[]{:S(2)}, u32[]{:S(2)}) collective-permute-start(bf16[2,528,128]{2,1,0:T(8,128)(2,1)S(1)} %shard_map.86), channel_id=1, source_target_pairs={{0,2},{4,0},{8,4},{12,8},{14,12},{10,14},{6,10},{2,6},{1,3},{5,1},... | collective-permute-start | bytes 811016 | tf_op jit(solution)/shard_map/ppermute | solution.py:507
  59.4 24.6 %copy-start.4 = (bf16[1,2,64,512]{3,2,1,0:T(8,128)(2,1)S(1)}, bf16[1,2,64,512]{3,2,1,0:T(8,128)(2,1)}, u32[]{:S(2)}) copy-start(bf16[1,2,64,512]{3,2,1,0:T(8,128)(2,1)} %param.7) | copy-start | bytes 393220
  59.4 8.8 %collective-permute-start.15 = (bf16[2,528,128]{2,1,0:T(8,128)(2,1)S(1)}, bf16[2,528,128]{2,1,0:T(8,128)(2,1)S(1)}, u32[]{:S(2)}, u32[]{:S(2)}) collective-permute-start(bf16[2,528,128]{2,1,0:T(8,128)(2,1)S(1)} %shard_map.90), channel_id=1, source_target_pairs={{0,4},{4,8},{8,12},{12,14},{14,10},{10,6},{6,2},{2,0},{1,5},{5,9},... | collective-permute-start | bytes 811016 | tf_op jit(solution)/shard_map/ppermute | solution.py:526
  60.5 7.9 %collective-permute-start.16 = (bf16[2,528,128]{2,1,0:T(8,128)(2,1)S(1)}, bf16[2,528,128]{2,1,0:T(8,128)(2,1)S(1)}, u32[]{:S(2)}, u32[]{:S(2)}) collective-permute-start(bf16[2,528,128]{2,1,0:T(8,128)(2,1)S(1)} %shard_map.88), channel_id=1, source_target_pairs={{0,2},{4,0},{8,4},{12,8},{14,12},{10,14},{6,10},{2,6},{1,3},{5,1},... | collective-permute-start | bytes 811016 | tf_op jit(solution)/shard_map/ppermute | solution.py:526
  63.1 10.9 %collective-permute-start.21 = (bf16[2,528,128]{2,1,0:T(8,128)(2,1)S(1)}, bf16[2,528,128]{2,1,0:T(8,128)(2,1)S(1)}, u32[]{:S(2)}, u32[]{:S(2)}) collective-permute-start(bf16[2,528,128]{2,1,0:T(8,128)(2,1)S(1)} %shard_map.91), channel_id=1, source_target_pairs={{0,4},{4,8},{8,12},{12,14},{14,10},{10,6},{6,2},{2,0},{1,5},{5,9},... | collective-permute-start | bytes 811016 | tf_op jit(solution)/shard_map/ppermute | solution.py:526
  66.1 8.4 %collective-permute-start.22 = (bf16[2,528,128]{2,1,0:T(8,128)(2,1)S(1)}, bf16[2,528,128]{2,1,0:T(8,128)(2,1)S(1)}, u32[]{:S(2)}, u32[]{:S(2)}) collective-permute-start(bf16[2,528,128]{2,1,0:T(8,128)(2,1)S(1)} %shard_map.92), channel_id=1, source_target_pairs={{0,2},{4,0},{8,4},{12,8},{14,12},{10,14},{6,10},{2,6},{1,3},{5,1},... | collective-permute-start | bytes 811016 | tf_op jit(solution)/shard_map/ppermute | solution.py:526
  69.0 10.7 %collective-permute-start.19 = (bf16[2,528,128]{2,1,0:T(8,128)(2,1)S(1)}, bf16[2,528,128]{2,1,0:T(8,128)(2,1)S(1)}, u32[]{:S(2)}, u32[]{:S(2)}) collective-permute-start(bf16[2,528,128]{2,1,0:T(8,128)(2,1)S(1)} %shard_map.93), channel_id=1, source_target_pairs={{0,4},{4,8},{8,12},{12,14},{14,10},{10,6},{6,2},{2,0},{1,5},{5,9},... | collective-permute-start | bytes 811016 | tf_op jit(solution)/shard_map/ppermute | solution.py:526
  72.3 8.0 %collective-permute-start.20 = (bf16[2,528,128]{2,1,0:T(8,128)(2,1)S(1)}, bf16[2,528,128]{2,1,0:T(8,128)(2,1)S(1)}, u32[]{:S(2)}, u32[]{:S(2)}) collective-permute-start(bf16[2,528,128]{2,1,0:T(8,128)(2,1)S(1)} %shard_map.94), channel_id=1, source_target_pairs={{0,2},{4,0},{8,4},{12,8},{14,12},{10,14},{6,10},{2,6},{1,3},{5,1},... | collective-permute-start | bytes 811016 | tf_op jit(solution)/shard_map/ppermute | solution.py:526
  75.1 12.1 %collective-permute-start.25 = (bf16[2,528,128]{2,1,0:T(8,128)(2,1)S(1)}, bf16[2,528,128]{2,1,0:T(8,128)(2,1)S(1)}, u32[]{:S(2)}, u32[]{:S(2)}) collective-permute-start(bf16[2,528,128]{2,1,0:T(8,128)(2,1)S(1)} %shard_map.95), channel_id=1, source_target_pairs={{0,4},{4,8},{8,12},{12,14},{14,10},{10,6},{6,2},{2,0},{1,5},{5,9},... | collective-permute-start | bytes 811016 | tf_op jit(solution)/shard_map/ppermute | solution.py:526
  78.1 9.2 %collective-permute-start.26 = (bf16[2,528,128]{2,1,0:T(8,128)(2,1)S(1)}, bf16[2,528,128]{2,1,0:T(8,128)(2,1)S(1)}, u32[]{:S(2)}, u32[]{:S(2)}) collective-permute-start(bf16[2,528,128]{2,1,0:T(8,128)(2,1)S(1)} %shard_map.96), channel_id=1, source_target_pairs={{0,2},{4,0},{8,4},{12,8},{14,12},{10,14},{6,10},{2,6},{1,3},{5,1},... | collective-permute-start | bytes 811016 | tf_op jit(solution)/shard_map/ppermute | solution.py:526
  81.0 8.1 %collective-permute-start.23 = (bf16[2,528,128]{2,1,0:T(8,128)(2,1)S(1)}, bf16[2,528,128]{2,1,0:T(8,128)(2,1)S(1)}, u32[]{:S(2)}, u32[]{:S(2)}) collective-permute-start(bf16[2,528,128]{2,1,0:T(8,128)(2,1)S(1)} %shard_map.97), channel_id=1, source_target_pairs={{0,4},{4,8},{8,12},{12,14},{14,10},{10,6},{6,2},{2,0},{1,5},{5,9},... | collective-permute-start | bytes 811016 | tf_op jit(solution)/shard_map/ppermute | solution.py:526
  83.9 7.0 %collective-permute-start.24 = (bf16[2,528,128]{2,1,0:T(8,128)(2,1)S(1)}, bf16[2,528,128]{2,1,0:T(8,128)(2,1)S(1)}, u32[]{:S(2)}, u32[]{:S(2)}) collective-permute-start(bf16[2,528,128]{2,1,0:T(8,128)(2,1)S(1)} %shard_map.98), channel_id=1, source_target_pairs={{0,2},{4,0},{8,4},{12,8},{14,12},{10,14},{6,10},{2,6},{1,3},{5,1},... | collective-permute-start | bytes 811016 | tf_op jit(solution)/shard_map/ppermute | solution.py:526
  91.6 6.8 %collective-permute-start.27 = (bf16[2,528,128]{2,1,0:T(8,128)(2,1)S(1)}, bf16[2,528,128]{2,1,0:T(8,128)(2,1)S(1)}, u32[]{:S(2)}, u32[]{:S(2)}) collective-permute-start(bf16[2,528,128]{2,1,0:T(8,128)(2,1)S(1)} %shard_map.100), channel_id=1, source_target_pairs={{0,2},{4,0},{8,4},{12,8},{14,12},{10,14},{6,10},{2,6},{1,3},{5,1},... | collective-permute-start | bytes 811016 | tf_op jit(solution)/shard_map/ppermute | solution.py:526
  92.6 8.1 %collective-permute-start.28 = (bf16[2,528,128]{2,1,0:T(8,128)(2,1)S(1)}, bf16[2,528,128]{2,1,0:T(8,128)(2,1)S(1)}, u32[]{:S(2)}, u32[]{:S(2)}) collective-permute-start(bf16[2,528,128]{2,1,0:T(8,128)(2,1)S(1)} %shard_map.101), channel_id=1, source_target_pairs={{0,4},{4,8},{8,12},{12,14},{14,10},{10,6},{6,2},{2,0},{1,5},{5,9},... | collective-permute-start | bytes 811016 | tf_op jit(solution)/shard_map/ppermute | solution.py:526

commit v11 on v10

v11 whole, which is shorter than its diff:
```python
import functools

import jax
import jax.numpy as jnp
from jax import lax
from jax.experimental import pallas as pl
from jax.experimental.pallas import tpu as pltpu
from jax.sharding import PartitionSpec as P

HEAD_SIZE = 128
LOG2E = 1.4426950408889634
DEAD = -1e30
FLOOR = -1e29
STAT_ROWS = 16
LIST_ROWS = 16
GRANT = 20 * 1024 * 1024
LIGHT = pl.CostEstimate(flops=1, bytes_accessed=1, transcendentals=0)
VMEM = pl.BlockSpec(memory_space=pltpu.VMEM)
SMEM = pl.BlockSpec(memory_space=pltpu.SMEM)
HBM = pl.BlockSpec(memory_space=pltpu.HBM)


def shifted(block, axis, distance):
    devices = range(lax.axis_size(axis))
    route = [((i - distance) % len(devices), i) for i in devices]
    return lax.ppermute(block, axis, route)


def block_update(state, head_count, key_rows, value_rows, live, scale):
    top_old, total_old, acc_old = state
    scores = (
        jnp.einsum("qhgd,khd->hgqk", head_count, key_rows, preferred_element_type=jnp.float32)
        * scale
    )
    scores = jnp.where(live, scores, -1e30)
    top_new = jnp.maximum(top_old, jnp.max(scores, axis=-1))
    weights = jnp.where(live, jnp.exp(scores - top_new[..., None]), 0.0)
    factor = jnp.exp(top_old - top_new)
    total_new = total_old * factor + jnp.sum(weights, axis=-1)
    product = jnp.einsum(
        "hgqk,khd->hgqd",
        weights.astype(jnp.bfloat16),
        value_rows,
        preferred_element_type=jnp.float32,
    )
    return (top_new, total_new, acc_old * factor[..., None] + product)


def pages_travel(queries, suffix_key_value, kv_pages, page_table, prefix_pages, new_slots):
    stores = lax.axis_size("store")
    pages_dev = kv_pages.shape[0]
    maxp = page_table.shape[1]
    cap = maxp // stores
    page_len = kv_pages.shape[2]
    width = kv_pages.shape[3]
    kv_heads = width // HEAD_SIZE
    suffix = queries.shape[1]
    groups_per_head = queries.shape[2] // width
    scale = HEAD_SIZE ** (-0.5)
    length = prefix_pages[0]
    table = page_table[0]
    owners = table // pages_dev
    local_ids = table % pages_dev
    entries = jnp.arange(maxp, dtype=jnp.int32)
    same_owner = (owners[:, None] == owners[None, :]) & (entries[:, None] < entries[None, :])
    ranks = jnp.sum(same_owner.astype(jnp.int32), axis=0)
    slots = owners * cap + ranks
    placed = slots[:, None] == entries[None, :]
    slot_entry = jnp.sum(jnp.where(placed, entries[:, None], 0), axis=0)
    wanted = jnp.sum(jnp.where(placed, local_ids[:, None], 0), axis=0)
    asked = lax.all_to_all(
        wanted.reshape(stores, cap), "store", split_axis=0, concat_axis=0, tiled=True
    )
    served = kv_pages[asked.reshape(-1)].reshape(stores, cap, 2, page_len, width)
    received = lax.all_to_all(served, "store", split_axis=0, concat_axis=0, tiled=True).reshape(
        maxp, 2, page_len, width
    )
    head_count = queries[0].reshape(suffix, kv_heads, groups_per_head, HEAD_SIZE)
    own_keys = suffix_key_value[0, 0].reshape(suffix, kv_heads, HEAD_SIZE)
    own_values = suffix_key_value[0, 1].reshape(suffix, kv_heads, HEAD_SIZE)
    rows = jnp.arange(suffix, dtype=jnp.int32)
    causal = rows[None, :] <= rows[:, None]
    start_state = (
        jnp.full((kv_heads, groups_per_head, suffix), -1e30, jnp.float32),
        jnp.zeros((kv_heads, groups_per_head, suffix), jnp.float32),
        jnp.zeros((kv_heads, groups_per_head, suffix, HEAD_SIZE), jnp.float32),
    )
    state = block_update(start_state, head_count, own_keys, own_values, causal, scale)
    block_pages = min(8, maxp)
    live_pages = slot_entry < length
    trips = maxp // block_pages

    def step_block(index, carry):
        first = index * block_pages
        block = lax.dynamic_slice_in_dim(received, first, block_pages, 0)
        alive = lax.dynamic_slice_in_dim(live_pages, first, block_pages, 0)
        alive = jnp.broadcast_to(alive[:, None], (block_pages, page_len)).reshape(
            1, block_pages * page_len
        )
        block_keys = block[:, 0].reshape(block_pages * page_len, kv_heads, HEAD_SIZE)
        block_values = block[:, 1].reshape(block_pages * page_len, kv_heads, HEAD_SIZE)
        return block_update(carry, head_count, block_keys, block_values, alive, scale)

    top_final, total_final, acc_final = lax.fori_loop(0, trips, step_block, state)
    output = acc_final / total_final[..., None]
    attended = (
        output.transpose(2, 0, 1, 3)
        .reshape(1, suffix, groups_per_head * width)
        .astype(jnp.bfloat16)
    )
    arrived, arrived_slot = shifted((suffix_key_value, new_slots), "store", stores // 2)
    new_store = lax.dynamic_update_slice_in_dim(kv_pages, arrived, arrived_slot[0], 0)
    return (attended, new_store)


def dot_nt(a, b):
    return lax.dot_general(a, b, (((1,), (1,)), ((), ())), preferred_element_type=jnp.float32)


def block_of(j):
    return slice(j * HEAD_SIZE, (j + 1) * HEAD_SIZE)


def iota(shape, dim):
    return lax.broadcasted_iota(jnp.int32, shape, dim)


def pack_stats(top, total):
    diagonal = iota((HEAD_SIZE, HEAD_SIZE), 0) == iota((HEAD_SIZE, HEAD_SIZE), 1)
    row = iota((STAT_ROWS, HEAD_SIZE), 0)
    tile = jnp.zeros((STAT_ROWS, HEAD_SIZE), jnp.float32)

    def along(x):
        return jnp.sum(jnp.where(diagonal, x, 0.0), 0, keepdims=True)

    for j, (m, l) in enumerate(zip(top, total)):
        l = along(l)
        high = l.astype(jnp.bfloat16).astype(jnp.float32)
        for t, x in enumerate((along(m), high, l - high)):
            tile = jnp.where(row == 4 * t + j, x, tile)
    return tile.astype(jnp.bfloat16)


def unpack_stats(tile):
    row = iota((STAT_ROWS, 8 * HEAD_SIZE), 0)
    block = iota((STAT_ROWS, 8 * HEAD_SIZE), 1) // HEAD_SIZE
    j = block // 2
    stat = block % 2
    spread = (
        ((row == j) & (stat == 0)) | ((row == j + 4) & (stat == 1)) | ((row == j + 8) & (stat == 1))
    )
    spread = spread.astype(jnp.float32).astype(jnp.bfloat16)
    turned = tile.astype(jnp.float32).T.astype(jnp.bfloat16)
    wide = jnp.dot(turned, spread, preferred_element_type=jnp.float32)
    part = lambda b: wide[:, b * HEAD_SIZE:(b + 1) * HEAD_SIZE]
    return [part(2 * j) for j in range(4)], [part(2 * j + 1) for j in range(4)]


def attend_kernel(sizes, own, keeping, *refs):
    heads, rows, suffix, cap, page_len = sizes
    refs = list(refs)
    meta, q_ref = refs.pop(0), refs.pop(0)
    own_kv = refs.pop(0) if own else None
    held, acc_ref, stat_ref = refs.pop(0), refs.pop(0), refs.pop(0)
    stored = refs.pop(0) if keeping else None
    scores = refs.pop(0)
    late_scores = refs.pop(0) if own else None
    if keeping:
        keep = pltpu.make_async_copy(held, stored, refs.pop(0))
        keep.start()
    factor = HEAD_SIZE ** (-0.5) * LOG2E
    keys = cap * page_len

    def stacked(part, h):
        return jnp.concatenate([held[meta[0, c], part, :, block_of(h)] for c in range(cap)], 0)

    def score(h):
        q = q_ref[h * rows:(h + 1) * rows, :]
        scores[h % 2] = dot_nt(q, stacked(0, h))
        if own:
            at = iota((rows, suffix), 0) % suffix
            causal = iota((rows, suffix), 1) <= at
            late_scores[h % 2] = jnp.where(causal, dot_nt(q, own_kv[0, :, block_of(h)]), DEAD)

    def weigh(h):
        live = iota((1, keys), 1) < meta[0, cap] * page_len
        s = jnp.where(live, scores[h % 2], DEAD)
        top = jnp.max(s, axis=-1, keepdims=True)
        if own:
            top = jnp.maximum(top, jnp.max(late_scores[h % 2], axis=-1, keepdims=True))
        top = jnp.maximum(top * factor, FLOOR).astype(jnp.bfloat16).astype(jnp.float32)
        p = jnp.exp2(s * factor - top).astype(jnp.bfloat16)
        v = stacked(1, h)
        v = jnp.concatenate([v, jnp.ones_like(v)], 1)
        out = jnp.dot(p, v, preferred_element_type=jnp.float32)
        if own:
            p = jnp.exp2(late_scores[h % 2] * factor - top).astype(jnp.bfloat16)
            v = own_kv[1, :, block_of(h)]
            v = jnp.concatenate([v, jnp.ones_like(v)], 1)
            out = out + jnp.dot(p, v, preferred_element_type=jnp.float32)
        acc_ref[h] = out[:, :HEAD_SIZE]
        total = out[:, HEAD_SIZE:]
        top = jnp.broadcast_to(top, total.shape)
        blocks = [block_of(j) for j in range(rows // HEAD_SIZE)]
        stat_ref[h] = pack_stats([top[j] for j in blocks], [total[j] for j in blocks])

    for h in range(heads + 1):
        if h < heads:
            score(h)
        if h > 0:
            weigh(h - 1)
    if keeping:
        keep.wait()


def attend(sizes, meta, queries, held, own=None, keeping=False, weight=1):
    heads, rows, suffix, cap, page_len = sizes
    keys = cap * page_len
    shapes = [
        jax.ShapeDtypeStruct((heads, rows, HEAD_SIZE), jnp.float32),
        jax.ShapeDtypeStruct((heads, STAT_ROWS, HEAD_SIZE), jnp.bfloat16),
    ]
    specs = [VMEM, VMEM]
    scratch = [pltpu.VMEM((2, rows, keys), jnp.float32)]
    more = [held]
    if own is not None:
        more = [own, held]
        scratch.append(pltpu.VMEM((2, rows, suffix), jnp.float32))
    if keeping:
        shapes.append(jax.ShapeDtypeStruct(held.shape, held.dtype))
        specs.append(HBM)
        scratch.append(pltpu.SemaphoreType.DMA)
    acc, stat, *pages = pl.pallas_call(
        functools.partial(attend_kernel, sizes, own is not None, keeping),
        out_shape=shapes,
        in_specs=[SMEM] + [VMEM] * (1 + len(more)),
        out_specs=specs,
        scratch_shapes=scratch,
        compiler_params=pltpu.CompilerParams(vmem_limit_bytes=GRANT),
        cost_estimate=pl.CostEstimate(
            flops=weight * heads * rows * keys * HEAD_SIZE * 8,
            bytes_accessed=weight * heads * (rows * 6 + keys * 4) * HEAD_SIZE,
            transcendentals=weight * heads * rows * keys,
        ),
    )(meta, queries, *more)
    return (acc, stat), *pages


def place_kernel(column, near_ref, below_ref, above_ref, page_ref, old_ref, out_ref, sem):
    slot = jnp.where(near_ref[0] == 1, below_ref[0, column], above_ref[0, column])
    copy = pltpu.make_async_copy(page_ref.at[0], out_ref.at[slot], sem)
    copy.start()
    copy.wait()


def place_page(column, near, below, above, page, store):
    return pl.pallas_call(
        functools.partial(place_kernel, column),
        out_shape=jax.ShapeDtypeStruct(store.shape, store.dtype),
        in_specs=[SMEM, SMEM, SMEM, VMEM, HBM],
        out_specs=HBM,
        scratch_shapes=[pltpu.SemaphoreType.DMA],
        input_output_aliases={4: 0},
        compiler_params=pltpu.CompilerParams(vmem_limit_bytes=GRANT),
        cost_estimate=LIGHT,
    )(near, below, above, page, store)


def blend(parts):
    top = functools.reduce(jnp.maximum, [m for _, m, _ in parts])
    scales = [jnp.exp2(m - top) for _, m, _ in parts]
    acc = sum(a * f for (a, _, _), f in zip(parts, scales))
    total = sum(l * f for (_, _, l), f in zip(parts, scales))
    return acc, top, total


def pack_kernel(acc_ref, stat_ref, out_ref):
    heads, rows = acc_ref.shape[:2]
    for h in range(heads):
        out_ref[h, :rows, :] = acc_ref[h].astype(jnp.bfloat16)
        out_ref[h, rows:, :] = stat_ref[h]


def merge_kernel(in_ref, acc_ref, stat_ref, out_ref):
    heads, rows = acc_ref.shape[:2]
    for h in range(heads):
        in_top, in_total = unpack_stats(in_ref[h, rows:, :])
        my_top, my_total = unpack_stats(stat_ref[h])
        tops, totals = [], []
        for j in range(rows // HEAD_SIZE):
            acc, top, total = blend(
                [
                    (in_ref[h, block_of(j), :].astype(jnp.float32), in_top[j], in_total[j]),
                    (acc_ref[h, block_of(j), :], my_top[j], my_total[j]),
                ]
            )
            out_ref[h, block_of(j), :] = acc.astype(out_ref.dtype)
            tops.append(top)
            totals.append(total)
        out_ref[h, rows:, :] = pack_stats(tops, totals)


def final_kernel(suffix, in_ref, acc_ref, stat_ref, out_ref, done, sems):
    heads, rows = acc_ref.shape[:2]
    groups = rows // suffix
    copies = []
    for h in range(heads):
        in_top, in_total = unpack_stats(in_ref[h, rows:, :])
        my_top, my_total = unpack_stats(stat_ref[h])
        for j in range(rows // HEAD_SIZE):
            acc, _, total = blend(
                [
                    (in_ref[h, block_of(j), :].astype(jnp.float32), in_top[j], in_total[j]),
                    (acc_ref[h, block_of(j), :], my_top[j], my_total[j]),
                ]
            )
            out = (acc / total).astype(jnp.bfloat16)
            for i in range(HEAD_SIZE // suffix):
                g = h * groups + j * (HEAD_SIZE // suffix) + i
                done[0, :, block_of(g)] = out[i * suffix:(i + 1) * suffix]
        span = pl.ds(h * groups * HEAD_SIZE, groups * HEAD_SIZE)
        copies.append(
            pltpu.make_async_copy(done.at[:, :, span], out_ref.at[:, :, span], sems.at[h])
        )
        copies[-1].start()
    for copy in copies:
        copy.wait()


def finish(suffix, like, block, part):
    return pl.pallas_call(
        functools.partial(final_kernel, suffix),
        out_shape=jax.ShapeDtypeStruct(like.shape, like.dtype),
        in_specs=[VMEM] * 3,
        out_specs=HBM,
        scratch_shapes=[
            pltpu.VMEM(like.shape, like.dtype),
            pltpu.SemaphoreType.DMA((part[0].shape[0],)),
        ],
        compiler_params=pltpu.CompilerParams(vmem_limit_bytes=GRANT),
    )(block, *part)


def call(kernel, shape, *args):
    size = sum(a.size * a.dtype.itemsize for a in args)
    return pl.pallas_call(
        kernel,
        out_shape=shape,
        in_specs=[VMEM] * len(args),
        out_specs=[VMEM] * len(shape) if isinstance(shape, list) else VMEM,
        compiler_params=pltpu.CompilerParams(vmem_limit_bytes=GRANT),
        cost_estimate=pl.CostEstimate(flops=size, bytes_accessed=2 * size, transcendentals=0),
    )(*args)


def prepare_kernel(cap, pages_dev, length_ref, slot_ref, table_ref, q_ref, out_ref):
    maxp = table_ref.shape[1]
    suffix = q_ref.shape[1]
    rows = out_ref.shape[0] - LIST_ROWS
    for g in range(rows // suffix):
        out_ref[g * suffix:(g + 1) * suffix, :] = q_ref[0, :, block_of(g)]
    table = table_ref[...]
    owner = lax.div(table, pages_dev)
    local = (table - owner * pages_dev).astype(jnp.float32)
    owner = owner.astype(jnp.float32)
    down, along = iota((maxp, maxp), 0), iota((maxp, maxp), 1)

    def turned(x):
        return jnp.sum(jnp.where(down == along, x, 0.0), 1, keepdims=True)

    before = (turned(owner) == owner) & (along < down)
    rank = jnp.sum(jnp.where(before, 1.0, 0.0), 1, keepdims=True)
    place = iota((maxp, HEAD_SIZE), 1)
    live = jnp.where(iota((maxp, HEAD_SIZE), 0) < length_ref[0], 1.0, 0.0)
    ids = jnp.where(rank == place.astype(jnp.float32), turned(local), 0.0)
    fields = jnp.where(place < cap, ids, jnp.where(place == cap, live, 0.0))
    owned = jnp.where(owner == iota((LIST_ROWS, maxp), 0).astype(jnp.float32), 1.0, 0.0)
    lists = jnp.dot(
        owned.astype(jnp.bfloat16), fields.astype(jnp.bfloat16), preferred_element_type=jnp.float32
    )
    slot = slot_ref[0].astype(jnp.float32)
    lists = jnp.where(iota(lists.shape, 1) == cap + 1, slot, lists)
    out_ref[rows:, :] = lists.astype(jnp.bfloat16)


def prepare(cap, pages_dev, queries, page_table, prefix_pages, new_slots):
    rows = queries.size // HEAD_SIZE
    return pl.pallas_call(
        functools.partial(prepare_kernel, cap, pages_dev),
        out_shape=jax.ShapeDtypeStruct((rows + LIST_ROWS, HEAD_SIZE), queries.dtype),
        in_specs=[SMEM, SMEM, VMEM, VMEM],
        out_specs=VMEM,
        compiler_params=pltpu.CompilerParams(vmem_limit_bytes=GRANT),
    )(prefix_pages, new_slots, page_table, queries)


def queries_travel(queries, suffix_key_value, kv_pages, page_table, prefix_pages, new_slots):
    stores = lax.axis_size("store")
    cores = lax.axis_size("tensor")
    pages_dev, _, page_len, width = kv_pages.shape
    cap = page_table.shape[1] // stores
    heads = width // HEAD_SIZE
    suffix = queries.shape[1]
    rows = queries.shape[2] // width * suffix
    sizes = (heads, rows, suffix, cap, page_len)
    half = stores // 2
    me = lax.axis_index("store")

    order = list(range(0, stores, 2)) + list(range(1, stores, 2))[::-1]
    route = [
        (order[i] * cores + core, order[(i + 1 - 2 * (core % 2)) % stores] * cores + core)
        for core in range(cores)
        for i in range(stores)
    ]

    def onward(x):
        return lax.ppermute(x, ("store", "tensor"), route)

    def listed(x):
        row = lax.dynamic_slice(x, (heads * rows + me, 0), (1, HEAD_SIZE))
        return row.astype(jnp.int32)

    def after(values, token):
        return lax.optimization_barrier((values, token))[0]

    mine = prepare(cap, pages_dev, queries, page_table, prefix_pages, new_slots)
    moving = onward(mine)
    arrived = shifted(after(suffix_key_value, mine), "store", half)

    own, store = attend(
        sizes, listed(mine), mine, kv_pages, suffix_key_value[0], True, weight=8
    )
    token = own
    partial = None
    lists = {}
    for step in range(1, stores):
        came = after(moving, token)
        if step < stores - 1:
            moving = onward(came)
        lists[step] = listed(came)
        part, = attend(sizes, lists[step], came, kv_pages)
        if step == 1:
            block = packed(after(part, arrived))
        else:
            block = merged(after(partial, part), part)
        partial = onward(block)
        token = block
    attended = finish(suffix, queries, partial, own)

    near = ((me >= half) == (me % 2 == 0)) == (lax.axis_index("tensor") % 2 == 0)
    quarter = stores // 4
    store = place_page(
        cap + 1,
        near.astype(jnp.int32)[None],
        lists[quarter],
        lists[stores - quarter],
        arrived,
        after(store, token),
    )
    return (attended, store)


def wire_of(part):
    heads, rows, columns = part[0].shape
    return jax.ShapeDtypeStruct((heads, rows + STAT_ROWS, columns), jnp.bfloat16)


def packed(part):
    return call(pack_kernel, wire_of(part), *part)


def merged(block, part):
    return call(merge_kernel, wire_of(part), block, *part)


def on_device(queries, suffix_key_value, kv_pages, page_table, prefix_pages, new_slots):
    stores = lax.axis_size("store")
    pulled = page_table.shape[1] // stores * kv_pages[0].size
    pushed = 2 * queries[0].size
    arrays = (queries, suffix_key_value, kv_pages, page_table, prefix_pages, new_slots)
    if pulled >= pushed and stores % 8 == 0 and stores <= LIST_ROWS:
        return queries_travel(*arrays)
    return pages_travel(*arrays)


def solution(mesh):
    return jax.shard_map(
        on_device,
        mesh=mesh,
        in_specs=(
            P(("groups", "store"), None, "tensor"),
            P(("groups", "store"), None, None, "tensor"),
            P(("groups", "store"), None, None, "tensor"),
            P(("groups", "store"), None),
            P(("groups", "store")),
            P(("groups", "store")),
        ),
        out_specs=(
            P(("groups", "store"), None, "tensor"),
            P(("groups", "store"), None, None, "tensor"),
        ),
        check_vma=False,
    )
```

time: 103 us -> 103 us (level)
  waiting for transfers between devices: 21.5 us -> 28.1 us
  Pallas kernels: 32.6 us -> 28.3 us
  starting transfers between devices: 41 us -> 38.8 us
    ppermute x28 -> x14, waiting for transfers between devices: 18.2 us -> 28.1 us  [onward(): return lax.ppermute(x, ('store', 'tensor'), route)]
    ppermute x1, waiting for transfers between devices: 3.29 us -> 0.01 us  [shifted(): return lax.ppermute(block, axis, route)]
    pallas_call x11 -> x9, Pallas kernels: 22.9 us -> 20.5 us  [the longest x8 19.3 us: attend(): pl.pallas_call(functools.partial(attend_kernel, sizes, own is not None, k...]
    pallas_call x16 -> x7, Pallas kernels: 7.75 us -> 5.93 us  [call(): pl.pallas_call(kernel, out_shape=shape, in_specs=[VMEM] * len(args), out_...]
    ppermute x1, starting transfers between devices: 4.06 us -> 2.59 us  [shifted(): return lax.ppermute(block, axis, route)]
    ppermute x28 -> x14, starting transfers between devices: 36.9 us -> 36.2 us  [onward(): return lax.ppermute(x, ('store', 'tensor'), route)]
    unnamed x12 -> x10, local copies, waits for them, and re-layouts: 4.79 us -> 4.78 us
  transfers between devices with their start and end apart: 29 -> 15, of which waited for: 14 -> 13; matrix products, arithmetic and copies ran while one was open for 0% -> 0% of each run, Pallas kernels for 29% -> 25%
where the time goes in v11:
time: 103 us; the launch traced here: 102 us
  starting transfers between devices  38.8 us (38%)
  Pallas kernels  28.3 us (27%)
  waiting for transfers between devices  28.1 us (27%)
  local copies, waits for them, and re-layouts  4.78 us (5%)
  between operations  2.24 us (2%)
    ppermute x14, starting transfers between devices, onward(): return lax.ppermute(x, ('store', 'tensor'), route)  36.2 us
    ppermute x14, waiting for transfers between devices, onward(): return lax.ppermute(x, ('store', 'tensor'), route)  28.1 us
    pallas_call x8, Pallas kernels, attend(): pl.pallas_call(functools.partial(attend_kernel, sizes, own is not None, k...  19.3 us
    pallas_call x7, Pallas kernels, call(): pl.pallas_call(kernel, out_shape=shape, in_specs=[VMEM] * len(args), out_...  5.93 us
    unnamed x10, local copies, waits for them, and re-layouts  4.78 us
    ppermute x1, starting transfers between devices, shifted(): return lax.ppermute(block, axis, route)  2.59 us
  transfers between devices with their start and end apart: 15, of which 13 were waited for; matrix products, arithmetic and copies ran while one was open for 0% of the time, Pallas kernels for 25%

profile of v11, /device:TPU:0, one launch (start us, length us, event | category | flops | bytes accessed | tf_op | source)
XLA Modules:
  0.0 102.3 jit_solution(16699260668160746601)
XLA Ops:
  1.9 0.0 copy-start.2
  1.9 1.0 %copy-done.2 = bf16[1,64,4096]{2,1,0:T(8,128)(2,1)S(1)} copy-done((bf16[1,64,4096]{2,1,0:T(8,128)(2,1)S(1)}, bf16[1,64,4096]{2,1,0:T(8,128)(2,1)}, u32[]{:S(2)}) %copy-start.2) | copy-done | bytes 524312
  3.0 0.0 copy-start.3
  3.0 0.7 copy-done.3
  3.6 0.3 shard_map.77.refs_1_
  3.9 3.0 %collective-permute-start = (bf16[2064,128]{1,0:T(8,128)(2,1)S(1)}, bf16[2064,128]{1,0:T(8,128)(2,1)S(1)}, u32[]{:S(2)}, u32[]{:S(2)}) collective-permute-start(bf16[2064,128]{1,0:T(8,128)(2,1)S(1)} %shard_map.77.refs_1_), channel_id=1, source_target_pairs={{0,4},{4,8},{8,12},{12,14},{14,10},{10,6},{6,2},{2,0},{1,3},{5,1},... | collective-permute-start | bytes 1585160 | tf_op jit(solution)/shard_map/ppermute | solution.py:417
  6.9 2.6 %collective-permute-start.1 = (bf16[1,2,64,512]{3,2,1,0:T(8,128)(2,1)}, bf16[1,2,64,512]{3,2,1,0:T(8,128)(2,1)S(1)}, u32[]{:S(2)}, u32[]{:S(2)}) collective-permute-start(bf16[1,2,64,512]{3,2,1,0:T(8,128)(2,1)} %param.7), channel_id=1, source_target_pairs={{8,0},{10,2},{12,4},{14,6},{0,8},{2,10},{4,12},{6,14},{9,1},{11,3}... | collective-permute-start | bytes 393224 | tf_op jit(solution)/shard_map/ppermute | solution.py:26
  9.5 0.0 copy-start
  9.5 2.2 %copy-done = bf16[32,2,64,512]{3,2,1,0:T(8,128)(2,1)S(1)} copy-done((bf16[32,2,64,512]{3,2,1,0:T(8,128)(2,1)S(1)}, bf16[32,2,64,512]{3,2,1,0:T(8,128)(2,1)}, u32[]{:S(2)}) %copy-start) | copy-done | bytes 4194328
  11.7 0.0 copy-start.4
  11.7 0.9 copy-done.4
  12.6 0.0 copy-start.1
  12.6 3.8 %shard_map.78 = (f32[4,512,128]{2,1,0:T(8,128)S(1)}, bf16[4,16,128]{2,1,0:T(8,128)(2,1)S(1)}, bf16[32,2,64,512]{3,2,1,0:T(8,128)(2,1)}) custom-call(s32[1,128]{1,0:T(1,128)S(1)} %fusion.refs_0_, bf16[2064,128]{1,0:T(8,128)(2,1)S(1)} %shard_map.77.refs_1_, bf16[2,64,512]{2,1,0:T(8,128)(2,1)S(1)} %bitcast.2, bf16[32,2,64,512]{3,2,1,0:T(8,128)(2,1)S(1)} %copy-done), custom_call_target="tpu_custom_call" | custom-call | flops 8589934592 | bytes 20971520 | tf_op jit(solution)/shard_map/pallas_call | solution.py:233
  16.4 0.0 collective-permute-done.refs_1_
  16.4 3.1 %collective-permute-start.3 = (bf16[2064,128]{1,0:T(8,128)(2,1)S(1)}, bf16[2064,128]{1,0:T(8,128)(2,1)S(1)}, u32[]{:S(2)}, u32[]{:S(2)}) collective-permute-start(bf16[2064,128]{1,0:T(8,128)(2,1)S(1)} %collective-permute-done.refs_1_), channel_id=1, source_target_pairs={{0,4},{4,8},{8,12},{12,14},{14,10},{10,6},{6,2},{2,0},{1,3},{5,1},... | collective-permute-start | bytes 1585160 | tf_op jit(solution)/shard_map/ppermute | solution.py:417
  19.5 0.0 copy-done.1
  19.5 2.2 %shard_map.79 = (f32[4,512,128]{2,1,0:T(8,128)S(1)}, bf16[4,16,128]{2,1,0:T(8,128)(2,1)S(1)}) custom-call(s32[1,128]{1,0:T(1,128)S(1)} %fusion.1.refs_0_, bf16[2064,128]{1,0:T(8,128)(2,1)S(1)} %collective-permute-done.refs_1_, bf16[32,2,64,512]{3,2,1,0:T(8,128)(2,1)S(1)} %copy-done.1), custom_call_target="tpu_custom_call" | custom-call | flops 1073741824 | bytes 2621440 | tf_op jit(solution)/shard_map/pallas_call | solution.py:233
  21.7 0.0 collective-permute-done.1.page_ref
  21.7 0.1 shard_map.80
  21.8 2.5 %collective-permute-start.2 = (bf16[4,528,128]{2,1,0:T(8,128)(2,1)S(1)}, bf16[4,528,128]{2,1,0:T(8,128)(2,1)S(1)}, u32[]{:S(2)}, u32[]{:S(2)}) collective-permute-start(bf16[4,528,128]{2,1,0:T(8,128)(2,1)S(1)} %shard_map.80), channel_id=1, source_target_pairs={{0,4},{4,8},{8,12},{12,14},{14,10},{10,6},{6,2},{2,0},{1,3},{5,1},... | collective-permute-start | bytes 1622024 | tf_op jit(solution)/shard_map/ppermute | solution.py:417
  24.3 1.9 %collective-permute-done.3.refs_1_ = bf16[2064,128]{1,0:T(8,128)(2,1)S(1)} collective-permute-done((bf16[2064,128]{1,0:T(8,128)(2,1)S(1)}, bf16[2064,128]{1,0:T(8,128)(2,1)S(1)}, u32[]{:S(2)}, u32[]{:S(2)}) %collective-permute-start.3) | collective-permute-done | bytes 528416 | tf_op jit(solution)/shard_map/ppermute | solution.py:417
  26.2 2.5 %collective-permute-start.5 = (bf16[2064,128]{1,0:T(8,128)(2,1)S(1)}, bf16[2064,128]{1,0:T(8,128)(2,1)S(1)}, u32[]{:S(2)}, u32[]{:S(2)}) collective-permute-start(bf16[2064,128]{1,0:T(8,128)(2,1)S(1)} %collective-permute-done.3.refs_1_), channel_id=1, source_target_pairs={{0,4},{4,8},{8,12},{12,14},{14,10},{10,6},{6,2},{2,0},{1,3},{5,1},... | collective-permute-start | bytes 1585160 | tf_op jit(solution)/shard_map/ppermute | solution.py:417
  28.7 2.2 %shard_map.81 = (f32[4,512,128]{2,1,0:T(8,128)S(1)}, bf16[4,16,128]{2,1,0:T(8,128)(2,1)S(1)}) custom-call(s32[1,128]{1,0:T(1,128)S(1)} %fusion.2.refs_0_.below_ref, bf16[2064,128]{1,0:T(8,128)(2,1)S(1)} %collective-permute-done.3.refs_1_, bf16[32,2,64,512]{3,2,1,0:T(8,128)(2,1)S(1)} %copy-done.1), custom_call_target="tpu_custom_call" | custom-call | flops 1073741824 | bytes 2621440 | tf_op jit(solution)/shard_map/pallas_call | solution.py:233
  30.9 1.1 %collective-permute-done.2.in_ref = bf16[4,528,128]{2,1,0:T(8,128)(2,1)S(1)} collective-permute-done((bf16[4,528,128]{2,1,0:T(8,128)(2,1)S(1)}, bf16[4,528,128]{2,1,0:T(8,128)(2,1)S(1)}, u32[]{:S(2)}, u32[]{:S(2)}) %collective-permute-start.2) | collective-permute-done | bytes 540704 | tf_op jit(solution)/shard_map/ppermute | solution.py:417
  32.0 1.0 shard_map.82
  33.0 2.5 %collective-permute-start.4 = (bf16[4,528,128]{2,1,0:T(8,128)(2,1)S(1)}, bf16[4,528,128]{2,1,0:T(8,128)(2,1)S(1)}, u32[]{:S(2)}, u32[]{:S(2)}) collective-permute-start(bf16[4,528,128]{2,1,0:T(8,128)(2,1)S(1)} %shard_map.82), channel_id=1, source_target_pairs={{0,4},{4,8},{8,12},{12,14},{14,10},{10,6},{6,2},{2,0},{1,3},{5,1},... | collective-permute-start | bytes 1622024 | tf_op jit(solution)/shard_map/ppermute | solution.py:417
  35.5 2.1 %collective-permute-done.5.refs_1_ = bf16[2064,128]{1,0:T(8,128)(2,1)S(1)} collective-permute-done((bf16[2064,128]{1,0:T(8,128)(2,1)S(1)}, bf16[2064,128]{1,0:T(8,128)(2,1)S(1)}, u32[]{:S(2)}, u32[]{:S(2)}) %collective-permute-start.5) | collective-permute-done | bytes 528416 | tf_op jit(solution)/shard_map/ppermute | solution.py:417
  37.7 2.5 %collective-permute-start.7 = (bf16[2064,128]{1,0:T(8,128)(2,1)S(1)}, bf16[2064,128]{1,0:T(8,128)(2,1)S(1)}, u32[]{:S(2)}, u32[]{:S(2)}) collective-permute-start(bf16[2064,128]{1,0:T(8,128)(2,1)S(1)} %collective-permute-done.5.refs_1_), channel_id=1, source_target_pairs={{0,4},{4,8},{8,12},{12,14},{14,10},{10,6},{6,2},{2,0},{1,3},{5,1},... | collective-permute-start | bytes 1585160 | tf_op jit(solution)/shard_map/ppermute | solution.py:417
  40.2 2.2 %shard_map.83 = (f32[4,512,128]{2,1,0:T(8,128)S(1)}, bf16[4,16,128]{2,1,0:T(8,128)(2,1)S(1)}) custom-call(s32[1,128]{1,0:T(1,128)S(1)} %fusion.3.refs_0_, bf16[2064,128]{1,0:T(8,128)(2,1)S(1)} %collective-permute-done.5.refs_1_, bf16[32,2,64,512]{3,2,1,0:T(8,128)(2,1)S(1)} %copy-done.1), custom_call_target="tpu_custom_call" | custom-call | flops 1073741824 | bytes 2621440 | tf_op jit(solution)/shard_map/pallas_call | solution.py:233
  42.4 1.1 %collective-permute-done.4.in_ref = bf16[4,528,128]{2,1,0:T(8,128)(2,1)S(1)} collective-permute-done((bf16[4,528,128]{2,1,0:T(8,128)(2,1)S(1)}, bf16[4,528,128]{2,1,0:T(8,128)(2,1)S(1)}, u32[]{:S(2)}, u32[]{:S(2)}) %collective-permute-start.4) | collective-permute-done | bytes 540704 | tf_op jit(solution)/shard_map/ppermute | solution.py:417
  43.5 1.0 shard_map.84
  44.4 2.5 %collective-permute-start.6 = (bf16[4,528,128]{2,1,0:T(8,128)(2,1)S(1)}, bf16[4,528,128]{2,1,0:T(8,128)(2,1)S(1)}, u32[]{:S(2)}, u32[]{:S(2)}) collective-permute-start(bf16[4,528,128]{2,1,0:T(8,128)(2,1)S(1)} %shard_map.84), channel_id=1, source_target_pairs={{0,4},{4,8},{8,12},{12,14},{14,10},{10,6},{6,2},{2,0},{1,3},{5,1},... | collective-permute-start | bytes 1622024 | tf_op jit(solution)/shard_map/ppermute | solution.py:417
  47.0 2.1 %collective-permute-done.7.refs_1_ = bf16[2064,128]{1,0:T(8,128)(2,1)S(1)} collective-permute-done((bf16[2064,128]{1,0:T(8,128)(2,1)S(1)}, bf16[2064,128]{1,0:T(8,128)(2,1)S(1)}, u32[]{:S(2)}, u32[]{:S(2)}) %collective-permute-start.7) | collective-permute-done | bytes 528416 | tf_op jit(solution)/shard_map/ppermute | solution.py:417
  49.1 2.5 %collective-permute-start.9 = (bf16[2064,128]{1,0:T(8,128)(2,1)S(1)}, bf16[2064,128]{1,0:T(8,128)(2,1)S(1)}, u32[]{:S(2)}, u32[]{:S(2)}) collective-permute-start(bf16[2064,128]{1,0:T(8,128)(2,1)S(1)} %collective-permute-done.7.refs_1_), channel_id=1, source_target_pairs={{0,4},{4,8},{8,12},{12,14},{14,10},{10,6},{6,2},{2,0},{1,3},{5,1},... | collective-permute-start | bytes 1585160 | tf_op jit(solution)/shard_map/ppermute | solution.py:417
  51.6 2.2 %shard_map.85 = (f32[4,512,128]{2,1,0:T(8,128)S(1)}, bf16[4,16,128]{2,1,0:T(8,128)(2,1)S(1)}) custom-call(s32[1,128]{1,0:T(1,128)S(1)} %fusion.4.refs_0_, bf16[2064,128]{1,0:T(8,128)(2,1)S(1)} %collective-permute-done.7.refs_1_, bf16[32,2,64,512]{3,2,1,0:T(8,128)(2,1)S(1)} %copy-done.1), custom_call_target="tpu_custom_call" | custom-call | flops 1073741824 | bytes 2621440 | tf_op jit(solution)/shard_map/pallas_call | solution.py:233
  53.8 1.1 %collective-permute-done.6.in_ref = bf16[4,528,128]{2,1,0:T(8,128)(2,1)S(1)} collective-permute-done((bf16[4,528,128]{2,1,0:T(8,128)(2,1)S(1)}, bf16[4,528,128]{2,1,0:T(8,128)(2,1)S(1)}, u32[]{:S(2)}, u32[]{:S(2)}) %collective-permute-start.6) | collective-permute-done | bytes 540704 | tf_op jit(solution)/shard_map/ppermute | solution.py:417
  54.9 1.0 shard_map.86
  55.9 2.5 %collective-permute-start.8 = (bf16[4,528,128]{2,1,0:T(8,128)(2,1)S(1)}, bf16[4,528,128]{2,1,0:T(8,128)(2,1)S(1)}, u32[]{:S(2)}, u32[]{:S(2)}) collective-permute-start(bf16[4,528,128]{2,1,0:T(8,128)(2,1)S(1)} %shard_map.86), channel_id=1, source_target_pairs={{0,4},{4,8},{8,12},{12,14},{14,10},{10,6},{6,2},{2,0},{1,3},{5,1},... | collective-permute-start | bytes 1622024 | tf_op jit(solution)/shard_map/ppermute | solution.py:417
  58.4 2.1 %collective-permute-done.9.refs_1_ = bf16[2064,128]{1,0:T(8,128)(2,1)S(1)} collective-permute-done((bf16[2064,128]{1,0:T(8,128)(2,1)S(1)}, bf16[2064,128]{1,0:T(8,128)(2,1)S(1)}, u32[]{:S(2)}, u32[]{:S(2)}) %collective-permute-start.9) | collective-permute-done | bytes 528416 | tf_op jit(solution)/shard_map/ppermute | solution.py:417
  60.6 2.5 %collective-permute-start.11 = (bf16[2064,128]{1,0:T(8,128)(2,1)S(1)}, bf16[2064,128]{1,0:T(8,128)(2,1)S(1)}, u32[]{:S(2)}, u32[]{:S(2)}) collective-permute-start(bf16[2064,128]{1,0:T(8,128)(2,1)S(1)} %collective-permute-done.9.refs_1_), channel_id=1, source_target_pairs={{0,4},{4,8},{8,12},{12,14},{14,10},{10,6},{6,2},{2,0},{1,3},{5,1},... | collective-permute-start | bytes 1585160 | tf_op jit(solution)/shard_map/ppermute | solution.py:417
  63.1 2.2 %shard_map.87 = (f32[4,512,128]{2,1,0:T(8,128)S(1)}, bf16[4,16,128]{2,1,0:T(8,128)(2,1)S(1)}) custom-call(s32[1,128]{1,0:T(1,128)S(1)} %fusion.5.refs_0_, bf16[2064,128]{1,0:T(8,128)(2,1)S(1)} %collective-permute-done.9.refs_1_, bf16[32,2,64,512]{3,2,1,0:T(8,128)(2,1)S(1)} %copy-done.1), custom_call_target="tpu_custom_call" | custom-call | flops 1073741824 | bytes 2621440 | tf_op jit(solution)/shard_map/pallas_call | solution.py:233
  65.3 1.1 %collective-permute-done.8.in_ref = bf16[4,528,128]{2,1,0:T(8,128)(2,1)S(1)} collective-permute-done((bf16[4,528,128]{2,1,0:T(8,128)(2,1)S(1)}, bf16[4,528,128]{2,1,0:T(8,128)(2,1)S(1)}, u32[]{:S(2)}, u32[]{:S(2)}) %collective-permute-start.8) | collective-permute-done | bytes 540704 | tf_op jit(solution)/shard_map/ppermute | solution.py:417
  66.4 1.0 shard_map.88
  67.4 2.5 %collective-permute-start.10 = (bf16[4,528,128]{2,1,0:T(8,128)(2,1)S(1)}, bf16[4,528,128]{2,1,0:T(8,128)(2,1)S(1)}, u32[]{:S(2)}, u32[]{:S(2)}) collective-permute-start(bf16[4,528,128]{2,1,0:T(8,128)(2,1)S(1)} %shard_map.88), channel_id=1, source_target_pairs={{0,4},{4,8},{8,12},{12,14},{14,10},{10,6},{6,2},{2,0},{1,3},{5,1},... | collective-permute-start | bytes 1622024 | tf_op jit(solution)/shard_map/ppermute | solution.py:417
  69.9 2.1 %collective-permute-done.11.refs_1_ = bf16[2064,128]{1,0:T(8,128)(2,1)S(1)} collective-permute-done((bf16[2064,128]{1,0:T(8,128)(2,1)S(1)}, bf16[2064,128]{1,0:T(8,128)(2,1)S(1)}, u32[]{:S(2)}, u32[]{:S(2)}) %collective-permute-start.11) | collective-permute-done | bytes 528416 | tf_op jit(solution)/shard_map/ppermute | solution.py:417
  72.0 2.5 %collective-permute-start.13 = (bf16[2064,128]{1,0:T(8,128)(2,1)S(1)}, bf16[2064,128]{1,0:T(8,128)(2,1)S(1)}, u32[]{:S(2)}, u32[]{:S(2)}) collective-permute-start(bf16[2064,128]{1,0:T(8,128)(2,1)S(1)} %collective-permute-done.11.refs_1_), channel_id=1, source_target_pairs={{0,4},{4,8},{8,12},{12,14},{14,10},{10,6},{6,2},{2,0},{1,3},{5,1},... | collective-permute-start | bytes 1585160 | tf_op jit(solution)/shard_map/ppermute | solution.py:417
  74.5 2.2 %shard_map.89 = (f32[4,512,128]{2,1,0:T(8,128)S(1)}, bf16[4,16,128]{2,1,0:T(8,128)(2,1)S(1)}) custom-call(s32[1,128]{1,0:T(1,128)S(1)} %fusion.6.refs_0_.above_ref, bf16[2064,128]{1,0:T(8,128)(2,1)S(1)} %collective-permute-done.11.refs_1_, bf16[32,2,64,512]{3,2,1,0:T(8,128)(2,1)S(1)} %copy-done.1), custom_call_target="tpu_custom_call" | custom-call | flops 1073741824 | bytes 2621440 | tf_op jit(solution)/shard_map/pallas_call | solution.py:233
  76.7 1.1 %collective-permute-done.10.in_ref = bf16[4,528,128]{2,1,0:T(8,128)(2,1)S(1)} collective-permute-done((bf16[4,528,128]{2,1,0:T(8,128)(2,1)S(1)}, bf16[4,528,128]{2,1,0:T(8,128)(2,1)S(1)}, u32[]{:S(2)}, u32[]{:S(2)}) %collective-permute-start.10) | collective-permute-done | bytes 540704 | tf_op jit(solution)/shard_map/ppermute | solution.py:417
  77.8 1.0 shard_map.90
  78.8 2.5 %collective-permute-start.12 = (bf16[4,528,128]{2,1,0:T(8,128)(2,1)S(1)}, bf16[4,528,128]{2,1,0:T(8,128)(2,1)S(1)}, u32[]{:S(2)}, u32[]{:S(2)}) collective-permute-start(bf16[4,528,128]{2,1,0:T(8,128)(2,1)S(1)} %shard_map.90), channel_id=1, source_target_pairs={{0,4},{4,8},{8,12},{12,14},{14,10},{10,6},{6,2},{2,0},{1,3},{5,1},... | collective-permute-start | bytes 1622024 | tf_op jit(solution)/shard_map/ppermute | solution.py:417
  81.3 2.1 %collective-permute-done.13.refs_1_ = bf16[2064,128]{1,0:T(8,128)(2,1)S(1)} collective-permute-done((bf16[2064,128]{1,0:T(8,128)(2,1)S(1)}, bf16[2064,128]{1,0:T(8,128)(2,1)S(1)}, u32[]{:S(2)}, u32[]{:S(2)}) %collective-permute-start.13) | collective-permute-done | bytes 528416 | tf_op jit(solution)/shard_map/ppermute | solution.py:417
  83.5 2.2 %shard_map.91 = (f32[4,512,128]{2,1,0:T(8,128)S(1)}, bf16[4,16,128]{2,1,0:T(8,128)(2,1)S(1)}) custom-call(s32[1,128]{1,0:T(1,128)S(1)} %fusion.7.refs_0_, bf16[2064,128]{1,0:T(8,128)(2,1)S(1)} %collective-permute-done.13.refs_1_, bf16[32,2,64,512]{3,2,1,0:T(8,128)(2,1)S(1)} %copy-done.1), custom_call_target="tpu_custom_call" | custom-call | flops 1073741824 | bytes 2621440 | tf_op jit(solution)/shard_map/pallas_call | solution.py:233
  85.7 3.6 %collective-permute-done.12.in_ref = bf16[4,528,128]{2,1,0:T(8,128)(2,1)S(1)} collective-permute-done((bf16[4,528,128]{2,1,0:T(8,128)(2,1)S(1)}, bf16[4,528,128]{2,1,0:T(8,128)(2,1)S(1)}, u32[]{:S(2)}, u32[]{:S(2)}) %collective-permute-start.12) | collective-permute-done | bytes 540704 | tf_op jit(solution)/shard_map/ppermute | solution.py:417
  89.3 1.0 shard_map.92
  90.3 2.5 %collective-permute-start.14 = (bf16[4,528,128]{2,1,0:T(8,128)(2,1)S(1)}, bf16[4,528,128]{2,1,0:T(8,128)(2,1)S(1)}, u32[]{:S(2)}, u32[]{:S(2)}) collective-permute-start(bf16[4,528,128]{2,1,0:T(8,128)(2,1)S(1)} %shard_map.92), channel_id=1, source_target_pairs={{0,4},{4,8},{8,12},{12,14},{14,10},{10,6},{6,2},{2,0},{1,3},{5,1},... | collective-permute-start | bytes 1622024 | tf_op jit(solution)/shard_map/ppermute | solution.py:417
  92.8 1.2 %shard_map.94 = bf16[32,2,64,512]{3,2,1,0:T(8,128)(2,1)} custom-call(s32[1]{0:T(128)} %bitcast.1.near_ref, s32[1,128]{1,0:T(1,128)S(1)} %fusion.2.refs_0_.below_ref, s32[1,128]{1,0:T(1,128)S(1)} %fusion.6.refs_0_.above_ref, bf16[1,2,64,512]{3,2,1,0:T(8,128)(2,1)S(1)} %collective-permute-done.1.page_ref, ...), custom_call_target="tpu_custom_call", output_to_operand_aliasing={{}: (4, {})} | custom-call | flops 1 | bytes 1 | tf_op jit(solution)/shard_map/pallas_call | solution.py:257
  94.0 6.5 %collective-permute-done.14.in_ref = bf16[4,528,128]{2,1,0:T(8,128)(2,1)S(1)} collective-permute-done((bf16[4,528,128]{2,1,0:T(8,128)(2,1)S(1)}, bf16[4,528,128]{2,1,0:T(8,128)(2,1)S(1)}, u32[]{:S(2)}, u32[]{:S(2)}) %collective-permute-start.14) | collective-permute-done | bytes 540704 | tf_op jit(solution)/shard_map/ppermute | solution.py:417
  100.5 1.6 %shard_map.93 = bf16[1,64,4096]{2,1,0:T(8,128)(2,1)} custom-call(bf16[4,528,128]{2,1,0:T(8,128)(2,1)S(1)} %collective-permute-done.14.in_ref, f32[4,512,128]{2,1,0:T(8,128)S(1)} %get-tuple-element.36.acc_ref, bf16[4,16,128]{2,1,0:T(8,128)(2,1)S(1)} %get-tuple-element.37.stat_ref), custom_call_target="tpu_custom_call" | custom-call | tf_op jit(solution)/shard_map/pallas_call | solution.py:331
  (8 shorter events, 0.1 us)
Async XLA Ops:
  1.9 1.0 %copy-start.2 = (bf16[1,64,4096]{2,1,0:T(8,128)(2,1)S(1)}, bf16[1,64,4096]{2,1,0:T(8,128)(2,1)}, u32[]{:S(2)}) copy-start(bf16[1,64,4096]{2,1,0:T(8,128)(2,1)} %q_ref.1) | copy-start | bytes 1572868
  3.0 0.7 copy-start.3
  3.9 12.5 %collective-permute-start = (bf16[2064,128]{1,0:T(8,128)(2,1)S(1)}, bf16[2064,128]{1,0:T(8,128)(2,1)S(1)}, u32[]{:S(2)}, u32[]{:S(2)}) collective-permute-start(bf16[2064,128]{1,0:T(8,128)(2,1)S(1)} %shard_map.77.refs_1_), channel_id=1, source_target_pairs={{0,4},{4,8},{8,12},{12,14},{14,10},{10,6},{6,2},{2,0},{1,3},{5,1},... | collective-permute-start | bytes 1585160 | tf_op jit(solution)/shard_map/ppermute | solution.py:417
  6.9 14.8 %collective-permute-start.1 = (bf16[1,2,64,512]{3,2,1,0:T(8,128)(2,1)}, bf16[1,2,64,512]{3,2,1,0:T(8,128)(2,1)S(1)}, u32[]{:S(2)}, u32[]{:S(2)}) collective-permute-start(bf16[1,2,64,512]{3,2,1,0:T(8,128)(2,1)} %param.7), channel_id=1, source_target_pairs={{8,0},{10,2},{12,4},{14,6},{0,8},{2,10},{4,12},{6,14},{9,1},{11,3}... | collective-permute-start | bytes 393224 | tf_op jit(solution)/shard_map/ppermute | solution.py:26
  9.5 2.2 %copy-start = (bf16[32,2,64,512]{3,2,1,0:T(8,128)(2,1)S(1)}, bf16[32,2,64,512]{3,2,1,0:T(8,128)(2,1)}, u32[]{:S(2)}) copy-start(bf16[32,2,64,512]{3,2,1,0:T(8,128)(2,1)} %refs_2_.13) | copy-start | bytes 12582916
  11.7 0.9 copy-start.4
  12.6 6.9 %copy-start.1 = (bf16[32,2,64,512]{3,2,1,0:T(8,128)(2,1)S(1)}, bf16[32,2,64,512]{3,2,1,0:T(8,128)(2,1)}, u32[]{:S(2)}) copy-start(bf16[32,2,64,512]{3,2,1,0:T(8,128)(2,1)} %refs_2_.13) | copy-start | bytes 12582916
  16.4 9.8 %collective-permute-start.3 = (bf16[2064,128]{1,0:T(8,128)(2,1)S(1)}, bf16[2064,128]{1,0:T(8,128)(2,1)S(1)}, u32[]{:S(2)}, u32[]{:S(2)}) collective-permute-start(bf16[2064,128]{1,0:T(8,128)(2,1)S(1)} %collective-permute-done.refs_1_), channel_id=1, source_target_pairs={{0,4},{4,8},{8,12},{12,14},{14,10},{10,6},{6,2},{2,0},{1,3},{5,1},... | collective-permute-start | bytes 1585160 | tf_op jit(solution)/shard_map/ppermute | solution.py:417
  21.8 10.2 %collective-permute-start.2 = (bf16[4,528,128]{2,1,0:T(8,128)(2,1)S(1)}, bf16[4,528,128]{2,1,0:T(8,128)(2,1)S(1)}, u32[]{:S(2)}, u32[]{:S(2)}) collective-permute-start(bf16[4,528,128]{2,1,0:T(8,128)(2,1)S(1)} %shard_map.80), channel_id=1, source_target_pairs={{0,4},{4,8},{8,12},{12,14},{14,10},{10,6},{6,2},{2,0},{1,3},{5,1},... | collective-permute-start | bytes 1622024 | tf_op jit(solution)/shard_map/ppermute | solution.py:417
  26.2 11.5 %collective-permute-start.5 = (bf16[2064,128]{1,0:T(8,128)(2,1)S(1)}, bf16[2064,128]{1,0:T(8,128)(2,1)S(1)}, u32[]{:S(2)}, u32[]{:S(2)}) collective-permute-start(bf16[2064,128]{1,0:T(8,128)(2,1)S(1)} %collective-permute-done.3.refs_1_), channel_id=1, source_target_pairs={{0,4},{4,8},{8,12},{12,14},{14,10},{10,6},{6,2},{2,0},{1,3},{5,1},... | collective-permute-start | bytes 1585160 | tf_op jit(solution)/shard_map/ppermute | solution.py:417
  33.0 10.5 %collective-permute-start.4 = (bf16[4,528,128]{2,1,0:T(8,128)(2,1)S(1)}, bf16[4,528,128]{2,1,0:T(8,128)(2,1)S(1)}, u32[]{:S(2)}, u32[]{:S(2)}) collective-permute-start(bf16[4,528,128]{2,1,0:T(8,128)(2,1)S(1)} %shard_map.82), channel_id=1, source_target_pairs={{0,4},{4,8},{8,12},{12,14},{14,10},{10,6},{6,2},{2,0},{1,3},{5,1},... | collective-permute-start | bytes 1622024 | tf_op jit(solution)/shard_map/ppermute | solution.py:417
  37.7 11.5 %collective-permute-start.7 = (bf16[2064,128]{1,0:T(8,128)(2,1)S(1)}, bf16[2064,128]{1,0:T(8,128)(2,1)S(1)}, u32[]{:S(2)}, u32[]{:S(2)}) collective-permute-start(bf16[2064,128]{1,0:T(8,128)(2,1)S(1)} %collective-permute-done.5.refs_1_), channel_id=1, source_target_pairs={{0,4},{4,8},{8,12},{12,14},{14,10},{10,6},{6,2},{2,0},{1,3},{5,1},... | collective-permute-start | bytes 1585160 | tf_op jit(solution)/shard_map/ppermute | solution.py:417
  44.4 10.5 %collective-permute-start.6 = (bf16[4,528,128]{2,1,0:T(8,128)(2,1)S(1)}, bf16[4,528,128]{2,1,0:T(8,128)(2,1)S(1)}, u32[]{:S(2)}, u32[]{:S(2)}) collective-permute-start(bf16[4,528,128]{2,1,0:T(8,128)(2,1)S(1)} %shard_map.84), channel_id=1, source_target_pairs={{0,4},{4,8},{8,12},{12,14},{14,10},{10,6},{6,2},{2,0},{1,3},{5,1},... | collective-permute-start | bytes 1622024 | tf_op jit(solution)/shard_map/ppermute | solution.py:417
  49.1 11.5 %collective-permute-start.9 = (bf16[2064,128]{1,0:T(8,128)(2,1)S(1)}, bf16[2064,128]{1,0:T(8,128)(2,1)S(1)}, u32[]{:S(2)}, u32[]{:S(2)}) collective-permute-start(bf16[2064,128]{1,0:T(8,128)(2,1)S(1)} %collective-permute-done.7.refs_1_), channel_id=1, source_target_pairs={{0,4},{4,8},{8,12},{12,14},{14,10},{10,6},{6,2},{2,0},{1,3},{5,1},... | collective-permute-start | bytes 1585160 | tf_op jit(solution)/shard_map/ppermute | solution.py:417
  55.9 10.5 %collective-permute-start.8 = (bf16[4,528,128]{2,1,0:T(8,128)(2,1)S(1)}, bf16[4,528,128]{2,1,0:T(8,128)(2,1)S(1)}, u32[]{:S(2)}, u32[]{:S(2)}) collective-permute-start(bf16[4,528,128]{2,1,0:T(8,128)(2,1)S(1)} %shard_map.86), channel_id=1, source_target_pairs={{0,4},{4,8},{8,12},{12,14},{14,10},{10,6},{6,2},{2,0},{1,3},{5,1},... | collective-permute-start | bytes 1622024 | tf_op jit(solution)/shard_map/ppermute | solution.py:417
  60.6 11.5 %collective-permute-start.11 = (bf16[2064,128]{1,0:T(8,128)(2,1)S(1)}, bf16[2064,128]{1,0:T(8,128)(2,1)S(1)}, u32[]{:S(2)}, u32[]{:S(2)}) collective-permute-start(bf16[2064,128]{1,0:T(8,128)(2,1)S(1)} %collective-permute-done.9.refs_1_), channel_id=1, source_target_pairs={{0,4},{4,8},{8,12},{12,14},{14,10},{10,6},{6,2},{2,0},{1,3},{5,1},... | collective-permute-start | bytes 1585160 | tf_op jit(solution)/shard_map/ppermute | solution.py:417
  67.4 10.5 %collective-permute-start.10 = (bf16[4,528,128]{2,1,0:T(8,128)(2,1)S(1)}, bf16[4,528,128]{2,1,0:T(8,128)(2,1)S(1)}, u32[]{:S(2)}, u32[]{:S(2)}) collective-permute-start(bf16[4,528,128]{2,1,0:T(8,128)(2,1)S(1)} %shard_map.88), channel_id=1, source_target_pairs={{0,4},{4,8},{8,12},{12,14},{14,10},{10,6},{6,2},{2,0},{1,3},{5,1},... | collective-permute-start | bytes 1622024 | tf_op jit(solution)/shard_map/ppermute | solution.py:417
  72.0 11.5 %collective-permute-start.13 = (bf16[2064,128]{1,0:T(8,128)(2,1)S(1)}, bf16[2064,128]{1,0:T(8,128)(2,1)S(1)}, u32[]{:S(2)}, u32[]{:S(2)}) collective-permute-start(bf16[2064,128]{1,0:T(8,128)(2,1)S(1)} %collective-permute-done.11.refs_1_), channel_id=1, source_target_pairs={{0,4},{4,8},{8,12},{12,14},{14,10},{10,6},{6,2},{2,0},{1,3},{5,1},... | collective-permute-start | bytes 1585160 | tf_op jit(solution)/shard_map/ppermute | solution.py:417
  78.8 10.5 %collective-permute-start.12 = (bf16[4,528,128]{2,1,0:T(8,128)(2,1)S(1)}, bf16[4,528,128]{2,1,0:T(8,128)(2,1)S(1)}, u32[]{:S(2)}, u32[]{:S(2)}) collective-permute-start(bf16[4,528,128]{2,1,0:T(8,128)(2,1)S(1)} %shard_map.90), channel_id=1, source_target_pairs={{0,4},{4,8},{8,12},{12,14},{14,10},{10,6},{6,2},{2,0},{1,3},{5,1},... | collective-permute-start | bytes 1622024 | tf_op jit(solution)/shard_map/ppermute | solution.py:417
  90.3 10.3 %collective-permute-start.14 = (bf16[4,528,128]{2,1,0:T(8,128)(2,1)S(1)}, bf16[4,528,128]{2,1,0:T(8,128)(2,1)S(1)}, u32[]{:S(2)}, u32[]{:S(2)}) collective-permute-start(bf16[4,528,128]{2,1,0:T(8,128)(2,1)S(1)} %shard_map.92), channel_id=1, source_target_pairs={{0,4},{4,8},{8,12},{12,14},{14,10},{10,6},{6,2},{2,0},{1,3},{5,1},... | collective-permute-start | bytes 1622024 | tf_op jit(solution)/shard_map/ppermute | solution.py:417

commit v12 on v11

--- a/solution.py
+++ b/solution.py
@@ -161,12 +161,16 @@
     refs = list(refs)
     meta, q_ref = refs.pop(0), refs.pop(0)
     own_kv = refs.pop(0) if own else None
-    held, acc_ref, stat_ref = refs.pop(0), refs.pop(0), refs.pop(0)
+    held = refs.pop(0)
+    if keeping and keeping[0]:
+        refs.pop(0)
+    acc_ref, stat_ref = refs.pop(0), refs.pop(0)
     stored = refs.pop(0) if keeping else None
     scores = refs.pop(0)
     late_scores = refs.pop(0) if own else None
     if keeping:
-        keep = pltpu.make_async_copy(held, stored, refs.pop(0))
+        span = pl.ds(*keeping)
+        keep = pltpu.make_async_copy(held.at[span], stored.at[span], refs.pop(0))
         keep.start()
     factor = HEAD_SIZE ** (-0.5) * LOG2E
     keys = cap * page_len
@@ -175,7 +179,12 @@
         return jnp.concatenate([held[meta[0, c], part, :, block_of(h)] for c in range(cap)], 0)
 
     def score(h):
-        q = q_ref[h * rows:(h + 1) * rows, :]
+        if own:
+            groups = rows // suffix
+            q = [q_ref[0, :, block_of(h * groups + g)] for g in range(groups)]
+            q = jnp.concatenate(q, 0)
+        else:
+            q = q_ref[h * rows:(h + 1) * rows, :]
         scores[h % 2] = dot_nt(q, stacked(0, h))
         if own:
             at = iota((rows, suffix), 0) % suffix
@@ -213,36 +222,42 @@
         keep.wait()
 
 
-def attend(sizes, meta, queries, held, own=None, keeping=False, weight=1):
+def attend(sizes, meta, queries, held, own=None, keeping=None, store=None):
     heads, rows, suffix, cap, page_len = sizes
     keys = cap * page_len
     shapes = [
         jax.ShapeDtypeStruct((heads, rows, HEAD_SIZE), jnp.float32),
         jax.ShapeDtypeStruct((heads, STAT_ROWS, HEAD_SIZE), jnp.bfloat16),
     ]
-    specs = [VMEM, VMEM]
+    in_specs, out_specs = [SMEM, VMEM, VMEM], [VMEM, VMEM]
     scratch = [pltpu.VMEM((2, rows, keys), jnp.float32)]
-    more = [held]
+    args, aliases = [meta, queries, held], {}
     if own is not None:
-        more = [own, held]
+        args.insert(2, own)
+        in_specs.append(VMEM)
         scratch.append(pltpu.VMEM((2, rows, suffix), jnp.float32))
     if keeping:
         shapes.append(jax.ShapeDtypeStruct(held.shape, held.dtype))
-        specs.append(HBM)
+        out_specs.append(HBM)
         scratch.append(pltpu.SemaphoreType.DMA)
+    if store is not None:
+        aliases[len(args)] = 2
+        args.append(store)
+        in_specs.append(HBM)
     acc, stat, *pages = pl.pallas_call(
         functools.partial(attend_kernel, sizes, own is not None, keeping),
         out_shape=shapes,
-        in_specs=[SMEM] + [VMEM] * (1 + len(more)),
-        out_specs=specs,
+        in_specs=in_specs,
+        out_specs=out_specs,
         scratch_shapes=scratch,
+        input_output_aliases=aliases,
         compiler_params=pltpu.CompilerParams(vmem_limit_bytes=GRANT),
         cost_estimate=pl.CostEstimate(
-            flops=weight * heads * rows * keys * HEAD_SIZE * 8,
-            bytes_accessed=weight * heads * (rows * 6 + keys * 4) * HEAD_SIZE,
-            transcendentals=weight * heads * rows * keys,
+            flops=heads * rows * keys * HEAD_SIZE * 8,
+            bytes_accessed=heads * (rows * 6 + keys * 4) * HEAD_SIZE,
+            transcendentals=heads * rows * keys,
         ),
-    )(meta, queries, *more)
+    )(*args)
     return (acc, stat), *pages
 
 
@@ -281,9 +296,9 @@
         out_ref[h, rows:, :] = stat_ref[h]
 
 
-def merge_kernel(in_ref, acc_ref, stat_ref, out_ref):
-    heads, rows = acc_ref.shape[:2]
-    for h in range(heads):
+def merge_kernel(first, in_ref, acc_ref, stat_ref, out_ref):
+    heads, rows = out_ref.shape[0], acc_ref.shape[1]
+    for h in range(first, first + heads):
         in_top, in_total = unpack_stats(in_ref[h, rows:, :])
         my_top, my_total = unpack_stats(stat_ref[h])
         tops, totals = [], []
@@ -294,51 +309,59 @@
                     (acc_ref[h, block_of(j), :], my_top[j], my_total[j]),
                 ]
             )
-            out_ref[h, block_of(j), :] = acc.astype(out_ref.dtype)
+            out_ref[h - first, block_of(j), :] = acc.astype(out_ref.dtype)
             tops.append(top)
             totals.append(total)
-        out_ref[h, rows:, :] = pack_stats(tops, totals)
-
-
-def final_kernel(suffix, in_ref, acc_ref, stat_ref, out_ref, done, sems):
-    heads, rows = acc_ref.shape[:2]
+        out_ref[h - first, rows:, :] = pack_stats(tops, totals)
+
+
+def final_kernel(suffix, first, in_ref, acc_ref, stat_ref, *refs):
+    out_ref, done, sems = refs[-3:]
+    heads, rows = in_ref.shape[0], acc_ref.shape[1]
     groups = rows // suffix
     copies = []
     for h in range(heads):
         in_top, in_total = unpack_stats(in_ref[h, rows:, :])
-        my_top, my_total = unpack_stats(stat_ref[h])
+        my_top, my_total = unpack_stats(stat_ref[first + h])
         for j in range(rows // HEAD_SIZE):
             acc, _, total = blend(
                 [
                     (in_ref[h, block_of(j), :].astype(jnp.float32), in_top[j], in_total[j]),
-                    (acc_ref[h, block_of(j), :], my_top[j], my_total[j]),
+                    (acc_ref[first + h, block_of(j), :], my_top[j], my_total[j]),
                 ]
             )
             out = (acc / total).astype(jnp.bfloat16)
             for i in range(HEAD_SIZE // suffix):
                 g = h * groups + j * (HEAD_SIZE // suffix) + i
                 done[0, :, block_of(g)] = out[i * suffix:(i + 1) * suffix]
-        span = pl.ds(h * groups * HEAD_SIZE, groups * HEAD_SIZE)
+        width = groups * HEAD_SIZE
         copies.append(
-            pltpu.make_async_copy(done.at[:, :, span], out_ref.at[:, :, span], sems.at[h])
+            pltpu.make_async_copy(
+                done.at[:, :, pl.ds(h * width, width)],
+                out_ref.at[:, :, pl.ds((first + h) * width, width)],
+                sems.at[h],
+            )
         )
         copies[-1].start()
     for copy in copies:
         copy.wait()
 
 
-def finish(suffix, like, block, part):
+def finish(suffix, first, like, block, part, before=None):
+    heads, rows = block.shape[0], part[0].shape[1]
+    args = [block, *part] + ([] if before is None else [before])
     return pl.pallas_call(
-        functools.partial(final_kernel, suffix),
+        functools.partial(final_kernel, suffix, first),
         out_shape=jax.ShapeDtypeStruct(like.shape, like.dtype),
-        in_specs=[VMEM] * 3,
+        in_specs=[VMEM] * 3 + [HBM] * (len(args) - 3),
         out_specs=HBM,
         scratch_shapes=[
-            pltpu.VMEM(like.shape, like.dtype),
-            pltpu.SemaphoreType.DMA((part[0].shape[0],)),
+            pltpu.VMEM((1, suffix, heads * rows // suffix * HEAD_SIZE), like.dtype),
+            pltpu.SemaphoreType.DMA((heads,)),
         ],
+        input_output_aliases={} if before is None else {3: 0},
         compiler_params=pltpu.CompilerParams(vmem_limit_bytes=GRANT),
-    )(block, *part)
+    )(*args)
 
 
 def call(kernel, shape, *args):
@@ -353,12 +376,8 @@
     )(*args)
 
 
-def prepare_kernel(cap, pages_dev, length_ref, slot_ref, table_ref, q_ref, out_ref):
+def lists_kernel(cap, pages_dev, length_ref, slot_ref, table_ref, out_ref):
     maxp = table_ref.shape[1]
-    suffix = q_ref.shape[1]
-    rows = out_ref.shape[0] - LIST_ROWS
-    for g in range(rows // suffix):
-        out_ref[g * suffix:(g + 1) * suffix, :] = q_ref[0, :, block_of(g)]
     table = table_ref[...]
     owner = lax.div(table, pages_dev)
     local = (table - owner * pages_dev).astype(jnp.float32)
@@ -380,18 +399,24 @@
     )
     slot = slot_ref[0].astype(jnp.float32)
     lists = jnp.where(iota(lists.shape, 1) == cap + 1, slot, lists)
-    out_ref[rows:, :] = lists.astype(jnp.bfloat16)
-
-
-def prepare(cap, pages_dev, queries, page_table, prefix_pages, new_slots):
-    rows = queries.size // HEAD_SIZE
+    out_ref[...] = lists.astype(jnp.bfloat16)
+
+
+def list_pages(cap, pages_dev, page_table, prefix_pages, new_slots):
     return pl.pallas_call(
-        functools.partial(prepare_kernel, cap, pages_dev),
-        out_shape=jax.ShapeDtypeStruct((rows + LIST_ROWS, HEAD_SIZE), queries.dtype),
-        in_specs=[SMEM, SMEM, VMEM, VMEM],
+        functools.partial(lists_kernel, cap, pages_dev),
+        out_shape=jax.ShapeDtypeStruct((LIST_ROWS, HEAD_SIZE), jnp.bfloat16),
+        in_specs=[SMEM, SMEM, VMEM],
         out_specs=VMEM,
         compiler_params=pltpu.CompilerParams(vmem_limit_bytes=GRANT),
-    )(prefix_pages, new_slots, page_table, queries)
+    )(prefix_pages, new_slots, page_table)
+
+
+def join_kernel(q_ref, lists_ref, out_ref):
+    suffix, columns = q_ref.shape[1:]
+    for g in range(columns // HEAD_SIZE):
+        out_ref[g * suffix:(g + 1) * suffix, :] = q_ref[0, :, block_of(g)]
+    out_ref[columns // HEAD_SIZE * suffix:, :] = lists_ref[...]
 
 
 def queries_travel(queries, suffix_key_value, kv_pages, page_table, prefix_pages, new_slots):
@@ -416,37 +441,56 @@
     def onward(x):
         return lax.ppermute(x, ("store", "tensor"), route)
 
-    def listed(x):
-        row = lax.dynamic_slice(x, (heads * rows + me, 0), (1, HEAD_SIZE))
+    def listed(x, below):
+        row = lax.dynamic_slice(x, (below + me, 0), (1, HEAD_SIZE))
         return row.astype(jnp.int32)
 
     def after(values, token):
         return lax.optimization_barrier((values, token))[0]
 
-    mine = prepare(cap, pages_dev, queries, page_table, prefix_pages, new_slots)
-    moving = onward(mine)
+    first = onward(queries)
+    mine = list_pages(cap, pages_dev, page_table, prefix_pages, new_slots)
+    first_lists = onward(mine)
     arrived = shifted(after(suffix_key_value, mine), "store", half)
-
-    own, store = attend(
-        sizes, listed(mine), mine, kv_pages, suffix_key_value[0], True, weight=8
-    )
-    token = own
-    partial = None
+    moving = call(
+        join_kernel,
+        jax.ShapeDtypeStruct((heads * rows + LIST_ROWS, HEAD_SIZE), queries.dtype),
+        first,
+        first_lists,
+    )
+
+    token = []
     lists = {}
     for step in range(1, stores):
         came = after(moving, token)
         if step < stores - 1:
             moving = onward(came)
-        lists[step] = listed(came)
-        part, = attend(sizes, lists[step], came, kv_pages)
+        lists[step] = listed(came, heads * rows)
+        if step == 2:
+            part, store = attend(
+                sizes, lists[step], came, kv_pages, keeping=(0, pages_dev // 2)
+            )
+        elif step == 3:
+            rest = (pages_dev // 2, pages_dev - pages_dev // 2)
+            part, store = attend(sizes, lists[step], came, kv_pages, None, rest, store)
+        else:
+            part, = attend(sizes, lists[step], came, kv_pages)
         if step == 1:
             block = packed(after(part, arrived))
+        elif step < stores - 1:
+            block = merged(after(partial, part), part, 0, heads)
         else:
-            block = merged(after(partial, part), part)
+            came = after(partial, part)
+            ends = [merged(came, part, first, heads // 2) for first in (0, heads // 2)]
+            token = ends
+            ends = [onward(x) for x in ends]
+            break
         partial = onward(block)
         token = block
-    attended = finish(suffix, queries, partial, own)
-
+
+    own, = attend(
+        sizes, listed(mine, 0), after(queries, token), kv_pages, suffix_key_value[0]
+    )
     near = ((me >= half) == (me % 2 == 0)) == (lax.axis_index("tensor") % 2 == 0)
     quarter = stores // 4
     store = place_page(
@@ -455,22 +499,24 @@
         lists[quarter],
         lists[stores - quarter],
         arrived,
-        after(store, token),
-    )
+        after(store, own),
+    )
+    attended = finish(suffix, 0, queries, after(ends[0], store), own)
+    attended = finish(suffix, heads // 2, queries, ends[1], own, attended)
     return (attended, store)
 
 
-def wire_of(part):
-    heads, rows, columns = part[0].shape
+def wire_of(part, heads):
+    rows, columns = part[0].shape[1:]
     return jax.ShapeDtypeStruct((heads, rows + STAT_ROWS, columns), jnp.bfloat16)
 
 
 def packed(part):
-    return call(pack_kernel, wire_of(part), *part)
-
-
-def merged(block, part):
-    return call(merge_kernel, wire_of(part), block, *part)
+    return call(pack_kernel, wire_of(part, part[0].shape[0]), *part)
+
+
+def merged(block, part, first, heads):
+    return call(functools.partial(merge_kernel, first), wire_of(part, heads), block, *part)
 
 
 def on_device(queries, suffix_key_value, kv_pages, page_table, prefix_pages, new_slots):

time: 103 us -> 102 us (level)
  waiting for transfers between devices: 28.1 us -> 22.4 us
  starting transfers between devices: 38.8 us -> 42 us
  Pallas kernels: 28.3 us -> 29.8 us
    ppermute x14 -> x16, waiting for transfers between devices: 28.1 us -> 22.4 us  [onward(): return lax.ppermute(x, ('store', 'tensor'), route)]
    ppermute x14 -> x16, starting transfers between devices: 36.2 us -> 39.5 us  [onward(): return lax.ppermute(x, ('store', 'tensor'), route)]
    pallas_call x2 -> x3, Pallas kernels: 1.9 us -> 2.83 us  [the longest x2 2.54 us: finish(): pl.pallas_call(functools.partial(final_kernel, suffix, first), out_shape=...]
    pallas_call x7 -> x9, Pallas kernels: 5.93 us -> 6.3 us  [call(): pl.pallas_call(kernel, out_shape=shape, in_specs=[VMEM] * len(args), out_...]
    unnamed x10 -> x12, local copies, waits for them, and re-layouts: 4.78 us -> 5.03 us
  transfers between devices with their start and end apart: 15 -> 17, of which waited for: 13 -> 12; matrix products, arithmetic and copies ran while one was open for 0% -> 0% of each run, Pallas kernels for 25% -> 27%
where the time goes in v12:
time: 102 us
  starting transfers between devices  42 us (41%)
  Pallas kernels  29.8 us (29%)
  waiting for transfers between devices  22.4 us (22%)
  local copies, waits for them, and re-layouts  5.03 us (5%)
  between operations  2.3 us (2%)
    ppermute x16, starting transfers between devices, onward(): return lax.ppermute(x, ('store', 'tensor'), route)  39.5 us
    ppermute x16, waiting for transfers between devices, onward(): return lax.ppermute(x, ('store', 'tensor'), route)  22.4 us
    pallas_call x8, Pallas kernels, attend(): pl.pallas_call(functools.partial(attend_kernel, sizes, own is not None, k...  19.5 us
    pallas_call x9, Pallas kernels, call(): pl.pallas_call(kernel, out_shape=shape, in_specs=[VMEM] * len(args), out_...  6.3 us
    unnamed x12, local copies, waits for them, and re-layouts  5.03 us
    pallas_call x2, Pallas kernels, finish(): pl.pallas_call(functools.partial(final_kernel, suffix, first), out_shape=...  2.54 us
    ppermute x1, starting transfers between devices, shifted(): return lax.ppermute(block, axis, route)  2.53 us
  transfers between devices with their start and end apart: 17, of which 12 were waited for; matrix products, arithmetic and copies ran while one was open for 0% of the time, Pallas kernels for 27%

profile of v12, /device:TPU:0, one launch (start us, length us, event | category | flops | bytes accessed | tf_op | source)
XLA Modules:
  0.0 101.6 jit_solution(6891629993270711800)
XLA Ops:
  0.6 3.1 %collective-permute-start = (bf16[1,64,4096]{2,1,0:T(8,128)(2,1)}, bf16[1,64,4096]{2,1,0:T(8,128)(2,1)S(1)}, u32[]{:S(2)}, u32[]{:S(2)}) collective-permute-start(bf16[1,64,4096]{2,1,0:T(8,128)(2,1)} %refs_1_), channel_id=1, source_target_pairs={{0,4},{4,8},{8,12},{12,14},{14,10},{10,6},{6,2},{2,0},{1,3},{5,1},... | collective-permute-start | bytes 1572872 | tf_op jit(solution)/shard_map/ppermute | solution.py:442
  5.0 0.0 copy-start.5
  5.0 0.6 copy-done.5
  5.7 0.3 shard_map.77
  5.9 1.6 %collective-permute-start.1 = (bf16[16,128]{1,0:T(8,128)(2,1)S(1)}, bf16[16,128]{1,0:T(8,128)(2,1)S(1)}, u32[]{:S(2)}, u32[]{:S(2)}) collective-permute-start(bf16[16,128]{1,0:T(8,128)(2,1)S(1)} %shard_map.77), channel_id=1, source_target_pairs={{0,4},{4,8},{8,12},{12,14},{14,10},{10,6},{6,2},{2,0},{1,3},{5,1},... | collective-permute-start | bytes 12296 | tf_op jit(solution)/shard_map/ppermute | solution.py:442
  7.5 2.5 %collective-permute-start.2 = (bf16[1,2,64,512]{3,2,1,0:T(8,128)(2,1)}, bf16[1,2,64,512]{3,2,1,0:T(8,128)(2,1)S(1)}, u32[]{:S(2)}, u32[]{:S(2)}) collective-permute-start(bf16[1,2,64,512]{3,2,1,0:T(8,128)(2,1)} %param.7), channel_id=1, source_target_pairs={{8,0},{10,2},{12,4},{14,6},{0,8},{2,10},{4,12},{6,14},{9,1},{11,3}... | collective-permute-start | bytes 393224 | tf_op jit(solution)/shard_map/ppermute | solution.py:26
  10.1 2.1 %collective-permute-done.1.lists_ref = bf16[16,128]{1,0:T(8,128)(2,1)S(1)} collective-permute-done((bf16[16,128]{1,0:T(8,128)(2,1)S(1)}, bf16[16,128]{1,0:T(8,128)(2,1)S(1)}, u32[]{:S(2)}, u32[]{:S(2)}) %collective-permute-start.1) | collective-permute-done | bytes 4128 | tf_op jit(solution)/shard_map/ppermute | solution.py:442
  12.1 0.0 collective-permute-done.q_ref
  12.1 0.1 shard_map.78.refs_1_
  12.2 4.4 %collective-permute-start.4 = (bf16[2064,128]{1,0:T(8,128)(2,1)S(1)}, bf16[2064,128]{1,0:T(8,128)(2,1)S(1)}, u32[]{:S(2)}, u32[]{:S(2)}) collective-permute-start(bf16[2064,128]{1,0:T(8,128)(2,1)S(1)} %shard_map.78.refs_1_), channel_id=1, source_target_pairs={{0,4},{4,8},{8,12},{12,14},{14,10},{10,6},{6,2},{2,0},{1,3},{5,1},... | collective-permute-start | bytes 1585160 | tf_op jit(solution)/shard_map/ppermute | solution.py:442
  16.7 2.2 %copy-done = bf16[32,2,64,512]{3,2,1,0:T(8,128)(2,1)S(1)} copy-done((bf16[32,2,64,512]{3,2,1,0:T(8,128)(2,1)S(1)}, bf16[32,2,64,512]{3,2,1,0:T(8,128)(2,1)}, u32[]{:S(2)}) %copy-start) | copy-done | bytes 4194328
  18.9 2.2 %shard_map.79 = (f32[4,512,128]{2,1,0:T(8,128)S(1)}, bf16[4,16,128]{2,1,0:T(8,128)(2,1)S(1)}) custom-call(s32[1,128]{1,0:T(1,128)S(1)} %fusion.refs_0_, bf16[2064,128]{1,0:T(8,128)(2,1)S(1)} %shard_map.78.refs_1_, bf16[32,2,64,512]{3,2,1,0:T(8,128)(2,1)S(1)} %copy-done), custom_call_target="tpu_custom_call" | custom-call | flops 1073741824 | bytes 2621440 | tf_op jit(solution)/shard_map/pallas_call | solution.py:247
  21.1 0.0 collective-permute-done.2.page_ref
  21.1 0.1 shard_map.80
  21.2 2.5 %collective-permute-start.3 = (bf16[4,528,128]{2,1,0:T(8,128)(2,1)S(1)}, bf16[4,528,128]{2,1,0:T(8,128)(2,1)S(1)}, u32[]{:S(2)}, u32[]{:S(2)}) collective-permute-start(bf16[4,528,128]{2,1,0:T(8,128)(2,1)S(1)} %shard_map.80), channel_id=1, source_target_pairs={{0,4},{4,8},{8,12},{12,14},{14,10},{10,6},{6,2},{2,0},{1,3},{5,1},... | collective-permute-start | bytes 1622024 | tf_op jit(solution)/shard_map/ppermute | solution.py:442
  23.6 0.0 collective-permute-done.4.refs_1_
  23.6 2.2 %collective-permute-start.6 = (bf16[2064,128]{1,0:T(8,128)(2,1)S(1)}, bf16[2064,128]{1,0:T(8,128)(2,1)S(1)}, u32[]{:S(2)}, u32[]{:S(2)}) collective-permute-start(bf16[2064,128]{1,0:T(8,128)(2,1)S(1)} %collective-permute-done.4.refs_1_), channel_id=1, source_target_pairs={{0,4},{4,8},{8,12},{12,14},{14,10},{10,6},{6,2},{2,0},{1,3},{5,1},... | collective-permute-start | bytes 1585160 | tf_op jit(solution)/shard_map/ppermute | solution.py:442
  25.9 0.0 copy-done.1
  25.9 2.8 %shard_map.81 = (f32[4,512,128]{2,1,0:T(8,128)S(1)}, bf16[4,16,128]{2,1,0:T(8,128)(2,1)S(1)}, bf16[32,2,64,512]{3,2,1,0:T(8,128)(2,1)}) custom-call(s32[1,128]{1,0:T(1,128)S(1)} %fusion.1.refs_0_.below_ref, bf16[2064,128]{1,0:T(8,128)(2,1)S(1)} %collective-permute-done.4.refs_1_, bf16[32,2,64,512]{3,2,1,0:T(8,128)(2,1)S(1)} %copy-done.1), custom_call_target="tpu_custom_call" | custom-call | flops 1073741824 | bytes 2621440 | tf_op jit(solution)/shard_map/pallas_call | solution.py:247
  28.7 1.9 %collective-permute-done.3.in_ref = bf16[4,528,128]{2,1,0:T(8,128)(2,1)S(1)} collective-permute-done((bf16[4,528,128]{2,1,0:T(8,128)(2,1)S(1)}, bf16[4,528,128]{2,1,0:T(8,128)(2,1)S(1)}, u32[]{:S(2)}, u32[]{:S(2)}) %collective-permute-start.3) | collective-permute-done | bytes 540704 | tf_op jit(solution)/shard_map/ppermute | solution.py:442
  30.6 1.0 shard_map.82
  31.6 2.5 %collective-permute-start.5 = (bf16[4,528,128]{2,1,0:T(8,128)(2,1)S(1)}, bf16[4,528,128]{2,1,0:T(8,128)(2,1)S(1)}, u32[]{:S(2)}, u32[]{:S(2)}) collective-permute-start(bf16[4,528,128]{2,1,0:T(8,128)(2,1)S(1)} %shard_map.82), channel_id=1, source_target_pairs={{0,4},{4,8},{8,12},{12,14},{14,10},{10,6},{6,2},{2,0},{1,3},{5,1},... | collective-permute-start | bytes 1622024 | tf_op jit(solution)/shard_map/ppermute | solution.py:442
  34.0 2.2 %collective-permute-done.6.refs_1_ = bf16[2064,128]{1,0:T(8,128)(2,1)S(1)} collective-permute-done((bf16[2064,128]{1,0:T(8,128)(2,1)S(1)}, bf16[2064,128]{1,0:T(8,128)(2,1)S(1)}, u32[]{:S(2)}, u32[]{:S(2)}) %collective-permute-start.6) | collective-permute-done | bytes 528416 | tf_op jit(solution)/shard_map/ppermute | solution.py:442
  36.2 2.4 %collective-permute-start.8 = (bf16[2064,128]{1,0:T(8,128)(2,1)S(1)}, bf16[2064,128]{1,0:T(8,128)(2,1)S(1)}, u32[]{:S(2)}, u32[]{:S(2)}) collective-permute-start(bf16[2064,128]{1,0:T(8,128)(2,1)S(1)} %collective-permute-done.6.refs_1_), channel_id=1, source_target_pairs={{0,4},{4,8},{8,12},{12,14},{14,10},{10,6},{6,2},{2,0},{1,3},{5,1},... | collective-permute-start | bytes 1585160 | tf_op jit(solution)/shard_map/ppermute | solution.py:442
  38.7 2.9 %shard_map.83 = (f32[4,512,128]{2,1,0:T(8,128)S(1)}, bf16[4,16,128]{2,1,0:T(8,128)(2,1)S(1)}, bf16[32,2,64,512]{3,2,1,0:T(8,128)(2,1)}) custom-call(s32[1,128]{1,0:T(1,128)S(1)} %fusion.2.refs_0_, bf16[2064,128]{1,0:T(8,128)(2,1)S(1)} %collective-permute-done.6.refs_1_, bf16[32,2,64,512]{3,2,1,0:T(8,128)(2,1)S(1)} %copy-done.1, ...), custom_call_target="tpu_custom_call", output_to_operand_aliasing={{2}: (3, {})} | custom-call | flops 1073741824 | bytes 2621440 | tf_op jit(solution)/shard_map/pallas_call | solution.py:247
  41.6 0.4 collective-permute-done.5.in_ref
  42.0 1.0 shard_map.84
  43.0 2.5 %collective-permute-start.7 = (bf16[4,528,128]{2,1,0:T(8,128)(2,1)S(1)}, bf16[4,528,128]{2,1,0:T(8,128)(2,1)S(1)}, u32[]{:S(2)}, u32[]{:S(2)}) collective-permute-start(bf16[4,528,128]{2,1,0:T(8,128)(2,1)S(1)} %shard_map.84), channel_id=1, source_target_pairs={{0,4},{4,8},{8,12},{12,14},{14,10},{10,6},{6,2},{2,0},{1,3},{5,1},... | collective-permute-start | bytes 1622024 | tf_op jit(solution)/shard_map/ppermute | solution.py:442
  45.5 2.2 %collective-permute-done.8.refs_1_ = bf16[2064,128]{1,0:T(8,128)(2,1)S(1)} collective-permute-done((bf16[2064,128]{1,0:T(8,128)(2,1)S(1)}, bf16[2064,128]{1,0:T(8,128)(2,1)S(1)}, u32[]{:S(2)}, u32[]{:S(2)}) %collective-permute-start.8) | collective-permute-done | bytes 528416 | tf_op jit(solution)/shard_map/ppermute | solution.py:442
  47.7 2.4 %collective-permute-start.10 = (bf16[2064,128]{1,0:T(8,128)(2,1)S(1)}, bf16[2064,128]{1,0:T(8,128)(2,1)S(1)}, u32[]{:S(2)}, u32[]{:S(2)}) collective-permute-start(bf16[2064,128]{1,0:T(8,128)(2,1)S(1)} %collective-permute-done.8.refs_1_), channel_id=1, source_target_pairs={{0,4},{4,8},{8,12},{12,14},{14,10},{10,6},{6,2},{2,0},{1,3},{5,1},... | collective-permute-start | bytes 1585160 | tf_op jit(solution)/shard_map/ppermute | solution.py:442
  50.1 2.2 %shard_map.85 = (f32[4,512,128]{2,1,0:T(8,128)S(1)}, bf16[4,16,128]{2,1,0:T(8,128)(2,1)S(1)}) custom-call(s32[1,128]{1,0:T(1,128)S(1)} %fusion.3.refs_0_, bf16[2064,128]{1,0:T(8,128)(2,1)S(1)} %collective-permute-done.8.refs_1_, bf16[32,2,64,512]{3,2,1,0:T(8,128)(2,1)S(1)} %copy-done.1), custom_call_target="tpu_custom_call" | custom-call | flops 1073741824 | bytes 2621440 | tf_op jit(solution)/shard_map/pallas_call | solution.py:247
  52.3 1.1 %collective-permute-done.7.in_ref = bf16[4,528,128]{2,1,0:T(8,128)(2,1)S(1)} collective-permute-done((bf16[4,528,128]{2,1,0:T(8,128)(2,1)S(1)}, bf16[4,528,128]{2,1,0:T(8,128)(2,1)S(1)}, u32[]{:S(2)}, u32[]{:S(2)}) %collective-permute-start.7) | collective-permute-done | bytes 540704 | tf_op jit(solution)/shard_map/ppermute | solution.py:442
  53.5 1.0 shard_map.86
  54.5 2.5 %collective-permute-start.9 = (bf16[4,528,128]{2,1,0:T(8,128)(2,1)S(1)}, bf16[4,528,128]{2,1,0:T(8,128)(2,1)S(1)}, u32[]{:S(2)}, u32[]{:S(2)}) collective-permute-start(bf16[4,528,128]{2,1,0:T(8,128)(2,1)S(1)} %shard_map.86), channel_id=1, source_target_pairs={{0,4},{4,8},{8,12},{12,14},{14,10},{10,6},{6,2},{2,0},{1,3},{5,1},... | collective-permute-start | bytes 1622024 | tf_op jit(solution)/shard_map/ppermute | solution.py:442
  56.9 2.2 %collective-permute-done.10.refs_1_ = bf16[2064,128]{1,0:T(8,128)(2,1)S(1)} collective-permute-done((bf16[2064,128]{1,0:T(8,128)(2,1)S(1)}, bf16[2064,128]{1,0:T(8,128)(2,1)S(1)}, u32[]{:S(2)}, u32[]{:S(2)}) %collective-permute-start.10) | collective-permute-done | bytes 528416 | tf_op jit(solution)/shard_map/ppermute | solution.py:442
  59.2 2.4 %collective-permute-start.12 = (bf16[2064,128]{1,0:T(8,128)(2,1)S(1)}, bf16[2064,128]{1,0:T(8,128)(2,1)S(1)}, u32[]{:S(2)}, u32[]{:S(2)}) collective-permute-start(bf16[2064,128]{1,0:T(8,128)(2,1)S(1)} %collective-permute-done.10.refs_1_), channel_id=1, source_target_pairs={{0,4},{4,8},{8,12},{12,14},{14,10},{10,6},{6,2},{2,0},{1,3},{5,1},... | collective-permute-start | bytes 1585160 | tf_op jit(solution)/shard_map/ppermute | solution.py:442
  61.6 2.2 %shard_map.87 = (f32[4,512,128]{2,1,0:T(8,128)S(1)}, bf16[4,16,128]{2,1,0:T(8,128)(2,1)S(1)}) custom-call(s32[1,128]{1,0:T(1,128)S(1)} %fusion.4.refs_0_, bf16[2064,128]{1,0:T(8,128)(2,1)S(1)} %collective-permute-done.10.refs_1_, bf16[32,2,64,512]{3,2,1,0:T(8,128)(2,1)S(1)} %copy-done.1), custom_call_target="tpu_custom_call" | custom-call | flops 1073741824 | bytes 2621440 | tf_op jit(solution)/shard_map/pallas_call | solution.py:247
  63.8 1.1 %collective-permute-done.9.in_ref = bf16[4,528,128]{2,1,0:T(8,128)(2,1)S(1)} collective-permute-done((bf16[4,528,128]{2,1,0:T(8,128)(2,1)S(1)}, bf16[4,528,128]{2,1,0:T(8,128)(2,1)S(1)}, u32[]{:S(2)}, u32[]{:S(2)}) %collective-permute-start.9) | collective-permute-done | bytes 540704 | tf_op jit(solution)/shard_map/ppermute | solution.py:442
  64.9 1.0 shard_map.88
  65.9 2.5 %collective-permute-start.11 = (bf16[4,528,128]{2,1,0:T(8,128)(2,1)S(1)}, bf16[4,528,128]{2,1,0:T(8,128)(2,1)S(1)}, u32[]{:S(2)}, u32[]{:S(2)}) collective-permute-start(bf16[4,528,128]{2,1,0:T(8,128)(2,1)S(1)} %shard_map.88), channel_id=1, source_target_pairs={{0,4},{4,8},{8,12},{12,14},{14,10},{10,6},{6,2},{2,0},{1,3},{5,1},... | collective-permute-start | bytes 1622024 | tf_op jit(solution)/shard_map/ppermute | solution.py:442
  68.4 2.2 %collective-permute-done.12.refs_1_ = bf16[2064,128]{1,0:T(8,128)(2,1)S(1)} collective-permute-done((bf16[2064,128]{1,0:T(8,128)(2,1)S(1)}, bf16[2064,128]{1,0:T(8,128)(2,1)S(1)}, u32[]{:S(2)}, u32[]{:S(2)}) %collective-permute-start.12) | collective-permute-done | bytes 528416 | tf_op jit(solution)/shard_map/ppermute | solution.py:442
  70.6 2.4 %collective-permute-start.14 = (bf16[2064,128]{1,0:T(8,128)(2,1)S(1)}, bf16[2064,128]{1,0:T(8,128)(2,1)S(1)}, u32[]{:S(2)}, u32[]{:S(2)}) collective-permute-start(bf16[2064,128]{1,0:T(8,128)(2,1)S(1)} %collective-permute-done.12.refs_1_), channel_id=1, source_target_pairs={{0,4},{4,8},{8,12},{12,14},{14,10},{10,6},{6,2},{2,0},{1,3},{5,1},... | collective-permute-start | bytes 1585160 | tf_op jit(solution)/shard_map/ppermute | solution.py:442
  73.0 2.2 %shard_map.89 = (f32[4,512,128]{2,1,0:T(8,128)S(1)}, bf16[4,16,128]{2,1,0:T(8,128)(2,1)S(1)}) custom-call(s32[1,128]{1,0:T(1,128)S(1)} %fusion.5.refs_0_.above_ref, bf16[2064,128]{1,0:T(8,128)(2,1)S(1)} %collective-permute-done.12.refs_1_, bf16[32,2,64,512]{3,2,1,0:T(8,128)(2,1)S(1)} %copy-done.1), custom_call_target="tpu_custom_call" | custom-call | flops 1073741824 | bytes 2621440 | tf_op jit(solution)/shard_map/pallas_call | solution.py:247
  75.3 1.1 %collective-permute-done.11.in_ref = bf16[4,528,128]{2,1,0:T(8,128)(2,1)S(1)} collective-permute-done((bf16[4,528,128]{2,1,0:T(8,128)(2,1)S(1)}, bf16[4,528,128]{2,1,0:T(8,128)(2,1)S(1)}, u32[]{:S(2)}, u32[]{:S(2)}) %collective-permute-start.11) | collective-permute-done | bytes 540704 | tf_op jit(solution)/shard_map/ppermute | solution.py:442
  76.4 1.0 shard_map.90
  77.4 2.5 %collective-permute-start.13 = (bf16[4,528,128]{2,1,0:T(8,128)(2,1)S(1)}, bf16[4,528,128]{2,1,0:T(8,128)(2,1)S(1)}, u32[]{:S(2)}, u32[]{:S(2)}) collective-permute-start(bf16[4,528,128]{2,1,0:T(8,128)(2,1)S(1)} %shard_map.90), channel_id=1, source_target_pairs={{0,4},{4,8},{8,12},{12,14},{14,10},{10,6},{6,2},{2,0},{1,3},{5,1},... | collective-permute-start | bytes 1622024 | tf_op jit(solution)/shard_map/ppermute | solution.py:442
  79.9 2.2 %collective-permute-done.14.refs_1_ = bf16[2064,128]{1,0:T(8,128)(2,1)S(1)} collective-permute-done((bf16[2064,128]{1,0:T(8,128)(2,1)S(1)}, bf16[2064,128]{1,0:T(8,128)(2,1)S(1)}, u32[]{:S(2)}, u32[]{:S(2)}) %collective-permute-start.14) | collective-permute-done | bytes 528416 | tf_op jit(solution)/shard_map/ppermute | solution.py:442
  82.1 0.0 copy-start.4
  82.1 2.2 %shard_map.91 = (f32[4,512,128]{2,1,0:T(8,128)S(1)}, bf16[4,16,128]{2,1,0:T(8,128)(2,1)S(1)}) custom-call(s32[1,128]{1,0:T(1,128)S(1)} %fusion.6.refs_0_, bf16[2064,128]{1,0:T(8,128)(2,1)S(1)} %collective-permute-done.14.refs_1_, bf16[32,2,64,512]{3,2,1,0:T(8,128)(2,1)S(1)} %copy-done.1), custom_call_target="tpu_custom_call" | custom-call | flops 1073741824 | bytes 2621440 | tf_op jit(solution)/shard_map/pallas_call | solution.py:247
  84.3 3.5 %collective-permute-done.13.in_ref = bf16[4,528,128]{2,1,0:T(8,128)(2,1)S(1)} collective-permute-done((bf16[4,528,128]{2,1,0:T(8,128)(2,1)S(1)}, bf16[4,528,128]{2,1,0:T(8,128)(2,1)S(1)}, u32[]{:S(2)}, u32[]{:S(2)}) %collective-permute-start.13) | collective-permute-done | bytes 540704 | tf_op jit(solution)/shard_map/ppermute | solution.py:442
  87.9 0.6 shard_map.93
  88.5 2.5 %collective-permute-start.16 = (bf16[2,528,128]{2,1,0:T(8,128)(2,1)S(1)}, bf16[2,528,128]{2,1,0:T(8,128)(2,1)S(1)}, u32[]{:S(2)}, u32[]{:S(2)}) collective-permute-start(bf16[2,528,128]{2,1,0:T(8,128)(2,1)S(1)} %shard_map.93), channel_id=1, source_target_pairs={{0,4},{4,8},{8,12},{12,14},{14,10},{10,6},{6,2},{2,0},{1,3},{5,1},... | collective-permute-start | bytes 811016 | tf_op jit(solution)/shard_map/ppermute | solution.py:442
  91.0 0.6 shard_map.92
  91.6 1.1 %collective-permute-start.15 = (bf16[2,528,128]{2,1,0:T(8,128)(2,1)S(1)}, bf16[2,528,128]{2,1,0:T(8,128)(2,1)S(1)}, u32[]{:S(2)}, u32[]{:S(2)}) collective-permute-start(bf16[2,528,128]{2,1,0:T(8,128)(2,1)S(1)} %shard_map.92), channel_id=1, source_target_pairs={{0,4},{4,8},{8,12},{12,14},{14,10},{10,6},{6,2},{2,0},{1,3},{5,1},... | collective-permute-start | bytes 811016 | tf_op jit(solution)/shard_map/ppermute | solution.py:442
  92.8 0.0 copy-done.3
  92.8 0.0 copy-done.4
  92.8 0.0 copy-start.2
  92.8 2.2 %copy-done.2 = bf16[32,2,64,512]{3,2,1,0:T(8,128)(2,1)S(1)} copy-done((bf16[32,2,64,512]{3,2,1,0:T(8,128)(2,1)S(1)}, bf16[32,2,64,512]{3,2,1,0:T(8,128)(2,1)}, u32[]{:S(2)}) %copy-start.2) | copy-done | bytes 4194328
  95.0 2.7 %shard_map.94 = (f32[4,512,128]{2,1,0:T(8,128)S(1)}, bf16[4,16,128]{2,1,0:T(8,128)(2,1)S(1)}) custom-call(s32[1,128]{1,0:T(1,128)S(1)} %fusion.7.refs_0_, bf16[1,64,4096]{2,1,0:T(8,128)(2,1)S(1)} %copy-done.3, bf16[2,64,512]{2,1,0:T(8,128)(2,1)S(1)} %bitcast.2, bf16[32,2,64,512]{3,2,1,0:T(8,128)(2,1)S(1)} %copy-done.2), custom_call_target="tpu_custom_call" | custom-call | flops 1073741824 | bytes 2621440 | tf_op jit(solution)/shard_map/pallas_call | solution.py:247
  97.7 1.2 %shard_map.95 = bf16[32,2,64,512]{3,2,1,0:T(8,128)(2,1)} custom-call(s32[1]{0:T(128)} %bitcast.1.near_ref, s32[1,128]{1,0:T(1,128)S(1)} %fusion.1.refs_0_.below_ref, s32[1,128]{1,0:T(1,128)S(1)} %fusion.5.refs_0_.above_ref, bf16[1,2,64,512]{3,2,1,0:T(8,128)(2,1)S(1)} %collective-permute-done.2.page_ref, ...), custom_call_target="tpu_custom_call", output_to_operand_aliasing={{}: (4, {})} | custom-call | flops 1 | bytes 1 | tf_op jit(solution)/shard_map/pallas_call | solution.py:272
  98.9 0.0 collective-permute-done.16.in_ref
  98.9 1.3 %shard_map.96.refs_0_ = bf16[1,64,4096]{2,1,0:T(8,128)(2,1)} custom-call(bf16[2,528,128]{2,1,0:T(8,128)(2,1)S(1)} %collective-permute-done.16.in_ref, f32[4,512,128]{2,1,0:T(8,128)S(1)} %get-tuple-element.69.acc_ref, bf16[4,16,128]{2,1,0:T(8,128)(2,1)S(1)} %get-tuple-element.70.stat_ref), custom_call_target="tpu_custom_call" | custom-call | tf_op jit(solution)/shard_map/pallas_call | solution.py:353
  100.2 0.0 collective-permute-done.15.in_ref
  100.2 1.3 %shard_map.97 = bf16[1,64,4096]{2,1,0:T(8,128)(2,1)} custom-call(bf16[2,528,128]{2,1,0:T(8,128)(2,1)S(1)} %collective-permute-done.15.in_ref, f32[4,512,128]{2,1,0:T(8,128)S(1)} %get-tuple-element.69.acc_ref, bf16[4,16,128]{2,1,0:T(8,128)(2,1)S(1)} %get-tuple-element.70.stat_ref, bf16[1,64,4096]{2,1,0:T(8,128)(2,1)} %shard_map.96.refs_0_), custom_call_target="tpu_custom_call", output_to_operand_aliasing={{}: (3, {})} | custom-call | tf_op jit(solution)/shard_map/pallas_call | solution.py:353
  (11 shorter events, 0.1 us)
Async XLA Ops:
  0.6 11.5 %collective-permute-start = (bf16[1,64,4096]{2,1,0:T(8,128)(2,1)}, bf16[1,64,4096]{2,1,0:T(8,128)(2,1)S(1)}, u32[]{:S(2)}, u32[]{:S(2)}) collective-permute-start(bf16[1,64,4096]{2,1,0:T(8,128)(2,1)} %refs_1_), channel_id=1, source_target_pairs={{0,4},{4,8},{8,12},{12,14},{14,10},{10,6},{6,2},{2,0},{1,3},{5,1},... | collective-permute-start | bytes 1572872 | tf_op jit(solution)/shard_map/ppermute | solution.py:442
  5.0 0.7 copy-start.5
  5.9 6.2 %collective-permute-start.1 = (bf16[16,128]{1,0:T(8,128)(2,1)S(1)}, bf16[16,128]{1,0:T(8,128)(2,1)S(1)}, u32[]{:S(2)}, u32[]{:S(2)}) collective-permute-start(bf16[16,128]{1,0:T(8,128)(2,1)S(1)} %shard_map.77), channel_id=1, source_target_pairs={{0,4},{4,8},{8,12},{12,14},{14,10},{10,6},{6,2},{2,0},{1,3},{5,1},... | collective-permute-start | bytes 12296 | tf_op jit(solution)/shard_map/ppermute | solution.py:442
  7.5 13.6 %collective-permute-start.2 = (bf16[1,2,64,512]{3,2,1,0:T(8,128)(2,1)}, bf16[1,2,64,512]{3,2,1,0:T(8,128)(2,1)S(1)}, u32[]{:S(2)}, u32[]{:S(2)}) collective-permute-start(bf16[1,2,64,512]{3,2,1,0:T(8,128)(2,1)} %param.7), channel_id=1, source_target_pairs={{8,0},{10,2},{12,4},{14,6},{0,8},{2,10},{4,12},{6,14},{9,1},{11,3}... | collective-permute-start | bytes 393224 | tf_op jit(solution)/shard_map/ppermute | solution.py:26
  12.2 11.4 %collective-permute-start.4 = (bf16[2064,128]{1,0:T(8,128)(2,1)S(1)}, bf16[2064,128]{1,0:T(8,128)(2,1)S(1)}, u32[]{:S(2)}, u32[]{:S(2)}) collective-permute-start(bf16[2064,128]{1,0:T(8,128)(2,1)S(1)} %shard_map.78.refs_1_), channel_id=1, source_target_pairs={{0,4},{4,8},{8,12},{12,14},{14,10},{10,6},{6,2},{2,0},{1,3},{5,1},... | collective-permute-start | bytes 1585160 | tf_op jit(solution)/shard_map/ppermute | solution.py:442
  16.7 2.2 %copy-start = (bf16[32,2,64,512]{3,2,1,0:T(8,128)(2,1)S(1)}, bf16[32,2,64,512]{3,2,1,0:T(8,128)(2,1)}, u32[]{:S(2)}) copy-start(bf16[32,2,64,512]{3,2,1,0:T(8,128)(2,1)} %refs_3_.1) | copy-start | bytes 12582916
  18.9 7.0 %copy-start.1 = (bf16[32,2,64,512]{3,2,1,0:T(8,128)(2,1)S(1)}, bf16[32,2,64,512]{3,2,1,0:T(8,128)(2,1)}, u32[]{:S(2)}) copy-start(bf16[32,2,64,512]{3,2,1,0:T(8,128)(2,1)} %refs_3_.1) | copy-start | bytes 12582916
  21.2 9.4 %collective-permute-start.3 = (bf16[4,528,128]{2,1,0:T(8,128)(2,1)S(1)}, bf16[4,528,128]{2,1,0:T(8,128)(2,1)S(1)}, u32[]{:S(2)}, u32[]{:S(2)}) collective-permute-start(bf16[4,528,128]{2,1,0:T(8,128)(2,1)S(1)} %shard_map.80), channel_id=1, source_target_pairs={{0,4},{4,8},{8,12},{12,14},{14,10},{10,6},{6,2},{2,0},{1,3},{5,1},... | collective-permute-start | bytes 1622024 | tf_op jit(solution)/shard_map/ppermute | solution.py:442
  23.6 12.6 %collective-permute-start.6 = (bf16[2064,128]{1,0:T(8,128)(2,1)S(1)}, bf16[2064,128]{1,0:T(8,128)(2,1)S(1)}, u32[]{:S(2)}, u32[]{:S(2)}) collective-permute-start(bf16[2064,128]{1,0:T(8,128)(2,1)S(1)} %collective-permute-done.4.refs_1_), channel_id=1, source_target_pairs={{0,4},{4,8},{8,12},{12,14},{14,10},{10,6},{6,2},{2,0},{1,3},{5,1},... | collective-permute-start | bytes 1585160 | tf_op jit(solution)/shard_map/ppermute | solution.py:442
  31.6 10.5 %collective-permute-start.5 = (bf16[4,528,128]{2,1,0:T(8,128)(2,1)S(1)}, bf16[4,528,128]{2,1,0:T(8,128)(2,1)S(1)}, u32[]{:S(2)}, u32[]{:S(2)}) collective-permute-start(bf16[4,528,128]{2,1,0:T(8,128)(2,1)S(1)} %shard_map.82), channel_id=1, source_target_pairs={{0,4},{4,8},{8,12},{12,14},{14,10},{10,6},{6,2},{2,0},{1,3},{5,1},... | collective-permute-start | bytes 1622024 | tf_op jit(solution)/shard_map/ppermute | solution.py:442
  36.2 11.5 %collective-permute-start.8 = (bf16[2064,128]{1,0:T(8,128)(2,1)S(1)}, bf16[2064,128]{1,0:T(8,128)(2,1)S(1)}, u32[]{:S(2)}, u32[]{:S(2)}) collective-permute-start(bf16[2064,128]{1,0:T(8,128)(2,1)S(1)} %collective-permute-done.6.refs_1_), channel_id=1, source_target_pairs={{0,4},{4,8},{8,12},{12,14},{14,10},{10,6},{6,2},{2,0},{1,3},{5,1},... | collective-permute-start | bytes 1585160 | tf_op jit(solution)/shard_map/ppermute | solution.py:442
  43.0 10.5 %collective-permute-start.7 = (bf16[4,528,128]{2,1,0:T(8,128)(2,1)S(1)}, bf16[4,528,128]{2,1,0:T(8,128)(2,1)S(1)}, u32[]{:S(2)}, u32[]{:S(2)}) collective-permute-start(bf16[4,528,128]{2,1,0:T(8,128)(2,1)S(1)} %shard_map.84), channel_id=1, source_target_pairs={{0,4},{4,8},{8,12},{12,14},{14,10},{10,6},{6,2},{2,0},{1,3},{5,1},... | collective-permute-start | bytes 1622024 | tf_op jit(solution)/shard_map/ppermute | solution.py:442
  47.7 11.5 %collective-permute-start.10 = (bf16[2064,128]{1,0:T(8,128)(2,1)S(1)}, bf16[2064,128]{1,0:T(8,128)(2,1)S(1)}, u32[]{:S(2)}, u32[]{:S(2)}) collective-permute-start(bf16[2064,128]{1,0:T(8,128)(2,1)S(1)} %collective-permute-done.8.refs_1_), channel_id=1, source_target_pairs={{0,4},{4,8},{8,12},{12,14},{14,10},{10,6},{6,2},{2,0},{1,3},{5,1},... | collective-permute-start | bytes 1585160 | tf_op jit(solution)/shard_map/ppermute | solution.py:442
  54.5 10.5 %collective-permute-start.9 = (bf16[4,528,128]{2,1,0:T(8,128)(2,1)S(1)}, bf16[4,528,128]{2,1,0:T(8,128)(2,1)S(1)}, u32[]{:S(2)}, u32[]{:S(2)}) collective-permute-start(bf16[4,528,128]{2,1,0:T(8,128)(2,1)S(1)} %shard_map.86), channel_id=1, source_target_pairs={{0,4},{4,8},{8,12},{12,14},{14,10},{10,6},{6,2},{2,0},{1,3},{5,1},... | collective-permute-start | bytes 1622024 | tf_op jit(solution)/shard_map/ppermute | solution.py:442
  59.2 11.5 %collective-permute-start.12 = (bf16[2064,128]{1,0:T(8,128)(2,1)S(1)}, bf16[2064,128]{1,0:T(8,128)(2,1)S(1)}, u32[]{:S(2)}, u32[]{:S(2)}) collective-permute-start(bf16[2064,128]{1,0:T(8,128)(2,1)S(1)} %collective-permute-done.10.refs_1_), channel_id=1, source_target_pairs={{0,4},{4,8},{8,12},{12,14},{14,10},{10,6},{6,2},{2,0},{1,3},{5,1},... | collective-permute-start | bytes 1585160 | tf_op jit(solution)/shard_map/ppermute | solution.py:442
  65.9 10.5 %collective-permute-start.11 = (bf16[4,528,128]{2,1,0:T(8,128)(2,1)S(1)}, bf16[4,528,128]{2,1,0:T(8,128)(2,1)S(1)}, u32[]{:S(2)}, u32[]{:S(2)}) collective-permute-start(bf16[4,528,128]{2,1,0:T(8,128)(2,1)S(1)} %shard_map.88), channel_id=1, source_target_pairs={{0,4},{4,8},{8,12},{12,14},{14,10},{10,6},{6,2},{2,0},{1,3},{5,1},... | collective-permute-start | bytes 1622024 | tf_op jit(solution)/shard_map/ppermute | solution.py:442
  70.6 11.5 %collective-permute-start.14 = (bf16[2064,128]{1,0:T(8,128)(2,1)S(1)}, bf16[2064,128]{1,0:T(8,128)(2,1)S(1)}, u32[]{:S(2)}, u32[]{:S(2)}) collective-permute-start(bf16[2064,128]{1,0:T(8,128)(2,1)S(1)} %collective-permute-done.12.refs_1_), channel_id=1, source_target_pairs={{0,4},{4,8},{8,12},{12,14},{14,10},{10,6},{6,2},{2,0},{1,3},{5,1},... | collective-permute-start | bytes 1585160 | tf_op jit(solution)/shard_map/ppermute | solution.py:442
  77.4 10.5 %collective-permute-start.13 = (bf16[4,528,128]{2,1,0:T(8,128)(2,1)S(1)}, bf16[4,528,128]{2,1,0:T(8,128)(2,1)S(1)}, u32[]{:S(2)}, u32[]{:S(2)}) collective-permute-start(bf16[4,528,128]{2,1,0:T(8,128)(2,1)S(1)} %shard_map.90), channel_id=1, source_target_pairs={{0,4},{4,8},{8,12},{12,14},{14,10},{10,6},{6,2},{2,0},{1,3},{5,1},... | collective-permute-start | bytes 1622024 | tf_op jit(solution)/shard_map/ppermute | solution.py:442
  82.1 10.7 %copy-start.3 = (bf16[1,64,4096]{2,1,0:T(8,128)(2,1)S(1)}, bf16[1,64,4096]{2,1,0:T(8,128)(2,1)}, u32[]{:S(2)}) copy-start(bf16[1,64,4096]{2,1,0:T(8,128)(2,1)} %refs_1_) | copy-start | bytes 1572868
  82.1 10.7 %copy-start.4 = (bf16[1,2,64,512]{3,2,1,0:T(8,128)(2,1)S(1)}, bf16[1,2,64,512]{3,2,1,0:T(8,128)(2,1)}, u32[]{:S(2)}) copy-start(bf16[1,2,64,512]{3,2,1,0:T(8,128)(2,1)} %param.7) | copy-start | bytes 393220
  88.5 10.4 %collective-permute-start.16 = (bf16[2,528,128]{2,1,0:T(8,128)(2,1)S(1)}, bf16[2,528,128]{2,1,0:T(8,128)(2,1)S(1)}, u32[]{:S(2)}, u32[]{:S(2)}) collective-permute-start(bf16[2,528,128]{2,1,0:T(8,128)(2,1)S(1)} %shard_map.93), channel_id=1, source_target_pairs={{0,4},{4,8},{8,12},{12,14},{14,10},{10,6},{6,2},{2,0},{1,3},{5,1},... | collective-permute-start | bytes 811016 | tf_op jit(solution)/shard_map/ppermute | solution.py:442
  91.6 8.6 %collective-permute-start.15 = (bf16[2,528,128]{2,1,0:T(8,128)(2,1)S(1)}, bf16[2,528,128]{2,1,0:T(8,128)(2,1)S(1)}, u32[]{:S(2)}, u32[]{:S(2)}) collective-permute-start(bf16[2,528,128]{2,1,0:T(8,128)(2,1)S(1)} %shard_map.92), channel_id=1, source_target_pairs={{0,4},{4,8},{8,12},{12,14},{14,10},{10,6},{6,2},{2,0},{1,3},{5,1},... | collective-permute-start | bytes 811016 | tf_op jit(solution)/shard_map/ppermute | solution.py:442
  92.8 2.2 %copy-start.2 = (bf16[32,2,64,512]{3,2,1,0:T(8,128)(2,1)S(1)}, bf16[32,2,64,512]{3,2,1,0:T(8,128)(2,1)}, u32[]{:S(2)}) copy-start(bf16[32,2,64,512]{3,2,1,0:T(8,128)(2,1)} %refs_3_.1) | copy-start | bytes 12582916

commit v13 on v11

--- a/solution.py
+++ b/solution.py
@@ -156,114 +156,132 @@
     return [part(2 * j) for j in range(4)], [part(2 * j + 1) for j in range(4)]
 
 
-def attend_kernel(sizes, own, keeping, *refs):
-    heads, rows, suffix, cap, page_len = sizes
+def attend_kernel(sizes, jobs, own, keeping, *refs):
+    rows, suffix, cap, page_len, count = sizes
     refs = list(refs)
-    meta, q_ref = refs.pop(0), refs.pop(0)
+    meta = refs.pop(0)
+    queries = [refs.pop(0) for _ in range(count)]
     own_kv = refs.pop(0) if own else None
-    held, acc_ref, stat_ref = refs.pop(0), refs.pop(0), refs.pop(0)
+    held = refs.pop(0)
+    if keeping and keeping[0]:
+        refs.pop(0)
+    outs = [(refs.pop(0), refs.pop(0)) for _ in range(count)]
     stored = refs.pop(0) if keeping else None
     scores = refs.pop(0)
     late_scores = refs.pop(0) if own else None
     if keeping:
-        keep = pltpu.make_async_copy(held, stored, refs.pop(0))
+        span = pl.ds(*keeping)
+        keep = pltpu.make_async_copy(held.at[span], stored.at[span], refs.pop(0))
         keep.start()
     factor = HEAD_SIZE ** (-0.5) * LOG2E
     keys = cap * page_len
 
-    def stacked(part, h):
-        return jnp.concatenate([held[meta[0, c], part, :, block_of(h)] for c in range(cap)], 0)
-
-    def score(h):
-        q = q_ref[h * rows:(h + 1) * rows, :]
-        scores[h % 2] = dot_nt(q, stacked(0, h))
+    def stacked(n, part, h):
+        return jnp.concatenate([held[meta[n, c], part, :, block_of(h)] for c in range(cap)], 0)
+
+    def score(i):
+        n, first, h = jobs[i]
+        q = queries[n][first * rows:(first + 1) * rows, :]
+        scores[i % 2] = dot_nt(q, stacked(n, 0, h))
         if own:
             at = iota((rows, suffix), 0) % suffix
             causal = iota((rows, suffix), 1) <= at
-            late_scores[h % 2] = jnp.where(causal, dot_nt(q, own_kv[0, :, block_of(h)]), DEAD)
-
-    def weigh(h):
-        live = iota((1, keys), 1) < meta[0, cap] * page_len
-        s = jnp.where(live, scores[h % 2], DEAD)
+            late_scores[i % 2] = jnp.where(causal, dot_nt(q, own_kv[0, :, block_of(h)]), DEAD)
+
+    def weigh(i):
+        n, first, h = jobs[i]
+        live = iota((1, keys), 1) < meta[n, cap] * page_len
+        s = jnp.where(live, scores[i % 2], DEAD)
         top = jnp.max(s, axis=-1, keepdims=True)
         if own:
-            top = jnp.maximum(top, jnp.max(late_scores[h % 2], axis=-1, keepdims=True))
+            top = jnp.maximum(top, jnp.max(late_scores[i % 2], axis=-1, keepdims=True))
         top = jnp.maximum(top * factor, FLOOR).astype(jnp.bfloat16).astype(jnp.float32)
         p = jnp.exp2(s * factor - top).astype(jnp.bfloat16)
-        v = stacked(1, h)
+        v = stacked(n, 1, h)
         v = jnp.concatenate([v, jnp.ones_like(v)], 1)
         out = jnp.dot(p, v, preferred_element_type=jnp.float32)
         if own:
-            p = jnp.exp2(late_scores[h % 2] * factor - top).astype(jnp.bfloat16)
+            p = jnp.exp2(late_scores[i % 2] * factor - top).astype(jnp.bfloat16)
             v = own_kv[1, :, block_of(h)]
             v = jnp.concatenate([v, jnp.ones_like(v)], 1)
             out = out + jnp.dot(p, v, preferred_element_type=jnp.float32)
-        acc_ref[h] = out[:, :HEAD_SIZE]
+        acc_ref, stat_ref = outs[n]
+        acc_ref[first] = out[:, :HEAD_SIZE]
         total = out[:, HEAD_SIZE:]
         top = jnp.broadcast_to(top, total.shape)
         blocks = [block_of(j) for j in range(rows // HEAD_SIZE)]
-        stat_ref[h] = pack_stats([top[j] for j in blocks], [total[j] for j in blocks])
-
-    for h in range(heads + 1):
-        if h < heads:
-            score(h)
-        if h > 0:
-            weigh(h - 1)
+        stat_ref[first] = pack_stats([top[j] for j in blocks], [total[j] for j in blocks])
+
+    for i in range(len(jobs) + 1):
+        if i < len(jobs):
+            score(i)
+        if i > 0:
+            weigh(i - 1)
     if keeping:
         keep.wait()
 
 
-def attend(sizes, meta, queries, held, own=None, keeping=False, weight=1):
-    heads, rows, suffix, cap, page_len = sizes
-    keys = cap * page_len
-    shapes = [
-        jax.ShapeDtypeStruct((heads, rows, HEAD_SIZE), jnp.float32),
-        jax.ShapeDtypeStruct((heads, STAT_ROWS, HEAD_SIZE), jnp.bfloat16),
-    ]
-    specs = [VMEM, VMEM]
+def attend(sizes, jobs, meta, queries, held, own=None, keeping=None, store=None):
+    rows, suffix, cap, page_len = sizes
+    keys, count = cap * page_len, len(queries)
+    heads = len(jobs) // count
+    shapes, out_specs = [], []
+    for _ in queries:
+        shapes.append(jax.ShapeDtypeStruct((heads, rows, HEAD_SIZE), jnp.float32))
+        shapes.append(jax.ShapeDtypeStruct((heads, STAT_ROWS, HEAD_SIZE), jnp.bfloat16))
+        out_specs += [VMEM, VMEM]
     scratch = [pltpu.VMEM((2, rows, keys), jnp.float32)]
-    more = [held]
+    args, aliases = [meta, *queries], {}
     if own is not None:
-        more = [own, held]
+        args.append(own)
         scratch.append(pltpu.VMEM((2, rows, suffix), jnp.float32))
+    args.append(held)
+    in_specs = [SMEM] + [VMEM] * (len(args) - 1)
     if keeping:
         shapes.append(jax.ShapeDtypeStruct(held.shape, held.dtype))
-        specs.append(HBM)
+        out_specs.append(HBM)
         scratch.append(pltpu.SemaphoreType.DMA)
-    acc, stat, *pages = pl.pallas_call(
-        functools.partial(attend_kernel, sizes, own is not None, keeping),
+    if store is not None:
+        aliases[len(args)] = 2 * count
+        args.append(store)
+        in_specs.append(HBM)
+    out = pl.pallas_call(
+        functools.partial(attend_kernel, sizes + (count,), jobs, own is not None, keeping),
         out_shape=shapes,
-        in_specs=[SMEM] + [VMEM] * (1 + len(more)),
-        out_specs=specs,
+        in_specs=in_specs,
+        out_specs=out_specs,
         scratch_shapes=scratch,
+        input_output_aliases=aliases,
         compiler_params=pltpu.CompilerParams(vmem_limit_bytes=GRANT),
         cost_estimate=pl.CostEstimate(
-            flops=weight * heads * rows * keys * HEAD_SIZE * 8,
-            bytes_accessed=weight * heads * (rows * 6 + keys * 4) * HEAD_SIZE,
-            transcendentals=weight * heads * rows * keys,
+            flops=len(jobs) * rows * keys * HEAD_SIZE * 8,
+            bytes_accessed=len(jobs) * (rows * 6 + keys * 4) * HEAD_SIZE,
+            transcendentals=len(jobs) * rows * keys,
         ),
-    )(meta, queries, *more)
-    return (acc, stat), *pages
-
-
-def place_kernel(column, near_ref, below_ref, above_ref, page_ref, old_ref, out_ref, sem):
-    slot = jnp.where(near_ref[0] == 1, below_ref[0, column], above_ref[0, column])
+    )(*args)
+    return [(out[2 * n], out[2 * n + 1]) for n in range(count)] + list(out[2 * count:])
+
+
+def place_kernel(half, column, me_ref, lists_ref, page_ref, old_ref, out_ref, sem):
+    me = me_ref[0]
+    from_below = (me >= half) == (me % 2 == 0)
+    slot = jnp.where(from_below, lists_ref[0, column], lists_ref[1, column])
     copy = pltpu.make_async_copy(page_ref.at[0], out_ref.at[slot], sem)
     copy.start()
     copy.wait()
 
 
-def place_page(column, near, below, above, page, store):
+def place_page(half, column, me, lists, page, store):
     return pl.pallas_call(
-        functools.partial(place_kernel, column),
+        functools.partial(place_kernel, half, column),
         out_shape=jax.ShapeDtypeStruct(store.shape, store.dtype),
-        in_specs=[SMEM, SMEM, SMEM, VMEM, HBM],
+        in_specs=[SMEM, SMEM, VMEM, HBM],
         out_specs=HBM,
         scratch_shapes=[pltpu.SemaphoreType.DMA],
-        input_output_aliases={4: 0},
+        input_output_aliases={3: 0},
         compiler_params=pltpu.CompilerParams(vmem_limit_bytes=GRANT),
         cost_estimate=LIGHT,
-    )(near, below, above, page, store)
+    )(me, lists, page, store)
 
 
 def blend(parts):
@@ -300,8 +318,9 @@
         out_ref[h, rows:, :] = pack_stats(tops, totals)
 
 
-def final_kernel(suffix, in_ref, acc_ref, stat_ref, out_ref, done, sems):
-    heads, rows = acc_ref.shape[:2]
+def final_kernel(suffix, first, in_ref, acc_ref, stat_ref, *refs):
+    out_ref, done, sems = refs[-3:]
+    heads, rows = in_ref.shape[0], acc_ref.shape[1]
     groups = rows // suffix
     copies = []
     for h in range(heads):
@@ -318,27 +337,34 @@
             for i in range(HEAD_SIZE // suffix):
                 g = h * groups + j * (HEAD_SIZE // suffix) + i
                 done[0, :, block_of(g)] = out[i * suffix:(i + 1) * suffix]
-        span = pl.ds(h * groups * HEAD_SIZE, groups * HEAD_SIZE)
+        width = groups * HEAD_SIZE
         copies.append(
-            pltpu.make_async_copy(done.at[:, :, span], out_ref.at[:, :, span], sems.at[h])
+            pltpu.make_async_copy(
+                done.at[:, :, pl.ds(h * width, width)],
+                out_ref.at[:, :, pl.ds((first + h) * width, width)],
+                sems.at[h],
+            )
         )
         copies[-1].start()
     for copy in copies:
         copy.wait()
 
 
-def finish(suffix, like, block, part):
+def finish(suffix, first, like, block, part, before=None):
+    heads, rows = block.shape[0], part[0].shape[1]
+    args = [block, *part] + ([] if before is None else [before])
     return pl.pallas_call(
-        functools.partial(final_kernel, suffix),
+        functools.partial(final_kernel, suffix, first),
         out_shape=jax.ShapeDtypeStruct(like.shape, like.dtype),
-        in_specs=[VMEM] * 3,
+        in_specs=[VMEM] * 3 + [HBM] * (len(args) - 3),
         out_specs=HBM,
         scratch_shapes=[
-            pltpu.VMEM(like.shape, like.dtype),
-            pltpu.SemaphoreType.DMA((part[0].shape[0],)),
+            pltpu.VMEM((1, suffix, heads * rows // suffix * HEAD_SIZE), like.dtype),
+            pltpu.SemaphoreType.DMA((heads,)),
         ],
+        input_output_aliases={} if before is None else {3: 0},
         compiler_params=pltpu.CompilerParams(vmem_limit_bytes=GRANT),
-    )(block, *part)
+    )(*args)
 
 
 def call(kernel, shape, *args):
@@ -353,12 +379,15 @@
     )(*args)
 
 
-def prepare_kernel(cap, pages_dev, length_ref, slot_ref, table_ref, q_ref, out_ref):
+def prepare_kernel(cap, pages_dev, length_ref, slot_ref, table_ref, q_ref, first_ref, second_ref):
     maxp = table_ref.shape[1]
     suffix = q_ref.shape[1]
-    rows = out_ref.shape[0] - LIST_ROWS
-    for g in range(rows // suffix):
-        out_ref[g * suffix:(g + 1) * suffix, :] = q_ref[0, :, block_of(g)]
+    rows = second_ref.shape[0] - LIST_ROWS
+    blocks = rows // suffix
+    for g in range(blocks):
+        into = slice(g * suffix, (g + 1) * suffix)
+        first_ref[into, :] = q_ref[0, :, block_of(g)]
+        second_ref[into, :] = q_ref[0, :, block_of(blocks + g)]
     table = table_ref[...]
     owner = lax.div(table, pages_dev)
     local = (table - owner * pages_dev).astype(jnp.float32)
@@ -380,83 +409,89 @@
     )
     slot = slot_ref[0].astype(jnp.float32)
     lists = jnp.where(iota(lists.shape, 1) == cap + 1, slot, lists)
-    out_ref[rows:, :] = lists.astype(jnp.bfloat16)
+    first_ref[rows:, :] = lists.astype(jnp.bfloat16)
+    second_ref[rows:, :] = lists.astype(jnp.bfloat16)
 
 
 def prepare(cap, pages_dev, queries, page_table, prefix_pages, new_slots):
-    rows = queries.size // HEAD_SIZE
+    rows = queries.size // HEAD_SIZE // 2
     return pl.pallas_call(
         functools.partial(prepare_kernel, cap, pages_dev),
-        out_shape=jax.ShapeDtypeStruct((rows + LIST_ROWS, HEAD_SIZE), queries.dtype),
+        out_shape=[jax.ShapeDtypeStruct((rows + LIST_ROWS, HEAD_SIZE), queries.dtype)] * 2,
         in_specs=[SMEM, SMEM, VMEM, VMEM],
-        out_specs=VMEM,
+        out_specs=[VMEM, VMEM],
         compiler_params=pltpu.CompilerParams(vmem_limit_bytes=GRANT),
     )(prefix_pages, new_slots, page_table, queries)
 
 
 def queries_travel(queries, suffix_key_value, kv_pages, page_table, prefix_pages, new_slots):
     stores = lax.axis_size("store")
-    cores = lax.axis_size("tensor")
     pages_dev, _, page_len, width = kv_pages.shape
     cap = page_table.shape[1] // stores
-    heads = width // HEAD_SIZE
     suffix = queries.shape[1]
     rows = queries.shape[2] // width * suffix
-    sizes = (heads, rows, suffix, cap, page_len)
+    sizes = (rows, suffix, cap, page_len)
     half = stores // 2
+    heads = width // HEAD_SIZE // 2
     me = lax.axis_index("store")
 
     order = list(range(0, stores, 2)) + list(range(1, stores, 2))[::-1]
-    route = [
-        (order[i] * cores + core, order[(i + 1 - 2 * (core % 2)) % stores] * cores + core)
-        for core in range(cores)
-        for i in range(stores)
-    ]
-
-    def onward(x):
-        return lax.ppermute(x, ("store", "tensor"), route)
-
-    def listed(x):
-        row = lax.dynamic_slice(x, (heads * rows + me, 0), (1, HEAD_SIZE))
-        return row.astype(jnp.int32)
+    up = [(order[i], order[(i + 1) % stores]) for i in range(stores)]
+    down = [(order[i], order[i - 1]) for i in range(stores)]
+    routes = (up, down)
+    sides = range(2)
+
+    def onward(side, x):
+        return lax.ppermute(x, "store", routes[side])
+
+    def listed(arrays):
+        found = [lax.dynamic_slice(x, (heads * rows + me, 0), (1, HEAD_SIZE)) for x in arrays]
+        return jnp.concatenate(found).astype(jnp.int32)
 
     def after(values, token):
         return lax.optimization_barrier((values, token))[0]
 
+    def attend_own(side, token):
+        jobs = [(0, h, side * heads + h) for h in range(heads)]
+        mine_here = after(mine[side], token)
+        return attend(sizes, jobs, listed(mine[:1]), [mine_here], kv_pages, suffix_key_value[0])
+
     mine = prepare(cap, pages_dev, queries, page_table, prefix_pages, new_slots)
-    moving = onward(mine)
-    arrived = shifted(after(suffix_key_value, mine), "store", half)
-
-    own, store = attend(
-        sizes, listed(mine), mine, kv_pages, suffix_key_value[0], True, weight=8
-    )
+    moving = [onward(side, mine[side]) for side in sides]
+    own = attend_own(0, [])
     token = own
-    partial = None
-    lists = {}
+    lists, partial = {}, None
+    jobs = [(side, h, side * heads + h) for side in sides for h in range(heads)]
+    pages = pages_dev // 2
     for step in range(1, stores):
         came = after(moving, token)
         if step < stores - 1:
-            moving = onward(came)
+            moving = [onward(side, came[side]) for side in sides]
         lists[step] = listed(came)
-        part, = attend(sizes, lists[step], came, kv_pages)
+        if step == 2:
+            *parts, store = attend(sizes, jobs, lists[step], came, kv_pages, None, (0, pages))
+        elif step == 3:
+            span = (pages, pages_dev - pages)
+            *parts, store = attend(sizes, jobs, lists[step], came, kv_pages, None, span, store)
+        else:
+            parts = attend(sizes, jobs, lists[step], came, kv_pages)
         if step == 1:
-            block = packed(after(part, arrived))
+            blocks = [packed(part) for part in parts]
         else:
-            block = merged(after(partial, part), part)
-        partial = onward(block)
-        token = block
-    attended = finish(suffix, queries, partial, own)
-
-    near = ((me >= half) == (me % 2 == 0)) == (lax.axis_index("tensor") % 2 == 0)
-    quarter = stores // 4
-    store = place_page(
-        cap + 1,
-        near.astype(jnp.int32)[None],
-        lists[quarter],
-        lists[stores - quarter],
-        arrived,
-        after(store, token),
-    )
+            if step == stores - 1:
+                parts = after(parts, arrived)
+            blocks = [merged(after(partial[side], parts), parts[side]) for side in sides]
+        partial = [onward(side, blocks[side]) for side in sides]
+        token = blocks
+        if step == half:
+            own += attend_own(1, token)
+            token = [blocks, own]
+        if step == stores - 2:
+            arrived = shifted(after(suffix_key_value, token), "store", half)
+    near = lists[stores // 4]
+    store = place_page(half, cap + 1, me[None], near, arrived, after(store, token))
+    attended = finish(suffix, 0, queries, after(partial[0], store), own[0])
+    attended = finish(suffix, heads, queries, partial[1], own[1], attended)
     return (attended, store)
 
 

time: 103 us -> 103 us (level)
  starting transfers between devices: 38.8 us -> 31.7 us
  Pallas kernels: 28.3 us -> 32.3 us
  waiting for transfers between devices: 28.1 us -> 31.4 us
    ppermute x1, waiting for transfers between devices: 0.01 us -> 7.96 us  [shifted(): return lax.ppermute(block, axis, route)]
    ppermute x14 -> x28, starting transfers between devices: 36.2 us -> 30.4 us  [onward(): return lax.ppermute(x, 'store', routes[side])]
    ppermute x14 -> x28, waiting for transfers between devices: 28.1 us -> 23.4 us  [onward(): return lax.ppermute(x, 'store', routes[side])]
    pallas_call x10 -> x12, Pallas kernels: 22.1 us -> 24.5 us  [the longest x9 20.7 us: attend(): pl.pallas_call(functools.partial(attend_kernel, sizes + (count,), jobs, o...]
    pallas_call x7 -> x14, Pallas kernels: 5.93 us -> 7.59 us  [call(): pl.pallas_call(kernel, out_shape=shape, in_specs=[VMEM] * len(args), out_...]
    ppermute x1, starting transfers between devices: 2.59 us -> 1.38 us  [shifted(): return lax.ppermute(block, axis, route)]
    unnamed x10 -> x12, local copies, waits for them, and re-layouts: 4.78 us -> 4.79 us
  transfers between devices with their start and end apart: 15 -> 29, of which waited for: 13 -> 20; matrix products, arithmetic and copies ran while one was open for 0% -> 0% of each run, Pallas kernels for 25% -> 30%
where the time goes in v13:
time: 103 us
  Pallas kernels  32.3 us (31%)
  starting transfers between devices  31.7 us (31%)
  waiting for transfers between devices  31.4 us (30%)
  local copies, waits for them, and re-layouts  4.9 us (5%)
  between operations  2.4 us (2%)
    ppermute x28, starting transfers between devices, onward(): return lax.ppermute(x, 'store', routes[side])  30.4 us
    ppermute x28, waiting for transfers between devices, onward(): return lax.ppermute(x, 'store', routes[side])  23.4 us
    pallas_call x9, Pallas kernels, attend(): pl.pallas_call(functools.partial(attend_kernel, sizes + (count,), jobs, o...  20.7 us
    ppermute x1, waiting for transfers between devices, shifted(): return lax.ppermute(block, axis, route)  7.96 us
    pallas_call x14, Pallas kernels, call(): pl.pallas_call(kernel, out_shape=shape, in_specs=[VMEM] * len(args), out_...  7.59 us
    unnamed x12, local copies, waits for them, and re-layouts  4.79 us
    pallas_call x2, Pallas kernels, finish(): pl.pallas_call(functools.partial(final_kernel, suffix, first), out_shape=...  2.54 us
  transfers between devices with their start and end apart: 29, of which 20 were waited for; matrix products, arithmetic and copies ran while one was open for 0% of the time, Pallas kernels for 30%

profile of v13, /device:TPU:0, one launch (start us, length us, event | category | flops | bytes accessed | tf_op | source)
XLA Modules:
  0.0 102.8 jit_solution(11344886466490158142)
XLA Ops:
  1.9 1.0 %copy-done.4 = bf16[1,64,4096]{2,1,0:T(8,128)(2,1)S(1)} copy-done((bf16[1,64,4096]{2,1,0:T(8,128)(2,1)S(1)}, bf16[1,64,4096]{2,1,0:T(8,128)(2,1)}, u32[]{:S(2)}) %copy-start.4) | copy-done | bytes 524312
  3.0 0.7 copy-done.5
  3.9 3.0 %collective-permute-start = (bf16[1040,128]{1,0:T(8,128)(2,1)S(1)}, bf16[1040,128]{1,0:T(8,128)(2,1)S(1)}, u32[]{:S(2)}, u32[]{:S(2)}) collective-permute-start(bf16[1040,128]{1,0:T(8,128)(2,1)S(1)} %get-tuple-element.72.refs_1_), channel_id=1, source_target_pairs={{0,4},{4,8},{8,12},{12,14},{14,10},{10,6},{6,2},{2,0},{1,5},{5,9},... | collective-permute-start | bytes 798728 | tf_op jit(solution)/shard_map/ppermute | solution.py:445
  7.0 2.2 %copy-done = bf16[32,2,64,512]{3,2,1,0:T(8,128)(2,1)S(1)} copy-done((bf16[32,2,64,512]{3,2,1,0:T(8,128)(2,1)S(1)}, bf16[32,2,64,512]{3,2,1,0:T(8,128)(2,1)}, u32[]{:S(2)}) %copy-start) | copy-done | bytes 4194328
  9.1 0.9 copy-done.2
  10.1 1.8 %shard_map.78 = (f32[2,512,128]{2,1,0:T(8,128)S(1)}, bf16[2,16,128]{2,1,0:T(8,128)(2,1)S(1)}) custom-call(s32[1,128]{1,0:T(1,128)S(1)} %fusion.refs_0_, bf16[1040,128]{1,0:T(8,128)(2,1)S(1)} %get-tuple-element.72.refs_1_, bf16[2,64,512]{2,1,0:T(8,128)(2,1)S(1)} %bitcast.2, bf16[32,2,64,512]{3,2,1,0:T(8,128)(2,1)S(1)} %copy-done), custom_call_target="tpu_custom_call" | custom-call | flops 536870912 | bytes 1310720 | tf_op jit(solution)/shard_map/pallas_call | solution.py:248
  11.8 1.4 %collective-permute-done.refs_1_ = bf16[1040,128]{1,0:T(8,128)(2,1)S(1)} collective-permute-done((bf16[1040,128]{1,0:T(8,128)(2,1)S(1)}, bf16[1040,128]{1,0:T(8,128)(2,1)S(1)}, u32[]{:S(2)}, u32[]{:S(2)}) %collective-permute-start) | collective-permute-done | bytes 266272 | tf_op jit(solution)/shard_map/ppermute | solution.py:445
  13.3 1.5 %collective-permute-done.1.refs_2_ = bf16[1040,128]{1,0:T(8,128)(2,1)S(1)} collective-permute-done((bf16[1040,128]{1,0:T(8,128)(2,1)S(1)}, bf16[1040,128]{1,0:T(8,128)(2,1)S(1)}, u32[]{:S(2)}, u32[]{:S(2)}) %collective-permute-start.1) | collective-permute-done | bytes 266272 | tf_op jit(solution)/shard_map/ppermute | solution.py:445
  14.8 1.6 %collective-permute-start.3 = (bf16[1040,128]{1,0:T(8,128)(2,1)S(1)}, bf16[1040,128]{1,0:T(8,128)(2,1)S(1)}, u32[]{:S(2)}, u32[]{:S(2)}) collective-permute-start(bf16[1040,128]{1,0:T(8,128)(2,1)S(1)} %collective-permute-done.refs_1_), channel_id=1, source_target_pairs={{0,4},{4,8},{8,12},{12,14},{14,10},{10,6},{6,2},{2,0},{1,5},{5,9},... | collective-permute-start | bytes 798728 | tf_op jit(solution)/shard_map/ppermute | solution.py:445
  16.9 2.3 %shard_map.79 = (f32[2,512,128]{2,1,0:T(8,128)S(1)}, bf16[2,16,128]{2,1,0:T(8,128)(2,1)S(1)}, f32[2,512,128]{2,1,0:T(8,128)S(1)}, bf16[2,16,128]{2,1,0:T(8,128)(2,1)S(1)}) custom-call(s32[2,128]{1,0:T(2,128)S(1)} %maximum_convert_fusion.refs_0_, bf16[1040,128]{1,0:T(8,128)(2,1)S(1)} %collective-permute-done.refs_1_, ...), custom_call_target="tpu_custom_call" | custom-call | flops 1073741824 | bytes 2621440 | tf_op jit(solution)/shard_map/pallas_call | solution.py:248
  19.2 1.6 %collective-permute-start.8 = (bf16[2,528,128]{2,1,0:T(8,128)(2,1)S(1)}, bf16[2,528,128]{2,1,0:T(8,128)(2,1)S(1)}, u32[]{:S(2)}, u32[]{:S(2)}) collective-permute-start(bf16[2,528,128]{2,1,0:T(8,128)(2,1)S(1)} %shard_map.81), channel_id=1, source_target_pairs={{0,4},{4,8},{8,12},{12,14},{14,10},{10,6},{6,2},{2,0},{1,5},{5,9},... | collective-permute-start | bytes 811016 | tf_op jit(solution)/shard_map/ppermute | solution.py:445
  21.3 2.2 %collective-permute-done.3.refs_1_ = bf16[1040,128]{1,0:T(8,128)(2,1)S(1)} collective-permute-done((bf16[1040,128]{1,0:T(8,128)(2,1)S(1)}, bf16[1040,128]{1,0:T(8,128)(2,1)S(1)}, u32[]{:S(2)}, u32[]{:S(2)}) %collective-permute-start.3) | collective-permute-done | bytes 266272 | tf_op jit(solution)/shard_map/ppermute | solution.py:445
  23.5 1.2 %collective-permute-done.4.refs_2_ = bf16[1040,128]{1,0:T(8,128)(2,1)S(1)} collective-permute-done((bf16[1040,128]{1,0:T(8,128)(2,1)S(1)}, bf16[1040,128]{1,0:T(8,128)(2,1)S(1)}, u32[]{:S(2)}, u32[]{:S(2)}) %collective-permute-start.4) | collective-permute-done | bytes 266272 | tf_op jit(solution)/shard_map/ppermute | solution.py:445
  24.8 1.6 %collective-permute-start.6 = (bf16[1040,128]{1,0:T(8,128)(2,1)S(1)}, bf16[1040,128]{1,0:T(8,128)(2,1)S(1)}, u32[]{:S(2)}, u32[]{:S(2)}) collective-permute-start(bf16[1040,128]{1,0:T(8,128)(2,1)S(1)} %collective-permute-done.3.refs_1_), channel_id=1, source_target_pairs={{0,4},{4,8},{8,12},{12,14},{14,10},{10,6},{6,2},{2,0},{1,5},{5,9},... | collective-permute-start | bytes 798728 | tf_op jit(solution)/shard_map/ppermute | solution.py:445
  26.8 2.6 %shard_map.82 = (f32[2,512,128]{2,1,0:T(8,128)S(1)}, bf16[2,16,128]{2,1,0:T(8,128)(2,1)S(1)}, f32[2,512,128]{2,1,0:T(8,128)S(1)}, bf16[2,16,128]{2,1,0:T(8,128)(2,1)S(1)}, bf16[32,2,64,512]{3,2,1,0:T(8,128)(2,1)}) custom-call(s32[2,128]{1,0:T(2,128)S(1)} %maximum_convert_fusion.1.refs_0_.lists_ref, bf16[1040,128]{1,0:T(8,128)(2,1)S(1)} %collective-permute-done.3.refs_1_, ...), custom_call_target="tpu_custom_call" | custom-call | flops 1073741824 | bytes 2621440 | tf_op jit(solution)/shard_map/pallas_call | solution.py:248
  29.4 1.1 %collective-permute-done.2.in_ref = bf16[2,528,128]{2,1,0:T(8,128)(2,1)S(1)} collective-permute-done((bf16[2,528,128]{2,1,0:T(8,128)(2,1)S(1)}, bf16[2,528,128]{2,1,0:T(8,128)(2,1)S(1)}, u32[]{:S(2)}, u32[]{:S(2)}) %collective-permute-start.2) | collective-permute-done | bytes 270368 | tf_op jit(solution)/shard_map/ppermute | solution.py:445
  30.5 0.6 shard_map.84
  31.2 1.6 %collective-permute-start.12 = (bf16[2,528,128]{2,1,0:T(8,128)(2,1)S(1)}, bf16[2,528,128]{2,1,0:T(8,128)(2,1)S(1)}, u32[]{:S(2)}, u32[]{:S(2)}) collective-permute-start(bf16[2,528,128]{2,1,0:T(8,128)(2,1)S(1)} %shard_map.84), channel_id=1, source_target_pairs={{0,4},{4,8},{8,12},{12,14},{14,10},{10,6},{6,2},{2,0},{1,5},{5,9},... | collective-permute-start | bytes 811016 | tf_op jit(solution)/shard_map/ppermute | solution.py:445
  32.8 0.6 shard_map.83
  33.9 1.1 %collective-permute-done.6.refs_1_ = bf16[1040,128]{1,0:T(8,128)(2,1)S(1)} collective-permute-done((bf16[1040,128]{1,0:T(8,128)(2,1)S(1)}, bf16[1040,128]{1,0:T(8,128)(2,1)S(1)}, u32[]{:S(2)}, u32[]{:S(2)}) %collective-permute-start.6) | collective-permute-done | bytes 266272 | tf_op jit(solution)/shard_map/ppermute | solution.py:445
  35.0 1.2 %collective-permute-done.7.refs_2_ = bf16[1040,128]{1,0:T(8,128)(2,1)S(1)} collective-permute-done((bf16[1040,128]{1,0:T(8,128)(2,1)S(1)}, bf16[1040,128]{1,0:T(8,128)(2,1)S(1)}, u32[]{:S(2)}, u32[]{:S(2)}) %collective-permute-start.7) | collective-permute-done | bytes 266272 | tf_op jit(solution)/shard_map/ppermute | solution.py:445
  36.3 1.6 %collective-permute-start.10 = (bf16[1040,128]{1,0:T(8,128)(2,1)S(1)}, bf16[1040,128]{1,0:T(8,128)(2,1)S(1)}, u32[]{:S(2)}, u32[]{:S(2)}) collective-permute-start(bf16[1040,128]{1,0:T(8,128)(2,1)S(1)} %collective-permute-done.6.refs_1_), channel_id=1, source_target_pairs={{0,4},{4,8},{8,12},{12,14},{14,10},{10,6},{6,2},{2,0},{1,5},{5,9},... | collective-permute-start | bytes 798728 | tf_op jit(solution)/shard_map/ppermute | solution.py:445
  38.3 3.2 %shard_map.85 = (f32[2,512,128]{2,1,0:T(8,128)S(1)}, bf16[2,16,128]{2,1,0:T(8,128)(2,1)S(1)}, f32[2,512,128]{2,1,0:T(8,128)S(1)}, bf16[2,16,128]{2,1,0:T(8,128)(2,1)S(1)}, bf16[32,2,64,512]{3,2,1,0:T(8,128)(2,1)}) custom-call(s32[2,128]{1,0:T(2,128)S(1)} %maximum_convert_fusion.2.refs_0_, ...), custom_call_target="tpu_custom_call", output_to_operand_aliasing={{4}: (4, {})} | custom-call | flops 1073741824 | bytes 2621440 | tf_op jit(solution)/shard_map/pallas_call | solution.py:248
  41.5 1.4 %collective-permute-done.5.in_ref = bf16[2,528,128]{2,1,0:T(8,128)(2,1)S(1)} collective-permute-done((bf16[2,528,128]{2,1,0:T(8,128)(2,1)S(1)}, bf16[2,528,128]{2,1,0:T(8,128)(2,1)S(1)}, u32[]{:S(2)}, u32[]{:S(2)}) %collective-permute-start.5) | collective-permute-done | bytes 270368 | tf_op jit(solution)/shard_map/ppermute | solution.py:445
  42.9 0.6 shard_map.87
  43.5 1.6 %collective-permute-start.16 = (bf16[2,528,128]{2,1,0:T(8,128)(2,1)S(1)}, bf16[2,528,128]{2,1,0:T(8,128)(2,1)S(1)}, u32[]{:S(2)}, u32[]{:S(2)}) collective-permute-start(bf16[2,528,128]{2,1,0:T(8,128)(2,1)S(1)} %shard_map.87), channel_id=1, source_target_pairs={{0,4},{4,8},{8,12},{12,14},{14,10},{10,6},{6,2},{2,0},{1,5},{5,9},... | collective-permute-start | bytes 811016 | tf_op jit(solution)/shard_map/ppermute | solution.py:445
  45.1 0.6 shard_map.86
  46.5 1.7 %collective-permute-done.11.refs_2_ = bf16[1040,128]{1,0:T(8,128)(2,1)S(1)} collective-permute-done((bf16[1040,128]{1,0:T(8,128)(2,1)S(1)}, bf16[1040,128]{1,0:T(8,128)(2,1)S(1)}, u32[]{:S(2)}, u32[]{:S(2)}) %collective-permute-start.11) | collective-permute-done | bytes 266272 | tf_op jit(solution)/shard_map/ppermute | solution.py:445
  48.2 1.4 %collective-permute-start.14 = (bf16[1040,128]{1,0:T(8,128)(2,1)S(1)}, bf16[1040,128]{1,0:T(8,128)(2,1)S(1)}, u32[]{:S(2)}, u32[]{:S(2)}) collective-permute-start(bf16[1040,128]{1,0:T(8,128)(2,1)S(1)} %collective-permute-done.10.refs_1_), channel_id=1, source_target_pairs={{0,4},{4,8},{8,12},{12,14},{14,10},{10,6},{6,2},{2,0},{1,5},{5,9},... | collective-permute-start | bytes 798728 | tf_op jit(solution)/shard_map/ppermute | solution.py:445
  50.3 2.3 %shard_map.88 = (f32[2,512,128]{2,1,0:T(8,128)S(1)}, bf16[2,16,128]{2,1,0:T(8,128)(2,1)S(1)}, f32[2,512,128]{2,1,0:T(8,128)S(1)}, bf16[2,16,128]{2,1,0:T(8,128)(2,1)S(1)}) custom-call(s32[2,128]{1,0:T(2,128)S(1)} %maximum_convert_fusion.3.refs_0_, bf16[1040,128]{1,0:T(8,128)(2,1)S(1)} %collective-permute-done.10.refs_1_, ...), custom_call_target="tpu_custom_call" | custom-call | flops 1073741824 | bytes 2621440 | tf_op jit(solution)/shard_map/pallas_call | solution.py:248
  53.0 1.7 %collective-permute-done.9.in_ref = bf16[2,528,128]{2,1,0:T(8,128)(2,1)S(1)} collective-permute-done((bf16[2,528,128]{2,1,0:T(8,128)(2,1)S(1)}, bf16[2,528,128]{2,1,0:T(8,128)(2,1)S(1)}, u32[]{:S(2)}, u32[]{:S(2)}) %collective-permute-start.9) | collective-permute-done | bytes 270368 | tf_op jit(solution)/shard_map/ppermute | solution.py:445
  54.7 0.6 shard_map.90
  55.3 1.3 %collective-permute-start.20 = (bf16[2,528,128]{2,1,0:T(8,128)(2,1)S(1)}, bf16[2,528,128]{2,1,0:T(8,128)(2,1)S(1)}, u32[]{:S(2)}, u32[]{:S(2)}) collective-permute-start(bf16[2,528,128]{2,1,0:T(8,128)(2,1)S(1)} %shard_map.90), channel_id=1, source_target_pairs={{0,4},{4,8},{8,12},{12,14},{14,10},{10,6},{6,2},{2,0},{1,5},{5,9},... | collective-permute-start | bytes 811016 | tf_op jit(solution)/shard_map/ppermute | solution.py:445
  56.6 0.6 shard_map.89
  57.3 0.8 collective-permute-start.13
  58.1 1.8 %shard_map.91 = (f32[2,512,128]{2,1,0:T(8,128)S(1)}, bf16[2,16,128]{2,1,0:T(8,128)(2,1)S(1)}) custom-call(s32[1,128]{1,0:T(1,128)S(1)} %fusion.refs_0_, bf16[1040,128]{1,0:T(8,128)(2,1)S(1)} %get-tuple-element.107.refs_1_, bf16[2,64,512]{2,1,0:T(8,128)(2,1)S(1)} %bitcast.3, bf16[32,2,64,512]{3,2,1,0:T(8,128)(2,1)S(1)} %copy-done.1), custom_call_target="tpu_custom_call" | custom-call | flops 536870912 | bytes 1310720 | tf_op jit(solution)/shard_map/pallas_call | solution.py:248
  59.9 1.3 %collective-permute-start.18 = (bf16[1040,128]{1,0:T(8,128)(2,1)S(1)}, bf16[1040,128]{1,0:T(8,128)(2,1)S(1)}, u32[]{:S(2)}, u32[]{:S(2)}) collective-permute-start(bf16[1040,128]{1,0:T(8,128)(2,1)S(1)} %collective-permute-done.14.refs_1_), channel_id=1, source_target_pairs={{0,4},{4,8},{8,12},{12,14},{14,10},{10,6},{6,2},{2,0},{1,5},{5,9},... | collective-permute-start | bytes 798728 | tf_op jit(solution)/shard_map/ppermute | solution.py:445
  61.2 0.8 collective-permute-start.19
  62.0 2.3 %shard_map.92 = (f32[2,512,128]{2,1,0:T(8,128)S(1)}, bf16[2,16,128]{2,1,0:T(8,128)(2,1)S(1)}, f32[2,512,128]{2,1,0:T(8,128)S(1)}, bf16[2,16,128]{2,1,0:T(8,128)(2,1)S(1)}) custom-call(s32[2,128]{1,0:T(2,128)S(1)} %maximum_convert_fusion.4.refs_0_, bf16[1040,128]{1,0:T(8,128)(2,1)S(1)} %collective-permute-done.14.refs_1_, ...), custom_call_target="tpu_custom_call" | custom-call | flops 1073741824 | bytes 2621440 | tf_op jit(solution)/shard_map/pallas_call | solution.py:248
  64.8 1.4 %collective-permute-done.13.in_ref = bf16[2,528,128]{2,1,0:T(8,128)(2,1)S(1)} collective-permute-done((bf16[2,528,128]{2,1,0:T(8,128)(2,1)S(1)}, bf16[2,528,128]{2,1,0:T(8,128)(2,1)S(1)}, u32[]{:S(2)}, u32[]{:S(2)}) %collective-permute-start.13) | collective-permute-done | bytes 270368 | tf_op jit(solution)/shard_map/ppermute | solution.py:445
  66.2 0.6 shard_map.94
  66.8 1.3 %collective-permute-start.24 = (bf16[2,528,128]{2,1,0:T(8,128)(2,1)S(1)}, bf16[2,528,128]{2,1,0:T(8,128)(2,1)S(1)}, u32[]{:S(2)}, u32[]{:S(2)}) collective-permute-start(bf16[2,528,128]{2,1,0:T(8,128)(2,1)S(1)} %shard_map.94), channel_id=1, source_target_pairs={{0,4},{4,8},{8,12},{12,14},{14,10},{10,6},{6,2},{2,0},{1,5},{5,9},... | collective-permute-start | bytes 811016 | tf_op jit(solution)/shard_map/ppermute | solution.py:445
  68.1 0.6 shard_map.93
  68.8 0.8 collective-permute-start.17
  69.6 0.9 collective-permute-done.18.refs_1_
  70.5 0.7 collective-permute-done.19.refs_2_
  71.2 1.4 %collective-permute-start.22 = (bf16[1040,128]{1,0:T(8,128)(2,1)S(1)}, bf16[1040,128]{1,0:T(8,128)(2,1)S(1)}, u32[]{:S(2)}, u32[]{:S(2)}) collective-permute-start(bf16[1040,128]{1,0:T(8,128)(2,1)S(1)} %collective-permute-done.18.refs_1_), channel_id=1, source_target_pairs={{0,4},{4,8},{8,12},{12,14},{14,10},{10,6},{6,2},{2,0},{1,5},{5,9},... | collective-permute-start | bytes 798728 | tf_op jit(solution)/shard_map/ppermute | solution.py:445
  73.3 2.3 %shard_map.95 = (f32[2,512,128]{2,1,0:T(8,128)S(1)}, bf16[2,16,128]{2,1,0:T(8,128)(2,1)S(1)}, f32[2,512,128]{2,1,0:T(8,128)S(1)}, bf16[2,16,128]{2,1,0:T(8,128)(2,1)S(1)}) custom-call(s32[2,128]{1,0:T(2,128)S(1)} %maximum_convert_fusion.5.refs_0_, bf16[1040,128]{1,0:T(8,128)(2,1)S(1)} %collective-permute-done.18.refs_1_, ...), custom_call_target="tpu_custom_call" | custom-call | flops 1073741824 | bytes 2621440 | tf_op jit(solution)/shard_map/pallas_call | solution.py:248
  75.6 0.7 collective-permute-done.24.in_ref
  76.3 1.4 %collective-permute-done.17.in_ref = bf16[2,528,128]{2,1,0:T(8,128)(2,1)S(1)} collective-permute-done((bf16[2,528,128]{2,1,0:T(8,128)(2,1)S(1)}, bf16[2,528,128]{2,1,0:T(8,128)(2,1)S(1)}, u32[]{:S(2)}, u32[]{:S(2)}) %collective-permute-start.17) | collective-permute-done | bytes 270368 | tf_op jit(solution)/shard_map/ppermute | solution.py:445
  77.7 0.6 shard_map.97
  78.3 1.3 %collective-permute-start.27 = (bf16[2,528,128]{2,1,0:T(8,128)(2,1)S(1)}, bf16[2,528,128]{2,1,0:T(8,128)(2,1)S(1)}, u32[]{:S(2)}, u32[]{:S(2)}) collective-permute-start(bf16[2,528,128]{2,1,0:T(8,128)(2,1)S(1)} %shard_map.97), channel_id=1, source_target_pairs={{0,4},{4,8},{8,12},{12,14},{14,10},{10,6},{6,2},{2,0},{1,5},{5,9},... | collective-permute-start | bytes 811016 | tf_op jit(solution)/shard_map/ppermute | solution.py:445
  79.6 0.6 shard_map.96
  80.2 1.1 %collective-permute-start.21 = (bf16[2,528,128]{2,1,0:T(8,128)(2,1)S(1)}, bf16[2,528,128]{2,1,0:T(8,128)(2,1)S(1)}, u32[]{:S(2)}, u32[]{:S(2)}) collective-permute-start(bf16[2,528,128]{2,1,0:T(8,128)(2,1)S(1)} %shard_map.96), channel_id=1, source_target_pairs={{0,2},{4,0},{8,4},{12,8},{14,12},{10,14},{6,10},{2,6},{1,3},{5,1},... | collective-permute-start | bytes 811016 | tf_op jit(solution)/shard_map/ppermute | solution.py:445
  81.3 1.4 %collective-permute-start.25 = (bf16[1,2,64,512]{3,2,1,0:T(8,128)(2,1)S(1)}, bf16[1,2,64,512]{3,2,1,0:T(8,128)(2,1)S(1)}, u32[]{:S(2)}, u32[]{:S(2)}) collective-permute-start(bf16[1,2,64,512]{3,2,1,0:T(8,128)(2,1)S(1)} %copy-done.3), channel_id=1, source_target_pairs={{8,0},{10,2},{12,4},{14,6},{0,8},{2,10},{4,12},{6,14},{9,1},{11,3}... | collective-permute-start | bytes 393224 | tf_op jit(solution)/shard_map/ppermute | solution.py:26
  82.7 2.3 %shard_map.98 = (f32[2,512,128]{2,1,0:T(8,128)S(1)}, bf16[2,16,128]{2,1,0:T(8,128)(2,1)S(1)}, f32[2,512,128]{2,1,0:T(8,128)S(1)}, bf16[2,16,128]{2,1,0:T(8,128)(2,1)S(1)}) custom-call(s32[2,128]{1,0:T(2,128)S(1)} %maximum_convert_fusion.6.refs_0_, bf16[1040,128]{1,0:T(8,128)(2,1)S(1)} %collective-permute-done.22.refs_1_, ...), custom_call_target="tpu_custom_call" | custom-call | flops 1073741824 | bytes 2621440 | tf_op jit(solution)/shard_map/pallas_call | solution.py:248
  85.0 8.0 %collective-permute-done.25.page_ref = bf16[1,2,64,512]{3,2,1,0:T(8,128)(2,1)S(1)} collective-permute-done((bf16[1,2,64,512]{3,2,1,0:T(8,128)(2,1)S(1)}, bf16[1,2,64,512]{3,2,1,0:T(8,128)(2,1)S(1)}, u32[]{:S(2)}, u32[]{:S(2)}) %collective-permute-start.25) | collective-permute-done | bytes 131104 | tf_op jit(solution)/shard_map/ppermute | solution.py:26
  93.0 0.6 shard_map.100
  93.7 0.6 shard_map.99
  94.3 2.1 %collective-permute-start.26 = (bf16[2,528,128]{2,1,0:T(8,128)(2,1)S(1)}, bf16[2,528,128]{2,1,0:T(8,128)(2,1)S(1)}, u32[]{:S(2)}, u32[]{:S(2)}) collective-permute-start(bf16[2,528,128]{2,1,0:T(8,128)(2,1)S(1)} %shard_map.99), channel_id=1, source_target_pairs={{0,2},{4,0},{8,4},{12,8},{14,12},{10,14},{6,10},{2,6},{1,3},{5,1},... | collective-permute-start | bytes 811016 | tf_op jit(solution)/shard_map/ppermute | solution.py:445
  96.4 1.2 %shard_map.101 = bf16[32,2,64,512]{3,2,1,0:T(8,128)(2,1)} custom-call(s32[1]{0:T(128)} %bitcast.1.me_ref, s32[2,128]{1,0:T(2,128)S(1)} %maximum_convert_fusion.1.refs_0_.lists_ref, bf16[1,2,64,512]{3,2,1,0:T(8,128)(2,1)S(1)} %collective-permute-done.25.page_ref, bf16[32,2,64,512]{3,2,1,0:T(8,128)(2,1)} %get-tuple-element.140.old_ref), custom_call_target="tpu_custom_call", output_to_operand_aliasing={{}: (3, {})} | custom-call | flops 1 | bytes 1 | tf_op jit(solution)/shard_map/pallas_call | solution.py:275
  97.6 2.5 %collective-permute-done.28.in_ref = bf16[2,528,128]{2,1,0:T(8,128)(2,1)S(1)} collective-permute-done((bf16[2,528,128]{2,1,0:T(8,128)(2,1)S(1)}, bf16[2,528,128]{2,1,0:T(8,128)(2,1)S(1)}, u32[]{:S(2)}, u32[]{:S(2)}) %collective-permute-start.28) | collective-permute-done | bytes 270368 | tf_op jit(solution)/shard_map/ppermute | solution.py:445
  100.1 1.3 %shard_map.102.refs_0_ = bf16[1,64,4096]{2,1,0:T(8,128)(2,1)} custom-call(bf16[2,528,128]{2,1,0:T(8,128)(2,1)S(1)} %collective-permute-done.28.in_ref, f32[2,512,128]{2,1,0:T(8,128)S(1)} %get-tuple-element.74.acc_ref, bf16[2,16,128]{2,1,0:T(8,128)(2,1)S(1)} %get-tuple-element.75.stat_ref), custom_call_target="tpu_custom_call" | custom-call | tf_op jit(solution)/shard_map/pallas_call | solution.py:356
  101.4 1.3 %shard_map.103 = bf16[1,64,4096]{2,1,0:T(8,128)(2,1)} custom-call(bf16[2,528,128]{2,1,0:T(8,128)(2,1)S(1)} %collective-permute-done.26.in_ref, f32[2,512,128]{2,1,0:T(8,128)S(1)} %get-tuple-element.108.acc_ref, bf16[2,16,128]{2,1,0:T(8,128)(2,1)S(1)} %get-tuple-element.109.stat_ref, ...), custom_call_target="tpu_custom_call", output_to_operand_aliasing={{}: (3, {})} | custom-call | tf_op jit(solution)/shard_map/pallas_call | solution.py:356
  (54 shorter events, 5.9 us)
Async XLA Ops:
  1.9 1.0 %copy-start.4 = (bf16[1,64,4096]{2,1,0:T(8,128)(2,1)S(1)}, bf16[1,64,4096]{2,1,0:T(8,128)(2,1)}, u32[]{:S(2)}) copy-start(bf16[1,64,4096]{2,1,0:T(8,128)(2,1)} %q_ref.1) | copy-start | bytes 1572868
  3.0 0.7 copy-start.5
  3.9 9.4 %collective-permute-start = (bf16[1040,128]{1,0:T(8,128)(2,1)S(1)}, bf16[1040,128]{1,0:T(8,128)(2,1)S(1)}, u32[]{:S(2)}, u32[]{:S(2)}) collective-permute-start(bf16[1040,128]{1,0:T(8,128)(2,1)S(1)} %get-tuple-element.72.refs_1_), channel_id=1, source_target_pairs={{0,4},{4,8},{8,12},{12,14},{14,10},{10,6},{6,2},{2,0},{1,5},{5,9},... | collective-permute-start | bytes 798728 | tf_op jit(solution)/shard_map/ppermute | solution.py:445
  6.9 7.9 %collective-permute-start.1 = (bf16[1040,128]{1,0:T(8,128)(2,1)S(1)}, bf16[1040,128]{1,0:T(8,128)(2,1)S(1)}, u32[]{:S(2)}, u32[]{:S(2)}) collective-permute-start(bf16[1040,128]{1,0:T(8,128)(2,1)S(1)} %get-tuple-element.107.refs_1_), channel_id=1, source_target_pairs={{0,2},{4,0},{8,4},{12,8},{14,12},{10,14},{6,10},{2,6},{1,3},{5,1},... | collective-permute-start | bytes 798728 | tf_op jit(solution)/shard_map/ppermute | solution.py:445
  7.0 2.2 %copy-start = (bf16[32,2,64,512]{3,2,1,0:T(8,128)(2,1)S(1)}, bf16[32,2,64,512]{3,2,1,0:T(8,128)(2,1)}, u32[]{:S(2)}) copy-start(bf16[32,2,64,512]{3,2,1,0:T(8,128)(2,1)} %refs_3_.17) | copy-start | bytes 12582916
  9.1 0.9 copy-start.2
  10.0 6.8 %copy-start.1 = (bf16[32,2,64,512]{3,2,1,0:T(8,128)(2,1)S(1)}, bf16[32,2,64,512]{3,2,1,0:T(8,128)(2,1)}, u32[]{:S(2)}) copy-start(bf16[32,2,64,512]{3,2,1,0:T(8,128)(2,1)} %refs_3_.17) | copy-start | bytes 12582916
  14.8 8.7 %collective-permute-start.3 = (bf16[1040,128]{1,0:T(8,128)(2,1)S(1)}, bf16[1040,128]{1,0:T(8,128)(2,1)S(1)}, u32[]{:S(2)}, u32[]{:S(2)}) collective-permute-start(bf16[1040,128]{1,0:T(8,128)(2,1)S(1)} %collective-permute-done.refs_1_), channel_id=1, source_target_pairs={{0,4},{4,8},{8,12},{12,14},{14,10},{10,6},{6,2},{2,0},{1,5},{5,9},... | collective-permute-start | bytes 798728 | tf_op jit(solution)/shard_map/ppermute | solution.py:445
  16.4 8.4 %collective-permute-start.4 = (bf16[1040,128]{1,0:T(8,128)(2,1)S(1)}, bf16[1040,128]{1,0:T(8,128)(2,1)S(1)}, u32[]{:S(2)}, u32[]{:S(2)}) collective-permute-start(bf16[1040,128]{1,0:T(8,128)(2,1)S(1)} %collective-permute-done.1.refs_2_), channel_id=1, source_target_pairs={{0,2},{4,0},{8,4},{12,8},{14,12},{10,14},{6,10},{2,6},{1,3},{5,1},... | collective-permute-start | bytes 798728 | tf_op jit(solution)/shard_map/ppermute | solution.py:445
  19.2 10.2 %collective-permute-start.8 = (bf16[2,528,128]{2,1,0:T(8,128)(2,1)S(1)}, bf16[2,528,128]{2,1,0:T(8,128)(2,1)S(1)}, u32[]{:S(2)}, u32[]{:S(2)}) collective-permute-start(bf16[2,528,128]{2,1,0:T(8,128)(2,1)S(1)} %shard_map.81), channel_id=1, source_target_pairs={{0,4},{4,8},{8,12},{12,14},{14,10},{10,6},{6,2},{2,0},{1,5},{5,9},... | collective-permute-start | bytes 811016 | tf_op jit(solution)/shard_map/ppermute | solution.py:445
  20.8 9.7 %collective-permute-start.2 = (bf16[2,528,128]{2,1,0:T(8,128)(2,1)S(1)}, bf16[2,528,128]{2,1,0:T(8,128)(2,1)S(1)}, u32[]{:S(2)}, u32[]{:S(2)}) collective-permute-start(bf16[2,528,128]{2,1,0:T(8,128)(2,1)S(1)} %shard_map.80), channel_id=1, source_target_pairs={{0,2},{4,0},{8,4},{12,8},{14,12},{10,14},{6,10},{2,6},{1,3},{5,1},... | collective-permute-start | bytes 811016 | tf_op jit(solution)/shard_map/ppermute | solution.py:445
  24.8 10.3 %collective-permute-start.6 = (bf16[1040,128]{1,0:T(8,128)(2,1)S(1)}, bf16[1040,128]{1,0:T(8,128)(2,1)S(1)}, u32[]{:S(2)}, u32[]{:S(2)}) collective-permute-start(bf16[1040,128]{1,0:T(8,128)(2,1)S(1)} %collective-permute-done.3.refs_1_), channel_id=1, source_target_pairs={{0,4},{4,8},{8,12},{12,14},{14,10},{10,6},{6,2},{2,0},{1,5},{5,9},... | collective-permute-start | bytes 798728 | tf_op jit(solution)/shard_map/ppermute | solution.py:445
  26.3 9.9 %collective-permute-start.7 = (bf16[1040,128]{1,0:T(8,128)(2,1)S(1)}, bf16[1040,128]{1,0:T(8,128)(2,1)S(1)}, u32[]{:S(2)}, u32[]{:S(2)}) collective-permute-start(bf16[1040,128]{1,0:T(8,128)(2,1)S(1)} %collective-permute-done.4.refs_2_), channel_id=1, source_target_pairs={{0,2},{4,0},{8,4},{12,8},{14,12},{10,14},{6,10},{2,6},{1,3},{5,1},... | collective-permute-start | bytes 798728 | tf_op jit(solution)/shard_map/ppermute | solution.py:445
  31.2 10.3 %collective-permute-start.12 = (bf16[2,528,128]{2,1,0:T(8,128)(2,1)S(1)}, bf16[2,528,128]{2,1,0:T(8,128)(2,1)S(1)}, u32[]{:S(2)}, u32[]{:S(2)}) collective-permute-start(bf16[2,528,128]{2,1,0:T(8,128)(2,1)S(1)} %shard_map.84), channel_id=1, source_target_pairs={{0,4},{4,8},{8,12},{12,14},{14,10},{10,6},{6,2},{2,0},{1,5},{5,9},... | collective-permute-start | bytes 811016 | tf_op jit(solution)/shard_map/ppermute | solution.py:445
  33.4 9.5 %collective-permute-start.5 = (bf16[2,528,128]{2,1,0:T(8,128)(2,1)S(1)}, bf16[2,528,128]{2,1,0:T(8,128)(2,1)S(1)}, u32[]{:S(2)}, u32[]{:S(2)}) collective-permute-start(bf16[2,528,128]{2,1,0:T(8,128)(2,1)S(1)} %shard_map.83), channel_id=1, source_target_pairs={{0,2},{4,0},{8,4},{12,8},{14,12},{10,14},{6,10},{2,6},{1,3},{5,1},... | collective-permute-start | bytes 811016 | tf_op jit(solution)/shard_map/ppermute | solution.py:445
  36.3 10.3 %collective-permute-start.10 = (bf16[1040,128]{1,0:T(8,128)(2,1)S(1)}, bf16[1040,128]{1,0:T(8,128)(2,1)S(1)}, u32[]{:S(2)}, u32[]{:S(2)}) collective-permute-start(bf16[1040,128]{1,0:T(8,128)(2,1)S(1)} %collective-permute-done.6.refs_1_), channel_id=1, source_target_pairs={{0,4},{4,8},{8,12},{12,14},{14,10},{10,6},{6,2},{2,0},{1,5},{5,9},... | collective-permute-start | bytes 798728 | tf_op jit(solution)/shard_map/ppermute | solution.py:445
  37.8 10.4 %collective-permute-start.11 = (bf16[1040,128]{1,0:T(8,128)(2,1)S(1)}, bf16[1040,128]{1,0:T(8,128)(2,1)S(1)}, u32[]{:S(2)}, u32[]{:S(2)}) collective-permute-start(bf16[1040,128]{1,0:T(8,128)(2,1)S(1)} %collective-permute-done.7.refs_2_), channel_id=1, source_target_pairs={{0,2},{4,0},{8,4},{12,8},{14,12},{10,14},{6,10},{2,6},{1,3},{5,1},... | collective-permute-start | bytes 798728 | tf_op jit(solution)/shard_map/ppermute | solution.py:445
  43.5 14.6 %copy-start.3 = (bf16[1,2,64,512]{3,2,1,0:T(8,128)(2,1)S(1)}, bf16[1,2,64,512]{3,2,1,0:T(8,128)(2,1)}, u32[]{:S(2)}) copy-start(bf16[1,2,64,512]{3,2,1,0:T(8,128)(2,1)} %param.7) | copy-start | bytes 393220
  43.5 9.5 %collective-permute-start.16 = (bf16[2,528,128]{2,1,0:T(8,128)(2,1)S(1)}, bf16[2,528,128]{2,1,0:T(8,128)(2,1)S(1)}, u32[]{:S(2)}, u32[]{:S(2)}) collective-permute-start(bf16[2,528,128]{2,1,0:T(8,128)(2,1)S(1)} %shard_map.87), channel_id=1, source_target_pairs={{0,4},{4,8},{8,12},{12,14},{14,10},{10,6},{6,2},{2,0},{1,5},{5,9},... | collective-permute-start | bytes 811016 | tf_op jit(solution)/shard_map/ppermute | solution.py:445
  45.8 8.9 %collective-permute-start.9 = (bf16[2,528,128]{2,1,0:T(8,128)(2,1)S(1)}, bf16[2,528,128]{2,1,0:T(8,128)(2,1)S(1)}, u32[]{:S(2)}, u32[]{:S(2)}) collective-permute-start(bf16[2,528,128]{2,1,0:T(8,128)(2,1)S(1)} %shard_map.86), channel_id=1, source_target_pairs={{0,2},{4,0},{8,4},{12,8},{14,12},{10,14},{6,10},{2,6},{1,3},{5,1},... | collective-permute-start | bytes 811016 | tf_op jit(solution)/shard_map/ppermute | solution.py:445
  48.2 11.7 %collective-permute-start.14 = (bf16[1040,128]{1,0:T(8,128)(2,1)S(1)}, bf16[1040,128]{1,0:T(8,128)(2,1)S(1)}, u32[]{:S(2)}, u32[]{:S(2)}) collective-permute-start(bf16[1040,128]{1,0:T(8,128)(2,1)S(1)} %collective-permute-done.10.refs_1_), channel_id=1, source_target_pairs={{0,4},{4,8},{8,12},{12,14},{14,10},{10,6},{6,2},{2,0},{1,5},{5,9},... | collective-permute-start | bytes 798728 | tf_op jit(solution)/shard_map/ppermute | solution.py:445
  49.6 10.3 %collective-permute-start.15 = (bf16[1040,128]{1,0:T(8,128)(2,1)S(1)}, bf16[1040,128]{1,0:T(8,128)(2,1)S(1)}, u32[]{:S(2)}, u32[]{:S(2)}) collective-permute-start(bf16[1040,128]{1,0:T(8,128)(2,1)S(1)} %collective-permute-done.11.refs_2_), channel_id=1, source_target_pairs={{0,2},{4,0},{8,4},{12,8},{14,12},{10,14},{6,10},{2,6},{1,3},{5,1},... | collective-permute-start | bytes 798728 | tf_op jit(solution)/shard_map/ppermute | solution.py:445
  55.3 9.5 %collective-permute-start.20 = (bf16[2,528,128]{2,1,0:T(8,128)(2,1)S(1)}, bf16[2,528,128]{2,1,0:T(8,128)(2,1)S(1)}, u32[]{:S(2)}, u32[]{:S(2)}) collective-permute-start(bf16[2,528,128]{2,1,0:T(8,128)(2,1)S(1)} %shard_map.90), channel_id=1, source_target_pairs={{0,4},{4,8},{8,12},{12,14},{14,10},{10,6},{6,2},{2,0},{1,5},{5,9},... | collective-permute-start | bytes 811016 | tf_op jit(solution)/shard_map/ppermute | solution.py:445
  57.3 8.9 %collective-permute-start.13 = (bf16[2,528,128]{2,1,0:T(8,128)(2,1)S(1)}, bf16[2,528,128]{2,1,0:T(8,128)(2,1)S(1)}, u32[]{:S(2)}, u32[]{:S(2)}) collective-permute-start(bf16[2,528,128]{2,1,0:T(8,128)(2,1)S(1)} %shard_map.89), channel_id=1, source_target_pairs={{0,2},{4,0},{8,4},{12,8},{14,12},{10,14},{6,10},{2,6},{1,3},{5,1},... | collective-permute-start | bytes 811016 | tf_op jit(solution)/shard_map/ppermute | solution.py:445
  59.9 10.6 %collective-permute-start.18 = (bf16[1040,128]{1,0:T(8,128)(2,1)S(1)}, bf16[1040,128]{1,0:T(8,128)(2,1)S(1)}, u32[]{:S(2)}, u32[]{:S(2)}) collective-permute-start(bf16[1040,128]{1,0:T(8,128)(2,1)S(1)} %collective-permute-done.14.refs_1_), channel_id=1, source_target_pairs={{0,4},{4,8},{8,12},{12,14},{14,10},{10,6},{6,2},{2,0},{1,5},{5,9},... | collective-permute-start | bytes 798728 | tf_op jit(solution)/shard_map/ppermute | solution.py:445
  61.2 10.0 %collective-permute-start.19 = (bf16[1040,128]{1,0:T(8,128)(2,1)S(1)}, bf16[1040,128]{1,0:T(8,128)(2,1)S(1)}, u32[]{:S(2)}, u32[]{:S(2)}) collective-permute-start(bf16[1040,128]{1,0:T(8,128)(2,1)S(1)} %collective-permute-done.15.refs_2_), channel_id=1, source_target_pairs={{0,2},{4,0},{8,4},{12,8},{14,12},{10,14},{6,10},{2,6},{1,3},{5,1},... | collective-permute-start | bytes 798728 | tf_op jit(solution)/shard_map/ppermute | solution.py:445
  66.8 9.5 %collective-permute-start.24 = (bf16[2,528,128]{2,1,0:T(8,128)(2,1)S(1)}, bf16[2,528,128]{2,1,0:T(8,128)(2,1)S(1)}, u32[]{:S(2)}, u32[]{:S(2)}) collective-permute-start(bf16[2,528,128]{2,1,0:T(8,128)(2,1)S(1)} %shard_map.94), channel_id=1, source_target_pairs={{0,4},{4,8},{8,12},{12,14},{14,10},{10,6},{6,2},{2,0},{1,5},{5,9},... | collective-permute-start | bytes 811016 | tf_op jit(solution)/shard_map/ppermute | solution.py:445
  68.8 8.9 %collective-permute-start.17 = (bf16[2,528,128]{2,1,0:T(8,128)(2,1)S(1)}, bf16[2,528,128]{2,1,0:T(8,128)(2,1)S(1)}, u32[]{:S(2)}, u32[]{:S(2)}) collective-permute-start(bf16[2,528,128]{2,1,0:T(8,128)(2,1)S(1)} %shard_map.93), channel_id=1, source_target_pairs={{0,2},{4,0},{8,4},{12,8},{14,12},{10,14},{6,10},{2,6},{1,3},{5,1},... | collective-permute-start | bytes 811016 | tf_op jit(solution)/shard_map/ppermute | solution.py:445
  71.2 11.4 %collective-permute-start.22 = (bf16[1040,128]{1,0:T(8,128)(2,1)S(1)}, bf16[1040,128]{1,0:T(8,128)(2,1)S(1)}, u32[]{:S(2)}, u32[]{:S(2)}) collective-permute-start(bf16[1040,128]{1,0:T(8,128)(2,1)S(1)} %collective-permute-done.18.refs_1_), channel_id=1, source_target_pairs={{0,4},{4,8},{8,12},{12,14},{14,10},{10,6},{6,2},{2,0},{1,5},{5,9},... | collective-permute-start | bytes 798728 | tf_op jit(solution)/shard_map/ppermute | solution.py:445
  72.7 10.0 %collective-permute-start.23 = (bf16[1040,128]{1,0:T(8,128)(2,1)S(1)}, bf16[1040,128]{1,0:T(8,128)(2,1)S(1)}, u32[]{:S(2)}, u32[]{:S(2)}) collective-permute-start(bf16[1040,128]{1,0:T(8,128)(2,1)S(1)} %collective-permute-done.19.refs_2_), channel_id=1, source_target_pairs={{0,2},{4,0},{8,4},{12,8},{14,12},{10,14},{6,10},{2,6},{1,3},{5,1},... | collective-permute-start | bytes 798728 | tf_op jit(solution)/shard_map/ppermute | solution.py:445
  78.3 14.6 %collective-permute-start.27 = (bf16[2,528,128]{2,1,0:T(8,128)(2,1)S(1)}, bf16[2,528,128]{2,1,0:T(8,128)(2,1)S(1)}, u32[]{:S(2)}, u32[]{:S(2)}) collective-permute-start(bf16[2,528,128]{2,1,0:T(8,128)(2,1)S(1)} %shard_map.97), channel_id=1, source_target_pairs={{0,4},{4,8},{8,12},{12,14},{14,10},{10,6},{6,2},{2,0},{1,5},{5,9},... | collective-permute-start | bytes 811016 | tf_op jit(solution)/shard_map/ppermute | solution.py:445
  80.2 13.4 %collective-permute-start.21 = (bf16[2,528,128]{2,1,0:T(8,128)(2,1)S(1)}, bf16[2,528,128]{2,1,0:T(8,128)(2,1)S(1)}, u32[]{:S(2)}, u32[]{:S(2)}) collective-permute-start(bf16[2,528,128]{2,1,0:T(8,128)(2,1)S(1)} %shard_map.96), channel_id=1, source_target_pairs={{0,2},{4,0},{8,4},{12,8},{14,12},{10,14},{6,10},{2,6},{1,3},{5,1},... | collective-permute-start | bytes 811016 | tf_op jit(solution)/shard_map/ppermute | solution.py:445
  81.3 11.7 %collective-permute-start.25 = (bf16[1,2,64,512]{3,2,1,0:T(8,128)(2,1)S(1)}, bf16[1,2,64,512]{3,2,1,0:T(8,128)(2,1)S(1)}, u32[]{:S(2)}, u32[]{:S(2)}) collective-permute-start(bf16[1,2,64,512]{3,2,1,0:T(8,128)(2,1)S(1)} %copy-done.3), channel_id=1, source_target_pairs={{8,0},{10,2},{12,4},{14,6},{0,8},{2,10},{4,12},{6,14},{9,1},{11,3}... | collective-permute-start | bytes 393224 | tf_op jit(solution)/shard_map/ppermute | solution.py:26
  93.6 6.5 %collective-permute-start.28 = (bf16[2,528,128]{2,1,0:T(8,128)(2,1)S(1)}, bf16[2,528,128]{2,1,0:T(8,128)(2,1)S(1)}, u32[]{:S(2)}, u32[]{:S(2)}) collective-permute-start(bf16[2,528,128]{2,1,0:T(8,128)(2,1)S(1)} %shard_map.100), channel_id=1, source_target_pairs={{0,4},{4,8},{8,12},{12,14},{14,10},{10,6},{6,2},{2,0},{1,5},{5,9},... | collective-permute-start | bytes 811016 | tf_op jit(solution)/shard_map/ppermute | solution.py:445
  94.3 7.1 %collective-permute-start.26 = (bf16[2,528,128]{2,1,0:T(8,128)(2,1)S(1)}, bf16[2,528,128]{2,1,0:T(8,128)(2,1)S(1)}, u32[]{:S(2)}, u32[]{:S(2)}) collective-permute-start(bf16[2,528,128]{2,1,0:T(8,128)(2,1)S(1)} %shard_map.99), channel_id=1, source_target_pairs={{0,2},{4,0},{8,4},{12,8},{14,12},{10,14},{6,10},{2,6},{1,3},{5,1},... | collective-permute-start | bytes 811016 | tf_op jit(solution)/shard_map/ppermute | solution.py:445

commit v14 on v13

--- a/solution.py
+++ b/solution.py
@@ -180,8 +180,8 @@
         return jnp.concatenate([held[meta[n, c], part, :, block_of(h)] for c in range(cap)], 0)
 
     def score(i):
-        n, first, h = jobs[i]
-        q = queries[n][first * rows:(first + 1) * rows, :]
+        n, _, h = jobs[i]
+        q = queries[n][h * rows:(h + 1) * rows, :]
         scores[i % 2] = dot_nt(q, stacked(n, 0, h))
         if own:
             at = iota((rows, suffix), 0) % suffix
@@ -189,7 +189,7 @@
             late_scores[i % 2] = jnp.where(causal, dot_nt(q, own_kv[0, :, block_of(h)]), DEAD)
 
     def weigh(i):
-        n, first, h = jobs[i]
+        n, spot, h = jobs[i]
         live = iota((1, keys), 1) < meta[n, cap] * page_len
         s = jnp.where(live, scores[i % 2], DEAD)
         top = jnp.max(s, axis=-1, keepdims=True)
@@ -206,11 +206,11 @@
             v = jnp.concatenate([v, jnp.ones_like(v)], 1)
             out = out + jnp.dot(p, v, preferred_element_type=jnp.float32)
         acc_ref, stat_ref = outs[n]
-        acc_ref[first] = out[:, :HEAD_SIZE]
+        acc_ref[spot] = out[:, :HEAD_SIZE]
         total = out[:, HEAD_SIZE:]
         top = jnp.broadcast_to(top, total.shape)
         blocks = [block_of(j) for j in range(rows // HEAD_SIZE)]
-        stat_ref[first] = pack_stats([top[j] for j in blocks], [total[j] for j in blocks])
+        stat_ref[spot] = pack_stats([top[j] for j in blocks], [total[j] for j in blocks])
 
     for i in range(len(jobs) + 1):
         if i < len(jobs):
@@ -245,6 +245,11 @@
         aliases[len(args)] = 2 * count
         args.append(store)
         in_specs.append(HBM)
+    work = pl.CostEstimate(
+        flops=len(jobs) * rows * keys * HEAD_SIZE * 8,
+        bytes_accessed=len(jobs) * (rows * 6 + keys * 4) * HEAD_SIZE,
+        transcendentals=len(jobs) * rows * keys,
+    )
     out = pl.pallas_call(
         functools.partial(attend_kernel, sizes + (count,), jobs, own is not None, keeping),
         out_shape=shapes,
@@ -253,35 +258,31 @@
         scratch_shapes=scratch,
         input_output_aliases=aliases,
         compiler_params=pltpu.CompilerParams(vmem_limit_bytes=GRANT),
-        cost_estimate=pl.CostEstimate(
-            flops=len(jobs) * rows * keys * HEAD_SIZE * 8,
-            bytes_accessed=len(jobs) * (rows * 6 + keys * 4) * HEAD_SIZE,
-            transcendentals=len(jobs) * rows * keys,
-        ),
+        cost_estimate=work,
     )(*args)
     return [(out[2 * n], out[2 * n + 1]) for n in range(count)] + list(out[2 * count:])
 
 
-def place_kernel(half, column, me_ref, lists_ref, page_ref, old_ref, out_ref, sem):
-    me = me_ref[0]
-    from_below = (me >= half) == (me % 2 == 0)
-    slot = jnp.where(from_below, lists_ref[0, column], lists_ref[1, column])
+def place_kernel(half, column, me_ref, core_ref, near_ref, far_ref, page_ref, old_ref, out_ref, sem):
+    me, core = me_ref[0], core_ref[0]
+    is_near = ((me >= half) == (me % 2 == 0)) == (core % 2 == 0)
+    slot = jnp.where(is_near, near_ref[0, column], far_ref[0, column])
     copy = pltpu.make_async_copy(page_ref.at[0], out_ref.at[slot], sem)
     copy.start()
     copy.wait()
 
 
-def place_page(half, column, me, lists, page, store):
+def place_page(half, column, me, core, near, far, page, store):
     return pl.pallas_call(
         functools.partial(place_kernel, half, column),
         out_shape=jax.ShapeDtypeStruct(store.shape, store.dtype),
-        in_specs=[SMEM, SMEM, VMEM, HBM],
+        in_specs=[SMEM] * 4 + [VMEM, HBM],
         out_specs=HBM,
         scratch_shapes=[pltpu.SemaphoreType.DMA],
-        input_output_aliases={3: 0},
+        input_output_aliases={5: 0},
         compiler_params=pltpu.CompilerParams(vmem_limit_bytes=GRANT),
         cost_estimate=LIGHT,
-    )(me, lists, page, store)
+    )(me[None], core[None], near, far, page, store)
 
 
 def blend(parts):
@@ -299,17 +300,17 @@
         out_ref[h, rows:, :] = stat_ref[h]
 
 
-def merge_kernel(in_ref, acc_ref, stat_ref, out_ref):
-    heads, rows = acc_ref.shape[:2]
+def merge_kernel(in_first, first, in_ref, acc_ref, stat_ref, out_ref):
+    heads, rows = out_ref.shape[0], acc_ref.shape[1]
     for h in range(heads):
-        in_top, in_total = unpack_stats(in_ref[h, rows:, :])
-        my_top, my_total = unpack_stats(stat_ref[h])
+        in_top, in_total = unpack_stats(in_ref[in_first + h, rows:, :])
+        my_top, my_total = unpack_stats(stat_ref[first + h])
         tops, totals = [], []
         for j in range(rows // HEAD_SIZE):
             acc, top, total = blend(
                 [
-                    (in_ref[h, block_of(j), :].astype(jnp.float32), in_top[j], in_total[j]),
-                    (acc_ref[h, block_of(j), :], my_top[j], my_total[j]),
+                    (in_ref[in_first + h, block_of(j), :].astype(jnp.float32), in_top[j], in_total[j]),
+                    (acc_ref[first + h, block_of(j), :], my_top[j], my_total[j]),
                 ]
             )
             out_ref[h, block_of(j), :] = acc.astype(out_ref.dtype)
@@ -379,15 +380,8 @@
     )(*args)
 
 
-def prepare_kernel(cap, pages_dev, length_ref, slot_ref, table_ref, q_ref, first_ref, second_ref):
+def lists_kernel(cap, pages_dev, length_ref, slot_ref, table_ref, out_ref):
     maxp = table_ref.shape[1]
-    suffix = q_ref.shape[1]
-    rows = second_ref.shape[0] - LIST_ROWS
-    blocks = rows // suffix
-    for g in range(blocks):
-        into = slice(g * suffix, (g + 1) * suffix)
-        first_ref[into, :] = q_ref[0, :, block_of(g)]
-        second_ref[into, :] = q_ref[0, :, block_of(blocks + g)]
     table = table_ref[...]
     owner = lax.div(table, pages_dev)
     local = (table - owner * pages_dev).astype(jnp.float32)
@@ -409,103 +403,127 @@
     )
     slot = slot_ref[0].astype(jnp.float32)
     lists = jnp.where(iota(lists.shape, 1) == cap + 1, slot, lists)
-    first_ref[rows:, :] = lists.astype(jnp.bfloat16)
-    second_ref[rows:, :] = lists.astype(jnp.bfloat16)
-
-
-def prepare(cap, pages_dev, queries, page_table, prefix_pages, new_slots):
-    rows = queries.size // HEAD_SIZE // 2
+    out_ref[...] = lists.astype(jnp.bfloat16)
+
+
+def list_pages(cap, pages_dev, page_table, prefix_pages, new_slots):
     return pl.pallas_call(
-        functools.partial(prepare_kernel, cap, pages_dev),
-        out_shape=[jax.ShapeDtypeStruct((rows + LIST_ROWS, HEAD_SIZE), queries.dtype)] * 2,
-        in_specs=[SMEM, SMEM, VMEM, VMEM],
-        out_specs=[VMEM, VMEM],
+        functools.partial(lists_kernel, cap, pages_dev),
+        out_shape=jax.ShapeDtypeStruct((LIST_ROWS, HEAD_SIZE), jnp.bfloat16),
+        in_specs=[SMEM, SMEM, VMEM],
+        out_specs=VMEM,
         compiler_params=pltpu.CompilerParams(vmem_limit_bytes=GRANT),
-    )(prefix_pages, new_slots, page_table, queries)
+    )(prefix_pages, new_slots, page_table)
+
+
+def join_kernel(q_ref, lists_ref, out_ref):
+    suffix, columns = q_ref.shape[1:]
+    for g in range(columns // HEAD_SIZE):
+        out_ref[g * suffix:(g + 1) * suffix, :] = q_ref[0, :, block_of(g)]
+    out_ref[columns // HEAD_SIZE * suffix:, :] = lists_ref[...]
 
 
 def queries_travel(queries, suffix_key_value, kv_pages, page_table, prefix_pages, new_slots):
     stores = lax.axis_size("store")
+    cores = lax.axis_size("tensor")
     pages_dev, _, page_len, width = kv_pages.shape
     cap = page_table.shape[1] // stores
+    heads = width // HEAD_SIZE
     suffix = queries.shape[1]
     rows = queries.shape[2] // width * suffix
     sizes = (rows, suffix, cap, page_len)
     half = stores // 2
-    heads = width // HEAD_SIZE // 2
     me = lax.axis_index("store")
 
     order = list(range(0, stores, 2)) + list(range(1, stores, 2))[::-1]
-    up = [(order[i], order[(i + 1) % stores]) for i in range(stores)]
-    down = [(order[i], order[i - 1]) for i in range(stores)]
-    routes = (up, down)
-    sides = range(2)
-
-    def onward(side, x):
-        return lax.ppermute(x, "store", routes[side])
-
-    def listed(arrays):
-        found = [lax.dynamic_slice(x, (heads * rows + me, 0), (1, HEAD_SIZE)) for x in arrays]
-        return jnp.concatenate(found).astype(jnp.int32)
+    route = [
+        (order[i] * cores + core, order[(i + 1 - 2 * (core % 2)) % stores] * cores + core)
+        for core in range(cores)
+        for i in range(stores)
+    ]
+
+    def onward(x):
+        return lax.ppermute(x, ("store", "tensor"), route)
+
+    def listed(x, below):
+        row = lax.dynamic_slice(x, (below + me, 0), (1, HEAD_SIZE))
+        return row.astype(jnp.int32)
 
     def after(values, token):
         return lax.optimization_barrier((values, token))[0]
 
-    def attend_own(side, token):
-        jobs = [(0, h, side * heads + h) for h in range(heads)]
-        mine_here = after(mine[side], token)
-        return attend(sizes, jobs, listed(mine[:1]), [mine_here], kv_pages, suffix_key_value[0])
-
-    mine = prepare(cap, pages_dev, queries, page_table, prefix_pages, new_slots)
-    moving = [onward(side, mine[side]) for side in sides]
-    own = attend_own(0, [])
-    token = own
-    lists, partial = {}, None
-    jobs = [(side, h, side * heads + h) for side in sides for h in range(heads)]
-    pages = pages_dev // 2
+    def joined(x, rows_below):
+        shape = jax.ShapeDtypeStruct((heads * rows + LIST_ROWS, HEAD_SIZE), queries.dtype)
+        return call(join_kernel, shape, x, rows_below)
+
+    first = onward(queries)
+    mine = list_pages(cap, pages_dev, page_table, prefix_pages, new_slots)
+    moving = joined(first, onward(mine))
+
+    own_queries = None
+    halves = [range(0, heads // 2), range(heads // 2, heads)]
+    token = []
+    lists, own = {}, []
     for step in range(1, stores):
         came = after(moving, token)
         if step < stores - 1:
-            moving = [onward(side, came[side]) for side in sides]
-        lists[step] = listed(came)
-        if step == 2:
-            *parts, store = attend(sizes, jobs, lists[step], came, kv_pages, None, (0, pages))
-        elif step == 3:
-            span = (pages, pages_dev - pages)
-            *parts, store = attend(sizes, jobs, lists[step], came, kv_pages, None, span, store)
+            moving = onward(came)
+        lists[step] = listed(came, heads * rows)
+        if step == stores - 3:
+            arrived = shifted(after(suffix_key_value, token), "store", half)
+        jobs = [(0, h, h) for h in range(heads)]
+        keeping, pages = None, pages_dev // 2
+        if step == 1:
+            keeping = (0, pages)
+            part, store = attend(sizes, jobs, lists[step], [came], kv_pages, None, keeping)
+        elif step == 2:
+            keeping = (pages, pages_dev - pages)
+            part, store = attend(sizes, jobs, lists[step], [came], kv_pages, None, keeping, store)
         else:
-            parts = attend(sizes, jobs, lists[step], came, kv_pages)
+            part, = attend(sizes, jobs, lists[step], [came], kv_pages)
         if step == 1:
-            blocks = [packed(part) for part in parts]
+            blocks = [packed(part)]
+        elif step < stores - 2:
+            blocks = [merged(after(partial[0], part), part, 0, 0, heads)]
         else:
-            if step == stores - 1:
-                parts = after(parts, arrived)
-            blocks = [merged(after(partial[side], parts), parts[side]) for side in sides]
-        partial = [onward(side, blocks[side]) for side in sides]
+            blocks = []
+            for n, half_heads in enumerate(halves):
+                block, at = (partial[0], half_heads[0]) if len(partial) == 1 else (partial[n], 0)
+                block = after(block, [part, blocks])
+                blocks.append(merged(block, part, at, half_heads[0], len(half_heads)))
+        partial = [onward(block) for block in blocks]
         token = blocks
-        if step == half:
-            own += attend_own(1, token)
+        if step == stores - 2:
+            token = [blocks, arrived]
+        if step in (half - 1, half):
+            if own_queries is None:
+                own_queries = joined(after(queries, token), mine)
+            jobs = [(0, n, h) for n, h in enumerate(halves[len(own)])]
+            x = after(own_queries, token)
+            own += attend(sizes, jobs, listed(mine, 0), [x], kv_pages, suffix_key_value[0])
             token = [blocks, own]
-        if step == stores - 2:
-            arrived = shifted(after(suffix_key_value, token), "store", half)
-    near = lists[stores // 4]
-    store = place_page(half, cap + 1, me[None], near, arrived, after(store, token))
+
+    quarter = stores // 4
+    near, far = lists[quarter], lists[stores - quarter]
+    core = lax.axis_index("tensor")
+    store = place_page(half, cap + 1, me, core, near, far, arrived, after(store, token))
     attended = finish(suffix, 0, queries, after(partial[0], store), own[0])
-    attended = finish(suffix, heads, queries, partial[1], own[1], attended)
+    attended = finish(suffix, heads // 2, queries, partial[1], own[1], attended)
     return (attended, store)
 
 
-def wire_of(part):
-    heads, rows, columns = part[0].shape
+def wire_of(part, heads):
+    rows, columns = part[0].shape[1:]
     return jax.ShapeDtypeStruct((heads, rows + STAT_ROWS, columns), jnp.bfloat16)
 
 
 def packed(part):
-    return call(pack_kernel, wire_of(part), *part)
-
-
-def merged(block, part):
-    return call(merge_kernel, wire_of(part), block, *part)
+    return call(pack_kernel, wire_of(part, part[0].shape[0]), *part)
+
+
+def merged(block, part, in_first, first, heads):
+    kernel = functools.partial(merge_kernel, in_first, first)
+    return call(kernel, wire_of(part, heads), block, *part)
 
 
 def on_device(queries, suffix_key_value, kv_pages, page_table, prefix_pages, new_slots):

time: 103 us -> 98.4 us (0.955)
  waiting for transfers between devices: 31.4 us -> 21.2 us
  starting transfers between devices: 31.7 us -> 38.5 us
  Pallas kernels: 32.3 us -> 31.1 us
    ppermute x1, waiting for transfers between devices: 7.96 us -> 0.27 us  [shifted(): return lax.ppermute(block, axis, route)]
    ppermute x28 -> x17, starting transfers between devices: 30.4 us -> 36 us  [onward(): return lax.ppermute(x, ('store', 'tensor'), route)]
    ppermute x28 -> x17, waiting for transfers between devices: 23.4 us -> 20.9 us  [onward(): return lax.ppermute(x, ('store', 'tensor'), route)]
    ppermute x1, starting transfers between devices: 1.38 us -> 2.53 us  [shifted(): return lax.ppermute(block, axis, route)]
    pallas_call x14 -> x11, Pallas kernels: 7.59 us -> 6.7 us  [call(): pl.pallas_call(kernel, out_shape=shape, in_specs=[VMEM] * len(args), out_...]
    unnamed x12 -> x14, local copies, waits for them, and re-layouts: 4.79 us -> 5.04 us
  transfers between devices with their start and end apart: 29 -> 18, of which waited for: 20 -> 13; matrix products, arithmetic and copies ran while one was open for 0% -> 0% of each run, Pallas kernels for 30% -> 30%
where the time goes in v14:
time: 98.4 us; the launch traced here: 98.2 us
  starting transfers between devices  38.5 us (39%)
  Pallas kernels  31.1 us (32%)
  waiting for transfers between devices  21.2 us (22%)
  local copies, waits for them, and re-layouts  5.04 us (5%)
  between operations  2.3 us (2%)
    ppermute x17, starting transfers between devices, onward(): return lax.ppermute(x, ('store', 'tensor'), route)  36 us
    ppermute x17, waiting for transfers between devices, onward(): return lax.ppermute(x, ('store', 'tensor'), route)  20.9 us
    pallas_call x9, Pallas kernels, attend(): pl.pallas_call(functools.partial(attend_kernel, sizes + (count,), jobs, o...  20.3 us
    pallas_call x11, Pallas kernels, call(): pl.pallas_call(kernel, out_shape=shape, in_specs=[VMEM] * len(args), out_...  6.7 us
    unnamed x14, local copies, waits for them, and re-layouts  5.04 us
    ppermute x1, starting transfers between devices, shifted(): return lax.ppermute(block, axis, route)  2.53 us
    pallas_call x2, Pallas kernels, finish(): pl.pallas_call(functools.partial(final_kernel, suffix, first), out_shape=...  2.53 us
  transfers between devices with their start and end apart: 18, of which 13 were waited for; matrix products, arithmetic and copies ran while one was open for 0% of the time, Pallas kernels for 30%

profile of v14, /device:TPU:0, one launch (start us, length us, event | category | flops | bytes accessed | tf_op | source)
XLA Modules:
  0.0 98.2 jit_solution(14696269945134847716)
XLA Ops:
  0.6 3.1 %collective-permute-start = (bf16[1,64,4096]{2,1,0:T(8,128)(2,1)}, bf16[1,64,4096]{2,1,0:T(8,128)(2,1)S(1)}, u32[]{:S(2)}, u32[]{:S(2)}) collective-permute-start(bf16[1,64,4096]{2,1,0:T(8,128)(2,1)} %q_ref), channel_id=1, source_target_pairs={{0,4},{4,8},{8,12},{12,14},{14,10},{10,6},{6,2},{2,0},{1,3},{5,1},... | collective-permute-start | bytes 1572872 | tf_op jit(solution)/shard_map/ppermute | solution.py:446
  5.0 0.6 copy-done.6
  5.7 0.3 shard_map.77.lists_ref
  5.9 1.6 %collective-permute-start.1 = (bf16[16,128]{1,0:T(8,128)(2,1)S(1)}, bf16[16,128]{1,0:T(8,128)(2,1)S(1)}, u32[]{:S(2)}, u32[]{:S(2)}) collective-permute-start(bf16[16,128]{1,0:T(8,128)(2,1)S(1)} %shard_map.77.lists_ref), channel_id=1, source_target_pairs={{0,4},{4,8},{8,12},{12,14},{14,10},{10,6},{6,2},{2,0},{1,3},{5,1},... | collective-permute-start | bytes 12296 | tf_op jit(solution)/shard_map/ppermute | solution.py:446
  7.5 3.5 %collective-permute-done.1.lists_ref = bf16[16,128]{1,0:T(8,128)(2,1)S(1)} collective-permute-done((bf16[16,128]{1,0:T(8,128)(2,1)S(1)}, bf16[16,128]{1,0:T(8,128)(2,1)S(1)}, u32[]{:S(2)}, u32[]{:S(2)}) %collective-permute-start.1) | collective-permute-done | bytes 4128 | tf_op jit(solution)/shard_map/ppermute | solution.py:446
  11.1 0.0 collective-permute-done.q_ref
  11.1 0.1 shard_map.78.refs_1_
  11.2 2.1 %collective-permute-start.3 = (bf16[2064,128]{1,0:T(8,128)(2,1)S(1)}, bf16[2064,128]{1,0:T(8,128)(2,1)S(1)}, u32[]{:S(2)}, u32[]{:S(2)}) collective-permute-start(bf16[2064,128]{1,0:T(8,128)(2,1)S(1)} %shard_map.78.refs_1_), channel_id=1, source_target_pairs={{0,4},{4,8},{8,12},{12,14},{14,10},{10,6},{6,2},{2,0},{1,3},{5,1},... | collective-permute-start | bytes 1585160 | tf_op jit(solution)/shard_map/ppermute | solution.py:446
  13.3 2.2 %copy-done = bf16[32,2,64,512]{3,2,1,0:T(8,128)(2,1)S(1)} copy-done((bf16[32,2,64,512]{3,2,1,0:T(8,128)(2,1)S(1)}, bf16[32,2,64,512]{3,2,1,0:T(8,128)(2,1)}, u32[]{:S(2)}) %copy-start) | copy-done | bytes 4194328
  15.5 2.7 %shard_map.79 = (f32[4,512,128]{2,1,0:T(8,128)S(1)}, bf16[4,16,128]{2,1,0:T(8,128)(2,1)S(1)}, bf16[32,2,64,512]{3,2,1,0:T(8,128)(2,1)}) custom-call(s32[1,128]{1,0:T(1,128)S(1)} %fusion.refs_0_, bf16[2064,128]{1,0:T(8,128)(2,1)S(1)} %shard_map.78.refs_1_, bf16[32,2,64,512]{3,2,1,0:T(8,128)(2,1)S(1)} %copy-done), custom_call_target="tpu_custom_call" | custom-call | flops 1073741824 | bytes 2621440 | tf_op jit(solution)/shard_map/pallas_call | solution.py:253
  18.2 0.1 shard_map.80
  18.3 1.6 %collective-permute-start.2 = (bf16[4,528,128]{2,1,0:T(8,128)(2,1)S(1)}, bf16[4,528,128]{2,1,0:T(8,128)(2,1)S(1)}, u32[]{:S(2)}, u32[]{:S(2)}) collective-permute-start(bf16[4,528,128]{2,1,0:T(8,128)(2,1)S(1)} %shard_map.80), channel_id=1, source_target_pairs={{0,4},{4,8},{8,12},{12,14},{14,10},{10,6},{6,2},{2,0},{1,3},{5,1},... | collective-permute-start | bytes 1622024 | tf_op jit(solution)/shard_map/ppermute | solution.py:446
  19.9 0.5 collective-permute-done.3.refs_1_
  20.4 2.1 %collective-permute-start.5 = (bf16[2064,128]{1,0:T(8,128)(2,1)S(1)}, bf16[2064,128]{1,0:T(8,128)(2,1)S(1)}, u32[]{:S(2)}, u32[]{:S(2)}) collective-permute-start(bf16[2064,128]{1,0:T(8,128)(2,1)S(1)} %collective-permute-done.3.refs_1_), channel_id=1, source_target_pairs={{0,4},{4,8},{8,12},{12,14},{14,10},{10,6},{6,2},{2,0},{1,3},{5,1},... | collective-permute-start | bytes 1585160 | tf_op jit(solution)/shard_map/ppermute | solution.py:446
  22.5 2.9 %shard_map.81 = (f32[4,512,128]{2,1,0:T(8,128)S(1)}, bf16[4,16,128]{2,1,0:T(8,128)(2,1)S(1)}, bf16[32,2,64,512]{3,2,1,0:T(8,128)(2,1)}) custom-call(s32[1,128]{1,0:T(1,128)S(1)} %fusion.1.refs_0_.near_ref, bf16[2064,128]{1,0:T(8,128)(2,1)S(1)} %collective-permute-done.3.refs_1_, ...), custom_call_target="tpu_custom_call", output_to_operand_aliasing={{2}: (3, {})} | custom-call | flops 1073741824 | bytes 2621440 | tf_op jit(solution)/shard_map/pallas_call | solution.py:253
  25.5 2.2 %collective-permute-done.2.in_ref = bf16[4,528,128]{2,1,0:T(8,128)(2,1)S(1)} collective-permute-done((bf16[4,528,128]{2,1,0:T(8,128)(2,1)S(1)}, bf16[4,528,128]{2,1,0:T(8,128)(2,1)S(1)}, u32[]{:S(2)}, u32[]{:S(2)}) %collective-permute-start.2) | collective-permute-done | bytes 540704 | tf_op jit(solution)/shard_map/ppermute | solution.py:446
  27.7 1.0 %shard_map.82 = bf16[4,528,128]{2,1,0:T(8,128)(2,1)S(1)} custom-call(bf16[4,528,128]{2,1,0:T(8,128)(2,1)S(1)} %collective-permute-done.2.in_ref, f32[4,512,128]{2,1,0:T(8,128)S(1)} %get-tuple-element.46.acc_ref, bf16[4,16,128]{2,1,0:T(8,128)(2,1)S(1)} %get-tuple-element.47.stat_ref), custom_call_target="tpu_custom_call" | custom-call | flops 1605632 | bytes 3211264 | tf_op jit(solution)/shard_map/pallas_call | solution.py:373
  28.7 1.6 %collective-permute-start.4 = (bf16[4,528,128]{2,1,0:T(8,128)(2,1)S(1)}, bf16[4,528,128]{2,1,0:T(8,128)(2,1)S(1)}, u32[]{:S(2)}, u32[]{:S(2)}) collective-permute-start(bf16[4,528,128]{2,1,0:T(8,128)(2,1)S(1)} %shard_map.82), channel_id=1, source_target_pairs={{0,4},{4,8},{8,12},{12,14},{14,10},{10,6},{6,2},{2,0},{1,3},{5,1},... | collective-permute-start | bytes 1622024 | tf_op jit(solution)/shard_map/ppermute | solution.py:446
  30.3 3.0 %collective-permute-done.5.refs_1_ = bf16[2064,128]{1,0:T(8,128)(2,1)S(1)} collective-permute-done((bf16[2064,128]{1,0:T(8,128)(2,1)S(1)}, bf16[2064,128]{1,0:T(8,128)(2,1)S(1)}, u32[]{:S(2)}, u32[]{:S(2)}) %collective-permute-start.5) | collective-permute-done | bytes 528416 | tf_op jit(solution)/shard_map/ppermute | solution.py:446
  33.4 1.6 %collective-permute-start.7 = (bf16[2064,128]{1,0:T(8,128)(2,1)S(1)}, bf16[2064,128]{1,0:T(8,128)(2,1)S(1)}, u32[]{:S(2)}, u32[]{:S(2)}) collective-permute-start(bf16[2064,128]{1,0:T(8,128)(2,1)S(1)} %collective-permute-done.5.refs_1_), channel_id=1, source_target_pairs={{0,4},{4,8},{8,12},{12,14},{14,10},{10,6},{6,2},{2,0},{1,3},{5,1},... | collective-permute-start | bytes 1585160 | tf_op jit(solution)/shard_map/ppermute | solution.py:446
  35.0 2.2 %copy-done.2 = bf16[32,2,64,512]{3,2,1,0:T(8,128)(2,1)S(1)} copy-done((bf16[32,2,64,512]{3,2,1,0:T(8,128)(2,1)S(1)}, bf16[32,2,64,512]{3,2,1,0:T(8,128)(2,1)}, u32[]{:S(2)}) %copy-start.2) | copy-done | bytes 4194328
  37.1 2.2 %shard_map.83 = (f32[4,512,128]{2,1,0:T(8,128)S(1)}, bf16[4,16,128]{2,1,0:T(8,128)(2,1)S(1)}) custom-call(s32[1,128]{1,0:T(1,128)S(1)} %fusion.2.refs_0_, bf16[2064,128]{1,0:T(8,128)(2,1)S(1)} %collective-permute-done.5.refs_1_, bf16[32,2,64,512]{3,2,1,0:T(8,128)(2,1)S(1)} %copy-done.2), custom_call_target="tpu_custom_call" | custom-call | flops 1073741824 | bytes 2621440 | tf_op jit(solution)/shard_map/pallas_call | solution.py:253
  39.4 0.0 collective-permute-done.4.in_ref
  39.4 1.0 %shard_map.84 = bf16[4,528,128]{2,1,0:T(8,128)(2,1)S(1)} custom-call(bf16[4,528,128]{2,1,0:T(8,128)(2,1)S(1)} %collective-permute-done.4.in_ref, f32[4,512,128]{2,1,0:T(8,128)S(1)} %get-tuple-element.50.acc_ref, bf16[4,16,128]{2,1,0:T(8,128)(2,1)S(1)} %get-tuple-element.51.stat_ref), custom_call_target="tpu_custom_call" | custom-call | flops 1605632 | bytes 3211264 | tf_op jit(solution)/shard_map/pallas_call | solution.py:373
  40.4 1.6 %collective-permute-start.6 = (bf16[4,528,128]{2,1,0:T(8,128)(2,1)S(1)}, bf16[4,528,128]{2,1,0:T(8,128)(2,1)S(1)}, u32[]{:S(2)}, u32[]{:S(2)}) collective-permute-start(bf16[4,528,128]{2,1,0:T(8,128)(2,1)S(1)} %shard_map.84), channel_id=1, source_target_pairs={{0,4},{4,8},{8,12},{12,14},{14,10},{10,6},{6,2},{2,0},{1,3},{5,1},... | collective-permute-start | bytes 1622024 | tf_op jit(solution)/shard_map/ppermute | solution.py:446
  42.0 0.0 copy-done.5
  42.0 0.1 shard_map.85.refs_1_
  42.2 1.8 %shard_map.86 = (f32[2,512,128]{2,1,0:T(8,128)S(1)}, bf16[2,16,128]{2,1,0:T(8,128)(2,1)S(1)}) custom-call(s32[1,128]{1,0:T(1,128)S(1)} %fusion.3.refs_0_, bf16[2064,128]{1,0:T(8,128)(2,1)S(1)} %shard_map.85.refs_1_, bf16[2,64,512]{2,1,0:T(8,128)(2,1)S(1)} %bitcast.3, bf16[32,2,64,512]{3,2,1,0:T(8,128)(2,1)S(1)} %copy-done.3), custom_call_target="tpu_custom_call" | custom-call | flops 536870912 | bytes 1310720 | tf_op jit(solution)/shard_map/pallas_call | solution.py:253
  43.9 0.9 collective-permute-done.7.refs_1_
  44.8 1.6 %collective-permute-start.9 = (bf16[2064,128]{1,0:T(8,128)(2,1)S(1)}, bf16[2064,128]{1,0:T(8,128)(2,1)S(1)}, u32[]{:S(2)}, u32[]{:S(2)}) collective-permute-start(bf16[2064,128]{1,0:T(8,128)(2,1)S(1)} %collective-permute-done.7.refs_1_), channel_id=1, source_target_pairs={{0,4},{4,8},{8,12},{12,14},{14,10},{10,6},{6,2},{2,0},{1,3},{5,1},... | collective-permute-start | bytes 1585160 | tf_op jit(solution)/shard_map/ppermute | solution.py:446
  46.4 2.2 %shard_map.87 = (f32[4,512,128]{2,1,0:T(8,128)S(1)}, bf16[4,16,128]{2,1,0:T(8,128)(2,1)S(1)}) custom-call(s32[1,128]{1,0:T(1,128)S(1)} %fusion.4.refs_0_, bf16[2064,128]{1,0:T(8,128)(2,1)S(1)} %collective-permute-done.7.refs_1_, bf16[32,2,64,512]{3,2,1,0:T(8,128)(2,1)S(1)} %copy-done.3), custom_call_target="tpu_custom_call" | custom-call | flops 1073741824 | bytes 2621440 | tf_op jit(solution)/shard_map/pallas_call | solution.py:253
  48.6 2.0 %collective-permute-done.6.in_ref = bf16[4,528,128]{2,1,0:T(8,128)(2,1)S(1)} collective-permute-done((bf16[4,528,128]{2,1,0:T(8,128)(2,1)S(1)}, bf16[4,528,128]{2,1,0:T(8,128)(2,1)S(1)}, u32[]{:S(2)}, u32[]{:S(2)}) %collective-permute-start.6) | collective-permute-done | bytes 540704 | tf_op jit(solution)/shard_map/ppermute | solution.py:446
  50.6 1.0 %shard_map.88 = bf16[4,528,128]{2,1,0:T(8,128)(2,1)S(1)} custom-call(bf16[4,528,128]{2,1,0:T(8,128)(2,1)S(1)} %collective-permute-done.6.in_ref, f32[4,512,128]{2,1,0:T(8,128)S(1)} %get-tuple-element.58.acc_ref, bf16[4,16,128]{2,1,0:T(8,128)(2,1)S(1)} %get-tuple-element.59.stat_ref), custom_call_target="tpu_custom_call" | custom-call | flops 1605632 | bytes 3211264 | tf_op jit(solution)/shard_map/pallas_call | solution.py:373
  51.6 1.8 %collective-permute-start.8 = (bf16[4,528,128]{2,1,0:T(8,128)(2,1)S(1)}, bf16[4,528,128]{2,1,0:T(8,128)(2,1)S(1)}, u32[]{:S(2)}, u32[]{:S(2)}) collective-permute-start(bf16[4,528,128]{2,1,0:T(8,128)(2,1)S(1)} %shard_map.88), channel_id=1, source_target_pairs={{0,4},{4,8},{8,12},{12,14},{14,10},{10,6},{6,2},{2,0},{1,3},{5,1},... | collective-permute-start | bytes 1622024 | tf_op jit(solution)/shard_map/ppermute | solution.py:446
  53.4 1.8 %shard_map.89 = (f32[2,512,128]{2,1,0:T(8,128)S(1)}, bf16[2,16,128]{2,1,0:T(8,128)(2,1)S(1)}) custom-call(s32[1,128]{1,0:T(1,128)S(1)} %fusion.3.refs_0_, bf16[2064,128]{1,0:T(8,128)(2,1)S(1)} %shard_map.85.refs_1_, bf16[2,64,512]{2,1,0:T(8,128)(2,1)S(1)} %bitcast.4, bf16[32,2,64,512]{3,2,1,0:T(8,128)(2,1)S(1)} %copy-done.3), custom_call_target="tpu_custom_call" | custom-call | flops 536870912 | bytes 1310720 | tf_op jit(solution)/shard_map/pallas_call | solution.py:253
  55.2 1.1 %collective-permute-done.9.refs_1_ = bf16[2064,128]{1,0:T(8,128)(2,1)S(1)} collective-permute-done((bf16[2064,128]{1,0:T(8,128)(2,1)S(1)}, bf16[2064,128]{1,0:T(8,128)(2,1)S(1)}, u32[]{:S(2)}, u32[]{:S(2)}) %collective-permute-start.9) | collective-permute-done | bytes 528416 | tf_op jit(solution)/shard_map/ppermute | solution.py:446
  56.3 1.6 %collective-permute-start.11 = (bf16[2064,128]{1,0:T(8,128)(2,1)S(1)}, bf16[2064,128]{1,0:T(8,128)(2,1)S(1)}, u32[]{:S(2)}, u32[]{:S(2)}) collective-permute-start(bf16[2064,128]{1,0:T(8,128)(2,1)S(1)} %collective-permute-done.9.refs_1_), channel_id=1, source_target_pairs={{0,4},{4,8},{8,12},{12,14},{14,10},{10,6},{6,2},{2,0},{1,3},{5,1},... | collective-permute-start | bytes 1585160 | tf_op jit(solution)/shard_map/ppermute | solution.py:446
  57.9 2.2 %shard_map.90 = (f32[4,512,128]{2,1,0:T(8,128)S(1)}, bf16[4,16,128]{2,1,0:T(8,128)(2,1)S(1)}) custom-call(s32[1,128]{1,0:T(1,128)S(1)} %fusion.5.refs_0_, bf16[2064,128]{1,0:T(8,128)(2,1)S(1)} %collective-permute-done.9.refs_1_, bf16[32,2,64,512]{3,2,1,0:T(8,128)(2,1)S(1)} %copy-done.3), custom_call_target="tpu_custom_call" | custom-call | flops 1073741824 | bytes 2621440 | tf_op jit(solution)/shard_map/pallas_call | solution.py:253
  60.1 2.0 %collective-permute-done.8.in_ref = bf16[4,528,128]{2,1,0:T(8,128)(2,1)S(1)} collective-permute-done((bf16[4,528,128]{2,1,0:T(8,128)(2,1)S(1)}, bf16[4,528,128]{2,1,0:T(8,128)(2,1)S(1)}, u32[]{:S(2)}, u32[]{:S(2)}) %collective-permute-start.8) | collective-permute-done | bytes 540704 | tf_op jit(solution)/shard_map/ppermute | solution.py:446
  62.1 1.0 shard_map.91
  63.1 1.6 %collective-permute-start.10 = (bf16[4,528,128]{2,1,0:T(8,128)(2,1)S(1)}, bf16[4,528,128]{2,1,0:T(8,128)(2,1)S(1)}, u32[]{:S(2)}, u32[]{:S(2)}) collective-permute-start(bf16[4,528,128]{2,1,0:T(8,128)(2,1)S(1)} %shard_map.91), channel_id=1, source_target_pairs={{0,4},{4,8},{8,12},{12,14},{14,10},{10,6},{6,2},{2,0},{1,3},{5,1},... | collective-permute-start | bytes 1622024 | tf_op jit(solution)/shard_map/ppermute | solution.py:446
  64.7 3.0 %collective-permute-done.11.refs_1_ = bf16[2064,128]{1,0:T(8,128)(2,1)S(1)} collective-permute-done((bf16[2064,128]{1,0:T(8,128)(2,1)S(1)}, bf16[2064,128]{1,0:T(8,128)(2,1)S(1)}, u32[]{:S(2)}, u32[]{:S(2)}) %collective-permute-start.11) | collective-permute-done | bytes 528416 | tf_op jit(solution)/shard_map/ppermute | solution.py:446
  67.7 1.6 %collective-permute-start.13 = (bf16[2064,128]{1,0:T(8,128)(2,1)S(1)}, bf16[2064,128]{1,0:T(8,128)(2,1)S(1)}, u32[]{:S(2)}, u32[]{:S(2)}) collective-permute-start(bf16[2064,128]{1,0:T(8,128)(2,1)S(1)} %collective-permute-done.11.refs_1_), channel_id=1, source_target_pairs={{0,4},{4,8},{8,12},{12,14},{14,10},{10,6},{6,2},{2,0},{1,3},{5,1},... | collective-permute-start | bytes 1585160 | tf_op jit(solution)/shard_map/ppermute | solution.py:446
  69.3 2.5 %collective-permute-start.14 = (bf16[1,2,64,512]{3,2,1,0:T(8,128)(2,1)S(1)}, bf16[1,2,64,512]{3,2,1,0:T(8,128)(2,1)S(1)}, u32[]{:S(2)}, u32[]{:S(2)}) collective-permute-start(bf16[1,2,64,512]{3,2,1,0:T(8,128)(2,1)S(1)} %copy-done.4), channel_id=1, source_target_pairs={{8,0},{10,2},{12,4},{14,6},{0,8},{2,10},{4,12},{6,14},{9,1},{11,3}... | collective-permute-start | bytes 393224 | tf_op jit(solution)/shard_map/ppermute | solution.py:26
  71.9 2.2 %shard_map.92 = (f32[4,512,128]{2,1,0:T(8,128)S(1)}, bf16[4,16,128]{2,1,0:T(8,128)(2,1)S(1)}) custom-call(s32[1,128]{1,0:T(1,128)S(1)} %fusion.6.refs_0_.far_ref, bf16[2064,128]{1,0:T(8,128)(2,1)S(1)} %collective-permute-done.11.refs_1_, bf16[32,2,64,512]{3,2,1,0:T(8,128)(2,1)S(1)} %copy-done.3), custom_call_target="tpu_custom_call" | custom-call | flops 1073741824 | bytes 2621440 | tf_op jit(solution)/shard_map/pallas_call | solution.py:253
  74.1 0.0 collective-permute-done.10.in_ref
  74.1 0.6 shard_map.93
  74.7 3.0 %collective-permute-start.15 = (bf16[2,528,128]{2,1,0:T(8,128)(2,1)S(1)}, bf16[2,528,128]{2,1,0:T(8,128)(2,1)S(1)}, u32[]{:S(2)}, u32[]{:S(2)}) collective-permute-start(bf16[2,528,128]{2,1,0:T(8,128)(2,1)S(1)} %shard_map.93), channel_id=1, source_target_pairs={{0,4},{4,8},{8,12},{12,14},{14,10},{10,6},{6,2},{2,0},{1,3},{5,1},... | collective-permute-start | bytes 811016 | tf_op jit(solution)/shard_map/ppermute | solution.py:446
  77.7 0.6 shard_map.94
  78.3 2.5 %collective-permute-start.12 = (bf16[2,528,128]{2,1,0:T(8,128)(2,1)S(1)}, bf16[2,528,128]{2,1,0:T(8,128)(2,1)S(1)}, u32[]{:S(2)}, u32[]{:S(2)}) collective-permute-start(bf16[2,528,128]{2,1,0:T(8,128)(2,1)S(1)} %shard_map.94), channel_id=1, source_target_pairs={{0,4},{4,8},{8,12},{12,14},{14,10},{10,6},{6,2},{2,0},{1,3},{5,1},... | collective-permute-start | bytes 811016 | tf_op jit(solution)/shard_map/ppermute | solution.py:446
  80.9 0.3 collective-permute-done.14.page_ref
  81.1 0.0 collective-permute-done.13.refs_1_
  81.2 2.2 %shard_map.95 = (f32[4,512,128]{2,1,0:T(8,128)S(1)}, bf16[4,16,128]{2,1,0:T(8,128)(2,1)S(1)}) custom-call(s32[1,128]{1,0:T(1,128)S(1)} %fusion.7.refs_0_, bf16[2064,128]{1,0:T(8,128)(2,1)S(1)} %collective-permute-done.13.refs_1_, bf16[32,2,64,512]{3,2,1,0:T(8,128)(2,1)S(1)} %copy-done.3), custom_call_target="tpu_custom_call" | custom-call | flops 1073741824 | bytes 2621440 | tf_op jit(solution)/shard_map/pallas_call | solution.py:253
  83.4 0.6 collective-permute-done.15.in_ref
  84.0 0.6 shard_map.96
  84.7 4.4 %collective-permute-start.17 = (bf16[2,528,128]{2,1,0:T(8,128)(2,1)S(1)}, bf16[2,528,128]{2,1,0:T(8,128)(2,1)S(1)}, u32[]{:S(2)}, u32[]{:S(2)}) collective-permute-start(bf16[2,528,128]{2,1,0:T(8,128)(2,1)S(1)} %shard_map.96), channel_id=1, source_target_pairs={{0,4},{4,8},{8,12},{12,14},{14,10},{10,6},{6,2},{2,0},{1,3},{5,1},... | collective-permute-start | bytes 811016 | tf_op jit(solution)/shard_map/ppermute | solution.py:446
  89.1 0.0 collective-permute-done.12.in_ref
  89.1 0.6 shard_map.97
  89.8 2.5 %collective-permute-start.16 = (bf16[2,528,128]{2,1,0:T(8,128)(2,1)S(1)}, bf16[2,528,128]{2,1,0:T(8,128)(2,1)S(1)}, u32[]{:S(2)}, u32[]{:S(2)}) collective-permute-start(bf16[2,528,128]{2,1,0:T(8,128)(2,1)S(1)} %shard_map.97), channel_id=1, source_target_pairs={{0,4},{4,8},{8,12},{12,14},{14,10},{10,6},{6,2},{2,0},{1,3},{5,1},... | collective-permute-start | bytes 811016 | tf_op jit(solution)/shard_map/ppermute | solution.py:446
  92.3 1.2 %shard_map.98 = bf16[32,2,64,512]{3,2,1,0:T(8,128)(2,1)} custom-call(s32[1]{0:T(128)} %bitcast.1.me_ref, s32[1]{0:T(128)} %bitcast.2.core_ref, s32[1,128]{1,0:T(1,128)S(1)} %fusion.1.refs_0_.near_ref, s32[1,128]{1,0:T(1,128)S(1)} %fusion.6.refs_0_.far_ref, ...), custom_call_target="tpu_custom_call", output_to_operand_aliasing={{}: (5, {})} | custom-call | flops 1 | bytes 1 | tf_op jit(solution)/shard_map/pallas_call | solution.py:276
  93.5 0.4 collective-permute-done.17.in_ref
  93.9 1.3 %shard_map.99.refs_0_ = bf16[1,64,4096]{2,1,0:T(8,128)(2,1)} custom-call(bf16[2,528,128]{2,1,0:T(8,128)(2,1)S(1)} %collective-permute-done.17.in_ref, f32[2,512,128]{2,1,0:T(8,128)S(1)} %get-tuple-element.55.acc_ref, bf16[2,16,128]{2,1,0:T(8,128)(2,1)S(1)} %get-tuple-element.56.stat_ref), custom_call_target="tpu_custom_call" | custom-call | tf_op jit(solution)/shard_map/pallas_call | solution.py:357
  95.1 1.6 %collective-permute-done.16.in_ref = bf16[2,528,128]{2,1,0:T(8,128)(2,1)S(1)} collective-permute-done((bf16[2,528,128]{2,1,0:T(8,128)(2,1)S(1)}, bf16[2,528,128]{2,1,0:T(8,128)(2,1)S(1)}, u32[]{:S(2)}, u32[]{:S(2)}) %collective-permute-start.16) | collective-permute-done | bytes 270368 | tf_op jit(solution)/shard_map/ppermute | solution.py:446
  96.8 1.3 %shard_map.100 = bf16[1,64,4096]{2,1,0:T(8,128)(2,1)} custom-call(bf16[2,528,128]{2,1,0:T(8,128)(2,1)S(1)} %collective-permute-done.16.in_ref, f32[2,512,128]{2,1,0:T(8,128)S(1)} %get-tuple-element.62.acc_ref, bf16[2,16,128]{2,1,0:T(8,128)(2,1)S(1)} %get-tuple-element.63.stat_ref, bf16[1,64,4096]{2,1,0:T(8,128)(2,1)} %shard_map.99.refs_0_), custom_call_target="tpu_custom_call", output_to_operand_aliasing={{}: (3, {})} | custom-call | tf_op jit(solution)/shard_map/pallas_call | solution.py:357
  (18 shorter events, 0.1 us)
Async XLA Ops:
  0.6 10.4 %collective-permute-start = (bf16[1,64,4096]{2,1,0:T(8,128)(2,1)}, bf16[1,64,4096]{2,1,0:T(8,128)(2,1)S(1)}, u32[]{:S(2)}, u32[]{:S(2)}) collective-permute-start(bf16[1,64,4096]{2,1,0:T(8,128)(2,1)} %q_ref), channel_id=1, source_target_pairs={{0,4},{4,8},{8,12},{12,14},{14,10},{10,6},{6,2},{2,0},{1,3},{5,1},... | collective-permute-start | bytes 1572872 | tf_op jit(solution)/shard_map/ppermute | solution.py:446
  5.0 0.7 copy-start.6
  5.9 5.1 %collective-permute-start.1 = (bf16[16,128]{1,0:T(8,128)(2,1)S(1)}, bf16[16,128]{1,0:T(8,128)(2,1)S(1)}, u32[]{:S(2)}, u32[]{:S(2)}) collective-permute-start(bf16[16,128]{1,0:T(8,128)(2,1)S(1)} %shard_map.77.lists_ref), channel_id=1, source_target_pairs={{0,4},{4,8},{8,12},{12,14},{14,10},{10,6},{6,2},{2,0},{1,3},{5,1},... | collective-permute-start | bytes 12296 | tf_op jit(solution)/shard_map/ppermute | solution.py:446
  11.2 9.3 %collective-permute-start.3 = (bf16[2064,128]{1,0:T(8,128)(2,1)S(1)}, bf16[2064,128]{1,0:T(8,128)(2,1)S(1)}, u32[]{:S(2)}, u32[]{:S(2)}) collective-permute-start(bf16[2064,128]{1,0:T(8,128)(2,1)S(1)} %shard_map.78.refs_1_), channel_id=1, source_target_pairs={{0,4},{4,8},{8,12},{12,14},{14,10},{10,6},{6,2},{2,0},{1,3},{5,1},... | collective-permute-start | bytes 1585160 | tf_op jit(solution)/shard_map/ppermute | solution.py:446
  13.3 2.2 %copy-start = (bf16[32,2,64,512]{3,2,1,0:T(8,128)(2,1)S(1)}, bf16[32,2,64,512]{3,2,1,0:T(8,128)(2,1)}, u32[]{:S(2)}) copy-start(bf16[32,2,64,512]{3,2,1,0:T(8,128)(2,1)} %refs_2_.13) | copy-start | bytes 12582916
  15.5 7.0 %copy-start.1 = (bf16[32,2,64,512]{3,2,1,0:T(8,128)(2,1)S(1)}, bf16[32,2,64,512]{3,2,1,0:T(8,128)(2,1)}, u32[]{:S(2)}) copy-start(bf16[32,2,64,512]{3,2,1,0:T(8,128)(2,1)} %refs_2_.13) | copy-start | bytes 12582916
  18.3 9.4 %collective-permute-start.2 = (bf16[4,528,128]{2,1,0:T(8,128)(2,1)S(1)}, bf16[4,528,128]{2,1,0:T(8,128)(2,1)S(1)}, u32[]{:S(2)}, u32[]{:S(2)}) collective-permute-start(bf16[4,528,128]{2,1,0:T(8,128)(2,1)S(1)} %shard_map.80), channel_id=1, source_target_pairs={{0,4},{4,8},{8,12},{12,14},{14,10},{10,6},{6,2},{2,0},{1,3},{5,1},... | collective-permute-start | bytes 1622024 | tf_op jit(solution)/shard_map/ppermute | solution.py:446
  20.4 12.9 %collective-permute-start.5 = (bf16[2064,128]{1,0:T(8,128)(2,1)S(1)}, bf16[2064,128]{1,0:T(8,128)(2,1)S(1)}, u32[]{:S(2)}, u32[]{:S(2)}) collective-permute-start(bf16[2064,128]{1,0:T(8,128)(2,1)S(1)} %collective-permute-done.3.refs_1_), channel_id=1, source_target_pairs={{0,4},{4,8},{8,12},{12,14},{14,10},{10,6},{6,2},{2,0},{1,3},{5,1},... | collective-permute-start | bytes 1585160 | tf_op jit(solution)/shard_map/ppermute | solution.py:446
  27.7 14.3 %copy-start.5 = (bf16[1,64,4096]{2,1,0:T(8,128)(2,1)S(1)}, bf16[1,64,4096]{2,1,0:T(8,128)(2,1)}, u32[]{:S(2)}) copy-start(bf16[1,64,4096]{2,1,0:T(8,128)(2,1)} %q_ref) | copy-start | bytes 1572868
  27.7 14.4 %copy-start.4 = (bf16[1,2,64,512]{3,2,1,0:T(8,128)(2,1)S(1)}, bf16[1,2,64,512]{3,2,1,0:T(8,128)(2,1)}, u32[]{:S(2)}) copy-start(bf16[1,2,64,512]{3,2,1,0:T(8,128)(2,1)} %param.7) | copy-start | bytes 393220
  28.7 10.7 %collective-permute-start.4 = (bf16[4,528,128]{2,1,0:T(8,128)(2,1)S(1)}, bf16[4,528,128]{2,1,0:T(8,128)(2,1)S(1)}, u32[]{:S(2)}, u32[]{:S(2)}) collective-permute-start(bf16[4,528,128]{2,1,0:T(8,128)(2,1)S(1)} %shard_map.82), channel_id=1, source_target_pairs={{0,4},{4,8},{8,12},{12,14},{14,10},{10,6},{6,2},{2,0},{1,3},{5,1},... | collective-permute-start | bytes 1622024 | tf_op jit(solution)/shard_map/ppermute | solution.py:446
  33.4 11.5 %collective-permute-start.7 = (bf16[2064,128]{1,0:T(8,128)(2,1)S(1)}, bf16[2064,128]{1,0:T(8,128)(2,1)S(1)}, u32[]{:S(2)}, u32[]{:S(2)}) collective-permute-start(bf16[2064,128]{1,0:T(8,128)(2,1)S(1)} %collective-permute-done.5.refs_1_), channel_id=1, source_target_pairs={{0,4},{4,8},{8,12},{12,14},{14,10},{10,6},{6,2},{2,0},{1,3},{5,1},... | collective-permute-start | bytes 1585160 | tf_op jit(solution)/shard_map/ppermute | solution.py:446
  35.0 2.2 %copy-start.2 = (bf16[32,2,64,512]{3,2,1,0:T(8,128)(2,1)S(1)}, bf16[32,2,64,512]{3,2,1,0:T(8,128)(2,1)}, u32[]{:S(2)}) copy-start(bf16[32,2,64,512]{3,2,1,0:T(8,128)(2,1)} %refs_2_.13) | copy-start | bytes 12582916
  37.1 5.0 %copy-start.3 = (bf16[32,2,64,512]{3,2,1,0:T(8,128)(2,1)S(1)}, bf16[32,2,64,512]{3,2,1,0:T(8,128)(2,1)}, u32[]{:S(2)}) copy-start(bf16[32,2,64,512]{3,2,1,0:T(8,128)(2,1)} %refs_2_.13) | copy-start | bytes 12582916
  40.4 10.2 %collective-permute-start.6 = (bf16[4,528,128]{2,1,0:T(8,128)(2,1)S(1)}, bf16[4,528,128]{2,1,0:T(8,128)(2,1)S(1)}, u32[]{:S(2)}, u32[]{:S(2)}) collective-permute-start(bf16[4,528,128]{2,1,0:T(8,128)(2,1)S(1)} %shard_map.84), channel_id=1, source_target_pairs={{0,4},{4,8},{8,12},{12,14},{14,10},{10,6},{6,2},{2,0},{1,3},{5,1},... | collective-permute-start | bytes 1622024 | tf_op jit(solution)/shard_map/ppermute | solution.py:446
  44.8 11.5 %collective-permute-start.9 = (bf16[2064,128]{1,0:T(8,128)(2,1)S(1)}, bf16[2064,128]{1,0:T(8,128)(2,1)S(1)}, u32[]{:S(2)}, u32[]{:S(2)}) collective-permute-start(bf16[2064,128]{1,0:T(8,128)(2,1)S(1)} %collective-permute-done.7.refs_1_), channel_id=1, source_target_pairs={{0,4},{4,8},{8,12},{12,14},{14,10},{10,6},{6,2},{2,0},{1,3},{5,1},... | collective-permute-start | bytes 1585160 | tf_op jit(solution)/shard_map/ppermute | solution.py:446
  51.6 10.5 %collective-permute-start.8 = (bf16[4,528,128]{2,1,0:T(8,128)(2,1)S(1)}, bf16[4,528,128]{2,1,0:T(8,128)(2,1)S(1)}, u32[]{:S(2)}, u32[]{:S(2)}) collective-permute-start(bf16[4,528,128]{2,1,0:T(8,128)(2,1)S(1)} %shard_map.88), channel_id=1, source_target_pairs={{0,4},{4,8},{8,12},{12,14},{14,10},{10,6},{6,2},{2,0},{1,3},{5,1},... | collective-permute-start | bytes 1622024 | tf_op jit(solution)/shard_map/ppermute | solution.py:446
  56.3 11.5 %collective-permute-start.11 = (bf16[2064,128]{1,0:T(8,128)(2,1)S(1)}, bf16[2064,128]{1,0:T(8,128)(2,1)S(1)}, u32[]{:S(2)}, u32[]{:S(2)}) collective-permute-start(bf16[2064,128]{1,0:T(8,128)(2,1)S(1)} %collective-permute-done.9.refs_1_), channel_id=1, source_target_pairs={{0,4},{4,8},{8,12},{12,14},{14,10},{10,6},{6,2},{2,0},{1,3},{5,1},... | collective-permute-start | bytes 1585160 | tf_op jit(solution)/shard_map/ppermute | solution.py:446
  63.1 11.0 %collective-permute-start.10 = (bf16[4,528,128]{2,1,0:T(8,128)(2,1)S(1)}, bf16[4,528,128]{2,1,0:T(8,128)(2,1)S(1)}, u32[]{:S(2)}, u32[]{:S(2)}) collective-permute-start(bf16[4,528,128]{2,1,0:T(8,128)(2,1)S(1)} %shard_map.91), channel_id=1, source_target_pairs={{0,4},{4,8},{8,12},{12,14},{14,10},{10,6},{6,2},{2,0},{1,3},{5,1},... | collective-permute-start | bytes 1622024 | tf_op jit(solution)/shard_map/ppermute | solution.py:446
  67.7 13.4 %collective-permute-start.13 = (bf16[2064,128]{1,0:T(8,128)(2,1)S(1)}, bf16[2064,128]{1,0:T(8,128)(2,1)S(1)}, u32[]{:S(2)}, u32[]{:S(2)}) collective-permute-start(bf16[2064,128]{1,0:T(8,128)(2,1)S(1)} %collective-permute-done.11.refs_1_), channel_id=1, source_target_pairs={{0,4},{4,8},{8,12},{12,14},{14,10},{10,6},{6,2},{2,0},{1,3},{5,1},... | collective-permute-start | bytes 1585160 | tf_op jit(solution)/shard_map/ppermute | solution.py:446
  69.3 11.8 %collective-permute-start.14 = (bf16[1,2,64,512]{3,2,1,0:T(8,128)(2,1)S(1)}, bf16[1,2,64,512]{3,2,1,0:T(8,128)(2,1)S(1)}, u32[]{:S(2)}, u32[]{:S(2)}) collective-permute-start(bf16[1,2,64,512]{3,2,1,0:T(8,128)(2,1)S(1)} %copy-done.4), channel_id=1, source_target_pairs={{8,0},{10,2},{12,4},{14,6},{0,8},{2,10},{4,12},{6,14},{9,1},{11,3}... | collective-permute-start | bytes 393224 | tf_op jit(solution)/shard_map/ppermute | solution.py:26
  74.7 9.3 %collective-permute-start.15 = (bf16[2,528,128]{2,1,0:T(8,128)(2,1)S(1)}, bf16[2,528,128]{2,1,0:T(8,128)(2,1)S(1)}, u32[]{:S(2)}, u32[]{:S(2)}) collective-permute-start(bf16[2,528,128]{2,1,0:T(8,128)(2,1)S(1)} %shard_map.93), channel_id=1, source_target_pairs={{0,4},{4,8},{8,12},{12,14},{14,10},{10,6},{6,2},{2,0},{1,3},{5,1},... | collective-permute-start | bytes 811016 | tf_op jit(solution)/shard_map/ppermute | solution.py:446
  78.3 10.8 %collective-permute-start.12 = (bf16[2,528,128]{2,1,0:T(8,128)(2,1)S(1)}, bf16[2,528,128]{2,1,0:T(8,128)(2,1)S(1)}, u32[]{:S(2)}, u32[]{:S(2)}) collective-permute-start(bf16[2,528,128]{2,1,0:T(8,128)(2,1)S(1)} %shard_map.94), channel_id=1, source_target_pairs={{0,4},{4,8},{8,12},{12,14},{14,10},{10,6},{6,2},{2,0},{1,3},{5,1},... | collective-permute-start | bytes 811016 | tf_op jit(solution)/shard_map/ppermute | solution.py:446
  84.7 9.2 %collective-permute-start.17 = (bf16[2,528,128]{2,1,0:T(8,128)(2,1)S(1)}, bf16[2,528,128]{2,1,0:T(8,128)(2,1)S(1)}, u32[]{:S(2)}, u32[]{:S(2)}) collective-permute-start(bf16[2,528,128]{2,1,0:T(8,128)(2,1)S(1)} %shard_map.96), channel_id=1, source_target_pairs={{0,4},{4,8},{8,12},{12,14},{14,10},{10,6},{6,2},{2,0},{1,3},{5,1},... | collective-permute-start | bytes 811016 | tf_op jit(solution)/shard_map/ppermute | solution.py:446
  89.8 7.0 %collective-permute-start.16 = (bf16[2,528,128]{2,1,0:T(8,128)(2,1)S(1)}, bf16[2,528,128]{2,1,0:T(8,128)(2,1)S(1)}, u32[]{:S(2)}, u32[]{:S(2)}) collective-permute-start(bf16[2,528,128]{2,1,0:T(8,128)(2,1)S(1)} %shard_map.97), channel_id=1, source_target_pairs={{0,4},{4,8},{8,12},{12,14},{14,10},{10,6},{6,2},{2,0},{1,3},{5,1},... | collective-permute-start | bytes 811016 | tf_op jit(solution)/shard_map/ppermute | solution.py:446

commit v15 on v14

--- a/solution.py
+++ b/solution.py
@@ -245,11 +245,6 @@
         aliases[len(args)] = 2 * count
         args.append(store)
         in_specs.append(HBM)
-    work = pl.CostEstimate(
-        flops=len(jobs) * rows * keys * HEAD_SIZE * 8,
-        bytes_accessed=len(jobs) * (rows * 6 + keys * 4) * HEAD_SIZE,
-        transcendentals=len(jobs) * rows * keys,
-    )
     out = pl.pallas_call(
         functools.partial(attend_kernel, sizes + (count,), jobs, own is not None, keeping),
         out_shape=shapes,
@@ -258,9 +253,31 @@
         scratch_shapes=scratch,
         input_output_aliases=aliases,
         compiler_params=pltpu.CompilerParams(vmem_limit_bytes=GRANT),
-        cost_estimate=work,
+        cost_estimate=pl.CostEstimate(
+            flops=len(jobs) * rows * keys * HEAD_SIZE * 8,
+            bytes_accessed=len(jobs) * (rows * 6 + keys * 4) * HEAD_SIZE,
+            transcendentals=len(jobs) * rows * keys,
+        ),
     )(*args)
     return [(out[2 * n], out[2 * n + 1]) for n in range(count)] + list(out[2 * count:])
+
+
+def hold_kernel(pages_ref, before_ref, out_ref, sem):
+    copy = pltpu.make_async_copy(pages_ref, out_ref, sem)
+    copy.start()
+    copy.wait()
+
+
+def hold(pages, before):
+    return pl.pallas_call(
+        hold_kernel,
+        out_shape=jax.ShapeDtypeStruct(pages.shape, pages.dtype),
+        in_specs=[HBM, VMEM],
+        out_specs=VMEM,
+        scratch_shapes=[pltpu.SemaphoreType.DMA],
+        compiler_params=pltpu.CompilerParams(vmem_limit_bytes=48 * 1024 * 1024),
+        cost_estimate=LIGHT,
+    )(pages, before)
 
 
 def place_kernel(half, column, me_ref, core_ref, near_ref, far_ref, page_ref, old_ref, out_ref, sem):
@@ -458,7 +475,8 @@
 
     first = onward(queries)
     mine = list_pages(cap, pages_dev, page_table, prefix_pages, new_slots)
-    moving = joined(first, onward(mine))
+    held = hold(kv_pages, mine)
+    moving = joined(after(first, held), onward(mine))
 
     own_queries = None
     halves = [range(0, heads // 2), range(heads // 2, heads)]
@@ -469,23 +487,24 @@
         if step < stores - 1:
             moving = onward(came)
         lists[step] = listed(came, heads * rows)
-        if step == stores - 3:
+        if step == stores - 2:
             arrived = shifted(after(suffix_key_value, token), "store", half)
         jobs = [(0, h, h) for h in range(heads)]
         keeping, pages = None, pages_dev // 2
         if step == 1:
             keeping = (0, pages)
-            part, store = attend(sizes, jobs, lists[step], [came], kv_pages, None, keeping)
+            part, store = attend(sizes, jobs, lists[step], [came], held, None, keeping)
         elif step == 2:
             keeping = (pages, pages_dev - pages)
-            part, store = attend(sizes, jobs, lists[step], [came], kv_pages, None, keeping, store)
+            part, store = attend(sizes, jobs, lists[step], [came], held, None, keeping, store)
         else:
-            part, = attend(sizes, jobs, lists[step], [came], kv_pages)
+            part, = attend(sizes, jobs, lists[step], [came], held)
         if step == 1:
             blocks = [packed(part)]
-        elif step < stores - 2:
+        elif step < stores - 1:
             blocks = [merged(after(partial[0], part), part, 0, 0, heads)]
         else:
+            part = after(part, arrived) if step == stores - 1 else part
             blocks = []
             for n, half_heads in enumerate(halves):
                 block, at = (partial[0], half_heads[0]) if len(partial) == 1 else (partial[n], 0)
@@ -493,14 +512,12 @@
                 blocks.append(merged(block, part, at, half_heads[0], len(half_heads)))
         partial = [onward(block) for block in blocks]
         token = blocks
-        if step == stores - 2:
-            token = [blocks, arrived]
         if step in (half - 1, half):
             if own_queries is None:
                 own_queries = joined(after(queries, token), mine)
             jobs = [(0, n, h) for n, h in enumerate(halves[len(own)])]
             x = after(own_queries, token)
-            own += attend(sizes, jobs, listed(mine, 0), [x], kv_pages, suffix_key_value[0])
+            own += attend(sizes, jobs, listed(mine, 0), [x], held, suffix_key_value[0])
             token = [blocks, own]
 
     quarter = stores // 4

time: 98.4 us -> 102 us (1.037)
  starting transfers between devices: 38.5 us -> 31.5 us
  waiting for transfers between devices: 21.2 us -> 27.7 us
  local copies, waits for them, and re-layouts: 5.04 us -> 6.99 us
  Pallas kernels: 31.1 us -> 33 us
    ppermute x17 -> x16, starting transfers between devices: 36 us -> 29 us  [onward(): return lax.ppermute(x, ('store', 'tensor'), route)]
    ppermute x1, waiting for transfers between devices: 0.27 us -> 5.01 us  [shifted(): return lax.ppermute(block, axis, route)]
    pallas_call x0 -> x1, Pallas kernels: none -> 2.2 us  [hold(): pl.pallas_call(hold_kernel, out_shape=jax.ShapeDtypeStruct(pages.shape, p...]
    unnamed x14 -> x16, local copies, waits for them, and re-layouts: 5.04 us -> 6.99 us
    ppermute x17 -> x16, waiting for transfers between devices: 20.9 us -> 22.7 us  [onward(): return lax.ppermute(x, ('store', 'tensor'), route)]
    pallas_call x11 -> x10, Pallas kernels: 6.7 us -> 6.41 us  [call(): pl.pallas_call(kernel, out_shape=shape, in_specs=[VMEM] * len(args), out_...]
  transfers between devices with their start and end apart: 18 -> 17, of which waited for: 13 -> 13; matrix products, arithmetic and copies ran while one was open for 0% -> 0% of each run, Pallas kernels for 30% -> 31%
where the time goes in v15:
time: 102 us
  Pallas kernels  33 us (32%)
  starting transfers between devices  31.5 us (31%)
  waiting for transfers between devices  27.7 us (27%)
  local copies, waits for them, and re-layouts  6.99 us (7%)
  between operations  2.32 us (2%)
    ppermute x16, starting transfers between devices, onward(): return lax.ppermute(x, ('store', 'tensor'), route)  29 us
    ppermute x16, waiting for transfers between devices, onward(): return lax.ppermute(x, ('store', 'tensor'), route)  22.7 us
    pallas_call x9, Pallas kernels, attend(): pl.pallas_call(functools.partial(attend_kernel, sizes + (count,), jobs, o...  20.4 us
    unnamed x16, local copies, waits for them, and re-layouts  6.99 us
    pallas_call x10, Pallas kernels, call(): pl.pallas_call(kernel, out_shape=shape, in_specs=[VMEM] * len(args), out_...  6.41 us
    ppermute x1, waiting for transfers between devices, shifted(): return lax.ppermute(block, axis, route)  5.01 us
    pallas_call x2, Pallas kernels, finish(): pl.pallas_call(functools.partial(final_kernel, suffix, first), out_shape=...  2.53 us
    ppermute x1, starting transfers between devices, shifted(): return lax.ppermute(block, axis, route)  2.45 us
  transfers between devices with their start and end apart: 17, of which 13 were waited for; matrix products, arithmetic and copies ran while one was open for 0% of the time, Pallas kernels for 31%

profile of v15, /device:TPU:0, one launch (start us, length us, event | category | flops | bytes accessed | tf_op | source)
XLA Modules:
  0.0 101.6 jit_solution(3761506819842124005)
XLA Ops:
  0.6 3.1 %collective-permute-start = (bf16[1,64,4096]{2,1,0:T(8,128)(2,1)}, bf16[1,64,4096]{2,1,0:T(8,128)(2,1)S(1)}, u32[]{:S(2)}, u32[]{:S(2)}) collective-permute-start(bf16[1,64,4096]{2,1,0:T(8,128)(2,1)} %q_ref), channel_id=1, source_target_pairs={{0,4},{4,8},{8,12},{12,14},{14,10},{10,6},{6,2},{2,0},{1,3},{5,1},... | collective-permute-start | bytes 1572872 | tf_op jit(solution)/shard_map/ppermute | solution.py:463
  5.0 0.0 copy-start.7
  5.0 0.6 copy-done.7
  5.7 0.3 shard_map.77.before_ref.lists_ref
  5.9 1.6 %collective-permute-start.1 = (bf16[16,128]{1,0:T(8,128)(2,1)S(1)}, bf16[16,128]{1,0:T(8,128)(2,1)S(1)}, u32[]{:S(2)}, u32[]{:S(2)}) collective-permute-start(bf16[16,128]{1,0:T(8,128)(2,1)S(1)} %shard_map.77.before_ref.lists_ref), channel_id=1, source_target_pairs={{0,4},{4,8},{8,12},{12,14},{14,10},{10,6},{6,2},{2,0},{1,3},{5,1},... | collective-permute-start | bytes 12296 | tf_op jit(solution)/shard_map/ppermute | solution.py:463
  7.5 2.2 %shard_map.78.refs_2_.refs_3_ = bf16[32,2,64,512]{3,2,1,0:T(8,128)(2,1)S(1)} custom-call(bf16[32,2,64,512]{3,2,1,0:T(8,128)(2,1)} %pages_ref.1, bf16[16,128]{1,0:T(8,128)(2,1)S(1)} %shard_map.77.before_ref.lists_ref), custom_call_target="tpu_custom_call" | custom-call | flops 1 | bytes 1 | tf_op jit(solution)/shard_map/pallas_call | solution.py:272
  9.7 1.9 %copy-done = bf16[32,2,64,512]{3,2,1,0:T(8,128)(2,1)} copy-done((bf16[32,2,64,512]{3,2,1,0:T(8,128)(2,1)}, bf16[32,2,64,512]{3,2,1,0:T(8,128)(2,1)S(1)}, u32[]{:S(2)}) %copy-start) | copy-done | bytes 4194328
  11.7 0.0 collective-permute-done.q_ref
  11.7 0.0 collective-permute-done.1.lists_ref
  11.7 0.1 shard_map.79.refs_1_
  11.8 1.6 %collective-permute-start.3 = (bf16[2064,128]{1,0:T(8,128)(2,1)S(1)}, bf16[2064,128]{1,0:T(8,128)(2,1)S(1)}, u32[]{:S(2)}, u32[]{:S(2)}) collective-permute-start(bf16[2064,128]{1,0:T(8,128)(2,1)S(1)} %shard_map.79.refs_1_), channel_id=1, source_target_pairs={{0,4},{4,8},{8,12},{12,14},{14,10},{10,6},{6,2},{2,0},{1,3},{5,1},... | collective-permute-start | bytes 1585160 | tf_op jit(solution)/shard_map/ppermute | solution.py:463
  13.4 2.2 %copy-done.1 = bf16[32,2,64,512]{3,2,1,0:T(8,128)(2,1)S(1)} copy-done((bf16[32,2,64,512]{3,2,1,0:T(8,128)(2,1)S(1)}, bf16[32,2,64,512]{3,2,1,0:T(8,128)(2,1)}, u32[]{:S(2)}) %copy-start.1) | copy-done | bytes 4194328
  15.6 2.8 %shard_map.80 = (f32[4,512,128]{2,1,0:T(8,128)S(1)}, bf16[4,16,128]{2,1,0:T(8,128)(2,1)S(1)}, bf16[32,2,64,512]{3,2,1,0:T(8,128)(2,1)}) custom-call(s32[1,128]{1,0:T(1,128)S(1)} %fusion.refs_0_, bf16[2064,128]{1,0:T(8,128)(2,1)S(1)} %shard_map.79.refs_1_, bf16[32,2,64,512]{3,2,1,0:T(8,128)(2,1)S(1)} %copy-done.1), custom_call_target="tpu_custom_call" | custom-call | flops 1073741824 | bytes 2621440 | tf_op jit(solution)/shard_map/pallas_call | solution.py:248
  18.4 0.1 shard_map.81
  18.5 1.6 %collective-permute-start.2 = (bf16[4,528,128]{2,1,0:T(8,128)(2,1)S(1)}, bf16[4,528,128]{2,1,0:T(8,128)(2,1)S(1)}, u32[]{:S(2)}, u32[]{:S(2)}) collective-permute-start(bf16[4,528,128]{2,1,0:T(8,128)(2,1)S(1)} %shard_map.81), channel_id=1, source_target_pairs={{0,4},{4,8},{8,12},{12,14},{14,10},{10,6},{6,2},{2,0},{1,3},{5,1},... | collective-permute-start | bytes 1622024 | tf_op jit(solution)/shard_map/ppermute | solution.py:463
  20.0 1.0 %collective-permute-done.3.refs_1_ = bf16[2064,128]{1,0:T(8,128)(2,1)S(1)} collective-permute-done((bf16[2064,128]{1,0:T(8,128)(2,1)S(1)}, bf16[2064,128]{1,0:T(8,128)(2,1)S(1)}, u32[]{:S(2)}, u32[]{:S(2)}) %collective-permute-start.3) | collective-permute-done | bytes 528416 | tf_op jit(solution)/shard_map/ppermute | solution.py:463
  21.1 1.6 %collective-permute-start.5 = (bf16[2064,128]{1,0:T(8,128)(2,1)S(1)}, bf16[2064,128]{1,0:T(8,128)(2,1)S(1)}, u32[]{:S(2)}, u32[]{:S(2)}) collective-permute-start(bf16[2064,128]{1,0:T(8,128)(2,1)S(1)} %collective-permute-done.3.refs_1_), channel_id=1, source_target_pairs={{0,4},{4,8},{8,12},{12,14},{14,10},{10,6},{6,2},{2,0},{1,3},{5,1},... | collective-permute-start | bytes 1585160 | tf_op jit(solution)/shard_map/ppermute | solution.py:463
  22.7 2.9 %shard_map.82 = (f32[4,512,128]{2,1,0:T(8,128)S(1)}, bf16[4,16,128]{2,1,0:T(8,128)(2,1)S(1)}, bf16[32,2,64,512]{3,2,1,0:T(8,128)(2,1)}) custom-call(s32[1,128]{1,0:T(1,128)S(1)} %fusion.1.refs_0_.near_ref, bf16[2064,128]{1,0:T(8,128)(2,1)S(1)} %collective-permute-done.3.refs_1_, ...), custom_call_target="tpu_custom_call", output_to_operand_aliasing={{2}: (3, {})} | custom-call | flops 1073741824 | bytes 2621440 | tf_op jit(solution)/shard_map/pallas_call | solution.py:248
  25.6 2.3 %collective-permute-done.2.in_ref = bf16[4,528,128]{2,1,0:T(8,128)(2,1)S(1)} collective-permute-done((bf16[4,528,128]{2,1,0:T(8,128)(2,1)S(1)}, bf16[4,528,128]{2,1,0:T(8,128)(2,1)S(1)}, u32[]{:S(2)}, u32[]{:S(2)}) %collective-permute-start.2) | collective-permute-done | bytes 540704 | tf_op jit(solution)/shard_map/ppermute | solution.py:463
  27.9 1.0 shard_map.83
  28.9 0.0 copy-start.5
  28.9 1.6 %collective-permute-start.4 = (bf16[4,528,128]{2,1,0:T(8,128)(2,1)S(1)}, bf16[4,528,128]{2,1,0:T(8,128)(2,1)S(1)}, u32[]{:S(2)}, u32[]{:S(2)}) collective-permute-start(bf16[4,528,128]{2,1,0:T(8,128)(2,1)S(1)} %shard_map.83), channel_id=1, source_target_pairs={{0,4},{4,8},{8,12},{12,14},{14,10},{10,6},{6,2},{2,0},{1,3},{5,1},... | collective-permute-start | bytes 1622024 | tf_op jit(solution)/shard_map/ppermute | solution.py:463
  30.4 3.1 %collective-permute-done.5.refs_1_ = bf16[2064,128]{1,0:T(8,128)(2,1)S(1)} collective-permute-done((bf16[2064,128]{1,0:T(8,128)(2,1)S(1)}, bf16[2064,128]{1,0:T(8,128)(2,1)S(1)}, u32[]{:S(2)}, u32[]{:S(2)}) %collective-permute-start.5) | collective-permute-done | bytes 528416 | tf_op jit(solution)/shard_map/ppermute | solution.py:463
  33.5 1.5 %collective-permute-start.7 = (bf16[2064,128]{1,0:T(8,128)(2,1)S(1)}, bf16[2064,128]{1,0:T(8,128)(2,1)S(1)}, u32[]{:S(2)}, u32[]{:S(2)}) collective-permute-start(bf16[2064,128]{1,0:T(8,128)(2,1)S(1)} %collective-permute-done.5.refs_1_), channel_id=1, source_target_pairs={{0,4},{4,8},{8,12},{12,14},{14,10},{10,6},{6,2},{2,0},{1,3},{5,1},... | collective-permute-start | bytes 1585160 | tf_op jit(solution)/shard_map/ppermute | solution.py:463
  35.1 2.2 %shard_map.84 = (f32[4,512,128]{2,1,0:T(8,128)S(1)}, bf16[4,16,128]{2,1,0:T(8,128)(2,1)S(1)}) custom-call(s32[1,128]{1,0:T(1,128)S(1)} %fusion.2.refs_0_, bf16[2064,128]{1,0:T(8,128)(2,1)S(1)} %collective-permute-done.5.refs_1_, bf16[32,2,64,512]{3,2,1,0:T(8,128)(2,1)S(1)} %copy-done.2), custom_call_target="tpu_custom_call" | custom-call | flops 1073741824 | bytes 2621440 | tf_op jit(solution)/shard_map/pallas_call | solution.py:248
  37.3 2.0 %collective-permute-done.4.in_ref = bf16[4,528,128]{2,1,0:T(8,128)(2,1)S(1)} collective-permute-done((bf16[4,528,128]{2,1,0:T(8,128)(2,1)S(1)}, bf16[4,528,128]{2,1,0:T(8,128)(2,1)S(1)}, u32[]{:S(2)}, u32[]{:S(2)}) %collective-permute-start.4) | collective-permute-done | bytes 540704 | tf_op jit(solution)/shard_map/ppermute | solution.py:463
  39.3 1.0 shard_map.85
  40.3 1.6 %collective-permute-start.6 = (bf16[4,528,128]{2,1,0:T(8,128)(2,1)S(1)}, bf16[4,528,128]{2,1,0:T(8,128)(2,1)S(1)}, u32[]{:S(2)}, u32[]{:S(2)}) collective-permute-start(bf16[4,528,128]{2,1,0:T(8,128)(2,1)S(1)} %shard_map.85), channel_id=1, source_target_pairs={{0,4},{4,8},{8,12},{12,14},{14,10},{10,6},{6,2},{2,0},{1,3},{5,1},... | collective-permute-start | bytes 1622024 | tf_op jit(solution)/shard_map/ppermute | solution.py:463
  41.9 0.1 shard_map.86.refs_1_
  42.0 2.2 %copy-done.3 = bf16[32,2,64,512]{3,2,1,0:T(8,128)(2,1)S(1)} copy-done((bf16[32,2,64,512]{3,2,1,0:T(8,128)(2,1)S(1)}, bf16[32,2,64,512]{3,2,1,0:T(8,128)(2,1)}, u32[]{:S(2)}) %copy-start.3) | copy-done | bytes 4194328
  44.2 1.8 %shard_map.87 = (f32[2,512,128]{2,1,0:T(8,128)S(1)}, bf16[2,16,128]{2,1,0:T(8,128)(2,1)S(1)}) custom-call(s32[1,128]{1,0:T(1,128)S(1)} %fusion.3.refs_0_, bf16[2064,128]{1,0:T(8,128)(2,1)S(1)} %shard_map.86.refs_1_, bf16[2,64,512]{2,1,0:T(8,128)(2,1)S(1)} %bitcast.3, bf16[32,2,64,512]{3,2,1,0:T(8,128)(2,1)S(1)} %copy-done.3), custom_call_target="tpu_custom_call" | custom-call | flops 536870912 | bytes 1310720 | tf_op jit(solution)/shard_map/pallas_call | solution.py:248
  46.0 0.0 collective-permute-done.7.refs_1_
  46.0 1.6 %collective-permute-start.9 = (bf16[2064,128]{1,0:T(8,128)(2,1)S(1)}, bf16[2064,128]{1,0:T(8,128)(2,1)S(1)}, u32[]{:S(2)}, u32[]{:S(2)}) collective-permute-start(bf16[2064,128]{1,0:T(8,128)(2,1)S(1)} %collective-permute-done.7.refs_1_), channel_id=1, source_target_pairs={{0,4},{4,8},{8,12},{12,14},{14,10},{10,6},{6,2},{2,0},{1,3},{5,1},... | collective-permute-start | bytes 1585160 | tf_op jit(solution)/shard_map/ppermute | solution.py:463
  47.6 2.2 %shard_map.88 = (f32[4,512,128]{2,1,0:T(8,128)S(1)}, bf16[4,16,128]{2,1,0:T(8,128)(2,1)S(1)}) custom-call(s32[1,128]{1,0:T(1,128)S(1)} %fusion.4.refs_0_, bf16[2064,128]{1,0:T(8,128)(2,1)S(1)} %collective-permute-done.7.refs_1_, bf16[32,2,64,512]{3,2,1,0:T(8,128)(2,1)S(1)} %copy-done.3), custom_call_target="tpu_custom_call" | custom-call | flops 1073741824 | bytes 2621440 | tf_op jit(solution)/shard_map/pallas_call | solution.py:248
  49.8 1.0 collective-permute-done.6.in_ref
  50.8 1.0 shard_map.89
  51.8 1.8 %collective-permute-start.8 = (bf16[4,528,128]{2,1,0:T(8,128)(2,1)S(1)}, bf16[4,528,128]{2,1,0:T(8,128)(2,1)S(1)}, u32[]{:S(2)}, u32[]{:S(2)}) collective-permute-start(bf16[4,528,128]{2,1,0:T(8,128)(2,1)S(1)} %shard_map.89), channel_id=1, source_target_pairs={{0,4},{4,8},{8,12},{12,14},{14,10},{10,6},{6,2},{2,0},{1,3},{5,1},... | collective-permute-start | bytes 1622024 | tf_op jit(solution)/shard_map/ppermute | solution.py:463
  53.5 1.8 %shard_map.90 = (f32[2,512,128]{2,1,0:T(8,128)S(1)}, bf16[2,16,128]{2,1,0:T(8,128)(2,1)S(1)}) custom-call(s32[1,128]{1,0:T(1,128)S(1)} %fusion.3.refs_0_, bf16[2064,128]{1,0:T(8,128)(2,1)S(1)} %shard_map.86.refs_1_, bf16[2,64,512]{2,1,0:T(8,128)(2,1)S(1)} %bitcast.4, bf16[32,2,64,512]{3,2,1,0:T(8,128)(2,1)S(1)} %copy-done.4), custom_call_target="tpu_custom_call" | custom-call | flops 536870912 | bytes 1310720 | tf_op jit(solution)/shard_map/pallas_call | solution.py:248
  55.3 1.1 %collective-permute-done.9.refs_1_ = bf16[2064,128]{1,0:T(8,128)(2,1)S(1)} collective-permute-done((bf16[2064,128]{1,0:T(8,128)(2,1)S(1)}, bf16[2064,128]{1,0:T(8,128)(2,1)S(1)}, u32[]{:S(2)}, u32[]{:S(2)}) %collective-permute-start.9) | collective-permute-done | bytes 528416 | tf_op jit(solution)/shard_map/ppermute | solution.py:463
  56.4 1.5 %collective-permute-start.11 = (bf16[2064,128]{1,0:T(8,128)(2,1)S(1)}, bf16[2064,128]{1,0:T(8,128)(2,1)S(1)}, u32[]{:S(2)}, u32[]{:S(2)}) collective-permute-start(bf16[2064,128]{1,0:T(8,128)(2,1)S(1)} %collective-permute-done.9.refs_1_), channel_id=1, source_target_pairs={{0,4},{4,8},{8,12},{12,14},{14,10},{10,6},{6,2},{2,0},{1,3},{5,1},... | collective-permute-start | bytes 1585160 | tf_op jit(solution)/shard_map/ppermute | solution.py:463
  58.0 2.2 %shard_map.91 = (f32[4,512,128]{2,1,0:T(8,128)S(1)}, bf16[4,16,128]{2,1,0:T(8,128)(2,1)S(1)}) custom-call(s32[1,128]{1,0:T(1,128)S(1)} %fusion.5.refs_0_, bf16[2064,128]{1,0:T(8,128)(2,1)S(1)} %collective-permute-done.9.refs_1_, bf16[32,2,64,512]{3,2,1,0:T(8,128)(2,1)S(1)} %copy-done.4), custom_call_target="tpu_custom_call" | custom-call | flops 1073741824 | bytes 2621440 | tf_op jit(solution)/shard_map/pallas_call | solution.py:248
  60.2 2.0 %collective-permute-done.8.in_ref = bf16[4,528,128]{2,1,0:T(8,128)(2,1)S(1)} collective-permute-done((bf16[4,528,128]{2,1,0:T(8,128)(2,1)S(1)}, bf16[4,528,128]{2,1,0:T(8,128)(2,1)S(1)}, u32[]{:S(2)}, u32[]{:S(2)}) %collective-permute-start.8) | collective-permute-done | bytes 540704 | tf_op jit(solution)/shard_map/ppermute | solution.py:463
  62.2 1.0 shard_map.92
  63.2 1.6 %collective-permute-start.10 = (bf16[4,528,128]{2,1,0:T(8,128)(2,1)S(1)}, bf16[4,528,128]{2,1,0:T(8,128)(2,1)S(1)}, u32[]{:S(2)}, u32[]{:S(2)}) collective-permute-start(bf16[4,528,128]{2,1,0:T(8,128)(2,1)S(1)} %shard_map.92), channel_id=1, source_target_pairs={{0,4},{4,8},{8,12},{12,14},{14,10},{10,6},{6,2},{2,0},{1,3},{5,1},... | collective-permute-start | bytes 1622024 | tf_op jit(solution)/shard_map/ppermute | solution.py:463
  64.8 3.1 %collective-permute-done.11.refs_1_ = bf16[2064,128]{1,0:T(8,128)(2,1)S(1)} collective-permute-done((bf16[2064,128]{1,0:T(8,128)(2,1)S(1)}, bf16[2064,128]{1,0:T(8,128)(2,1)S(1)}, u32[]{:S(2)}, u32[]{:S(2)}) %collective-permute-start.11) | collective-permute-done | bytes 528416 | tf_op jit(solution)/shard_map/ppermute | solution.py:463
  67.9 1.5 %collective-permute-start.13 = (bf16[2064,128]{1,0:T(8,128)(2,1)S(1)}, bf16[2064,128]{1,0:T(8,128)(2,1)S(1)}, u32[]{:S(2)}, u32[]{:S(2)}) collective-permute-start(bf16[2064,128]{1,0:T(8,128)(2,1)S(1)} %collective-permute-done.11.refs_1_), channel_id=1, source_target_pairs={{0,4},{4,8},{8,12},{12,14},{14,10},{10,6},{6,2},{2,0},{1,3},{5,1},... | collective-permute-start | bytes 1585160 | tf_op jit(solution)/shard_map/ppermute | solution.py:463
  69.4 2.2 %shard_map.93 = (f32[4,512,128]{2,1,0:T(8,128)S(1)}, bf16[4,16,128]{2,1,0:T(8,128)(2,1)S(1)}) custom-call(s32[1,128]{1,0:T(1,128)S(1)} %fusion.6.refs_0_.far_ref, bf16[2064,128]{1,0:T(8,128)(2,1)S(1)} %collective-permute-done.11.refs_1_, bf16[32,2,64,512]{3,2,1,0:T(8,128)(2,1)S(1)} %copy-done.4), custom_call_target="tpu_custom_call" | custom-call | flops 1073741824 | bytes 2621440 | tf_op jit(solution)/shard_map/pallas_call | solution.py:248
  71.7 2.0 %collective-permute-done.10.in_ref = bf16[4,528,128]{2,1,0:T(8,128)(2,1)S(1)} collective-permute-done((bf16[4,528,128]{2,1,0:T(8,128)(2,1)S(1)}, bf16[4,528,128]{2,1,0:T(8,128)(2,1)S(1)}, u32[]{:S(2)}, u32[]{:S(2)}) %collective-permute-start.10) | collective-permute-done | bytes 540704 | tf_op jit(solution)/shard_map/ppermute | solution.py:463
  73.7 1.0 shard_map.94
  74.7 1.6 %collective-permute-start.12 = (bf16[4,528,128]{2,1,0:T(8,128)(2,1)S(1)}, bf16[4,528,128]{2,1,0:T(8,128)(2,1)S(1)}, u32[]{:S(2)}, u32[]{:S(2)}) collective-permute-start(bf16[4,528,128]{2,1,0:T(8,128)(2,1)S(1)} %shard_map.94), channel_id=1, source_target_pairs={{0,4},{4,8},{8,12},{12,14},{14,10},{10,6},{6,2},{2,0},{1,3},{5,1},... | collective-permute-start | bytes 1622024 | tf_op jit(solution)/shard_map/ppermute | solution.py:463
  76.3 2.5 %collective-permute-start.14 = (bf16[1,2,64,512]{3,2,1,0:T(8,128)(2,1)S(1)}, bf16[1,2,64,512]{3,2,1,0:T(8,128)(2,1)S(1)}, u32[]{:S(2)}, u32[]{:S(2)}) collective-permute-start(bf16[1,2,64,512]{3,2,1,0:T(8,128)(2,1)S(1)} %copy-done.5), channel_id=1, source_target_pairs={{8,0},{10,2},{12,4},{14,6},{0,8},{2,10},{4,12},{6,14},{9,1},{11,3}... | collective-permute-start | bytes 393224 | tf_op jit(solution)/shard_map/ppermute | solution.py:26
  78.7 1.1 %collective-permute-done.13.refs_1_ = bf16[2064,128]{1,0:T(8,128)(2,1)S(1)} collective-permute-done((bf16[2064,128]{1,0:T(8,128)(2,1)S(1)}, bf16[2064,128]{1,0:T(8,128)(2,1)S(1)}, u32[]{:S(2)}, u32[]{:S(2)}) %collective-permute-start.13) | collective-permute-done | bytes 528416 | tf_op jit(solution)/shard_map/ppermute | solution.py:463
  79.8 2.2 %shard_map.95 = (f32[4,512,128]{2,1,0:T(8,128)S(1)}, bf16[4,16,128]{2,1,0:T(8,128)(2,1)S(1)}) custom-call(s32[1,128]{1,0:T(1,128)S(1)} %fusion.7.refs_0_, bf16[2064,128]{1,0:T(8,128)(2,1)S(1)} %collective-permute-done.13.refs_1_, bf16[32,2,64,512]{3,2,1,0:T(8,128)(2,1)S(1)} %copy-done.4), custom_call_target="tpu_custom_call" | custom-call | flops 1073741824 | bytes 2621440 | tf_op jit(solution)/shard_map/pallas_call | solution.py:248
  82.0 5.0 %collective-permute-done.14.page_ref = bf16[1,2,64,512]{3,2,1,0:T(8,128)(2,1)S(1)} collective-permute-done((bf16[1,2,64,512]{3,2,1,0:T(8,128)(2,1)S(1)}, bf16[1,2,64,512]{3,2,1,0:T(8,128)(2,1)S(1)}, u32[]{:S(2)}, u32[]{:S(2)}) %collective-permute-start.14) | collective-permute-done | bytes 131104 | tf_op jit(solution)/shard_map/ppermute | solution.py:26
  87.0 0.0 collective-permute-done.12.in_ref
  87.0 0.6 shard_map.96
  87.7 4.3 %collective-permute-start.16 = (bf16[2,528,128]{2,1,0:T(8,128)(2,1)S(1)}, bf16[2,528,128]{2,1,0:T(8,128)(2,1)S(1)}, u32[]{:S(2)}, u32[]{:S(2)}) collective-permute-start(bf16[2,528,128]{2,1,0:T(8,128)(2,1)S(1)} %shard_map.96), channel_id=1, source_target_pairs={{0,4},{4,8},{8,12},{12,14},{14,10},{10,6},{6,2},{2,0},{1,3},{5,1},... | collective-permute-start | bytes 811016 | tf_op jit(solution)/shard_map/ppermute | solution.py:463
  92.0 0.6 shard_map.97
  92.6 1.1 %collective-permute-start.15 = (bf16[2,528,128]{2,1,0:T(8,128)(2,1)S(1)}, bf16[2,528,128]{2,1,0:T(8,128)(2,1)S(1)}, u32[]{:S(2)}, u32[]{:S(2)}) collective-permute-start(bf16[2,528,128]{2,1,0:T(8,128)(2,1)S(1)} %shard_map.97), channel_id=1, source_target_pairs={{0,4},{4,8},{8,12},{12,14},{14,10},{10,6},{6,2},{2,0},{1,3},{5,1},... | collective-permute-start | bytes 811016 | tf_op jit(solution)/shard_map/ppermute | solution.py:463
  93.8 1.2 %shard_map.98 = bf16[32,2,64,512]{3,2,1,0:T(8,128)(2,1)} custom-call(s32[1]{0:T(128)} %bitcast.1.me_ref, s32[1]{0:T(128)} %bitcast.2.core_ref, s32[1,128]{1,0:T(1,128)S(1)} %fusion.1.refs_0_.near_ref, s32[1,128]{1,0:T(1,128)S(1)} %fusion.6.refs_0_.far_ref, ...), custom_call_target="tpu_custom_call", output_to_operand_aliasing={{}: (5, {})} | custom-call | flops 1 | bytes 1 | tf_op jit(solution)/shard_map/pallas_call | solution.py:293
  95.0 2.3 %collective-permute-done.16.in_ref = bf16[2,528,128]{2,1,0:T(8,128)(2,1)S(1)} collective-permute-done((bf16[2,528,128]{2,1,0:T(8,128)(2,1)S(1)}, bf16[2,528,128]{2,1,0:T(8,128)(2,1)S(1)}, u32[]{:S(2)}, u32[]{:S(2)}) %collective-permute-start.16) | collective-permute-done | bytes 270368 | tf_op jit(solution)/shard_map/ppermute | solution.py:463
  97.3 1.3 %shard_map.99.refs_0_ = bf16[1,64,4096]{2,1,0:T(8,128)(2,1)} custom-call(bf16[2,528,128]{2,1,0:T(8,128)(2,1)S(1)} %collective-permute-done.16.in_ref, f32[2,512,128]{2,1,0:T(8,128)S(1)} %get-tuple-element.58.acc_ref, bf16[2,16,128]{2,1,0:T(8,128)(2,1)S(1)} %get-tuple-element.59.stat_ref), custom_call_target="tpu_custom_call" | custom-call | tf_op jit(solution)/shard_map/pallas_call | solution.py:374
  98.6 1.6 %collective-permute-done.15.in_ref = bf16[2,528,128]{2,1,0:T(8,128)(2,1)S(1)} collective-permute-done((bf16[2,528,128]{2,1,0:T(8,128)(2,1)S(1)}, bf16[2,528,128]{2,1,0:T(8,128)(2,1)S(1)}, u32[]{:S(2)}, u32[]{:S(2)}) %collective-permute-start.15) | collective-permute-done | bytes 270368 | tf_op jit(solution)/shard_map/ppermute | solution.py:463
  100.2 1.3 %shard_map.100 = bf16[1,64,4096]{2,1,0:T(8,128)(2,1)} custom-call(bf16[2,528,128]{2,1,0:T(8,128)(2,1)S(1)} %collective-permute-done.15.in_ref, f32[2,512,128]{2,1,0:T(8,128)S(1)} %get-tuple-element.65.acc_ref, bf16[2,16,128]{2,1,0:T(8,128)(2,1)S(1)} %get-tuple-element.66.stat_ref, bf16[1,64,4096]{2,1,0:T(8,128)(2,1)} %shard_map.99.refs_0_), custom_call_target="tpu_custom_call", output_to_operand_aliasing={{}: (3, {})} | custom-call | tf_op jit(solution)/shard_map/pallas_call | solution.py:374
  (18 shorter events, 0.1 us)
Async XLA Ops:
  0.6 11.1 %collective-permute-start = (bf16[1,64,4096]{2,1,0:T(8,128)(2,1)}, bf16[1,64,4096]{2,1,0:T(8,128)(2,1)S(1)}, u32[]{:S(2)}, u32[]{:S(2)}) collective-permute-start(bf16[1,64,4096]{2,1,0:T(8,128)(2,1)} %q_ref), channel_id=1, source_target_pairs={{0,4},{4,8},{8,12},{12,14},{14,10},{10,6},{6,2},{2,0},{1,3},{5,1},... | collective-permute-start | bytes 1572872 | tf_op jit(solution)/shard_map/ppermute | solution.py:463
  5.0 0.7 copy-start.7
  5.9 5.8 %collective-permute-start.1 = (bf16[16,128]{1,0:T(8,128)(2,1)S(1)}, bf16[16,128]{1,0:T(8,128)(2,1)S(1)}, u32[]{:S(2)}, u32[]{:S(2)}) collective-permute-start(bf16[16,128]{1,0:T(8,128)(2,1)S(1)} %shard_map.77.before_ref.lists_ref), channel_id=1, source_target_pairs={{0,4},{4,8},{8,12},{12,14},{14,10},{10,6},{6,2},{2,0},{1,3},{5,1},... | collective-permute-start | bytes 12296 | tf_op jit(solution)/shard_map/ppermute | solution.py:463
  9.7 2.0 %copy-start = (bf16[32,2,64,512]{3,2,1,0:T(8,128)(2,1)}, bf16[32,2,64,512]{3,2,1,0:T(8,128)(2,1)S(1)}, u32[]{:S(2)}) copy-start(bf16[32,2,64,512]{3,2,1,0:T(8,128)(2,1)S(1)} %shard_map.78.refs_2_.refs_3_) | copy-start | bytes 12582916
  11.8 9.3 %collective-permute-start.3 = (bf16[2064,128]{1,0:T(8,128)(2,1)S(1)}, bf16[2064,128]{1,0:T(8,128)(2,1)S(1)}, u32[]{:S(2)}, u32[]{:S(2)}) collective-permute-start(bf16[2064,128]{1,0:T(8,128)(2,1)S(1)} %shard_map.79.refs_1_), channel_id=1, source_target_pairs={{0,4},{4,8},{8,12},{12,14},{14,10},{10,6},{6,2},{2,0},{1,3},{5,1},... | collective-permute-start | bytes 1585160 | tf_op jit(solution)/shard_map/ppermute | solution.py:463
  13.4 2.2 %copy-start.1 = (bf16[32,2,64,512]{3,2,1,0:T(8,128)(2,1)S(1)}, bf16[32,2,64,512]{3,2,1,0:T(8,128)(2,1)}, u32[]{:S(2)}) copy-start(bf16[32,2,64,512]{3,2,1,0:T(8,128)(2,1)} %copy-done) | copy-start | bytes 12582916
  15.6 7.0 %copy-start.2 = (bf16[32,2,64,512]{3,2,1,0:T(8,128)(2,1)S(1)}, bf16[32,2,64,512]{3,2,1,0:T(8,128)(2,1)}, u32[]{:S(2)}) copy-start(bf16[32,2,64,512]{3,2,1,0:T(8,128)(2,1)} %copy-done) | copy-start | bytes 12582916
  18.5 9.4 %collective-permute-start.2 = (bf16[4,528,128]{2,1,0:T(8,128)(2,1)S(1)}, bf16[4,528,128]{2,1,0:T(8,128)(2,1)S(1)}, u32[]{:S(2)}, u32[]{:S(2)}) collective-permute-start(bf16[4,528,128]{2,1,0:T(8,128)(2,1)S(1)} %shard_map.81), channel_id=1, source_target_pairs={{0,4},{4,8},{8,12},{12,14},{14,10},{10,6},{6,2},{2,0},{1,3},{5,1},... | collective-permute-start | bytes 1622024 | tf_op jit(solution)/shard_map/ppermute | solution.py:463
  21.1 12.5 %collective-permute-start.5 = (bf16[2064,128]{1,0:T(8,128)(2,1)S(1)}, bf16[2064,128]{1,0:T(8,128)(2,1)S(1)}, u32[]{:S(2)}, u32[]{:S(2)}) collective-permute-start(bf16[2064,128]{1,0:T(8,128)(2,1)S(1)} %collective-permute-done.3.refs_1_), channel_id=1, source_target_pairs={{0,4},{4,8},{8,12},{12,14},{14,10},{10,6},{6,2},{2,0},{1,3},{5,1},... | collective-permute-start | bytes 1585160 | tf_op jit(solution)/shard_map/ppermute | solution.py:463
  27.9 14.0 %copy-start.6 = (bf16[1,64,4096]{2,1,0:T(8,128)(2,1)S(1)}, bf16[1,64,4096]{2,1,0:T(8,128)(2,1)}, u32[]{:S(2)}) copy-start(bf16[1,64,4096]{2,1,0:T(8,128)(2,1)} %q_ref) | copy-start | bytes 1572868
  28.9 13.1 %copy-start.5 = (bf16[1,2,64,512]{3,2,1,0:T(8,128)(2,1)S(1)}, bf16[1,2,64,512]{3,2,1,0:T(8,128)(2,1)}, u32[]{:S(2)}) copy-start(bf16[1,2,64,512]{3,2,1,0:T(8,128)(2,1)} %param.7) | copy-start | bytes 393220
  28.9 10.5 %collective-permute-start.4 = (bf16[4,528,128]{2,1,0:T(8,128)(2,1)S(1)}, bf16[4,528,128]{2,1,0:T(8,128)(2,1)S(1)}, u32[]{:S(2)}, u32[]{:S(2)}) collective-permute-start(bf16[4,528,128]{2,1,0:T(8,128)(2,1)S(1)} %shard_map.83), channel_id=1, source_target_pairs={{0,4},{4,8},{8,12},{12,14},{14,10},{10,6},{6,2},{2,0},{1,3},{5,1},... | collective-permute-start | bytes 1622024 | tf_op jit(solution)/shard_map/ppermute | solution.py:463
  33.5 12.5 %collective-permute-start.7 = (bf16[2064,128]{1,0:T(8,128)(2,1)S(1)}, bf16[2064,128]{1,0:T(8,128)(2,1)S(1)}, u32[]{:S(2)}, u32[]{:S(2)}) collective-permute-start(bf16[2064,128]{1,0:T(8,128)(2,1)S(1)} %collective-permute-done.5.refs_1_), channel_id=1, source_target_pairs={{0,4},{4,8},{8,12},{12,14},{14,10},{10,6},{6,2},{2,0},{1,3},{5,1},... | collective-permute-start | bytes 1585160 | tf_op jit(solution)/shard_map/ppermute | solution.py:463
  40.3 10.5 %collective-permute-start.6 = (bf16[4,528,128]{2,1,0:T(8,128)(2,1)S(1)}, bf16[4,528,128]{2,1,0:T(8,128)(2,1)S(1)}, u32[]{:S(2)}, u32[]{:S(2)}) collective-permute-start(bf16[4,528,128]{2,1,0:T(8,128)(2,1)S(1)} %shard_map.85), channel_id=1, source_target_pairs={{0,4},{4,8},{8,12},{12,14},{14,10},{10,6},{6,2},{2,0},{1,3},{5,1},... | collective-permute-start | bytes 1622024 | tf_op jit(solution)/shard_map/ppermute | solution.py:463
  42.0 2.2 %copy-start.3 = (bf16[32,2,64,512]{3,2,1,0:T(8,128)(2,1)S(1)}, bf16[32,2,64,512]{3,2,1,0:T(8,128)(2,1)}, u32[]{:S(2)}) copy-start(bf16[32,2,64,512]{3,2,1,0:T(8,128)(2,1)} %copy-done) | copy-start | bytes 12582916
  46.0 7.6 %copy-start.4 = (bf16[32,2,64,512]{3,2,1,0:T(8,128)(2,1)S(1)}, bf16[32,2,64,512]{3,2,1,0:T(8,128)(2,1)}, u32[]{:S(2)}) copy-start(bf16[32,2,64,512]{3,2,1,0:T(8,128)(2,1)} %copy-done) | copy-start | bytes 12582916
  46.0 10.4 %collective-permute-start.9 = (bf16[2064,128]{1,0:T(8,128)(2,1)S(1)}, bf16[2064,128]{1,0:T(8,128)(2,1)S(1)}, u32[]{:S(2)}, u32[]{:S(2)}) collective-permute-start(bf16[2064,128]{1,0:T(8,128)(2,1)S(1)} %collective-permute-done.7.refs_1_), channel_id=1, source_target_pairs={{0,4},{4,8},{8,12},{12,14},{14,10},{10,6},{6,2},{2,0},{1,3},{5,1},... | collective-permute-start | bytes 1585160 | tf_op jit(solution)/shard_map/ppermute | solution.py:463
  51.8 10.5 %collective-permute-start.8 = (bf16[4,528,128]{2,1,0:T(8,128)(2,1)S(1)}, bf16[4,528,128]{2,1,0:T(8,128)(2,1)S(1)}, u32[]{:S(2)}, u32[]{:S(2)}) collective-permute-start(bf16[4,528,128]{2,1,0:T(8,128)(2,1)S(1)} %shard_map.89), channel_id=1, source_target_pairs={{0,4},{4,8},{8,12},{12,14},{14,10},{10,6},{6,2},{2,0},{1,3},{5,1},... | collective-permute-start | bytes 1622024 | tf_op jit(solution)/shard_map/ppermute | solution.py:463
  56.4 11.5 %collective-permute-start.11 = (bf16[2064,128]{1,0:T(8,128)(2,1)S(1)}, bf16[2064,128]{1,0:T(8,128)(2,1)S(1)}, u32[]{:S(2)}, u32[]{:S(2)}) collective-permute-start(bf16[2064,128]{1,0:T(8,128)(2,1)S(1)} %collective-permute-done.9.refs_1_), channel_id=1, source_target_pairs={{0,4},{4,8},{8,12},{12,14},{14,10},{10,6},{6,2},{2,0},{1,3},{5,1},... | collective-permute-start | bytes 1585160 | tf_op jit(solution)/shard_map/ppermute | solution.py:463
  63.2 10.5 %collective-permute-start.10 = (bf16[4,528,128]{2,1,0:T(8,128)(2,1)S(1)}, bf16[4,528,128]{2,1,0:T(8,128)(2,1)S(1)}, u32[]{:S(2)}, u32[]{:S(2)}) collective-permute-start(bf16[4,528,128]{2,1,0:T(8,128)(2,1)S(1)} %shard_map.92), channel_id=1, source_target_pairs={{0,4},{4,8},{8,12},{12,14},{14,10},{10,6},{6,2},{2,0},{1,3},{5,1},... | collective-permute-start | bytes 1622024 | tf_op jit(solution)/shard_map/ppermute | solution.py:463
  67.9 11.9 %collective-permute-start.13 = (bf16[2064,128]{1,0:T(8,128)(2,1)S(1)}, bf16[2064,128]{1,0:T(8,128)(2,1)S(1)}, u32[]{:S(2)}, u32[]{:S(2)}) collective-permute-start(bf16[2064,128]{1,0:T(8,128)(2,1)S(1)} %collective-permute-done.11.refs_1_), channel_id=1, source_target_pairs={{0,4},{4,8},{8,12},{12,14},{14,10},{10,6},{6,2},{2,0},{1,3},{5,1},... | collective-permute-start | bytes 1585160 | tf_op jit(solution)/shard_map/ppermute | solution.py:463
  74.7 12.4 %collective-permute-start.12 = (bf16[4,528,128]{2,1,0:T(8,128)(2,1)S(1)}, bf16[4,528,128]{2,1,0:T(8,128)(2,1)S(1)}, u32[]{:S(2)}, u32[]{:S(2)}) collective-permute-start(bf16[4,528,128]{2,1,0:T(8,128)(2,1)S(1)} %shard_map.94), channel_id=1, source_target_pairs={{0,4},{4,8},{8,12},{12,14},{14,10},{10,6},{6,2},{2,0},{1,3},{5,1},... | collective-permute-start | bytes 1622024 | tf_op jit(solution)/shard_map/ppermute | solution.py:463
  76.3 10.8 %collective-permute-start.14 = (bf16[1,2,64,512]{3,2,1,0:T(8,128)(2,1)S(1)}, bf16[1,2,64,512]{3,2,1,0:T(8,128)(2,1)S(1)}, u32[]{:S(2)}, u32[]{:S(2)}) collective-permute-start(bf16[1,2,64,512]{3,2,1,0:T(8,128)(2,1)S(1)} %copy-done.5), channel_id=1, source_target_pairs={{8,0},{10,2},{12,4},{14,6},{0,8},{2,10},{4,12},{6,14},{9,1},{11,3}... | collective-permute-start | bytes 393224 | tf_op jit(solution)/shard_map/ppermute | solution.py:26
  87.7 9.6 %collective-permute-start.16 = (bf16[2,528,128]{2,1,0:T(8,128)(2,1)S(1)}, bf16[2,528,128]{2,1,0:T(8,128)(2,1)S(1)}, u32[]{:S(2)}, u32[]{:S(2)}) collective-permute-start(bf16[2,528,128]{2,1,0:T(8,128)(2,1)S(1)} %shard_map.96), channel_id=1, source_target_pairs={{0,4},{4,8},{8,12},{12,14},{14,10},{10,6},{6,2},{2,0},{1,3},{5,1},... | collective-permute-start | bytes 811016 | tf_op jit(solution)/shard_map/ppermute | solution.py:463
  92.6 7.5 %collective-permute-start.15 = (bf16[2,528,128]{2,1,0:T(8,128)(2,1)S(1)}, bf16[2,528,128]{2,1,0:T(8,128)(2,1)S(1)}, u32[]{:S(2)}, u32[]{:S(2)}) collective-permute-start(bf16[2,528,128]{2,1,0:T(8,128)(2,1)S(1)} %shard_map.97), channel_id=1, source_target_pairs={{0,4},{4,8},{8,12},{12,14},{14,10},{10,6},{6,2},{2,0},{1,3},{5,1},... | collective-permute-start | bytes 811016 | tf_op jit(solution)/shard_map/ppermute | solution.py:463

commit v16 on v15

--- a/solution.py
+++ b/solution.py
@@ -245,6 +245,11 @@
         aliases[len(args)] = 2 * count
         args.append(store)
         in_specs.append(HBM)
+    work = pl.CostEstimate(
+        flops=len(jobs) * rows * keys * HEAD_SIZE * 8,
+        bytes_accessed=len(jobs) * (rows * 6 + keys * 4) * HEAD_SIZE,
+        transcendentals=len(jobs) * rows * keys,
+    )
     out = pl.pallas_call(
         functools.partial(attend_kernel, sizes + (count,), jobs, own is not None, keeping),
         out_shape=shapes,
@@ -253,11 +258,7 @@
         scratch_shapes=scratch,
         input_output_aliases=aliases,
         compiler_params=pltpu.CompilerParams(vmem_limit_bytes=GRANT),
-        cost_estimate=pl.CostEstimate(
-            flops=len(jobs) * rows * keys * HEAD_SIZE * 8,
-            bytes_accessed=len(jobs) * (rows * 6 + keys * 4) * HEAD_SIZE,
-            transcendentals=len(jobs) * rows * keys,
-        ),
+        cost_estimate=work,
     )(*args)
     return [(out[2 * n], out[2 * n + 1]) for n in range(count)] + list(out[2 * count:])
 
@@ -275,7 +276,7 @@
         in_specs=[HBM, VMEM],
         out_specs=VMEM,
         scratch_shapes=[pltpu.SemaphoreType.DMA],
-        compiler_params=pltpu.CompilerParams(vmem_limit_bytes=48 * 1024 * 1024),
+        compiler_params=pltpu.CompilerParams(vmem_limit_bytes=2 * GRANT),
         cost_estimate=LIGHT,
     )(pages, before)
 
@@ -487,7 +488,7 @@
         if step < stores - 1:
             moving = onward(came)
         lists[step] = listed(came, heads * rows)
-        if step == stores - 2:
+        if step == stores - 3:
             arrived = shifted(after(suffix_key_value, token), "store", half)
         jobs = [(0, h, h) for h in range(heads)]
         keeping, pages = None, pages_dev // 2
@@ -501,10 +502,9 @@
             part, = attend(sizes, jobs, lists[step], [came], held)
         if step == 1:
             blocks = [packed(part)]
-        elif step < stores - 1:
+        elif step < stores - 2:
             blocks = [merged(after(partial[0], part), part, 0, 0, heads)]
         else:
-            part = after(part, arrived) if step == stores - 1 else part
             blocks = []
             for n, half_heads in enumerate(halves):
                 block, at = (partial[0], half_heads[0]) if len(partial) == 1 else (partial[n], 0)
@@ -512,6 +512,8 @@
                 blocks.append(merged(block, part, at, half_heads[0], len(half_heads)))
         partial = [onward(block) for block in blocks]
         token = blocks
+        if step == stores - 2:
+            token = [blocks, arrived]
         if step in (half - 1, half):
             if own_queries is None:
                 own_queries = joined(after(queries, token), mine)

time: 102 us -> 98.4 us (0.965)
  waiting for transfers between devices: 27.7 us -> 19.5 us
  starting transfers between devices: 31.5 us -> 35.8 us
  local copies, waits for them, and re-layouts: 6.99 us -> 9.18 us
  Pallas kernels: 33 us -> 31.4 us
    ppermute x16 -> x17, starting transfers between devices: 29 us -> 33.6 us  [onward(): return lax.ppermute(x, ('store', 'tensor'), route)]
    ppermute x1, waiting for transfers between devices: 5.01 us -> 0.64 us  [shifted(): return lax.ppermute(block, axis, route)]
    ppermute x16 -> x17, waiting for transfers between devices: 22.7 us -> 18.8 us  [onward(): return lax.ppermute(x, ('store', 'tensor'), route)]
    unnamed x16 -> x18, local copies, waits for them, and re-layouts: 6.99 us -> 9.18 us
    pallas_call x1, Pallas kernels: 2.2 us -> 0.29 us  [hold(): pl.pallas_call(hold_kernel, out_shape=jax.ShapeDtypeStruct(pages.shape, p...]
    pallas_call x10 -> x11, Pallas kernels: 6.41 us -> 6.71 us  [call(): pl.pallas_call(kernel, out_shape=shape, in_specs=[VMEM] * len(args), out_...]
  transfers between devices with their start and end apart: 17 -> 18, of which waited for: 13 -> 13; matrix products, arithmetic and copies ran while one was open for 0% -> 0% of each run, Pallas kernels for 31% -> 31%
where the time goes in v16:
time: 98.4 us; the launch traced here: 98.2 us
  starting transfers between devices  35.8 us (36%)
  Pallas kernels  31.4 us (32%)
  waiting for transfers between devices  19.5 us (20%)
  local copies, waits for them, and re-layouts  9.18 us (9%)
  between operations  2.31 us (2%)
    ppermute x17, starting transfers between devices, onward(): return lax.ppermute(x, ('store', 'tensor'), route)  33.6 us
    pallas_call x9, Pallas kernels, attend(): pl.pallas_call(functools.partial(attend_kernel, sizes + (count,), jobs, o...  20.3 us
    ppermute x17, waiting for transfers between devices, onward(): return lax.ppermute(x, ('store', 'tensor'), route)  18.8 us
    unnamed x18, local copies, waits for them, and re-layouts  9.18 us
    pallas_call x11, Pallas kernels, call(): pl.pallas_call(kernel, out_shape=shape, in_specs=[VMEM] * len(args), out_...  6.71 us
    pallas_call x2, Pallas kernels, finish(): pl.pallas_call(functools.partial(final_kernel, suffix, first), out_shape=...  2.53 us
    ppermute x1, starting transfers between devices, shifted(): return lax.ppermute(block, axis, route)  2.17 us
  transfers between devices with their start and end apart: 18, of which 13 were waited for; matrix products, arithmetic and copies ran while one was open for 0% of the time, Pallas kernels for 31%

profile of v16, /device:TPU:0, one launch (start us, length us, event | category | flops | bytes accessed | tf_op | source)
XLA Modules:
  0.0 98.2 jit_solution(15655880765338303357)
XLA Ops:
  0.6 3.1 %collective-permute-start = (bf16[1,64,4096]{2,1,0:T(8,128)(2,1)}, bf16[1,64,4096]{2,1,0:T(8,128)(2,1)S(1)}, u32[]{:S(2)}, u32[]{:S(2)}) collective-permute-start(bf16[1,64,4096]{2,1,0:T(8,128)(2,1)} %q_ref), channel_id=1, source_target_pairs={{0,4},{4,8},{8,12},{12,14},{14,10},{10,6},{6,2},{2,0},{1,3},{5,1},... | collective-permute-start | bytes 1572872 | tf_op jit(solution)/shard_map/ppermute | solution.py:464
  5.0 0.6 copy-done.8
  5.7 0.3 shard_map.77.before_ref.lists_ref
  5.9 1.6 %collective-permute-start.1 = (bf16[16,128]{1,0:T(8,128)(2,1)S(1)}, bf16[16,128]{1,0:T(8,128)(2,1)S(1)}, u32[]{:S(2)}, u32[]{:S(2)}) collective-permute-start(bf16[16,128]{1,0:T(8,128)(2,1)S(1)} %shard_map.77.before_ref.lists_ref), channel_id=1, source_target_pairs={{0,4},{4,8},{8,12},{12,14},{14,10},{10,6},{6,2},{2,0},{1,3},{5,1},... | collective-permute-start | bytes 12296 | tf_op jit(solution)/shard_map/ppermute | solution.py:464
  7.5 2.2 %copy-done.5 = bf16[32,2,64,512]{3,2,1,0:T(8,128)(2,1)S(1)} copy-done((bf16[32,2,64,512]{3,2,1,0:T(8,128)(2,1)S(1)}, bf16[32,2,64,512]{3,2,1,0:T(8,128)(2,1)}, u32[]{:S(2)}) %copy-start.5) | copy-done | bytes 4194328
  9.7 0.3 shard_map.78.refs_2_.refs_3_
  10.0 2.0 %copy-done = bf16[32,2,64,512]{3,2,1,0:T(8,128)(2,1)} copy-done((bf16[32,2,64,512]{3,2,1,0:T(8,128)(2,1)}, bf16[32,2,64,512]{3,2,1,0:T(8,128)(2,1)S(1)}, u32[]{:S(2)}) %copy-start) | copy-done | bytes 4194328
  12.0 0.0 collective-permute-done.q_ref
  12.0 0.0 collective-permute-done.1.lists_ref
  12.0 0.1 shard_map.79.refs_1_
  12.1 1.6 %collective-permute-start.3 = (bf16[2064,128]{1,0:T(8,128)(2,1)S(1)}, bf16[2064,128]{1,0:T(8,128)(2,1)S(1)}, u32[]{:S(2)}, u32[]{:S(2)}) collective-permute-start(bf16[2064,128]{1,0:T(8,128)(2,1)S(1)} %shard_map.79.refs_1_), channel_id=1, source_target_pairs={{0,4},{4,8},{8,12},{12,14},{14,10},{10,6},{6,2},{2,0},{1,3},{5,1},... | collective-permute-start | bytes 1585160 | tf_op jit(solution)/shard_map/ppermute | solution.py:464
  13.7 2.2 %copy-done.1 = bf16[32,2,64,512]{3,2,1,0:T(8,128)(2,1)S(1)} copy-done((bf16[32,2,64,512]{3,2,1,0:T(8,128)(2,1)S(1)}, bf16[32,2,64,512]{3,2,1,0:T(8,128)(2,1)}, u32[]{:S(2)}) %copy-start.1) | copy-done | bytes 4194328
  15.9 2.8 %shard_map.80 = (f32[4,512,128]{2,1,0:T(8,128)S(1)}, bf16[4,16,128]{2,1,0:T(8,128)(2,1)S(1)}, bf16[32,2,64,512]{3,2,1,0:T(8,128)(2,1)}) custom-call(s32[1,128]{1,0:T(1,128)S(1)} %fusion.refs_0_, bf16[2064,128]{1,0:T(8,128)(2,1)S(1)} %shard_map.79.refs_1_, bf16[32,2,64,512]{3,2,1,0:T(8,128)(2,1)S(1)} %copy-done.1), custom_call_target="tpu_custom_call" | custom-call | flops 1073741824 | bytes 2621440 | tf_op jit(solution)/shard_map/pallas_call | solution.py:253
  18.7 0.1 shard_map.81
  18.7 1.6 %collective-permute-start.2 = (bf16[4,528,128]{2,1,0:T(8,128)(2,1)S(1)}, bf16[4,528,128]{2,1,0:T(8,128)(2,1)S(1)}, u32[]{:S(2)}, u32[]{:S(2)}) collective-permute-start(bf16[4,528,128]{2,1,0:T(8,128)(2,1)S(1)} %shard_map.81), channel_id=1, source_target_pairs={{0,4},{4,8},{8,12},{12,14},{14,10},{10,6},{6,2},{2,0},{1,3},{5,1},... | collective-permute-start | bytes 1622024 | tf_op jit(solution)/shard_map/ppermute | solution.py:464
  20.3 1.0 %collective-permute-done.3.refs_1_ = bf16[2064,128]{1,0:T(8,128)(2,1)S(1)} collective-permute-done((bf16[2064,128]{1,0:T(8,128)(2,1)S(1)}, bf16[2064,128]{1,0:T(8,128)(2,1)S(1)}, u32[]{:S(2)}, u32[]{:S(2)}) %collective-permute-start.3) | collective-permute-done | bytes 528416 | tf_op jit(solution)/shard_map/ppermute | solution.py:464
  21.4 1.6 %collective-permute-start.5 = (bf16[2064,128]{1,0:T(8,128)(2,1)S(1)}, bf16[2064,128]{1,0:T(8,128)(2,1)S(1)}, u32[]{:S(2)}, u32[]{:S(2)}) collective-permute-start(bf16[2064,128]{1,0:T(8,128)(2,1)S(1)} %collective-permute-done.3.refs_1_), channel_id=1, source_target_pairs={{0,4},{4,8},{8,12},{12,14},{14,10},{10,6},{6,2},{2,0},{1,3},{5,1},... | collective-permute-start | bytes 1585160 | tf_op jit(solution)/shard_map/ppermute | solution.py:464
  22.9 2.9 %shard_map.82 = (f32[4,512,128]{2,1,0:T(8,128)S(1)}, bf16[4,16,128]{2,1,0:T(8,128)(2,1)S(1)}, bf16[32,2,64,512]{3,2,1,0:T(8,128)(2,1)}) custom-call(s32[1,128]{1,0:T(1,128)S(1)} %fusion.1.refs_0_.near_ref, bf16[2064,128]{1,0:T(8,128)(2,1)S(1)} %collective-permute-done.3.refs_1_, ...), custom_call_target="tpu_custom_call", output_to_operand_aliasing={{2}: (3, {})} | custom-call | flops 1073741824 | bytes 2621440 | tf_op jit(solution)/shard_map/pallas_call | solution.py:253
  25.9 2.3 %collective-permute-done.2.in_ref = bf16[4,528,128]{2,1,0:T(8,128)(2,1)S(1)} collective-permute-done((bf16[4,528,128]{2,1,0:T(8,128)(2,1)S(1)}, bf16[4,528,128]{2,1,0:T(8,128)(2,1)S(1)}, u32[]{:S(2)}, u32[]{:S(2)}) %collective-permute-start.2) | collective-permute-done | bytes 540704 | tf_op jit(solution)/shard_map/ppermute | solution.py:464
  28.2 1.0 shard_map.83
  29.1 1.6 %collective-permute-start.4 = (bf16[4,528,128]{2,1,0:T(8,128)(2,1)S(1)}, bf16[4,528,128]{2,1,0:T(8,128)(2,1)S(1)}, u32[]{:S(2)}, u32[]{:S(2)}) collective-permute-start(bf16[4,528,128]{2,1,0:T(8,128)(2,1)S(1)} %shard_map.83), channel_id=1, source_target_pairs={{0,4},{4,8},{8,12},{12,14},{14,10},{10,6},{6,2},{2,0},{1,3},{5,1},... | collective-permute-start | bytes 1622024 | tf_op jit(solution)/shard_map/ppermute | solution.py:464
  30.7 3.1 %collective-permute-done.5.refs_1_ = bf16[2064,128]{1,0:T(8,128)(2,1)S(1)} collective-permute-done((bf16[2064,128]{1,0:T(8,128)(2,1)S(1)}, bf16[2064,128]{1,0:T(8,128)(2,1)S(1)}, u32[]{:S(2)}, u32[]{:S(2)}) %collective-permute-start.5) | collective-permute-done | bytes 528416 | tf_op jit(solution)/shard_map/ppermute | solution.py:464
  33.8 1.5 %collective-permute-start.7 = (bf16[2064,128]{1,0:T(8,128)(2,1)S(1)}, bf16[2064,128]{1,0:T(8,128)(2,1)S(1)}, u32[]{:S(2)}, u32[]{:S(2)}) collective-permute-start(bf16[2064,128]{1,0:T(8,128)(2,1)S(1)} %collective-permute-done.5.refs_1_), channel_id=1, source_target_pairs={{0,4},{4,8},{8,12},{12,14},{14,10},{10,6},{6,2},{2,0},{1,3},{5,1},... | collective-permute-start | bytes 1585160 | tf_op jit(solution)/shard_map/ppermute | solution.py:464
  35.3 2.2 %copy-done.3 = bf16[32,2,64,512]{3,2,1,0:T(8,128)(2,1)S(1)} copy-done((bf16[32,2,64,512]{3,2,1,0:T(8,128)(2,1)S(1)}, bf16[32,2,64,512]{3,2,1,0:T(8,128)(2,1)}, u32[]{:S(2)}) %copy-start.3) | copy-done | bytes 4194328
  37.5 2.2 %shard_map.84 = (f32[4,512,128]{2,1,0:T(8,128)S(1)}, bf16[4,16,128]{2,1,0:T(8,128)(2,1)S(1)}) custom-call(s32[1,128]{1,0:T(1,128)S(1)} %fusion.2.refs_0_, bf16[2064,128]{1,0:T(8,128)(2,1)S(1)} %collective-permute-done.5.refs_1_, bf16[32,2,64,512]{3,2,1,0:T(8,128)(2,1)S(1)} %copy-done.3), custom_call_target="tpu_custom_call" | custom-call | flops 1073741824 | bytes 2621440 | tf_op jit(solution)/shard_map/pallas_call | solution.py:253
  39.8 0.0 collective-permute-done.4.in_ref
  39.8 1.0 %shard_map.85 = bf16[4,528,128]{2,1,0:T(8,128)(2,1)S(1)} custom-call(bf16[4,528,128]{2,1,0:T(8,128)(2,1)S(1)} %collective-permute-done.4.in_ref, f32[4,512,128]{2,1,0:T(8,128)S(1)} %get-tuple-element.52.acc_ref, bf16[4,16,128]{2,1,0:T(8,128)(2,1)S(1)} %get-tuple-element.53.stat_ref), custom_call_target="tpu_custom_call" | custom-call | flops 1605632 | bytes 3211264 | tf_op jit(solution)/shard_map/pallas_call | solution.py:391
  40.8 1.4 %collective-permute-start.6 = (bf16[4,528,128]{2,1,0:T(8,128)(2,1)S(1)}, bf16[4,528,128]{2,1,0:T(8,128)(2,1)S(1)}, u32[]{:S(2)}, u32[]{:S(2)}) collective-permute-start(bf16[4,528,128]{2,1,0:T(8,128)(2,1)S(1)} %shard_map.85), channel_id=1, source_target_pairs={{0,4},{4,8},{8,12},{12,14},{14,10},{10,6},{6,2},{2,0},{1,3},{5,1},... | collective-permute-start | bytes 1622024 | tf_op jit(solution)/shard_map/ppermute | solution.py:464
  42.2 0.1 shard_map.86.refs_1_
  42.3 1.8 %shard_map.87 = (f32[2,512,128]{2,1,0:T(8,128)S(1)}, bf16[2,16,128]{2,1,0:T(8,128)(2,1)S(1)}) custom-call(s32[1,128]{1,0:T(1,128)S(1)} %fusion.3.refs_0_, bf16[2064,128]{1,0:T(8,128)(2,1)S(1)} %shard_map.86.refs_1_, bf16[2,64,512]{2,1,0:T(8,128)(2,1)S(1)} %bitcast.3, bf16[32,2,64,512]{3,2,1,0:T(8,128)(2,1)S(1)} %copy-done.4), custom_call_target="tpu_custom_call" | custom-call | flops 536870912 | bytes 1310720 | tf_op jit(solution)/shard_map/pallas_call | solution.py:253
  44.1 1.2 %collective-permute-done.7.refs_1_ = bf16[2064,128]{1,0:T(8,128)(2,1)S(1)} collective-permute-done((bf16[2064,128]{1,0:T(8,128)(2,1)S(1)}, bf16[2064,128]{1,0:T(8,128)(2,1)S(1)}, u32[]{:S(2)}, u32[]{:S(2)}) %collective-permute-start.7) | collective-permute-done | bytes 528416 | tf_op jit(solution)/shard_map/ppermute | solution.py:464
  45.3 1.5 %collective-permute-start.9 = (bf16[2064,128]{1,0:T(8,128)(2,1)S(1)}, bf16[2064,128]{1,0:T(8,128)(2,1)S(1)}, u32[]{:S(2)}, u32[]{:S(2)}) collective-permute-start(bf16[2064,128]{1,0:T(8,128)(2,1)S(1)} %collective-permute-done.7.refs_1_), channel_id=1, source_target_pairs={{0,4},{4,8},{8,12},{12,14},{14,10},{10,6},{6,2},{2,0},{1,3},{5,1},... | collective-permute-start | bytes 1585160 | tf_op jit(solution)/shard_map/ppermute | solution.py:464
  46.8 2.2 %shard_map.88 = (f32[4,512,128]{2,1,0:T(8,128)S(1)}, bf16[4,16,128]{2,1,0:T(8,128)(2,1)S(1)}) custom-call(s32[1,128]{1,0:T(1,128)S(1)} %fusion.4.refs_0_, bf16[2064,128]{1,0:T(8,128)(2,1)S(1)} %collective-permute-done.7.refs_1_, bf16[32,2,64,512]{3,2,1,0:T(8,128)(2,1)S(1)} %copy-done.4), custom_call_target="tpu_custom_call" | custom-call | flops 1073741824 | bytes 2621440 | tf_op jit(solution)/shard_map/pallas_call | solution.py:253
  49.0 2.0 %collective-permute-done.6.in_ref = bf16[4,528,128]{2,1,0:T(8,128)(2,1)S(1)} collective-permute-done((bf16[4,528,128]{2,1,0:T(8,128)(2,1)S(1)}, bf16[4,528,128]{2,1,0:T(8,128)(2,1)S(1)}, u32[]{:S(2)}, u32[]{:S(2)}) %collective-permute-start.6) | collective-permute-done | bytes 540704 | tf_op jit(solution)/shard_map/ppermute | solution.py:464
  51.1 1.0 %shard_map.89 = bf16[4,528,128]{2,1,0:T(8,128)(2,1)S(1)} custom-call(bf16[4,528,128]{2,1,0:T(8,128)(2,1)S(1)} %collective-permute-done.6.in_ref, f32[4,512,128]{2,1,0:T(8,128)S(1)} %get-tuple-element.60.acc_ref, bf16[4,16,128]{2,1,0:T(8,128)(2,1)S(1)} %get-tuple-element.61.stat_ref), custom_call_target="tpu_custom_call" | custom-call | flops 1605632 | bytes 3211264 | tf_op jit(solution)/shard_map/pallas_call | solution.py:391
  52.1 1.8 %collective-permute-start.8 = (bf16[4,528,128]{2,1,0:T(8,128)(2,1)S(1)}, bf16[4,528,128]{2,1,0:T(8,128)(2,1)S(1)}, u32[]{:S(2)}, u32[]{:S(2)}) collective-permute-start(bf16[4,528,128]{2,1,0:T(8,128)(2,1)S(1)} %shard_map.89), channel_id=1, source_target_pairs={{0,4},{4,8},{8,12},{12,14},{14,10},{10,6},{6,2},{2,0},{1,3},{5,1},... | collective-permute-start | bytes 1622024 | tf_op jit(solution)/shard_map/ppermute | solution.py:464
  53.8 1.8 %shard_map.90 = (f32[2,512,128]{2,1,0:T(8,128)S(1)}, bf16[2,16,128]{2,1,0:T(8,128)(2,1)S(1)}) custom-call(s32[1,128]{1,0:T(1,128)S(1)} %fusion.3.refs_0_, bf16[2064,128]{1,0:T(8,128)(2,1)S(1)} %shard_map.86.refs_1_, bf16[2,64,512]{2,1,0:T(8,128)(2,1)S(1)} %bitcast.4, bf16[32,2,64,512]{3,2,1,0:T(8,128)(2,1)S(1)} %copy-done.4), custom_call_target="tpu_custom_call" | custom-call | flops 536870912 | bytes 1310720 | tf_op jit(solution)/shard_map/pallas_call | solution.py:253
  55.6 1.1 %collective-permute-done.9.refs_1_ = bf16[2064,128]{1,0:T(8,128)(2,1)S(1)} collective-permute-done((bf16[2064,128]{1,0:T(8,128)(2,1)S(1)}, bf16[2064,128]{1,0:T(8,128)(2,1)S(1)}, u32[]{:S(2)}, u32[]{:S(2)}) %collective-permute-start.9) | collective-permute-done | bytes 528416 | tf_op jit(solution)/shard_map/ppermute | solution.py:464
  56.7 1.5 %collective-permute-start.11 = (bf16[2064,128]{1,0:T(8,128)(2,1)S(1)}, bf16[2064,128]{1,0:T(8,128)(2,1)S(1)}, u32[]{:S(2)}, u32[]{:S(2)}) collective-permute-start(bf16[2064,128]{1,0:T(8,128)(2,1)S(1)} %collective-permute-done.9.refs_1_), channel_id=1, source_target_pairs={{0,4},{4,8},{8,12},{12,14},{14,10},{10,6},{6,2},{2,0},{1,3},{5,1},... | collective-permute-start | bytes 1585160 | tf_op jit(solution)/shard_map/ppermute | solution.py:464
  58.3 2.2 %shard_map.91 = (f32[4,512,128]{2,1,0:T(8,128)S(1)}, bf16[4,16,128]{2,1,0:T(8,128)(2,1)S(1)}) custom-call(s32[1,128]{1,0:T(1,128)S(1)} %fusion.5.refs_0_, bf16[2064,128]{1,0:T(8,128)(2,1)S(1)} %collective-permute-done.9.refs_1_, bf16[32,2,64,512]{3,2,1,0:T(8,128)(2,1)S(1)} %copy-done.4), custom_call_target="tpu_custom_call" | custom-call | flops 1073741824 | bytes 2621440 | tf_op jit(solution)/shard_map/pallas_call | solution.py:253
  60.5 2.0 %collective-permute-done.8.in_ref = bf16[4,528,128]{2,1,0:T(8,128)(2,1)S(1)} collective-permute-done((bf16[4,528,128]{2,1,0:T(8,128)(2,1)S(1)}, bf16[4,528,128]{2,1,0:T(8,128)(2,1)S(1)}, u32[]{:S(2)}, u32[]{:S(2)}) %collective-permute-start.8) | collective-permute-done | bytes 540704 | tf_op jit(solution)/shard_map/ppermute | solution.py:464
  62.5 1.0 %shard_map.92 = bf16[4,528,128]{2,1,0:T(8,128)(2,1)S(1)} custom-call(bf16[4,528,128]{2,1,0:T(8,128)(2,1)S(1)} %collective-permute-done.8.in_ref, f32[4,512,128]{2,1,0:T(8,128)S(1)} %get-tuple-element.67.acc_ref, bf16[4,16,128]{2,1,0:T(8,128)(2,1)S(1)} %get-tuple-element.68.stat_ref), custom_call_target="tpu_custom_call" | custom-call | flops 1605632 | bytes 3211264 | tf_op jit(solution)/shard_map/pallas_call | solution.py:391
  63.5 1.6 %collective-permute-start.10 = (bf16[4,528,128]{2,1,0:T(8,128)(2,1)S(1)}, bf16[4,528,128]{2,1,0:T(8,128)(2,1)S(1)}, u32[]{:S(2)}, u32[]{:S(2)}) collective-permute-start(bf16[4,528,128]{2,1,0:T(8,128)(2,1)S(1)} %shard_map.92), channel_id=1, source_target_pairs={{0,4},{4,8},{8,12},{12,14},{14,10},{10,6},{6,2},{2,0},{1,3},{5,1},... | collective-permute-start | bytes 1622024 | tf_op jit(solution)/shard_map/ppermute | solution.py:464
  65.1 3.1 %collective-permute-done.11.refs_1_ = bf16[2064,128]{1,0:T(8,128)(2,1)S(1)} collective-permute-done((bf16[2064,128]{1,0:T(8,128)(2,1)S(1)}, bf16[2064,128]{1,0:T(8,128)(2,1)S(1)}, u32[]{:S(2)}, u32[]{:S(2)}) %collective-permute-start.11) | collective-permute-done | bytes 528416 | tf_op jit(solution)/shard_map/ppermute | solution.py:464
  68.2 1.5 %collective-permute-start.13 = (bf16[2064,128]{1,0:T(8,128)(2,1)S(1)}, bf16[2064,128]{1,0:T(8,128)(2,1)S(1)}, u32[]{:S(2)}, u32[]{:S(2)}) collective-permute-start(bf16[2064,128]{1,0:T(8,128)(2,1)S(1)} %collective-permute-done.11.refs_1_), channel_id=1, source_target_pairs={{0,4},{4,8},{8,12},{12,14},{14,10},{10,6},{6,2},{2,0},{1,3},{5,1},... | collective-permute-start | bytes 1585160 | tf_op jit(solution)/shard_map/ppermute | solution.py:464
  69.7 2.2 %collective-permute-start.14 = (bf16[1,2,64,512]{3,2,1,0:T(8,128)(2,1)S(1)}, bf16[1,2,64,512]{3,2,1,0:T(8,128)(2,1)S(1)}, u32[]{:S(2)}, u32[]{:S(2)}) collective-permute-start(bf16[1,2,64,512]{3,2,1,0:T(8,128)(2,1)S(1)} %copy-done.6), channel_id=1, source_target_pairs={{8,0},{10,2},{12,4},{14,6},{0,8},{2,10},{4,12},{6,14},{9,1},{11,3}... | collective-permute-start | bytes 393224 | tf_op jit(solution)/shard_map/ppermute | solution.py:26
  71.9 2.2 %shard_map.93 = (f32[4,512,128]{2,1,0:T(8,128)S(1)}, bf16[4,16,128]{2,1,0:T(8,128)(2,1)S(1)}) custom-call(s32[1,128]{1,0:T(1,128)S(1)} %fusion.6.refs_0_.far_ref, bf16[2064,128]{1,0:T(8,128)(2,1)S(1)} %collective-permute-done.11.refs_1_, bf16[32,2,64,512]{3,2,1,0:T(8,128)(2,1)S(1)} %copy-done.4), custom_call_target="tpu_custom_call" | custom-call | flops 1073741824 | bytes 2621440 | tf_op jit(solution)/shard_map/pallas_call | solution.py:253
  74.1 0.3 collective-permute-done.10.in_ref
  74.4 0.6 shard_map.94
  75.1 2.7 %collective-permute-start.15 = (bf16[2,528,128]{2,1,0:T(8,128)(2,1)S(1)}, bf16[2,528,128]{2,1,0:T(8,128)(2,1)S(1)}, u32[]{:S(2)}, u32[]{:S(2)}) collective-permute-start(bf16[2,528,128]{2,1,0:T(8,128)(2,1)S(1)} %shard_map.94), channel_id=1, source_target_pairs={{0,4},{4,8},{8,12},{12,14},{14,10},{10,6},{6,2},{2,0},{1,3},{5,1},... | collective-permute-start | bytes 811016 | tf_op jit(solution)/shard_map/ppermute | solution.py:464
  77.7 0.6 shard_map.95
  78.3 2.5 %collective-permute-start.12 = (bf16[2,528,128]{2,1,0:T(8,128)(2,1)S(1)}, bf16[2,528,128]{2,1,0:T(8,128)(2,1)S(1)}, u32[]{:S(2)}, u32[]{:S(2)}) collective-permute-start(bf16[2,528,128]{2,1,0:T(8,128)(2,1)S(1)} %shard_map.95), channel_id=1, source_target_pairs={{0,4},{4,8},{8,12},{12,14},{14,10},{10,6},{6,2},{2,0},{1,3},{5,1},... | collective-permute-start | bytes 811016 | tf_op jit(solution)/shard_map/ppermute | solution.py:464
  80.9 0.6 collective-permute-done.14.page_ref
  81.5 2.2 %shard_map.96 = (f32[4,512,128]{2,1,0:T(8,128)S(1)}, bf16[4,16,128]{2,1,0:T(8,128)(2,1)S(1)}) custom-call(s32[1,128]{1,0:T(1,128)S(1)} %fusion.7.refs_0_, bf16[2064,128]{1,0:T(8,128)(2,1)S(1)} %collective-permute-done.13.refs_1_, bf16[32,2,64,512]{3,2,1,0:T(8,128)(2,1)S(1)} %copy-done.4), custom_call_target="tpu_custom_call" | custom-call | flops 1073741824 | bytes 2621440 | tf_op jit(solution)/shard_map/pallas_call | solution.py:253
  83.8 0.6 collective-permute-done.15.in_ref
  84.4 0.6 shard_map.97
  85.1 4.1 %collective-permute-start.17 = (bf16[2,528,128]{2,1,0:T(8,128)(2,1)S(1)}, bf16[2,528,128]{2,1,0:T(8,128)(2,1)S(1)}, u32[]{:S(2)}, u32[]{:S(2)}) collective-permute-start(bf16[2,528,128]{2,1,0:T(8,128)(2,1)S(1)} %shard_map.97), channel_id=1, source_target_pairs={{0,4},{4,8},{8,12},{12,14},{14,10},{10,6},{6,2},{2,0},{1,3},{5,1},... | collective-permute-start | bytes 811016 | tf_op jit(solution)/shard_map/ppermute | solution.py:464
  89.1 0.6 shard_map.98
  89.8 2.5 %collective-permute-start.16 = (bf16[2,528,128]{2,1,0:T(8,128)(2,1)S(1)}, bf16[2,528,128]{2,1,0:T(8,128)(2,1)S(1)}, u32[]{:S(2)}, u32[]{:S(2)}) collective-permute-start(bf16[2,528,128]{2,1,0:T(8,128)(2,1)S(1)} %shard_map.98), channel_id=1, source_target_pairs={{0,4},{4,8},{8,12},{12,14},{14,10},{10,6},{6,2},{2,0},{1,3},{5,1},... | collective-permute-start | bytes 811016 | tf_op jit(solution)/shard_map/ppermute | solution.py:464
  92.3 1.2 %shard_map.99 = bf16[32,2,64,512]{3,2,1,0:T(8,128)(2,1)} custom-call(s32[1]{0:T(128)} %bitcast.1.me_ref, s32[1]{0:T(128)} %bitcast.2.core_ref, s32[1,128]{1,0:T(1,128)S(1)} %fusion.1.refs_0_.near_ref, s32[1,128]{1,0:T(1,128)S(1)} %fusion.6.refs_0_.far_ref, ...), custom_call_target="tpu_custom_call", output_to_operand_aliasing={{}: (5, {})} | custom-call | flops 1 | bytes 1 | tf_op jit(solution)/shard_map/pallas_call | solution.py:294
  93.5 0.3 collective-permute-done.17.in_ref
  93.9 1.3 %shard_map.100.refs_0_ = bf16[1,64,4096]{2,1,0:T(8,128)(2,1)} custom-call(bf16[2,528,128]{2,1,0:T(8,128)(2,1)S(1)} %collective-permute-done.17.in_ref, f32[2,512,128]{2,1,0:T(8,128)S(1)} %get-tuple-element.57.acc_ref, bf16[2,16,128]{2,1,0:T(8,128)(2,1)S(1)} %get-tuple-element.58.stat_ref), custom_call_target="tpu_custom_call" | custom-call | tf_op jit(solution)/shard_map/pallas_call | solution.py:375
  95.1 1.6 %collective-permute-done.16.in_ref = bf16[2,528,128]{2,1,0:T(8,128)(2,1)S(1)} collective-permute-done((bf16[2,528,128]{2,1,0:T(8,128)(2,1)S(1)}, bf16[2,528,128]{2,1,0:T(8,128)(2,1)S(1)}, u32[]{:S(2)}, u32[]{:S(2)}) %collective-permute-start.16) | collective-permute-done | bytes 270368 | tf_op jit(solution)/shard_map/ppermute | solution.py:464
  96.8 1.3 %shard_map.101 = bf16[1,64,4096]{2,1,0:T(8,128)(2,1)} custom-call(bf16[2,528,128]{2,1,0:T(8,128)(2,1)S(1)} %collective-permute-done.16.in_ref, f32[2,512,128]{2,1,0:T(8,128)S(1)} %get-tuple-element.64.acc_ref, bf16[2,16,128]{2,1,0:T(8,128)(2,1)S(1)} %get-tuple-element.65.stat_ref, ...), custom_call_target="tpu_custom_call", output_to_operand_aliasing={{}: (3, {})} | custom-call | tf_op jit(solution)/shard_map/pallas_call | solution.py:375
  (23 shorter events, 0.1 us)
Async XLA Ops:
  0.6 11.4 %collective-permute-start = (bf16[1,64,4096]{2,1,0:T(8,128)(2,1)}, bf16[1,64,4096]{2,1,0:T(8,128)(2,1)S(1)}, u32[]{:S(2)}, u32[]{:S(2)}) collective-permute-start(bf16[1,64,4096]{2,1,0:T(8,128)(2,1)} %q_ref), channel_id=1, source_target_pairs={{0,4},{4,8},{8,12},{12,14},{14,10},{10,6},{6,2},{2,0},{1,3},{5,1},... | collective-permute-start | bytes 1572872 | tf_op jit(solution)/shard_map/ppermute | solution.py:464
  5.0 0.7 copy-start.8
  5.9 6.0 %collective-permute-start.1 = (bf16[16,128]{1,0:T(8,128)(2,1)S(1)}, bf16[16,128]{1,0:T(8,128)(2,1)S(1)}, u32[]{:S(2)}, u32[]{:S(2)}) collective-permute-start(bf16[16,128]{1,0:T(8,128)(2,1)S(1)} %shard_map.77.before_ref.lists_ref), channel_id=1, source_target_pairs={{0,4},{4,8},{8,12},{12,14},{14,10},{10,6},{6,2},{2,0},{1,3},{5,1},... | collective-permute-start | bytes 12296 | tf_op jit(solution)/shard_map/ppermute | solution.py:464
  7.5 2.2 %copy-start.5 = (bf16[32,2,64,512]{3,2,1,0:T(8,128)(2,1)S(1)}, bf16[32,2,64,512]{3,2,1,0:T(8,128)(2,1)}, u32[]{:S(2)}) copy-start(bf16[32,2,64,512]{3,2,1,0:T(8,128)(2,1)} %pages_ref.1) | copy-start | bytes 12582916
  10.0 2.0 %copy-start = (bf16[32,2,64,512]{3,2,1,0:T(8,128)(2,1)}, bf16[32,2,64,512]{3,2,1,0:T(8,128)(2,1)S(1)}, u32[]{:S(2)}) copy-start(bf16[32,2,64,512]{3,2,1,0:T(8,128)(2,1)S(1)} %shard_map.78.refs_2_.refs_3_) | copy-start | bytes 12582916
  12.1 9.3 %collective-permute-start.3 = (bf16[2064,128]{1,0:T(8,128)(2,1)S(1)}, bf16[2064,128]{1,0:T(8,128)(2,1)S(1)}, u32[]{:S(2)}, u32[]{:S(2)}) collective-permute-start(bf16[2064,128]{1,0:T(8,128)(2,1)S(1)} %shard_map.79.refs_1_), channel_id=1, source_target_pairs={{0,4},{4,8},{8,12},{12,14},{14,10},{10,6},{6,2},{2,0},{1,3},{5,1},... | collective-permute-start | bytes 1585160 | tf_op jit(solution)/shard_map/ppermute | solution.py:464
  13.7 2.2 %copy-start.1 = (bf16[32,2,64,512]{3,2,1,0:T(8,128)(2,1)S(1)}, bf16[32,2,64,512]{3,2,1,0:T(8,128)(2,1)}, u32[]{:S(2)}) copy-start(bf16[32,2,64,512]{3,2,1,0:T(8,128)(2,1)} %copy-done) | copy-start | bytes 12582916
  15.9 7.0 %copy-start.2 = (bf16[32,2,64,512]{3,2,1,0:T(8,128)(2,1)S(1)}, bf16[32,2,64,512]{3,2,1,0:T(8,128)(2,1)}, u32[]{:S(2)}) copy-start(bf16[32,2,64,512]{3,2,1,0:T(8,128)(2,1)} %copy-done) | copy-start | bytes 12582916
  18.7 9.4 %collective-permute-start.2 = (bf16[4,528,128]{2,1,0:T(8,128)(2,1)S(1)}, bf16[4,528,128]{2,1,0:T(8,128)(2,1)S(1)}, u32[]{:S(2)}, u32[]{:S(2)}) collective-permute-start(bf16[4,528,128]{2,1,0:T(8,128)(2,1)S(1)} %shard_map.81), channel_id=1, source_target_pairs={{0,4},{4,8},{8,12},{12,14},{14,10},{10,6},{6,2},{2,0},{1,3},{5,1},... | collective-permute-start | bytes 1622024 | tf_op jit(solution)/shard_map/ppermute | solution.py:464
  21.4 12.5 %collective-permute-start.5 = (bf16[2064,128]{1,0:T(8,128)(2,1)S(1)}, bf16[2064,128]{1,0:T(8,128)(2,1)S(1)}, u32[]{:S(2)}, u32[]{:S(2)}) collective-permute-start(bf16[2064,128]{1,0:T(8,128)(2,1)S(1)} %collective-permute-done.3.refs_1_), channel_id=1, source_target_pairs={{0,4},{4,8},{8,12},{12,14},{14,10},{10,6},{6,2},{2,0},{1,3},{5,1},... | collective-permute-start | bytes 1585160 | tf_op jit(solution)/shard_map/ppermute | solution.py:464
  28.2 14.0 %copy-start.7 = (bf16[1,64,4096]{2,1,0:T(8,128)(2,1)S(1)}, bf16[1,64,4096]{2,1,0:T(8,128)(2,1)}, u32[]{:S(2)}) copy-start(bf16[1,64,4096]{2,1,0:T(8,128)(2,1)} %q_ref) | copy-start | bytes 1572868
  28.2 14.1 %copy-start.6 = (bf16[1,2,64,512]{3,2,1,0:T(8,128)(2,1)S(1)}, bf16[1,2,64,512]{3,2,1,0:T(8,128)(2,1)}, u32[]{:S(2)}) copy-start(bf16[1,2,64,512]{3,2,1,0:T(8,128)(2,1)} %param.7) | copy-start | bytes 393220
  29.1 10.6 %collective-permute-start.4 = (bf16[4,528,128]{2,1,0:T(8,128)(2,1)S(1)}, bf16[4,528,128]{2,1,0:T(8,128)(2,1)S(1)}, u32[]{:S(2)}, u32[]{:S(2)}) collective-permute-start(bf16[4,528,128]{2,1,0:T(8,128)(2,1)S(1)} %shard_map.83), channel_id=1, source_target_pairs={{0,4},{4,8},{8,12},{12,14},{14,10},{10,6},{6,2},{2,0},{1,3},{5,1},... | collective-permute-start | bytes 1622024 | tf_op jit(solution)/shard_map/ppermute | solution.py:464
  33.8 11.5 %collective-permute-start.7 = (bf16[2064,128]{1,0:T(8,128)(2,1)S(1)}, bf16[2064,128]{1,0:T(8,128)(2,1)S(1)}, u32[]{:S(2)}, u32[]{:S(2)}) collective-permute-start(bf16[2064,128]{1,0:T(8,128)(2,1)S(1)} %collective-permute-done.5.refs_1_), channel_id=1, source_target_pairs={{0,4},{4,8},{8,12},{12,14},{14,10},{10,6},{6,2},{2,0},{1,3},{5,1},... | collective-permute-start | bytes 1585160 | tf_op jit(solution)/shard_map/ppermute | solution.py:464
  35.3 2.2 %copy-start.3 = (bf16[32,2,64,512]{3,2,1,0:T(8,128)(2,1)S(1)}, bf16[32,2,64,512]{3,2,1,0:T(8,128)(2,1)}, u32[]{:S(2)}) copy-start(bf16[32,2,64,512]{3,2,1,0:T(8,128)(2,1)} %copy-done) | copy-start | bytes 12582916
  37.5 4.8 %copy-start.4 = (bf16[32,2,64,512]{3,2,1,0:T(8,128)(2,1)S(1)}, bf16[32,2,64,512]{3,2,1,0:T(8,128)(2,1)}, u32[]{:S(2)}) copy-start(bf16[32,2,64,512]{3,2,1,0:T(8,128)(2,1)} %copy-done) | copy-start | bytes 12582916
  40.8 10.3 %collective-permute-start.6 = (bf16[4,528,128]{2,1,0:T(8,128)(2,1)S(1)}, bf16[4,528,128]{2,1,0:T(8,128)(2,1)S(1)}, u32[]{:S(2)}, u32[]{:S(2)}) collective-permute-start(bf16[4,528,128]{2,1,0:T(8,128)(2,1)S(1)} %shard_map.85), channel_id=1, source_target_pairs={{0,4},{4,8},{8,12},{12,14},{14,10},{10,6},{6,2},{2,0},{1,3},{5,1},... | collective-permute-start | bytes 1622024 | tf_op jit(solution)/shard_map/ppermute | solution.py:464
  45.3 11.5 %collective-permute-start.9 = (bf16[2064,128]{1,0:T(8,128)(2,1)S(1)}, bf16[2064,128]{1,0:T(8,128)(2,1)S(1)}, u32[]{:S(2)}, u32[]{:S(2)}) collective-permute-start(bf16[2064,128]{1,0:T(8,128)(2,1)S(1)} %collective-permute-done.7.refs_1_), channel_id=1, source_target_pairs={{0,4},{4,8},{8,12},{12,14},{14,10},{10,6},{6,2},{2,0},{1,3},{5,1},... | collective-permute-start | bytes 1585160 | tf_op jit(solution)/shard_map/ppermute | solution.py:464
  52.1 10.5 %collective-permute-start.8 = (bf16[4,528,128]{2,1,0:T(8,128)(2,1)S(1)}, bf16[4,528,128]{2,1,0:T(8,128)(2,1)S(1)}, u32[]{:S(2)}, u32[]{:S(2)}) collective-permute-start(bf16[4,528,128]{2,1,0:T(8,128)(2,1)S(1)} %shard_map.89), channel_id=1, source_target_pairs={{0,4},{4,8},{8,12},{12,14},{14,10},{10,6},{6,2},{2,0},{1,3},{5,1},... | collective-permute-start | bytes 1622024 | tf_op jit(solution)/shard_map/ppermute | solution.py:464
  56.7 11.5 %collective-permute-start.11 = (bf16[2064,128]{1,0:T(8,128)(2,1)S(1)}, bf16[2064,128]{1,0:T(8,128)(2,1)S(1)}, u32[]{:S(2)}, u32[]{:S(2)}) collective-permute-start(bf16[2064,128]{1,0:T(8,128)(2,1)S(1)} %collective-permute-done.9.refs_1_), channel_id=1, source_target_pairs={{0,4},{4,8},{8,12},{12,14},{14,10},{10,6},{6,2},{2,0},{1,3},{5,1},... | collective-permute-start | bytes 1585160 | tf_op jit(solution)/shard_map/ppermute | solution.py:464
  63.5 10.9 %collective-permute-start.10 = (bf16[4,528,128]{2,1,0:T(8,128)(2,1)S(1)}, bf16[4,528,128]{2,1,0:T(8,128)(2,1)S(1)}, u32[]{:S(2)}, u32[]{:S(2)}) collective-permute-start(bf16[4,528,128]{2,1,0:T(8,128)(2,1)S(1)} %shard_map.92), channel_id=1, source_target_pairs={{0,4},{4,8},{8,12},{12,14},{14,10},{10,6},{6,2},{2,0},{1,3},{5,1},... | collective-permute-start | bytes 1622024 | tf_op jit(solution)/shard_map/ppermute | solution.py:464
  68.2 13.4 %collective-permute-start.13 = (bf16[2064,128]{1,0:T(8,128)(2,1)S(1)}, bf16[2064,128]{1,0:T(8,128)(2,1)S(1)}, u32[]{:S(2)}, u32[]{:S(2)}) collective-permute-start(bf16[2064,128]{1,0:T(8,128)(2,1)S(1)} %collective-permute-done.11.refs_1_), channel_id=1, source_target_pairs={{0,4},{4,8},{8,12},{12,14},{14,10},{10,6},{6,2},{2,0},{1,3},{5,1},... | collective-permute-start | bytes 1585160 | tf_op jit(solution)/shard_map/ppermute | solution.py:464
  69.7 11.8 %collective-permute-start.14 = (bf16[1,2,64,512]{3,2,1,0:T(8,128)(2,1)S(1)}, bf16[1,2,64,512]{3,2,1,0:T(8,128)(2,1)S(1)}, u32[]{:S(2)}, u32[]{:S(2)}) collective-permute-start(bf16[1,2,64,512]{3,2,1,0:T(8,128)(2,1)S(1)} %copy-done.6), channel_id=1, source_target_pairs={{8,0},{10,2},{12,4},{14,6},{0,8},{2,10},{4,12},{6,14},{9,1},{11,3}... | collective-permute-start | bytes 393224 | tf_op jit(solution)/shard_map/ppermute | solution.py:26
  75.1 9.4 %collective-permute-start.15 = (bf16[2,528,128]{2,1,0:T(8,128)(2,1)S(1)}, bf16[2,528,128]{2,1,0:T(8,128)(2,1)S(1)}, u32[]{:S(2)}, u32[]{:S(2)}) collective-permute-start(bf16[2,528,128]{2,1,0:T(8,128)(2,1)S(1)} %shard_map.94), channel_id=1, source_target_pairs={{0,4},{4,8},{8,12},{12,14},{14,10},{10,6},{6,2},{2,0},{1,3},{5,1},... | collective-permute-start | bytes 811016 | tf_op jit(solution)/shard_map/ppermute | solution.py:464
  78.3 10.8 %collective-permute-start.12 = (bf16[2,528,128]{2,1,0:T(8,128)(2,1)S(1)}, bf16[2,528,128]{2,1,0:T(8,128)(2,1)S(1)}, u32[]{:S(2)}, u32[]{:S(2)}) collective-permute-start(bf16[2,528,128]{2,1,0:T(8,128)(2,1)S(1)} %shard_map.95), channel_id=1, source_target_pairs={{0,4},{4,8},{8,12},{12,14},{14,10},{10,6},{6,2},{2,0},{1,3},{5,1},... | collective-permute-start | bytes 811016 | tf_op jit(solution)/shard_map/ppermute | solution.py:464
  85.1 8.8 %collective-permute-start.17 = (bf16[2,528,128]{2,1,0:T(8,128)(2,1)S(1)}, bf16[2,528,128]{2,1,0:T(8,128)(2,1)S(1)}, u32[]{:S(2)}, u32[]{:S(2)}) collective-permute-start(bf16[2,528,128]{2,1,0:T(8,128)(2,1)S(1)} %shard_map.97), channel_id=1, source_target_pairs={{0,4},{4,8},{8,12},{12,14},{14,10},{10,6},{6,2},{2,0},{1,3},{5,1},... | collective-permute-start | bytes 811016 | tf_op jit(solution)/shard_map/ppermute | solution.py:464
  89.8 7.0 %collective-permute-start.16 = (bf16[2,528,128]{2,1,0:T(8,128)(2,1)S(1)}, bf16[2,528,128]{2,1,0:T(8,128)(2,1)S(1)}, u32[]{:S(2)}, u32[]{:S(2)}) collective-permute-start(bf16[2,528,128]{2,1,0:T(8,128)(2,1)S(1)} %shard_map.98), channel_id=1, source_target_pairs={{0,4},{4,8},{8,12},{12,14},{14,10},{10,6},{6,2},{2,0},{1,3},{5,1},... | collective-permute-start | bytes 811016 | tf_op jit(solution)/shard_map/ppermute | solution.py:464

commit v17 on v14

--- a/solution.py
+++ b/solution.py
@@ -263,26 +263,47 @@
     return [(out[2 * n], out[2 * n + 1]) for n in range(count)] + list(out[2 * count:])
 
 
-def place_kernel(half, column, me_ref, core_ref, near_ref, far_ref, page_ref, old_ref, out_ref, sem):
+def touch_kernel(held_ref, lists_ref, out_ref):
+    out_ref[...] = lists_ref[...]
+
+
+def touch(held, lists):
+    return pl.pallas_call(
+        touch_kernel,
+        out_shape=jax.ShapeDtypeStruct(lists.shape, lists.dtype),
+        in_specs=[VMEM, VMEM],
+        out_specs=VMEM,
+        compiler_params=pltpu.CompilerParams(vmem_limit_bytes=GRANT),
+        cost_estimate=LIGHT,
+    )(held, lists)
+
+
+def place_kernel(half, column, me_ref, core_ref, near_ref, far_ref, *refs):
+    keys_ref, values_ref, old_ref, out_ref, sems = refs
     me, core = me_ref[0], core_ref[0]
     is_near = ((me >= half) == (me % 2 == 0)) == (core % 2 == 0)
     slot = jnp.where(is_near, near_ref[0, column], far_ref[0, column])
-    copy = pltpu.make_async_copy(page_ref.at[0], out_ref.at[slot], sem)
-    copy.start()
-    copy.wait()
-
-
-def place_page(half, column, me, core, near, far, page, store):
+    copies = [
+        pltpu.make_async_copy(piece.at[0, 0], out_ref.at[slot, n], sems.at[n])
+        for n, piece in enumerate((keys_ref, values_ref))
+    ]
+    for copy in copies:
+        copy.start()
+    for copy in copies:
+        copy.wait()
+
+
+def place_page(half, column, me, core, near, far, pieces, store):
     return pl.pallas_call(
         functools.partial(place_kernel, half, column),
         out_shape=jax.ShapeDtypeStruct(store.shape, store.dtype),
-        in_specs=[SMEM] * 4 + [VMEM, HBM],
+        in_specs=[SMEM] * 4 + [VMEM, VMEM, HBM],
         out_specs=HBM,
-        scratch_shapes=[pltpu.SemaphoreType.DMA],
-        input_output_aliases={5: 0},
+        scratch_shapes=[pltpu.SemaphoreType.DMA((2,))],
+        input_output_aliases={6: 0},
         compiler_params=pltpu.CompilerParams(vmem_limit_bytes=GRANT),
         cost_estimate=LIGHT,
-    )(me[None], core[None], near, far, page, store)
+    )(me[None], core[None], near, far, *pieces, store)
 
 
 def blend(parts):
@@ -458,19 +479,23 @@
 
     first = onward(queries)
     mine = list_pages(cap, pages_dev, page_table, prefix_pages, new_slots)
-    moving = joined(first, onward(mine))
+    their_lists = onward(mine)
+    mine = touch(kv_pages, mine)
+    moving = joined(after(first, mine), their_lists)
 
     own_queries = None
     halves = [range(0, heads // 2), range(heads // 2, heads)]
     token = []
-    lists, own = {}, []
+    lists, own, arrived = {}, [], []
+    travel = (half - 1, half)
     for step in range(1, stores):
         came = after(moving, token)
         if step < stores - 1:
             moving = onward(came)
         lists[step] = listed(came, heads * rows)
-        if step == stores - 3:
-            arrived = shifted(after(suffix_key_value, token), "store", half)
+        if step + 1 in travel:
+            piece = suffix_key_value[:, len(arrived):len(arrived) + 1]
+            arrived.append(shifted(after(piece, token), "store", half))
         jobs = [(0, h, h) for h in range(heads)]
         keeping, pages = None, pages_dev // 2
         if step == 1:
@@ -493,15 +518,15 @@
                 blocks.append(merged(block, part, at, half_heads[0], len(half_heads)))
         partial = [onward(block) for block in blocks]
         token = blocks
-        if step == stores - 2:
-            token = [blocks, arrived]
+        if step in travel:
+            token = [blocks, arrived[travel.index(step)]]
         if step in (half - 1, half):
             if own_queries is None:
                 own_queries = joined(after(queries, token), mine)
             jobs = [(0, n, h) for n, h in enumerate(halves[len(own)])]
             x = after(own_queries, token)
             own += attend(sizes, jobs, listed(mine, 0), [x], kv_pages, suffix_key_value[0])
-            token = [blocks, own]
+            token = [token, own]
 
     quarter = stores // 4
     near, far = lists[quarter], lists[stores - quarter]

time: 98.4 us -> 98.7 us (level)
  local copies, waits for them, and re-layouts: 5.04 us -> 7.24 us
  waiting for transfers between devices: 21.2 us -> 19.3 us
    ppermute x17, waiting for transfers between devices: 20.9 us -> 16.6 us  [onward(): return lax.ppermute(x, ('store', 'tensor'), route)]
    ppermute x17, starting transfers between devices: 36 us -> 32.4 us  [onward(): return lax.ppermute(x, ('store', 'tensor'), route)]
    ppermute x1 -> x2, starting transfers between devices: 2.53 us -> 6.09 us  [shifted(): return lax.ppermute(block, axis, route)]
    ppermute x1 -> x2, waiting for transfers between devices: 0.27 us -> 2.7 us  [shifted(): return lax.ppermute(block, axis, route)]
    unnamed x14 -> x16, local copies, waits for them, and re-layouts: 5.04 us -> 7.23 us
  transfers between devices with their start and end apart: 18 -> 19, of which waited for: 13 -> 13; matrix products, arithmetic and copies ran while one was open for 0% -> 0% of each run, Pallas kernels for 30% -> 30%
where the time goes in v17:
time: 98.7 us; the launch traced here: 98.4 us
  starting transfers between devices  38.5 us (39%)
  Pallas kernels  31.1 us (32%)
  waiting for transfers between devices  19.3 us (20%)
  local copies, waits for them, and re-layouts  7.24 us (7%)
  between operations  2.33 us (2%)
    ppermute x17, starting transfers between devices, onward(): return lax.ppermute(x, ('store', 'tensor'), route)  32.4 us
    pallas_call x9, Pallas kernels, attend(): pl.pallas_call(functools.partial(attend_kernel, sizes + (count,), jobs, o...  20.3 us
    ppermute x17, waiting for transfers between devices, onward(): return lax.ppermute(x, ('store', 'tensor'), route)  16.6 us
    unnamed x16, local copies, waits for them, and re-layouts  7.23 us
    pallas_call x11, Pallas kernels, call(): pl.pallas_call(kernel, out_shape=shape, in_specs=[VMEM] * len(args), out_...  6.7 us
    ppermute x2, starting transfers between devices, shifted(): return lax.ppermute(block, axis, route)  6.09 us
    ppermute x2, waiting for transfers between devices, shifted(): return lax.ppermute(block, axis, route)  2.7 us
    pallas_call x2, Pallas kernels, finish(): pl.pallas_call(functools.partial(final_kernel, suffix, first), out_shape=...  2.53 us
  transfers between devices with their start and end apart: 19, of which 13 were waited for; matrix products, arithmetic and copies ran while one was open for 0% of the time, Pallas kernels for 30%

profile of v17, /device:TPU:0, one launch (start us, length us, event | category | flops | bytes accessed | tf_op | source)
XLA Modules:
  0.0 98.4 jit_solution(18059024260178000255)
XLA Ops:
  0.6 3.1 %collective-permute-start = (bf16[1,64,4096]{2,1,0:T(8,128)(2,1)}, bf16[1,64,4096]{2,1,0:T(8,128)(2,1)S(1)}, u32[]{:S(2)}, u32[]{:S(2)}) collective-permute-start(bf16[1,64,4096]{2,1,0:T(8,128)(2,1)} %q_ref), channel_id=1, source_target_pairs={{0,4},{4,8},{8,12},{12,14},{14,10},{10,6},{6,2},{2,0},{1,3},{5,1},... | collective-permute-start | bytes 1572872 | tf_op jit(solution)/shard_map/ppermute | solution.py:467
  5.0 0.6 copy-done.7
  5.7 0.3 shard_map.77.lists_ref
  5.9 1.6 %collective-permute-start.1 = (bf16[16,128]{1,0:T(8,128)(2,1)S(1)}, bf16[16,128]{1,0:T(8,128)(2,1)S(1)}, u32[]{:S(2)}, u32[]{:S(2)}) collective-permute-start(bf16[16,128]{1,0:T(8,128)(2,1)S(1)} %shard_map.77.lists_ref), channel_id=1, source_target_pairs={{0,4},{4,8},{8,12},{12,14},{14,10},{10,6},{6,2},{2,0},{1,3},{5,1},... | collective-permute-start | bytes 12296 | tf_op jit(solution)/shard_map/ppermute | solution.py:467
  7.5 2.2 %copy-done = bf16[32,2,64,512]{3,2,1,0:T(8,128)(2,1)S(1)} copy-done((bf16[32,2,64,512]{3,2,1,0:T(8,128)(2,1)S(1)}, bf16[32,2,64,512]{3,2,1,0:T(8,128)(2,1)}, u32[]{:S(2)}) %copy-start) | copy-done | bytes 4194328
  9.7 1.3 %collective-permute-done.q_ref = bf16[1,64,4096]{2,1,0:T(8,128)(2,1)S(1)} collective-permute-done((bf16[1,64,4096]{2,1,0:T(8,128)(2,1)}, bf16[1,64,4096]{2,1,0:T(8,128)(2,1)S(1)}, u32[]{:S(2)}, u32[]{:S(2)}) %collective-permute-start) | collective-permute-done | bytes 524320 | tf_op jit(solution)/shard_map/ppermute | solution.py:467
  11.0 0.0 collective-permute-done.1.lists_ref
  11.1 0.1 shard_map.79.refs_1_
  11.2 2.1 %collective-permute-start.3 = (bf16[2064,128]{1,0:T(8,128)(2,1)S(1)}, bf16[2064,128]{1,0:T(8,128)(2,1)S(1)}, u32[]{:S(2)}, u32[]{:S(2)}) collective-permute-start(bf16[2064,128]{1,0:T(8,128)(2,1)S(1)} %shard_map.79.refs_1_), channel_id=1, source_target_pairs={{0,4},{4,8},{8,12},{12,14},{14,10},{10,6},{6,2},{2,0},{1,3},{5,1},... | collective-permute-start | bytes 1585160 | tf_op jit(solution)/shard_map/ppermute | solution.py:467
  13.3 2.2 %copy-done.1 = bf16[32,2,64,512]{3,2,1,0:T(8,128)(2,1)S(1)} copy-done((bf16[32,2,64,512]{3,2,1,0:T(8,128)(2,1)S(1)}, bf16[32,2,64,512]{3,2,1,0:T(8,128)(2,1)}, u32[]{:S(2)}) %copy-start.1) | copy-done | bytes 4194328
  15.5 2.7 %shard_map.80 = (f32[4,512,128]{2,1,0:T(8,128)S(1)}, bf16[4,16,128]{2,1,0:T(8,128)(2,1)S(1)}, bf16[32,2,64,512]{3,2,1,0:T(8,128)(2,1)}) custom-call(s32[1,128]{1,0:T(1,128)S(1)} %fusion.refs_0_, bf16[2064,128]{1,0:T(8,128)(2,1)S(1)} %shard_map.79.refs_1_, bf16[32,2,64,512]{3,2,1,0:T(8,128)(2,1)S(1)} %copy-done.1), custom_call_target="tpu_custom_call" | custom-call | flops 1073741824 | bytes 2621440 | tf_op jit(solution)/shard_map/pallas_call | solution.py:253
  18.2 0.1 shard_map.81
  18.3 1.6 %collective-permute-start.2 = (bf16[4,528,128]{2,1,0:T(8,128)(2,1)S(1)}, bf16[4,528,128]{2,1,0:T(8,128)(2,1)S(1)}, u32[]{:S(2)}, u32[]{:S(2)}) collective-permute-start(bf16[4,528,128]{2,1,0:T(8,128)(2,1)S(1)} %shard_map.81), channel_id=1, source_target_pairs={{0,4},{4,8},{8,12},{12,14},{14,10},{10,6},{6,2},{2,0},{1,3},{5,1},... | collective-permute-start | bytes 1622024 | tf_op jit(solution)/shard_map/ppermute | solution.py:467
  19.9 0.5 collective-permute-done.3.refs_1_
  20.4 2.1 %collective-permute-start.5 = (bf16[2064,128]{1,0:T(8,128)(2,1)S(1)}, bf16[2064,128]{1,0:T(8,128)(2,1)S(1)}, u32[]{:S(2)}, u32[]{:S(2)}) collective-permute-start(bf16[2064,128]{1,0:T(8,128)(2,1)S(1)} %collective-permute-done.3.refs_1_), channel_id=1, source_target_pairs={{0,4},{4,8},{8,12},{12,14},{14,10},{10,6},{6,2},{2,0},{1,3},{5,1},... | collective-permute-start | bytes 1585160 | tf_op jit(solution)/shard_map/ppermute | solution.py:467
  22.5 0.0 copy-start.5
  22.5 2.9 %shard_map.82 = (f32[4,512,128]{2,1,0:T(8,128)S(1)}, bf16[4,16,128]{2,1,0:T(8,128)(2,1)S(1)}, bf16[32,2,64,512]{3,2,1,0:T(8,128)(2,1)}) custom-call(s32[1,128]{1,0:T(1,128)S(1)} %fusion.1.refs_0_.near_ref, bf16[2064,128]{1,0:T(8,128)(2,1)S(1)} %collective-permute-done.3.refs_1_, ...), custom_call_target="tpu_custom_call", output_to_operand_aliasing={{2}: (3, {})} | custom-call | flops 1073741824 | bytes 2621440 | tf_op jit(solution)/shard_map/pallas_call | solution.py:253
  25.5 2.2 %collective-permute-done.2.in_ref = bf16[4,528,128]{2,1,0:T(8,128)(2,1)S(1)} collective-permute-done((bf16[4,528,128]{2,1,0:T(8,128)(2,1)S(1)}, bf16[4,528,128]{2,1,0:T(8,128)(2,1)S(1)}, u32[]{:S(2)}, u32[]{:S(2)}) %collective-permute-start.2) | collective-permute-done | bytes 540704 | tf_op jit(solution)/shard_map/ppermute | solution.py:467
  27.7 1.0 shard_map.83
  28.7 1.6 %collective-permute-start.4 = (bf16[4,528,128]{2,1,0:T(8,128)(2,1)S(1)}, bf16[4,528,128]{2,1,0:T(8,128)(2,1)S(1)}, u32[]{:S(2)}, u32[]{:S(2)}) collective-permute-start(bf16[4,528,128]{2,1,0:T(8,128)(2,1)S(1)} %shard_map.83), channel_id=1, source_target_pairs={{0,4},{4,8},{8,12},{12,14},{14,10},{10,6},{6,2},{2,0},{1,3},{5,1},... | collective-permute-start | bytes 1622024 | tf_op jit(solution)/shard_map/ppermute | solution.py:467
  30.3 3.0 %collective-permute-done.5.refs_1_ = bf16[2064,128]{1,0:T(8,128)(2,1)S(1)} collective-permute-done((bf16[2064,128]{1,0:T(8,128)(2,1)S(1)}, bf16[2064,128]{1,0:T(8,128)(2,1)S(1)}, u32[]{:S(2)}, u32[]{:S(2)}) %collective-permute-start.5) | collective-permute-done | bytes 528416 | tf_op jit(solution)/shard_map/ppermute | solution.py:467
  33.4 1.6 %collective-permute-start.7 = (bf16[2064,128]{1,0:T(8,128)(2,1)S(1)}, bf16[2064,128]{1,0:T(8,128)(2,1)S(1)}, u32[]{:S(2)}, u32[]{:S(2)}) collective-permute-start(bf16[2064,128]{1,0:T(8,128)(2,1)S(1)} %collective-permute-done.5.refs_1_), channel_id=1, source_target_pairs={{0,4},{4,8},{8,12},{12,14},{14,10},{10,6},{6,2},{2,0},{1,3},{5,1},... | collective-permute-start | bytes 1585160 | tf_op jit(solution)/shard_map/ppermute | solution.py:467
  35.0 2.6 %collective-permute-start.8 = (bf16[1,1,64,512]{3,2,1,0:T(8,128)(2,1)S(1)}, bf16[1,1,64,512]{3,2,1,0:T(8,128)(2,1)S(1)}, u32[]{:S(2)}, u32[]{:S(2)}) collective-permute-start(bf16[1,1,64,512]{3,2,1,0:T(8,128)(2,1)S(1)} %get-tuple-element.56), channel_id=1, source_target_pairs={{8,0},{10,2},{12,4},{14,6},{0,8},{2,10},{4,12},{6,14},{9,1},{11,3}... | collective-permute-start | bytes 196616 | tf_op jit(solution)/shard_map/ppermute | solution.py:26
  37.6 2.2 %copy-done.3 = bf16[32,2,64,512]{3,2,1,0:T(8,128)(2,1)S(1)} copy-done((bf16[32,2,64,512]{3,2,1,0:T(8,128)(2,1)S(1)}, bf16[32,2,64,512]{3,2,1,0:T(8,128)(2,1)}, u32[]{:S(2)}) %copy-start.3) | copy-done | bytes 4194328
  39.8 2.2 %shard_map.84 = (f32[4,512,128]{2,1,0:T(8,128)S(1)}, bf16[4,16,128]{2,1,0:T(8,128)(2,1)S(1)}) custom-call(s32[1,128]{1,0:T(1,128)S(1)} %fusion.2.refs_0_, bf16[2064,128]{1,0:T(8,128)(2,1)S(1)} %collective-permute-done.5.refs_1_, bf16[32,2,64,512]{3,2,1,0:T(8,128)(2,1)S(1)} %copy-done.3), custom_call_target="tpu_custom_call" | custom-call | flops 1073741824 | bytes 2621440 | tf_op jit(solution)/shard_map/pallas_call | solution.py:253
  42.0 1.0 %shard_map.85 = bf16[4,528,128]{2,1,0:T(8,128)(2,1)S(1)} custom-call(bf16[4,528,128]{2,1,0:T(8,128)(2,1)S(1)} %collective-permute-done.4.in_ref, f32[4,512,128]{2,1,0:T(8,128)S(1)} %get-tuple-element.53.acc_ref, bf16[4,16,128]{2,1,0:T(8,128)(2,1)S(1)} %get-tuple-element.54.stat_ref), custom_call_target="tpu_custom_call" | custom-call | flops 1605632 | bytes 3211264 | tf_op jit(solution)/shard_map/pallas_call | solution.py:394
  43.0 0.7 collective-permute-start.6
  43.7 1.7 %collective-permute-done.8.refs_0_ = bf16[1,1,64,512]{3,2,1,0:T(8,128)(2,1)S(1)} collective-permute-done((bf16[1,1,64,512]{3,2,1,0:T(8,128)(2,1)S(1)}, bf16[1,1,64,512]{3,2,1,0:T(8,128)(2,1)S(1)}, u32[]{:S(2)}, u32[]{:S(2)}) %collective-permute-start.8) | collective-permute-done | bytes 65568 | tf_op jit(solution)/shard_map/ppermute | solution.py:26
  45.3 0.1 shard_map.86.refs_1_
  45.4 1.8 %shard_map.87 = (f32[2,512,128]{2,1,0:T(8,128)S(1)}, bf16[2,16,128]{2,1,0:T(8,128)(2,1)S(1)}) custom-call(s32[1,128]{1,0:T(1,128)S(1)} %fusion.3.refs_0_, bf16[2064,128]{1,0:T(8,128)(2,1)S(1)} %shard_map.86.refs_1_, bf16[2,64,512]{2,1,0:T(8,128)(2,1)S(1)} %bitcast.3, bf16[32,2,64,512]{3,2,1,0:T(8,128)(2,1)S(1)} %copy-done.4), custom_call_target="tpu_custom_call" | custom-call | flops 536870912 | bytes 1310720 | tf_op jit(solution)/shard_map/pallas_call | solution.py:253
  47.2 3.2 %collective-permute-start.10 = (bf16[2064,128]{1,0:T(8,128)(2,1)S(1)}, bf16[2064,128]{1,0:T(8,128)(2,1)S(1)}, u32[]{:S(2)}, u32[]{:S(2)}) collective-permute-start(bf16[2064,128]{1,0:T(8,128)(2,1)S(1)} %collective-permute-done.7.refs_1_), channel_id=1, source_target_pairs={{0,4},{4,8},{8,12},{12,14},{14,10},{10,6},{6,2},{2,0},{1,3},{5,1},... | collective-permute-start | bytes 1585160 | tf_op jit(solution)/shard_map/ppermute | solution.py:467
  50.4 3.5 %collective-permute-start.11 = (bf16[1,1,64,512]{3,2,1,0:T(8,128)(2,1)S(1)}, bf16[1,1,64,512]{3,2,1,0:T(8,128)(2,1)S(1)}, u32[]{:S(2)}, u32[]{:S(2)}) collective-permute-start(bf16[1,1,64,512]{3,2,1,0:T(8,128)(2,1)S(1)} %get-tuple-element.65), channel_id=1, source_target_pairs={{8,0},{10,2},{12,4},{14,6},{0,8},{2,10},{4,12},{6,14},{9,1},{11,3}... | collective-permute-start | bytes 196616 | tf_op jit(solution)/shard_map/ppermute | solution.py:26
  53.9 2.2 %shard_map.88 = (f32[4,512,128]{2,1,0:T(8,128)S(1)}, bf16[4,16,128]{2,1,0:T(8,128)(2,1)S(1)}) custom-call(s32[1,128]{1,0:T(1,128)S(1)} %fusion.4.refs_0_, bf16[2064,128]{1,0:T(8,128)(2,1)S(1)} %collective-permute-done.7.refs_1_, bf16[32,2,64,512]{3,2,1,0:T(8,128)(2,1)S(1)} %copy-done.4), custom_call_target="tpu_custom_call" | custom-call | flops 1073741824 | bytes 2621440 | tf_op jit(solution)/shard_map/pallas_call | solution.py:253
  56.2 0.0 collective-permute-done.6.in_ref
  56.2 1.0 shard_map.89
  57.2 0.1 collective-permute-start.9
  57.3 1.0 %collective-permute-done.11.refs_1_ = bf16[1,1,64,512]{3,2,1,0:T(8,128)(2,1)S(1)} collective-permute-done((bf16[1,1,64,512]{3,2,1,0:T(8,128)(2,1)S(1)}, bf16[1,1,64,512]{3,2,1,0:T(8,128)(2,1)S(1)}, u32[]{:S(2)}, u32[]{:S(2)}) %collective-permute-start.11) | collective-permute-done | bytes 65568 | tf_op jit(solution)/shard_map/ppermute | solution.py:26
  58.3 1.8 %shard_map.90 = (f32[2,512,128]{2,1,0:T(8,128)S(1)}, bf16[2,16,128]{2,1,0:T(8,128)(2,1)S(1)}) custom-call(s32[1,128]{1,0:T(1,128)S(1)} %fusion.3.refs_0_, bf16[2064,128]{1,0:T(8,128)(2,1)S(1)} %shard_map.86.refs_1_, bf16[2,64,512]{2,1,0:T(8,128)(2,1)S(1)} %bitcast.4, bf16[32,2,64,512]{3,2,1,0:T(8,128)(2,1)S(1)} %copy-done.4), custom_call_target="tpu_custom_call" | custom-call | flops 536870912 | bytes 1310720 | tf_op jit(solution)/shard_map/pallas_call | solution.py:253
  60.1 0.0 collective-permute-done.10.refs_1_
  60.1 4.3 %collective-permute-start.13 = (bf16[2064,128]{1,0:T(8,128)(2,1)S(1)}, bf16[2064,128]{1,0:T(8,128)(2,1)S(1)}, u32[]{:S(2)}, u32[]{:S(2)}) collective-permute-start(bf16[2064,128]{1,0:T(8,128)(2,1)S(1)} %collective-permute-done.10.refs_1_), channel_id=1, source_target_pairs={{0,4},{4,8},{8,12},{12,14},{14,10},{10,6},{6,2},{2,0},{1,3},{5,1},... | collective-permute-start | bytes 1585160 | tf_op jit(solution)/shard_map/ppermute | solution.py:467
  64.4 2.2 %shard_map.91 = (f32[4,512,128]{2,1,0:T(8,128)S(1)}, bf16[4,16,128]{2,1,0:T(8,128)(2,1)S(1)}) custom-call(s32[1,128]{1,0:T(1,128)S(1)} %fusion.5.refs_0_, bf16[2064,128]{1,0:T(8,128)(2,1)S(1)} %collective-permute-done.10.refs_1_, bf16[32,2,64,512]{3,2,1,0:T(8,128)(2,1)S(1)} %copy-done.4), custom_call_target="tpu_custom_call" | custom-call | flops 1073741824 | bytes 2621440 | tf_op jit(solution)/shard_map/pallas_call | solution.py:253
  66.6 1.0 shard_map.92
  67.6 1.8 %collective-permute-start.12 = (bf16[4,528,128]{2,1,0:T(8,128)(2,1)S(1)}, bf16[4,528,128]{2,1,0:T(8,128)(2,1)S(1)}, u32[]{:S(2)}, u32[]{:S(2)}) collective-permute-start(bf16[4,528,128]{2,1,0:T(8,128)(2,1)S(1)} %shard_map.92), channel_id=1, source_target_pairs={{0,4},{4,8},{8,12},{12,14},{14,10},{10,6},{6,2},{2,0},{1,3},{5,1},... | collective-permute-start | bytes 1622024 | tf_op jit(solution)/shard_map/ppermute | solution.py:467
  69.4 3.2 %collective-permute-done.13.refs_1_ = bf16[2064,128]{1,0:T(8,128)(2,1)S(1)} collective-permute-done((bf16[2064,128]{1,0:T(8,128)(2,1)S(1)}, bf16[2064,128]{1,0:T(8,128)(2,1)S(1)}, u32[]{:S(2)}, u32[]{:S(2)}) %collective-permute-start.13) | collective-permute-done | bytes 528416 | tf_op jit(solution)/shard_map/ppermute | solution.py:467
  72.6 1.4 %collective-permute-start.15 = (bf16[2064,128]{1,0:T(8,128)(2,1)S(1)}, bf16[2064,128]{1,0:T(8,128)(2,1)S(1)}, u32[]{:S(2)}, u32[]{:S(2)}) collective-permute-start(bf16[2064,128]{1,0:T(8,128)(2,1)S(1)} %collective-permute-done.13.refs_1_), channel_id=1, source_target_pairs={{0,4},{4,8},{8,12},{12,14},{14,10},{10,6},{6,2},{2,0},{1,3},{5,1},... | collective-permute-start | bytes 1585160 | tf_op jit(solution)/shard_map/ppermute | solution.py:467
  74.0 2.2 %shard_map.93 = (f32[4,512,128]{2,1,0:T(8,128)S(1)}, bf16[4,16,128]{2,1,0:T(8,128)(2,1)S(1)}) custom-call(s32[1,128]{1,0:T(1,128)S(1)} %fusion.6.refs_0_.far_ref, bf16[2064,128]{1,0:T(8,128)(2,1)S(1)} %collective-permute-done.13.refs_1_, bf16[32,2,64,512]{3,2,1,0:T(8,128)(2,1)S(1)} %copy-done.4), custom_call_target="tpu_custom_call" | custom-call | flops 1073741824 | bytes 2621440 | tf_op jit(solution)/shard_map/pallas_call | solution.py:253
  76.3 2.1 %collective-permute-done.12.in_ref = bf16[4,528,128]{2,1,0:T(8,128)(2,1)S(1)} collective-permute-done((bf16[4,528,128]{2,1,0:T(8,128)(2,1)S(1)}, bf16[4,528,128]{2,1,0:T(8,128)(2,1)S(1)}, u32[]{:S(2)}, u32[]{:S(2)}) %collective-permute-start.12) | collective-permute-done | bytes 540704 | tf_op jit(solution)/shard_map/ppermute | solution.py:467
  78.4 0.6 shard_map.94
  79.0 1.5 %collective-permute-start.16 = (bf16[2,528,128]{2,1,0:T(8,128)(2,1)S(1)}, bf16[2,528,128]{2,1,0:T(8,128)(2,1)S(1)}, u32[]{:S(2)}, u32[]{:S(2)}) collective-permute-start(bf16[2,528,128]{2,1,0:T(8,128)(2,1)S(1)} %shard_map.94), channel_id=1, source_target_pairs={{0,4},{4,8},{8,12},{12,14},{14,10},{10,6},{6,2},{2,0},{1,3},{5,1},... | collective-permute-start | bytes 811016 | tf_op jit(solution)/shard_map/ppermute | solution.py:467
  80.5 0.6 shard_map.95
  81.1 2.5 %collective-permute-start.14 = (bf16[2,528,128]{2,1,0:T(8,128)(2,1)S(1)}, bf16[2,528,128]{2,1,0:T(8,128)(2,1)S(1)}, u32[]{:S(2)}, u32[]{:S(2)}) collective-permute-start(bf16[2,528,128]{2,1,0:T(8,128)(2,1)S(1)} %shard_map.95), channel_id=1, source_target_pairs={{0,4},{4,8},{8,12},{12,14},{14,10},{10,6},{6,2},{2,0},{1,3},{5,1},... | collective-permute-start | bytes 811016 | tf_op jit(solution)/shard_map/ppermute | solution.py:467
  83.7 0.4 collective-permute-done.15.refs_1_
  84.1 2.2 %shard_map.96 = (f32[4,512,128]{2,1,0:T(8,128)S(1)}, bf16[4,16,128]{2,1,0:T(8,128)(2,1)S(1)}) custom-call(s32[1,128]{1,0:T(1,128)S(1)} %fusion.7.refs_0_, bf16[2064,128]{1,0:T(8,128)(2,1)S(1)} %collective-permute-done.15.refs_1_, bf16[32,2,64,512]{3,2,1,0:T(8,128)(2,1)S(1)} %copy-done.4), custom_call_target="tpu_custom_call" | custom-call | flops 1073741824 | bytes 2621440 | tf_op jit(solution)/shard_map/pallas_call | solution.py:253
  86.3 0.7 collective-permute-done.16.in_ref
  87.0 0.6 shard_map.97
  87.6 1.5 %collective-permute-start.18 = (bf16[2,528,128]{2,1,0:T(8,128)(2,1)S(1)}, bf16[2,528,128]{2,1,0:T(8,128)(2,1)S(1)}, u32[]{:S(2)}, u32[]{:S(2)}) collective-permute-start(bf16[2,528,128]{2,1,0:T(8,128)(2,1)S(1)} %shard_map.97), channel_id=1, source_target_pairs={{0,4},{4,8},{8,12},{12,14},{14,10},{10,6},{6,2},{2,0},{1,3},{5,1},... | collective-permute-start | bytes 811016 | tf_op jit(solution)/shard_map/ppermute | solution.py:467
  89.1 0.8 collective-permute-done.14.in_ref
  89.9 0.6 shard_map.98
  90.5 1.7 %collective-permute-start.17 = (bf16[2,528,128]{2,1,0:T(8,128)(2,1)S(1)}, bf16[2,528,128]{2,1,0:T(8,128)(2,1)S(1)}, u32[]{:S(2)}, u32[]{:S(2)}) collective-permute-start(bf16[2,528,128]{2,1,0:T(8,128)(2,1)S(1)} %shard_map.98), channel_id=1, source_target_pairs={{0,4},{4,8},{8,12},{12,14},{14,10},{10,6},{6,2},{2,0},{1,3},{5,1},... | collective-permute-start | bytes 811016 | tf_op jit(solution)/shard_map/ppermute | solution.py:467
  92.2 1.2 %shard_map.99 = bf16[32,2,64,512]{3,2,1,0:T(8,128)(2,1)} custom-call(s32[1]{0:T(128)} %bitcast.1.me_ref, s32[1]{0:T(128)} %bitcast.2.core_ref, s32[1,128]{1,0:T(1,128)S(1)} %fusion.1.refs_0_.near_ref, s32[1,128]{1,0:T(1,128)S(1)} %fusion.6.refs_0_.far_ref, ...), custom_call_target="tpu_custom_call", output_to_operand_aliasing={{}: (6, {})} | custom-call | flops 1 | bytes 1 | tf_op jit(solution)/shard_map/pallas_call | solution.py:297
  93.5 0.6 collective-permute-done.18.in_ref
  94.1 1.3 %shard_map.100.refs_0_ = bf16[1,64,4096]{2,1,0:T(8,128)(2,1)} custom-call(bf16[2,528,128]{2,1,0:T(8,128)(2,1)S(1)} %collective-permute-done.18.in_ref, f32[2,512,128]{2,1,0:T(8,128)S(1)} %get-tuple-element.59.acc_ref, bf16[2,16,128]{2,1,0:T(8,128)(2,1)S(1)} %get-tuple-element.60.stat_ref), custom_call_target="tpu_custom_call" | custom-call | tf_op jit(solution)/shard_map/pallas_call | solution.py:378
  95.4 1.6 %collective-permute-done.17.in_ref = bf16[2,528,128]{2,1,0:T(8,128)(2,1)S(1)} collective-permute-done((bf16[2,528,128]{2,1,0:T(8,128)(2,1)S(1)}, bf16[2,528,128]{2,1,0:T(8,128)(2,1)S(1)}, u32[]{:S(2)}, u32[]{:S(2)}) %collective-permute-start.17) | collective-permute-done | bytes 270368 | tf_op jit(solution)/shard_map/ppermute | solution.py:467
  97.0 1.3 %shard_map.101 = bf16[1,64,4096]{2,1,0:T(8,128)(2,1)} custom-call(bf16[2,528,128]{2,1,0:T(8,128)(2,1)S(1)} %collective-permute-done.17.in_ref, f32[2,512,128]{2,1,0:T(8,128)S(1)} %get-tuple-element.67.acc_ref, bf16[2,16,128]{2,1,0:T(8,128)(2,1)S(1)} %get-tuple-element.68.stat_ref, ...), custom_call_target="tpu_custom_call", output_to_operand_aliasing={{}: (3, {})} | custom-call | tf_op jit(solution)/shard_map/pallas_call | solution.py:378
  (24 shorter events, 0.1 us)
Async XLA Ops:
  0.6 10.4 %collective-permute-start = (bf16[1,64,4096]{2,1,0:T(8,128)(2,1)}, bf16[1,64,4096]{2,1,0:T(8,128)(2,1)S(1)}, u32[]{:S(2)}, u32[]{:S(2)}) collective-permute-start(bf16[1,64,4096]{2,1,0:T(8,128)(2,1)} %q_ref), channel_id=1, source_target_pairs={{0,4},{4,8},{8,12},{12,14},{14,10},{10,6},{6,2},{2,0},{1,3},{5,1},... | collective-permute-start | bytes 1572872 | tf_op jit(solution)/shard_map/ppermute | solution.py:467
  5.0 0.7 copy-start.7
  5.9 5.1 %collective-permute-start.1 = (bf16[16,128]{1,0:T(8,128)(2,1)S(1)}, bf16[16,128]{1,0:T(8,128)(2,1)S(1)}, u32[]{:S(2)}, u32[]{:S(2)}) collective-permute-start(bf16[16,128]{1,0:T(8,128)(2,1)S(1)} %shard_map.77.lists_ref), channel_id=1, source_target_pairs={{0,4},{4,8},{8,12},{12,14},{14,10},{10,6},{6,2},{2,0},{1,3},{5,1},... | collective-permute-start | bytes 12296 | tf_op jit(solution)/shard_map/ppermute | solution.py:467
  7.5 2.2 %copy-start = (bf16[32,2,64,512]{3,2,1,0:T(8,128)(2,1)S(1)}, bf16[32,2,64,512]{3,2,1,0:T(8,128)(2,1)}, u32[]{:S(2)}) copy-start(bf16[32,2,64,512]{3,2,1,0:T(8,128)(2,1)} %refs_2_.13) | copy-start | bytes 12582916
  11.2 9.3 %collective-permute-start.3 = (bf16[2064,128]{1,0:T(8,128)(2,1)S(1)}, bf16[2064,128]{1,0:T(8,128)(2,1)S(1)}, u32[]{:S(2)}, u32[]{:S(2)}) collective-permute-start(bf16[2064,128]{1,0:T(8,128)(2,1)S(1)} %shard_map.79.refs_1_), channel_id=1, source_target_pairs={{0,4},{4,8},{8,12},{12,14},{14,10},{10,6},{6,2},{2,0},{1,3},{5,1},... | collective-permute-start | bytes 1585160 | tf_op jit(solution)/shard_map/ppermute | solution.py:467
  13.3 2.2 %copy-start.1 = (bf16[32,2,64,512]{3,2,1,0:T(8,128)(2,1)S(1)}, bf16[32,2,64,512]{3,2,1,0:T(8,128)(2,1)}, u32[]{:S(2)}) copy-start(bf16[32,2,64,512]{3,2,1,0:T(8,128)(2,1)} %refs_2_.13) | copy-start | bytes 12582916
  15.5 7.0 %copy-start.2 = (bf16[32,2,64,512]{3,2,1,0:T(8,128)(2,1)S(1)}, bf16[32,2,64,512]{3,2,1,0:T(8,128)(2,1)}, u32[]{:S(2)}) copy-start(bf16[32,2,64,512]{3,2,1,0:T(8,128)(2,1)} %refs_2_.13) | copy-start | bytes 12582916
  18.3 9.4 %collective-permute-start.2 = (bf16[4,528,128]{2,1,0:T(8,128)(2,1)S(1)}, bf16[4,528,128]{2,1,0:T(8,128)(2,1)S(1)}, u32[]{:S(2)}, u32[]{:S(2)}) collective-permute-start(bf16[4,528,128]{2,1,0:T(8,128)(2,1)S(1)} %shard_map.81), channel_id=1, source_target_pairs={{0,4},{4,8},{8,12},{12,14},{14,10},{10,6},{6,2},{2,0},{1,3},{5,1},... | collective-permute-start | bytes 1622024 | tf_op jit(solution)/shard_map/ppermute | solution.py:467
  20.4 12.9 %collective-permute-start.5 = (bf16[2064,128]{1,0:T(8,128)(2,1)S(1)}, bf16[2064,128]{1,0:T(8,128)(2,1)S(1)}, u32[]{:S(2)}, u32[]{:S(2)}) collective-permute-start(bf16[2064,128]{1,0:T(8,128)(2,1)S(1)} %collective-permute-done.3.refs_1_), channel_id=1, source_target_pairs={{0,4},{4,8},{8,12},{12,14},{14,10},{10,6},{6,2},{2,0},{1,3},{5,1},... | collective-permute-start | bytes 1585160 | tf_op jit(solution)/shard_map/ppermute | solution.py:467
  22.5 12.4 %copy-start.5 = (bf16[1,2,64,512]{3,2,1,0:T(8,128)(2,1)S(1)}, bf16[1,2,64,512]{3,2,1,0:T(8,128)(2,1)}, u32[]{:S(2)}) copy-start(bf16[1,2,64,512]{3,2,1,0:T(8,128)(2,1)} %param.7) | copy-start | bytes 393220
  27.7 17.6 %copy-start.6 = (bf16[1,64,4096]{2,1,0:T(8,128)(2,1)S(1)}, bf16[1,64,4096]{2,1,0:T(8,128)(2,1)}, u32[]{:S(2)}) copy-start(bf16[1,64,4096]{2,1,0:T(8,128)(2,1)} %q_ref) | copy-start | bytes 1572868
  28.7 13.3 %collective-permute-start.4 = (bf16[4,528,128]{2,1,0:T(8,128)(2,1)S(1)}, bf16[4,528,128]{2,1,0:T(8,128)(2,1)S(1)}, u32[]{:S(2)}, u32[]{:S(2)}) collective-permute-start(bf16[4,528,128]{2,1,0:T(8,128)(2,1)S(1)} %shard_map.83), channel_id=1, source_target_pairs={{0,4},{4,8},{8,12},{12,14},{14,10},{10,6},{6,2},{2,0},{1,3},{5,1},... | collective-permute-start | bytes 1622024 | tf_op jit(solution)/shard_map/ppermute | solution.py:467
  33.4 13.8 %collective-permute-start.7 = (bf16[2064,128]{1,0:T(8,128)(2,1)S(1)}, bf16[2064,128]{1,0:T(8,128)(2,1)S(1)}, u32[]{:S(2)}, u32[]{:S(2)}) collective-permute-start(bf16[2064,128]{1,0:T(8,128)(2,1)S(1)} %collective-permute-done.5.refs_1_), channel_id=1, source_target_pairs={{0,4},{4,8},{8,12},{12,14},{14,10},{10,6},{6,2},{2,0},{1,3},{5,1},... | collective-permute-start | bytes 1585160 | tf_op jit(solution)/shard_map/ppermute | solution.py:467
  35.0 10.4 %collective-permute-start.8 = (bf16[1,1,64,512]{3,2,1,0:T(8,128)(2,1)S(1)}, bf16[1,1,64,512]{3,2,1,0:T(8,128)(2,1)S(1)}, u32[]{:S(2)}, u32[]{:S(2)}) collective-permute-start(bf16[1,1,64,512]{3,2,1,0:T(8,128)(2,1)S(1)} %get-tuple-element.56), channel_id=1, source_target_pairs={{8,0},{10,2},{12,4},{14,6},{0,8},{2,10},{4,12},{6,14},{9,1},{11,3}... | collective-permute-start | bytes 196616 | tf_op jit(solution)/shard_map/ppermute | solution.py:26
  37.6 2.2 %copy-start.3 = (bf16[32,2,64,512]{3,2,1,0:T(8,128)(2,1)S(1)}, bf16[32,2,64,512]{3,2,1,0:T(8,128)(2,1)}, u32[]{:S(2)}) copy-start(bf16[32,2,64,512]{3,2,1,0:T(8,128)(2,1)} %refs_2_.13) | copy-start | bytes 12582916
  39.8 5.7 %copy-start.4 = (bf16[32,2,64,512]{3,2,1,0:T(8,128)(2,1)S(1)}, bf16[32,2,64,512]{3,2,1,0:T(8,128)(2,1)}, u32[]{:S(2)}) copy-start(bf16[32,2,64,512]{3,2,1,0:T(8,128)(2,1)} %refs_2_.13) | copy-start | bytes 12582916
  43.0 13.2 %collective-permute-start.6 = (bf16[4,528,128]{2,1,0:T(8,128)(2,1)S(1)}, bf16[4,528,128]{2,1,0:T(8,128)(2,1)S(1)}, u32[]{:S(2)}, u32[]{:S(2)}) collective-permute-start(bf16[4,528,128]{2,1,0:T(8,128)(2,1)S(1)} %shard_map.85), channel_id=1, source_target_pairs={{0,4},{4,8},{8,12},{12,14},{14,10},{10,6},{6,2},{2,0},{1,3},{5,1},... | collective-permute-start | bytes 1622024 | tf_op jit(solution)/shard_map/ppermute | solution.py:467
  47.2 12.9 %collective-permute-start.10 = (bf16[2064,128]{1,0:T(8,128)(2,1)S(1)}, bf16[2064,128]{1,0:T(8,128)(2,1)S(1)}, u32[]{:S(2)}, u32[]{:S(2)}) collective-permute-start(bf16[2064,128]{1,0:T(8,128)(2,1)S(1)} %collective-permute-done.7.refs_1_), channel_id=1, source_target_pairs={{0,4},{4,8},{8,12},{12,14},{14,10},{10,6},{6,2},{2,0},{1,3},{5,1},... | collective-permute-start | bytes 1585160 | tf_op jit(solution)/shard_map/ppermute | solution.py:467
  50.4 7.9 %collective-permute-start.11 = (bf16[1,1,64,512]{3,2,1,0:T(8,128)(2,1)S(1)}, bf16[1,1,64,512]{3,2,1,0:T(8,128)(2,1)S(1)}, u32[]{:S(2)}, u32[]{:S(2)}) collective-permute-start(bf16[1,1,64,512]{3,2,1,0:T(8,128)(2,1)S(1)} %get-tuple-element.65), channel_id=1, source_target_pairs={{8,0},{10,2},{12,4},{14,6},{0,8},{2,10},{4,12},{6,14},{9,1},{11,3}... | collective-permute-start | bytes 196616 | tf_op jit(solution)/shard_map/ppermute | solution.py:26
  57.2 9.5 %collective-permute-start.9 = (bf16[4,528,128]{2,1,0:T(8,128)(2,1)S(1)}, bf16[4,528,128]{2,1,0:T(8,128)(2,1)S(1)}, u32[]{:S(2)}, u32[]{:S(2)}) collective-permute-start(bf16[4,528,128]{2,1,0:T(8,128)(2,1)S(1)} %shard_map.89), channel_id=1, source_target_pairs={{0,4},{4,8},{8,12},{12,14},{14,10},{10,6},{6,2},{2,0},{1,3},{5,1},... | collective-permute-start | bytes 1622024 | tf_op jit(solution)/shard_map/ppermute | solution.py:467
  60.1 12.5 %collective-permute-start.13 = (bf16[2064,128]{1,0:T(8,128)(2,1)S(1)}, bf16[2064,128]{1,0:T(8,128)(2,1)S(1)}, u32[]{:S(2)}, u32[]{:S(2)}) collective-permute-start(bf16[2064,128]{1,0:T(8,128)(2,1)S(1)} %collective-permute-done.10.refs_1_), channel_id=1, source_target_pairs={{0,4},{4,8},{8,12},{12,14},{14,10},{10,6},{6,2},{2,0},{1,3},{5,1},... | collective-permute-start | bytes 1585160 | tf_op jit(solution)/shard_map/ppermute | solution.py:467
  67.6 10.8 %collective-permute-start.12 = (bf16[4,528,128]{2,1,0:T(8,128)(2,1)S(1)}, bf16[4,528,128]{2,1,0:T(8,128)(2,1)S(1)}, u32[]{:S(2)}, u32[]{:S(2)}) collective-permute-start(bf16[4,528,128]{2,1,0:T(8,128)(2,1)S(1)} %shard_map.92), channel_id=1, source_target_pairs={{0,4},{4,8},{8,12},{12,14},{14,10},{10,6},{6,2},{2,0},{1,3},{5,1},... | collective-permute-start | bytes 1622024 | tf_op jit(solution)/shard_map/ppermute | solution.py:467
  72.6 11.5 %collective-permute-start.15 = (bf16[2064,128]{1,0:T(8,128)(2,1)S(1)}, bf16[2064,128]{1,0:T(8,128)(2,1)S(1)}, u32[]{:S(2)}, u32[]{:S(2)}) collective-permute-start(bf16[2064,128]{1,0:T(8,128)(2,1)S(1)} %collective-permute-done.13.refs_1_), channel_id=1, source_target_pairs={{0,4},{4,8},{8,12},{12,14},{14,10},{10,6},{6,2},{2,0},{1,3},{5,1},... | collective-permute-start | bytes 1585160 | tf_op jit(solution)/shard_map/ppermute | solution.py:467
  79.0 7.9 %collective-permute-start.16 = (bf16[2,528,128]{2,1,0:T(8,128)(2,1)S(1)}, bf16[2,528,128]{2,1,0:T(8,128)(2,1)S(1)}, u32[]{:S(2)}, u32[]{:S(2)}) collective-permute-start(bf16[2,528,128]{2,1,0:T(8,128)(2,1)S(1)} %shard_map.94), channel_id=1, source_target_pairs={{0,4},{4,8},{8,12},{12,14},{14,10},{10,6},{6,2},{2,0},{1,3},{5,1},... | collective-permute-start | bytes 811016 | tf_op jit(solution)/shard_map/ppermute | solution.py:467
  81.1 8.7 %collective-permute-start.14 = (bf16[2,528,128]{2,1,0:T(8,128)(2,1)S(1)}, bf16[2,528,128]{2,1,0:T(8,128)(2,1)S(1)}, u32[]{:S(2)}, u32[]{:S(2)}) collective-permute-start(bf16[2,528,128]{2,1,0:T(8,128)(2,1)S(1)} %shard_map.95), channel_id=1, source_target_pairs={{0,4},{4,8},{8,12},{12,14},{14,10},{10,6},{6,2},{2,0},{1,3},{5,1},... | collective-permute-start | bytes 811016 | tf_op jit(solution)/shard_map/ppermute | solution.py:467
  87.6 6.5 %collective-permute-start.18 = (bf16[2,528,128]{2,1,0:T(8,128)(2,1)S(1)}, bf16[2,528,128]{2,1,0:T(8,128)(2,1)S(1)}, u32[]{:S(2)}, u32[]{:S(2)}) collective-permute-start(bf16[2,528,128]{2,1,0:T(8,128)(2,1)S(1)} %shard_map.97), channel_id=1, source_target_pairs={{0,4},{4,8},{8,12},{12,14},{14,10},{10,6},{6,2},{2,0},{1,3},{5,1},... | collective-permute-start | bytes 811016 | tf_op jit(solution)/shard_map/ppermute | solution.py:467
  90.5 6.5 %collective-permute-start.17 = (bf16[2,528,128]{2,1,0:T(8,128)(2,1)S(1)}, bf16[2,528,128]{2,1,0:T(8,128)(2,1)S(1)}, u32[]{:S(2)}, u32[]{:S(2)}) collective-permute-start(bf16[2,528,128]{2,1,0:T(8,128)(2,1)S(1)} %shard_map.98), channel_id=1, source_target_pairs={{0,4},{4,8},{8,12},{12,14},{14,10},{10,6},{6,2},{2,0},{1,3},{5,1},... | collective-permute-start | bytes 811016 | tf_op jit(solution)/shard_map/ppermute | solution.py:467

commit v18 on v14

--- a/solution.py
+++ b/solution.py
@@ -15,6 +15,7 @@
 LIST_ROWS = 16
 GRANT = 20 * 1024 * 1024
 LIGHT = pl.CostEstimate(flops=1, bytes_accessed=1, transcendentals=0)
+HEAVY = pl.CostEstimate(flops=1 << 33, bytes_accessed=1 << 25, transcendentals=1 << 24)
 VMEM = pl.BlockSpec(memory_space=pltpu.VMEM)
 SMEM = pl.BlockSpec(memory_space=pltpu.SMEM)
 HBM = pl.BlockSpec(memory_space=pltpu.HBM)
@@ -261,6 +262,21 @@
         cost_estimate=work,
     )(*args)
     return [(out[2 * n], out[2 * n + 1]) for n in range(count)] + list(out[2 * count:])
+
+
+def touch_kernel(held_ref, lists_ref, out_ref):
+    out_ref[...] = lists_ref[...]
+
+
+def touch(held, lists):
+    return pl.pallas_call(
+        touch_kernel,
+        out_shape=jax.ShapeDtypeStruct(lists.shape, lists.dtype),
+        in_specs=[VMEM, VMEM],
+        out_specs=VMEM,
+        compiler_params=pltpu.CompilerParams(vmem_limit_bytes=GRANT),
+        cost_estimate=HEAVY,
+    )(held, lists)
 
 
 def place_kernel(half, column, me_ref, core_ref, near_ref, far_ref, page_ref, old_ref, out_ref, sem):
@@ -456,9 +472,12 @@
         shape = jax.ShapeDtypeStruct((heads * rows + LIST_ROWS, HEAD_SIZE), queries.dtype)
         return call(join_kernel, shape, x, rows_below)
 
+    arrived = shifted(suffix_key_value, "store", half)
     first = onward(queries)
     mine = list_pages(cap, pages_dev, page_table, prefix_pages, new_slots)
-    moving = joined(first, onward(mine))
+    their_lists = onward(mine)
+    mine = touch(kv_pages, after(mine, arrived))
+    moving = joined(after(first, mine), their_lists)
 
     own_queries = None
     halves = [range(0, heads // 2), range(heads // 2, heads)]
@@ -469,8 +488,6 @@
         if step < stores - 1:
             moving = onward(came)
         lists[step] = listed(came, heads * rows)
-        if step == stores - 3:
-            arrived = shifted(after(suffix_key_value, token), "store", half)
         jobs = [(0, h, h) for h in range(heads)]
         keeping, pages = None, pages_dev // 2
         if step == 1:
@@ -483,7 +500,7 @@
             part, = attend(sizes, jobs, lists[step], [came], kv_pages)
         if step == 1:
             blocks = [packed(part)]
-        elif step < stores - 2:
+        elif step < stores - 1:
             blocks = [merged(after(partial[0], part), part, 0, 0, heads)]
         else:
             blocks = []
@@ -493,8 +510,6 @@
                 blocks.append(merged(block, part, at, half_heads[0], len(half_heads)))
         partial = [onward(block) for block in blocks]
         token = blocks
-        if step == stores - 2:
-            token = [blocks, arrived]
         if step in (half - 1, half):
             if own_queries is None:
                 own_queries = joined(after(queries, token), mine)

time: 98.4 us -> 99.7 us (1.013)
  starting transfers between devices: 38.5 us -> 40.1 us
    ppermute x17 -> x16, waiting for transfers between devices: 20.9 us -> 17.6 us  [onward(): return lax.ppermute(x, ('store', 'tensor'), route)]
    ppermute x1, waiting for transfers between devices: 0.27 us -> 3.53 us  [shifted(): return lax.ppermute(block, axis, route)]
    ppermute x1, starting transfers between devices: 2.53 us -> 4.1 us  [shifted(): return lax.ppermute(block, axis, route)]
    pallas_call x11 -> x10, Pallas kernels: 6.7 us -> 6.4 us  [call(): pl.pallas_call(kernel, out_shape=shape, in_specs=[VMEM] * len(args), out_...]
    ppermute x17 -> x16, starting transfers between devices: 36 us -> 36 us  [onward(): return lax.ppermute(x, ('store', 'tensor'), route)]
  transfers between devices with their start and end apart: 18 -> 17, of which waited for: 13 -> 12; matrix products, arithmetic and copies ran while one was open for 0% -> 0% of each run, Pallas kernels for 30% -> 29%
where the time goes in v18:
time: 99.7 us; the launch traced here: 99.4 us
  starting transfers between devices  40.1 us (40%)
  Pallas kernels  30.8 us (31%)
  waiting for transfers between devices  21.1 us (21%)
  local copies, waits for them, and re-layouts  5.04 us (5%)
  between operations  2.32 us (2%)
    ppermute x16, starting transfers between devices, onward(): return lax.ppermute(x, ('store', 'tensor'), route)  36 us
    pallas_call x9, Pallas kernels, attend(): pl.pallas_call(functools.partial(attend_kernel, sizes + (count,), jobs, o...  20.3 us
    ppermute x16, waiting for transfers between devices, onward(): return lax.ppermute(x, ('store', 'tensor'), route)  17.6 us
    pallas_call x10, Pallas kernels, call(): pl.pallas_call(kernel, out_shape=shape, in_specs=[VMEM] * len(args), out_...  6.4 us
    unnamed x14, local copies, waits for them, and re-layouts  5.04 us
    ppermute x1, starting transfers between devices, shifted(): return lax.ppermute(block, axis, route)  4.1 us
    ppermute x1, waiting for transfers between devices, shifted(): return lax.ppermute(block, axis, route)  3.53 us
    pallas_call x2, Pallas kernels, finish(): pl.pallas_call(functools.partial(final_kernel, suffix, first), out_shape=...  2.53 us
  transfers between devices with their start and end apart: 17, of which 12 were waited for; matrix products, arithmetic and copies ran while one was open for 0% of the time, Pallas kernels for 29%

profile of v18, /device:TPU:0, one launch (start us, length us, event | category | flops | bytes accessed | tf_op | source)
XLA Modules:
  0.0 99.4 jit_solution(17945944112860119394)
XLA Ops:
  0.6 4.1 %collective-permute-start.1 = (bf16[1,2,64,512]{3,2,1,0:T(8,128)(2,1)}, bf16[1,2,64,512]{3,2,1,0:T(8,128)(2,1)S(1)}, u32[]{:S(2)}, u32[]{:S(2)}) collective-permute-start(bf16[1,2,64,512]{3,2,1,0:T(8,128)(2,1)} %param.7), channel_id=1, source_target_pairs={{8,0},{10,2},{12,4},{14,6},{0,8},{2,10},{4,12},{6,14},{9,1},{11,3}... | collective-permute-start | bytes 393224 | tf_op jit(solution)/shard_map/ppermute | solution.py:27
  4.7 1.6 %collective-permute-start = (bf16[1,64,4096]{2,1,0:T(8,128)(2,1)}, bf16[1,64,4096]{2,1,0:T(8,128)(2,1)S(1)}, u32[]{:S(2)}, u32[]{:S(2)}) collective-permute-start(bf16[1,64,4096]{2,1,0:T(8,128)(2,1)} %q_ref), channel_id=1, source_target_pairs={{0,4},{4,8},{8,12},{12,14},{14,10},{10,6},{6,2},{2,0},{1,3},{5,1},... | collective-permute-start | bytes 1572872 | tf_op jit(solution)/shard_map/ppermute | solution.py:462
  7.6 0.0 copy-start.6
  7.6 0.6 copy-done.6
  8.3 0.3 shard_map.77.lists_ref
  8.5 0.0 collective-permute-start.2
  8.6 3.5 %collective-permute-done.1.page_ref = bf16[1,2,64,512]{3,2,1,0:T(8,128)(2,1)S(1)} collective-permute-done((bf16[1,2,64,512]{3,2,1,0:T(8,128)(2,1)}, bf16[1,2,64,512]{3,2,1,0:T(8,128)(2,1)S(1)}, u32[]{:S(2)}, u32[]{:S(2)}) %collective-permute-start.1) | collective-permute-done | bytes 131104 | tf_op jit(solution)/shard_map/ppermute | solution.py:27
  12.1 2.2 %copy-done = bf16[32,2,64,512]{3,2,1,0:T(8,128)(2,1)S(1)} copy-done((bf16[32,2,64,512]{3,2,1,0:T(8,128)(2,1)S(1)}, bf16[32,2,64,512]{3,2,1,0:T(8,128)(2,1)}, u32[]{:S(2)}) %copy-start) | copy-done | bytes 4194328
  14.3 0.0 collective-permute-done.q_ref
  14.3 0.0 collective-permute-done.2.lists_ref
  14.3 0.1 shard_map.79.refs_1_
  14.4 3.5 %collective-permute-start.4 = (bf16[2064,128]{1,0:T(8,128)(2,1)S(1)}, bf16[2064,128]{1,0:T(8,128)(2,1)S(1)}, u32[]{:S(2)}, u32[]{:S(2)}) collective-permute-start(bf16[2064,128]{1,0:T(8,128)(2,1)S(1)} %shard_map.79.refs_1_), channel_id=1, source_target_pairs={{0,4},{4,8},{8,12},{12,14},{14,10},{10,6},{6,2},{2,0},{1,3},{5,1},... | collective-permute-start | bytes 1585160 | tf_op jit(solution)/shard_map/ppermute | solution.py:462
  17.9 2.7 %shard_map.80 = (f32[4,512,128]{2,1,0:T(8,128)S(1)}, bf16[4,16,128]{2,1,0:T(8,128)(2,1)S(1)}, bf16[32,2,64,512]{3,2,1,0:T(8,128)(2,1)}) custom-call(s32[1,128]{1,0:T(1,128)S(1)} %fusion.refs_0_, bf16[2064,128]{1,0:T(8,128)(2,1)S(1)} %shard_map.79.refs_1_, bf16[32,2,64,512]{3,2,1,0:T(8,128)(2,1)S(1)} %copy-done.1), custom_call_target="tpu_custom_call" | custom-call | flops 1073741824 | bytes 2621440 | tf_op jit(solution)/shard_map/pallas_call | solution.py:254
  20.6 0.1 shard_map.81
  20.7 2.5 %collective-permute-start.3 = (bf16[4,528,128]{2,1,0:T(8,128)(2,1)S(1)}, bf16[4,528,128]{2,1,0:T(8,128)(2,1)S(1)}, u32[]{:S(2)}, u32[]{:S(2)}) collective-permute-start(bf16[4,528,128]{2,1,0:T(8,128)(2,1)S(1)} %shard_map.81), channel_id=1, source_target_pairs={{0,4},{4,8},{8,12},{12,14},{14,10},{10,6},{6,2},{2,0},{1,3},{5,1},... | collective-permute-start | bytes 1622024 | tf_op jit(solution)/shard_map/ppermute | solution.py:462
  23.2 1.6 %collective-permute-done.4.refs_1_ = bf16[2064,128]{1,0:T(8,128)(2,1)S(1)} collective-permute-done((bf16[2064,128]{1,0:T(8,128)(2,1)S(1)}, bf16[2064,128]{1,0:T(8,128)(2,1)S(1)}, u32[]{:S(2)}, u32[]{:S(2)}) %collective-permute-start.4) | collective-permute-done | bytes 528416 | tf_op jit(solution)/shard_map/ppermute | solution.py:462
  24.7 2.4 %collective-permute-start.6 = (bf16[2064,128]{1,0:T(8,128)(2,1)S(1)}, bf16[2064,128]{1,0:T(8,128)(2,1)S(1)}, u32[]{:S(2)}, u32[]{:S(2)}) collective-permute-start(bf16[2064,128]{1,0:T(8,128)(2,1)S(1)} %collective-permute-done.4.refs_1_), channel_id=1, source_target_pairs={{0,4},{4,8},{8,12},{12,14},{14,10},{10,6},{6,2},{2,0},{1,3},{5,1},... | collective-permute-start | bytes 1585160 | tf_op jit(solution)/shard_map/ppermute | solution.py:462
  27.1 2.9 %shard_map.82 = (f32[4,512,128]{2,1,0:T(8,128)S(1)}, bf16[4,16,128]{2,1,0:T(8,128)(2,1)S(1)}, bf16[32,2,64,512]{3,2,1,0:T(8,128)(2,1)}) custom-call(s32[1,128]{1,0:T(1,128)S(1)} %fusion.1.refs_0_.near_ref, bf16[2064,128]{1,0:T(8,128)(2,1)S(1)} %collective-permute-done.4.refs_1_, ...), custom_call_target="tpu_custom_call", output_to_operand_aliasing={{2}: (3, {})} | custom-call | flops 1073741824 | bytes 2621440 | tf_op jit(solution)/shard_map/pallas_call | solution.py:254
  30.1 0.5 collective-permute-done.3.in_ref
  30.5 1.0 shard_map.83
  31.5 0.0 copy-start.4
  31.5 2.4 %collective-permute-start.5 = (bf16[4,528,128]{2,1,0:T(8,128)(2,1)S(1)}, bf16[4,528,128]{2,1,0:T(8,128)(2,1)S(1)}, u32[]{:S(2)}, u32[]{:S(2)}) collective-permute-start(bf16[4,528,128]{2,1,0:T(8,128)(2,1)S(1)} %shard_map.83), channel_id=1, source_target_pairs={{0,4},{4,8},{8,12},{12,14},{14,10},{10,6},{6,2},{2,0},{1,3},{5,1},... | collective-permute-start | bytes 1622024 | tf_op jit(solution)/shard_map/ppermute | solution.py:462
  34.0 2.2 %collective-permute-done.6.refs_1_ = bf16[2064,128]{1,0:T(8,128)(2,1)S(1)} collective-permute-done((bf16[2064,128]{1,0:T(8,128)(2,1)S(1)}, bf16[2064,128]{1,0:T(8,128)(2,1)S(1)}, u32[]{:S(2)}, u32[]{:S(2)}) %collective-permute-start.6) | collective-permute-done | bytes 528416 | tf_op jit(solution)/shard_map/ppermute | solution.py:462
  36.2 2.4 %collective-permute-start.8 = (bf16[2064,128]{1,0:T(8,128)(2,1)S(1)}, bf16[2064,128]{1,0:T(8,128)(2,1)S(1)}, u32[]{:S(2)}, u32[]{:S(2)}) collective-permute-start(bf16[2064,128]{1,0:T(8,128)(2,1)S(1)} %collective-permute-done.6.refs_1_), channel_id=1, source_target_pairs={{0,4},{4,8},{8,12},{12,14},{14,10},{10,6},{6,2},{2,0},{1,3},{5,1},... | collective-permute-start | bytes 1585160 | tf_op jit(solution)/shard_map/ppermute | solution.py:462
  38.6 2.2 %shard_map.84 = (f32[4,512,128]{2,1,0:T(8,128)S(1)}, bf16[4,16,128]{2,1,0:T(8,128)(2,1)S(1)}) custom-call(s32[1,128]{1,0:T(1,128)S(1)} %fusion.2.refs_0_, bf16[2064,128]{1,0:T(8,128)(2,1)S(1)} %collective-permute-done.6.refs_1_, bf16[32,2,64,512]{3,2,1,0:T(8,128)(2,1)S(1)} %copy-done.1), custom_call_target="tpu_custom_call" | custom-call | flops 1073741824 | bytes 2621440 | tf_op jit(solution)/shard_map/pallas_call | solution.py:254
  40.8 1.2 %collective-permute-done.5.in_ref = bf16[4,528,128]{2,1,0:T(8,128)(2,1)S(1)} collective-permute-done((bf16[4,528,128]{2,1,0:T(8,128)(2,1)S(1)}, bf16[4,528,128]{2,1,0:T(8,128)(2,1)S(1)}, u32[]{:S(2)}, u32[]{:S(2)}) %collective-permute-start.5) | collective-permute-done | bytes 540704 | tf_op jit(solution)/shard_map/ppermute | solution.py:462
  42.0 1.0 shard_map.85
  43.0 2.4 %collective-permute-start.7 = (bf16[4,528,128]{2,1,0:T(8,128)(2,1)S(1)}, bf16[4,528,128]{2,1,0:T(8,128)(2,1)S(1)}, u32[]{:S(2)}, u32[]{:S(2)}) collective-permute-start(bf16[4,528,128]{2,1,0:T(8,128)(2,1)S(1)} %shard_map.85), channel_id=1, source_target_pairs={{0,4},{4,8},{8,12},{12,14},{14,10},{10,6},{6,2},{2,0},{1,3},{5,1},... | collective-permute-start | bytes 1622024 | tf_op jit(solution)/shard_map/ppermute | solution.py:462
  45.4 0.1 shard_map.86.refs_1_
  45.5 0.0 copy-start.2
  45.5 2.2 %copy-done.2 = bf16[32,2,64,512]{3,2,1,0:T(8,128)(2,1)S(1)} copy-done((bf16[32,2,64,512]{3,2,1,0:T(8,128)(2,1)S(1)}, bf16[32,2,64,512]{3,2,1,0:T(8,128)(2,1)}, u32[]{:S(2)}) %copy-start.2) | copy-done | bytes 4194328
  47.7 1.8 %shard_map.87 = (f32[2,512,128]{2,1,0:T(8,128)S(1)}, bf16[2,16,128]{2,1,0:T(8,128)(2,1)S(1)}) custom-call(s32[1,128]{1,0:T(1,128)S(1)} %fusion.3.refs_0_, bf16[2064,128]{1,0:T(8,128)(2,1)S(1)} %shard_map.86.refs_1_, bf16[2,64,512]{2,1,0:T(8,128)(2,1)S(1)} %bitcast.3, bf16[32,2,64,512]{3,2,1,0:T(8,128)(2,1)S(1)} %copy-done.2), custom_call_target="tpu_custom_call" | custom-call | flops 536870912 | bytes 1310720 | tf_op jit(solution)/shard_map/pallas_call | solution.py:254
  49.5 0.0 copy-start.3
  49.5 0.0 collective-permute-done.8.refs_1_
  49.5 2.5 %collective-permute-start.10 = (bf16[2064,128]{1,0:T(8,128)(2,1)S(1)}, bf16[2064,128]{1,0:T(8,128)(2,1)S(1)}, u32[]{:S(2)}, u32[]{:S(2)}) collective-permute-start(bf16[2064,128]{1,0:T(8,128)(2,1)S(1)} %collective-permute-done.8.refs_1_), channel_id=1, source_target_pairs={{0,4},{4,8},{8,12},{12,14},{14,10},{10,6},{6,2},{2,0},{1,3},{5,1},... | collective-permute-start | bytes 1585160 | tf_op jit(solution)/shard_map/ppermute | solution.py:462
  52.0 2.2 %shard_map.88 = (f32[4,512,128]{2,1,0:T(8,128)S(1)}, bf16[4,16,128]{2,1,0:T(8,128)(2,1)S(1)}) custom-call(s32[1,128]{1,0:T(1,128)S(1)} %fusion.4.refs_0_, bf16[2064,128]{1,0:T(8,128)(2,1)S(1)} %collective-permute-done.8.refs_1_, bf16[32,2,64,512]{3,2,1,0:T(8,128)(2,1)S(1)} %copy-done.2), custom_call_target="tpu_custom_call" | custom-call | flops 1073741824 | bytes 2621440 | tf_op jit(solution)/shard_map/pallas_call | solution.py:254
  54.2 0.0 collective-permute-done.7.in_ref
  54.2 1.0 %shard_map.89 = bf16[4,528,128]{2,1,0:T(8,128)(2,1)S(1)} custom-call(bf16[4,528,128]{2,1,0:T(8,128)(2,1)S(1)} %collective-permute-done.7.in_ref, f32[4,512,128]{2,1,0:T(8,128)S(1)} %get-tuple-element.60.acc_ref, bf16[4,16,128]{2,1,0:T(8,128)(2,1)S(1)} %get-tuple-element.61.stat_ref), custom_call_target="tpu_custom_call" | custom-call | flops 1605632 | bytes 3211264 | tf_op jit(solution)/shard_map/pallas_call | solution.py:389
  55.2 1.8 %collective-permute-start.9 = (bf16[4,528,128]{2,1,0:T(8,128)(2,1)S(1)}, bf16[4,528,128]{2,1,0:T(8,128)(2,1)S(1)}, u32[]{:S(2)}, u32[]{:S(2)}) collective-permute-start(bf16[4,528,128]{2,1,0:T(8,128)(2,1)S(1)} %shard_map.89), channel_id=1, source_target_pairs={{0,4},{4,8},{8,12},{12,14},{14,10},{10,6},{6,2},{2,0},{1,3},{5,1},... | collective-permute-start | bytes 1622024 | tf_op jit(solution)/shard_map/ppermute | solution.py:462
  57.1 1.8 %shard_map.90 = (f32[2,512,128]{2,1,0:T(8,128)S(1)}, bf16[2,16,128]{2,1,0:T(8,128)(2,1)S(1)}) custom-call(s32[1,128]{1,0:T(1,128)S(1)} %fusion.3.refs_0_, bf16[2064,128]{1,0:T(8,128)(2,1)S(1)} %shard_map.86.refs_1_, bf16[2,64,512]{2,1,0:T(8,128)(2,1)S(1)} %bitcast.4, bf16[32,2,64,512]{3,2,1,0:T(8,128)(2,1)S(1)} %copy-done.3), custom_call_target="tpu_custom_call" | custom-call | flops 536870912 | bytes 1310720 | tf_op jit(solution)/shard_map/pallas_call | solution.py:254
  58.8 0.3 collective-permute-done.10.refs_1_
  59.1 2.4 %collective-permute-start.12 = (bf16[2064,128]{1,0:T(8,128)(2,1)S(1)}, bf16[2064,128]{1,0:T(8,128)(2,1)S(1)}, u32[]{:S(2)}, u32[]{:S(2)}) collective-permute-start(bf16[2064,128]{1,0:T(8,128)(2,1)S(1)} %collective-permute-done.10.refs_1_), channel_id=1, source_target_pairs={{0,4},{4,8},{8,12},{12,14},{14,10},{10,6},{6,2},{2,0},{1,3},{5,1},... | collective-permute-start | bytes 1585160 | tf_op jit(solution)/shard_map/ppermute | solution.py:462
  61.5 2.2 %shard_map.91 = (f32[4,512,128]{2,1,0:T(8,128)S(1)}, bf16[4,16,128]{2,1,0:T(8,128)(2,1)S(1)}) custom-call(s32[1,128]{1,0:T(1,128)S(1)} %fusion.5.refs_0_, bf16[2064,128]{1,0:T(8,128)(2,1)S(1)} %collective-permute-done.10.refs_1_, bf16[32,2,64,512]{3,2,1,0:T(8,128)(2,1)S(1)} %copy-done.3), custom_call_target="tpu_custom_call" | custom-call | flops 1073741824 | bytes 2621440 | tf_op jit(solution)/shard_map/pallas_call | solution.py:254
  63.7 1.2 %collective-permute-done.9.in_ref = bf16[4,528,128]{2,1,0:T(8,128)(2,1)S(1)} collective-permute-done((bf16[4,528,128]{2,1,0:T(8,128)(2,1)S(1)}, bf16[4,528,128]{2,1,0:T(8,128)(2,1)S(1)}, u32[]{:S(2)}, u32[]{:S(2)}) %collective-permute-start.9) | collective-permute-done | bytes 540704 | tf_op jit(solution)/shard_map/ppermute | solution.py:462
  64.9 1.0 shard_map.92
  65.9 2.4 %collective-permute-start.11 = (bf16[4,528,128]{2,1,0:T(8,128)(2,1)S(1)}, bf16[4,528,128]{2,1,0:T(8,128)(2,1)S(1)}, u32[]{:S(2)}, u32[]{:S(2)}) collective-permute-start(bf16[4,528,128]{2,1,0:T(8,128)(2,1)S(1)} %shard_map.92), channel_id=1, source_target_pairs={{0,4},{4,8},{8,12},{12,14},{14,10},{10,6},{6,2},{2,0},{1,3},{5,1},... | collective-permute-start | bytes 1622024 | tf_op jit(solution)/shard_map/ppermute | solution.py:462
  68.3 2.2 %collective-permute-done.12.refs_1_ = bf16[2064,128]{1,0:T(8,128)(2,1)S(1)} collective-permute-done((bf16[2064,128]{1,0:T(8,128)(2,1)S(1)}, bf16[2064,128]{1,0:T(8,128)(2,1)S(1)}, u32[]{:S(2)}, u32[]{:S(2)}) %collective-permute-start.12) | collective-permute-done | bytes 528416 | tf_op jit(solution)/shard_map/ppermute | solution.py:462
  70.6 2.4 %collective-permute-start.14 = (bf16[2064,128]{1,0:T(8,128)(2,1)S(1)}, bf16[2064,128]{1,0:T(8,128)(2,1)S(1)}, u32[]{:S(2)}, u32[]{:S(2)}) collective-permute-start(bf16[2064,128]{1,0:T(8,128)(2,1)S(1)} %collective-permute-done.12.refs_1_), channel_id=1, source_target_pairs={{0,4},{4,8},{8,12},{12,14},{14,10},{10,6},{6,2},{2,0},{1,3},{5,1},... | collective-permute-start | bytes 1585160 | tf_op jit(solution)/shard_map/ppermute | solution.py:462
  72.9 2.2 %shard_map.93 = (f32[4,512,128]{2,1,0:T(8,128)S(1)}, bf16[4,16,128]{2,1,0:T(8,128)(2,1)S(1)}) custom-call(s32[1,128]{1,0:T(1,128)S(1)} %fusion.6.refs_0_.far_ref, bf16[2064,128]{1,0:T(8,128)(2,1)S(1)} %collective-permute-done.12.refs_1_, bf16[32,2,64,512]{3,2,1,0:T(8,128)(2,1)S(1)} %copy-done.3), custom_call_target="tpu_custom_call" | custom-call | flops 1073741824 | bytes 2621440 | tf_op jit(solution)/shard_map/pallas_call | solution.py:254
  75.2 1.2 %collective-permute-done.11.in_ref = bf16[4,528,128]{2,1,0:T(8,128)(2,1)S(1)} collective-permute-done((bf16[4,528,128]{2,1,0:T(8,128)(2,1)S(1)}, bf16[4,528,128]{2,1,0:T(8,128)(2,1)S(1)}, u32[]{:S(2)}, u32[]{:S(2)}) %collective-permute-start.11) | collective-permute-done | bytes 540704 | tf_op jit(solution)/shard_map/ppermute | solution.py:462
  76.3 1.0 shard_map.94
  77.3 2.4 %collective-permute-start.13 = (bf16[4,528,128]{2,1,0:T(8,128)(2,1)S(1)}, bf16[4,528,128]{2,1,0:T(8,128)(2,1)S(1)}, u32[]{:S(2)}, u32[]{:S(2)}) collective-permute-start(bf16[4,528,128]{2,1,0:T(8,128)(2,1)S(1)} %shard_map.94), channel_id=1, source_target_pairs={{0,4},{4,8},{8,12},{12,14},{14,10},{10,6},{6,2},{2,0},{1,3},{5,1},... | collective-permute-start | bytes 1622024 | tf_op jit(solution)/shard_map/ppermute | solution.py:462
  79.8 2.2 %collective-permute-done.14.refs_1_ = bf16[2064,128]{1,0:T(8,128)(2,1)S(1)} collective-permute-done((bf16[2064,128]{1,0:T(8,128)(2,1)S(1)}, bf16[2064,128]{1,0:T(8,128)(2,1)S(1)}, u32[]{:S(2)}, u32[]{:S(2)}) %collective-permute-start.14) | collective-permute-done | bytes 528416 | tf_op jit(solution)/shard_map/ppermute | solution.py:462
  82.0 2.2 %shard_map.95 = (f32[4,512,128]{2,1,0:T(8,128)S(1)}, bf16[4,16,128]{2,1,0:T(8,128)(2,1)S(1)}) custom-call(s32[1,128]{1,0:T(1,128)S(1)} %fusion.7.refs_0_, bf16[2064,128]{1,0:T(8,128)(2,1)S(1)} %collective-permute-done.14.refs_1_, bf16[32,2,64,512]{3,2,1,0:T(8,128)(2,1)S(1)} %copy-done.3), custom_call_target="tpu_custom_call" | custom-call | flops 1073741824 | bytes 2621440 | tf_op jit(solution)/shard_map/pallas_call | solution.py:254
  84.2 3.6 %collective-permute-done.13.in_ref = bf16[4,528,128]{2,1,0:T(8,128)(2,1)S(1)} collective-permute-done((bf16[4,528,128]{2,1,0:T(8,128)(2,1)S(1)}, bf16[4,528,128]{2,1,0:T(8,128)(2,1)S(1)}, u32[]{:S(2)}, u32[]{:S(2)}) %collective-permute-start.13) | collective-permute-done | bytes 540704 | tf_op jit(solution)/shard_map/ppermute | solution.py:462
  87.8 0.6 shard_map.96
  88.4 2.4 %collective-permute-start.16 = (bf16[2,528,128]{2,1,0:T(8,128)(2,1)S(1)}, bf16[2,528,128]{2,1,0:T(8,128)(2,1)S(1)}, u32[]{:S(2)}, u32[]{:S(2)}) collective-permute-start(bf16[2,528,128]{2,1,0:T(8,128)(2,1)S(1)} %shard_map.96), channel_id=1, source_target_pairs={{0,4},{4,8},{8,12},{12,14},{14,10},{10,6},{6,2},{2,0},{1,3},{5,1},... | collective-permute-start | bytes 811016 | tf_op jit(solution)/shard_map/ppermute | solution.py:462
  90.9 0.6 shard_map.97
  91.5 2.5 %collective-permute-start.15 = (bf16[2,528,128]{2,1,0:T(8,128)(2,1)S(1)}, bf16[2,528,128]{2,1,0:T(8,128)(2,1)S(1)}, u32[]{:S(2)}, u32[]{:S(2)}) collective-permute-start(bf16[2,528,128]{2,1,0:T(8,128)(2,1)S(1)} %shard_map.97), channel_id=1, source_target_pairs={{0,4},{4,8},{8,12},{12,14},{14,10},{10,6},{6,2},{2,0},{1,3},{5,1},... | collective-permute-start | bytes 811016 | tf_op jit(solution)/shard_map/ppermute | solution.py:462
  94.0 1.2 %shard_map.98 = bf16[32,2,64,512]{3,2,1,0:T(8,128)(2,1)} custom-call(s32[1]{0:T(128)} %bitcast.1.me_ref, s32[1]{0:T(128)} %bitcast.2.core_ref, s32[1,128]{1,0:T(1,128)S(1)} %fusion.1.refs_0_.near_ref, s32[1,128]{1,0:T(1,128)S(1)} %fusion.6.refs_0_.far_ref, ...), custom_call_target="tpu_custom_call", output_to_operand_aliasing={{}: (5, {})} | custom-call | flops 1 | bytes 1 | tf_op jit(solution)/shard_map/pallas_call | solution.py:292
  95.2 0.0 collective-permute-done.16.in_ref
  95.2 1.3 %shard_map.99.refs_0_ = bf16[1,64,4096]{2,1,0:T(8,128)(2,1)} custom-call(bf16[2,528,128]{2,1,0:T(8,128)(2,1)S(1)} %collective-permute-done.16.in_ref, f32[2,512,128]{2,1,0:T(8,128)S(1)} %get-tuple-element.57.acc_ref, bf16[2,16,128]{2,1,0:T(8,128)(2,1)S(1)} %get-tuple-element.58.stat_ref), custom_call_target="tpu_custom_call" | custom-call | tf_op jit(solution)/shard_map/pallas_call | solution.py:373
  96.5 1.5 %collective-permute-done.15.in_ref = bf16[2,528,128]{2,1,0:T(8,128)(2,1)S(1)} collective-permute-done((bf16[2,528,128]{2,1,0:T(8,128)(2,1)S(1)}, bf16[2,528,128]{2,1,0:T(8,128)(2,1)S(1)}, u32[]{:S(2)}, u32[]{:S(2)}) %collective-permute-start.15) | collective-permute-done | bytes 270368 | tf_op jit(solution)/shard_map/ppermute | solution.py:462
  98.0 1.3 %shard_map.100 = bf16[1,64,4096]{2,1,0:T(8,128)(2,1)} custom-call(bf16[2,528,128]{2,1,0:T(8,128)(2,1)S(1)} %collective-permute-done.15.in_ref, f32[2,512,128]{2,1,0:T(8,128)S(1)} %get-tuple-element.64.acc_ref, bf16[2,16,128]{2,1,0:T(8,128)(2,1)S(1)} %get-tuple-element.65.stat_ref, bf16[1,64,4096]{2,1,0:T(8,128)(2,1)} %shard_map.99.refs_0_), custom_call_target="tpu_custom_call", output_to_operand_aliasing={{}: (3, {})} | custom-call | tf_op jit(solution)/shard_map/pallas_call | solution.py:373
  (16 shorter events, 0.1 us)
Async XLA Ops:
  0.6 11.5 %collective-permute-start.1 = (bf16[1,2,64,512]{3,2,1,0:T(8,128)(2,1)}, bf16[1,2,64,512]{3,2,1,0:T(8,128)(2,1)S(1)}, u32[]{:S(2)}, u32[]{:S(2)}) collective-permute-start(bf16[1,2,64,512]{3,2,1,0:T(8,128)(2,1)} %param.7), channel_id=1, source_target_pairs={{8,0},{10,2},{12,4},{14,6},{0,8},{2,10},{4,12},{6,14},{9,1},{11,3}... | collective-permute-start | bytes 393224 | tf_op jit(solution)/shard_map/ppermute | solution.py:27
  4.7 9.5 %collective-permute-start = (bf16[1,64,4096]{2,1,0:T(8,128)(2,1)}, bf16[1,64,4096]{2,1,0:T(8,128)(2,1)S(1)}, u32[]{:S(2)}, u32[]{:S(2)}) collective-permute-start(bf16[1,64,4096]{2,1,0:T(8,128)(2,1)} %q_ref), channel_id=1, source_target_pairs={{0,4},{4,8},{8,12},{12,14},{14,10},{10,6},{6,2},{2,0},{1,3},{5,1},... | collective-permute-start | bytes 1572872 | tf_op jit(solution)/shard_map/ppermute | solution.py:462
  7.6 0.7 copy-start.6
  8.5 5.7 %collective-permute-start.2 = (bf16[16,128]{1,0:T(8,128)(2,1)S(1)}, bf16[16,128]{1,0:T(8,128)(2,1)S(1)}, u32[]{:S(2)}, u32[]{:S(2)}) collective-permute-start(bf16[16,128]{1,0:T(8,128)(2,1)S(1)} %shard_map.77.lists_ref), channel_id=1, source_target_pairs={{0,4},{4,8},{8,12},{12,14},{14,10},{10,6},{6,2},{2,0},{1,3},{5,1},... | collective-permute-start | bytes 12296 | tf_op jit(solution)/shard_map/ppermute | solution.py:462
  12.1 2.2 %copy-start = (bf16[32,2,64,512]{3,2,1,0:T(8,128)(2,1)S(1)}, bf16[32,2,64,512]{3,2,1,0:T(8,128)(2,1)}, u32[]{:S(2)}) copy-start(bf16[32,2,64,512]{3,2,1,0:T(8,128)(2,1)} %refs_2_.13) | copy-start | bytes 12582916
  14.3 3.6 %copy-start.1 = (bf16[32,2,64,512]{3,2,1,0:T(8,128)(2,1)S(1)}, bf16[32,2,64,512]{3,2,1,0:T(8,128)(2,1)}, u32[]{:S(2)}) copy-start(bf16[32,2,64,512]{3,2,1,0:T(8,128)(2,1)} %refs_2_.13) | copy-start | bytes 12582916
  14.4 10.3 %collective-permute-start.4 = (bf16[2064,128]{1,0:T(8,128)(2,1)S(1)}, bf16[2064,128]{1,0:T(8,128)(2,1)S(1)}, u32[]{:S(2)}, u32[]{:S(2)}) collective-permute-start(bf16[2064,128]{1,0:T(8,128)(2,1)S(1)} %shard_map.79.refs_1_), channel_id=1, source_target_pairs={{0,4},{4,8},{8,12},{12,14},{14,10},{10,6},{6,2},{2,0},{1,3},{5,1},... | collective-permute-start | bytes 1585160 | tf_op jit(solution)/shard_map/ppermute | solution.py:462
  20.7 9.8 %collective-permute-start.3 = (bf16[4,528,128]{2,1,0:T(8,128)(2,1)S(1)}, bf16[4,528,128]{2,1,0:T(8,128)(2,1)S(1)}, u32[]{:S(2)}, u32[]{:S(2)}) collective-permute-start(bf16[4,528,128]{2,1,0:T(8,128)(2,1)S(1)} %shard_map.81), channel_id=1, source_target_pairs={{0,4},{4,8},{8,12},{12,14},{14,10},{10,6},{6,2},{2,0},{1,3},{5,1},... | collective-permute-start | bytes 1622024 | tf_op jit(solution)/shard_map/ppermute | solution.py:462
  24.7 11.5 %collective-permute-start.6 = (bf16[2064,128]{1,0:T(8,128)(2,1)S(1)}, bf16[2064,128]{1,0:T(8,128)(2,1)S(1)}, u32[]{:S(2)}, u32[]{:S(2)}) collective-permute-start(bf16[2064,128]{1,0:T(8,128)(2,1)S(1)} %collective-permute-done.4.refs_1_), channel_id=1, source_target_pairs={{0,4},{4,8},{8,12},{12,14},{14,10},{10,6},{6,2},{2,0},{1,3},{5,1},... | collective-permute-start | bytes 1585160 | tf_op jit(solution)/shard_map/ppermute | solution.py:462
  30.5 14.9 %copy-start.5 = (bf16[1,64,4096]{2,1,0:T(8,128)(2,1)S(1)}, bf16[1,64,4096]{2,1,0:T(8,128)(2,1)}, u32[]{:S(2)}) copy-start(bf16[1,64,4096]{2,1,0:T(8,128)(2,1)} %q_ref) | copy-start | bytes 1572868
  31.5 14.0 %copy-start.4 = (bf16[1,2,64,512]{3,2,1,0:T(8,128)(2,1)S(1)}, bf16[1,2,64,512]{3,2,1,0:T(8,128)(2,1)}, u32[]{:S(2)}) copy-start(bf16[1,2,64,512]{3,2,1,0:T(8,128)(2,1)} %param.7) | copy-start | bytes 393220
  31.5 10.5 %collective-permute-start.5 = (bf16[4,528,128]{2,1,0:T(8,128)(2,1)S(1)}, bf16[4,528,128]{2,1,0:T(8,128)(2,1)S(1)}, u32[]{:S(2)}, u32[]{:S(2)}) collective-permute-start(bf16[4,528,128]{2,1,0:T(8,128)(2,1)S(1)} %shard_map.83), channel_id=1, source_target_pairs={{0,4},{4,8},{8,12},{12,14},{14,10},{10,6},{6,2},{2,0},{1,3},{5,1},... | collective-permute-start | bytes 1622024 | tf_op jit(solution)/shard_map/ppermute | solution.py:462
  36.2 13.3 %collective-permute-start.8 = (bf16[2064,128]{1,0:T(8,128)(2,1)S(1)}, bf16[2064,128]{1,0:T(8,128)(2,1)S(1)}, u32[]{:S(2)}, u32[]{:S(2)}) collective-permute-start(bf16[2064,128]{1,0:T(8,128)(2,1)S(1)} %collective-permute-done.6.refs_1_), channel_id=1, source_target_pairs={{0,4},{4,8},{8,12},{12,14},{14,10},{10,6},{6,2},{2,0},{1,3},{5,1},... | collective-permute-start | bytes 1585160 | tf_op jit(solution)/shard_map/ppermute | solution.py:462
  43.0 11.2 %collective-permute-start.7 = (bf16[4,528,128]{2,1,0:T(8,128)(2,1)S(1)}, bf16[4,528,128]{2,1,0:T(8,128)(2,1)S(1)}, u32[]{:S(2)}, u32[]{:S(2)}) collective-permute-start(bf16[4,528,128]{2,1,0:T(8,128)(2,1)S(1)} %shard_map.85), channel_id=1, source_target_pairs={{0,4},{4,8},{8,12},{12,14},{14,10},{10,6},{6,2},{2,0},{1,3},{5,1},... | collective-permute-start | bytes 1622024 | tf_op jit(solution)/shard_map/ppermute | solution.py:462
  45.5 2.2 %copy-start.2 = (bf16[32,2,64,512]{3,2,1,0:T(8,128)(2,1)S(1)}, bf16[32,2,64,512]{3,2,1,0:T(8,128)(2,1)}, u32[]{:S(2)}) copy-start(bf16[32,2,64,512]{3,2,1,0:T(8,128)(2,1)} %refs_2_.13) | copy-start | bytes 12582916
  49.5 7.6 %copy-start.3 = (bf16[32,2,64,512]{3,2,1,0:T(8,128)(2,1)S(1)}, bf16[32,2,64,512]{3,2,1,0:T(8,128)(2,1)}, u32[]{:S(2)}) copy-start(bf16[32,2,64,512]{3,2,1,0:T(8,128)(2,1)} %refs_2_.13) | copy-start | bytes 12582916
  49.5 9.6 %collective-permute-start.10 = (bf16[2064,128]{1,0:T(8,128)(2,1)S(1)}, bf16[2064,128]{1,0:T(8,128)(2,1)S(1)}, u32[]{:S(2)}, u32[]{:S(2)}) collective-permute-start(bf16[2064,128]{1,0:T(8,128)(2,1)S(1)} %collective-permute-done.8.refs_1_), channel_id=1, source_target_pairs={{0,4},{4,8},{8,12},{12,14},{14,10},{10,6},{6,2},{2,0},{1,3},{5,1},... | collective-permute-start | bytes 1585160 | tf_op jit(solution)/shard_map/ppermute | solution.py:462
  55.2 9.7 %collective-permute-start.9 = (bf16[4,528,128]{2,1,0:T(8,128)(2,1)S(1)}, bf16[4,528,128]{2,1,0:T(8,128)(2,1)S(1)}, u32[]{:S(2)}, u32[]{:S(2)}) collective-permute-start(bf16[4,528,128]{2,1,0:T(8,128)(2,1)S(1)} %shard_map.89), channel_id=1, source_target_pairs={{0,4},{4,8},{8,12},{12,14},{14,10},{10,6},{6,2},{2,0},{1,3},{5,1},... | collective-permute-start | bytes 1622024 | tf_op jit(solution)/shard_map/ppermute | solution.py:462
  59.1 11.5 %collective-permute-start.12 = (bf16[2064,128]{1,0:T(8,128)(2,1)S(1)}, bf16[2064,128]{1,0:T(8,128)(2,1)S(1)}, u32[]{:S(2)}, u32[]{:S(2)}) collective-permute-start(bf16[2064,128]{1,0:T(8,128)(2,1)S(1)} %collective-permute-done.10.refs_1_), channel_id=1, source_target_pairs={{0,4},{4,8},{8,12},{12,14},{14,10},{10,6},{6,2},{2,0},{1,3},{5,1},... | collective-permute-start | bytes 1585160 | tf_op jit(solution)/shard_map/ppermute | solution.py:462
  65.9 10.5 %collective-permute-start.11 = (bf16[4,528,128]{2,1,0:T(8,128)(2,1)S(1)}, bf16[4,528,128]{2,1,0:T(8,128)(2,1)S(1)}, u32[]{:S(2)}, u32[]{:S(2)}) collective-permute-start(bf16[4,528,128]{2,1,0:T(8,128)(2,1)S(1)} %shard_map.92), channel_id=1, source_target_pairs={{0,4},{4,8},{8,12},{12,14},{14,10},{10,6},{6,2},{2,0},{1,3},{5,1},... | collective-permute-start | bytes 1622024 | tf_op jit(solution)/shard_map/ppermute | solution.py:462
  70.6 11.5 %collective-permute-start.14 = (bf16[2064,128]{1,0:T(8,128)(2,1)S(1)}, bf16[2064,128]{1,0:T(8,128)(2,1)S(1)}, u32[]{:S(2)}, u32[]{:S(2)}) collective-permute-start(bf16[2064,128]{1,0:T(8,128)(2,1)S(1)} %collective-permute-done.12.refs_1_), channel_id=1, source_target_pairs={{0,4},{4,8},{8,12},{12,14},{14,10},{10,6},{6,2},{2,0},{1,3},{5,1},... | collective-permute-start | bytes 1585160 | tf_op jit(solution)/shard_map/ppermute | solution.py:462
  77.3 10.5 %collective-permute-start.13 = (bf16[4,528,128]{2,1,0:T(8,128)(2,1)S(1)}, bf16[4,528,128]{2,1,0:T(8,128)(2,1)S(1)}, u32[]{:S(2)}, u32[]{:S(2)}) collective-permute-start(bf16[4,528,128]{2,1,0:T(8,128)(2,1)S(1)} %shard_map.94), channel_id=1, source_target_pairs={{0,4},{4,8},{8,12},{12,14},{14,10},{10,6},{6,2},{2,0},{1,3},{5,1},... | collective-permute-start | bytes 1622024 | tf_op jit(solution)/shard_map/ppermute | solution.py:462
  88.4 6.8 %collective-permute-start.16 = (bf16[2,528,128]{2,1,0:T(8,128)(2,1)S(1)}, bf16[2,528,128]{2,1,0:T(8,128)(2,1)S(1)}, u32[]{:S(2)}, u32[]{:S(2)}) collective-permute-start(bf16[2,528,128]{2,1,0:T(8,128)(2,1)S(1)} %shard_map.96), channel_id=1, source_target_pairs={{0,4},{4,8},{8,12},{12,14},{14,10},{10,6},{6,2},{2,0},{1,3},{5,1},... | collective-permute-start | bytes 811016 | tf_op jit(solution)/shard_map/ppermute | solution.py:462
  91.5 6.5 %collective-permute-start.15 = (bf16[2,528,128]{2,1,0:T(8,128)(2,1)S(1)}, bf16[2,528,128]{2,1,0:T(8,128)(2,1)S(1)}, u32[]{:S(2)}, u32[]{:S(2)}) collective-permute-start(bf16[2,528,128]{2,1,0:T(8,128)(2,1)S(1)} %shard_map.97), channel_id=1, source_target_pairs={{0,4},{4,8},{8,12},{12,14},{14,10},{10,6},{6,2},{2,0},{1,3},{5,1},... | collective-permute-start | bytes 811016 | tf_op jit(solution)/shard_map/ppermute | solution.py:462

commit v19 on v16

--- a/solution.py
+++ b/solution.py
@@ -221,7 +221,7 @@
         keep.wait()
 
 
-def attend(sizes, jobs, meta, queries, held, own=None, keeping=None, store=None):
+def attend(sizes, jobs, meta, queries, held, own=None, keeping=None, store=None, light=True):
     rows, suffix, cap, page_len = sizes
     keys, count = cap * page_len, len(queries)
     heads = len(jobs) // count
@@ -257,8 +257,8 @@
         out_specs=out_specs,
         scratch_shapes=scratch,
         input_output_aliases=aliases,
-        compiler_params=pltpu.CompilerParams(vmem_limit_bytes=GRANT),
-        cost_estimate=work,
+        compiler_params=pltpu.CompilerParams(vmem_limit_bytes=2 * GRANT),
+        cost_estimate=LIGHT if light else work,
     )(*args)
     return [(out[2 * n], out[2 * n + 1]) for n in range(count)] + list(out[2 * count:])
 
@@ -499,7 +499,8 @@
             keeping = (pages, pages_dev - pages)
             part, store = attend(sizes, jobs, lists[step], [came], held, None, keeping, store)
         else:
-            part, = attend(sizes, jobs, lists[step], [came], held)
+            light = step < half + 2
+            part, = attend(sizes, jobs, lists[step], [came], held, light=light)
         if step == 1:
             blocks = [packed(part)]
         elif step < stores - 2:

time: 98.4 us -> 98.4 us (level)
    unnamed x18 -> x16, local copies, waits for them, and re-layouts: 9.18 us -> 9.17 us
where the time goes in v19:
time: 98.4 us; the launch traced here: 98.2 us
  starting transfers between devices  35.8 us (36%)
  Pallas kernels  31.4 us (32%)
  waiting for transfers between devices  19.4 us (20%)
  local copies, waits for them, and re-layouts  9.17 us (9%)
  between operations  2.3 us (2%)
    ppermute x17, starting transfers between devices, onward(): return lax.ppermute(x, ('store', 'tensor'), route)  33.6 us
    pallas_call x9, Pallas kernels, attend(): pl.pallas_call(functools.partial(attend_kernel, sizes + (count,), jobs, o...  20.4 us
    ppermute x17, waiting for transfers between devices, onward(): return lax.ppermute(x, ('store', 'tensor'), route)  18.8 us
    unnamed x16, local copies, waits for them, and re-layouts  9.17 us
    pallas_call x11, Pallas kernels, call(): pl.pallas_call(kernel, out_shape=shape, in_specs=[VMEM] * len(args), out_...  6.76 us
    pallas_call x2, Pallas kernels, finish(): pl.pallas_call(functools.partial(final_kernel, suffix, first), out_shape=...  2.52 us
    ppermute x1, starting transfers between devices, shifted(): return lax.ppermute(block, axis, route)  2.17 us
  transfers between devices with their start and end apart: 18, of which 13 were waited for; matrix products, arithmetic and copies ran while one was open for 0% of the time, Pallas kernels for 31%

profile of v19, /device:TPU:0, one launch (start us, length us, event | category | flops | bytes accessed | tf_op | source)
XLA Modules:
  0.0 98.2 jit_solution(14827396821707606759)
XLA Ops:
  0.6 3.1 %collective-permute-start = (bf16[1,64,4096]{2,1,0:T(8,128)(2,1)}, bf16[1,64,4096]{2,1,0:T(8,128)(2,1)S(1)}, u32[]{:S(2)}, u32[]{:S(2)}) collective-permute-start(bf16[1,64,4096]{2,1,0:T(8,128)(2,1)} %q_ref), channel_id=1, source_target_pairs={{0,4},{4,8},{8,12},{12,14},{14,10},{10,6},{6,2},{2,0},{1,3},{5,1},... | collective-permute-start | bytes 1572872 | tf_op jit(solution)/shard_map/ppermute | solution.py:464
  5.0 0.6 copy-done.7
  5.7 0.3 shard_map.77.before_ref.lists_ref
  5.9 1.6 %collective-permute-start.1 = (bf16[16,128]{1,0:T(8,128)(2,1)S(1)}, bf16[16,128]{1,0:T(8,128)(2,1)S(1)}, u32[]{:S(2)}, u32[]{:S(2)}) collective-permute-start(bf16[16,128]{1,0:T(8,128)(2,1)S(1)} %shard_map.77.before_ref.lists_ref), channel_id=1, source_target_pairs={{0,4},{4,8},{8,12},{12,14},{14,10},{10,6},{6,2},{2,0},{1,3},{5,1},... | collective-permute-start | bytes 12296 | tf_op jit(solution)/shard_map/ppermute | solution.py:464
  7.5 2.2 %copy-done.4 = bf16[32,2,64,512]{3,2,1,0:T(8,128)(2,1)S(1)} copy-done((bf16[32,2,64,512]{3,2,1,0:T(8,128)(2,1)S(1)}, bf16[32,2,64,512]{3,2,1,0:T(8,128)(2,1)}, u32[]{:S(2)}) %copy-start.4) | copy-done | bytes 4194328
  9.7 0.3 shard_map.78.refs_2_.refs_3_
  10.0 1.9 %copy-done = bf16[32,2,64,512]{3,2,1,0:T(8,128)(2,1)} copy-done((bf16[32,2,64,512]{3,2,1,0:T(8,128)(2,1)}, bf16[32,2,64,512]{3,2,1,0:T(8,128)(2,1)S(1)}, u32[]{:S(2)}) %copy-start) | copy-done | bytes 4194328
  12.0 0.0 collective-permute-done.q_ref
  12.0 0.0 collective-permute-done.1.lists_ref
  12.0 0.1 shard_map.79.refs_1_
  12.1 1.6 %collective-permute-start.3 = (bf16[2064,128]{1,0:T(8,128)(2,1)S(1)}, bf16[2064,128]{1,0:T(8,128)(2,1)S(1)}, u32[]{:S(2)}, u32[]{:S(2)}) collective-permute-start(bf16[2064,128]{1,0:T(8,128)(2,1)S(1)} %shard_map.79.refs_1_), channel_id=1, source_target_pairs={{0,4},{4,8},{8,12},{12,14},{14,10},{10,6},{6,2},{2,0},{1,3},{5,1},... | collective-permute-start | bytes 1585160 | tf_op jit(solution)/shard_map/ppermute | solution.py:464
  13.7 2.2 %copy-done.1 = bf16[32,2,64,512]{3,2,1,0:T(8,128)(2,1)S(1)} copy-done((bf16[32,2,64,512]{3,2,1,0:T(8,128)(2,1)S(1)}, bf16[32,2,64,512]{3,2,1,0:T(8,128)(2,1)}, u32[]{:S(2)}) %copy-start.1) | copy-done | bytes 4194328
  15.9 2.8 %shard_map.80 = (f32[4,512,128]{2,1,0:T(8,128)S(1)}, bf16[4,16,128]{2,1,0:T(8,128)(2,1)S(1)}, bf16[32,2,64,512]{3,2,1,0:T(8,128)(2,1)}) custom-call(s32[1,128]{1,0:T(1,128)S(1)} %fusion.refs_0_, bf16[2064,128]{1,0:T(8,128)(2,1)S(1)} %shard_map.79.refs_1_, bf16[32,2,64,512]{3,2,1,0:T(8,128)(2,1)S(1)} %copy-done.1), custom_call_target="tpu_custom_call" | custom-call | flops 1 | bytes 1 | tf_op jit(solution)/shard_map/pallas_call | solution.py:253
  18.7 0.1 shard_map.81
  18.7 1.6 %collective-permute-start.2 = (bf16[4,528,128]{2,1,0:T(8,128)(2,1)S(1)}, bf16[4,528,128]{2,1,0:T(8,128)(2,1)S(1)}, u32[]{:S(2)}, u32[]{:S(2)}) collective-permute-start(bf16[4,528,128]{2,1,0:T(8,128)(2,1)S(1)} %shard_map.81), channel_id=1, source_target_pairs={{0,4},{4,8},{8,12},{12,14},{14,10},{10,6},{6,2},{2,0},{1,3},{5,1},... | collective-permute-start | bytes 1622024 | tf_op jit(solution)/shard_map/ppermute | solution.py:464
  20.3 1.0 %collective-permute-done.3.refs_1_ = bf16[2064,128]{1,0:T(8,128)(2,1)S(1)} collective-permute-done((bf16[2064,128]{1,0:T(8,128)(2,1)S(1)}, bf16[2064,128]{1,0:T(8,128)(2,1)S(1)}, u32[]{:S(2)}, u32[]{:S(2)}) %collective-permute-start.3) | collective-permute-done | bytes 528416 | tf_op jit(solution)/shard_map/ppermute | solution.py:464
  21.4 1.6 %collective-permute-start.5 = (bf16[2064,128]{1,0:T(8,128)(2,1)S(1)}, bf16[2064,128]{1,0:T(8,128)(2,1)S(1)}, u32[]{:S(2)}, u32[]{:S(2)}) collective-permute-start(bf16[2064,128]{1,0:T(8,128)(2,1)S(1)} %collective-permute-done.3.refs_1_), channel_id=1, source_target_pairs={{0,4},{4,8},{8,12},{12,14},{14,10},{10,6},{6,2},{2,0},{1,3},{5,1},... | collective-permute-start | bytes 1585160 | tf_op jit(solution)/shard_map/ppermute | solution.py:464
  22.9 2.9 %shard_map.82 = (f32[4,512,128]{2,1,0:T(8,128)S(1)}, bf16[4,16,128]{2,1,0:T(8,128)(2,1)S(1)}, bf16[32,2,64,512]{3,2,1,0:T(8,128)(2,1)}) custom-call(s32[1,128]{1,0:T(1,128)S(1)} %fusion.1.refs_0_.near_ref, bf16[2064,128]{1,0:T(8,128)(2,1)S(1)} %collective-permute-done.3.refs_1_, ...), custom_call_target="tpu_custom_call", output_to_operand_aliasing={{2}: (3, {})} | custom-call | flops 1 | bytes 1 | tf_op jit(solution)/shard_map/pallas_call | solution.py:253
  25.9 2.3 %collective-permute-done.2.in_ref = bf16[4,528,128]{2,1,0:T(8,128)(2,1)S(1)} collective-permute-done((bf16[4,528,128]{2,1,0:T(8,128)(2,1)S(1)}, bf16[4,528,128]{2,1,0:T(8,128)(2,1)S(1)}, u32[]{:S(2)}, u32[]{:S(2)}) %collective-permute-start.2) | collective-permute-done | bytes 540704 | tf_op jit(solution)/shard_map/ppermute | solution.py:464
  28.2 1.0 %shard_map.83 = bf16[4,528,128]{2,1,0:T(8,128)(2,1)S(1)} custom-call(bf16[4,528,128]{2,1,0:T(8,128)(2,1)S(1)} %collective-permute-done.2.in_ref, f32[4,512,128]{2,1,0:T(8,128)S(1)} %get-tuple-element.48.acc_ref, bf16[4,16,128]{2,1,0:T(8,128)(2,1)S(1)} %get-tuple-element.49.stat_ref), custom_call_target="tpu_custom_call" | custom-call | flops 1605632 | bytes 3211264 | tf_op jit(solution)/shard_map/pallas_call | solution.py:391
  29.2 1.6 %collective-permute-start.4 = (bf16[4,528,128]{2,1,0:T(8,128)(2,1)S(1)}, bf16[4,528,128]{2,1,0:T(8,128)(2,1)S(1)}, u32[]{:S(2)}, u32[]{:S(2)}) collective-permute-start(bf16[4,528,128]{2,1,0:T(8,128)(2,1)S(1)} %shard_map.83), channel_id=1, source_target_pairs={{0,4},{4,8},{8,12},{12,14},{14,10},{10,6},{6,2},{2,0},{1,3},{5,1},... | collective-permute-start | bytes 1622024 | tf_op jit(solution)/shard_map/ppermute | solution.py:464
  30.7 3.1 %collective-permute-done.5.refs_1_ = bf16[2064,128]{1,0:T(8,128)(2,1)S(1)} collective-permute-done((bf16[2064,128]{1,0:T(8,128)(2,1)S(1)}, bf16[2064,128]{1,0:T(8,128)(2,1)S(1)}, u32[]{:S(2)}, u32[]{:S(2)}) %collective-permute-start.5) | collective-permute-done | bytes 528416 | tf_op jit(solution)/shard_map/ppermute | solution.py:464
  33.8 1.5 %collective-permute-start.7 = (bf16[2064,128]{1,0:T(8,128)(2,1)S(1)}, bf16[2064,128]{1,0:T(8,128)(2,1)S(1)}, u32[]{:S(2)}, u32[]{:S(2)}) collective-permute-start(bf16[2064,128]{1,0:T(8,128)(2,1)S(1)} %collective-permute-done.5.refs_1_), channel_id=1, source_target_pairs={{0,4},{4,8},{8,12},{12,14},{14,10},{10,6},{6,2},{2,0},{1,3},{5,1},... | collective-permute-start | bytes 1585160 | tf_op jit(solution)/shard_map/ppermute | solution.py:464
  35.3 2.2 %copy-done.3 = bf16[32,2,64,512]{3,2,1,0:T(8,128)(2,1)S(1)} copy-done((bf16[32,2,64,512]{3,2,1,0:T(8,128)(2,1)S(1)}, bf16[32,2,64,512]{3,2,1,0:T(8,128)(2,1)}, u32[]{:S(2)}) %copy-start.3) | copy-done | bytes 4194328
  37.5 2.2 %shard_map.84 = (f32[4,512,128]{2,1,0:T(8,128)S(1)}, bf16[4,16,128]{2,1,0:T(8,128)(2,1)S(1)}) custom-call(s32[1,128]{1,0:T(1,128)S(1)} %fusion.2.refs_0_, bf16[2064,128]{1,0:T(8,128)(2,1)S(1)} %collective-permute-done.5.refs_1_, bf16[32,2,64,512]{3,2,1,0:T(8,128)(2,1)S(1)} %copy-done.3), custom_call_target="tpu_custom_call" | custom-call | flops 1 | bytes 1 | tf_op jit(solution)/shard_map/pallas_call | solution.py:253
  39.8 1.0 %shard_map.85 = bf16[4,528,128]{2,1,0:T(8,128)(2,1)S(1)} custom-call(bf16[4,528,128]{2,1,0:T(8,128)(2,1)S(1)} %collective-permute-done.4.in_ref, f32[4,512,128]{2,1,0:T(8,128)S(1)} %get-tuple-element.52.acc_ref, bf16[4,16,128]{2,1,0:T(8,128)(2,1)S(1)} %get-tuple-element.53.stat_ref), custom_call_target="tpu_custom_call" | custom-call | flops 1605632 | bytes 3211264 | tf_op jit(solution)/shard_map/pallas_call | solution.py:391
  40.8 1.4 %collective-permute-start.6 = (bf16[4,528,128]{2,1,0:T(8,128)(2,1)S(1)}, bf16[4,528,128]{2,1,0:T(8,128)(2,1)S(1)}, u32[]{:S(2)}, u32[]{:S(2)}) collective-permute-start(bf16[4,528,128]{2,1,0:T(8,128)(2,1)S(1)} %shard_map.85), channel_id=1, source_target_pairs={{0,4},{4,8},{8,12},{12,14},{14,10},{10,6},{6,2},{2,0},{1,3},{5,1},... | collective-permute-start | bytes 1622024 | tf_op jit(solution)/shard_map/ppermute | solution.py:464
  42.2 0.1 shard_map.86.refs_1_
  42.3 1.8 %shard_map.87 = (f32[2,512,128]{2,1,0:T(8,128)S(1)}, bf16[2,16,128]{2,1,0:T(8,128)(2,1)S(1)}) custom-call(s32[1,128]{1,0:T(1,128)S(1)} %fusion.3.refs_0_, bf16[2064,128]{1,0:T(8,128)(2,1)S(1)} %shard_map.86.refs_1_, bf16[2,64,512]{2,1,0:T(8,128)(2,1)S(1)} %bitcast.3, bf16[32,2,64,512]{3,2,1,0:T(8,128)(2,1)S(1)} %copy-done.3), custom_call_target="tpu_custom_call" | custom-call | flops 1 | bytes 1 | tf_op jit(solution)/shard_map/pallas_call | solution.py:253
  44.1 1.2 %collective-permute-done.7.refs_1_ = bf16[2064,128]{1,0:T(8,128)(2,1)S(1)} collective-permute-done((bf16[2064,128]{1,0:T(8,128)(2,1)S(1)}, bf16[2064,128]{1,0:T(8,128)(2,1)S(1)}, u32[]{:S(2)}, u32[]{:S(2)}) %collective-permute-start.7) | collective-permute-done | bytes 528416 | tf_op jit(solution)/shard_map/ppermute | solution.py:464
  45.3 1.5 %collective-permute-start.9 = (bf16[2064,128]{1,0:T(8,128)(2,1)S(1)}, bf16[2064,128]{1,0:T(8,128)(2,1)S(1)}, u32[]{:S(2)}, u32[]{:S(2)}) collective-permute-start(bf16[2064,128]{1,0:T(8,128)(2,1)S(1)} %collective-permute-done.7.refs_1_), channel_id=1, source_target_pairs={{0,4},{4,8},{8,12},{12,14},{14,10},{10,6},{6,2},{2,0},{1,3},{5,1},... | collective-permute-start | bytes 1585160 | tf_op jit(solution)/shard_map/ppermute | solution.py:464
  46.8 2.2 %shard_map.88 = (f32[4,512,128]{2,1,0:T(8,128)S(1)}, bf16[4,16,128]{2,1,0:T(8,128)(2,1)S(1)}) custom-call(s32[1,128]{1,0:T(1,128)S(1)} %fusion.4.refs_0_, bf16[2064,128]{1,0:T(8,128)(2,1)S(1)} %collective-permute-done.7.refs_1_, bf16[32,2,64,512]{3,2,1,0:T(8,128)(2,1)S(1)} %copy-done.3), custom_call_target="tpu_custom_call" | custom-call | flops 1 | bytes 1 | tf_op jit(solution)/shard_map/pallas_call | solution.py:253
  49.0 2.0 %collective-permute-done.6.in_ref = bf16[4,528,128]{2,1,0:T(8,128)(2,1)S(1)} collective-permute-done((bf16[4,528,128]{2,1,0:T(8,128)(2,1)S(1)}, bf16[4,528,128]{2,1,0:T(8,128)(2,1)S(1)}, u32[]{:S(2)}, u32[]{:S(2)}) %collective-permute-start.6) | collective-permute-done | bytes 540704 | tf_op jit(solution)/shard_map/ppermute | solution.py:464
  51.1 1.0 %shard_map.89 = bf16[4,528,128]{2,1,0:T(8,128)(2,1)S(1)} custom-call(bf16[4,528,128]{2,1,0:T(8,128)(2,1)S(1)} %collective-permute-done.6.in_ref, f32[4,512,128]{2,1,0:T(8,128)S(1)} %get-tuple-element.60.acc_ref, bf16[4,16,128]{2,1,0:T(8,128)(2,1)S(1)} %get-tuple-element.61.stat_ref), custom_call_target="tpu_custom_call" | custom-call | flops 1605632 | bytes 3211264 | tf_op jit(solution)/shard_map/pallas_call | solution.py:391
  52.1 1.7 %collective-permute-start.8 = (bf16[4,528,128]{2,1,0:T(8,128)(2,1)S(1)}, bf16[4,528,128]{2,1,0:T(8,128)(2,1)S(1)}, u32[]{:S(2)}, u32[]{:S(2)}) collective-permute-start(bf16[4,528,128]{2,1,0:T(8,128)(2,1)S(1)} %shard_map.89), channel_id=1, source_target_pairs={{0,4},{4,8},{8,12},{12,14},{14,10},{10,6},{6,2},{2,0},{1,3},{5,1},... | collective-permute-start | bytes 1622024 | tf_op jit(solution)/shard_map/ppermute | solution.py:464
  53.8 1.8 %shard_map.90 = (f32[2,512,128]{2,1,0:T(8,128)S(1)}, bf16[2,16,128]{2,1,0:T(8,128)(2,1)S(1)}) custom-call(s32[1,128]{1,0:T(1,128)S(1)} %fusion.3.refs_0_, bf16[2064,128]{1,0:T(8,128)(2,1)S(1)} %shard_map.86.refs_1_, bf16[2,64,512]{2,1,0:T(8,128)(2,1)S(1)} %bitcast.4, bf16[32,2,64,512]{3,2,1,0:T(8,128)(2,1)S(1)} %copy-done.3), custom_call_target="tpu_custom_call" | custom-call | flops 1 | bytes 1 | tf_op jit(solution)/shard_map/pallas_call | solution.py:253
  55.6 1.1 %collective-permute-done.9.refs_1_ = bf16[2064,128]{1,0:T(8,128)(2,1)S(1)} collective-permute-done((bf16[2064,128]{1,0:T(8,128)(2,1)S(1)}, bf16[2064,128]{1,0:T(8,128)(2,1)S(1)}, u32[]{:S(2)}, u32[]{:S(2)}) %collective-permute-start.9) | collective-permute-done | bytes 528416 | tf_op jit(solution)/shard_map/ppermute | solution.py:464
  56.7 1.5 %collective-permute-start.11 = (bf16[2064,128]{1,0:T(8,128)(2,1)S(1)}, bf16[2064,128]{1,0:T(8,128)(2,1)S(1)}, u32[]{:S(2)}, u32[]{:S(2)}) collective-permute-start(bf16[2064,128]{1,0:T(8,128)(2,1)S(1)} %collective-permute-done.9.refs_1_), channel_id=1, source_target_pairs={{0,4},{4,8},{8,12},{12,14},{14,10},{10,6},{6,2},{2,0},{1,3},{5,1},... | collective-permute-start | bytes 1585160 | tf_op jit(solution)/shard_map/ppermute | solution.py:464
  58.2 2.2 %shard_map.91 = (f32[4,512,128]{2,1,0:T(8,128)S(1)}, bf16[4,16,128]{2,1,0:T(8,128)(2,1)S(1)}) custom-call(s32[1,128]{1,0:T(1,128)S(1)} %fusion.5.refs_0_, bf16[2064,128]{1,0:T(8,128)(2,1)S(1)} %collective-permute-done.9.refs_1_, bf16[32,2,64,512]{3,2,1,0:T(8,128)(2,1)S(1)} %copy-done.3), custom_call_target="tpu_custom_call" | custom-call | flops 1 | bytes 1 | tf_op jit(solution)/shard_map/pallas_call | solution.py:253
  60.5 2.0 %collective-permute-done.8.in_ref = bf16[4,528,128]{2,1,0:T(8,128)(2,1)S(1)} collective-permute-done((bf16[4,528,128]{2,1,0:T(8,128)(2,1)S(1)}, bf16[4,528,128]{2,1,0:T(8,128)(2,1)S(1)}, u32[]{:S(2)}, u32[]{:S(2)}) %collective-permute-start.8) | collective-permute-done | bytes 540704 | tf_op jit(solution)/shard_map/ppermute | solution.py:464
  62.5 1.0 %shard_map.92 = bf16[4,528,128]{2,1,0:T(8,128)(2,1)S(1)} custom-call(bf16[4,528,128]{2,1,0:T(8,128)(2,1)S(1)} %collective-permute-done.8.in_ref, f32[4,512,128]{2,1,0:T(8,128)S(1)} %get-tuple-element.67.acc_ref, bf16[4,16,128]{2,1,0:T(8,128)(2,1)S(1)} %get-tuple-element.68.stat_ref), custom_call_target="tpu_custom_call" | custom-call | flops 1605632 | bytes 3211264 | tf_op jit(solution)/shard_map/pallas_call | solution.py:391
  63.5 1.6 %collective-permute-start.10 = (bf16[4,528,128]{2,1,0:T(8,128)(2,1)S(1)}, bf16[4,528,128]{2,1,0:T(8,128)(2,1)S(1)}, u32[]{:S(2)}, u32[]{:S(2)}) collective-permute-start(bf16[4,528,128]{2,1,0:T(8,128)(2,1)S(1)} %shard_map.92), channel_id=1, source_target_pairs={{0,4},{4,8},{8,12},{12,14},{14,10},{10,6},{6,2},{2,0},{1,3},{5,1},... | collective-permute-start | bytes 1622024 | tf_op jit(solution)/shard_map/ppermute | solution.py:464
  65.1 3.1 %collective-permute-done.11.refs_1_ = bf16[2064,128]{1,0:T(8,128)(2,1)S(1)} collective-permute-done((bf16[2064,128]{1,0:T(8,128)(2,1)S(1)}, bf16[2064,128]{1,0:T(8,128)(2,1)S(1)}, u32[]{:S(2)}, u32[]{:S(2)}) %collective-permute-start.11) | collective-permute-done | bytes 528416 | tf_op jit(solution)/shard_map/ppermute | solution.py:464
  68.2 1.5 %collective-permute-start.13 = (bf16[2064,128]{1,0:T(8,128)(2,1)S(1)}, bf16[2064,128]{1,0:T(8,128)(2,1)S(1)}, u32[]{:S(2)}, u32[]{:S(2)}) collective-permute-start(bf16[2064,128]{1,0:T(8,128)(2,1)S(1)} %collective-permute-done.11.refs_1_), channel_id=1, source_target_pairs={{0,4},{4,8},{8,12},{12,14},{14,10},{10,6},{6,2},{2,0},{1,3},{5,1},... | collective-permute-start | bytes 1585160 | tf_op jit(solution)/shard_map/ppermute | solution.py:464
  69.7 2.2 %collective-permute-start.14 = (bf16[1,2,64,512]{3,2,1,0:T(8,128)(2,1)S(1)}, bf16[1,2,64,512]{3,2,1,0:T(8,128)(2,1)S(1)}, u32[]{:S(2)}, u32[]{:S(2)}) collective-permute-start(bf16[1,2,64,512]{3,2,1,0:T(8,128)(2,1)S(1)} %copy-done.5), channel_id=1, source_target_pairs={{8,0},{10,2},{12,4},{14,6},{0,8},{2,10},{4,12},{6,14},{9,1},{11,3}... | collective-permute-start | bytes 393224 | tf_op jit(solution)/shard_map/ppermute | solution.py:26
  71.9 2.2 %shard_map.93 = (f32[4,512,128]{2,1,0:T(8,128)S(1)}, bf16[4,16,128]{2,1,0:T(8,128)(2,1)S(1)}) custom-call(s32[1,128]{1,0:T(1,128)S(1)} %fusion.6.refs_0_.far_ref, bf16[2064,128]{1,0:T(8,128)(2,1)S(1)} %collective-permute-done.11.refs_1_, bf16[32,2,64,512]{3,2,1,0:T(8,128)(2,1)S(1)} %copy-done.3), custom_call_target="tpu_custom_call" | custom-call | flops 1073741824 | bytes 2621440 | tf_op jit(solution)/shard_map/pallas_call | solution.py:253
  74.1 0.3 collective-permute-done.10.in_ref
  74.4 0.6 shard_map.94
  75.0 2.7 %collective-permute-start.15 = (bf16[2,528,128]{2,1,0:T(8,128)(2,1)S(1)}, bf16[2,528,128]{2,1,0:T(8,128)(2,1)S(1)}, u32[]{:S(2)}, u32[]{:S(2)}) collective-permute-start(bf16[2,528,128]{2,1,0:T(8,128)(2,1)S(1)} %shard_map.94), channel_id=1, source_target_pairs={{0,4},{4,8},{8,12},{12,14},{14,10},{10,6},{6,2},{2,0},{1,3},{5,1},... | collective-permute-start | bytes 811016 | tf_op jit(solution)/shard_map/ppermute | solution.py:464
  77.7 0.6 shard_map.95
  78.4 2.5 %collective-permute-start.12 = (bf16[2,528,128]{2,1,0:T(8,128)(2,1)S(1)}, bf16[2,528,128]{2,1,0:T(8,128)(2,1)S(1)}, u32[]{:S(2)}, u32[]{:S(2)}) collective-permute-start(bf16[2,528,128]{2,1,0:T(8,128)(2,1)S(1)} %shard_map.95), channel_id=1, source_target_pairs={{0,4},{4,8},{8,12},{12,14},{14,10},{10,6},{6,2},{2,0},{1,3},{5,1},... | collective-permute-start | bytes 811016 | tf_op jit(solution)/shard_map/ppermute | solution.py:464
  80.9 0.6 collective-permute-done.14.page_ref
  81.5 0.0 collective-permute-done.13.refs_1_
  81.5 2.2 %shard_map.96 = (f32[4,512,128]{2,1,0:T(8,128)S(1)}, bf16[4,16,128]{2,1,0:T(8,128)(2,1)S(1)}) custom-call(s32[1,128]{1,0:T(1,128)S(1)} %fusion.7.refs_0_, bf16[2064,128]{1,0:T(8,128)(2,1)S(1)} %collective-permute-done.13.refs_1_, bf16[32,2,64,512]{3,2,1,0:T(8,128)(2,1)S(1)} %copy-done.3), custom_call_target="tpu_custom_call" | custom-call | flops 1073741824 | bytes 2621440 | tf_op jit(solution)/shard_map/pallas_call | solution.py:253
  83.8 0.6 collective-permute-done.15.in_ref
  84.4 0.6 shard_map.97
  85.1 4.1 %collective-permute-start.17 = (bf16[2,528,128]{2,1,0:T(8,128)(2,1)S(1)}, bf16[2,528,128]{2,1,0:T(8,128)(2,1)S(1)}, u32[]{:S(2)}, u32[]{:S(2)}) collective-permute-start(bf16[2,528,128]{2,1,0:T(8,128)(2,1)S(1)} %shard_map.97), channel_id=1, source_target_pairs={{0,4},{4,8},{8,12},{12,14},{14,10},{10,6},{6,2},{2,0},{1,3},{5,1},... | collective-permute-start | bytes 811016 | tf_op jit(solution)/shard_map/ppermute | solution.py:464
  89.1 0.6 shard_map.98
  89.8 2.5 %collective-permute-start.16 = (bf16[2,528,128]{2,1,0:T(8,128)(2,1)S(1)}, bf16[2,528,128]{2,1,0:T(8,128)(2,1)S(1)}, u32[]{:S(2)}, u32[]{:S(2)}) collective-permute-start(bf16[2,528,128]{2,1,0:T(8,128)(2,1)S(1)} %shard_map.98), channel_id=1, source_target_pairs={{0,4},{4,8},{8,12},{12,14},{14,10},{10,6},{6,2},{2,0},{1,3},{5,1},... | collective-permute-start | bytes 811016 | tf_op jit(solution)/shard_map/ppermute | solution.py:464
  92.3 1.2 %shard_map.99 = bf16[32,2,64,512]{3,2,1,0:T(8,128)(2,1)} custom-call(s32[1]{0:T(128)} %bitcast.1.me_ref, s32[1]{0:T(128)} %bitcast.2.core_ref, s32[1,128]{1,0:T(1,128)S(1)} %fusion.1.refs_0_.near_ref, s32[1,128]{1,0:T(1,128)S(1)} %fusion.6.refs_0_.far_ref, ...), custom_call_target="tpu_custom_call", output_to_operand_aliasing={{}: (5, {})} | custom-call | flops 1 | bytes 1 | tf_op jit(solution)/shard_map/pallas_call | solution.py:294
  93.5 0.3 collective-permute-done.17.in_ref
  93.9 1.3 %shard_map.100.refs_0_ = bf16[1,64,4096]{2,1,0:T(8,128)(2,1)} custom-call(bf16[2,528,128]{2,1,0:T(8,128)(2,1)S(1)} %collective-permute-done.17.in_ref, f32[2,512,128]{2,1,0:T(8,128)S(1)} %get-tuple-element.57.acc_ref, bf16[2,16,128]{2,1,0:T(8,128)(2,1)S(1)} %get-tuple-element.58.stat_ref), custom_call_target="tpu_custom_call" | custom-call | tf_op jit(solution)/shard_map/pallas_call | solution.py:375
  95.1 1.6 %collective-permute-done.16.in_ref = bf16[2,528,128]{2,1,0:T(8,128)(2,1)S(1)} collective-permute-done((bf16[2,528,128]{2,1,0:T(8,128)(2,1)S(1)}, bf16[2,528,128]{2,1,0:T(8,128)(2,1)S(1)}, u32[]{:S(2)}, u32[]{:S(2)}) %collective-permute-start.16) | collective-permute-done | bytes 270368 | tf_op jit(solution)/shard_map/ppermute | solution.py:464
  96.8 1.3 %shard_map.101 = bf16[1,64,4096]{2,1,0:T(8,128)(2,1)} custom-call(bf16[2,528,128]{2,1,0:T(8,128)(2,1)S(1)} %collective-permute-done.16.in_ref, f32[2,512,128]{2,1,0:T(8,128)S(1)} %get-tuple-element.64.acc_ref, bf16[2,16,128]{2,1,0:T(8,128)(2,1)S(1)} %get-tuple-element.65.stat_ref, ...), custom_call_target="tpu_custom_call", output_to_operand_aliasing={{}: (3, {})} | custom-call | tf_op jit(solution)/shard_map/pallas_call | solution.py:375
  (21 shorter events, 0.1 us)
Async XLA Ops:
  0.6 11.3 %collective-permute-start = (bf16[1,64,4096]{2,1,0:T(8,128)(2,1)}, bf16[1,64,4096]{2,1,0:T(8,128)(2,1)S(1)}, u32[]{:S(2)}, u32[]{:S(2)}) collective-permute-start(bf16[1,64,4096]{2,1,0:T(8,128)(2,1)} %q_ref), channel_id=1, source_target_pairs={{0,4},{4,8},{8,12},{12,14},{14,10},{10,6},{6,2},{2,0},{1,3},{5,1},... | collective-permute-start | bytes 1572872 | tf_op jit(solution)/shard_map/ppermute | solution.py:464
  5.0 0.7 copy-start.7
  5.9 6.0 %collective-permute-start.1 = (bf16[16,128]{1,0:T(8,128)(2,1)S(1)}, bf16[16,128]{1,0:T(8,128)(2,1)S(1)}, u32[]{:S(2)}, u32[]{:S(2)}) collective-permute-start(bf16[16,128]{1,0:T(8,128)(2,1)S(1)} %shard_map.77.before_ref.lists_ref), channel_id=1, source_target_pairs={{0,4},{4,8},{8,12},{12,14},{14,10},{10,6},{6,2},{2,0},{1,3},{5,1},... | collective-permute-start | bytes 12296 | tf_op jit(solution)/shard_map/ppermute | solution.py:464
  7.5 2.2 %copy-start.4 = (bf16[32,2,64,512]{3,2,1,0:T(8,128)(2,1)S(1)}, bf16[32,2,64,512]{3,2,1,0:T(8,128)(2,1)}, u32[]{:S(2)}) copy-start(bf16[32,2,64,512]{3,2,1,0:T(8,128)(2,1)} %pages_ref.1) | copy-start | bytes 12582916
  10.0 2.0 %copy-start = (bf16[32,2,64,512]{3,2,1,0:T(8,128)(2,1)}, bf16[32,2,64,512]{3,2,1,0:T(8,128)(2,1)S(1)}, u32[]{:S(2)}) copy-start(bf16[32,2,64,512]{3,2,1,0:T(8,128)(2,1)S(1)} %shard_map.78.refs_2_.refs_3_) | copy-start | bytes 12582916
  12.1 9.3 %collective-permute-start.3 = (bf16[2064,128]{1,0:T(8,128)(2,1)S(1)}, bf16[2064,128]{1,0:T(8,128)(2,1)S(1)}, u32[]{:S(2)}, u32[]{:S(2)}) collective-permute-start(bf16[2064,128]{1,0:T(8,128)(2,1)S(1)} %shard_map.79.refs_1_), channel_id=1, source_target_pairs={{0,4},{4,8},{8,12},{12,14},{14,10},{10,6},{6,2},{2,0},{1,3},{5,1},... | collective-permute-start | bytes 1585160 | tf_op jit(solution)/shard_map/ppermute | solution.py:464
  13.7 2.2 %copy-start.1 = (bf16[32,2,64,512]{3,2,1,0:T(8,128)(2,1)S(1)}, bf16[32,2,64,512]{3,2,1,0:T(8,128)(2,1)}, u32[]{:S(2)}) copy-start(bf16[32,2,64,512]{3,2,1,0:T(8,128)(2,1)} %copy-done) | copy-start | bytes 12582916
  15.9 7.0 %copy-start.2 = (bf16[32,2,64,512]{3,2,1,0:T(8,128)(2,1)S(1)}, bf16[32,2,64,512]{3,2,1,0:T(8,128)(2,1)}, u32[]{:S(2)}) copy-start(bf16[32,2,64,512]{3,2,1,0:T(8,128)(2,1)} %copy-done) | copy-start | bytes 12582916
  18.7 9.4 %collective-permute-start.2 = (bf16[4,528,128]{2,1,0:T(8,128)(2,1)S(1)}, bf16[4,528,128]{2,1,0:T(8,128)(2,1)S(1)}, u32[]{:S(2)}, u32[]{:S(2)}) collective-permute-start(bf16[4,528,128]{2,1,0:T(8,128)(2,1)S(1)} %shard_map.81), channel_id=1, source_target_pairs={{0,4},{4,8},{8,12},{12,14},{14,10},{10,6},{6,2},{2,0},{1,3},{5,1},... | collective-permute-start | bytes 1622024 | tf_op jit(solution)/shard_map/ppermute | solution.py:464
  21.4 12.5 %collective-permute-start.5 = (bf16[2064,128]{1,0:T(8,128)(2,1)S(1)}, bf16[2064,128]{1,0:T(8,128)(2,1)S(1)}, u32[]{:S(2)}, u32[]{:S(2)}) collective-permute-start(bf16[2064,128]{1,0:T(8,128)(2,1)S(1)} %collective-permute-done.3.refs_1_), channel_id=1, source_target_pairs={{0,4},{4,8},{8,12},{12,14},{14,10},{10,6},{6,2},{2,0},{1,3},{5,1},... | collective-permute-start | bytes 1585160 | tf_op jit(solution)/shard_map/ppermute | solution.py:464
  28.1 14.0 %copy-start.6 = (bf16[1,64,4096]{2,1,0:T(8,128)(2,1)S(1)}, bf16[1,64,4096]{2,1,0:T(8,128)(2,1)}, u32[]{:S(2)}) copy-start(bf16[1,64,4096]{2,1,0:T(8,128)(2,1)} %q_ref) | copy-start | bytes 1572868
  28.1 14.1 %copy-start.5 = (bf16[1,2,64,512]{3,2,1,0:T(8,128)(2,1)S(1)}, bf16[1,2,64,512]{3,2,1,0:T(8,128)(2,1)}, u32[]{:S(2)}) copy-start(bf16[1,2,64,512]{3,2,1,0:T(8,128)(2,1)} %param.7) | copy-start | bytes 393220
  29.2 10.6 %collective-permute-start.4 = (bf16[4,528,128]{2,1,0:T(8,128)(2,1)S(1)}, bf16[4,528,128]{2,1,0:T(8,128)(2,1)S(1)}, u32[]{:S(2)}, u32[]{:S(2)}) collective-permute-start(bf16[4,528,128]{2,1,0:T(8,128)(2,1)S(1)} %shard_map.83), channel_id=1, source_target_pairs={{0,4},{4,8},{8,12},{12,14},{14,10},{10,6},{6,2},{2,0},{1,3},{5,1},... | collective-permute-start | bytes 1622024 | tf_op jit(solution)/shard_map/ppermute | solution.py:464
  33.8 11.5 %collective-permute-start.7 = (bf16[2064,128]{1,0:T(8,128)(2,1)S(1)}, bf16[2064,128]{1,0:T(8,128)(2,1)S(1)}, u32[]{:S(2)}, u32[]{:S(2)}) collective-permute-start(bf16[2064,128]{1,0:T(8,128)(2,1)S(1)} %collective-permute-done.5.refs_1_), channel_id=1, source_target_pairs={{0,4},{4,8},{8,12},{12,14},{14,10},{10,6},{6,2},{2,0},{1,3},{5,1},... | collective-permute-start | bytes 1585160 | tf_op jit(solution)/shard_map/ppermute | solution.py:464
  35.3 2.2 %copy-start.3 = (bf16[32,2,64,512]{3,2,1,0:T(8,128)(2,1)S(1)}, bf16[32,2,64,512]{3,2,1,0:T(8,128)(2,1)}, u32[]{:S(2)}) copy-start(bf16[32,2,64,512]{3,2,1,0:T(8,128)(2,1)} %copy-done) | copy-start | bytes 12582916
  40.8 10.3 %collective-permute-start.6 = (bf16[4,528,128]{2,1,0:T(8,128)(2,1)S(1)}, bf16[4,528,128]{2,1,0:T(8,128)(2,1)S(1)}, u32[]{:S(2)}, u32[]{:S(2)}) collective-permute-start(bf16[4,528,128]{2,1,0:T(8,128)(2,1)S(1)} %shard_map.85), channel_id=1, source_target_pairs={{0,4},{4,8},{8,12},{12,14},{14,10},{10,6},{6,2},{2,0},{1,3},{5,1},... | collective-permute-start | bytes 1622024 | tf_op jit(solution)/shard_map/ppermute | solution.py:464
  45.3 11.5 %collective-permute-start.9 = (bf16[2064,128]{1,0:T(8,128)(2,1)S(1)}, bf16[2064,128]{1,0:T(8,128)(2,1)S(1)}, u32[]{:S(2)}, u32[]{:S(2)}) collective-permute-start(bf16[2064,128]{1,0:T(8,128)(2,1)S(1)} %collective-permute-done.7.refs_1_), channel_id=1, source_target_pairs={{0,4},{4,8},{8,12},{12,14},{14,10},{10,6},{6,2},{2,0},{1,3},{5,1},... | collective-permute-start | bytes 1585160 | tf_op jit(solution)/shard_map/ppermute | solution.py:464
  52.1 10.4 %collective-permute-start.8 = (bf16[4,528,128]{2,1,0:T(8,128)(2,1)S(1)}, bf16[4,528,128]{2,1,0:T(8,128)(2,1)S(1)}, u32[]{:S(2)}, u32[]{:S(2)}) collective-permute-start(bf16[4,528,128]{2,1,0:T(8,128)(2,1)S(1)} %shard_map.89), channel_id=1, source_target_pairs={{0,4},{4,8},{8,12},{12,14},{14,10},{10,6},{6,2},{2,0},{1,3},{5,1},... | collective-permute-start | bytes 1622024 | tf_op jit(solution)/shard_map/ppermute | solution.py:464
  56.7 11.5 %collective-permute-start.11 = (bf16[2064,128]{1,0:T(8,128)(2,1)S(1)}, bf16[2064,128]{1,0:T(8,128)(2,1)S(1)}, u32[]{:S(2)}, u32[]{:S(2)}) collective-permute-start(bf16[2064,128]{1,0:T(8,128)(2,1)S(1)} %collective-permute-done.9.refs_1_), channel_id=1, source_target_pairs={{0,4},{4,8},{8,12},{12,14},{14,10},{10,6},{6,2},{2,0},{1,3},{5,1},... | collective-permute-start | bytes 1585160 | tf_op jit(solution)/shard_map/ppermute | solution.py:464
  63.5 10.9 %collective-permute-start.10 = (bf16[4,528,128]{2,1,0:T(8,128)(2,1)S(1)}, bf16[4,528,128]{2,1,0:T(8,128)(2,1)S(1)}, u32[]{:S(2)}, u32[]{:S(2)}) collective-permute-start(bf16[4,528,128]{2,1,0:T(8,128)(2,1)S(1)} %shard_map.92), channel_id=1, source_target_pairs={{0,4},{4,8},{8,12},{12,14},{14,10},{10,6},{6,2},{2,0},{1,3},{5,1},... | collective-permute-start | bytes 1622024 | tf_op jit(solution)/shard_map/ppermute | solution.py:464
  68.2 13.4 %collective-permute-start.13 = (bf16[2064,128]{1,0:T(8,128)(2,1)S(1)}, bf16[2064,128]{1,0:T(8,128)(2,1)S(1)}, u32[]{:S(2)}, u32[]{:S(2)}) collective-permute-start(bf16[2064,128]{1,0:T(8,128)(2,1)S(1)} %collective-permute-done.11.refs_1_), channel_id=1, source_target_pairs={{0,4},{4,8},{8,12},{12,14},{14,10},{10,6},{6,2},{2,0},{1,3},{5,1},... | collective-permute-start | bytes 1585160 | tf_op jit(solution)/shard_map/ppermute | solution.py:464
  69.7 11.8 %collective-permute-start.14 = (bf16[1,2,64,512]{3,2,1,0:T(8,128)(2,1)S(1)}, bf16[1,2,64,512]{3,2,1,0:T(8,128)(2,1)S(1)}, u32[]{:S(2)}, u32[]{:S(2)}) collective-permute-start(bf16[1,2,64,512]{3,2,1,0:T(8,128)(2,1)S(1)} %copy-done.5), channel_id=1, source_target_pairs={{8,0},{10,2},{12,4},{14,6},{0,8},{2,10},{4,12},{6,14},{9,1},{11,3}... | collective-permute-start | bytes 393224 | tf_op jit(solution)/shard_map/ppermute | solution.py:26
  75.0 9.4 %collective-permute-start.15 = (bf16[2,528,128]{2,1,0:T(8,128)(2,1)S(1)}, bf16[2,528,128]{2,1,0:T(8,128)(2,1)S(1)}, u32[]{:S(2)}, u32[]{:S(2)}) collective-permute-start(bf16[2,528,128]{2,1,0:T(8,128)(2,1)S(1)} %shard_map.94), channel_id=1, source_target_pairs={{0,4},{4,8},{8,12},{12,14},{14,10},{10,6},{6,2},{2,0},{1,3},{5,1},... | collective-permute-start | bytes 811016 | tf_op jit(solution)/shard_map/ppermute | solution.py:464
  78.4 10.8 %collective-permute-start.12 = (bf16[2,528,128]{2,1,0:T(8,128)(2,1)S(1)}, bf16[2,528,128]{2,1,0:T(8,128)(2,1)S(1)}, u32[]{:S(2)}, u32[]{:S(2)}) collective-permute-start(bf16[2,528,128]{2,1,0:T(8,128)(2,1)S(1)} %shard_map.95), channel_id=1, source_target_pairs={{0,4},{4,8},{8,12},{12,14},{14,10},{10,6},{6,2},{2,0},{1,3},{5,1},... | collective-permute-start | bytes 811016 | tf_op jit(solution)/shard_map/ppermute | solution.py:464
  85.1 8.8 %collective-permute-start.17 = (bf16[2,528,128]{2,1,0:T(8,128)(2,1)S(1)}, bf16[2,528,128]{2,1,0:T(8,128)(2,1)S(1)}, u32[]{:S(2)}, u32[]{:S(2)}) collective-permute-start(bf16[2,528,128]{2,1,0:T(8,128)(2,1)S(1)} %shard_map.97), channel_id=1, source_target_pairs={{0,4},{4,8},{8,12},{12,14},{14,10},{10,6},{6,2},{2,0},{1,3},{5,1},... | collective-permute-start | bytes 811016 | tf_op jit(solution)/shard_map/ppermute | solution.py:464
  89.8 7.0 %collective-permute-start.16 = (bf16[2,528,128]{2,1,0:T(8,128)(2,1)S(1)}, bf16[2,528,128]{2,1,0:T(8,128)(2,1)S(1)}, u32[]{:S(2)}, u32[]{:S(2)}) collective-permute-start(bf16[2,528,128]{2,1,0:T(8,128)(2,1)S(1)} %shard_map.98), channel_id=1, source_target_pairs={{0,4},{4,8},{8,12},{12,14},{14,10},{10,6},{6,2},{2,0},{1,3},{5,1},... | collective-permute-start | bytes 811016 | tf_op jit(solution)/shard_map/ppermute | solution.py:464

commit v20 on v14

--- a/solution.py
+++ b/solution.py
@@ -15,6 +15,7 @@
 LIST_ROWS = 16
 GRANT = 20 * 1024 * 1024
 LIGHT = pl.CostEstimate(flops=1, bytes_accessed=1, transcendentals=0)
+HEAVY = pl.CostEstimate(flops=1 << 33, bytes_accessed=1 << 25, transcendentals=1 << 24)
 VMEM = pl.BlockSpec(memory_space=pltpu.VMEM)
 SMEM = pl.BlockSpec(memory_space=pltpu.SMEM)
 HBM = pl.BlockSpec(memory_space=pltpu.HBM)
@@ -221,7 +222,7 @@
         keep.wait()
 
 
-def attend(sizes, jobs, meta, queries, held, own=None, keeping=None, store=None):
+def attend(sizes, jobs, meta, queries, held, own=None, keeping=None, store=None, cost=None):
     rows, suffix, cap, page_len = sizes
     keys, count = cap * page_len, len(queries)
     heads = len(jobs) // count
@@ -258,7 +259,7 @@
         scratch_shapes=scratch,
         input_output_aliases=aliases,
         compiler_params=pltpu.CompilerParams(vmem_limit_bytes=GRANT),
-        cost_estimate=work,
+        cost_estimate=cost or work,
     )(*args)
     return [(out[2 * n], out[2 * n + 1]) for n in range(count)] + list(out[2 * count:])
 
@@ -480,12 +481,14 @@
             keeping = (pages, pages_dev - pages)
             part, store = attend(sizes, jobs, lists[step], [came], kv_pages, None, keeping, store)
         else:
-            part, = attend(sizes, jobs, lists[step], [came], kv_pages)
+            cost = {stores - 2: LIGHT, stores - 1: HEAVY}.get(step)
+            part, = attend(sizes, jobs, lists[step], [came], kv_pages, cost=cost)
         if step == 1:
             blocks = [packed(part)]
         elif step < stores - 2:
             blocks = [merged(after(partial[0], part), part, 0, 0, heads)]
         else:
+            part = after(part, arrived) if step == stores - 1 else part
             blocks = []
             for n, half_heads in enumerate(halves):
                 block, at = (partial[0], half_heads[0]) if len(partial) == 1 else (partial[n], 0)
@@ -493,8 +496,6 @@
                 blocks.append(merged(block, part, at, half_heads[0], len(half_heads)))
         partial = [onward(block) for block in blocks]
         token = blocks
-        if step == stores - 2:
-            token = [blocks, arrived]
         if step in (half - 1, half):
             if own_queries is None:
                 own_queries = joined(after(queries, token), mine)

time: 98.4 us -> 98 us (level)
  transfers between devices with their start and end apart: 18 -> 18, of which waited for: 13 -> 11; matrix products, arithmetic and copies ran while one was open for 0% -> 0% of each run, Pallas kernels for 30% -> 30%
where the time goes in v20:
time: 98 us; the launch traced here: 97.7 us
  starting transfers between devices  38.5 us (39%)
  Pallas kernels  31 us (32%)
  waiting for transfers between devices  20.7 us (21%)
  local copies, waits for them, and re-layouts  5.04 us (5%)
  between operations  2.32 us (2%)
    ppermute x17, starting transfers between devices, onward(): return lax.ppermute(x, ('store', 'tensor'), route)  36 us
    ppermute x17, waiting for transfers between devices, onward(): return lax.ppermute(x, ('store', 'tensor'), route)  20.7 us
    pallas_call x9, Pallas kernels, attend(): pl.pallas_call(functools.partial(attend_kernel, sizes + (count,), jobs, o...  20.3 us
    pallas_call x11, Pallas kernels, call(): pl.pallas_call(kernel, out_shape=shape, in_specs=[VMEM] * len(args), out_...  6.71 us
    unnamed x14, local copies, waits for them, and re-layouts  5.04 us
    ppermute x1, starting transfers between devices, shifted(): return lax.ppermute(block, axis, route)  2.53 us
    pallas_call x2, Pallas kernels, finish(): pl.pallas_call(functools.partial(final_kernel, suffix, first), out_shape=...  2.53 us
  transfers between devices with their start and end apart: 18, of which 11 were waited for; matrix products, arithmetic and copies ran while one was open for 0% of the time, Pallas kernels for 30%

profile of v20, /device:TPU:0, one launch (start us, length us, event | category | flops | bytes accessed | tf_op | source)
XLA Modules:
  0.0 97.7 jit_solution(4472331266619021590)
XLA Ops:
  0.6 3.1 %collective-permute-start = (bf16[1,64,4096]{2,1,0:T(8,128)(2,1)}, bf16[1,64,4096]{2,1,0:T(8,128)(2,1)S(1)}, u32[]{:S(2)}, u32[]{:S(2)}) collective-permute-start(bf16[1,64,4096]{2,1,0:T(8,128)(2,1)} %q_ref), channel_id=1, source_target_pairs={{0,4},{4,8},{8,12},{12,14},{14,10},{10,6},{6,2},{2,0},{1,3},{5,1},... | collective-permute-start | bytes 1572872 | tf_op jit(solution)/shard_map/ppermute | solution.py:447
  5.0 0.0 copy-start.6
  5.0 0.6 copy-done.6
  5.7 0.3 shard_map.77.lists_ref
  5.9 1.6 %collective-permute-start.1 = (bf16[16,128]{1,0:T(8,128)(2,1)S(1)}, bf16[16,128]{1,0:T(8,128)(2,1)S(1)}, u32[]{:S(2)}, u32[]{:S(2)}) collective-permute-start(bf16[16,128]{1,0:T(8,128)(2,1)S(1)} %shard_map.77.lists_ref), channel_id=1, source_target_pairs={{0,4},{4,8},{8,12},{12,14},{14,10},{10,6},{6,2},{2,0},{1,3},{5,1},... | collective-permute-start | bytes 12296 | tf_op jit(solution)/shard_map/ppermute | solution.py:447
  7.5 3.5 %collective-permute-done.1.lists_ref = bf16[16,128]{1,0:T(8,128)(2,1)S(1)} collective-permute-done((bf16[16,128]{1,0:T(8,128)(2,1)S(1)}, bf16[16,128]{1,0:T(8,128)(2,1)S(1)}, u32[]{:S(2)}, u32[]{:S(2)}) %collective-permute-start.1) | collective-permute-done | bytes 4128 | tf_op jit(solution)/shard_map/ppermute | solution.py:447
  11.1 0.0 collective-permute-done.q_ref
  11.1 0.1 shard_map.78.refs_1_
  11.2 2.1 %collective-permute-start.3 = (bf16[2064,128]{1,0:T(8,128)(2,1)S(1)}, bf16[2064,128]{1,0:T(8,128)(2,1)S(1)}, u32[]{:S(2)}, u32[]{:S(2)}) collective-permute-start(bf16[2064,128]{1,0:T(8,128)(2,1)S(1)} %shard_map.78.refs_1_), channel_id=1, source_target_pairs={{0,4},{4,8},{8,12},{12,14},{14,10},{10,6},{6,2},{2,0},{1,3},{5,1},... | collective-permute-start | bytes 1585160 | tf_op jit(solution)/shard_map/ppermute | solution.py:447
  13.3 2.2 %copy-done = bf16[32,2,64,512]{3,2,1,0:T(8,128)(2,1)S(1)} copy-done((bf16[32,2,64,512]{3,2,1,0:T(8,128)(2,1)S(1)}, bf16[32,2,64,512]{3,2,1,0:T(8,128)(2,1)}, u32[]{:S(2)}) %copy-start) | copy-done | bytes 4194328
  15.5 2.7 %shard_map.79 = (f32[4,512,128]{2,1,0:T(8,128)S(1)}, bf16[4,16,128]{2,1,0:T(8,128)(2,1)S(1)}, bf16[32,2,64,512]{3,2,1,0:T(8,128)(2,1)}) custom-call(s32[1,128]{1,0:T(1,128)S(1)} %fusion.refs_0_, bf16[2064,128]{1,0:T(8,128)(2,1)S(1)} %shard_map.78.refs_1_, bf16[32,2,64,512]{3,2,1,0:T(8,128)(2,1)S(1)} %copy-done), custom_call_target="tpu_custom_call" | custom-call | flops 1073741824 | bytes 2621440 | tf_op jit(solution)/shard_map/pallas_call | solution.py:254
  18.2 0.1 shard_map.80
  18.3 1.6 %collective-permute-start.2 = (bf16[4,528,128]{2,1,0:T(8,128)(2,1)S(1)}, bf16[4,528,128]{2,1,0:T(8,128)(2,1)S(1)}, u32[]{:S(2)}, u32[]{:S(2)}) collective-permute-start(bf16[4,528,128]{2,1,0:T(8,128)(2,1)S(1)} %shard_map.80), channel_id=1, source_target_pairs={{0,4},{4,8},{8,12},{12,14},{14,10},{10,6},{6,2},{2,0},{1,3},{5,1},... | collective-permute-start | bytes 1622024 | tf_op jit(solution)/shard_map/ppermute | solution.py:447
  19.9 0.5 collective-permute-done.3.refs_1_
  20.4 2.1 %collective-permute-start.5 = (bf16[2064,128]{1,0:T(8,128)(2,1)S(1)}, bf16[2064,128]{1,0:T(8,128)(2,1)S(1)}, u32[]{:S(2)}, u32[]{:S(2)}) collective-permute-start(bf16[2064,128]{1,0:T(8,128)(2,1)S(1)} %collective-permute-done.3.refs_1_), channel_id=1, source_target_pairs={{0,4},{4,8},{8,12},{12,14},{14,10},{10,6},{6,2},{2,0},{1,3},{5,1},... | collective-permute-start | bytes 1585160 | tf_op jit(solution)/shard_map/ppermute | solution.py:447
  22.5 2.9 %shard_map.81 = (f32[4,512,128]{2,1,0:T(8,128)S(1)}, bf16[4,16,128]{2,1,0:T(8,128)(2,1)S(1)}, bf16[32,2,64,512]{3,2,1,0:T(8,128)(2,1)}) custom-call(s32[1,128]{1,0:T(1,128)S(1)} %fusion.1.refs_0_.near_ref, bf16[2064,128]{1,0:T(8,128)(2,1)S(1)} %collective-permute-done.3.refs_1_, ...), custom_call_target="tpu_custom_call", output_to_operand_aliasing={{2}: (3, {})} | custom-call | flops 1073741824 | bytes 2621440 | tf_op jit(solution)/shard_map/pallas_call | solution.py:254
  25.5 2.2 %collective-permute-done.2.in_ref = bf16[4,528,128]{2,1,0:T(8,128)(2,1)S(1)} collective-permute-done((bf16[4,528,128]{2,1,0:T(8,128)(2,1)S(1)}, bf16[4,528,128]{2,1,0:T(8,128)(2,1)S(1)}, u32[]{:S(2)}, u32[]{:S(2)}) %collective-permute-start.2) | collective-permute-done | bytes 540704 | tf_op jit(solution)/shard_map/ppermute | solution.py:447
  27.7 1.0 %shard_map.82 = bf16[4,528,128]{2,1,0:T(8,128)(2,1)S(1)} custom-call(bf16[4,528,128]{2,1,0:T(8,128)(2,1)S(1)} %collective-permute-done.2.in_ref, f32[4,512,128]{2,1,0:T(8,128)S(1)} %get-tuple-element.48.acc_ref, bf16[4,16,128]{2,1,0:T(8,128)(2,1)S(1)} %get-tuple-element.49.stat_ref), custom_call_target="tpu_custom_call" | custom-call | flops 1605632 | bytes 3211264 | tf_op jit(solution)/shard_map/pallas_call | solution.py:374
  28.7 1.6 %collective-permute-start.4 = (bf16[4,528,128]{2,1,0:T(8,128)(2,1)S(1)}, bf16[4,528,128]{2,1,0:T(8,128)(2,1)S(1)}, u32[]{:S(2)}, u32[]{:S(2)}) collective-permute-start(bf16[4,528,128]{2,1,0:T(8,128)(2,1)S(1)} %shard_map.82), channel_id=1, source_target_pairs={{0,4},{4,8},{8,12},{12,14},{14,10},{10,6},{6,2},{2,0},{1,3},{5,1},... | collective-permute-start | bytes 1622024 | tf_op jit(solution)/shard_map/ppermute | solution.py:447
  30.3 3.0 %collective-permute-done.5.refs_1_ = bf16[2064,128]{1,0:T(8,128)(2,1)S(1)} collective-permute-done((bf16[2064,128]{1,0:T(8,128)(2,1)S(1)}, bf16[2064,128]{1,0:T(8,128)(2,1)S(1)}, u32[]{:S(2)}, u32[]{:S(2)}) %collective-permute-start.5) | collective-permute-done | bytes 528416 | tf_op jit(solution)/shard_map/ppermute | solution.py:447
  33.4 1.6 %collective-permute-start.7 = (bf16[2064,128]{1,0:T(8,128)(2,1)S(1)}, bf16[2064,128]{1,0:T(8,128)(2,1)S(1)}, u32[]{:S(2)}, u32[]{:S(2)}) collective-permute-start(bf16[2064,128]{1,0:T(8,128)(2,1)S(1)} %collective-permute-done.5.refs_1_), channel_id=1, source_target_pairs={{0,4},{4,8},{8,12},{12,14},{14,10},{10,6},{6,2},{2,0},{1,3},{5,1},... | collective-permute-start | bytes 1585160 | tf_op jit(solution)/shard_map/ppermute | solution.py:447
  35.0 2.2 %copy-done.2 = bf16[32,2,64,512]{3,2,1,0:T(8,128)(2,1)S(1)} copy-done((bf16[32,2,64,512]{3,2,1,0:T(8,128)(2,1)S(1)}, bf16[32,2,64,512]{3,2,1,0:T(8,128)(2,1)}, u32[]{:S(2)}) %copy-start.2) | copy-done | bytes 4194328
  37.1 2.2 %shard_map.83 = (f32[4,512,128]{2,1,0:T(8,128)S(1)}, bf16[4,16,128]{2,1,0:T(8,128)(2,1)S(1)}) custom-call(s32[1,128]{1,0:T(1,128)S(1)} %fusion.2.refs_0_, bf16[2064,128]{1,0:T(8,128)(2,1)S(1)} %collective-permute-done.5.refs_1_, bf16[32,2,64,512]{3,2,1,0:T(8,128)(2,1)S(1)} %copy-done.2), custom_call_target="tpu_custom_call" | custom-call | flops 1073741824 | bytes 2621440 | tf_op jit(solution)/shard_map/pallas_call | solution.py:254
  39.4 0.0 collective-permute-done.4.in_ref
  39.4 1.0 %shard_map.84 = bf16[4,528,128]{2,1,0:T(8,128)(2,1)S(1)} custom-call(bf16[4,528,128]{2,1,0:T(8,128)(2,1)S(1)} %collective-permute-done.4.in_ref, f32[4,512,128]{2,1,0:T(8,128)S(1)} %get-tuple-element.52.acc_ref, bf16[4,16,128]{2,1,0:T(8,128)(2,1)S(1)} %get-tuple-element.53.stat_ref), custom_call_target="tpu_custom_call" | custom-call | flops 1605632 | bytes 3211264 | tf_op jit(solution)/shard_map/pallas_call | solution.py:374
  40.4 1.6 %collective-permute-start.6 = (bf16[4,528,128]{2,1,0:T(8,128)(2,1)S(1)}, bf16[4,528,128]{2,1,0:T(8,128)(2,1)S(1)}, u32[]{:S(2)}, u32[]{:S(2)}) collective-permute-start(bf16[4,528,128]{2,1,0:T(8,128)(2,1)S(1)} %shard_map.84), channel_id=1, source_target_pairs={{0,4},{4,8},{8,12},{12,14},{14,10},{10,6},{6,2},{2,0},{1,3},{5,1},... | collective-permute-start | bytes 1622024 | tf_op jit(solution)/shard_map/ppermute | solution.py:447
  42.0 0.1 shard_map.85.refs_1_
  42.2 1.8 %shard_map.86 = (f32[2,512,128]{2,1,0:T(8,128)S(1)}, bf16[2,16,128]{2,1,0:T(8,128)(2,1)S(1)}) custom-call(s32[1,128]{1,0:T(1,128)S(1)} %fusion.3.refs_0_, bf16[2064,128]{1,0:T(8,128)(2,1)S(1)} %shard_map.85.refs_1_, bf16[2,64,512]{2,1,0:T(8,128)(2,1)S(1)} %bitcast.3, bf16[32,2,64,512]{3,2,1,0:T(8,128)(2,1)S(1)} %copy-done.3), custom_call_target="tpu_custom_call" | custom-call | flops 536870912 | bytes 1310720 | tf_op jit(solution)/shard_map/pallas_call | solution.py:254
  43.9 0.9 collective-permute-done.7.refs_1_
  44.8 1.6 %collective-permute-start.9 = (bf16[2064,128]{1,0:T(8,128)(2,1)S(1)}, bf16[2064,128]{1,0:T(8,128)(2,1)S(1)}, u32[]{:S(2)}, u32[]{:S(2)}) collective-permute-start(bf16[2064,128]{1,0:T(8,128)(2,1)S(1)} %collective-permute-done.7.refs_1_), channel_id=1, source_target_pairs={{0,4},{4,8},{8,12},{12,14},{14,10},{10,6},{6,2},{2,0},{1,3},{5,1},... | collective-permute-start | bytes 1585160 | tf_op jit(solution)/shard_map/ppermute | solution.py:447
  46.4 2.2 %shard_map.87 = (f32[4,512,128]{2,1,0:T(8,128)S(1)}, bf16[4,16,128]{2,1,0:T(8,128)(2,1)S(1)}) custom-call(s32[1,128]{1,0:T(1,128)S(1)} %fusion.4.refs_0_, bf16[2064,128]{1,0:T(8,128)(2,1)S(1)} %collective-permute-done.7.refs_1_, bf16[32,2,64,512]{3,2,1,0:T(8,128)(2,1)S(1)} %copy-done.3), custom_call_target="tpu_custom_call" | custom-call | flops 1073741824 | bytes 2621440 | tf_op jit(solution)/shard_map/pallas_call | solution.py:254
  48.6 2.0 %collective-permute-done.6.in_ref = bf16[4,528,128]{2,1,0:T(8,128)(2,1)S(1)} collective-permute-done((bf16[4,528,128]{2,1,0:T(8,128)(2,1)S(1)}, bf16[4,528,128]{2,1,0:T(8,128)(2,1)S(1)}, u32[]{:S(2)}, u32[]{:S(2)}) %collective-permute-start.6) | collective-permute-done | bytes 540704 | tf_op jit(solution)/shard_map/ppermute | solution.py:447
  50.6 1.0 %shard_map.88 = bf16[4,528,128]{2,1,0:T(8,128)(2,1)S(1)} custom-call(bf16[4,528,128]{2,1,0:T(8,128)(2,1)S(1)} %collective-permute-done.6.in_ref, f32[4,512,128]{2,1,0:T(8,128)S(1)} %get-tuple-element.60.acc_ref, bf16[4,16,128]{2,1,0:T(8,128)(2,1)S(1)} %get-tuple-element.61.stat_ref), custom_call_target="tpu_custom_call" | custom-call | flops 1605632 | bytes 3211264 | tf_op jit(solution)/shard_map/pallas_call | solution.py:374
  51.6 1.8 %collective-permute-start.8 = (bf16[4,528,128]{2,1,0:T(8,128)(2,1)S(1)}, bf16[4,528,128]{2,1,0:T(8,128)(2,1)S(1)}, u32[]{:S(2)}, u32[]{:S(2)}) collective-permute-start(bf16[4,528,128]{2,1,0:T(8,128)(2,1)S(1)} %shard_map.88), channel_id=1, source_target_pairs={{0,4},{4,8},{8,12},{12,14},{14,10},{10,6},{6,2},{2,0},{1,3},{5,1},... | collective-permute-start | bytes 1622024 | tf_op jit(solution)/shard_map/ppermute | solution.py:447
  53.4 1.8 %shard_map.89 = (f32[2,512,128]{2,1,0:T(8,128)S(1)}, bf16[2,16,128]{2,1,0:T(8,128)(2,1)S(1)}) custom-call(s32[1,128]{1,0:T(1,128)S(1)} %fusion.3.refs_0_, bf16[2064,128]{1,0:T(8,128)(2,1)S(1)} %shard_map.85.refs_1_, bf16[2,64,512]{2,1,0:T(8,128)(2,1)S(1)} %bitcast.4, bf16[32,2,64,512]{3,2,1,0:T(8,128)(2,1)S(1)} %copy-done.3), custom_call_target="tpu_custom_call" | custom-call | flops 536870912 | bytes 1310720 | tf_op jit(solution)/shard_map/pallas_call | solution.py:254
  55.2 1.1 %collective-permute-done.9.refs_1_ = bf16[2064,128]{1,0:T(8,128)(2,1)S(1)} collective-permute-done((bf16[2064,128]{1,0:T(8,128)(2,1)S(1)}, bf16[2064,128]{1,0:T(8,128)(2,1)S(1)}, u32[]{:S(2)}, u32[]{:S(2)}) %collective-permute-start.9) | collective-permute-done | bytes 528416 | tf_op jit(solution)/shard_map/ppermute | solution.py:447
  56.3 1.6 %collective-permute-start.11 = (bf16[2064,128]{1,0:T(8,128)(2,1)S(1)}, bf16[2064,128]{1,0:T(8,128)(2,1)S(1)}, u32[]{:S(2)}, u32[]{:S(2)}) collective-permute-start(bf16[2064,128]{1,0:T(8,128)(2,1)S(1)} %collective-permute-done.9.refs_1_), channel_id=1, source_target_pairs={{0,4},{4,8},{8,12},{12,14},{14,10},{10,6},{6,2},{2,0},{1,3},{5,1},... | collective-permute-start | bytes 1585160 | tf_op jit(solution)/shard_map/ppermute | solution.py:447
  57.9 2.2 %shard_map.90 = (f32[4,512,128]{2,1,0:T(8,128)S(1)}, bf16[4,16,128]{2,1,0:T(8,128)(2,1)S(1)}) custom-call(s32[1,128]{1,0:T(1,128)S(1)} %fusion.5.refs_0_, bf16[2064,128]{1,0:T(8,128)(2,1)S(1)} %collective-permute-done.9.refs_1_, bf16[32,2,64,512]{3,2,1,0:T(8,128)(2,1)S(1)} %copy-done.3), custom_call_target="tpu_custom_call" | custom-call | flops 1073741824 | bytes 2621440 | tf_op jit(solution)/shard_map/pallas_call | solution.py:254
  60.1 2.0 %collective-permute-done.8.in_ref = bf16[4,528,128]{2,1,0:T(8,128)(2,1)S(1)} collective-permute-done((bf16[4,528,128]{2,1,0:T(8,128)(2,1)S(1)}, bf16[4,528,128]{2,1,0:T(8,128)(2,1)S(1)}, u32[]{:S(2)}, u32[]{:S(2)}) %collective-permute-start.8) | collective-permute-done | bytes 540704 | tf_op jit(solution)/shard_map/ppermute | solution.py:447
  62.1 1.0 %shard_map.91 = bf16[4,528,128]{2,1,0:T(8,128)(2,1)S(1)} custom-call(bf16[4,528,128]{2,1,0:T(8,128)(2,1)S(1)} %collective-permute-done.8.in_ref, f32[4,512,128]{2,1,0:T(8,128)S(1)} %get-tuple-element.67.acc_ref, bf16[4,16,128]{2,1,0:T(8,128)(2,1)S(1)} %get-tuple-element.68.stat_ref), custom_call_target="tpu_custom_call" | custom-call | flops 1605632 | bytes 3211264 | tf_op jit(solution)/shard_map/pallas_call | solution.py:374
  63.1 1.6 %collective-permute-start.10 = (bf16[4,528,128]{2,1,0:T(8,128)(2,1)S(1)}, bf16[4,528,128]{2,1,0:T(8,128)(2,1)S(1)}, u32[]{:S(2)}, u32[]{:S(2)}) collective-permute-start(bf16[4,528,128]{2,1,0:T(8,128)(2,1)S(1)} %shard_map.91), channel_id=1, source_target_pairs={{0,4},{4,8},{8,12},{12,14},{14,10},{10,6},{6,2},{2,0},{1,3},{5,1},... | collective-permute-start | bytes 1622024 | tf_op jit(solution)/shard_map/ppermute | solution.py:447
  64.7 3.0 %collective-permute-done.11.refs_1_ = bf16[2064,128]{1,0:T(8,128)(2,1)S(1)} collective-permute-done((bf16[2064,128]{1,0:T(8,128)(2,1)S(1)}, bf16[2064,128]{1,0:T(8,128)(2,1)S(1)}, u32[]{:S(2)}, u32[]{:S(2)}) %collective-permute-start.11) | collective-permute-done | bytes 528416 | tf_op jit(solution)/shard_map/ppermute | solution.py:447
  67.7 1.6 %collective-permute-start.13 = (bf16[2064,128]{1,0:T(8,128)(2,1)S(1)}, bf16[2064,128]{1,0:T(8,128)(2,1)S(1)}, u32[]{:S(2)}, u32[]{:S(2)}) collective-permute-start(bf16[2064,128]{1,0:T(8,128)(2,1)S(1)} %collective-permute-done.11.refs_1_), channel_id=1, source_target_pairs={{0,4},{4,8},{8,12},{12,14},{14,10},{10,6},{6,2},{2,0},{1,3},{5,1},... | collective-permute-start | bytes 1585160 | tf_op jit(solution)/shard_map/ppermute | solution.py:447
  69.3 2.5 %collective-permute-start.14 = (bf16[1,2,64,512]{3,2,1,0:T(8,128)(2,1)S(1)}, bf16[1,2,64,512]{3,2,1,0:T(8,128)(2,1)S(1)}, u32[]{:S(2)}, u32[]{:S(2)}) collective-permute-start(bf16[1,2,64,512]{3,2,1,0:T(8,128)(2,1)S(1)} %copy-done.4), channel_id=1, source_target_pairs={{8,0},{10,2},{12,4},{14,6},{0,8},{2,10},{4,12},{6,14},{9,1},{11,3}... | collective-permute-start | bytes 393224 | tf_op jit(solution)/shard_map/ppermute | solution.py:27
  71.9 2.2 %shard_map.92 = (f32[4,512,128]{2,1,0:T(8,128)S(1)}, bf16[4,16,128]{2,1,0:T(8,128)(2,1)S(1)}) custom-call(s32[1,128]{1,0:T(1,128)S(1)} %fusion.6.refs_0_.far_ref, bf16[2064,128]{1,0:T(8,128)(2,1)S(1)} %collective-permute-done.11.refs_1_, bf16[32,2,64,512]{3,2,1,0:T(8,128)(2,1)S(1)} %copy-done.3), custom_call_target="tpu_custom_call" | custom-call | flops 1 | bytes 1 | tf_op jit(solution)/shard_map/pallas_call | solution.py:254
  74.1 0.0 collective-permute-done.10.in_ref
  74.1 0.6 shard_map.93
  74.7 3.0 %collective-permute-start.15 = (bf16[2,528,128]{2,1,0:T(8,128)(2,1)S(1)}, bf16[2,528,128]{2,1,0:T(8,128)(2,1)S(1)}, u32[]{:S(2)}, u32[]{:S(2)}) collective-permute-start(bf16[2,528,128]{2,1,0:T(8,128)(2,1)S(1)} %shard_map.93), channel_id=1, source_target_pairs={{0,4},{4,8},{8,12},{12,14},{14,10},{10,6},{6,2},{2,0},{1,3},{5,1},... | collective-permute-start | bytes 811016 | tf_op jit(solution)/shard_map/ppermute | solution.py:447
  77.7 0.6 shard_map.94
  78.3 2.5 %collective-permute-start.12 = (bf16[2,528,128]{2,1,0:T(8,128)(2,1)S(1)}, bf16[2,528,128]{2,1,0:T(8,128)(2,1)S(1)}, u32[]{:S(2)}, u32[]{:S(2)}) collective-permute-start(bf16[2,528,128]{2,1,0:T(8,128)(2,1)S(1)} %shard_map.94), channel_id=1, source_target_pairs={{0,4},{4,8},{8,12},{12,14},{14,10},{10,6},{6,2},{2,0},{1,3},{5,1},... | collective-permute-start | bytes 811016 | tf_op jit(solution)/shard_map/ppermute | solution.py:447
  80.9 0.0 collective-permute-done.13.refs_1_
  80.9 2.2 %shard_map.95 = (f32[4,512,128]{2,1,0:T(8,128)S(1)}, bf16[4,16,128]{2,1,0:T(8,128)(2,1)S(1)}) custom-call(s32[1,128]{1,0:T(1,128)S(1)} %fusion.7.refs_0_, bf16[2064,128]{1,0:T(8,128)(2,1)S(1)} %collective-permute-done.13.refs_1_, bf16[32,2,64,512]{3,2,1,0:T(8,128)(2,1)S(1)} %copy-done.3), custom_call_target="tpu_custom_call" | custom-call | flops 8589934592 | bytes 33554432 | tf_op jit(solution)/shard_map/pallas_call | solution.py:254
  83.1 0.0 collective-permute-done.14.page_ref
  83.1 0.9 collective-permute-done.15.in_ref
  84.0 0.6 shard_map.96
  84.7 4.4 %collective-permute-start.17 = (bf16[2,528,128]{2,1,0:T(8,128)(2,1)S(1)}, bf16[2,528,128]{2,1,0:T(8,128)(2,1)S(1)}, u32[]{:S(2)}, u32[]{:S(2)}) collective-permute-start(bf16[2,528,128]{2,1,0:T(8,128)(2,1)S(1)} %shard_map.96), channel_id=1, source_target_pairs={{0,4},{4,8},{8,12},{12,14},{14,10},{10,6},{6,2},{2,0},{1,3},{5,1},... | collective-permute-start | bytes 811016 | tf_op jit(solution)/shard_map/ppermute | solution.py:447
  89.1 0.0 collective-permute-done.12.in_ref
  89.1 0.6 shard_map.97
  89.8 2.5 %collective-permute-start.16 = (bf16[2,528,128]{2,1,0:T(8,128)(2,1)S(1)}, bf16[2,528,128]{2,1,0:T(8,128)(2,1)S(1)}, u32[]{:S(2)}, u32[]{:S(2)}) collective-permute-start(bf16[2,528,128]{2,1,0:T(8,128)(2,1)S(1)} %shard_map.97), channel_id=1, source_target_pairs={{0,4},{4,8},{8,12},{12,14},{14,10},{10,6},{6,2},{2,0},{1,3},{5,1},... | collective-permute-start | bytes 811016 | tf_op jit(solution)/shard_map/ppermute | solution.py:447
  92.3 1.2 %shard_map.98 = bf16[32,2,64,512]{3,2,1,0:T(8,128)(2,1)} custom-call(s32[1]{0:T(128)} %bitcast.1.me_ref, s32[1]{0:T(128)} %bitcast.2.core_ref, s32[1,128]{1,0:T(1,128)S(1)} %fusion.1.refs_0_.near_ref, s32[1,128]{1,0:T(1,128)S(1)} %fusion.6.refs_0_.far_ref, ...), custom_call_target="tpu_custom_call", output_to_operand_aliasing={{}: (5, {})} | custom-call | flops 1 | bytes 1 | tf_op jit(solution)/shard_map/pallas_call | solution.py:277
  93.5 0.0 collective-permute-done.17.in_ref
  93.5 1.3 %shard_map.99.refs_0_ = bf16[1,64,4096]{2,1,0:T(8,128)(2,1)} custom-call(bf16[2,528,128]{2,1,0:T(8,128)(2,1)S(1)} %collective-permute-done.17.in_ref, f32[2,512,128]{2,1,0:T(8,128)S(1)} %get-tuple-element.57.acc_ref, bf16[2,16,128]{2,1,0:T(8,128)(2,1)S(1)} %get-tuple-element.58.stat_ref), custom_call_target="tpu_custom_call" | custom-call | tf_op jit(solution)/shard_map/pallas_call | solution.py:358
  94.8 1.5 %collective-permute-done.16.in_ref = bf16[2,528,128]{2,1,0:T(8,128)(2,1)S(1)} collective-permute-done((bf16[2,528,128]{2,1,0:T(8,128)(2,1)S(1)}, bf16[2,528,128]{2,1,0:T(8,128)(2,1)S(1)}, u32[]{:S(2)}, u32[]{:S(2)}) %collective-permute-start.16) | collective-permute-done | bytes 270368 | tf_op jit(solution)/shard_map/ppermute | solution.py:447
  96.3 1.3 %shard_map.100 = bf16[1,64,4096]{2,1,0:T(8,128)(2,1)} custom-call(bf16[2,528,128]{2,1,0:T(8,128)(2,1)S(1)} %collective-permute-done.16.in_ref, f32[2,512,128]{2,1,0:T(8,128)S(1)} %get-tuple-element.64.acc_ref, bf16[2,16,128]{2,1,0:T(8,128)(2,1)S(1)} %get-tuple-element.65.stat_ref, bf16[1,64,4096]{2,1,0:T(8,128)(2,1)} %shard_map.99.refs_0_), custom_call_target="tpu_custom_call", output_to_operand_aliasing={{}: (3, {})} | custom-call | tf_op jit(solution)/shard_map/pallas_call | solution.py:358
  (18 shorter events, 0.1 us)
Async XLA Ops:
  0.6 10.4 %collective-permute-start = (bf16[1,64,4096]{2,1,0:T(8,128)(2,1)}, bf16[1,64,4096]{2,1,0:T(8,128)(2,1)S(1)}, u32[]{:S(2)}, u32[]{:S(2)}) collective-permute-start(bf16[1,64,4096]{2,1,0:T(8,128)(2,1)} %q_ref), channel_id=1, source_target_pairs={{0,4},{4,8},{8,12},{12,14},{14,10},{10,6},{6,2},{2,0},{1,3},{5,1},... | collective-permute-start | bytes 1572872 | tf_op jit(solution)/shard_map/ppermute | solution.py:447
  5.0 0.7 copy-start.6
  5.9 5.1 %collective-permute-start.1 = (bf16[16,128]{1,0:T(8,128)(2,1)S(1)}, bf16[16,128]{1,0:T(8,128)(2,1)S(1)}, u32[]{:S(2)}, u32[]{:S(2)}) collective-permute-start(bf16[16,128]{1,0:T(8,128)(2,1)S(1)} %shard_map.77.lists_ref), channel_id=1, source_target_pairs={{0,4},{4,8},{8,12},{12,14},{14,10},{10,6},{6,2},{2,0},{1,3},{5,1},... | collective-permute-start | bytes 12296 | tf_op jit(solution)/shard_map/ppermute | solution.py:447
  11.2 9.3 %collective-permute-start.3 = (bf16[2064,128]{1,0:T(8,128)(2,1)S(1)}, bf16[2064,128]{1,0:T(8,128)(2,1)S(1)}, u32[]{:S(2)}, u32[]{:S(2)}) collective-permute-start(bf16[2064,128]{1,0:T(8,128)(2,1)S(1)} %shard_map.78.refs_1_), channel_id=1, source_target_pairs={{0,4},{4,8},{8,12},{12,14},{14,10},{10,6},{6,2},{2,0},{1,3},{5,1},... | collective-permute-start | bytes 1585160 | tf_op jit(solution)/shard_map/ppermute | solution.py:447
  13.3 2.2 %copy-start = (bf16[32,2,64,512]{3,2,1,0:T(8,128)(2,1)S(1)}, bf16[32,2,64,512]{3,2,1,0:T(8,128)(2,1)}, u32[]{:S(2)}) copy-start(bf16[32,2,64,512]{3,2,1,0:T(8,128)(2,1)} %refs_2_.13) | copy-start | bytes 12582916
  15.5 7.0 %copy-start.1 = (bf16[32,2,64,512]{3,2,1,0:T(8,128)(2,1)S(1)}, bf16[32,2,64,512]{3,2,1,0:T(8,128)(2,1)}, u32[]{:S(2)}) copy-start(bf16[32,2,64,512]{3,2,1,0:T(8,128)(2,1)} %refs_2_.13) | copy-start | bytes 12582916
  18.3 9.4 %collective-permute-start.2 = (bf16[4,528,128]{2,1,0:T(8,128)(2,1)S(1)}, bf16[4,528,128]{2,1,0:T(8,128)(2,1)S(1)}, u32[]{:S(2)}, u32[]{:S(2)}) collective-permute-start(bf16[4,528,128]{2,1,0:T(8,128)(2,1)S(1)} %shard_map.80), channel_id=1, source_target_pairs={{0,4},{4,8},{8,12},{12,14},{14,10},{10,6},{6,2},{2,0},{1,3},{5,1},... | collective-permute-start | bytes 1622024 | tf_op jit(solution)/shard_map/ppermute | solution.py:447
  20.4 12.9 %collective-permute-start.5 = (bf16[2064,128]{1,0:T(8,128)(2,1)S(1)}, bf16[2064,128]{1,0:T(8,128)(2,1)S(1)}, u32[]{:S(2)}, u32[]{:S(2)}) collective-permute-start(bf16[2064,128]{1,0:T(8,128)(2,1)S(1)} %collective-permute-done.3.refs_1_), channel_id=1, source_target_pairs={{0,4},{4,8},{8,12},{12,14},{14,10},{10,6},{6,2},{2,0},{1,3},{5,1},... | collective-permute-start | bytes 1585160 | tf_op jit(solution)/shard_map/ppermute | solution.py:447
  27.7 14.3 %copy-start.5 = (bf16[1,64,4096]{2,1,0:T(8,128)(2,1)S(1)}, bf16[1,64,4096]{2,1,0:T(8,128)(2,1)}, u32[]{:S(2)}) copy-start(bf16[1,64,4096]{2,1,0:T(8,128)(2,1)} %q_ref) | copy-start | bytes 1572868
  27.7 14.4 %copy-start.4 = (bf16[1,2,64,512]{3,2,1,0:T(8,128)(2,1)S(1)}, bf16[1,2,64,512]{3,2,1,0:T(8,128)(2,1)}, u32[]{:S(2)}) copy-start(bf16[1,2,64,512]{3,2,1,0:T(8,128)(2,1)} %param.7) | copy-start | bytes 393220
  28.7 10.7 %collective-permute-start.4 = (bf16[4,528,128]{2,1,0:T(8,128)(2,1)S(1)}, bf16[4,528,128]{2,1,0:T(8,128)(2,1)S(1)}, u32[]{:S(2)}, u32[]{:S(2)}) collective-permute-start(bf16[4,528,128]{2,1,0:T(8,128)(2,1)S(1)} %shard_map.82), channel_id=1, source_target_pairs={{0,4},{4,8},{8,12},{12,14},{14,10},{10,6},{6,2},{2,0},{1,3},{5,1},... | collective-permute-start | bytes 1622024 | tf_op jit(solution)/shard_map/ppermute | solution.py:447
  33.4 11.5 %collective-permute-start.7 = (bf16[2064,128]{1,0:T(8,128)(2,1)S(1)}, bf16[2064,128]{1,0:T(8,128)(2,1)S(1)}, u32[]{:S(2)}, u32[]{:S(2)}) collective-permute-start(bf16[2064,128]{1,0:T(8,128)(2,1)S(1)} %collective-permute-done.5.refs_1_), channel_id=1, source_target_pairs={{0,4},{4,8},{8,12},{12,14},{14,10},{10,6},{6,2},{2,0},{1,3},{5,1},... | collective-permute-start | bytes 1585160 | tf_op jit(solution)/shard_map/ppermute | solution.py:447
  35.0 2.2 %copy-start.2 = (bf16[32,2,64,512]{3,2,1,0:T(8,128)(2,1)S(1)}, bf16[32,2,64,512]{3,2,1,0:T(8,128)(2,1)}, u32[]{:S(2)}) copy-start(bf16[32,2,64,512]{3,2,1,0:T(8,128)(2,1)} %refs_2_.13) | copy-start | bytes 12582916
  37.1 5.0 %copy-start.3 = (bf16[32,2,64,512]{3,2,1,0:T(8,128)(2,1)S(1)}, bf16[32,2,64,512]{3,2,1,0:T(8,128)(2,1)}, u32[]{:S(2)}) copy-start(bf16[32,2,64,512]{3,2,1,0:T(8,128)(2,1)} %refs_2_.13) | copy-start | bytes 12582916
  40.4 10.2 %collective-permute-start.6 = (bf16[4,528,128]{2,1,0:T(8,128)(2,1)S(1)}, bf16[4,528,128]{2,1,0:T(8,128)(2,1)S(1)}, u32[]{:S(2)}, u32[]{:S(2)}) collective-permute-start(bf16[4,528,128]{2,1,0:T(8,128)(2,1)S(1)} %shard_map.84), channel_id=1, source_target_pairs={{0,4},{4,8},{8,12},{12,14},{14,10},{10,6},{6,2},{2,0},{1,3},{5,1},... | collective-permute-start | bytes 1622024 | tf_op jit(solution)/shard_map/ppermute | solution.py:447
  44.8 11.5 %collective-permute-start.9 = (bf16[2064,128]{1,0:T(8,128)(2,1)S(1)}, bf16[2064,128]{1,0:T(8,128)(2,1)S(1)}, u32[]{:S(2)}, u32[]{:S(2)}) collective-permute-start(bf16[2064,128]{1,0:T(8,128)(2,1)S(1)} %collective-permute-done.7.refs_1_), channel_id=1, source_target_pairs={{0,4},{4,8},{8,12},{12,14},{14,10},{10,6},{6,2},{2,0},{1,3},{5,1},... | collective-permute-start | bytes 1585160 | tf_op jit(solution)/shard_map/ppermute | solution.py:447
  51.6 10.5 %collective-permute-start.8 = (bf16[4,528,128]{2,1,0:T(8,128)(2,1)S(1)}, bf16[4,528,128]{2,1,0:T(8,128)(2,1)S(1)}, u32[]{:S(2)}, u32[]{:S(2)}) collective-permute-start(bf16[4,528,128]{2,1,0:T(8,128)(2,1)S(1)} %shard_map.88), channel_id=1, source_target_pairs={{0,4},{4,8},{8,12},{12,14},{14,10},{10,6},{6,2},{2,0},{1,3},{5,1},... | collective-permute-start | bytes 1622024 | tf_op jit(solution)/shard_map/ppermute | solution.py:447
  56.3 11.5 %collective-permute-start.11 = (bf16[2064,128]{1,0:T(8,128)(2,1)S(1)}, bf16[2064,128]{1,0:T(8,128)(2,1)S(1)}, u32[]{:S(2)}, u32[]{:S(2)}) collective-permute-start(bf16[2064,128]{1,0:T(8,128)(2,1)S(1)} %collective-permute-done.9.refs_1_), channel_id=1, source_target_pairs={{0,4},{4,8},{8,12},{12,14},{14,10},{10,6},{6,2},{2,0},{1,3},{5,1},... | collective-permute-start | bytes 1585160 | tf_op jit(solution)/shard_map/ppermute | solution.py:447
  63.1 11.0 %collective-permute-start.10 = (bf16[4,528,128]{2,1,0:T(8,128)(2,1)S(1)}, bf16[4,528,128]{2,1,0:T(8,128)(2,1)S(1)}, u32[]{:S(2)}, u32[]{:S(2)}) collective-permute-start(bf16[4,528,128]{2,1,0:T(8,128)(2,1)S(1)} %shard_map.91), channel_id=1, source_target_pairs={{0,4},{4,8},{8,12},{12,14},{14,10},{10,6},{6,2},{2,0},{1,3},{5,1},... | collective-permute-start | bytes 1622024 | tf_op jit(solution)/shard_map/ppermute | solution.py:447
  67.7 13.1 %collective-permute-start.13 = (bf16[2064,128]{1,0:T(8,128)(2,1)S(1)}, bf16[2064,128]{1,0:T(8,128)(2,1)S(1)}, u32[]{:S(2)}, u32[]{:S(2)}) collective-permute-start(bf16[2064,128]{1,0:T(8,128)(2,1)S(1)} %collective-permute-done.11.refs_1_), channel_id=1, source_target_pairs={{0,4},{4,8},{8,12},{12,14},{14,10},{10,6},{6,2},{2,0},{1,3},{5,1},... | collective-permute-start | bytes 1585160 | tf_op jit(solution)/shard_map/ppermute | solution.py:447
  69.3 13.8 %collective-permute-start.14 = (bf16[1,2,64,512]{3,2,1,0:T(8,128)(2,1)S(1)}, bf16[1,2,64,512]{3,2,1,0:T(8,128)(2,1)S(1)}, u32[]{:S(2)}, u32[]{:S(2)}) collective-permute-start(bf16[1,2,64,512]{3,2,1,0:T(8,128)(2,1)S(1)} %copy-done.4), channel_id=1, source_target_pairs={{8,0},{10,2},{12,4},{14,6},{0,8},{2,10},{4,12},{6,14},{9,1},{11,3}... | collective-permute-start | bytes 393224 | tf_op jit(solution)/shard_map/ppermute | solution.py:27
  74.7 9.3 %collective-permute-start.15 = (bf16[2,528,128]{2,1,0:T(8,128)(2,1)S(1)}, bf16[2,528,128]{2,1,0:T(8,128)(2,1)S(1)}, u32[]{:S(2)}, u32[]{:S(2)}) collective-permute-start(bf16[2,528,128]{2,1,0:T(8,128)(2,1)S(1)} %shard_map.93), channel_id=1, source_target_pairs={{0,4},{4,8},{8,12},{12,14},{14,10},{10,6},{6,2},{2,0},{1,3},{5,1},... | collective-permute-start | bytes 811016 | tf_op jit(solution)/shard_map/ppermute | solution.py:447
  78.3 10.8 %collective-permute-start.12 = (bf16[2,528,128]{2,1,0:T(8,128)(2,1)S(1)}, bf16[2,528,128]{2,1,0:T(8,128)(2,1)S(1)}, u32[]{:S(2)}, u32[]{:S(2)}) collective-permute-start(bf16[2,528,128]{2,1,0:T(8,128)(2,1)S(1)} %shard_map.94), channel_id=1, source_target_pairs={{0,4},{4,8},{8,12},{12,14},{14,10},{10,6},{6,2},{2,0},{1,3},{5,1},... | collective-permute-start | bytes 811016 | tf_op jit(solution)/shard_map/ppermute | solution.py:447
  84.7 8.8 %collective-permute-start.17 = (bf16[2,528,128]{2,1,0:T(8,128)(2,1)S(1)}, bf16[2,528,128]{2,1,0:T(8,128)(2,1)S(1)}, u32[]{:S(2)}, u32[]{:S(2)}) collective-permute-start(bf16[2,528,128]{2,1,0:T(8,128)(2,1)S(1)} %shard_map.96), channel_id=1, source_target_pairs={{0,4},{4,8},{8,12},{12,14},{14,10},{10,6},{6,2},{2,0},{1,3},{5,1},... | collective-permute-start | bytes 811016 | tf_op jit(solution)/shard_map/ppermute | solution.py:447
  89.8 6.5 %collective-permute-start.16 = (bf16[2,528,128]{2,1,0:T(8,128)(2,1)S(1)}, bf16[2,528,128]{2,1,0:T(8,128)(2,1)S(1)}, u32[]{:S(2)}, u32[]{:S(2)}) collective-permute-start(bf16[2,528,128]{2,1,0:T(8,128)(2,1)S(1)} %shard_map.97), channel_id=1, source_target_pairs={{0,4},{4,8},{8,12},{12,14},{14,10},{10,6},{6,2},{2,0},{1,3},{5,1},... | collective-permute-start | bytes 811016 | tf_op jit(solution)/shard_map/ppermute | solution.py:447

commit v21 on v20

--- a/solution.py
+++ b/solution.py
@@ -262,6 +262,21 @@
         cost_estimate=cost or work,
     )(*args)
     return [(out[2 * n], out[2 * n + 1]) for n in range(count)] + list(out[2 * count:])
+
+
+def touch_kernel(held_ref, lists_ref, out_ref):
+    out_ref[...] = lists_ref[...]
+
+
+def touch(held, lists):
+    return pl.pallas_call(
+        touch_kernel,
+        out_shape=jax.ShapeDtypeStruct(lists.shape, lists.dtype),
+        in_specs=[VMEM, VMEM],
+        out_specs=VMEM,
+        compiler_params=pltpu.CompilerParams(vmem_limit_bytes=GRANT),
+        cost_estimate=LIGHT,
+    )(held, lists)
 
 
 def place_kernel(half, column, me_ref, core_ref, near_ref, far_ref, page_ref, old_ref, out_ref, sem):
@@ -459,7 +474,9 @@
 
     first = onward(queries)
     mine = list_pages(cap, pages_dev, page_table, prefix_pages, new_slots)
-    moving = joined(first, onward(mine))
+    their_lists = onward(mine)
+    mine = touch(kv_pages, mine)
+    moving = joined(after(first, mine), their_lists)
 
     own_queries = None
     halves = [range(0, heads // 2), range(heads // 2, heads)]
@@ -474,10 +491,10 @@
             arrived = shifted(after(suffix_key_value, token), "store", half)
         jobs = [(0, h, h) for h in range(heads)]
         keeping, pages = None, pages_dev // 2
-        if step == 1:
+        if step == 2:
             keeping = (0, pages)
             part, store = attend(sizes, jobs, lists[step], [came], kv_pages, None, keeping)
-        elif step == 2:
+        elif step == 3:
             keeping = (pages, pages_dev - pages)
             part, store = attend(sizes, jobs, lists[step], [came], kv_pages, None, keeping, store)
         else:

time: 98 us -> 97.5 us (level)
  waiting for transfers between devices: 20.7 us -> 18 us
  local copies, waits for them, and re-layouts: 5.04 us -> 7.23 us
    ppermute x17, waiting for transfers between devices: 20.7 us -> 18 us  [onward(): return lax.ppermute(x, ('store', 'tensor'), route)]
    unnamed x14 -> x16, local copies, waits for them, and re-layouts: 5.04 us -> 7.23 us
  transfers between devices with their start and end apart: 18 -> 18, of which waited for: 11 -> 11; matrix products, arithmetic and copies ran while one was open for 0% -> 0% of each run, Pallas kernels for 30% -> 31%
where the time goes in v21:
time: 97.5 us; the launch traced here: 97.2 us
  starting transfers between devices  38.5 us (39%)
  Pallas kernels  31 us (32%)
  waiting for transfers between devices  18 us (18%)
  local copies, waits for them, and re-layouts  7.23 us (7%)
  between operations  2.32 us (2%)
    ppermute x17, starting transfers between devices, onward(): return lax.ppermute(x, ('store', 'tensor'), route)  36 us
    pallas_call x9, Pallas kernels, attend(): pl.pallas_call(functools.partial(attend_kernel, sizes + (count,), jobs, o...  20.3 us
    ppermute x17, waiting for transfers between devices, onward(): return lax.ppermute(x, ('store', 'tensor'), route)  18 us
    unnamed x16, local copies, waits for them, and re-layouts  7.23 us
    pallas_call x11, Pallas kernels, call(): pl.pallas_call(kernel, out_shape=shape, in_specs=[VMEM] * len(args), out_...  6.7 us
    ppermute x1, starting transfers between devices, shifted(): return lax.ppermute(block, axis, route)  2.53 us
    pallas_call x2, Pallas kernels, finish(): pl.pallas_call(functools.partial(final_kernel, suffix, first), out_shape=...  2.53 us
  transfers between devices with their start and end apart: 18, of which 11 were waited for; matrix products, arithmetic and copies ran while one was open for 0% of the time, Pallas kernels for 31%

profile of v21, /device:TPU:0, one launch (start us, length us, event | category | flops | bytes accessed | tf_op | source)
XLA Modules:
  0.0 97.2 jit_solution(7416997928734718550)
XLA Ops:
  0.6 3.1 %collective-permute-start = (bf16[1,64,4096]{2,1,0:T(8,128)(2,1)}, bf16[1,64,4096]{2,1,0:T(8,128)(2,1)S(1)}, u32[]{:S(2)}, u32[]{:S(2)}) collective-permute-start(bf16[1,64,4096]{2,1,0:T(8,128)(2,1)} %q_ref), channel_id=1, source_target_pairs={{0,4},{4,8},{8,12},{12,14},{14,10},{10,6},{6,2},{2,0},{1,3},{5,1},... | collective-permute-start | bytes 1572872 | tf_op jit(solution)/shard_map/ppermute | solution.py:462
  5.0 0.6 copy-done.7
  5.7 0.3 shard_map.77.lists_ref
  5.9 1.6 %collective-permute-start.1 = (bf16[16,128]{1,0:T(8,128)(2,1)S(1)}, bf16[16,128]{1,0:T(8,128)(2,1)S(1)}, u32[]{:S(2)}, u32[]{:S(2)}) collective-permute-start(bf16[16,128]{1,0:T(8,128)(2,1)S(1)} %shard_map.77.lists_ref), channel_id=1, source_target_pairs={{0,4},{4,8},{8,12},{12,14},{14,10},{10,6},{6,2},{2,0},{1,3},{5,1},... | collective-permute-start | bytes 12296 | tf_op jit(solution)/shard_map/ppermute | solution.py:462
  7.5 2.2 %copy-done = bf16[32,2,64,512]{3,2,1,0:T(8,128)(2,1)S(1)} copy-done((bf16[32,2,64,512]{3,2,1,0:T(8,128)(2,1)S(1)}, bf16[32,2,64,512]{3,2,1,0:T(8,128)(2,1)}, u32[]{:S(2)}) %copy-start) | copy-done | bytes 4194328
  9.7 1.3 %collective-permute-done.q_ref = bf16[1,64,4096]{2,1,0:T(8,128)(2,1)S(1)} collective-permute-done((bf16[1,64,4096]{2,1,0:T(8,128)(2,1)}, bf16[1,64,4096]{2,1,0:T(8,128)(2,1)S(1)}, u32[]{:S(2)}, u32[]{:S(2)}) %collective-permute-start) | collective-permute-done | bytes 524320 | tf_op jit(solution)/shard_map/ppermute | solution.py:462
  11.0 0.0 collective-permute-done.1.lists_ref
  11.1 0.1 shard_map.79.refs_1_
  11.2 2.1 %collective-permute-start.3 = (bf16[2064,128]{1,0:T(8,128)(2,1)S(1)}, bf16[2064,128]{1,0:T(8,128)(2,1)S(1)}, u32[]{:S(2)}, u32[]{:S(2)}) collective-permute-start(bf16[2064,128]{1,0:T(8,128)(2,1)S(1)} %shard_map.79.refs_1_), channel_id=1, source_target_pairs={{0,4},{4,8},{8,12},{12,14},{14,10},{10,6},{6,2},{2,0},{1,3},{5,1},... | collective-permute-start | bytes 1585160 | tf_op jit(solution)/shard_map/ppermute | solution.py:462
  13.3 2.2 %copy-done.1 = bf16[32,2,64,512]{3,2,1,0:T(8,128)(2,1)S(1)} copy-done((bf16[32,2,64,512]{3,2,1,0:T(8,128)(2,1)S(1)}, bf16[32,2,64,512]{3,2,1,0:T(8,128)(2,1)}, u32[]{:S(2)}) %copy-start.1) | copy-done | bytes 4194328
  15.5 2.2 %shard_map.80 = (f32[4,512,128]{2,1,0:T(8,128)S(1)}, bf16[4,16,128]{2,1,0:T(8,128)(2,1)S(1)}) custom-call(s32[1,128]{1,0:T(1,128)S(1)} %fusion.refs_0_, bf16[2064,128]{1,0:T(8,128)(2,1)S(1)} %shard_map.79.refs_1_, bf16[32,2,64,512]{3,2,1,0:T(8,128)(2,1)S(1)} %copy-done.1), custom_call_target="tpu_custom_call" | custom-call | flops 1073741824 | bytes 2621440 | tf_op jit(solution)/shard_map/pallas_call | solution.py:254
  17.7 0.1 shard_map.81
  17.8 1.6 %collective-permute-start.2 = (bf16[4,528,128]{2,1,0:T(8,128)(2,1)S(1)}, bf16[4,528,128]{2,1,0:T(8,128)(2,1)S(1)}, u32[]{:S(2)}, u32[]{:S(2)}) collective-permute-start(bf16[4,528,128]{2,1,0:T(8,128)(2,1)S(1)} %shard_map.81), channel_id=1, source_target_pairs={{0,4},{4,8},{8,12},{12,14},{14,10},{10,6},{6,2},{2,0},{1,3},{5,1},... | collective-permute-start | bytes 1622024 | tf_op jit(solution)/shard_map/ppermute | solution.py:462
  19.4 1.0 %collective-permute-done.3.refs_1_ = bf16[2064,128]{1,0:T(8,128)(2,1)S(1)} collective-permute-done((bf16[2064,128]{1,0:T(8,128)(2,1)S(1)}, bf16[2064,128]{1,0:T(8,128)(2,1)S(1)}, u32[]{:S(2)}, u32[]{:S(2)}) %collective-permute-start.3) | collective-permute-done | bytes 528416 | tf_op jit(solution)/shard_map/ppermute | solution.py:462
  20.4 2.1 %collective-permute-start.5 = (bf16[2064,128]{1,0:T(8,128)(2,1)S(1)}, bf16[2064,128]{1,0:T(8,128)(2,1)S(1)}, u32[]{:S(2)}, u32[]{:S(2)}) collective-permute-start(bf16[2064,128]{1,0:T(8,128)(2,1)S(1)} %collective-permute-done.3.refs_1_), channel_id=1, source_target_pairs={{0,4},{4,8},{8,12},{12,14},{14,10},{10,6},{6,2},{2,0},{1,3},{5,1},... | collective-permute-start | bytes 1585160 | tf_op jit(solution)/shard_map/ppermute | solution.py:462
  22.5 2.7 %shard_map.82 = (f32[4,512,128]{2,1,0:T(8,128)S(1)}, bf16[4,16,128]{2,1,0:T(8,128)(2,1)S(1)}, bf16[32,2,64,512]{3,2,1,0:T(8,128)(2,1)}) custom-call(s32[1,128]{1,0:T(1,128)S(1)} %fusion.1.refs_0_.near_ref, bf16[2064,128]{1,0:T(8,128)(2,1)S(1)} %collective-permute-done.3.refs_1_, bf16[32,2,64,512]{3,2,1,0:T(8,128)(2,1)S(1)} %copy-done.2), custom_call_target="tpu_custom_call" | custom-call | flops 1073741824 | bytes 2621440 | tf_op jit(solution)/shard_map/pallas_call | solution.py:254
  25.3 1.9 %collective-permute-done.2.in_ref = bf16[4,528,128]{2,1,0:T(8,128)(2,1)S(1)} collective-permute-done((bf16[4,528,128]{2,1,0:T(8,128)(2,1)S(1)}, bf16[4,528,128]{2,1,0:T(8,128)(2,1)S(1)}, u32[]{:S(2)}, u32[]{:S(2)}) %collective-permute-start.2) | collective-permute-done | bytes 540704 | tf_op jit(solution)/shard_map/ppermute | solution.py:462
  27.2 1.0 %shard_map.83 = bf16[4,528,128]{2,1,0:T(8,128)(2,1)S(1)} custom-call(bf16[4,528,128]{2,1,0:T(8,128)(2,1)S(1)} %collective-permute-done.2.in_ref, f32[4,512,128]{2,1,0:T(8,128)S(1)} %get-tuple-element.49.acc_ref, bf16[4,16,128]{2,1,0:T(8,128)(2,1)S(1)} %get-tuple-element.50.stat_ref), custom_call_target="tpu_custom_call" | custom-call | flops 1605632 | bytes 3211264 | tf_op jit(solution)/shard_map/pallas_call | solution.py:389
  28.2 1.6 %collective-permute-start.4 = (bf16[4,528,128]{2,1,0:T(8,128)(2,1)S(1)}, bf16[4,528,128]{2,1,0:T(8,128)(2,1)S(1)}, u32[]{:S(2)}, u32[]{:S(2)}) collective-permute-start(bf16[4,528,128]{2,1,0:T(8,128)(2,1)S(1)} %shard_map.83), channel_id=1, source_target_pairs={{0,4},{4,8},{8,12},{12,14},{14,10},{10,6},{6,2},{2,0},{1,3},{5,1},... | collective-permute-start | bytes 1622024 | tf_op jit(solution)/shard_map/ppermute | solution.py:462
  29.8 3.0 %collective-permute-done.5.refs_1_ = bf16[2064,128]{1,0:T(8,128)(2,1)S(1)} collective-permute-done((bf16[2064,128]{1,0:T(8,128)(2,1)S(1)}, bf16[2064,128]{1,0:T(8,128)(2,1)S(1)}, u32[]{:S(2)}, u32[]{:S(2)}) %collective-permute-start.5) | collective-permute-done | bytes 528416 | tf_op jit(solution)/shard_map/ppermute | solution.py:462
  32.8 1.6 %collective-permute-start.7 = (bf16[2064,128]{1,0:T(8,128)(2,1)S(1)}, bf16[2064,128]{1,0:T(8,128)(2,1)S(1)}, u32[]{:S(2)}, u32[]{:S(2)}) collective-permute-start(bf16[2064,128]{1,0:T(8,128)(2,1)S(1)} %collective-permute-done.5.refs_1_), channel_id=1, source_target_pairs={{0,4},{4,8},{8,12},{12,14},{14,10},{10,6},{6,2},{2,0},{1,3},{5,1},... | collective-permute-start | bytes 1585160 | tf_op jit(solution)/shard_map/ppermute | solution.py:462
  34.4 2.2 %copy-done.3 = bf16[32,2,64,512]{3,2,1,0:T(8,128)(2,1)S(1)} copy-done((bf16[32,2,64,512]{3,2,1,0:T(8,128)(2,1)S(1)}, bf16[32,2,64,512]{3,2,1,0:T(8,128)(2,1)}, u32[]{:S(2)}) %copy-start.3) | copy-done | bytes 4194328
  36.6 2.9 %shard_map.84 = (f32[4,512,128]{2,1,0:T(8,128)S(1)}, bf16[4,16,128]{2,1,0:T(8,128)(2,1)S(1)}, bf16[32,2,64,512]{3,2,1,0:T(8,128)(2,1)}) custom-call(s32[1,128]{1,0:T(1,128)S(1)} %fusion.2.refs_0_, bf16[2064,128]{1,0:T(8,128)(2,1)S(1)} %collective-permute-done.5.refs_1_, bf16[32,2,64,512]{3,2,1,0:T(8,128)(2,1)S(1)} %copy-done.3, ...), custom_call_target="tpu_custom_call", output_to_operand_aliasing={{2}: (3, {})} | custom-call | flops 1073741824 | bytes 2621440 | tf_op jit(solution)/shard_map/pallas_call | solution.py:254
  39.6 0.0 collective-permute-done.4.in_ref
  39.6 1.0 %shard_map.85 = bf16[4,528,128]{2,1,0:T(8,128)(2,1)S(1)} custom-call(bf16[4,528,128]{2,1,0:T(8,128)(2,1)S(1)} %collective-permute-done.4.in_ref, f32[4,512,128]{2,1,0:T(8,128)S(1)} %get-tuple-element.54.acc_ref, bf16[4,16,128]{2,1,0:T(8,128)(2,1)S(1)} %get-tuple-element.55.stat_ref), custom_call_target="tpu_custom_call" | custom-call | flops 1605632 | bytes 3211264 | tf_op jit(solution)/shard_map/pallas_call | solution.py:389
  40.6 1.6 %collective-permute-start.6 = (bf16[4,528,128]{2,1,0:T(8,128)(2,1)S(1)}, bf16[4,528,128]{2,1,0:T(8,128)(2,1)S(1)}, u32[]{:S(2)}, u32[]{:S(2)}) collective-permute-start(bf16[4,528,128]{2,1,0:T(8,128)(2,1)S(1)} %shard_map.85), channel_id=1, source_target_pairs={{0,4},{4,8},{8,12},{12,14},{14,10},{10,6},{6,2},{2,0},{1,3},{5,1},... | collective-permute-start | bytes 1622024 | tf_op jit(solution)/shard_map/ppermute | solution.py:462
  42.2 0.1 shard_map.86.refs_1_
  42.3 1.8 %shard_map.87 = (f32[2,512,128]{2,1,0:T(8,128)S(1)}, bf16[2,16,128]{2,1,0:T(8,128)(2,1)S(1)}) custom-call(s32[1,128]{1,0:T(1,128)S(1)} %fusion.3.refs_0_, bf16[2064,128]{1,0:T(8,128)(2,1)S(1)} %shard_map.86.refs_1_, bf16[2,64,512]{2,1,0:T(8,128)(2,1)S(1)} %bitcast.3, bf16[32,2,64,512]{3,2,1,0:T(8,128)(2,1)S(1)} %copy-done.4), custom_call_target="tpu_custom_call" | custom-call | flops 536870912 | bytes 1310720 | tf_op jit(solution)/shard_map/pallas_call | solution.py:254
  44.1 0.2 collective-permute-done.7.refs_1_
  44.3 1.6 %collective-permute-start.9 = (bf16[2064,128]{1,0:T(8,128)(2,1)S(1)}, bf16[2064,128]{1,0:T(8,128)(2,1)S(1)}, u32[]{:S(2)}, u32[]{:S(2)}) collective-permute-start(bf16[2064,128]{1,0:T(8,128)(2,1)S(1)} %collective-permute-done.7.refs_1_), channel_id=1, source_target_pairs={{0,4},{4,8},{8,12},{12,14},{14,10},{10,6},{6,2},{2,0},{1,3},{5,1},... | collective-permute-start | bytes 1585160 | tf_op jit(solution)/shard_map/ppermute | solution.py:462
  45.9 2.2 %shard_map.88 = (f32[4,512,128]{2,1,0:T(8,128)S(1)}, bf16[4,16,128]{2,1,0:T(8,128)(2,1)S(1)}) custom-call(s32[1,128]{1,0:T(1,128)S(1)} %fusion.4.refs_0_, bf16[2064,128]{1,0:T(8,128)(2,1)S(1)} %collective-permute-done.7.refs_1_, bf16[32,2,64,512]{3,2,1,0:T(8,128)(2,1)S(1)} %copy-done.4), custom_call_target="tpu_custom_call" | custom-call | flops 1073741824 | bytes 2621440 | tf_op jit(solution)/shard_map/pallas_call | solution.py:254
  48.1 2.0 %collective-permute-done.6.in_ref = bf16[4,528,128]{2,1,0:T(8,128)(2,1)S(1)} collective-permute-done((bf16[4,528,128]{2,1,0:T(8,128)(2,1)S(1)}, bf16[4,528,128]{2,1,0:T(8,128)(2,1)S(1)}, u32[]{:S(2)}, u32[]{:S(2)}) %collective-permute-start.6) | collective-permute-done | bytes 540704 | tf_op jit(solution)/shard_map/ppermute | solution.py:462
  50.1 1.0 %shard_map.89 = bf16[4,528,128]{2,1,0:T(8,128)(2,1)S(1)} custom-call(bf16[4,528,128]{2,1,0:T(8,128)(2,1)S(1)} %collective-permute-done.6.in_ref, f32[4,512,128]{2,1,0:T(8,128)S(1)} %get-tuple-element.62.acc_ref, bf16[4,16,128]{2,1,0:T(8,128)(2,1)S(1)} %get-tuple-element.63.stat_ref), custom_call_target="tpu_custom_call" | custom-call | flops 1605632 | bytes 3211264 | tf_op jit(solution)/shard_map/pallas_call | solution.py:389
  51.1 1.8 %collective-permute-start.8 = (bf16[4,528,128]{2,1,0:T(8,128)(2,1)S(1)}, bf16[4,528,128]{2,1,0:T(8,128)(2,1)S(1)}, u32[]{:S(2)}, u32[]{:S(2)}) collective-permute-start(bf16[4,528,128]{2,1,0:T(8,128)(2,1)S(1)} %shard_map.89), channel_id=1, source_target_pairs={{0,4},{4,8},{8,12},{12,14},{14,10},{10,6},{6,2},{2,0},{1,3},{5,1},... | collective-permute-start | bytes 1622024 | tf_op jit(solution)/shard_map/ppermute | solution.py:462
  52.9 1.8 %shard_map.90 = (f32[2,512,128]{2,1,0:T(8,128)S(1)}, bf16[2,16,128]{2,1,0:T(8,128)(2,1)S(1)}) custom-call(s32[1,128]{1,0:T(1,128)S(1)} %fusion.3.refs_0_, bf16[2064,128]{1,0:T(8,128)(2,1)S(1)} %shard_map.86.refs_1_, bf16[2,64,512]{2,1,0:T(8,128)(2,1)S(1)} %bitcast.4, bf16[32,2,64,512]{3,2,1,0:T(8,128)(2,1)S(1)} %copy-done.4), custom_call_target="tpu_custom_call" | custom-call | flops 536870912 | bytes 1310720 | tf_op jit(solution)/shard_map/pallas_call | solution.py:254
  54.7 1.1 %collective-permute-done.9.refs_1_ = bf16[2064,128]{1,0:T(8,128)(2,1)S(1)} collective-permute-done((bf16[2064,128]{1,0:T(8,128)(2,1)S(1)}, bf16[2064,128]{1,0:T(8,128)(2,1)S(1)}, u32[]{:S(2)}, u32[]{:S(2)}) %collective-permute-start.9) | collective-permute-done | bytes 528416 | tf_op jit(solution)/shard_map/ppermute | solution.py:462
  55.8 1.6 %collective-permute-start.11 = (bf16[2064,128]{1,0:T(8,128)(2,1)S(1)}, bf16[2064,128]{1,0:T(8,128)(2,1)S(1)}, u32[]{:S(2)}, u32[]{:S(2)}) collective-permute-start(bf16[2064,128]{1,0:T(8,128)(2,1)S(1)} %collective-permute-done.9.refs_1_), channel_id=1, source_target_pairs={{0,4},{4,8},{8,12},{12,14},{14,10},{10,6},{6,2},{2,0},{1,3},{5,1},... | collective-permute-start | bytes 1585160 | tf_op jit(solution)/shard_map/ppermute | solution.py:462
  57.3 2.2 %shard_map.91 = (f32[4,512,128]{2,1,0:T(8,128)S(1)}, bf16[4,16,128]{2,1,0:T(8,128)(2,1)S(1)}) custom-call(s32[1,128]{1,0:T(1,128)S(1)} %fusion.5.refs_0_, bf16[2064,128]{1,0:T(8,128)(2,1)S(1)} %collective-permute-done.9.refs_1_, bf16[32,2,64,512]{3,2,1,0:T(8,128)(2,1)S(1)} %copy-done.4), custom_call_target="tpu_custom_call" | custom-call | flops 1073741824 | bytes 2621440 | tf_op jit(solution)/shard_map/pallas_call | solution.py:254
  59.6 2.0 %collective-permute-done.8.in_ref = bf16[4,528,128]{2,1,0:T(8,128)(2,1)S(1)} collective-permute-done((bf16[4,528,128]{2,1,0:T(8,128)(2,1)S(1)}, bf16[4,528,128]{2,1,0:T(8,128)(2,1)S(1)}, u32[]{:S(2)}, u32[]{:S(2)}) %collective-permute-start.8) | collective-permute-done | bytes 540704 | tf_op jit(solution)/shard_map/ppermute | solution.py:462
  61.5 1.0 %shard_map.92 = bf16[4,528,128]{2,1,0:T(8,128)(2,1)S(1)} custom-call(bf16[4,528,128]{2,1,0:T(8,128)(2,1)S(1)} %collective-permute-done.8.in_ref, f32[4,512,128]{2,1,0:T(8,128)S(1)} %get-tuple-element.69.acc_ref, bf16[4,16,128]{2,1,0:T(8,128)(2,1)S(1)} %get-tuple-element.70.stat_ref), custom_call_target="tpu_custom_call" | custom-call | flops 1605632 | bytes 3211264 | tf_op jit(solution)/shard_map/pallas_call | solution.py:389
  62.5 1.6 %collective-permute-start.10 = (bf16[4,528,128]{2,1,0:T(8,128)(2,1)S(1)}, bf16[4,528,128]{2,1,0:T(8,128)(2,1)S(1)}, u32[]{:S(2)}, u32[]{:S(2)}) collective-permute-start(bf16[4,528,128]{2,1,0:T(8,128)(2,1)S(1)} %shard_map.92), channel_id=1, source_target_pairs={{0,4},{4,8},{8,12},{12,14},{14,10},{10,6},{6,2},{2,0},{1,3},{5,1},... | collective-permute-start | bytes 1622024 | tf_op jit(solution)/shard_map/ppermute | solution.py:462
  64.2 3.0 %collective-permute-done.11.refs_1_ = bf16[2064,128]{1,0:T(8,128)(2,1)S(1)} collective-permute-done((bf16[2064,128]{1,0:T(8,128)(2,1)S(1)}, bf16[2064,128]{1,0:T(8,128)(2,1)S(1)}, u32[]{:S(2)}, u32[]{:S(2)}) %collective-permute-start.11) | collective-permute-done | bytes 528416 | tf_op jit(solution)/shard_map/ppermute | solution.py:462
  67.2 1.6 %collective-permute-start.13 = (bf16[2064,128]{1,0:T(8,128)(2,1)S(1)}, bf16[2064,128]{1,0:T(8,128)(2,1)S(1)}, u32[]{:S(2)}, u32[]{:S(2)}) collective-permute-start(bf16[2064,128]{1,0:T(8,128)(2,1)S(1)} %collective-permute-done.11.refs_1_), channel_id=1, source_target_pairs={{0,4},{4,8},{8,12},{12,14},{14,10},{10,6},{6,2},{2,0},{1,3},{5,1},... | collective-permute-start | bytes 1585160 | tf_op jit(solution)/shard_map/ppermute | solution.py:462
  68.8 2.5 %collective-permute-start.14 = (bf16[1,2,64,512]{3,2,1,0:T(8,128)(2,1)S(1)}, bf16[1,2,64,512]{3,2,1,0:T(8,128)(2,1)S(1)}, u32[]{:S(2)}, u32[]{:S(2)}) collective-permute-start(bf16[1,2,64,512]{3,2,1,0:T(8,128)(2,1)S(1)} %copy-done.5), channel_id=1, source_target_pairs={{8,0},{10,2},{12,4},{14,6},{0,8},{2,10},{4,12},{6,14},{9,1},{11,3}... | collective-permute-start | bytes 393224 | tf_op jit(solution)/shard_map/ppermute | solution.py:27
  71.3 2.2 %shard_map.93 = (f32[4,512,128]{2,1,0:T(8,128)S(1)}, bf16[4,16,128]{2,1,0:T(8,128)(2,1)S(1)}) custom-call(s32[1,128]{1,0:T(1,128)S(1)} %fusion.6.refs_0_.far_ref, bf16[2064,128]{1,0:T(8,128)(2,1)S(1)} %collective-permute-done.11.refs_1_, bf16[32,2,64,512]{3,2,1,0:T(8,128)(2,1)S(1)} %copy-done.4), custom_call_target="tpu_custom_call" | custom-call | flops 1 | bytes 1 | tf_op jit(solution)/shard_map/pallas_call | solution.py:254
  73.5 0.0 collective-permute-done.10.in_ref
  73.6 0.6 shard_map.94
  74.2 3.0 %collective-permute-start.15 = (bf16[2,528,128]{2,1,0:T(8,128)(2,1)S(1)}, bf16[2,528,128]{2,1,0:T(8,128)(2,1)S(1)}, u32[]{:S(2)}, u32[]{:S(2)}) collective-permute-start(bf16[2,528,128]{2,1,0:T(8,128)(2,1)S(1)} %shard_map.94), channel_id=1, source_target_pairs={{0,4},{4,8},{8,12},{12,14},{14,10},{10,6},{6,2},{2,0},{1,3},{5,1},... | collective-permute-start | bytes 811016 | tf_op jit(solution)/shard_map/ppermute | solution.py:462
  77.2 0.6 shard_map.95
  77.8 2.5 %collective-permute-start.12 = (bf16[2,528,128]{2,1,0:T(8,128)(2,1)S(1)}, bf16[2,528,128]{2,1,0:T(8,128)(2,1)S(1)}, u32[]{:S(2)}, u32[]{:S(2)}) collective-permute-start(bf16[2,528,128]{2,1,0:T(8,128)(2,1)S(1)} %shard_map.95), channel_id=1, source_target_pairs={{0,4},{4,8},{8,12},{12,14},{14,10},{10,6},{6,2},{2,0},{1,3},{5,1},... | collective-permute-start | bytes 811016 | tf_op jit(solution)/shard_map/ppermute | solution.py:462
  80.3 0.0 collective-permute-done.13.refs_1_
  80.3 2.2 %shard_map.96 = (f32[4,512,128]{2,1,0:T(8,128)S(1)}, bf16[4,16,128]{2,1,0:T(8,128)(2,1)S(1)}) custom-call(s32[1,128]{1,0:T(1,128)S(1)} %fusion.7.refs_0_, bf16[2064,128]{1,0:T(8,128)(2,1)S(1)} %collective-permute-done.13.refs_1_, bf16[32,2,64,512]{3,2,1,0:T(8,128)(2,1)S(1)} %copy-done.4), custom_call_target="tpu_custom_call" | custom-call | flops 8589934592 | bytes 33554432 | tf_op jit(solution)/shard_map/pallas_call | solution.py:254
  82.6 0.0 collective-permute-done.14.page_ref
  82.6 0.9 collective-permute-done.15.in_ref
  83.5 0.6 shard_map.97
  84.1 4.4 %collective-permute-start.17 = (bf16[2,528,128]{2,1,0:T(8,128)(2,1)S(1)}, bf16[2,528,128]{2,1,0:T(8,128)(2,1)S(1)}, u32[]{:S(2)}, u32[]{:S(2)}) collective-permute-start(bf16[2,528,128]{2,1,0:T(8,128)(2,1)S(1)} %shard_map.97), channel_id=1, source_target_pairs={{0,4},{4,8},{8,12},{12,14},{14,10},{10,6},{6,2},{2,0},{1,3},{5,1},... | collective-permute-start | bytes 811016 | tf_op jit(solution)/shard_map/ppermute | solution.py:462
  88.6 0.0 collective-permute-done.12.in_ref
  88.6 0.6 shard_map.98
  89.2 2.5 %collective-permute-start.16 = (bf16[2,528,128]{2,1,0:T(8,128)(2,1)S(1)}, bf16[2,528,128]{2,1,0:T(8,128)(2,1)S(1)}, u32[]{:S(2)}, u32[]{:S(2)}) collective-permute-start(bf16[2,528,128]{2,1,0:T(8,128)(2,1)S(1)} %shard_map.98), channel_id=1, source_target_pairs={{0,4},{4,8},{8,12},{12,14},{14,10},{10,6},{6,2},{2,0},{1,3},{5,1},... | collective-permute-start | bytes 811016 | tf_op jit(solution)/shard_map/ppermute | solution.py:462
  91.8 1.2 %shard_map.99 = bf16[32,2,64,512]{3,2,1,0:T(8,128)(2,1)} custom-call(s32[1]{0:T(128)} %bitcast.1.me_ref, s32[1]{0:T(128)} %bitcast.2.core_ref, s32[1,128]{1,0:T(1,128)S(1)} %fusion.1.refs_0_.near_ref, s32[1,128]{1,0:T(1,128)S(1)} %fusion.6.refs_0_.far_ref, ...), custom_call_target="tpu_custom_call", output_to_operand_aliasing={{}: (5, {})} | custom-call | flops 1 | bytes 1 | tf_op jit(solution)/shard_map/pallas_call | solution.py:292
  93.0 0.0 collective-permute-done.17.in_ref
  93.0 1.3 %shard_map.100.refs_0_ = bf16[1,64,4096]{2,1,0:T(8,128)(2,1)} custom-call(bf16[2,528,128]{2,1,0:T(8,128)(2,1)S(1)} %collective-permute-done.17.in_ref, f32[2,512,128]{2,1,0:T(8,128)S(1)} %get-tuple-element.59.acc_ref, bf16[2,16,128]{2,1,0:T(8,128)(2,1)S(1)} %get-tuple-element.60.stat_ref), custom_call_target="tpu_custom_call" | custom-call | tf_op jit(solution)/shard_map/pallas_call | solution.py:373
  94.3 1.5 %collective-permute-done.16.in_ref = bf16[2,528,128]{2,1,0:T(8,128)(2,1)S(1)} collective-permute-done((bf16[2,528,128]{2,1,0:T(8,128)(2,1)S(1)}, bf16[2,528,128]{2,1,0:T(8,128)(2,1)S(1)}, u32[]{:S(2)}, u32[]{:S(2)}) %collective-permute-start.16) | collective-permute-done | bytes 270368 | tf_op jit(solution)/shard_map/ppermute | solution.py:462
  95.7 1.3 %shard_map.101 = bf16[1,64,4096]{2,1,0:T(8,128)(2,1)} custom-call(bf16[2,528,128]{2,1,0:T(8,128)(2,1)S(1)} %collective-permute-done.16.in_ref, f32[2,512,128]{2,1,0:T(8,128)S(1)} %get-tuple-element.66.acc_ref, bf16[2,16,128]{2,1,0:T(8,128)(2,1)S(1)} %get-tuple-element.67.stat_ref, ...), custom_call_target="tpu_custom_call", output_to_operand_aliasing={{}: (3, {})} | custom-call | tf_op jit(solution)/shard_map/pallas_call | solution.py:373
  (21 shorter events, 0.1 us)
Async XLA Ops:
  0.6 10.4 %collective-permute-start = (bf16[1,64,4096]{2,1,0:T(8,128)(2,1)}, bf16[1,64,4096]{2,1,0:T(8,128)(2,1)S(1)}, u32[]{:S(2)}, u32[]{:S(2)}) collective-permute-start(bf16[1,64,4096]{2,1,0:T(8,128)(2,1)} %q_ref), channel_id=1, source_target_pairs={{0,4},{4,8},{8,12},{12,14},{14,10},{10,6},{6,2},{2,0},{1,3},{5,1},... | collective-permute-start | bytes 1572872 | tf_op jit(solution)/shard_map/ppermute | solution.py:462
  5.0 0.7 copy-start.7
  5.9 5.1 %collective-permute-start.1 = (bf16[16,128]{1,0:T(8,128)(2,1)S(1)}, bf16[16,128]{1,0:T(8,128)(2,1)S(1)}, u32[]{:S(2)}, u32[]{:S(2)}) collective-permute-start(bf16[16,128]{1,0:T(8,128)(2,1)S(1)} %shard_map.77.lists_ref), channel_id=1, source_target_pairs={{0,4},{4,8},{8,12},{12,14},{14,10},{10,6},{6,2},{2,0},{1,3},{5,1},... | collective-permute-start | bytes 12296 | tf_op jit(solution)/shard_map/ppermute | solution.py:462
  7.5 2.2 %copy-start = (bf16[32,2,64,512]{3,2,1,0:T(8,128)(2,1)S(1)}, bf16[32,2,64,512]{3,2,1,0:T(8,128)(2,1)}, u32[]{:S(2)}) copy-start(bf16[32,2,64,512]{3,2,1,0:T(8,128)(2,1)} %refs_2_.13) | copy-start | bytes 12582916
  11.2 9.3 %collective-permute-start.3 = (bf16[2064,128]{1,0:T(8,128)(2,1)S(1)}, bf16[2064,128]{1,0:T(8,128)(2,1)S(1)}, u32[]{:S(2)}, u32[]{:S(2)}) collective-permute-start(bf16[2064,128]{1,0:T(8,128)(2,1)S(1)} %shard_map.79.refs_1_), channel_id=1, source_target_pairs={{0,4},{4,8},{8,12},{12,14},{14,10},{10,6},{6,2},{2,0},{1,3},{5,1},... | collective-permute-start | bytes 1585160 | tf_op jit(solution)/shard_map/ppermute | solution.py:462
  13.3 2.2 %copy-start.1 = (bf16[32,2,64,512]{3,2,1,0:T(8,128)(2,1)S(1)}, bf16[32,2,64,512]{3,2,1,0:T(8,128)(2,1)}, u32[]{:S(2)}) copy-start(bf16[32,2,64,512]{3,2,1,0:T(8,128)(2,1)} %refs_2_.13) | copy-start | bytes 12582916
  15.5 7.0 %copy-start.2 = (bf16[32,2,64,512]{3,2,1,0:T(8,128)(2,1)S(1)}, bf16[32,2,64,512]{3,2,1,0:T(8,128)(2,1)}, u32[]{:S(2)}) copy-start(bf16[32,2,64,512]{3,2,1,0:T(8,128)(2,1)} %refs_2_.13) | copy-start | bytes 12582916
  17.8 9.4 %collective-permute-start.2 = (bf16[4,528,128]{2,1,0:T(8,128)(2,1)S(1)}, bf16[4,528,128]{2,1,0:T(8,128)(2,1)S(1)}, u32[]{:S(2)}, u32[]{:S(2)}) collective-permute-start(bf16[4,528,128]{2,1,0:T(8,128)(2,1)S(1)} %shard_map.81), channel_id=1, source_target_pairs={{0,4},{4,8},{8,12},{12,14},{14,10},{10,6},{6,2},{2,0},{1,3},{5,1},... | collective-permute-start | bytes 1622024 | tf_op jit(solution)/shard_map/ppermute | solution.py:462
  20.4 12.4 %collective-permute-start.5 = (bf16[2064,128]{1,0:T(8,128)(2,1)S(1)}, bf16[2064,128]{1,0:T(8,128)(2,1)S(1)}, u32[]{:S(2)}, u32[]{:S(2)}) collective-permute-start(bf16[2064,128]{1,0:T(8,128)(2,1)S(1)} %collective-permute-done.3.refs_1_), channel_id=1, source_target_pairs={{0,4},{4,8},{8,12},{12,14},{14,10},{10,6},{6,2},{2,0},{1,3},{5,1},... | collective-permute-start | bytes 1585160 | tf_op jit(solution)/shard_map/ppermute | solution.py:462
  28.2 11.4 %collective-permute-start.4 = (bf16[4,528,128]{2,1,0:T(8,128)(2,1)S(1)}, bf16[4,528,128]{2,1,0:T(8,128)(2,1)S(1)}, u32[]{:S(2)}, u32[]{:S(2)}) collective-permute-start(bf16[4,528,128]{2,1,0:T(8,128)(2,1)S(1)} %shard_map.83), channel_id=1, source_target_pairs={{0,4},{4,8},{8,12},{12,14},{14,10},{10,6},{6,2},{2,0},{1,3},{5,1},... | collective-permute-start | bytes 1622024 | tf_op jit(solution)/shard_map/ppermute | solution.py:462
  32.8 11.5 %collective-permute-start.7 = (bf16[2064,128]{1,0:T(8,128)(2,1)S(1)}, bf16[2064,128]{1,0:T(8,128)(2,1)S(1)}, u32[]{:S(2)}, u32[]{:S(2)}) collective-permute-start(bf16[2064,128]{1,0:T(8,128)(2,1)S(1)} %collective-permute-done.5.refs_1_), channel_id=1, source_target_pairs={{0,4},{4,8},{8,12},{12,14},{14,10},{10,6},{6,2},{2,0},{1,3},{5,1},... | collective-permute-start | bytes 1585160 | tf_op jit(solution)/shard_map/ppermute | solution.py:462
  34.4 2.2 %copy-start.3 = (bf16[32,2,64,512]{3,2,1,0:T(8,128)(2,1)S(1)}, bf16[32,2,64,512]{3,2,1,0:T(8,128)(2,1)}, u32[]{:S(2)}) copy-start(bf16[32,2,64,512]{3,2,1,0:T(8,128)(2,1)} %refs_2_.13) | copy-start | bytes 12582916
  36.6 5.6 %copy-start.6 = (bf16[1,64,4096]{2,1,0:T(8,128)(2,1)S(1)}, bf16[1,64,4096]{2,1,0:T(8,128)(2,1)}, u32[]{:S(2)}) copy-start(bf16[1,64,4096]{2,1,0:T(8,128)(2,1)} %q_ref) | copy-start | bytes 1572868
  36.6 5.7 %copy-start.4 = (bf16[32,2,64,512]{3,2,1,0:T(8,128)(2,1)S(1)}, bf16[32,2,64,512]{3,2,1,0:T(8,128)(2,1)}, u32[]{:S(2)}) copy-start(bf16[32,2,64,512]{3,2,1,0:T(8,128)(2,1)} %refs_2_.13) | copy-start | bytes 12582916
  36.6 5.7 %copy-start.5 = (bf16[1,2,64,512]{3,2,1,0:T(8,128)(2,1)S(1)}, bf16[1,2,64,512]{3,2,1,0:T(8,128)(2,1)}, u32[]{:S(2)}) copy-start(bf16[1,2,64,512]{3,2,1,0:T(8,128)(2,1)} %param.7) | copy-start | bytes 393220
  40.6 9.5 %collective-permute-start.6 = (bf16[4,528,128]{2,1,0:T(8,128)(2,1)S(1)}, bf16[4,528,128]{2,1,0:T(8,128)(2,1)S(1)}, u32[]{:S(2)}, u32[]{:S(2)}) collective-permute-start(bf16[4,528,128]{2,1,0:T(8,128)(2,1)S(1)} %shard_map.85), channel_id=1, source_target_pairs={{0,4},{4,8},{8,12},{12,14},{14,10},{10,6},{6,2},{2,0},{1,3},{5,1},... | collective-permute-start | bytes 1622024 | tf_op jit(solution)/shard_map/ppermute | solution.py:462
  44.3 11.5 %collective-permute-start.9 = (bf16[2064,128]{1,0:T(8,128)(2,1)S(1)}, bf16[2064,128]{1,0:T(8,128)(2,1)S(1)}, u32[]{:S(2)}, u32[]{:S(2)}) collective-permute-start(bf16[2064,128]{1,0:T(8,128)(2,1)S(1)} %collective-permute-done.7.refs_1_), channel_id=1, source_target_pairs={{0,4},{4,8},{8,12},{12,14},{14,10},{10,6},{6,2},{2,0},{1,3},{5,1},... | collective-permute-start | bytes 1585160 | tf_op jit(solution)/shard_map/ppermute | solution.py:462
  51.1 10.5 %collective-permute-start.8 = (bf16[4,528,128]{2,1,0:T(8,128)(2,1)S(1)}, bf16[4,528,128]{2,1,0:T(8,128)(2,1)S(1)}, u32[]{:S(2)}, u32[]{:S(2)}) collective-permute-start(bf16[4,528,128]{2,1,0:T(8,128)(2,1)S(1)} %shard_map.89), channel_id=1, source_target_pairs={{0,4},{4,8},{8,12},{12,14},{14,10},{10,6},{6,2},{2,0},{1,3},{5,1},... | collective-permute-start | bytes 1622024 | tf_op jit(solution)/shard_map/ppermute | solution.py:462
  55.8 11.5 %collective-permute-start.11 = (bf16[2064,128]{1,0:T(8,128)(2,1)S(1)}, bf16[2064,128]{1,0:T(8,128)(2,1)S(1)}, u32[]{:S(2)}, u32[]{:S(2)}) collective-permute-start(bf16[2064,128]{1,0:T(8,128)(2,1)S(1)} %collective-permute-done.9.refs_1_), channel_id=1, source_target_pairs={{0,4},{4,8},{8,12},{12,14},{14,10},{10,6},{6,2},{2,0},{1,3},{5,1},... | collective-permute-start | bytes 1585160 | tf_op jit(solution)/shard_map/ppermute | solution.py:462
  62.5 11.0 %collective-permute-start.10 = (bf16[4,528,128]{2,1,0:T(8,128)(2,1)S(1)}, bf16[4,528,128]{2,1,0:T(8,128)(2,1)S(1)}, u32[]{:S(2)}, u32[]{:S(2)}) collective-permute-start(bf16[4,528,128]{2,1,0:T(8,128)(2,1)S(1)} %shard_map.92), channel_id=1, source_target_pairs={{0,4},{4,8},{8,12},{12,14},{14,10},{10,6},{6,2},{2,0},{1,3},{5,1},... | collective-permute-start | bytes 1622024 | tf_op jit(solution)/shard_map/ppermute | solution.py:462
  67.2 13.1 %collective-permute-start.13 = (bf16[2064,128]{1,0:T(8,128)(2,1)S(1)}, bf16[2064,128]{1,0:T(8,128)(2,1)S(1)}, u32[]{:S(2)}, u32[]{:S(2)}) collective-permute-start(bf16[2064,128]{1,0:T(8,128)(2,1)S(1)} %collective-permute-done.11.refs_1_), channel_id=1, source_target_pairs={{0,4},{4,8},{8,12},{12,14},{14,10},{10,6},{6,2},{2,0},{1,3},{5,1},... | collective-permute-start | bytes 1585160 | tf_op jit(solution)/shard_map/ppermute | solution.py:462
  68.8 13.8 %collective-permute-start.14 = (bf16[1,2,64,512]{3,2,1,0:T(8,128)(2,1)S(1)}, bf16[1,2,64,512]{3,2,1,0:T(8,128)(2,1)S(1)}, u32[]{:S(2)}, u32[]{:S(2)}) collective-permute-start(bf16[1,2,64,512]{3,2,1,0:T(8,128)(2,1)S(1)} %copy-done.5), channel_id=1, source_target_pairs={{8,0},{10,2},{12,4},{14,6},{0,8},{2,10},{4,12},{6,14},{9,1},{11,3}... | collective-permute-start | bytes 393224 | tf_op jit(solution)/shard_map/ppermute | solution.py:27
  74.2 9.3 %collective-permute-start.15 = (bf16[2,528,128]{2,1,0:T(8,128)(2,1)S(1)}, bf16[2,528,128]{2,1,0:T(8,128)(2,1)S(1)}, u32[]{:S(2)}, u32[]{:S(2)}) collective-permute-start(bf16[2,528,128]{2,1,0:T(8,128)(2,1)S(1)} %shard_map.94), channel_id=1, source_target_pairs={{0,4},{4,8},{8,12},{12,14},{14,10},{10,6},{6,2},{2,0},{1,3},{5,1},... | collective-permute-start | bytes 811016 | tf_op jit(solution)/shard_map/ppermute | solution.py:462
  77.8 10.8 %collective-permute-start.12 = (bf16[2,528,128]{2,1,0:T(8,128)(2,1)S(1)}, bf16[2,528,128]{2,1,0:T(8,128)(2,1)S(1)}, u32[]{:S(2)}, u32[]{:S(2)}) collective-permute-start(bf16[2,528,128]{2,1,0:T(8,128)(2,1)S(1)} %shard_map.95), channel_id=1, source_target_pairs={{0,4},{4,8},{8,12},{12,14},{14,10},{10,6},{6,2},{2,0},{1,3},{5,1},... | collective-permute-start | bytes 811016 | tf_op jit(solution)/shard_map/ppermute | solution.py:462
  84.1 8.8 %collective-permute-start.17 = (bf16[2,528,128]{2,1,0:T(8,128)(2,1)S(1)}, bf16[2,528,128]{2,1,0:T(8,128)(2,1)S(1)}, u32[]{:S(2)}, u32[]{:S(2)}) collective-permute-start(bf16[2,528,128]{2,1,0:T(8,128)(2,1)S(1)} %shard_map.97), channel_id=1, source_target_pairs={{0,4},{4,8},{8,12},{12,14},{14,10},{10,6},{6,2},{2,0},{1,3},{5,1},... | collective-permute-start | bytes 811016 | tf_op jit(solution)/shard_map/ppermute | solution.py:462
  89.2 6.5 %collective-permute-start.16 = (bf16[2,528,128]{2,1,0:T(8,128)(2,1)S(1)}, bf16[2,528,128]{2,1,0:T(8,128)(2,1)S(1)}, u32[]{:S(2)}, u32[]{:S(2)}) collective-permute-start(bf16[2,528,128]{2,1,0:T(8,128)(2,1)S(1)} %shard_map.98), channel_id=1, source_target_pairs={{0,4},{4,8},{8,12},{12,14},{14,10},{10,6},{6,2},{2,0},{1,3},{5,1},... | collective-permute-start | bytes 811016 | tf_op jit(solution)/shard_map/ppermute | solution.py:462

commit v22 on v21

--- a/solution.py
+++ b/solution.py
@@ -513,7 +513,7 @@
                 blocks.append(merged(block, part, at, half_heads[0], len(half_heads)))
         partial = [onward(block) for block in blocks]
         token = blocks
-        if step in (half - 1, half):
+        if step in (half, half + 1):
             if own_queries is None:
                 own_queries = joined(after(queries, token), mine)
             jobs = [(0, n, h) for n, h in enumerate(halves[len(own)])]

time: 97.5 us -> 97.5 us (level)
  no operation moved by 1% of the time
where the time goes in v22:
time: 97.5 us; the launch traced here: 97.2 us
  starting transfers between devices  38.5 us (39%)
  Pallas kernels  31 us (32%)
  waiting for transfers between devices  18 us (18%)
  local copies, waits for them, and re-layouts  7.23 us (7%)
  between operations  2.32 us (2%)
    ppermute x17, starting transfers between devices, onward(): return lax.ppermute(x, ('store', 'tensor'), route)  36 us
    pallas_call x9, Pallas kernels, attend(): pl.pallas_call(functools.partial(attend_kernel, sizes + (count,), jobs, o...  20.3 us
    ppermute x17, waiting for transfers between devices, onward(): return lax.ppermute(x, ('store', 'tensor'), route)  18 us
    unnamed x16, local copies, waits for them, and re-layouts  7.23 us
    pallas_call x11, Pallas kernels, call(): pl.pallas_call(kernel, out_shape=shape, in_specs=[VMEM] * len(args), out_...  6.69 us
    ppermute x1, starting transfers between devices, shifted(): return lax.ppermute(block, axis, route)  2.53 us
    pallas_call x2, Pallas kernels, finish(): pl.pallas_call(functools.partial(final_kernel, suffix, first), out_shape=...  2.53 us
  transfers between devices with their start and end apart: 18, of which 11 were waited for; matrix products, arithmetic and copies ran while one was open for 0% of the time, Pallas kernels for 31%

profile of v22, /device:TPU:0, one launch (start us, length us, event | category | flops | bytes accessed | tf_op | source)
XLA Modules:
  0.0 97.2 jit_solution(7881867091252334393)
XLA Ops:
  0.6 3.1 %collective-permute-start = (bf16[1,64,4096]{2,1,0:T(8,128)(2,1)}, bf16[1,64,4096]{2,1,0:T(8,128)(2,1)S(1)}, u32[]{:S(2)}, u32[]{:S(2)}) collective-permute-start(bf16[1,64,4096]{2,1,0:T(8,128)(2,1)} %q_ref), channel_id=1, source_target_pairs={{0,4},{4,8},{8,12},{12,14},{14,10},{10,6},{6,2},{2,0},{1,3},{5,1},... | collective-permute-start | bytes 1572872 | tf_op jit(solution)/shard_map/ppermute | solution.py:462
  5.0 0.6 copy-done.7
  5.7 0.3 shard_map.77.lists_ref
  5.9 1.6 %collective-permute-start.1 = (bf16[16,128]{1,0:T(8,128)(2,1)S(1)}, bf16[16,128]{1,0:T(8,128)(2,1)S(1)}, u32[]{:S(2)}, u32[]{:S(2)}) collective-permute-start(bf16[16,128]{1,0:T(8,128)(2,1)S(1)} %shard_map.77.lists_ref), channel_id=1, source_target_pairs={{0,4},{4,8},{8,12},{12,14},{14,10},{10,6},{6,2},{2,0},{1,3},{5,1},... | collective-permute-start | bytes 12296 | tf_op jit(solution)/shard_map/ppermute | solution.py:462
  7.5 2.2 %copy-done = bf16[32,2,64,512]{3,2,1,0:T(8,128)(2,1)S(1)} copy-done((bf16[32,2,64,512]{3,2,1,0:T(8,128)(2,1)S(1)}, bf16[32,2,64,512]{3,2,1,0:T(8,128)(2,1)}, u32[]{:S(2)}) %copy-start) | copy-done | bytes 4194328
  9.7 1.3 %collective-permute-done.q_ref = bf16[1,64,4096]{2,1,0:T(8,128)(2,1)S(1)} collective-permute-done((bf16[1,64,4096]{2,1,0:T(8,128)(2,1)}, bf16[1,64,4096]{2,1,0:T(8,128)(2,1)S(1)}, u32[]{:S(2)}, u32[]{:S(2)}) %collective-permute-start) | collective-permute-done | bytes 524320 | tf_op jit(solution)/shard_map/ppermute | solution.py:462
  11.0 0.0 collective-permute-done.1.lists_ref
  11.1 0.1 shard_map.79.refs_1_
  11.2 2.1 %collective-permute-start.3 = (bf16[2064,128]{1,0:T(8,128)(2,1)S(1)}, bf16[2064,128]{1,0:T(8,128)(2,1)S(1)}, u32[]{:S(2)}, u32[]{:S(2)}) collective-permute-start(bf16[2064,128]{1,0:T(8,128)(2,1)S(1)} %shard_map.79.refs_1_), channel_id=1, source_target_pairs={{0,4},{4,8},{8,12},{12,14},{14,10},{10,6},{6,2},{2,0},{1,3},{5,1},... | collective-permute-start | bytes 1585160 | tf_op jit(solution)/shard_map/ppermute | solution.py:462
  13.3 2.2 %copy-done.1 = bf16[32,2,64,512]{3,2,1,0:T(8,128)(2,1)S(1)} copy-done((bf16[32,2,64,512]{3,2,1,0:T(8,128)(2,1)S(1)}, bf16[32,2,64,512]{3,2,1,0:T(8,128)(2,1)}, u32[]{:S(2)}) %copy-start.1) | copy-done | bytes 4194328
  15.5 2.2 %shard_map.80 = (f32[4,512,128]{2,1,0:T(8,128)S(1)}, bf16[4,16,128]{2,1,0:T(8,128)(2,1)S(1)}) custom-call(s32[1,128]{1,0:T(1,128)S(1)} %fusion.refs_0_, bf16[2064,128]{1,0:T(8,128)(2,1)S(1)} %shard_map.79.refs_1_, bf16[32,2,64,512]{3,2,1,0:T(8,128)(2,1)S(1)} %copy-done.1), custom_call_target="tpu_custom_call" | custom-call | flops 1073741824 | bytes 2621440 | tf_op jit(solution)/shard_map/pallas_call | solution.py:254
  17.7 0.1 shard_map.81
  17.8 1.6 %collective-permute-start.2 = (bf16[4,528,128]{2,1,0:T(8,128)(2,1)S(1)}, bf16[4,528,128]{2,1,0:T(8,128)(2,1)S(1)}, u32[]{:S(2)}, u32[]{:S(2)}) collective-permute-start(bf16[4,528,128]{2,1,0:T(8,128)(2,1)S(1)} %shard_map.81), channel_id=1, source_target_pairs={{0,4},{4,8},{8,12},{12,14},{14,10},{10,6},{6,2},{2,0},{1,3},{5,1},... | collective-permute-start | bytes 1622024 | tf_op jit(solution)/shard_map/ppermute | solution.py:462
  19.4 1.0 %collective-permute-done.3.refs_1_ = bf16[2064,128]{1,0:T(8,128)(2,1)S(1)} collective-permute-done((bf16[2064,128]{1,0:T(8,128)(2,1)S(1)}, bf16[2064,128]{1,0:T(8,128)(2,1)S(1)}, u32[]{:S(2)}, u32[]{:S(2)}) %collective-permute-start.3) | collective-permute-done | bytes 528416 | tf_op jit(solution)/shard_map/ppermute | solution.py:462
  20.4 2.1 %collective-permute-start.5 = (bf16[2064,128]{1,0:T(8,128)(2,1)S(1)}, bf16[2064,128]{1,0:T(8,128)(2,1)S(1)}, u32[]{:S(2)}, u32[]{:S(2)}) collective-permute-start(bf16[2064,128]{1,0:T(8,128)(2,1)S(1)} %collective-permute-done.3.refs_1_), channel_id=1, source_target_pairs={{0,4},{4,8},{8,12},{12,14},{14,10},{10,6},{6,2},{2,0},{1,3},{5,1},... | collective-permute-start | bytes 1585160 | tf_op jit(solution)/shard_map/ppermute | solution.py:462
  22.5 2.7 %shard_map.82 = (f32[4,512,128]{2,1,0:T(8,128)S(1)}, bf16[4,16,128]{2,1,0:T(8,128)(2,1)S(1)}, bf16[32,2,64,512]{3,2,1,0:T(8,128)(2,1)}) custom-call(s32[1,128]{1,0:T(1,128)S(1)} %fusion.1.refs_0_.near_ref, bf16[2064,128]{1,0:T(8,128)(2,1)S(1)} %collective-permute-done.3.refs_1_, bf16[32,2,64,512]{3,2,1,0:T(8,128)(2,1)S(1)} %copy-done.2), custom_call_target="tpu_custom_call" | custom-call | flops 1073741824 | bytes 2621440 | tf_op jit(solution)/shard_map/pallas_call | solution.py:254
  25.3 1.9 %collective-permute-done.2.in_ref = bf16[4,528,128]{2,1,0:T(8,128)(2,1)S(1)} collective-permute-done((bf16[4,528,128]{2,1,0:T(8,128)(2,1)S(1)}, bf16[4,528,128]{2,1,0:T(8,128)(2,1)S(1)}, u32[]{:S(2)}, u32[]{:S(2)}) %collective-permute-start.2) | collective-permute-done | bytes 540704 | tf_op jit(solution)/shard_map/ppermute | solution.py:462
  27.2 1.0 %shard_map.83 = bf16[4,528,128]{2,1,0:T(8,128)(2,1)S(1)} custom-call(bf16[4,528,128]{2,1,0:T(8,128)(2,1)S(1)} %collective-permute-done.2.in_ref, f32[4,512,128]{2,1,0:T(8,128)S(1)} %get-tuple-element.49.acc_ref, bf16[4,16,128]{2,1,0:T(8,128)(2,1)S(1)} %get-tuple-element.50.stat_ref), custom_call_target="tpu_custom_call" | custom-call | flops 1605632 | bytes 3211264 | tf_op jit(solution)/shard_map/pallas_call | solution.py:389
  28.2 1.6 %collective-permute-start.4 = (bf16[4,528,128]{2,1,0:T(8,128)(2,1)S(1)}, bf16[4,528,128]{2,1,0:T(8,128)(2,1)S(1)}, u32[]{:S(2)}, u32[]{:S(2)}) collective-permute-start(bf16[4,528,128]{2,1,0:T(8,128)(2,1)S(1)} %shard_map.83), channel_id=1, source_target_pairs={{0,4},{4,8},{8,12},{12,14},{14,10},{10,6},{6,2},{2,0},{1,3},{5,1},... | collective-permute-start | bytes 1622024 | tf_op jit(solution)/shard_map/ppermute | solution.py:462
  29.8 3.0 %collective-permute-done.5.refs_1_ = bf16[2064,128]{1,0:T(8,128)(2,1)S(1)} collective-permute-done((bf16[2064,128]{1,0:T(8,128)(2,1)S(1)}, bf16[2064,128]{1,0:T(8,128)(2,1)S(1)}, u32[]{:S(2)}, u32[]{:S(2)}) %collective-permute-start.5) | collective-permute-done | bytes 528416 | tf_op jit(solution)/shard_map/ppermute | solution.py:462
  32.8 1.6 %collective-permute-start.7 = (bf16[2064,128]{1,0:T(8,128)(2,1)S(1)}, bf16[2064,128]{1,0:T(8,128)(2,1)S(1)}, u32[]{:S(2)}, u32[]{:S(2)}) collective-permute-start(bf16[2064,128]{1,0:T(8,128)(2,1)S(1)} %collective-permute-done.5.refs_1_), channel_id=1, source_target_pairs={{0,4},{4,8},{8,12},{12,14},{14,10},{10,6},{6,2},{2,0},{1,3},{5,1},... | collective-permute-start | bytes 1585160 | tf_op jit(solution)/shard_map/ppermute | solution.py:462
  34.4 2.9 %shard_map.84 = (f32[4,512,128]{2,1,0:T(8,128)S(1)}, bf16[4,16,128]{2,1,0:T(8,128)(2,1)S(1)}, bf16[32,2,64,512]{3,2,1,0:T(8,128)(2,1)}) custom-call(s32[1,128]{1,0:T(1,128)S(1)} %fusion.2.refs_0_, bf16[2064,128]{1,0:T(8,128)(2,1)S(1)} %collective-permute-done.5.refs_1_, bf16[32,2,64,512]{3,2,1,0:T(8,128)(2,1)S(1)} %copy-done.2, ...), custom_call_target="tpu_custom_call", output_to_operand_aliasing={{2}: (3, {})} | custom-call | flops 1073741824 | bytes 2621440 | tf_op jit(solution)/shard_map/pallas_call | solution.py:254
  37.4 1.3 %collective-permute-done.4.in_ref = bf16[4,528,128]{2,1,0:T(8,128)(2,1)S(1)} collective-permute-done((bf16[4,528,128]{2,1,0:T(8,128)(2,1)S(1)}, bf16[4,528,128]{2,1,0:T(8,128)(2,1)S(1)}, u32[]{:S(2)}, u32[]{:S(2)}) %collective-permute-start.4) | collective-permute-done | bytes 540704 | tf_op jit(solution)/shard_map/ppermute | solution.py:462
  38.6 1.0 %shard_map.85 = bf16[4,528,128]{2,1,0:T(8,128)(2,1)S(1)} custom-call(bf16[4,528,128]{2,1,0:T(8,128)(2,1)S(1)} %collective-permute-done.4.in_ref, f32[4,512,128]{2,1,0:T(8,128)S(1)} %get-tuple-element.54.acc_ref, bf16[4,16,128]{2,1,0:T(8,128)(2,1)S(1)} %get-tuple-element.55.stat_ref), custom_call_target="tpu_custom_call" | custom-call | flops 1605632 | bytes 3211264 | tf_op jit(solution)/shard_map/pallas_call | solution.py:389
  39.6 1.6 %collective-permute-start.6 = (bf16[4,528,128]{2,1,0:T(8,128)(2,1)S(1)}, bf16[4,528,128]{2,1,0:T(8,128)(2,1)S(1)}, u32[]{:S(2)}, u32[]{:S(2)}) collective-permute-start(bf16[4,528,128]{2,1,0:T(8,128)(2,1)S(1)} %shard_map.85), channel_id=1, source_target_pairs={{0,4},{4,8},{8,12},{12,14},{14,10},{10,6},{6,2},{2,0},{1,3},{5,1},... | collective-permute-start | bytes 1622024 | tf_op jit(solution)/shard_map/ppermute | solution.py:462
  41.3 3.0 %collective-permute-done.7.refs_1_ = bf16[2064,128]{1,0:T(8,128)(2,1)S(1)} collective-permute-done((bf16[2064,128]{1,0:T(8,128)(2,1)S(1)}, bf16[2064,128]{1,0:T(8,128)(2,1)S(1)}, u32[]{:S(2)}, u32[]{:S(2)}) %collective-permute-start.7) | collective-permute-done | bytes 528416 | tf_op jit(solution)/shard_map/ppermute | solution.py:462
  44.3 1.6 %collective-permute-start.9 = (bf16[2064,128]{1,0:T(8,128)(2,1)S(1)}, bf16[2064,128]{1,0:T(8,128)(2,1)S(1)}, u32[]{:S(2)}, u32[]{:S(2)}) collective-permute-start(bf16[2064,128]{1,0:T(8,128)(2,1)S(1)} %collective-permute-done.7.refs_1_), channel_id=1, source_target_pairs={{0,4},{4,8},{8,12},{12,14},{14,10},{10,6},{6,2},{2,0},{1,3},{5,1},... | collective-permute-start | bytes 1585160 | tf_op jit(solution)/shard_map/ppermute | solution.py:462
  45.9 2.2 %copy-done.3 = bf16[32,2,64,512]{3,2,1,0:T(8,128)(2,1)S(1)} copy-done((bf16[32,2,64,512]{3,2,1,0:T(8,128)(2,1)S(1)}, bf16[32,2,64,512]{3,2,1,0:T(8,128)(2,1)}, u32[]{:S(2)}) %copy-start.3) | copy-done | bytes 4194328
  48.1 2.2 %shard_map.86 = (f32[4,512,128]{2,1,0:T(8,128)S(1)}, bf16[4,16,128]{2,1,0:T(8,128)(2,1)S(1)}) custom-call(s32[1,128]{1,0:T(1,128)S(1)} %fusion.3.refs_0_, bf16[2064,128]{1,0:T(8,128)(2,1)S(1)} %collective-permute-done.7.refs_1_, bf16[32,2,64,512]{3,2,1,0:T(8,128)(2,1)S(1)} %copy-done.3), custom_call_target="tpu_custom_call" | custom-call | flops 1073741824 | bytes 2621440 | tf_op jit(solution)/shard_map/pallas_call | solution.py:254
  50.3 0.0 collective-permute-done.6.in_ref
  50.3 1.0 %shard_map.87 = bf16[4,528,128]{2,1,0:T(8,128)(2,1)S(1)} custom-call(bf16[4,528,128]{2,1,0:T(8,128)(2,1)S(1)} %collective-permute-done.6.in_ref, f32[4,512,128]{2,1,0:T(8,128)S(1)} %get-tuple-element.58.acc_ref, bf16[4,16,128]{2,1,0:T(8,128)(2,1)S(1)} %get-tuple-element.59.stat_ref), custom_call_target="tpu_custom_call" | custom-call | flops 1605632 | bytes 3211264 | tf_op jit(solution)/shard_map/pallas_call | solution.py:389
  51.3 1.8 %collective-permute-start.8 = (bf16[4,528,128]{2,1,0:T(8,128)(2,1)S(1)}, bf16[4,528,128]{2,1,0:T(8,128)(2,1)S(1)}, u32[]{:S(2)}, u32[]{:S(2)}) collective-permute-start(bf16[4,528,128]{2,1,0:T(8,128)(2,1)S(1)} %shard_map.87), channel_id=1, source_target_pairs={{0,4},{4,8},{8,12},{12,14},{14,10},{10,6},{6,2},{2,0},{1,3},{5,1},... | collective-permute-start | bytes 1622024 | tf_op jit(solution)/shard_map/ppermute | solution.py:462
  53.2 0.1 shard_map.88.refs_1_
  53.3 1.8 %shard_map.89 = (f32[2,512,128]{2,1,0:T(8,128)S(1)}, bf16[2,16,128]{2,1,0:T(8,128)(2,1)S(1)}) custom-call(s32[1,128]{1,0:T(1,128)S(1)} %fusion.4.refs_0_, bf16[2064,128]{1,0:T(8,128)(2,1)S(1)} %shard_map.88.refs_1_, bf16[2,64,512]{2,1,0:T(8,128)(2,1)S(1)} %bitcast.3, bf16[32,2,64,512]{3,2,1,0:T(8,128)(2,1)S(1)} %copy-done.4), custom_call_target="tpu_custom_call" | custom-call | flops 536870912 | bytes 1310720 | tf_op jit(solution)/shard_map/pallas_call | solution.py:254
  55.1 0.7 collective-permute-done.9.refs_1_
  55.8 1.6 %collective-permute-start.11 = (bf16[2064,128]{1,0:T(8,128)(2,1)S(1)}, bf16[2064,128]{1,0:T(8,128)(2,1)S(1)}, u32[]{:S(2)}, u32[]{:S(2)}) collective-permute-start(bf16[2064,128]{1,0:T(8,128)(2,1)S(1)} %collective-permute-done.9.refs_1_), channel_id=1, source_target_pairs={{0,4},{4,8},{8,12},{12,14},{14,10},{10,6},{6,2},{2,0},{1,3},{5,1},... | collective-permute-start | bytes 1585160 | tf_op jit(solution)/shard_map/ppermute | solution.py:462
  57.3 2.2 %shard_map.90 = (f32[4,512,128]{2,1,0:T(8,128)S(1)}, bf16[4,16,128]{2,1,0:T(8,128)(2,1)S(1)}) custom-call(s32[1,128]{1,0:T(1,128)S(1)} %fusion.5.refs_0_, bf16[2064,128]{1,0:T(8,128)(2,1)S(1)} %collective-permute-done.9.refs_1_, bf16[32,2,64,512]{3,2,1,0:T(8,128)(2,1)S(1)} %copy-done.4), custom_call_target="tpu_custom_call" | custom-call | flops 1073741824 | bytes 2621440 | tf_op jit(solution)/shard_map/pallas_call | solution.py:254
  59.6 2.0 %collective-permute-done.8.in_ref = bf16[4,528,128]{2,1,0:T(8,128)(2,1)S(1)} collective-permute-done((bf16[4,528,128]{2,1,0:T(8,128)(2,1)S(1)}, bf16[4,528,128]{2,1,0:T(8,128)(2,1)S(1)}, u32[]{:S(2)}, u32[]{:S(2)}) %collective-permute-start.8) | collective-permute-done | bytes 540704 | tf_op jit(solution)/shard_map/ppermute | solution.py:462
  61.5 1.0 %shard_map.91 = bf16[4,528,128]{2,1,0:T(8,128)(2,1)S(1)} custom-call(bf16[4,528,128]{2,1,0:T(8,128)(2,1)S(1)} %collective-permute-done.8.in_ref, f32[4,512,128]{2,1,0:T(8,128)S(1)} %get-tuple-element.66.acc_ref, bf16[4,16,128]{2,1,0:T(8,128)(2,1)S(1)} %get-tuple-element.67.stat_ref), custom_call_target="tpu_custom_call" | custom-call | flops 1605632 | bytes 3211264 | tf_op jit(solution)/shard_map/pallas_call | solution.py:389
  62.5 1.6 %collective-permute-start.10 = (bf16[4,528,128]{2,1,0:T(8,128)(2,1)S(1)}, bf16[4,528,128]{2,1,0:T(8,128)(2,1)S(1)}, u32[]{:S(2)}, u32[]{:S(2)}) collective-permute-start(bf16[4,528,128]{2,1,0:T(8,128)(2,1)S(1)} %shard_map.91), channel_id=1, source_target_pairs={{0,4},{4,8},{8,12},{12,14},{14,10},{10,6},{6,2},{2,0},{1,3},{5,1},... | collective-permute-start | bytes 1622024 | tf_op jit(solution)/shard_map/ppermute | solution.py:462
  64.2 1.8 %shard_map.92 = (f32[2,512,128]{2,1,0:T(8,128)S(1)}, bf16[2,16,128]{2,1,0:T(8,128)(2,1)S(1)}) custom-call(s32[1,128]{1,0:T(1,128)S(1)} %fusion.4.refs_0_, bf16[2064,128]{1,0:T(8,128)(2,1)S(1)} %shard_map.88.refs_1_, bf16[2,64,512]{2,1,0:T(8,128)(2,1)S(1)} %bitcast.4, bf16[32,2,64,512]{3,2,1,0:T(8,128)(2,1)S(1)} %copy-done.4), custom_call_target="tpu_custom_call" | custom-call | flops 536870912 | bytes 1310720 | tf_op jit(solution)/shard_map/pallas_call | solution.py:254
  65.9 1.3 %collective-permute-done.11.refs_1_ = bf16[2064,128]{1,0:T(8,128)(2,1)S(1)} collective-permute-done((bf16[2064,128]{1,0:T(8,128)(2,1)S(1)}, bf16[2064,128]{1,0:T(8,128)(2,1)S(1)}, u32[]{:S(2)}, u32[]{:S(2)}) %collective-permute-start.11) | collective-permute-done | bytes 528416 | tf_op jit(solution)/shard_map/ppermute | solution.py:462
  67.2 1.6 %collective-permute-start.13 = (bf16[2064,128]{1,0:T(8,128)(2,1)S(1)}, bf16[2064,128]{1,0:T(8,128)(2,1)S(1)}, u32[]{:S(2)}, u32[]{:S(2)}) collective-permute-start(bf16[2064,128]{1,0:T(8,128)(2,1)S(1)} %collective-permute-done.11.refs_1_), channel_id=1, source_target_pairs={{0,4},{4,8},{8,12},{12,14},{14,10},{10,6},{6,2},{2,0},{1,3},{5,1},... | collective-permute-start | bytes 1585160 | tf_op jit(solution)/shard_map/ppermute | solution.py:462
  68.8 2.5 %collective-permute-start.14 = (bf16[1,2,64,512]{3,2,1,0:T(8,128)(2,1)S(1)}, bf16[1,2,64,512]{3,2,1,0:T(8,128)(2,1)S(1)}, u32[]{:S(2)}, u32[]{:S(2)}) collective-permute-start(bf16[1,2,64,512]{3,2,1,0:T(8,128)(2,1)S(1)} %copy-done.5), channel_id=1, source_target_pairs={{8,0},{10,2},{12,4},{14,6},{0,8},{2,10},{4,12},{6,14},{9,1},{11,3}... | collective-permute-start | bytes 393224 | tf_op jit(solution)/shard_map/ppermute | solution.py:27
  71.3 2.2 %shard_map.93 = (f32[4,512,128]{2,1,0:T(8,128)S(1)}, bf16[4,16,128]{2,1,0:T(8,128)(2,1)S(1)}) custom-call(s32[1,128]{1,0:T(1,128)S(1)} %fusion.6.refs_0_.far_ref, bf16[2064,128]{1,0:T(8,128)(2,1)S(1)} %collective-permute-done.11.refs_1_, bf16[32,2,64,512]{3,2,1,0:T(8,128)(2,1)S(1)} %copy-done.4), custom_call_target="tpu_custom_call" | custom-call | flops 1 | bytes 1 | tf_op jit(solution)/shard_map/pallas_call | solution.py:254
  73.5 0.0 collective-permute-done.10.in_ref
  73.6 0.6 shard_map.94
  74.2 3.0 %collective-permute-start.15 = (bf16[2,528,128]{2,1,0:T(8,128)(2,1)S(1)}, bf16[2,528,128]{2,1,0:T(8,128)(2,1)S(1)}, u32[]{:S(2)}, u32[]{:S(2)}) collective-permute-start(bf16[2,528,128]{2,1,0:T(8,128)(2,1)S(1)} %shard_map.94), channel_id=1, source_target_pairs={{0,4},{4,8},{8,12},{12,14},{14,10},{10,6},{6,2},{2,0},{1,3},{5,1},... | collective-permute-start | bytes 811016 | tf_op jit(solution)/shard_map/ppermute | solution.py:462
  77.2 0.6 shard_map.95
  77.8 2.5 %collective-permute-start.12 = (bf16[2,528,128]{2,1,0:T(8,128)(2,1)S(1)}, bf16[2,528,128]{2,1,0:T(8,128)(2,1)S(1)}, u32[]{:S(2)}, u32[]{:S(2)}) collective-permute-start(bf16[2,528,128]{2,1,0:T(8,128)(2,1)S(1)} %shard_map.95), channel_id=1, source_target_pairs={{0,4},{4,8},{8,12},{12,14},{14,10},{10,6},{6,2},{2,0},{1,3},{5,1},... | collective-permute-start | bytes 811016 | tf_op jit(solution)/shard_map/ppermute | solution.py:462
  80.3 0.0 collective-permute-done.13.refs_1_
  80.3 2.2 %shard_map.96 = (f32[4,512,128]{2,1,0:T(8,128)S(1)}, bf16[4,16,128]{2,1,0:T(8,128)(2,1)S(1)}) custom-call(s32[1,128]{1,0:T(1,128)S(1)} %fusion.7.refs_0_, bf16[2064,128]{1,0:T(8,128)(2,1)S(1)} %collective-permute-done.13.refs_1_, bf16[32,2,64,512]{3,2,1,0:T(8,128)(2,1)S(1)} %copy-done.4), custom_call_target="tpu_custom_call" | custom-call | flops 8589934592 | bytes 33554432 | tf_op jit(solution)/shard_map/pallas_call | solution.py:254
  82.6 0.0 collective-permute-done.14.page_ref
  82.6 0.9 collective-permute-done.15.in_ref
  83.5 0.6 shard_map.97
  84.1 4.4 %collective-permute-start.17 = (bf16[2,528,128]{2,1,0:T(8,128)(2,1)S(1)}, bf16[2,528,128]{2,1,0:T(8,128)(2,1)S(1)}, u32[]{:S(2)}, u32[]{:S(2)}) collective-permute-start(bf16[2,528,128]{2,1,0:T(8,128)(2,1)S(1)} %shard_map.97), channel_id=1, source_target_pairs={{0,4},{4,8},{8,12},{12,14},{14,10},{10,6},{6,2},{2,0},{1,3},{5,1},... | collective-permute-start | bytes 811016 | tf_op jit(solution)/shard_map/ppermute | solution.py:462
  88.6 0.0 collective-permute-done.12.in_ref
  88.6 0.6 shard_map.98
  89.2 2.5 %collective-permute-start.16 = (bf16[2,528,128]{2,1,0:T(8,128)(2,1)S(1)}, bf16[2,528,128]{2,1,0:T(8,128)(2,1)S(1)}, u32[]{:S(2)}, u32[]{:S(2)}) collective-permute-start(bf16[2,528,128]{2,1,0:T(8,128)(2,1)S(1)} %shard_map.98), channel_id=1, source_target_pairs={{0,4},{4,8},{8,12},{12,14},{14,10},{10,6},{6,2},{2,0},{1,3},{5,1},... | collective-permute-start | bytes 811016 | tf_op jit(solution)/shard_map/ppermute | solution.py:462
  91.8 1.2 %shard_map.99 = bf16[32,2,64,512]{3,2,1,0:T(8,128)(2,1)} custom-call(s32[1]{0:T(128)} %bitcast.1.me_ref, s32[1]{0:T(128)} %bitcast.2.core_ref, s32[1,128]{1,0:T(1,128)S(1)} %fusion.1.refs_0_.near_ref, s32[1,128]{1,0:T(1,128)S(1)} %fusion.6.refs_0_.far_ref, ...), custom_call_target="tpu_custom_call", output_to_operand_aliasing={{}: (5, {})} | custom-call | flops 1 | bytes 1 | tf_op jit(solution)/shard_map/pallas_call | solution.py:292
  93.0 0.0 collective-permute-done.17.in_ref
  93.0 1.3 %shard_map.100.refs_0_ = bf16[1,64,4096]{2,1,0:T(8,128)(2,1)} custom-call(bf16[2,528,128]{2,1,0:T(8,128)(2,1)S(1)} %collective-permute-done.17.in_ref, f32[2,512,128]{2,1,0:T(8,128)S(1)} %get-tuple-element.63.acc_ref, bf16[2,16,128]{2,1,0:T(8,128)(2,1)S(1)} %get-tuple-element.64.stat_ref), custom_call_target="tpu_custom_call" | custom-call | tf_op jit(solution)/shard_map/pallas_call | solution.py:373
  94.3 1.5 %collective-permute-done.16.in_ref = bf16[2,528,128]{2,1,0:T(8,128)(2,1)S(1)} collective-permute-done((bf16[2,528,128]{2,1,0:T(8,128)(2,1)S(1)}, bf16[2,528,128]{2,1,0:T(8,128)(2,1)S(1)}, u32[]{:S(2)}, u32[]{:S(2)}) %collective-permute-start.16) | collective-permute-done | bytes 270368 | tf_op jit(solution)/shard_map/ppermute | solution.py:462
  95.7 1.3 %shard_map.101 = bf16[1,64,4096]{2,1,0:T(8,128)(2,1)} custom-call(bf16[2,528,128]{2,1,0:T(8,128)(2,1)S(1)} %collective-permute-done.16.in_ref, f32[2,512,128]{2,1,0:T(8,128)S(1)} %get-tuple-element.70.acc_ref, bf16[2,16,128]{2,1,0:T(8,128)(2,1)S(1)} %get-tuple-element.71.stat_ref, ...), custom_call_target="tpu_custom_call", output_to_operand_aliasing={{}: (3, {})} | custom-call | tf_op jit(solution)/shard_map/pallas_call | solution.py:373
  (21 shorter events, 0.1 us)
Async XLA Ops:
  0.6 10.4 %collective-permute-start = (bf16[1,64,4096]{2,1,0:T(8,128)(2,1)}, bf16[1,64,4096]{2,1,0:T(8,128)(2,1)S(1)}, u32[]{:S(2)}, u32[]{:S(2)}) collective-permute-start(bf16[1,64,4096]{2,1,0:T(8,128)(2,1)} %q_ref), channel_id=1, source_target_pairs={{0,4},{4,8},{8,12},{12,14},{14,10},{10,6},{6,2},{2,0},{1,3},{5,1},... | collective-permute-start | bytes 1572872 | tf_op jit(solution)/shard_map/ppermute | solution.py:462
  5.0 0.7 copy-start.7
  5.9 5.1 %collective-permute-start.1 = (bf16[16,128]{1,0:T(8,128)(2,1)S(1)}, bf16[16,128]{1,0:T(8,128)(2,1)S(1)}, u32[]{:S(2)}, u32[]{:S(2)}) collective-permute-start(bf16[16,128]{1,0:T(8,128)(2,1)S(1)} %shard_map.77.lists_ref), channel_id=1, source_target_pairs={{0,4},{4,8},{8,12},{12,14},{14,10},{10,6},{6,2},{2,0},{1,3},{5,1},... | collective-permute-start | bytes 12296 | tf_op jit(solution)/shard_map/ppermute | solution.py:462
  7.5 2.2 %copy-start = (bf16[32,2,64,512]{3,2,1,0:T(8,128)(2,1)S(1)}, bf16[32,2,64,512]{3,2,1,0:T(8,128)(2,1)}, u32[]{:S(2)}) copy-start(bf16[32,2,64,512]{3,2,1,0:T(8,128)(2,1)} %refs_2_.13) | copy-start | bytes 12582916
  11.2 9.3 %collective-permute-start.3 = (bf16[2064,128]{1,0:T(8,128)(2,1)S(1)}, bf16[2064,128]{1,0:T(8,128)(2,1)S(1)}, u32[]{:S(2)}, u32[]{:S(2)}) collective-permute-start(bf16[2064,128]{1,0:T(8,128)(2,1)S(1)} %shard_map.79.refs_1_), channel_id=1, source_target_pairs={{0,4},{4,8},{8,12},{12,14},{14,10},{10,6},{6,2},{2,0},{1,3},{5,1},... | collective-permute-start | bytes 1585160 | tf_op jit(solution)/shard_map/ppermute | solution.py:462
  13.3 2.2 %copy-start.1 = (bf16[32,2,64,512]{3,2,1,0:T(8,128)(2,1)S(1)}, bf16[32,2,64,512]{3,2,1,0:T(8,128)(2,1)}, u32[]{:S(2)}) copy-start(bf16[32,2,64,512]{3,2,1,0:T(8,128)(2,1)} %refs_2_.13) | copy-start | bytes 12582916
  15.5 7.0 %copy-start.2 = (bf16[32,2,64,512]{3,2,1,0:T(8,128)(2,1)S(1)}, bf16[32,2,64,512]{3,2,1,0:T(8,128)(2,1)}, u32[]{:S(2)}) copy-start(bf16[32,2,64,512]{3,2,1,0:T(8,128)(2,1)} %refs_2_.13) | copy-start | bytes 12582916
  17.8 9.4 %collective-permute-start.2 = (bf16[4,528,128]{2,1,0:T(8,128)(2,1)S(1)}, bf16[4,528,128]{2,1,0:T(8,128)(2,1)S(1)}, u32[]{:S(2)}, u32[]{:S(2)}) collective-permute-start(bf16[4,528,128]{2,1,0:T(8,128)(2,1)S(1)} %shard_map.81), channel_id=1, source_target_pairs={{0,4},{4,8},{8,12},{12,14},{14,10},{10,6},{6,2},{2,0},{1,3},{5,1},... | collective-permute-start | bytes 1622024 | tf_op jit(solution)/shard_map/ppermute | solution.py:462
  20.4 12.4 %collective-permute-start.5 = (bf16[2064,128]{1,0:T(8,128)(2,1)S(1)}, bf16[2064,128]{1,0:T(8,128)(2,1)S(1)}, u32[]{:S(2)}, u32[]{:S(2)}) collective-permute-start(bf16[2064,128]{1,0:T(8,128)(2,1)S(1)} %collective-permute-done.3.refs_1_), channel_id=1, source_target_pairs={{0,4},{4,8},{8,12},{12,14},{14,10},{10,6},{6,2},{2,0},{1,3},{5,1},... | collective-permute-start | bytes 1585160 | tf_op jit(solution)/shard_map/ppermute | solution.py:462
  28.2 10.5 %collective-permute-start.4 = (bf16[4,528,128]{2,1,0:T(8,128)(2,1)S(1)}, bf16[4,528,128]{2,1,0:T(8,128)(2,1)S(1)}, u32[]{:S(2)}, u32[]{:S(2)}) collective-permute-start(bf16[4,528,128]{2,1,0:T(8,128)(2,1)S(1)} %shard_map.83), channel_id=1, source_target_pairs={{0,4},{4,8},{8,12},{12,14},{14,10},{10,6},{6,2},{2,0},{1,3},{5,1},... | collective-permute-start | bytes 1622024 | tf_op jit(solution)/shard_map/ppermute | solution.py:462
  32.8 11.5 %collective-permute-start.7 = (bf16[2064,128]{1,0:T(8,128)(2,1)S(1)}, bf16[2064,128]{1,0:T(8,128)(2,1)S(1)}, u32[]{:S(2)}, u32[]{:S(2)}) collective-permute-start(bf16[2064,128]{1,0:T(8,128)(2,1)S(1)} %collective-permute-done.5.refs_1_), channel_id=1, source_target_pairs={{0,4},{4,8},{8,12},{12,14},{14,10},{10,6},{6,2},{2,0},{1,3},{5,1},... | collective-permute-start | bytes 1585160 | tf_op jit(solution)/shard_map/ppermute | solution.py:462
  38.6 14.5 %copy-start.6 = (bf16[1,64,4096]{2,1,0:T(8,128)(2,1)S(1)}, bf16[1,64,4096]{2,1,0:T(8,128)(2,1)}, u32[]{:S(2)}) copy-start(bf16[1,64,4096]{2,1,0:T(8,128)(2,1)} %q_ref) | copy-start | bytes 1572868
  38.6 14.6 %copy-start.5 = (bf16[1,2,64,512]{3,2,1,0:T(8,128)(2,1)S(1)}, bf16[1,2,64,512]{3,2,1,0:T(8,128)(2,1)}, u32[]{:S(2)}) copy-start(bf16[1,2,64,512]{3,2,1,0:T(8,128)(2,1)} %param.7) | copy-start | bytes 393220
  39.6 10.7 %collective-permute-start.6 = (bf16[4,528,128]{2,1,0:T(8,128)(2,1)S(1)}, bf16[4,528,128]{2,1,0:T(8,128)(2,1)S(1)}, u32[]{:S(2)}, u32[]{:S(2)}) collective-permute-start(bf16[4,528,128]{2,1,0:T(8,128)(2,1)S(1)} %shard_map.85), channel_id=1, source_target_pairs={{0,4},{4,8},{8,12},{12,14},{14,10},{10,6},{6,2},{2,0},{1,3},{5,1},... | collective-permute-start | bytes 1622024 | tf_op jit(solution)/shard_map/ppermute | solution.py:462
  44.3 11.5 %collective-permute-start.9 = (bf16[2064,128]{1,0:T(8,128)(2,1)S(1)}, bf16[2064,128]{1,0:T(8,128)(2,1)S(1)}, u32[]{:S(2)}, u32[]{:S(2)}) collective-permute-start(bf16[2064,128]{1,0:T(8,128)(2,1)S(1)} %collective-permute-done.7.refs_1_), channel_id=1, source_target_pairs={{0,4},{4,8},{8,12},{12,14},{14,10},{10,6},{6,2},{2,0},{1,3},{5,1},... | collective-permute-start | bytes 1585160 | tf_op jit(solution)/shard_map/ppermute | solution.py:462
  45.9 2.2 %copy-start.3 = (bf16[32,2,64,512]{3,2,1,0:T(8,128)(2,1)S(1)}, bf16[32,2,64,512]{3,2,1,0:T(8,128)(2,1)}, u32[]{:S(2)}) copy-start(bf16[32,2,64,512]{3,2,1,0:T(8,128)(2,1)} %refs_2_.13) | copy-start | bytes 12582916
  48.1 5.2 %copy-start.4 = (bf16[32,2,64,512]{3,2,1,0:T(8,128)(2,1)S(1)}, bf16[32,2,64,512]{3,2,1,0:T(8,128)(2,1)}, u32[]{:S(2)}) copy-start(bf16[32,2,64,512]{3,2,1,0:T(8,128)(2,1)} %refs_2_.13) | copy-start | bytes 12582916
  51.3 10.2 %collective-permute-start.8 = (bf16[4,528,128]{2,1,0:T(8,128)(2,1)S(1)}, bf16[4,528,128]{2,1,0:T(8,128)(2,1)S(1)}, u32[]{:S(2)}, u32[]{:S(2)}) collective-permute-start(bf16[4,528,128]{2,1,0:T(8,128)(2,1)S(1)} %shard_map.87), channel_id=1, source_target_pairs={{0,4},{4,8},{8,12},{12,14},{14,10},{10,6},{6,2},{2,0},{1,3},{5,1},... | collective-permute-start | bytes 1622024 | tf_op jit(solution)/shard_map/ppermute | solution.py:462
  55.8 11.5 %collective-permute-start.11 = (bf16[2064,128]{1,0:T(8,128)(2,1)S(1)}, bf16[2064,128]{1,0:T(8,128)(2,1)S(1)}, u32[]{:S(2)}, u32[]{:S(2)}) collective-permute-start(bf16[2064,128]{1,0:T(8,128)(2,1)S(1)} %collective-permute-done.9.refs_1_), channel_id=1, source_target_pairs={{0,4},{4,8},{8,12},{12,14},{14,10},{10,6},{6,2},{2,0},{1,3},{5,1},... | collective-permute-start | bytes 1585160 | tf_op jit(solution)/shard_map/ppermute | solution.py:462
  62.5 11.0 %collective-permute-start.10 = (bf16[4,528,128]{2,1,0:T(8,128)(2,1)S(1)}, bf16[4,528,128]{2,1,0:T(8,128)(2,1)S(1)}, u32[]{:S(2)}, u32[]{:S(2)}) collective-permute-start(bf16[4,528,128]{2,1,0:T(8,128)(2,1)S(1)} %shard_map.91), channel_id=1, source_target_pairs={{0,4},{4,8},{8,12},{12,14},{14,10},{10,6},{6,2},{2,0},{1,3},{5,1},... | collective-permute-start | bytes 1622024 | tf_op jit(solution)/shard_map/ppermute | solution.py:462
  67.2 13.1 %collective-permute-start.13 = (bf16[2064,128]{1,0:T(8,128)(2,1)S(1)}, bf16[2064,128]{1,0:T(8,128)(2,1)S(1)}, u32[]{:S(2)}, u32[]{:S(2)}) collective-permute-start(bf16[2064,128]{1,0:T(8,128)(2,1)S(1)} %collective-permute-done.11.refs_1_), channel_id=1, source_target_pairs={{0,4},{4,8},{8,12},{12,14},{14,10},{10,6},{6,2},{2,0},{1,3},{5,1},... | collective-permute-start | bytes 1585160 | tf_op jit(solution)/shard_map/ppermute | solution.py:462
  68.8 13.8 %collective-permute-start.14 = (bf16[1,2,64,512]{3,2,1,0:T(8,128)(2,1)S(1)}, bf16[1,2,64,512]{3,2,1,0:T(8,128)(2,1)S(1)}, u32[]{:S(2)}, u32[]{:S(2)}) collective-permute-start(bf16[1,2,64,512]{3,2,1,0:T(8,128)(2,1)S(1)} %copy-done.5), channel_id=1, source_target_pairs={{8,0},{10,2},{12,4},{14,6},{0,8},{2,10},{4,12},{6,14},{9,1},{11,3}... | collective-permute-start | bytes 393224 | tf_op jit(solution)/shard_map/ppermute | solution.py:27
  74.2 9.3 %collective-permute-start.15 = (bf16[2,528,128]{2,1,0:T(8,128)(2,1)S(1)}, bf16[2,528,128]{2,1,0:T(8,128)(2,1)S(1)}, u32[]{:S(2)}, u32[]{:S(2)}) collective-permute-start(bf16[2,528,128]{2,1,0:T(8,128)(2,1)S(1)} %shard_map.94), channel_id=1, source_target_pairs={{0,4},{4,8},{8,12},{12,14},{14,10},{10,6},{6,2},{2,0},{1,3},{5,1},... | collective-permute-start | bytes 811016 | tf_op jit(solution)/shard_map/ppermute | solution.py:462
  77.8 10.8 %collective-permute-start.12 = (bf16[2,528,128]{2,1,0:T(8,128)(2,1)S(1)}, bf16[2,528,128]{2,1,0:T(8,128)(2,1)S(1)}, u32[]{:S(2)}, u32[]{:S(2)}) collective-permute-start(bf16[2,528,128]{2,1,0:T(8,128)(2,1)S(1)} %shard_map.95), channel_id=1, source_target_pairs={{0,4},{4,8},{8,12},{12,14},{14,10},{10,6},{6,2},{2,0},{1,3},{5,1},... | collective-permute-start | bytes 811016 | tf_op jit(solution)/shard_map/ppermute | solution.py:462
  84.1 8.8 %collective-permute-start.17 = (bf16[2,528,128]{2,1,0:T(8,128)(2,1)S(1)}, bf16[2,528,128]{2,1,0:T(8,128)(2,1)S(1)}, u32[]{:S(2)}, u32[]{:S(2)}) collective-permute-start(bf16[2,528,128]{2,1,0:T(8,128)(2,1)S(1)} %shard_map.97), channel_id=1, source_target_pairs={{0,4},{4,8},{8,12},{12,14},{14,10},{10,6},{6,2},{2,0},{1,3},{5,1},... | collective-permute-start | bytes 811016 | tf_op jit(solution)/shard_map/ppermute | solution.py:462
  89.2 6.5 %collective-permute-start.16 = (bf16[2,528,128]{2,1,0:T(8,128)(2,1)S(1)}, bf16[2,528,128]{2,1,0:T(8,128)(2,1)S(1)}, u32[]{:S(2)}, u32[]{:S(2)}) collective-permute-start(bf16[2,528,128]{2,1,0:T(8,128)(2,1)S(1)} %shard_map.98), channel_id=1, source_target_pairs={{0,4},{4,8},{8,12},{12,14},{14,10},{10,6},{6,2},{2,0},{1,3},{5,1},... | collective-permute-start | bytes 811016 | tf_op jit(solution)/shard_map/ppermute | solution.py:462

commit v23 on v21

--- a/solution.py
+++ b/solution.py
@@ -502,7 +502,7 @@
             part, = attend(sizes, jobs, lists[step], [came], kv_pages, cost=cost)
         if step == 1:
             blocks = [packed(part)]
-        elif step < stores - 2:
+        elif step < stores - 1:
             blocks = [merged(after(partial[0], part), part, 0, 0, heads)]
         else:
             part = after(part, arrived) if step == stores - 1 else part

time: 97.5 us -> 100 us (1.026)
  waiting for transfers between devices: 18 us -> 23.7 us
  starting transfers between devices: 38.5 us -> 36 us
    ppermute x17 -> x16, waiting for transfers between devices: 18 us -> 23.7 us  [onward(): return lax.ppermute(x, ('store', 'tensor'), route)]
    ppermute x17 -> x16, starting transfers between devices: 36 us -> 33.4 us  [onward(): return lax.ppermute(x, ('store', 'tensor'), route)]
    pallas_call x11 -> x10, Pallas kernels: 6.7 us -> 6.42 us  [call(): pl.pallas_call(kernel, out_shape=shape, in_specs=[VMEM] * len(args), out_...]
  transfers between devices with their start and end apart: 18 -> 17, of which waited for: 11 -> 12; matrix products, arithmetic and copies ran while one was open for 0% -> 0% of each run, Pallas kernels for 31% -> 29%
where the time goes in v23:
time: 100 us
  starting transfers between devices  36 us (36%)
  Pallas kernels  30.8 us (31%)
  waiting for transfers between devices  23.7 us (24%)
  local copies, waits for them, and re-layouts  7.23 us (7%)
  between operations  2.31 us (2%)
    ppermute x16, starting transfers between devices, onward(): return lax.ppermute(x, ('store', 'tensor'), route)  33.4 us
    ppermute x16, waiting for transfers between devices, onward(): return lax.ppermute(x, ('store', 'tensor'), route)  23.7 us
    pallas_call x9, Pallas kernels, attend(): pl.pallas_call(functools.partial(attend_kernel, sizes + (count,), jobs, o...  20.3 us
    unnamed x16, local copies, waits for them, and re-layouts  7.23 us
    pallas_call x10, Pallas kernels, call(): pl.pallas_call(kernel, out_shape=shape, in_specs=[VMEM] * len(args), out_...  6.42 us
    ppermute x1, starting transfers between devices, shifted(): return lax.ppermute(block, axis, route)  2.53 us
    pallas_call x2, Pallas kernels, finish(): pl.pallas_call(functools.partial(final_kernel, suffix, first), out_shape=...  2.53 us
  transfers between devices with their start and end apart: 17, of which 12 were waited for; matrix products, arithmetic and copies ran while one was open for 0% of the time, Pallas kernels for 29%

profile of v23, /device:TPU:0, one launch (start us, length us, event | category | flops | bytes accessed | tf_op | source)
XLA Modules:
  0.0 100.0 jit_solution(8063469138568378165)
XLA Ops:
  0.6 3.1 %collective-permute-start = (bf16[1,64,4096]{2,1,0:T(8,128)(2,1)}, bf16[1,64,4096]{2,1,0:T(8,128)(2,1)S(1)}, u32[]{:S(2)}, u32[]{:S(2)}) collective-permute-start(bf16[1,64,4096]{2,1,0:T(8,128)(2,1)} %q_ref), channel_id=1, source_target_pairs={{0,4},{4,8},{8,12},{12,14},{14,10},{10,6},{6,2},{2,0},{1,3},{5,1},... | collective-permute-start | bytes 1572872 | tf_op jit(solution)/shard_map/ppermute | solution.py:462
  5.0 0.0 copy-start.7
  5.0 0.6 copy-done.7
  5.7 0.3 shard_map.77.lists_ref
  5.9 1.6 %collective-permute-start.1 = (bf16[16,128]{1,0:T(8,128)(2,1)S(1)}, bf16[16,128]{1,0:T(8,128)(2,1)S(1)}, u32[]{:S(2)}, u32[]{:S(2)}) collective-permute-start(bf16[16,128]{1,0:T(8,128)(2,1)S(1)} %shard_map.77.lists_ref), channel_id=1, source_target_pairs={{0,4},{4,8},{8,12},{12,14},{14,10},{10,6},{6,2},{2,0},{1,3},{5,1},... | collective-permute-start | bytes 12296 | tf_op jit(solution)/shard_map/ppermute | solution.py:462
  7.5 2.2 %copy-done = bf16[32,2,64,512]{3,2,1,0:T(8,128)(2,1)S(1)} copy-done((bf16[32,2,64,512]{3,2,1,0:T(8,128)(2,1)S(1)}, bf16[32,2,64,512]{3,2,1,0:T(8,128)(2,1)}, u32[]{:S(2)}) %copy-start) | copy-done | bytes 4194328
  9.7 1.3 %collective-permute-done.q_ref = bf16[1,64,4096]{2,1,0:T(8,128)(2,1)S(1)} collective-permute-done((bf16[1,64,4096]{2,1,0:T(8,128)(2,1)}, bf16[1,64,4096]{2,1,0:T(8,128)(2,1)S(1)}, u32[]{:S(2)}, u32[]{:S(2)}) %collective-permute-start) | collective-permute-done | bytes 524320 | tf_op jit(solution)/shard_map/ppermute | solution.py:462
  11.0 0.0 collective-permute-done.1.lists_ref
  11.1 0.1 shard_map.79.refs_1_
  11.2 2.1 %collective-permute-start.3 = (bf16[2064,128]{1,0:T(8,128)(2,1)S(1)}, bf16[2064,128]{1,0:T(8,128)(2,1)S(1)}, u32[]{:S(2)}, u32[]{:S(2)}) collective-permute-start(bf16[2064,128]{1,0:T(8,128)(2,1)S(1)} %shard_map.79.refs_1_), channel_id=1, source_target_pairs={{0,4},{4,8},{8,12},{12,14},{14,10},{10,6},{6,2},{2,0},{1,3},{5,1},... | collective-permute-start | bytes 1585160 | tf_op jit(solution)/shard_map/ppermute | solution.py:462
  13.3 2.2 %copy-done.1 = bf16[32,2,64,512]{3,2,1,0:T(8,128)(2,1)S(1)} copy-done((bf16[32,2,64,512]{3,2,1,0:T(8,128)(2,1)S(1)}, bf16[32,2,64,512]{3,2,1,0:T(8,128)(2,1)}, u32[]{:S(2)}) %copy-start.1) | copy-done | bytes 4194328
  15.5 2.2 %shard_map.80 = (f32[4,512,128]{2,1,0:T(8,128)S(1)}, bf16[4,16,128]{2,1,0:T(8,128)(2,1)S(1)}) custom-call(s32[1,128]{1,0:T(1,128)S(1)} %fusion.refs_0_, bf16[2064,128]{1,0:T(8,128)(2,1)S(1)} %shard_map.79.refs_1_, bf16[32,2,64,512]{3,2,1,0:T(8,128)(2,1)S(1)} %copy-done.1), custom_call_target="tpu_custom_call" | custom-call | flops 1073741824 | bytes 2621440 | tf_op jit(solution)/shard_map/pallas_call | solution.py:254
  17.7 0.1 shard_map.81
  17.8 1.6 %collective-permute-start.2 = (bf16[4,528,128]{2,1,0:T(8,128)(2,1)S(1)}, bf16[4,528,128]{2,1,0:T(8,128)(2,1)S(1)}, u32[]{:S(2)}, u32[]{:S(2)}) collective-permute-start(bf16[4,528,128]{2,1,0:T(8,128)(2,1)S(1)} %shard_map.81), channel_id=1, source_target_pairs={{0,4},{4,8},{8,12},{12,14},{14,10},{10,6},{6,2},{2,0},{1,3},{5,1},... | collective-permute-start | bytes 1622024 | tf_op jit(solution)/shard_map/ppermute | solution.py:462
  19.4 1.0 %collective-permute-done.3.refs_1_ = bf16[2064,128]{1,0:T(8,128)(2,1)S(1)} collective-permute-done((bf16[2064,128]{1,0:T(8,128)(2,1)S(1)}, bf16[2064,128]{1,0:T(8,128)(2,1)S(1)}, u32[]{:S(2)}, u32[]{:S(2)}) %collective-permute-start.3) | collective-permute-done | bytes 528416 | tf_op jit(solution)/shard_map/ppermute | solution.py:462
  20.4 2.1 %collective-permute-start.5 = (bf16[2064,128]{1,0:T(8,128)(2,1)S(1)}, bf16[2064,128]{1,0:T(8,128)(2,1)S(1)}, u32[]{:S(2)}, u32[]{:S(2)}) collective-permute-start(bf16[2064,128]{1,0:T(8,128)(2,1)S(1)} %collective-permute-done.3.refs_1_), channel_id=1, source_target_pairs={{0,4},{4,8},{8,12},{12,14},{14,10},{10,6},{6,2},{2,0},{1,3},{5,1},... | collective-permute-start | bytes 1585160 | tf_op jit(solution)/shard_map/ppermute | solution.py:462
  22.5 0.0 copy-done.2
  22.5 2.7 %shard_map.82 = (f32[4,512,128]{2,1,0:T(8,128)S(1)}, bf16[4,16,128]{2,1,0:T(8,128)(2,1)S(1)}, bf16[32,2,64,512]{3,2,1,0:T(8,128)(2,1)}) custom-call(s32[1,128]{1,0:T(1,128)S(1)} %fusion.1.refs_0_.near_ref, bf16[2064,128]{1,0:T(8,128)(2,1)S(1)} %collective-permute-done.3.refs_1_, bf16[32,2,64,512]{3,2,1,0:T(8,128)(2,1)S(1)} %copy-done.2), custom_call_target="tpu_custom_call" | custom-call | flops 1073741824 | bytes 2621440 | tf_op jit(solution)/shard_map/pallas_call | solution.py:254
  25.3 1.9 %collective-permute-done.2.in_ref = bf16[4,528,128]{2,1,0:T(8,128)(2,1)S(1)} collective-permute-done((bf16[4,528,128]{2,1,0:T(8,128)(2,1)S(1)}, bf16[4,528,128]{2,1,0:T(8,128)(2,1)S(1)}, u32[]{:S(2)}, u32[]{:S(2)}) %collective-permute-start.2) | collective-permute-done | bytes 540704 | tf_op jit(solution)/shard_map/ppermute | solution.py:462
  27.2 1.0 shard_map.83
  28.2 1.6 %collective-permute-start.4 = (bf16[4,528,128]{2,1,0:T(8,128)(2,1)S(1)}, bf16[4,528,128]{2,1,0:T(8,128)(2,1)S(1)}, u32[]{:S(2)}, u32[]{:S(2)}) collective-permute-start(bf16[4,528,128]{2,1,0:T(8,128)(2,1)S(1)} %shard_map.83), channel_id=1, source_target_pairs={{0,4},{4,8},{8,12},{12,14},{14,10},{10,6},{6,2},{2,0},{1,3},{5,1},... | collective-permute-start | bytes 1622024 | tf_op jit(solution)/shard_map/ppermute | solution.py:462
  29.8 3.0 %collective-permute-done.5.refs_1_ = bf16[2064,128]{1,0:T(8,128)(2,1)S(1)} collective-permute-done((bf16[2064,128]{1,0:T(8,128)(2,1)S(1)}, bf16[2064,128]{1,0:T(8,128)(2,1)S(1)}, u32[]{:S(2)}, u32[]{:S(2)}) %collective-permute-start.5) | collective-permute-done | bytes 528416 | tf_op jit(solution)/shard_map/ppermute | solution.py:462
  32.8 1.6 %collective-permute-start.7 = (bf16[2064,128]{1,0:T(8,128)(2,1)S(1)}, bf16[2064,128]{1,0:T(8,128)(2,1)S(1)}, u32[]{:S(2)}, u32[]{:S(2)}) collective-permute-start(bf16[2064,128]{1,0:T(8,128)(2,1)S(1)} %collective-permute-done.5.refs_1_), channel_id=1, source_target_pairs={{0,4},{4,8},{8,12},{12,14},{14,10},{10,6},{6,2},{2,0},{1,3},{5,1},... | collective-permute-start | bytes 1585160 | tf_op jit(solution)/shard_map/ppermute | solution.py:462
  34.4 2.2 %copy-done.3 = bf16[32,2,64,512]{3,2,1,0:T(8,128)(2,1)S(1)} copy-done((bf16[32,2,64,512]{3,2,1,0:T(8,128)(2,1)S(1)}, bf16[32,2,64,512]{3,2,1,0:T(8,128)(2,1)}, u32[]{:S(2)}) %copy-start.3) | copy-done | bytes 4194328
  36.6 2.9 %shard_map.84 = (f32[4,512,128]{2,1,0:T(8,128)S(1)}, bf16[4,16,128]{2,1,0:T(8,128)(2,1)S(1)}, bf16[32,2,64,512]{3,2,1,0:T(8,128)(2,1)}) custom-call(s32[1,128]{1,0:T(1,128)S(1)} %fusion.2.refs_0_, bf16[2064,128]{1,0:T(8,128)(2,1)S(1)} %collective-permute-done.5.refs_1_, bf16[32,2,64,512]{3,2,1,0:T(8,128)(2,1)S(1)} %copy-done.3, ...), custom_call_target="tpu_custom_call", output_to_operand_aliasing={{2}: (3, {})} | custom-call | flops 1073741824 | bytes 2621440 | tf_op jit(solution)/shard_map/pallas_call | solution.py:254
  39.6 0.0 collective-permute-done.4.in_ref
  39.6 1.0 shard_map.85
  40.6 1.6 %collective-permute-start.6 = (bf16[4,528,128]{2,1,0:T(8,128)(2,1)S(1)}, bf16[4,528,128]{2,1,0:T(8,128)(2,1)S(1)}, u32[]{:S(2)}, u32[]{:S(2)}) collective-permute-start(bf16[4,528,128]{2,1,0:T(8,128)(2,1)S(1)} %shard_map.85), channel_id=1, source_target_pairs={{0,4},{4,8},{8,12},{12,14},{14,10},{10,6},{6,2},{2,0},{1,3},{5,1},... | collective-permute-start | bytes 1622024 | tf_op jit(solution)/shard_map/ppermute | solution.py:462
  42.2 0.0 copy-done.6
  42.2 0.1 shard_map.86.refs_1_
  42.3 1.8 %shard_map.87 = (f32[2,512,128]{2,1,0:T(8,128)S(1)}, bf16[2,16,128]{2,1,0:T(8,128)(2,1)S(1)}) custom-call(s32[1,128]{1,0:T(1,128)S(1)} %fusion.3.refs_0_, bf16[2064,128]{1,0:T(8,128)(2,1)S(1)} %shard_map.86.refs_1_, bf16[2,64,512]{2,1,0:T(8,128)(2,1)S(1)} %bitcast.3, bf16[32,2,64,512]{3,2,1,0:T(8,128)(2,1)S(1)} %copy-done.4), custom_call_target="tpu_custom_call" | custom-call | flops 536870912 | bytes 1310720 | tf_op jit(solution)/shard_map/pallas_call | solution.py:254
  44.1 0.2 collective-permute-done.7.refs_1_
  44.3 1.6 %collective-permute-start.9 = (bf16[2064,128]{1,0:T(8,128)(2,1)S(1)}, bf16[2064,128]{1,0:T(8,128)(2,1)S(1)}, u32[]{:S(2)}, u32[]{:S(2)}) collective-permute-start(bf16[2064,128]{1,0:T(8,128)(2,1)S(1)} %collective-permute-done.7.refs_1_), channel_id=1, source_target_pairs={{0,4},{4,8},{8,12},{12,14},{14,10},{10,6},{6,2},{2,0},{1,3},{5,1},... | collective-permute-start | bytes 1585160 | tf_op jit(solution)/shard_map/ppermute | solution.py:462
  45.9 2.2 %shard_map.88 = (f32[4,512,128]{2,1,0:T(8,128)S(1)}, bf16[4,16,128]{2,1,0:T(8,128)(2,1)S(1)}) custom-call(s32[1,128]{1,0:T(1,128)S(1)} %fusion.4.refs_0_, bf16[2064,128]{1,0:T(8,128)(2,1)S(1)} %collective-permute-done.7.refs_1_, bf16[32,2,64,512]{3,2,1,0:T(8,128)(2,1)S(1)} %copy-done.4), custom_call_target="tpu_custom_call" | custom-call | flops 1073741824 | bytes 2621440 | tf_op jit(solution)/shard_map/pallas_call | solution.py:254
  48.1 2.0 %collective-permute-done.6.in_ref = bf16[4,528,128]{2,1,0:T(8,128)(2,1)S(1)} collective-permute-done((bf16[4,528,128]{2,1,0:T(8,128)(2,1)S(1)}, bf16[4,528,128]{2,1,0:T(8,128)(2,1)S(1)}, u32[]{:S(2)}, u32[]{:S(2)}) %collective-permute-start.6) | collective-permute-done | bytes 540704 | tf_op jit(solution)/shard_map/ppermute | solution.py:462
  50.1 1.0 shard_map.89
  51.1 1.8 %collective-permute-start.8 = (bf16[4,528,128]{2,1,0:T(8,128)(2,1)S(1)}, bf16[4,528,128]{2,1,0:T(8,128)(2,1)S(1)}, u32[]{:S(2)}, u32[]{:S(2)}) collective-permute-start(bf16[4,528,128]{2,1,0:T(8,128)(2,1)S(1)} %shard_map.89), channel_id=1, source_target_pairs={{0,4},{4,8},{8,12},{12,14},{14,10},{10,6},{6,2},{2,0},{1,3},{5,1},... | collective-permute-start | bytes 1622024 | tf_op jit(solution)/shard_map/ppermute | solution.py:462
  52.9 1.8 %shard_map.90 = (f32[2,512,128]{2,1,0:T(8,128)S(1)}, bf16[2,16,128]{2,1,0:T(8,128)(2,1)S(1)}) custom-call(s32[1,128]{1,0:T(1,128)S(1)} %fusion.3.refs_0_, bf16[2064,128]{1,0:T(8,128)(2,1)S(1)} %shard_map.86.refs_1_, bf16[2,64,512]{2,1,0:T(8,128)(2,1)S(1)} %bitcast.4, bf16[32,2,64,512]{3,2,1,0:T(8,128)(2,1)S(1)} %copy-done.4), custom_call_target="tpu_custom_call" | custom-call | flops 536870912 | bytes 1310720 | tf_op jit(solution)/shard_map/pallas_call | solution.py:254
  54.7 1.1 %collective-permute-done.9.refs_1_ = bf16[2064,128]{1,0:T(8,128)(2,1)S(1)} collective-permute-done((bf16[2064,128]{1,0:T(8,128)(2,1)S(1)}, bf16[2064,128]{1,0:T(8,128)(2,1)S(1)}, u32[]{:S(2)}, u32[]{:S(2)}) %collective-permute-start.9) | collective-permute-done | bytes 528416 | tf_op jit(solution)/shard_map/ppermute | solution.py:462
  55.8 1.6 %collective-permute-start.11 = (bf16[2064,128]{1,0:T(8,128)(2,1)S(1)}, bf16[2064,128]{1,0:T(8,128)(2,1)S(1)}, u32[]{:S(2)}, u32[]{:S(2)}) collective-permute-start(bf16[2064,128]{1,0:T(8,128)(2,1)S(1)} %collective-permute-done.9.refs_1_), channel_id=1, source_target_pairs={{0,4},{4,8},{8,12},{12,14},{14,10},{10,6},{6,2},{2,0},{1,3},{5,1},... | collective-permute-start | bytes 1585160 | tf_op jit(solution)/shard_map/ppermute | solution.py:462
  57.3 2.2 %shard_map.91 = (f32[4,512,128]{2,1,0:T(8,128)S(1)}, bf16[4,16,128]{2,1,0:T(8,128)(2,1)S(1)}) custom-call(s32[1,128]{1,0:T(1,128)S(1)} %fusion.5.refs_0_, bf16[2064,128]{1,0:T(8,128)(2,1)S(1)} %collective-permute-done.9.refs_1_, bf16[32,2,64,512]{3,2,1,0:T(8,128)(2,1)S(1)} %copy-done.4), custom_call_target="tpu_custom_call" | custom-call | flops 1073741824 | bytes 2621440 | tf_op jit(solution)/shard_map/pallas_call | solution.py:254
  59.6 2.0 %collective-permute-done.8.in_ref = bf16[4,528,128]{2,1,0:T(8,128)(2,1)S(1)} collective-permute-done((bf16[4,528,128]{2,1,0:T(8,128)(2,1)S(1)}, bf16[4,528,128]{2,1,0:T(8,128)(2,1)S(1)}, u32[]{:S(2)}, u32[]{:S(2)}) %collective-permute-start.8) | collective-permute-done | bytes 540704 | tf_op jit(solution)/shard_map/ppermute | solution.py:462
  61.5 1.0 shard_map.92
  62.5 1.6 %collective-permute-start.10 = (bf16[4,528,128]{2,1,0:T(8,128)(2,1)S(1)}, bf16[4,528,128]{2,1,0:T(8,128)(2,1)S(1)}, u32[]{:S(2)}, u32[]{:S(2)}) collective-permute-start(bf16[4,528,128]{2,1,0:T(8,128)(2,1)S(1)} %shard_map.92), channel_id=1, source_target_pairs={{0,4},{4,8},{8,12},{12,14},{14,10},{10,6},{6,2},{2,0},{1,3},{5,1},... | collective-permute-start | bytes 1622024 | tf_op jit(solution)/shard_map/ppermute | solution.py:462
  64.2 3.0 %collective-permute-done.11.refs_1_ = bf16[2064,128]{1,0:T(8,128)(2,1)S(1)} collective-permute-done((bf16[2064,128]{1,0:T(8,128)(2,1)S(1)}, bf16[2064,128]{1,0:T(8,128)(2,1)S(1)}, u32[]{:S(2)}, u32[]{:S(2)}) %collective-permute-start.11) | collective-permute-done | bytes 528416 | tf_op jit(solution)/shard_map/ppermute | solution.py:462
  67.2 1.6 %collective-permute-start.13 = (bf16[2064,128]{1,0:T(8,128)(2,1)S(1)}, bf16[2064,128]{1,0:T(8,128)(2,1)S(1)}, u32[]{:S(2)}, u32[]{:S(2)}) collective-permute-start(bf16[2064,128]{1,0:T(8,128)(2,1)S(1)} %collective-permute-done.11.refs_1_), channel_id=1, source_target_pairs={{0,4},{4,8},{8,12},{12,14},{14,10},{10,6},{6,2},{2,0},{1,3},{5,1},... | collective-permute-start | bytes 1585160 | tf_op jit(solution)/shard_map/ppermute | solution.py:462
  68.8 2.5 %collective-permute-start.14 = (bf16[1,2,64,512]{3,2,1,0:T(8,128)(2,1)S(1)}, bf16[1,2,64,512]{3,2,1,0:T(8,128)(2,1)S(1)}, u32[]{:S(2)}, u32[]{:S(2)}) collective-permute-start(bf16[1,2,64,512]{3,2,1,0:T(8,128)(2,1)S(1)} %copy-done.5), channel_id=1, source_target_pairs={{8,0},{10,2},{12,4},{14,6},{0,8},{2,10},{4,12},{6,14},{9,1},{11,3}... | collective-permute-start | bytes 393224 | tf_op jit(solution)/shard_map/ppermute | solution.py:27
  71.3 2.2 %shard_map.93 = (f32[4,512,128]{2,1,0:T(8,128)S(1)}, bf16[4,16,128]{2,1,0:T(8,128)(2,1)S(1)}) custom-call(s32[1,128]{1,0:T(1,128)S(1)} %fusion.6.refs_0_.far_ref, bf16[2064,128]{1,0:T(8,128)(2,1)S(1)} %collective-permute-done.11.refs_1_, bf16[32,2,64,512]{3,2,1,0:T(8,128)(2,1)S(1)} %copy-done.4), custom_call_target="tpu_custom_call" | custom-call | flops 1 | bytes 1 | tf_op jit(solution)/shard_map/pallas_call | solution.py:254
  73.6 0.0 collective-permute-done.10.in_ref
  73.6 1.0 shard_map.94
  74.6 3.0 %collective-permute-start.12 = (bf16[4,528,128]{2,1,0:T(8,128)(2,1)S(1)}, bf16[4,528,128]{2,1,0:T(8,128)(2,1)S(1)}, u32[]{:S(2)}, u32[]{:S(2)}) collective-permute-start(bf16[4,528,128]{2,1,0:T(8,128)(2,1)S(1)} %shard_map.94), channel_id=1, source_target_pairs={{0,4},{4,8},{8,12},{12,14},{14,10},{10,6},{6,2},{2,0},{1,3},{5,1},... | collective-permute-start | bytes 1622024 | tf_op jit(solution)/shard_map/ppermute | solution.py:462
  77.5 1.6 %collective-permute-done.13.refs_1_ = bf16[2064,128]{1,0:T(8,128)(2,1)S(1)} collective-permute-done((bf16[2064,128]{1,0:T(8,128)(2,1)S(1)}, bf16[2064,128]{1,0:T(8,128)(2,1)S(1)}, u32[]{:S(2)}, u32[]{:S(2)}) %collective-permute-start.13) | collective-permute-done | bytes 528416 | tf_op jit(solution)/shard_map/ppermute | solution.py:462
  79.2 2.2 %shard_map.95 = (f32[4,512,128]{2,1,0:T(8,128)S(1)}, bf16[4,16,128]{2,1,0:T(8,128)(2,1)S(1)}) custom-call(s32[1,128]{1,0:T(1,128)S(1)} %fusion.7.refs_0_, bf16[2064,128]{1,0:T(8,128)(2,1)S(1)} %collective-permute-done.13.refs_1_, bf16[32,2,64,512]{3,2,1,0:T(8,128)(2,1)S(1)} %copy-done.4), custom_call_target="tpu_custom_call" | custom-call | flops 8589934592 | bytes 33554432 | tf_op jit(solution)/shard_map/pallas_call | solution.py:254
  81.4 0.0 collective-permute-done.14.page_ref
  81.4 5.0 %collective-permute-done.12.in_ref = bf16[4,528,128]{2,1,0:T(8,128)(2,1)S(1)} collective-permute-done((bf16[4,528,128]{2,1,0:T(8,128)(2,1)S(1)}, bf16[4,528,128]{2,1,0:T(8,128)(2,1)S(1)}, u32[]{:S(2)}, u32[]{:S(2)}) %collective-permute-start.12) | collective-permute-done | bytes 540704 | tf_op jit(solution)/shard_map/ppermute | solution.py:462
  86.4 0.6 shard_map.96
  87.0 4.4 %collective-permute-start.16 = (bf16[2,528,128]{2,1,0:T(8,128)(2,1)S(1)}, bf16[2,528,128]{2,1,0:T(8,128)(2,1)S(1)}, u32[]{:S(2)}, u32[]{:S(2)}) collective-permute-start(bf16[2,528,128]{2,1,0:T(8,128)(2,1)S(1)} %shard_map.96), channel_id=1, source_target_pairs={{0,4},{4,8},{8,12},{12,14},{14,10},{10,6},{6,2},{2,0},{1,3},{5,1},... | collective-permute-start | bytes 811016 | tf_op jit(solution)/shard_map/ppermute | solution.py:462
  91.5 0.6 shard_map.97
  92.1 2.5 %collective-permute-start.15 = (bf16[2,528,128]{2,1,0:T(8,128)(2,1)S(1)}, bf16[2,528,128]{2,1,0:T(8,128)(2,1)S(1)}, u32[]{:S(2)}, u32[]{:S(2)}) collective-permute-start(bf16[2,528,128]{2,1,0:T(8,128)(2,1)S(1)} %shard_map.97), channel_id=1, source_target_pairs={{0,4},{4,8},{8,12},{12,14},{14,10},{10,6},{6,2},{2,0},{1,3},{5,1},... | collective-permute-start | bytes 811016 | tf_op jit(solution)/shard_map/ppermute | solution.py:462
  94.6 1.2 %shard_map.98 = bf16[32,2,64,512]{3,2,1,0:T(8,128)(2,1)} custom-call(s32[1]{0:T(128)} %bitcast.1.me_ref, s32[1]{0:T(128)} %bitcast.2.core_ref, s32[1,128]{1,0:T(1,128)S(1)} %fusion.1.refs_0_.near_ref, s32[1,128]{1,0:T(1,128)S(1)} %fusion.6.refs_0_.far_ref, ...), custom_call_target="tpu_custom_call", output_to_operand_aliasing={{}: (5, {})} | custom-call | flops 1 | bytes 1 | tf_op jit(solution)/shard_map/pallas_call | solution.py:292
  95.9 0.0 collective-permute-done.16.in_ref
  95.9 1.3 %shard_map.99.refs_0_ = bf16[1,64,4096]{2,1,0:T(8,128)(2,1)} custom-call(bf16[2,528,128]{2,1,0:T(8,128)(2,1)S(1)} %collective-permute-done.16.in_ref, f32[2,512,128]{2,1,0:T(8,128)S(1)} %get-tuple-element.58.acc_ref, bf16[2,16,128]{2,1,0:T(8,128)(2,1)S(1)} %get-tuple-element.59.stat_ref), custom_call_target="tpu_custom_call" | custom-call | tf_op jit(solution)/shard_map/pallas_call | solution.py:373
  97.2 1.5 %collective-permute-done.15.in_ref = bf16[2,528,128]{2,1,0:T(8,128)(2,1)S(1)} collective-permute-done((bf16[2,528,128]{2,1,0:T(8,128)(2,1)S(1)}, bf16[2,528,128]{2,1,0:T(8,128)(2,1)S(1)}, u32[]{:S(2)}, u32[]{:S(2)}) %collective-permute-start.15) | collective-permute-done | bytes 270368 | tf_op jit(solution)/shard_map/ppermute | solution.py:462
  98.6 1.3 %shard_map.100 = bf16[1,64,4096]{2,1,0:T(8,128)(2,1)} custom-call(bf16[2,528,128]{2,1,0:T(8,128)(2,1)S(1)} %collective-permute-done.15.in_ref, f32[2,512,128]{2,1,0:T(8,128)S(1)} %get-tuple-element.65.acc_ref, bf16[2,16,128]{2,1,0:T(8,128)(2,1)S(1)} %get-tuple-element.66.stat_ref, bf16[1,64,4096]{2,1,0:T(8,128)(2,1)} %shard_map.99.refs_0_), custom_call_target="tpu_custom_call", output_to_operand_aliasing={{}: (3, {})} | custom-call | tf_op jit(solution)/shard_map/pallas_call | solution.py:373
  (18 shorter events, 0.1 us)
Async XLA Ops:
  0.6 10.4 %collective-permute-start = (bf16[1,64,4096]{2,1,0:T(8,128)(2,1)}, bf16[1,64,4096]{2,1,0:T(8,128)(2,1)S(1)}, u32[]{:S(2)}, u32[]{:S(2)}) collective-permute-start(bf16[1,64,4096]{2,1,0:T(8,128)(2,1)} %q_ref), channel_id=1, source_target_pairs={{0,4},{4,8},{8,12},{12,14},{14,10},{10,6},{6,2},{2,0},{1,3},{5,1},... | collective-permute-start | bytes 1572872 | tf_op jit(solution)/shard_map/ppermute | solution.py:462
  5.0 0.7 copy-start.7
  5.9 5.1 %collective-permute-start.1 = (bf16[16,128]{1,0:T(8,128)(2,1)S(1)}, bf16[16,128]{1,0:T(8,128)(2,1)S(1)}, u32[]{:S(2)}, u32[]{:S(2)}) collective-permute-start(bf16[16,128]{1,0:T(8,128)(2,1)S(1)} %shard_map.77.lists_ref), channel_id=1, source_target_pairs={{0,4},{4,8},{8,12},{12,14},{14,10},{10,6},{6,2},{2,0},{1,3},{5,1},... | collective-permute-start | bytes 12296 | tf_op jit(solution)/shard_map/ppermute | solution.py:462
  7.5 2.2 %copy-start = (bf16[32,2,64,512]{3,2,1,0:T(8,128)(2,1)S(1)}, bf16[32,2,64,512]{3,2,1,0:T(8,128)(2,1)}, u32[]{:S(2)}) copy-start(bf16[32,2,64,512]{3,2,1,0:T(8,128)(2,1)} %refs_2_.13) | copy-start | bytes 12582916
  11.2 9.3 %collective-permute-start.3 = (bf16[2064,128]{1,0:T(8,128)(2,1)S(1)}, bf16[2064,128]{1,0:T(8,128)(2,1)S(1)}, u32[]{:S(2)}, u32[]{:S(2)}) collective-permute-start(bf16[2064,128]{1,0:T(8,128)(2,1)S(1)} %shard_map.79.refs_1_), channel_id=1, source_target_pairs={{0,4},{4,8},{8,12},{12,14},{14,10},{10,6},{6,2},{2,0},{1,3},{5,1},... | collective-permute-start | bytes 1585160 | tf_op jit(solution)/shard_map/ppermute | solution.py:462
  13.3 2.2 %copy-start.1 = (bf16[32,2,64,512]{3,2,1,0:T(8,128)(2,1)S(1)}, bf16[32,2,64,512]{3,2,1,0:T(8,128)(2,1)}, u32[]{:S(2)}) copy-start(bf16[32,2,64,512]{3,2,1,0:T(8,128)(2,1)} %refs_2_.13) | copy-start | bytes 12582916
  15.5 7.0 %copy-start.2 = (bf16[32,2,64,512]{3,2,1,0:T(8,128)(2,1)S(1)}, bf16[32,2,64,512]{3,2,1,0:T(8,128)(2,1)}, u32[]{:S(2)}) copy-start(bf16[32,2,64,512]{3,2,1,0:T(8,128)(2,1)} %refs_2_.13) | copy-start | bytes 12582916
  17.8 9.4 %collective-permute-start.2 = (bf16[4,528,128]{2,1,0:T(8,128)(2,1)S(1)}, bf16[4,528,128]{2,1,0:T(8,128)(2,1)S(1)}, u32[]{:S(2)}, u32[]{:S(2)}) collective-permute-start(bf16[4,528,128]{2,1,0:T(8,128)(2,1)S(1)} %shard_map.81), channel_id=1, source_target_pairs={{0,4},{4,8},{8,12},{12,14},{14,10},{10,6},{6,2},{2,0},{1,3},{5,1},... | collective-permute-start | bytes 1622024 | tf_op jit(solution)/shard_map/ppermute | solution.py:462
  20.4 12.4 %collective-permute-start.5 = (bf16[2064,128]{1,0:T(8,128)(2,1)S(1)}, bf16[2064,128]{1,0:T(8,128)(2,1)S(1)}, u32[]{:S(2)}, u32[]{:S(2)}) collective-permute-start(bf16[2064,128]{1,0:T(8,128)(2,1)S(1)} %collective-permute-done.3.refs_1_), channel_id=1, source_target_pairs={{0,4},{4,8},{8,12},{12,14},{14,10},{10,6},{6,2},{2,0},{1,3},{5,1},... | collective-permute-start | bytes 1585160 | tf_op jit(solution)/shard_map/ppermute | solution.py:462
  28.2 11.4 %collective-permute-start.4 = (bf16[4,528,128]{2,1,0:T(8,128)(2,1)S(1)}, bf16[4,528,128]{2,1,0:T(8,128)(2,1)S(1)}, u32[]{:S(2)}, u32[]{:S(2)}) collective-permute-start(bf16[4,528,128]{2,1,0:T(8,128)(2,1)S(1)} %shard_map.83), channel_id=1, source_target_pairs={{0,4},{4,8},{8,12},{12,14},{14,10},{10,6},{6,2},{2,0},{1,3},{5,1},... | collective-permute-start | bytes 1622024 | tf_op jit(solution)/shard_map/ppermute | solution.py:462
  32.8 11.5 %collective-permute-start.7 = (bf16[2064,128]{1,0:T(8,128)(2,1)S(1)}, bf16[2064,128]{1,0:T(8,128)(2,1)S(1)}, u32[]{:S(2)}, u32[]{:S(2)}) collective-permute-start(bf16[2064,128]{1,0:T(8,128)(2,1)S(1)} %collective-permute-done.5.refs_1_), channel_id=1, source_target_pairs={{0,4},{4,8},{8,12},{12,14},{14,10},{10,6},{6,2},{2,0},{1,3},{5,1},... | collective-permute-start | bytes 1585160 | tf_op jit(solution)/shard_map/ppermute | solution.py:462
  34.4 2.2 %copy-start.3 = (bf16[32,2,64,512]{3,2,1,0:T(8,128)(2,1)S(1)}, bf16[32,2,64,512]{3,2,1,0:T(8,128)(2,1)}, u32[]{:S(2)}) copy-start(bf16[32,2,64,512]{3,2,1,0:T(8,128)(2,1)} %refs_2_.13) | copy-start | bytes 12582916
  36.6 5.6 %copy-start.6 = (bf16[1,64,4096]{2,1,0:T(8,128)(2,1)S(1)}, bf16[1,64,4096]{2,1,0:T(8,128)(2,1)}, u32[]{:S(2)}) copy-start(bf16[1,64,4096]{2,1,0:T(8,128)(2,1)} %q_ref) | copy-start | bytes 1572868
  36.6 5.7 %copy-start.4 = (bf16[32,2,64,512]{3,2,1,0:T(8,128)(2,1)S(1)}, bf16[32,2,64,512]{3,2,1,0:T(8,128)(2,1)}, u32[]{:S(2)}) copy-start(bf16[32,2,64,512]{3,2,1,0:T(8,128)(2,1)} %refs_2_.13) | copy-start | bytes 12582916
  36.6 5.7 %copy-start.5 = (bf16[1,2,64,512]{3,2,1,0:T(8,128)(2,1)S(1)}, bf16[1,2,64,512]{3,2,1,0:T(8,128)(2,1)}, u32[]{:S(2)}) copy-start(bf16[1,2,64,512]{3,2,1,0:T(8,128)(2,1)} %param.7) | copy-start | bytes 393220
  40.6 9.5 %collective-permute-start.6 = (bf16[4,528,128]{2,1,0:T(8,128)(2,1)S(1)}, bf16[4,528,128]{2,1,0:T(8,128)(2,1)S(1)}, u32[]{:S(2)}, u32[]{:S(2)}) collective-permute-start(bf16[4,528,128]{2,1,0:T(8,128)(2,1)S(1)} %shard_map.85), channel_id=1, source_target_pairs={{0,4},{4,8},{8,12},{12,14},{14,10},{10,6},{6,2},{2,0},{1,3},{5,1},... | collective-permute-start | bytes 1622024 | tf_op jit(solution)/shard_map/ppermute | solution.py:462
  44.3 11.5 %collective-permute-start.9 = (bf16[2064,128]{1,0:T(8,128)(2,1)S(1)}, bf16[2064,128]{1,0:T(8,128)(2,1)S(1)}, u32[]{:S(2)}, u32[]{:S(2)}) collective-permute-start(bf16[2064,128]{1,0:T(8,128)(2,1)S(1)} %collective-permute-done.7.refs_1_), channel_id=1, source_target_pairs={{0,4},{4,8},{8,12},{12,14},{14,10},{10,6},{6,2},{2,0},{1,3},{5,1},... | collective-permute-start | bytes 1585160 | tf_op jit(solution)/shard_map/ppermute | solution.py:462
  51.1 10.5 %collective-permute-start.8 = (bf16[4,528,128]{2,1,0:T(8,128)(2,1)S(1)}, bf16[4,528,128]{2,1,0:T(8,128)(2,1)S(1)}, u32[]{:S(2)}, u32[]{:S(2)}) collective-permute-start(bf16[4,528,128]{2,1,0:T(8,128)(2,1)S(1)} %shard_map.89), channel_id=1, source_target_pairs={{0,4},{4,8},{8,12},{12,14},{14,10},{10,6},{6,2},{2,0},{1,3},{5,1},... | collective-permute-start | bytes 1622024 | tf_op jit(solution)/shard_map/ppermute | solution.py:462
  55.8 11.5 %collective-permute-start.11 = (bf16[2064,128]{1,0:T(8,128)(2,1)S(1)}, bf16[2064,128]{1,0:T(8,128)(2,1)S(1)}, u32[]{:S(2)}, u32[]{:S(2)}) collective-permute-start(bf16[2064,128]{1,0:T(8,128)(2,1)S(1)} %collective-permute-done.9.refs_1_), channel_id=1, source_target_pairs={{0,4},{4,8},{8,12},{12,14},{14,10},{10,6},{6,2},{2,0},{1,3},{5,1},... | collective-permute-start | bytes 1585160 | tf_op jit(solution)/shard_map/ppermute | solution.py:462
  62.5 11.0 %collective-permute-start.10 = (bf16[4,528,128]{2,1,0:T(8,128)(2,1)S(1)}, bf16[4,528,128]{2,1,0:T(8,128)(2,1)S(1)}, u32[]{:S(2)}, u32[]{:S(2)}) collective-permute-start(bf16[4,528,128]{2,1,0:T(8,128)(2,1)S(1)} %shard_map.92), channel_id=1, source_target_pairs={{0,4},{4,8},{8,12},{12,14},{14,10},{10,6},{6,2},{2,0},{1,3},{5,1},... | collective-permute-start | bytes 1622024 | tf_op jit(solution)/shard_map/ppermute | solution.py:462
  67.2 12.0 %collective-permute-start.13 = (bf16[2064,128]{1,0:T(8,128)(2,1)S(1)}, bf16[2064,128]{1,0:T(8,128)(2,1)S(1)}, u32[]{:S(2)}, u32[]{:S(2)}) collective-permute-start(bf16[2064,128]{1,0:T(8,128)(2,1)S(1)} %collective-permute-done.11.refs_1_), channel_id=1, source_target_pairs={{0,4},{4,8},{8,12},{12,14},{14,10},{10,6},{6,2},{2,0},{1,3},{5,1},... | collective-permute-start | bytes 1585160 | tf_op jit(solution)/shard_map/ppermute | solution.py:462
  68.8 12.6 %collective-permute-start.14 = (bf16[1,2,64,512]{3,2,1,0:T(8,128)(2,1)S(1)}, bf16[1,2,64,512]{3,2,1,0:T(8,128)(2,1)S(1)}, u32[]{:S(2)}, u32[]{:S(2)}) collective-permute-start(bf16[1,2,64,512]{3,2,1,0:T(8,128)(2,1)S(1)} %copy-done.5), channel_id=1, source_target_pairs={{8,0},{10,2},{12,4},{14,6},{0,8},{2,10},{4,12},{6,14},{9,1},{11,3}... | collective-permute-start | bytes 393224 | tf_op jit(solution)/shard_map/ppermute | solution.py:27
  74.6 11.8 %collective-permute-start.12 = (bf16[4,528,128]{2,1,0:T(8,128)(2,1)S(1)}, bf16[4,528,128]{2,1,0:T(8,128)(2,1)S(1)}, u32[]{:S(2)}, u32[]{:S(2)}) collective-permute-start(bf16[4,528,128]{2,1,0:T(8,128)(2,1)S(1)} %shard_map.94), channel_id=1, source_target_pairs={{0,4},{4,8},{8,12},{12,14},{14,10},{10,6},{6,2},{2,0},{1,3},{5,1},... | collective-permute-start | bytes 1622024 | tf_op jit(solution)/shard_map/ppermute | solution.py:462
  87.0 8.8 %collective-permute-start.16 = (bf16[2,528,128]{2,1,0:T(8,128)(2,1)S(1)}, bf16[2,528,128]{2,1,0:T(8,128)(2,1)S(1)}, u32[]{:S(2)}, u32[]{:S(2)}) collective-permute-start(bf16[2,528,128]{2,1,0:T(8,128)(2,1)S(1)} %shard_map.96), channel_id=1, source_target_pairs={{0,4},{4,8},{8,12},{12,14},{14,10},{10,6},{6,2},{2,0},{1,3},{5,1},... | collective-permute-start | bytes 811016 | tf_op jit(solution)/shard_map/ppermute | solution.py:462
  92.1 6.5 %collective-permute-start.15 = (bf16[2,528,128]{2,1,0:T(8,128)(2,1)S(1)}, bf16[2,528,128]{2,1,0:T(8,128)(2,1)S(1)}, u32[]{:S(2)}, u32[]{:S(2)}) collective-permute-start(bf16[2,528,128]{2,1,0:T(8,128)(2,1)S(1)} %shard_map.97), channel_id=1, source_target_pairs={{0,4},{4,8},{8,12},{12,14},{14,10},{10,6},{6,2},{2,0},{1,3},{5,1},... | collective-permute-start | bytes 811016 | tf_op jit(solution)/shard_map/ppermute | solution.py:462

commit v24 on v23

--- a/solution.py
+++ b/solution.py
@@ -502,7 +502,7 @@
             part, = attend(sizes, jobs, lists[step], [came], kv_pages, cost=cost)
         if step == 1:
             blocks = [packed(part)]
-        elif step < stores - 1:
+        elif step < stores - 3:
             blocks = [merged(after(partial[0], part), part, 0, 0, heads)]
         else:
             part = after(part, arrived) if step == stores - 1 else part

time: 100 us -> 101 us (1.010)
    ppermute x1, starting transfers between devices: 2.53 us -> 1.01 us  [shifted(): return lax.ppermute(block, axis, route)]
    ppermute x16 -> x18, starting transfers between devices: 33.4 us -> 34.5 us  [onward(): return lax.ppermute(x, ('store', 'tensor'), route)]
    ppermute x16 -> x18, waiting for transfers between devices: 23.7 us -> 24.3 us  [onward(): return lax.ppermute(x, ('store', 'tensor'), route)]
    pallas_call x10 -> x12, Pallas kernels: 6.42 us -> 6.98 us  [call(): pl.pallas_call(kernel, out_shape=shape, in_specs=[VMEM] * len(args), out_...]
  transfers between devices with their start and end apart: 17 -> 19, of which waited for: 12 -> 12; matrix products, arithmetic and copies ran while one was open for 0% -> 0% of each run, Pallas kernels for 29% -> 30%
where the time goes in v24:
time: 101 us
  starting transfers between devices  35.5 us (35%)
  Pallas kernels  31.4 us (31%)
  waiting for transfers between devices  24.3 us (24%)
  local copies, waits for them, and re-layouts  7.23 us (7%)
  between operations  2.32 us (2%)
    ppermute x18, starting transfers between devices, onward(): return lax.ppermute(x, ('store', 'tensor'), route)  34.5 us
    ppermute x18, waiting for transfers between devices, onward(): return lax.ppermute(x, ('store', 'tensor'), route)  24.3 us
    pallas_call x9, Pallas kernels, attend(): pl.pallas_call(functools.partial(attend_kernel, sizes + (count,), jobs, o...  20.3 us
    unnamed x16, local copies, waits for them, and re-layouts  7.23 us
    pallas_call x12, Pallas kernels, call(): pl.pallas_call(kernel, out_shape=shape, in_specs=[VMEM] * len(args), out_...  6.98 us
    pallas_call x2, Pallas kernels, finish(): pl.pallas_call(functools.partial(final_kernel, suffix, first), out_shape=...  2.53 us
  transfers between devices with their start and end apart: 19, of which 12 were waited for; matrix products, arithmetic and copies ran while one was open for 0% of the time, Pallas kernels for 30%

profile of v24, /device:TPU:0, one launch (start us, length us, event | category | flops | bytes accessed | tf_op | source)
XLA Modules:
  0.0 100.8 jit_solution(2580204515401932428)
XLA Ops:
  0.6 3.1 %collective-permute-start = (bf16[1,64,4096]{2,1,0:T(8,128)(2,1)}, bf16[1,64,4096]{2,1,0:T(8,128)(2,1)S(1)}, u32[]{:S(2)}, u32[]{:S(2)}) collective-permute-start(bf16[1,64,4096]{2,1,0:T(8,128)(2,1)} %q_ref), channel_id=1, source_target_pairs={{0,4},{4,8},{8,12},{12,14},{14,10},{10,6},{6,2},{2,0},{1,3},{5,1},... | collective-permute-start | bytes 1572872 | tf_op jit(solution)/shard_map/ppermute | solution.py:462
  5.0 0.6 copy-done.7
  5.7 0.3 shard_map.77.lists_ref
  5.9 1.6 %collective-permute-start.1 = (bf16[16,128]{1,0:T(8,128)(2,1)S(1)}, bf16[16,128]{1,0:T(8,128)(2,1)S(1)}, u32[]{:S(2)}, u32[]{:S(2)}) collective-permute-start(bf16[16,128]{1,0:T(8,128)(2,1)S(1)} %shard_map.77.lists_ref), channel_id=1, source_target_pairs={{0,4},{4,8},{8,12},{12,14},{14,10},{10,6},{6,2},{2,0},{1,3},{5,1},... | collective-permute-start | bytes 12296 | tf_op jit(solution)/shard_map/ppermute | solution.py:462
  7.5 2.2 %copy-done = bf16[32,2,64,512]{3,2,1,0:T(8,128)(2,1)S(1)} copy-done((bf16[32,2,64,512]{3,2,1,0:T(8,128)(2,1)S(1)}, bf16[32,2,64,512]{3,2,1,0:T(8,128)(2,1)}, u32[]{:S(2)}) %copy-start) | copy-done | bytes 4194328
  9.7 1.3 %collective-permute-done.q_ref = bf16[1,64,4096]{2,1,0:T(8,128)(2,1)S(1)} collective-permute-done((bf16[1,64,4096]{2,1,0:T(8,128)(2,1)}, bf16[1,64,4096]{2,1,0:T(8,128)(2,1)S(1)}, u32[]{:S(2)}, u32[]{:S(2)}) %collective-permute-start) | collective-permute-done | bytes 524320 | tf_op jit(solution)/shard_map/ppermute | solution.py:462
  11.0 0.0 collective-permute-done.1.lists_ref
  11.1 0.1 shard_map.79.refs_1_
  11.2 2.1 %collective-permute-start.3 = (bf16[2064,128]{1,0:T(8,128)(2,1)S(1)}, bf16[2064,128]{1,0:T(8,128)(2,1)S(1)}, u32[]{:S(2)}, u32[]{:S(2)}) collective-permute-start(bf16[2064,128]{1,0:T(8,128)(2,1)S(1)} %shard_map.79.refs_1_), channel_id=1, source_target_pairs={{0,4},{4,8},{8,12},{12,14},{14,10},{10,6},{6,2},{2,0},{1,3},{5,1},... | collective-permute-start | bytes 1585160 | tf_op jit(solution)/shard_map/ppermute | solution.py:462
  13.3 2.2 %copy-done.1 = bf16[32,2,64,512]{3,2,1,0:T(8,128)(2,1)S(1)} copy-done((bf16[32,2,64,512]{3,2,1,0:T(8,128)(2,1)S(1)}, bf16[32,2,64,512]{3,2,1,0:T(8,128)(2,1)}, u32[]{:S(2)}) %copy-start.1) | copy-done | bytes 4194328
  15.5 2.2 %shard_map.80 = (f32[4,512,128]{2,1,0:T(8,128)S(1)}, bf16[4,16,128]{2,1,0:T(8,128)(2,1)S(1)}) custom-call(s32[1,128]{1,0:T(1,128)S(1)} %fusion.refs_0_, bf16[2064,128]{1,0:T(8,128)(2,1)S(1)} %shard_map.79.refs_1_, bf16[32,2,64,512]{3,2,1,0:T(8,128)(2,1)S(1)} %copy-done.1), custom_call_target="tpu_custom_call" | custom-call | flops 1073741824 | bytes 2621440 | tf_op jit(solution)/shard_map/pallas_call | solution.py:254
  17.7 0.1 shard_map.81
  17.8 1.6 %collective-permute-start.2 = (bf16[4,528,128]{2,1,0:T(8,128)(2,1)S(1)}, bf16[4,528,128]{2,1,0:T(8,128)(2,1)S(1)}, u32[]{:S(2)}, u32[]{:S(2)}) collective-permute-start(bf16[4,528,128]{2,1,0:T(8,128)(2,1)S(1)} %shard_map.81), channel_id=1, source_target_pairs={{0,4},{4,8},{8,12},{12,14},{14,10},{10,6},{6,2},{2,0},{1,3},{5,1},... | collective-permute-start | bytes 1622024 | tf_op jit(solution)/shard_map/ppermute | solution.py:462
  19.4 1.0 %collective-permute-done.3.refs_1_ = bf16[2064,128]{1,0:T(8,128)(2,1)S(1)} collective-permute-done((bf16[2064,128]{1,0:T(8,128)(2,1)S(1)}, bf16[2064,128]{1,0:T(8,128)(2,1)S(1)}, u32[]{:S(2)}, u32[]{:S(2)}) %collective-permute-start.3) | collective-permute-done | bytes 528416 | tf_op jit(solution)/shard_map/ppermute | solution.py:462
  20.4 2.1 %collective-permute-start.5 = (bf16[2064,128]{1,0:T(8,128)(2,1)S(1)}, bf16[2064,128]{1,0:T(8,128)(2,1)S(1)}, u32[]{:S(2)}, u32[]{:S(2)}) collective-permute-start(bf16[2064,128]{1,0:T(8,128)(2,1)S(1)} %collective-permute-done.3.refs_1_), channel_id=1, source_target_pairs={{0,4},{4,8},{8,12},{12,14},{14,10},{10,6},{6,2},{2,0},{1,3},{5,1},... | collective-permute-start | bytes 1585160 | tf_op jit(solution)/shard_map/ppermute | solution.py:462
  22.5 2.7 %shard_map.82 = (f32[4,512,128]{2,1,0:T(8,128)S(1)}, bf16[4,16,128]{2,1,0:T(8,128)(2,1)S(1)}, bf16[32,2,64,512]{3,2,1,0:T(8,128)(2,1)}) custom-call(s32[1,128]{1,0:T(1,128)S(1)} %fusion.1.refs_0_.near_ref, bf16[2064,128]{1,0:T(8,128)(2,1)S(1)} %collective-permute-done.3.refs_1_, bf16[32,2,64,512]{3,2,1,0:T(8,128)(2,1)S(1)} %copy-done.2), custom_call_target="tpu_custom_call" | custom-call | flops 1073741824 | bytes 2621440 | tf_op jit(solution)/shard_map/pallas_call | solution.py:254
  25.3 1.9 %collective-permute-done.2.in_ref = bf16[4,528,128]{2,1,0:T(8,128)(2,1)S(1)} collective-permute-done((bf16[4,528,128]{2,1,0:T(8,128)(2,1)S(1)}, bf16[4,528,128]{2,1,0:T(8,128)(2,1)S(1)}, u32[]{:S(2)}, u32[]{:S(2)}) %collective-permute-start.2) | collective-permute-done | bytes 540704 | tf_op jit(solution)/shard_map/ppermute | solution.py:462
  27.2 1.0 shard_map.83
  28.2 1.6 %collective-permute-start.4 = (bf16[4,528,128]{2,1,0:T(8,128)(2,1)S(1)}, bf16[4,528,128]{2,1,0:T(8,128)(2,1)S(1)}, u32[]{:S(2)}, u32[]{:S(2)}) collective-permute-start(bf16[4,528,128]{2,1,0:T(8,128)(2,1)S(1)} %shard_map.83), channel_id=1, source_target_pairs={{0,4},{4,8},{8,12},{12,14},{14,10},{10,6},{6,2},{2,0},{1,3},{5,1},... | collective-permute-start | bytes 1622024 | tf_op jit(solution)/shard_map/ppermute | solution.py:462
  29.8 3.0 %collective-permute-done.5.refs_1_ = bf16[2064,128]{1,0:T(8,128)(2,1)S(1)} collective-permute-done((bf16[2064,128]{1,0:T(8,128)(2,1)S(1)}, bf16[2064,128]{1,0:T(8,128)(2,1)S(1)}, u32[]{:S(2)}, u32[]{:S(2)}) %collective-permute-start.5) | collective-permute-done | bytes 528416 | tf_op jit(solution)/shard_map/ppermute | solution.py:462
  32.8 1.6 %collective-permute-start.7 = (bf16[2064,128]{1,0:T(8,128)(2,1)S(1)}, bf16[2064,128]{1,0:T(8,128)(2,1)S(1)}, u32[]{:S(2)}, u32[]{:S(2)}) collective-permute-start(bf16[2064,128]{1,0:T(8,128)(2,1)S(1)} %collective-permute-done.5.refs_1_), channel_id=1, source_target_pairs={{0,4},{4,8},{8,12},{12,14},{14,10},{10,6},{6,2},{2,0},{1,3},{5,1},... | collective-permute-start | bytes 1585160 | tf_op jit(solution)/shard_map/ppermute | solution.py:462
  34.4 2.2 %copy-done.3 = bf16[32,2,64,512]{3,2,1,0:T(8,128)(2,1)S(1)} copy-done((bf16[32,2,64,512]{3,2,1,0:T(8,128)(2,1)S(1)}, bf16[32,2,64,512]{3,2,1,0:T(8,128)(2,1)}, u32[]{:S(2)}) %copy-start.3) | copy-done | bytes 4194328
  36.6 2.9 %shard_map.84 = (f32[4,512,128]{2,1,0:T(8,128)S(1)}, bf16[4,16,128]{2,1,0:T(8,128)(2,1)S(1)}, bf16[32,2,64,512]{3,2,1,0:T(8,128)(2,1)}) custom-call(s32[1,128]{1,0:T(1,128)S(1)} %fusion.2.refs_0_, bf16[2064,128]{1,0:T(8,128)(2,1)S(1)} %collective-permute-done.5.refs_1_, bf16[32,2,64,512]{3,2,1,0:T(8,128)(2,1)S(1)} %copy-done.3, ...), custom_call_target="tpu_custom_call", output_to_operand_aliasing={{2}: (3, {})} | custom-call | flops 1073741824 | bytes 2621440 | tf_op jit(solution)/shard_map/pallas_call | solution.py:254
  39.6 0.0 collective-permute-done.4.in_ref
  39.6 1.0 shard_map.85
  40.6 1.6 %collective-permute-start.6 = (bf16[4,528,128]{2,1,0:T(8,128)(2,1)S(1)}, bf16[4,528,128]{2,1,0:T(8,128)(2,1)S(1)}, u32[]{:S(2)}, u32[]{:S(2)}) collective-permute-start(bf16[4,528,128]{2,1,0:T(8,128)(2,1)S(1)} %shard_map.85), channel_id=1, source_target_pairs={{0,4},{4,8},{8,12},{12,14},{14,10},{10,6},{6,2},{2,0},{1,3},{5,1},... | collective-permute-start | bytes 1622024 | tf_op jit(solution)/shard_map/ppermute | solution.py:462
  42.2 0.1 shard_map.86.refs_1_
  42.3 1.8 %shard_map.87 = (f32[2,512,128]{2,1,0:T(8,128)S(1)}, bf16[2,16,128]{2,1,0:T(8,128)(2,1)S(1)}) custom-call(s32[1,128]{1,0:T(1,128)S(1)} %fusion.3.refs_0_, bf16[2064,128]{1,0:T(8,128)(2,1)S(1)} %shard_map.86.refs_1_, bf16[2,64,512]{2,1,0:T(8,128)(2,1)S(1)} %bitcast.3, bf16[32,2,64,512]{3,2,1,0:T(8,128)(2,1)S(1)} %copy-done.4), custom_call_target="tpu_custom_call" | custom-call | flops 536870912 | bytes 1310720 | tf_op jit(solution)/shard_map/pallas_call | solution.py:254
  44.1 0.2 collective-permute-done.7.refs_1_
  44.3 1.6 %collective-permute-start.9 = (bf16[2064,128]{1,0:T(8,128)(2,1)S(1)}, bf16[2064,128]{1,0:T(8,128)(2,1)S(1)}, u32[]{:S(2)}, u32[]{:S(2)}) collective-permute-start(bf16[2064,128]{1,0:T(8,128)(2,1)S(1)} %collective-permute-done.7.refs_1_), channel_id=1, source_target_pairs={{0,4},{4,8},{8,12},{12,14},{14,10},{10,6},{6,2},{2,0},{1,3},{5,1},... | collective-permute-start | bytes 1585160 | tf_op jit(solution)/shard_map/ppermute | solution.py:462
  45.9 2.2 %shard_map.88 = (f32[4,512,128]{2,1,0:T(8,128)S(1)}, bf16[4,16,128]{2,1,0:T(8,128)(2,1)S(1)}) custom-call(s32[1,128]{1,0:T(1,128)S(1)} %fusion.4.refs_0_, bf16[2064,128]{1,0:T(8,128)(2,1)S(1)} %collective-permute-done.7.refs_1_, bf16[32,2,64,512]{3,2,1,0:T(8,128)(2,1)S(1)} %copy-done.4), custom_call_target="tpu_custom_call" | custom-call | flops 1073741824 | bytes 2621440 | tf_op jit(solution)/shard_map/pallas_call | solution.py:254
  48.1 2.0 %collective-permute-done.6.in_ref = bf16[4,528,128]{2,1,0:T(8,128)(2,1)S(1)} collective-permute-done((bf16[4,528,128]{2,1,0:T(8,128)(2,1)S(1)}, bf16[4,528,128]{2,1,0:T(8,128)(2,1)S(1)}, u32[]{:S(2)}, u32[]{:S(2)}) %collective-permute-start.6) | collective-permute-done | bytes 540704 | tf_op jit(solution)/shard_map/ppermute | solution.py:462
  50.1 1.0 shard_map.89
  51.1 1.8 %collective-permute-start.8 = (bf16[4,528,128]{2,1,0:T(8,128)(2,1)S(1)}, bf16[4,528,128]{2,1,0:T(8,128)(2,1)S(1)}, u32[]{:S(2)}, u32[]{:S(2)}) collective-permute-start(bf16[4,528,128]{2,1,0:T(8,128)(2,1)S(1)} %shard_map.89), channel_id=1, source_target_pairs={{0,4},{4,8},{8,12},{12,14},{14,10},{10,6},{6,2},{2,0},{1,3},{5,1},... | collective-permute-start | bytes 1622024 | tf_op jit(solution)/shard_map/ppermute | solution.py:462
  52.9 1.8 %shard_map.90 = (f32[2,512,128]{2,1,0:T(8,128)S(1)}, bf16[2,16,128]{2,1,0:T(8,128)(2,1)S(1)}) custom-call(s32[1,128]{1,0:T(1,128)S(1)} %fusion.3.refs_0_, bf16[2064,128]{1,0:T(8,128)(2,1)S(1)} %shard_map.86.refs_1_, bf16[2,64,512]{2,1,0:T(8,128)(2,1)S(1)} %bitcast.4, bf16[32,2,64,512]{3,2,1,0:T(8,128)(2,1)S(1)} %copy-done.4), custom_call_target="tpu_custom_call" | custom-call | flops 536870912 | bytes 1310720 | tf_op jit(solution)/shard_map/pallas_call | solution.py:254
  54.7 1.1 %collective-permute-done.9.refs_1_ = bf16[2064,128]{1,0:T(8,128)(2,1)S(1)} collective-permute-done((bf16[2064,128]{1,0:T(8,128)(2,1)S(1)}, bf16[2064,128]{1,0:T(8,128)(2,1)S(1)}, u32[]{:S(2)}, u32[]{:S(2)}) %collective-permute-start.9) | collective-permute-done | bytes 528416 | tf_op jit(solution)/shard_map/ppermute | solution.py:462
  55.8 1.6 %collective-permute-start.11 = (bf16[2064,128]{1,0:T(8,128)(2,1)S(1)}, bf16[2064,128]{1,0:T(8,128)(2,1)S(1)}, u32[]{:S(2)}, u32[]{:S(2)}) collective-permute-start(bf16[2064,128]{1,0:T(8,128)(2,1)S(1)} %collective-permute-done.9.refs_1_), channel_id=1, source_target_pairs={{0,4},{4,8},{8,12},{12,14},{14,10},{10,6},{6,2},{2,0},{1,3},{5,1},... | collective-permute-start | bytes 1585160 | tf_op jit(solution)/shard_map/ppermute | solution.py:462
  57.3 2.2 %shard_map.91 = (f32[4,512,128]{2,1,0:T(8,128)S(1)}, bf16[4,16,128]{2,1,0:T(8,128)(2,1)S(1)}) custom-call(s32[1,128]{1,0:T(1,128)S(1)} %fusion.5.refs_0_, bf16[2064,128]{1,0:T(8,128)(2,1)S(1)} %collective-permute-done.9.refs_1_, bf16[32,2,64,512]{3,2,1,0:T(8,128)(2,1)S(1)} %copy-done.4), custom_call_target="tpu_custom_call" | custom-call | flops 1073741824 | bytes 2621440 | tf_op jit(solution)/shard_map/pallas_call | solution.py:254
  59.6 2.0 %collective-permute-done.8.in_ref = bf16[4,528,128]{2,1,0:T(8,128)(2,1)S(1)} collective-permute-done((bf16[4,528,128]{2,1,0:T(8,128)(2,1)S(1)}, bf16[4,528,128]{2,1,0:T(8,128)(2,1)S(1)}, u32[]{:S(2)}, u32[]{:S(2)}) %collective-permute-start.8) | collective-permute-done | bytes 540704 | tf_op jit(solution)/shard_map/ppermute | solution.py:462
  61.5 0.6 shard_map.92
  62.2 0.6 shard_map.93
  62.8 4.4 %collective-permute-done.11.refs_1_ = bf16[2064,128]{1,0:T(8,128)(2,1)S(1)} collective-permute-done((bf16[2064,128]{1,0:T(8,128)(2,1)S(1)}, bf16[2064,128]{1,0:T(8,128)(2,1)S(1)}, u32[]{:S(2)}, u32[]{:S(2)}) %collective-permute-start.11) | collective-permute-done | bytes 528416 | tf_op jit(solution)/shard_map/ppermute | solution.py:462
  67.2 1.6 %collective-permute-start.14 = (bf16[2064,128]{1,0:T(8,128)(2,1)S(1)}, bf16[2064,128]{1,0:T(8,128)(2,1)S(1)}, u32[]{:S(2)}, u32[]{:S(2)}) collective-permute-start(bf16[2064,128]{1,0:T(8,128)(2,1)S(1)} %collective-permute-done.11.refs_1_), channel_id=1, source_target_pairs={{0,4},{4,8},{8,12},{12,14},{14,10},{10,6},{6,2},{2,0},{1,3},{5,1},... | collective-permute-start | bytes 1585160 | tf_op jit(solution)/shard_map/ppermute | solution.py:462
  68.8 1.6 %collective-permute-start.12 = (bf16[2,528,128]{2,1,0:T(8,128)(2,1)S(1)}, bf16[2,528,128]{2,1,0:T(8,128)(2,1)S(1)}, u32[]{:S(2)}, u32[]{:S(2)}) collective-permute-start(bf16[2,528,128]{2,1,0:T(8,128)(2,1)S(1)} %shard_map.92), channel_id=1, source_target_pairs={{0,4},{4,8},{8,12},{12,14},{14,10},{10,6},{6,2},{2,0},{1,3},{5,1},... | collective-permute-start | bytes 811016 | tf_op jit(solution)/shard_map/ppermute | solution.py:462
  70.4 1.5 %collective-permute-start.10 = (bf16[2,528,128]{2,1,0:T(8,128)(2,1)S(1)}, bf16[2,528,128]{2,1,0:T(8,128)(2,1)S(1)}, u32[]{:S(2)}, u32[]{:S(2)}) collective-permute-start(bf16[2,528,128]{2,1,0:T(8,128)(2,1)S(1)} %shard_map.93), channel_id=1, source_target_pairs={{0,4},{4,8},{8,12},{12,14},{14,10},{10,6},{6,2},{2,0},{1,3},{5,1},... | collective-permute-start | bytes 811016 | tf_op jit(solution)/shard_map/ppermute | solution.py:462
  71.9 1.0 %collective-permute-start.15 = (bf16[1,2,64,512]{3,2,1,0:T(8,128)(2,1)S(1)}, bf16[1,2,64,512]{3,2,1,0:T(8,128)(2,1)S(1)}, u32[]{:S(2)}, u32[]{:S(2)}) collective-permute-start(bf16[1,2,64,512]{3,2,1,0:T(8,128)(2,1)S(1)} %copy-done.5), channel_id=1, source_target_pairs={{8,0},{10,2},{12,4},{14,6},{0,8},{2,10},{4,12},{6,14},{9,1},{11,3}... | collective-permute-start | bytes 393224 | tf_op jit(solution)/shard_map/ppermute | solution.py:27
  72.9 2.2 %shard_map.94 = (f32[4,512,128]{2,1,0:T(8,128)S(1)}, bf16[4,16,128]{2,1,0:T(8,128)(2,1)S(1)}) custom-call(s32[1,128]{1,0:T(1,128)S(1)} %fusion.6.refs_0_.far_ref, bf16[2064,128]{1,0:T(8,128)(2,1)S(1)} %collective-permute-done.11.refs_1_, bf16[32,2,64,512]{3,2,1,0:T(8,128)(2,1)S(1)} %copy-done.4), custom_call_target="tpu_custom_call" | custom-call | flops 1 | bytes 1 | tf_op jit(solution)/shard_map/pallas_call | solution.py:254
  75.1 4.2 %collective-permute-done.12.in_ref = bf16[2,528,128]{2,1,0:T(8,128)(2,1)S(1)} collective-permute-done((bf16[2,528,128]{2,1,0:T(8,128)(2,1)S(1)}, bf16[2,528,128]{2,1,0:T(8,128)(2,1)S(1)}, u32[]{:S(2)}, u32[]{:S(2)}) %collective-permute-start.12) | collective-permute-done | bytes 270368 | tf_op jit(solution)/shard_map/ppermute | solution.py:462
  79.3 0.6 shard_map.95
  80.0 2.5 %collective-permute-start.16 = (bf16[2,528,128]{2,1,0:T(8,128)(2,1)S(1)}, bf16[2,528,128]{2,1,0:T(8,128)(2,1)S(1)}, u32[]{:S(2)}, u32[]{:S(2)}) collective-permute-start(bf16[2,528,128]{2,1,0:T(8,128)(2,1)S(1)} %shard_map.95), channel_id=1, source_target_pairs={{0,4},{4,8},{8,12},{12,14},{14,10},{10,6},{6,2},{2,0},{1,3},{5,1},... | collective-permute-start | bytes 811016 | tf_op jit(solution)/shard_map/ppermute | solution.py:462
  82.5 0.6 shard_map.96
  83.1 3.1 %collective-permute-start.13 = (bf16[2,528,128]{2,1,0:T(8,128)(2,1)S(1)}, bf16[2,528,128]{2,1,0:T(8,128)(2,1)S(1)}, u32[]{:S(2)}, u32[]{:S(2)}) collective-permute-start(bf16[2,528,128]{2,1,0:T(8,128)(2,1)S(1)} %shard_map.96), channel_id=1, source_target_pairs={{0,4},{4,8},{8,12},{12,14},{14,10},{10,6},{6,2},{2,0},{1,3},{5,1},... | collective-permute-start | bytes 811016 | tf_op jit(solution)/shard_map/ppermute | solution.py:462
  86.2 0.0 collective-permute-done.14.refs_1_
  86.2 2.2 %shard_map.97 = (f32[4,512,128]{2,1,0:T(8,128)S(1)}, bf16[4,16,128]{2,1,0:T(8,128)(2,1)S(1)}) custom-call(s32[1,128]{1,0:T(1,128)S(1)} %fusion.7.refs_0_, bf16[2064,128]{1,0:T(8,128)(2,1)S(1)} %collective-permute-done.14.refs_1_, bf16[32,2,64,512]{3,2,1,0:T(8,128)(2,1)S(1)} %copy-done.4), custom_call_target="tpu_custom_call" | custom-call | flops 8589934592 | bytes 33554432 | tf_op jit(solution)/shard_map/pallas_call | solution.py:254
  88.4 0.0 collective-permute-done.15.page_ref
  88.5 0.6 shard_map.98
  89.1 2.5 %collective-permute-start.18 = (bf16[2,528,128]{2,1,0:T(8,128)(2,1)S(1)}, bf16[2,528,128]{2,1,0:T(8,128)(2,1)S(1)}, u32[]{:S(2)}, u32[]{:S(2)}) collective-permute-start(bf16[2,528,128]{2,1,0:T(8,128)(2,1)S(1)} %shard_map.98), channel_id=1, source_target_pairs={{0,4},{4,8},{8,12},{12,14},{14,10},{10,6},{6,2},{2,0},{1,3},{5,1},... | collective-permute-start | bytes 811016 | tf_op jit(solution)/shard_map/ppermute | solution.py:462
  91.6 0.6 shard_map.99
  92.2 1.4 %collective-permute-start.17 = (bf16[2,528,128]{2,1,0:T(8,128)(2,1)S(1)}, bf16[2,528,128]{2,1,0:T(8,128)(2,1)S(1)}, u32[]{:S(2)}, u32[]{:S(2)}) collective-permute-start(bf16[2,528,128]{2,1,0:T(8,128)(2,1)S(1)} %shard_map.99), channel_id=1, source_target_pairs={{0,4},{4,8},{8,12},{12,14},{14,10},{10,6},{6,2},{2,0},{1,3},{5,1},... | collective-permute-start | bytes 811016 | tf_op jit(solution)/shard_map/ppermute | solution.py:462
  93.7 1.2 %shard_map.100 = bf16[32,2,64,512]{3,2,1,0:T(8,128)(2,1)} custom-call(s32[1]{0:T(128)} %bitcast.1.me_ref, s32[1]{0:T(128)} %bitcast.2.core_ref, s32[1,128]{1,0:T(1,128)S(1)} %fusion.1.refs_0_.near_ref, s32[1,128]{1,0:T(1,128)S(1)} %fusion.6.refs_0_.far_ref, ...), custom_call_target="tpu_custom_call", output_to_operand_aliasing={{}: (5, {})} | custom-call | flops 1 | bytes 1 | tf_op jit(solution)/shard_map/pallas_call | solution.py:292
  94.9 1.6 %collective-permute-done.18.in_ref = bf16[2,528,128]{2,1,0:T(8,128)(2,1)S(1)} collective-permute-done((bf16[2,528,128]{2,1,0:T(8,128)(2,1)S(1)}, bf16[2,528,128]{2,1,0:T(8,128)(2,1)S(1)}, u32[]{:S(2)}, u32[]{:S(2)}) %collective-permute-start.18) | collective-permute-done | bytes 270368 | tf_op jit(solution)/shard_map/ppermute | solution.py:462
  96.4 1.3 %shard_map.101.refs_0_ = bf16[1,64,4096]{2,1,0:T(8,128)(2,1)} custom-call(bf16[2,528,128]{2,1,0:T(8,128)(2,1)S(1)} %collective-permute-done.18.in_ref, f32[2,512,128]{2,1,0:T(8,128)S(1)} %get-tuple-element.60.acc_ref, bf16[2,16,128]{2,1,0:T(8,128)(2,1)S(1)} %get-tuple-element.61.stat_ref), custom_call_target="tpu_custom_call" | custom-call | tf_op jit(solution)/shard_map/pallas_call | solution.py:373
  97.7 1.6 %collective-permute-done.17.in_ref = bf16[2,528,128]{2,1,0:T(8,128)(2,1)S(1)} collective-permute-done((bf16[2,528,128]{2,1,0:T(8,128)(2,1)S(1)}, bf16[2,528,128]{2,1,0:T(8,128)(2,1)S(1)}, u32[]{:S(2)}, u32[]{:S(2)}) %collective-permute-start.17) | collective-permute-done | bytes 270368 | tf_op jit(solution)/shard_map/ppermute | solution.py:462
  99.3 1.3 %shard_map.102 = bf16[1,64,4096]{2,1,0:T(8,128)(2,1)} custom-call(bf16[2,528,128]{2,1,0:T(8,128)(2,1)S(1)} %collective-permute-done.17.in_ref, f32[2,512,128]{2,1,0:T(8,128)S(1)} %get-tuple-element.67.acc_ref, bf16[2,16,128]{2,1,0:T(8,128)(2,1)S(1)} %get-tuple-element.68.stat_ref, ...), custom_call_target="tpu_custom_call", output_to_operand_aliasing={{}: (3, {})} | custom-call | tf_op jit(solution)/shard_map/pallas_call | solution.py:373
  (24 shorter events, 0.1 us)
Async XLA Ops:
  0.6 10.4 %collective-permute-start = (bf16[1,64,4096]{2,1,0:T(8,128)(2,1)}, bf16[1,64,4096]{2,1,0:T(8,128)(2,1)S(1)}, u32[]{:S(2)}, u32[]{:S(2)}) collective-permute-start(bf16[1,64,4096]{2,1,0:T(8,128)(2,1)} %q_ref), channel_id=1, source_target_pairs={{0,4},{4,8},{8,12},{12,14},{14,10},{10,6},{6,2},{2,0},{1,3},{5,1},... | collective-permute-start | bytes 1572872 | tf_op jit(solution)/shard_map/ppermute | solution.py:462
  5.0 0.7 copy-start.7
  5.9 5.1 %collective-permute-start.1 = (bf16[16,128]{1,0:T(8,128)(2,1)S(1)}, bf16[16,128]{1,0:T(8,128)(2,1)S(1)}, u32[]{:S(2)}, u32[]{:S(2)}) collective-permute-start(bf16[16,128]{1,0:T(8,128)(2,1)S(1)} %shard_map.77.lists_ref), channel_id=1, source_target_pairs={{0,4},{4,8},{8,12},{12,14},{14,10},{10,6},{6,2},{2,0},{1,3},{5,1},... | collective-permute-start | bytes 12296 | tf_op jit(solution)/shard_map/ppermute | solution.py:462
  7.5 2.2 %copy-start = (bf16[32,2,64,512]{3,2,1,0:T(8,128)(2,1)S(1)}, bf16[32,2,64,512]{3,2,1,0:T(8,128)(2,1)}, u32[]{:S(2)}) copy-start(bf16[32,2,64,512]{3,2,1,0:T(8,128)(2,1)} %refs_2_.13) | copy-start | bytes 12582916
  11.2 9.3 %collective-permute-start.3 = (bf16[2064,128]{1,0:T(8,128)(2,1)S(1)}, bf16[2064,128]{1,0:T(8,128)(2,1)S(1)}, u32[]{:S(2)}, u32[]{:S(2)}) collective-permute-start(bf16[2064,128]{1,0:T(8,128)(2,1)S(1)} %shard_map.79.refs_1_), channel_id=1, source_target_pairs={{0,4},{4,8},{8,12},{12,14},{14,10},{10,6},{6,2},{2,0},{1,3},{5,1},... | collective-permute-start | bytes 1585160 | tf_op jit(solution)/shard_map/ppermute | solution.py:462
  13.3 2.2 %copy-start.1 = (bf16[32,2,64,512]{3,2,1,0:T(8,128)(2,1)S(1)}, bf16[32,2,64,512]{3,2,1,0:T(8,128)(2,1)}, u32[]{:S(2)}) copy-start(bf16[32,2,64,512]{3,2,1,0:T(8,128)(2,1)} %refs_2_.13) | copy-start | bytes 12582916
  15.5 7.0 %copy-start.2 = (bf16[32,2,64,512]{3,2,1,0:T(8,128)(2,1)S(1)}, bf16[32,2,64,512]{3,2,1,0:T(8,128)(2,1)}, u32[]{:S(2)}) copy-start(bf16[32,2,64,512]{3,2,1,0:T(8,128)(2,1)} %refs_2_.13) | copy-start | bytes 12582916
  17.8 9.4 %collective-permute-start.2 = (bf16[4,528,128]{2,1,0:T(8,128)(2,1)S(1)}, bf16[4,528,128]{2,1,0:T(8,128)(2,1)S(1)}, u32[]{:S(2)}, u32[]{:S(2)}) collective-permute-start(bf16[4,528,128]{2,1,0:T(8,128)(2,1)S(1)} %shard_map.81), channel_id=1, source_target_pairs={{0,4},{4,8},{8,12},{12,14},{14,10},{10,6},{6,2},{2,0},{1,3},{5,1},... | collective-permute-start | bytes 1622024 | tf_op jit(solution)/shard_map/ppermute | solution.py:462
  20.4 12.4 %collective-permute-start.5 = (bf16[2064,128]{1,0:T(8,128)(2,1)S(1)}, bf16[2064,128]{1,0:T(8,128)(2,1)S(1)}, u32[]{:S(2)}, u32[]{:S(2)}) collective-permute-start(bf16[2064,128]{1,0:T(8,128)(2,1)S(1)} %collective-permute-done.3.refs_1_), channel_id=1, source_target_pairs={{0,4},{4,8},{8,12},{12,14},{14,10},{10,6},{6,2},{2,0},{1,3},{5,1},... | collective-permute-start | bytes 1585160 | tf_op jit(solution)/shard_map/ppermute | solution.py:462
  28.2 11.4 %collective-permute-start.4 = (bf16[4,528,128]{2,1,0:T(8,128)(2,1)S(1)}, bf16[4,528,128]{2,1,0:T(8,128)(2,1)S(1)}, u32[]{:S(2)}, u32[]{:S(2)}) collective-permute-start(bf16[4,528,128]{2,1,0:T(8,128)(2,1)S(1)} %shard_map.83), channel_id=1, source_target_pairs={{0,4},{4,8},{8,12},{12,14},{14,10},{10,6},{6,2},{2,0},{1,3},{5,1},... | collective-permute-start | bytes 1622024 | tf_op jit(solution)/shard_map/ppermute | solution.py:462
  32.8 11.5 %collective-permute-start.7 = (bf16[2064,128]{1,0:T(8,128)(2,1)S(1)}, bf16[2064,128]{1,0:T(8,128)(2,1)S(1)}, u32[]{:S(2)}, u32[]{:S(2)}) collective-permute-start(bf16[2064,128]{1,0:T(8,128)(2,1)S(1)} %collective-permute-done.5.refs_1_), channel_id=1, source_target_pairs={{0,4},{4,8},{8,12},{12,14},{14,10},{10,6},{6,2},{2,0},{1,3},{5,1},... | collective-permute-start | bytes 1585160 | tf_op jit(solution)/shard_map/ppermute | solution.py:462
  34.4 2.2 %copy-start.3 = (bf16[32,2,64,512]{3,2,1,0:T(8,128)(2,1)S(1)}, bf16[32,2,64,512]{3,2,1,0:T(8,128)(2,1)}, u32[]{:S(2)}) copy-start(bf16[32,2,64,512]{3,2,1,0:T(8,128)(2,1)} %refs_2_.13) | copy-start | bytes 12582916
  36.6 5.6 %copy-start.6 = (bf16[1,64,4096]{2,1,0:T(8,128)(2,1)S(1)}, bf16[1,64,4096]{2,1,0:T(8,128)(2,1)}, u32[]{:S(2)}) copy-start(bf16[1,64,4096]{2,1,0:T(8,128)(2,1)} %q_ref) | copy-start | bytes 1572868
  36.6 5.7 %copy-start.4 = (bf16[32,2,64,512]{3,2,1,0:T(8,128)(2,1)S(1)}, bf16[32,2,64,512]{3,2,1,0:T(8,128)(2,1)}, u32[]{:S(2)}) copy-start(bf16[32,2,64,512]{3,2,1,0:T(8,128)(2,1)} %refs_2_.13) | copy-start | bytes 12582916
  36.6 5.7 %copy-start.5 = (bf16[1,2,64,512]{3,2,1,0:T(8,128)(2,1)S(1)}, bf16[1,2,64,512]{3,2,1,0:T(8,128)(2,1)}, u32[]{:S(2)}) copy-start(bf16[1,2,64,512]{3,2,1,0:T(8,128)(2,1)} %param.7) | copy-start | bytes 393220
  40.6 9.5 %collective-permute-start.6 = (bf16[4,528,128]{2,1,0:T(8,128)(2,1)S(1)}, bf16[4,528,128]{2,1,0:T(8,128)(2,1)S(1)}, u32[]{:S(2)}, u32[]{:S(2)}) collective-permute-start(bf16[4,528,128]{2,1,0:T(8,128)(2,1)S(1)} %shard_map.85), channel_id=1, source_target_pairs={{0,4},{4,8},{8,12},{12,14},{14,10},{10,6},{6,2},{2,0},{1,3},{5,1},... | collective-permute-start | bytes 1622024 | tf_op jit(solution)/shard_map/ppermute | solution.py:462
  44.3 11.5 %collective-permute-start.9 = (bf16[2064,128]{1,0:T(8,128)(2,1)S(1)}, bf16[2064,128]{1,0:T(8,128)(2,1)S(1)}, u32[]{:S(2)}, u32[]{:S(2)}) collective-permute-start(bf16[2064,128]{1,0:T(8,128)(2,1)S(1)} %collective-permute-done.7.refs_1_), channel_id=1, source_target_pairs={{0,4},{4,8},{8,12},{12,14},{14,10},{10,6},{6,2},{2,0},{1,3},{5,1},... | collective-permute-start | bytes 1585160 | tf_op jit(solution)/shard_map/ppermute | solution.py:462
  51.1 10.5 %collective-permute-start.8 = (bf16[4,528,128]{2,1,0:T(8,128)(2,1)S(1)}, bf16[4,528,128]{2,1,0:T(8,128)(2,1)S(1)}, u32[]{:S(2)}, u32[]{:S(2)}) collective-permute-start(bf16[4,528,128]{2,1,0:T(8,128)(2,1)S(1)} %shard_map.89), channel_id=1, source_target_pairs={{0,4},{4,8},{8,12},{12,14},{14,10},{10,6},{6,2},{2,0},{1,3},{5,1},... | collective-permute-start | bytes 1622024 | tf_op jit(solution)/shard_map/ppermute | solution.py:462
  55.8 11.5 %collective-permute-start.11 = (bf16[2064,128]{1,0:T(8,128)(2,1)S(1)}, bf16[2064,128]{1,0:T(8,128)(2,1)S(1)}, u32[]{:S(2)}, u32[]{:S(2)}) collective-permute-start(bf16[2064,128]{1,0:T(8,128)(2,1)S(1)} %collective-permute-done.9.refs_1_), channel_id=1, source_target_pairs={{0,4},{4,8},{8,12},{12,14},{14,10},{10,6},{6,2},{2,0},{1,3},{5,1},... | collective-permute-start | bytes 1585160 | tf_op jit(solution)/shard_map/ppermute | solution.py:462
  67.2 19.0 %collective-permute-start.14 = (bf16[2064,128]{1,0:T(8,128)(2,1)S(1)}, bf16[2064,128]{1,0:T(8,128)(2,1)S(1)}, u32[]{:S(2)}, u32[]{:S(2)}) collective-permute-start(bf16[2064,128]{1,0:T(8,128)(2,1)S(1)} %collective-permute-done.11.refs_1_), channel_id=1, source_target_pairs={{0,4},{4,8},{8,12},{12,14},{14,10},{10,6},{6,2},{2,0},{1,3},{5,1},... | collective-permute-start | bytes 1585160 | tf_op jit(solution)/shard_map/ppermute | solution.py:462
  68.8 10.5 %collective-permute-start.12 = (bf16[2,528,128]{2,1,0:T(8,128)(2,1)S(1)}, bf16[2,528,128]{2,1,0:T(8,128)(2,1)S(1)}, u32[]{:S(2)}, u32[]{:S(2)}) collective-permute-start(bf16[2,528,128]{2,1,0:T(8,128)(2,1)S(1)} %shard_map.92), channel_id=1, source_target_pairs={{0,4},{4,8},{8,12},{12,14},{14,10},{10,6},{6,2},{2,0},{1,3},{5,1},... | collective-permute-start | bytes 811016 | tf_op jit(solution)/shard_map/ppermute | solution.py:462
  70.4 12.1 %collective-permute-start.10 = (bf16[2,528,128]{2,1,0:T(8,128)(2,1)S(1)}, bf16[2,528,128]{2,1,0:T(8,128)(2,1)S(1)}, u32[]{:S(2)}, u32[]{:S(2)}) collective-permute-start(bf16[2,528,128]{2,1,0:T(8,128)(2,1)S(1)} %shard_map.93), channel_id=1, source_target_pairs={{0,4},{4,8},{8,12},{12,14},{14,10},{10,6},{6,2},{2,0},{1,3},{5,1},... | collective-permute-start | bytes 811016 | tf_op jit(solution)/shard_map/ppermute | solution.py:462
  71.9 16.5 %collective-permute-start.15 = (bf16[1,2,64,512]{3,2,1,0:T(8,128)(2,1)S(1)}, bf16[1,2,64,512]{3,2,1,0:T(8,128)(2,1)S(1)}, u32[]{:S(2)}, u32[]{:S(2)}) collective-permute-start(bf16[1,2,64,512]{3,2,1,0:T(8,128)(2,1)S(1)} %copy-done.5), channel_id=1, source_target_pairs={{8,0},{10,2},{12,4},{14,6},{0,8},{2,10},{4,12},{6,14},{9,1},{11,3}... | collective-permute-start | bytes 393224 | tf_op jit(solution)/shard_map/ppermute | solution.py:27
  80.0 8.5 %collective-permute-start.16 = (bf16[2,528,128]{2,1,0:T(8,128)(2,1)S(1)}, bf16[2,528,128]{2,1,0:T(8,128)(2,1)S(1)}, u32[]{:S(2)}, u32[]{:S(2)}) collective-permute-start(bf16[2,528,128]{2,1,0:T(8,128)(2,1)S(1)} %shard_map.95), channel_id=1, source_target_pairs={{0,4},{4,8},{8,12},{12,14},{14,10},{10,6},{6,2},{2,0},{1,3},{5,1},... | collective-permute-start | bytes 811016 | tf_op jit(solution)/shard_map/ppermute | solution.py:462
  83.1 8.5 %collective-permute-start.13 = (bf16[2,528,128]{2,1,0:T(8,128)(2,1)S(1)}, bf16[2,528,128]{2,1,0:T(8,128)(2,1)S(1)}, u32[]{:S(2)}, u32[]{:S(2)}) collective-permute-start(bf16[2,528,128]{2,1,0:T(8,128)(2,1)S(1)} %shard_map.96), channel_id=1, source_target_pairs={{0,4},{4,8},{8,12},{12,14},{14,10},{10,6},{6,2},{2,0},{1,3},{5,1},... | collective-permute-start | bytes 811016 | tf_op jit(solution)/shard_map/ppermute | solution.py:462
  89.1 7.3 %collective-permute-start.18 = (bf16[2,528,128]{2,1,0:T(8,128)(2,1)S(1)}, bf16[2,528,128]{2,1,0:T(8,128)(2,1)S(1)}, u32[]{:S(2)}, u32[]{:S(2)}) collective-permute-start(bf16[2,528,128]{2,1,0:T(8,128)(2,1)S(1)} %shard_map.98), channel_id=1, source_target_pairs={{0,4},{4,8},{8,12},{12,14},{14,10},{10,6},{6,2},{2,0},{1,3},{5,1},... | collective-permute-start | bytes 811016 | tf_op jit(solution)/shard_map/ppermute | solution.py:462
  92.2 7.1 %collective-permute-start.17 = (bf16[2,528,128]{2,1,0:T(8,128)(2,1)S(1)}, bf16[2,528,128]{2,1,0:T(8,128)(2,1)S(1)}, u32[]{:S(2)}, u32[]{:S(2)}) collective-permute-start(bf16[2,528,128]{2,1,0:T(8,128)(2,1)S(1)} %shard_map.99), channel_id=1, source_target_pairs={{0,4},{4,8},{8,12},{12,14},{14,10},{10,6},{6,2},{2,0},{1,3},{5,1},... | collective-permute-start | bytes 811016 | tf_op jit(solution)/shard_map/ppermute | solution.py:462
